TPU v7x, 32 devices: a whole 2x2x4 slice. The times are simulated.
32 devices in a mesh: chain: 2 (over core), leaf: 4 (over y, x), head: 4 (over z).
Axes of the slice: x: 2, y: 2, z: 4, core: 2. Of those that a mesh axis runs over, the one named last changes fastest.
Arguments:
- query_in: bfloat16 [4096, 16, 128], P(('chain', 'leaf'), 'head'), may hold values from -6 to 6
- key_in: bfloat16 [4096, 16, 128], P(('chain', 'leaf'), 'head'), may hold values from -120 to 120
- value_in: bfloat16 [4096, 16, 128], P(('chain', 'leaf'), 'head'), may hold values from -6 to 6
- gate_in: bfloat16 [4096, 16, 128], P(('chain', 'leaf'), 'head'), may hold values from -6 to 6
- write_strength: float32 [16, 4096], P('head', ('chain', 'leaf')), as said below
- log_decay: float32 [16, 4096], P('head', ('chain', 'leaf')), as said below
- doc_resets: int32 [64], P(('chain', 'leaf')), may hold values from 0 to 1, as said below
- conv_weight: float32 [3, 4, 16, 128], P(None, None, 'head'), may hold values from -3 to 3
- output_norm_gain: float32 [128], replicated, may hold values from 0.25 to 1.75
- output_projection_weight: bfloat16 [2048, 4096], P(None, 'head'), may hold values from -0.125 to 0.125
Outputs:
- mixed: bfloat16 [4096, 4096], P(('chain', 'leaf'), 'head')
Inputs may be any that keep to these rules, and one draw needn't show every extreme that they name: `write_strength`: strictly positive. `log_decay`: strictly negative. `doc_resets`: at least one block of every draw starts a document.
All inputs are finite; a program needn't handle non-finite values.
Results may differ from a plain program's by a relative error of at most 0.0064.
Values may be sent and summed in bfloat16 or wider, within the bound.
No kernel may reach another device: no remote copies, remote signals or barrier semaphores. Data moves between devices by JAX's collectives and lax.ppermute only.
A program may use at most 64 MiB of HBM per device.

v0:
```python
import jax
import jax.numpy as jnp
from jax import lax
from jax.sharding import PartitionSpec as P

BLOCK = 64


highest = lax.Precision.HIGHEST
epsilon = 1e-06


def from_behind(value, axis, steps):
    count = lax.axis_size(axis)
    initial, last = (max(0, -steps), min(count, count - steps))
    return lax.ppermute(value, axis, [(source, source + steps) for source in range(initial, last)])


def prefix(part, axis, combine, identity):
    place = lax.axis_index(axis)
    gathered = jax.tree.map(lambda a: lax.all_gather(a, axis), part)
    state = jax.tree.map(lambda a, e: jnp.zeros_like(a) + jnp.asarray(e, a.dtype), part, identity)

    def one(lap, state):
        return combine(
            state, jax.tree.map(lambda a: lax.dynamic_index_in_dim(a, lap, 0, False), gathered)
        )

    return lax.fori_loop(0, place, one, state)


def from_root(shard, axis, root):
    mine = lax.axis_index(axis) == root
    return lax.psum(jnp.where(mine, shard, jnp.zeros_like(shard)), axis)


def unit_rows(matrix):
    return matrix / jnp.sqrt(jnp.sum(matrix * matrix, axis=-1, keepdims=True) + epsilon)


def chain_pair(earlier, later_pair):
    joined = jnp.einsum("...ij,...jk->...ik", later_pair[0], earlier[0], precision=highest)
    carried = (
        jnp.einsum("...ij,...jk->...ik", later_pair[0], earlier[1], precision=highest)
        + later_pair[1]
    )
    return (joined, carried)


def causal_filter(signal, rim_rows, weights):
    kernel = weights.shape[0]
    length = signal.shape[0]
    padded = jnp.concatenate([rim_rows, signal], axis=0)
    running = weights[0] * padded[0:length]
    for offset in range(1, kernel):
        running = running + weights[offset] * padded[offset : offset + length]
    return jax.nn.silu(running)


def on_device(
    query_in,
    key_in,
    value_in,
    gate_in,
    write_strength,
    log_decay,
    doc_resets,
    conv_weight,
    output_norm_gain,
    output_projection_weight,
):
    length, head_count, depth_k = query_in.shape
    value_width = value_in.shape[2]
    kernel = conv_weight.shape[1]
    tail_rows = jnp.stack(
        [
            query_in[length - kernel + 1 :],
            key_in[length - kernel + 1 :],
            value_in[length - kernel + 1 :],
        ]
    )
    rim_rows = from_behind(tail_rows, ("chain", "leaf"), 1)
    query_conv = causal_filter(query_in, rim_rows[0], conv_weight[0])
    key_conv = causal_filter(key_in, rim_rows[1], conv_weight[1])
    value_conv = causal_filter(value_in, rim_rows[2], conv_weight[2])
    query_unit = (unit_rows(query_conv) * depth_k ** (-0.5)).astype(jnp.bfloat16)
    key_unit = unit_rows(key_conv).astype(jnp.bfloat16)
    value_act = value_conv.astype(jnp.bfloat16)
    blocks = length // BLOCK
    query_blk = query_unit.reshape(blocks, BLOCK, head_count, depth_k)
    key_blk = key_unit.reshape(blocks, BLOCK, head_count, depth_k)
    value_blk = value_act.reshape(blocks, BLOCK, head_count, value_width)
    key_gram = jnp.einsum("nthe,nshe->nhts", key_blk, key_blk, preferred_element_type=jnp.float32)
    query_gram = jnp.einsum(
        "nthe,nshe->nhts", query_blk, key_blk, preferred_element_type=jnp.float32
    )
    strength = write_strength.reshape(head_count, blocks, BLOCK).transpose(1, 0, 2)
    decays = log_decay.reshape(head_count, blocks, BLOCK).transpose(1, 0, 2)
    row_index = lax.broadcasted_iota(jnp.int32, (BLOCK, BLOCK), 0)
    col_index = lax.broadcasted_iota(jnp.int32, (BLOCK, BLOCK), 1)
    strict_mask = row_index > col_index
    causal_mask = row_index >= col_index
    cumulative = jnp.cumsum(decays, axis=-1)
    spread_log = cumulative[..., :, None] - cumulative[..., None, :]
    fading = jnp.where(causal_mask, jnp.exp(jnp.where(causal_mask, spread_log, 0.0)), 0.0)
    growth = jnp.exp(cumulative)
    lower = jnp.where(strict_mask, strength[..., :, None] * fading * key_gram, 0.0)
    mixing = fading * query_gram
    query_float = jnp.transpose(query_blk, (0, 2, 1, 3)).astype(jnp.float32)
    key_float = jnp.transpose(key_blk, (0, 2, 1, 3)).astype(jnp.float32)
    value_float = jnp.transpose(value_blk, (0, 2, 1, 3)).astype(jnp.float32)
    targets = jnp.concatenate(
        [strength[..., None] * value_float, (strength * growth)[..., None] * key_float], axis=-1
    )
    solved = jax.scipy.linalg.solve_triangular(
        jnp.eye(BLOCK, dtype=jnp.float32) + lower, targets, lower=True, unit_diagonal=True
    )
    local_values = solved[..., :value_width]
    write_keys = solved[..., value_width:]
    tail_fade = jnp.exp(cumulative[..., -1:] - cumulative)
    decayed_addresses = tail_fade[..., None] * key_float
    key_eye = jnp.eye(depth_k, dtype=jnp.float32)
    keep_mat = (1 - doc_resets).astype(jnp.float32)[:, None, None, None]
    transition = keep_mat * (
        growth[..., -1, None, None] * key_eye
        - jnp.einsum("nhce,nhcf->nhef", decayed_addresses, write_keys, precision=highest)
    )
    addition = jnp.einsum("nhce,nhcf->nhef", decayed_addresses, local_values, precision=highest)
    query_eff = keep_mat * (
        growth[..., None] * query_float
        - jnp.einsum("nhts,nhse->nhte", mixing, write_keys, precision=highest)
    )
    own_output = jnp.einsum("nhts,nhsf->nhtf", mixing, local_values, precision=highest)
    prefix_trans, prefix_state = lax.associative_scan(chain_pair, (transition, addition), axis=0)
    start_trans = jnp.concatenate(
        [jnp.broadcast_to(key_eye, (1, head_count, depth_k, depth_k)), prefix_trans[:-1]], axis=0
    )
    start_state = jnp.concatenate(
        [jnp.zeros((1, head_count, depth_k, value_width), jnp.float32), prefix_state[:-1]], axis=0
    )
    device_trans = prefix_trans[-1]
    device_state = prefix_state[-1]
    partial_out = own_output + jnp.einsum(
        "nhtd,nhdf->nhtf", query_eff, start_state, precision=highest
    )
    reach_map = jnp.einsum("nhtd,nhde->nhte", query_eff, start_trans, precision=highest)
    identity_pair = (
        jnp.broadcast_to(key_eye, (head_count, depth_k, depth_k)),
        jnp.zeros((head_count, depth_k, value_width), jnp.float32),
    )
    leaf_trans, leaf_state = prefix((device_trans, device_state), "leaf", chain_pair, identity_pair)
    through = chain_pair((leaf_trans, leaf_state), (device_trans, device_state))
    group_pair = from_root(jnp.stack(through), "leaf", lax.axis_size("leaf") - 1)
    outer_trans, outer_state = prefix(
        (group_pair[0], group_pair[1]), "chain", chain_pair, identity_pair
    )
    incoming = jnp.einsum("hij,hjk->hik", leaf_trans, outer_state, precision=highest) + leaf_state
    core = partial_out + jnp.einsum("nhte,hef->nhtf", reach_map, incoming, precision=highest)
    core = jnp.transpose(core, (0, 2, 1, 3)).reshape(length, head_count, value_width)
    scale_rms = jnp.sqrt(jnp.mean(core * core, axis=-1, keepdims=True) + epsilon)
    normed = (
        core / scale_rms * output_norm_gain * jax.nn.silu(gate_in.astype(jnp.float32))
    ).astype(jnp.bfloat16)
    shard_piece = lax.all_gather(normed, "head", axis=1, tiled=True)
    count = shard_piece.shape[1]
    flat_piece = shard_piece.reshape(shard_piece.shape[0], count * value_width)
    mixed = jnp.dot(flat_piece, output_projection_weight, preferred_element_type=jnp.float32)
    return mixed.astype(jnp.bfloat16)


def solution(mesh):
    return jax.shard_map(
        on_device,
        mesh=mesh,
        in_specs=(
            P(("chain", "leaf"), "head", None),
            P(("chain", "leaf"), "head", None),
            P(("chain", "leaf"), "head", None),
            P(("chain", "leaf"), "head", None),
            P("head", ("chain", "leaf")),
            P("head", ("chain", "leaf")),
            P(("chain", "leaf")),
            P(None, None, "head", None),
            P(),
            P(None, "head"),
        ),
        out_specs=P(("chain", "leaf"), "head"),
        check_vma=False,
    )
```

profile of v0, /device:TPU:0, one launch (start us, length us, event | category | flops | bytes accessed | tf_op | source)
XLA Modules:
  0.0 423.4 jit_solution(13381261487751908808)
XLA Ops:
  9.9 4.8 %collective-permute-start = (bf16[3,3,4,128]{3,1,2,0:T(4,128)(2,1)S(1)}, bf16[3,3,4,128]{3,1,2,0:T(4,128)(2,1)S(1)}, u32[]{:S(2)}, u32[]{:S(2)}) collective-permute-start(bf16[3,3,4,128]{3,1,2,0:T(4,128)(2,1)S(1)} %pad_maximum_fusion.7), channel_id=1, source_target_pairs={{0,4},{4,8},{8,12},{12,16},{16,20},{20,24},{24,28},{1,5},{5,9},{9,... | collective-permute-start | bytes 27656 | tf_op jit(solution)/shard_map/ppermute | solution.py:16
  20.1 158.1 %custom-call.4 = f32[8,4,1,64,64]{3,4,2,1,0:T(8,128)S(1)} custom-call(f32[8,4,1,64,64]{4,3,2,1,0:T(8,128)} %fusion.34), custom_call_target="InvertDiagBlocksLowerTriangular" | custom-call | tf_op jit(solution)/shard_map/jit(_solve_triangular)/vmap(vmap())/triangular_solve | solution.py:115
  180.9 3.8 fusion.44
  184.7 4.1 subtract_multiply_fusion
  196.8 3.5 pad.41
  200.3 3.6 pad.42
  205.5 6.3 %pad.185 = f32[7,4,128,128]{3,2,1,0:T(8,128)} pad(f32[4,4,128,128]{3,2,1,0:T(8,128)S(1)} %add.203, f32[]{:T(128)} %constant.55.clone.1), padding=0_0_1x0_0_0x0_0_0x0_0_0 | pad | bytes 2883588
  215.3 5.7 %pad.47 = f32[4,4,128,128]{3,2,1,0:T(8,128)} pad(f32[2,4,128,128]{3,2,1,0:T(8,128)} %pad_maximum_fusion.6, f32[]{:T(128)} %constant.55.clone.1), padding=0_1_1x0_0_0x0_0_0x0_0_0 | pad | bytes 1572868 | tf_op jit(solution)/shard_map/pad | solution.py:134
  221.0 5.7 %pad.48 = f32[4,4,128,128]{3,2,1,0:T(8,128)} pad(f32[2,4,128,128]{3,2,1,0:T(8,128)} %pad_add_fusion, f32[]{:T(128)} %constant.55.clone.1), padding=1_0_1x0_0_0x0_0_0x0_0_0 | pad | bytes 1572868 | tf_op jit(solution)/shard_map/pad | solution.py:134
  226.8 2.7 add.209
  229.4 10.1 %pad.50 = f32[8,4,128,128]{3,2,1,0:T(8,128)} pad(f32[4,4,128,128]{3,2,1,0:T(8,128)} %add.209, f32[]{:T(128)} %constant.55.clone.1), padding=1_0_1x0_0_0x0_0_0x0_0_0 | pad | bytes 3145732 | tf_op jit(solution)/shard_map/pad | solution.py:134
  239.6 2.3 fusion.57
  242.9 10.1 %pad.49 = f32[8,4,128,128]{3,2,1,0:T(8,128)} pad(f32[4,4,128,128]{3,2,1,0:T(8,128)} %pad_maximum_fusion.1, f32[]{:T(128)} %constant.55.clone.1), padding=0_1_1x0_0_0x0_0_0x0_0_0 | pad | bytes 3145732 | tf_op jit(solution)/shard_map/pad | solution.py:134
  253.1 3.7 multiply_reduce_fusion.2
  258.5 3.5 convolution_add_fusion.3
  264.3 6.4 %pad.44 = f32[8,4,128,128]{3,2,1,0:T(8,128)} pad(f32[4,4,128,128]{3,2,1,0:T(8,128)S(1)} %add.203, f32[]{:T(128)} %constant.55.clone.1), padding=1_0_1x0_0_0x0_0_0x0_0_0 | pad | bytes 3145732 | tf_op jit(solution)/shard_map/pad | solution.py:134
  270.7 6.2 %pad.84 = f32[7,4,128,128]{3,2,1,0:T(8,128)} pad(f32[4,4,128,128]{3,2,1,0:T(8,128)S(1)} %copy-done.3, f32[]{:T(128)} %constant.55.clone.1), padding=0_0_1x0_0_0x0_0_0x0_0_0 | pad | bytes 2883588 | tf_op jit(solution)/shard_map/slice | solution.py:136
  277.0 6.4 %pad.43 = f32[8,4,128,128]{3,2,1,0:T(8,128)} pad(f32[4,4,128,128]{3,2,1,0:T(8,128)S(1)} %copy-done.15, f32[]{:T(128)} %constant.55.clone.1), padding=0_1_1x0_0_0x0_0_0x0_0_0 | pad | bytes 3145732 | tf_op jit(solution)/shard_map/pad | solution.py:134
  294.2 4.6 %fusion.14 = f32[8,4,64,128]{3,2,1,0:T(8,128)} fusion(f32[8,4,64,128]{3,2,1,0:T(8,128)S(1)} %fusion.29, f32[7,4,128,128]{3,2,1,0:T(8,128)} %slice_add_fusion.2, f32[1,4,128,128]{3,2,1,0:T(8,128)S(1)} %broadcast_in_dim.49), kind=kOutput, calls=%fused_computation.16 | convolution fusion | flops 403177472 | bytes 4194304 | tf_op jit(solution)/shard_map/nhtd,nhde->nhte/dot_general | solution.py:146
  300.2 48.7 %all-reduce.15.cloned.1.call-done = f32[2,4,128,128]{3,2,1,0:T(8,128)} async-done(((f32[2,4,128,128]{3,2,1,0:T(8,128)}), f32[2,4,128,128]{3,2,1,0:T(8,128)}) %all-reduce.15.cloned.1.call-update) | async-done | bytes 524304 | tf_op jit(solution)/shard_map/psum | solution.py:34
  354.8 2.4 convolution_bitcast_fusion
  361.7 46.3 %all-gather.8.cloned.1.call-done = bf16[512,16,128]{2,0,1:T(8,128)(2,1)} async-done(((bf16[512,4,128]{2,0,1:T(8,128)(2,1)}), bf16[512,16,128]{2,0,1:T(8,128)(2,1)}) %all-gather.8.cloned.1.call-update) | async-done | bytes 2097168 | tf_op jit(solution)/shard_map/all_gather | solution.py:164
  408.0 2.9 copy.174
  410.9 5.5 %convolution_convert_fusion = bf16[512,1024]{1,0:T(8,128)(2,1)} fusion(bf16[512,2048]{0,1:T(8,128)(2,1)S(1)} %bitcast.170, bf16[2048,1024]{1,0:T(8,128)(2,1)} %param.23), kind=kOutput, calls=%fused_computation.24 | convolution fusion | flops 2148007936 | bytes 7340032 | tf_op jit(solution)/shard_map/dot_general | solution.py:167
  (145 shorter events, 51.8 us)
Async XLA Ops:
  6.5 3.2 copy-start.19
  6.5 8.2 %copy-start.24 = (s32[8]{0:T(128)S(1)}, s32[8]{0:T(128)}, u32[]{:S(2)}) copy-start(s32[8]{0:T(128)} %param.20) | copy-start | bytes 100
  6.5 8.3 %copy-start.21 = (f32[4,512]{1,0:T(4,128)S(1)}, f32[4,512]{1,0:T(4,128)}, u32[]{:S(2)}) copy-start(f32[4,512]{1,0:T(4,128)} %param.18) | copy-start | bytes 24580
  6.5 8.4 %copy-start.22 = (f32[4,512]{1,0:T(4,128)S(1)}, f32[4,512]{1,0:T(4,128)}, u32[]{:S(2)}) copy-start(f32[4,512]{1,0:T(4,128)} %param.19) | copy-start | bytes 24580
  6.5 9.5 %copy-start.20 = (f32[3,4,4,128]{3,2,1,0:T(4,128)S(1)}, f32[3,4,4,128]{3,2,1,0:T(4,128)}, u32[]{:S(2)}) copy-start(f32[3,4,4,128]{3,2,1,0:T(4,128)} %param.21) | copy-start | bytes 73732
  6.5 283.6 %all-gather.6.cloned.1.call-start = ((), (), s32[]{:S(2)}) async-start(), calls=%async_computation.1 | async-start | bytes 1310720 | tf_op jit(solution)/shard_map/all_gather | solution.py:21
  9.9 6.6 %collective-permute-start = (bf16[3,3,4,128]{3,1,2,0:T(4,128)(2,1)S(1)}, bf16[3,3,4,128]{3,1,2,0:T(4,128)(2,1)S(1)}, u32[]{:S(2)}, u32[]{:S(2)}) collective-permute-start(bf16[3,3,4,128]{3,1,2,0:T(4,128)(2,1)S(1)} %pad_maximum_fusion.7), channel_id=1, source_target_pairs={{0,4},{4,8},{8,12},{12,16},{16,20},{20,24},{24,28},{1,5},{5,9},{9,... | collective-permute-start | bytes 27656 | tf_op jit(solution)/shard_map/ppermute | solution.py:16
  18.5 166.2 %copy-start.4 = (bf16[512,4,128]{2,0,1:T(8,128)(2,1)}, bf16[512,4,128]{2,0,1:T(8,128)(2,1)S(1)}, u32[]{:S(2)}) copy-start(bf16[512,4,128]{2,0,1:T(8,128)(2,1)S(1)} %divide_convert_fusion) | copy-start | bytes 1572868
  180.9 7.9 %copy-start = (f32[8,4,64,256]{3,2,1,0:T(8,128)}, f32[8,4,64,256]{3,2,1,0:T(8,128)S(1)}, u32[]{:S(2)}) copy-start(f32[8,4,64,256]{3,2,1,0:T(8,128)S(1)} %fusion.10) | copy-start | bytes 6291460
  184.7 9.3 %copy-start.6 = (f32[8,4,128,128]{3,2,1,0:T(8,128)}, f32[8,4,128,128]{3,2,1,0:T(8,128)S(1)}, u32[]{:S(2)}) copy-start(f32[8,4,128,128]{3,2,1,0:T(8,128)S(1)} %fusion.44) | copy-start | bytes 6291460
  190.7 5.6 %copy-start.2 = (f32[4,4,128,128]{3,2,1,0:T(8,128)}, f32[4,4,128,128]{3,2,1,0:T(8,128)S(1)}, u32[]{:S(2)}) copy-start(f32[4,4,128,128]{3,2,1,0:T(8,128)S(1)} %fusion.46) | copy-start | bytes 3145732
  205.5 8.0 %slice-start = ((f32[4,4,128,128]{3,2,1,0:T(8,128)}), f32[1,4,128,128]{3,2,1,0:T(8,128)S(1)}, s32[]{:S(2)}) async-start(f32[4,4,128,128]{3,2,1,0:T(8,128)} %copy-done.2), calls=%async_computation.4 | async-start | bytes 524288 | tf_op jit(solution)/shard_map/slice | solution.py:134
  213.5 77.0 %all-gather.4.cloned.1.call-start = ((), (), s32[]{:S(2)}) async-start(), calls=%async_computation | async-start | bytes 1310720 | tf_op jit(solution)/shard_map/all_gather | solution.py:21
  258.5 3.5 slice-start.1
  262.0 86.9 %all-reduce.15.cloned.1.call-start = ((), (), s32[]{:S(2)}) async-start(), calls=%async_computation.2 | async-start | bytes 1048576 | tf_op jit(solution)/shard_map/psum | solution.py:34
  264.3 6.4 %copy-start.3 = (f32[4,4,128,128]{3,2,1,0:T(8,128)S(1)}, f32[4,4,128,128]{3,2,1,0:T(8,128)}, u32[]{:S(2)}) copy-start(f32[4,4,128,128]{3,2,1,0:T(8,128)} %pad_maximum_fusion.1) | copy-start | bytes 3145732
  270.7 6.2 %copy-start.15 = (f32[4,4,128,128]{3,2,1,0:T(8,128)S(1)}, f32[4,4,128,128]{3,2,1,0:T(8,128)}, u32[]{:S(2)}) copy-start(f32[4,4,128,128]{3,2,1,0:T(8,128)} %pad_maximum_fusion) | copy-start | bytes 3145732
  277.0 6.4 %copy-start.12 = (f32[512,4,128]{2,0,1:T(8,128)S(1)}, f32[512,4,128]{2,0,1:T(8,128)}, u32[]{:S(2)}) copy-start(f32[512,4,128]{2,0,1:T(8,128)} %get-tuple-element.109) | copy-start | bytes 3145732
  277.0 6.8 %copy-start.5 = (bf16[512,4,128]{2,0,1:T(8,128)(2,1)S(1)}, bf16[512,4,128]{2,0,1:T(8,128)(2,1)}, u32[]{:S(2)}) copy-start(bf16[512,4,128]{2,0,1:T(8,128)(2,1)} %copy-done.4) | copy-start | bytes 1572868
  285.0 3.6 copy-start.10
  294.1 113.9 %all-gather.8.cloned.1.call-start = ((), (), s32[]{:S(2)}) async-start(), calls=%async_computation.3 | async-start | bytes 2621440 | tf_op jit(solution)/shard_map/all_gather | solution.py:164
  294.1 4.6 %copy-start.8 = (f32[8,4,128,128]{3,2,1,0:T(8,128)S(1)}, f32[8,4,128,128]{3,2,1,0:T(8,128)}, u32[]{:S(2)}) copy-start(f32[8,4,128,128]{3,2,1,0:T(8,128)} %pad.44) | copy-start | bytes 6291460
  294.2 4.6 %copy-start.9 = (f32[8,4,128,128]{3,2,1,0:T(8,128)S(1)}, f32[8,4,128,128]{3,2,1,0:T(8,128)}, u32[]{:S(2)}) copy-start(f32[8,4,128,128]{3,2,1,0:T(8,128)} %pad.43) | copy-start | bytes 6291460
  354.4 2.9 copy-start.11
  (8 other events, 12.3 us)
Sparse Core Ops, SparseCore 0:
  213.6 28.3 all-gather.5
  262.1 28.3 all-gather.3
  294.2 54.6 all-reduce.14
  361.8 46.1 all-gather.7
where the time goes:
time: 429 us; the launch traced here: 423 us
  other arithmetic  183 us (43%)
  waiting for transfers between devices  95.4 us (22%)
  local copies, waits for them, and re-layouts  76.9 us (18%)
  matrix products  44.1 us (10%)
  between operations  14.2 us (3%)
  starting transfers between devices  5.01 us (1%)
  blocking collectives  4.35 us (1%)
    another operation x3, other arithmetic, on_device(): jax.scipy.linalg.solve_triangular(jnp.eye(BLOCK, dtype=jnp.float32) + low...  158 us
    pad x8, local copies, waits for them, and re-layouts, on_device(): lax.associative_scan(chain_pair, (transition, addition), axis=0)  51.5 us
    psum x1, waiting for transfers between devices, from_root(): return lax.psum(jnp.where(mine, shard, jnp.zeros_like(shard)), axis)  48.7 us
    all_gather x1, waiting for transfers between devices, on_device(): shard_piece = lax.all_gather(normed, 'head', axis=1, tiled=True)  46.3 us
    unnamed x54, local copies, waits for them, and re-layouts  12 us
    add x7, other arithmetic, on_device(): lax.associative_scan(chain_pair, (transition, addition), axis=0)  9.89 us
  transfers between devices with their start and end apart: 5, of which 3 were waited for; matrix products, arithmetic and copies ran while one was open for 20% of the time, Pallas kernels for 0%

commit v1 on v0

v1 whole, which is shorter than its diff:
```python
import functools

import jax
import jax.numpy as jnp
from jax import lax
from jax.experimental import pallas as pl
from jax.experimental.pallas import tpu as pltpu
from jax.sharding import PartitionSpec as P

BLOCK = 64
CHUNK = 128
EPSILON = 1e-06
FAR = -1e30
F32 = jnp.float32
BF16 = jnp.bfloat16
NN = (((1,), (0,)), ((), ()))
NT = (((1,), (1,)), ((), ()))
TN = (((0,), (0,)), ((), ()))


def split(a):
    high = a.astype(BF16)
    return high, (a - high.astype(F32)).astype(BF16)


def mul(a, b, dims=NN):
    return lax.dot_general(a, b, dims, preferred_element_type=F32)


def mul_one(a, b):
    return mul(a.astype(BF16), b.astype(BF16))


def mul_split(a, b):
    a_high, a_low = split(a)
    b_high, b_low = split(b)
    return mul(a_high, b_high) + (mul(a_low, b_high) + mul(a_high, b_low))


def indices():
    shape = (CHUNK, CHUNK)
    return (
        lax.broadcasted_iota(jnp.int32, shape, 0),
        lax.broadcasted_iota(jnp.int32, shape, 1),
    )


def running_decay(row_scalars, chunks):
    row, col = indices()
    upto = (row <= col).astype(F32)
    return lax.dot_general(
        row_scalars[:chunks], upto, NN, precision=lax.Precision.HIGHEST, preferred_element_type=F32
    )


def convolve(x_ref, rim_ref, taps_ref, which, head, padded, store):
    length = x_ref.shape[1]
    padded[0:8] = rim_ref[which, head]
    padded[8 : 8 + length] = x_ref[head].astype(F32)
    taps = taps_ref[which, head]
    count = taps.shape[0]
    for c in range(length // CHUNK):
        begin = c * CHUNK + 9 - count
        total = taps[0:1] * padded[begin : begin + CHUNK]
        for j in range(1, count):
            total = total + taps[j : j + 1] * padded[begin + j : begin + j + CHUNK]
        store(c, total / (1.0 + jnp.exp(-total)))


def unit(rows):
    return rows * lax.rsqrt(jnp.sum(rows * rows, axis=-1, keepdims=True) + EPSILON)


def fading_of(cum_col, cum_row, second_resets, row, col):
    apart = ((row // BLOCK) != (col // BLOCK)).astype(jnp.int32) * second_resets
    mask = (row >= col) & (apart == 0)
    return jnp.exp(jnp.where(mask, cum_col - cum_row, FAR))


def lower_inverse(lowers, row, col):
    differ = row ^ col
    eye = (row == col).astype(F32)
    diagonal = [jnp.where(differ < 8, low, 0.0) for low in lowers]
    powers = [d.astype(BF16) for d in diagonal]
    squares = [mul(p, p).astype(BF16) for p in powers]
    inverse = [eye - d for d in diagonal]
    fourths = [mul(s, s).astype(BF16) for s in squares]
    inverse = [x + mul(x.astype(BF16), s) for x, s in zip(inverse, squares)]
    inverse = [x + mul(x.astype(BF16), s) for x, s in zip(inverse, fourths)]
    size = 8
    while size < CHUNK:
        joint = (differ >= size) & (differ < 2 * size)
        rounded = [x.astype(BF16) for x in inverse]
        inner = [
            mul(jnp.where(joint, low, 0.0).astype(BF16), x) for low, x in zip(lowers, rounded)
        ]
        inverse = [
            x - mul(r, i.astype(BF16)) for x, r, i in zip(inverse, rounded, inner)
        ]
        size *= 2
    return inverse


def maps_kernel(
    resets, key_ref, value_ref, rim_ref, taps_ref, scalars_ref,
    unit_ref, solved_ref, starts_ref, map_ref,
    padded, value_s, step_s,
):
    heads, length, depth = key_ref.shape
    chunks = length // CHUNK
    row, col = indices()

    def filters(h, carry):
        def store_key(c, rows):
            unit_ref[h, c * CHUNK : (c + 1) * CHUNK] = unit(rows).astype(BF16)

        def store_value(c, rows):
            value_s[h, c * CHUNK : (c + 1) * CHUNK] = rows.astype(BF16)

        convolve(key_ref, rim_ref, taps_ref, 1, h, padded, store_key)
        convolve(value_ref, rim_ref, taps_ref, 2, h, padded, store_value)
        return carry

    lax.fori_loop(0, heads, filters, 0)

    together = 2

    def solve(p, carry):
        parts = []
        lowers = []
        for k in range(together):
            h = p * together + k
            scalars = scalars_ref[h]
            cum = running_decay(scalars, chunks)
            columns = jnp.transpose(jnp.concatenate([cum, scalars[chunks:]], axis=0))
            for c in range(chunks):
                first, second = resets[2 * c], resets[2 * c + 1]
                cum_col = columns[:, c : c + 1]
                strength = columns[:, chunks + c : chunks + c + 1]
                cum_row = cum[c : c + 1]
                key = unit_ref[h, c * CHUNK : (c + 1) * CHUNK]
                gram = mul(key, key, NT)
                fading = fading_of(cum_col, cum_row, second, row, col)
                lowers.append(jnp.where(row > col, strength * fading * gram, 0.0))
                parts.append((h, c, first, second, cum_col, cum_row, scalars[chunks + c : chunks + c + 1]))
        inverses = lower_inverse(lowers, row, col)
        for (h, c, first, second, cum_col, cum_row, strength_row), inverse in zip(parts, inverses):
            keep_first = (1 - first).astype(F32)
            keep_second = (1 - second).astype(F32)
            keep_both = keep_first * keep_second
            key = unit_ref[h, c * CHUNK : (c + 1) * CHUNK]
            value = value_s[h, c * CHUNK : (c + 1) * CHUNK]
            in_first = lax.broadcasted_iota(jnp.int32, (1, CHUNK), 1) < BLOCK
            growth_row = jnp.exp(cum_row) * jnp.where(in_first, keep_first, keep_both)
            by_strength = inverse * strength_row
            high, low = split(by_strength * growth_row)
            write_keys = mul(high, key) + mul(low, key)
            high, low = split(by_strength)
            local_values = mul(high, value) + mul(low, value)
            solved = jnp.concatenate([write_keys, local_values], axis=1)
            solved_ref[h, c * CHUNK : (c + 1) * CHUNK] = solved
            end = cum_row[:, CHUNK - 1 : CHUNK]
            first_rows = lax.broadcasted_iota(jnp.int32, (CHUNK, 1), 0) < BLOCK
            tail = jnp.exp(end - cum_col) * jnp.where(first_rows, keep_second, 1.0)
            high, low = split(tail * solved)
            product = mul(key, high, TN) + mul(key, low, TN)
            passed = jnp.exp(end) * keep_both
            step_s[h, c, :, :depth] = jnp.where(row == col, passed, 0.0) - product[:, :depth]
            step_s[h, c, :, depth:] = product[:, depth:]
        return carry

    lax.fori_loop(0, heads // together, solve, 0)

    states = [step_s[h, 0] for h in range(heads)]
    for c in range(1, chunks):
        for h in range(heads):
            starts_ref[h, c - 1] = states[h]
            step = step_s[h, c]
            joined = mul_split(step[:, :depth], states[h])
            states[h] = jnp.concatenate(
                [joined[:, :depth], joined[:, depth:] + step[:, depth:]], axis=1
            )
    for h in range(heads):
        map_ref[h] = states[h].astype(BF16)


def reads_kernel(
    resets, query_ref, gate_ref, gain_ref, rim_ref, taps_ref, scalars_ref,
    unit_ref, solved_ref, starts_ref,
    reach_ref, part_ref, gating_ref,
    padded, query_s,
):
    heads, length, depth = query_ref.shape
    chunks = length // CHUNK
    row, col = indices()

    def one_head(h, carry):
        def store_query(c, rows):
            query_s[c * CHUNK : (c + 1) * CHUNK] = (unit(rows) * depth**-0.5).astype(BF16)

        convolve(query_ref, rim_ref, taps_ref, 0, h, padded, store_query)
        scalars = scalars_ref[h]
        cum = running_decay(scalars, chunks)
        columns = jnp.transpose(jnp.concatenate([cum, scalars[chunks:]], axis=0))
        for c in range(chunks):
            here = slice(c * CHUNK, (c + 1) * CHUNK)
            first, second = resets[2 * c], resets[2 * c + 1]
            keep_first = (1 - first).astype(F32)
            keep_both = keep_first * (1 - second).astype(F32)
            cum_col = columns[:, c : c + 1]
            query = query_s[here]
            gram = mul(query, unit_ref[h, here], NT)
            mixing = fading_of(cum_col, cum[c : c + 1], second, row, col) * gram
            own = mul_split(mixing, solved_ref[h, here])
            first_rows = lax.broadcasted_iota(jnp.int32, (CHUNK, 1), 0) < BLOCK
            growth = jnp.exp(cum_col) * jnp.where(first_rows, keep_first, keep_both)
            reach = growth * query.astype(F32) - own[:, :depth]
            part = own[:, depth:]
            if c:
                both = mul_split(reach, starts_ref[h, c - 1])
                reach = both[:, :depth]
                part = part + both[:, depth:]
            reach_ref[h, here] = reach
            part_ref[h, here] = part
            gate = gate_ref[h, here].astype(F32)
            gating_ref[h, here] = gain_ref[...] * (gate / (1.0 + jnp.exp(-gate)))
        return carry

    lax.fori_loop(0, heads, one_head, 0)


def join_kernel(place, count, *refs):
    maps = refs[:count]
    before_ref, whole_ref, ordered = refs[count:]
    heads, depth, _ = before_ref.shape
    me = place[0]
    for k in range(count):
        ordered[partner(me, k, count)] = maps[k][...]
    row, col = indices()
    eye = (row == col).astype(F32)
    states = [jnp.concatenate([eye, jnp.zeros((depth, depth), F32)], axis=1)] * heads
    for lap in range(count):

        @pl.when(lap == me)
        def _():
            for h in range(heads):
                before_ref[h] = states[h]

        for h in range(heads):
            step = ordered[lap, h]
            if lap:
                high, low = split(states[h])
                trans = step[:, :depth]
                joined = mul(trans, high) + mul(trans, low)
                states[h] = jnp.concatenate(
                    [joined[:, :depth], joined[:, depth:] + step[:, depth:].astype(F32)], axis=1
                )
            else:
                states[h] = step.astype(F32)
    for h in range(heads):
        whole_ref[h] = states[h]


def outputs_kernel(arrived_ref, before_ref, reach_ref, part_ref, gating_ref, normed_ref):
    heads, length, depth = reach_ref.shape
    chunks = length // CHUNK
    for h in range(heads):
        before = before_ref[h]
        incoming = mul_split(before[:, :depth], arrived_ref[h].astype(F32)) + before[:, depth:]
        high, low = split(incoming)
        for c in range(chunks):
            here = slice(c * CHUNK, (c + 1) * CHUNK)
            reach_high, reach_low = split(reach_ref[h, here])
            core = part_ref[h, here] + (
                mul(reach_high, high) + (mul(reach_high, low) + mul(reach_low, high))
            )
            scale = lax.rsqrt(jnp.sum(core * core, axis=-1, keepdims=True) / depth + EPSILON)
            normed_ref[here, h * depth : (h + 1) * depth] = (
                core * scale * gating_ref[h, here]
            ).astype(BF16)


def partner(place, k, count):
    if count & (count - 1) == 0:
        return place ^ k
    return lax.rem(place + count - k, count)


def pairs_at(k, count):
    if count & (count - 1) == 0:
        return [(i, i ^ k) for i in range(count)]
    return [(i, (i + k) % count) for i in range(count)]


def from_behind(value, axis, steps):
    count = lax.axis_size(axis)
    return lax.ppermute(value, axis, [(i, i + steps) for i in range(count - steps)])


VMEM = pl.BlockSpec(memory_space=pltpu.VMEM)
SMEM = pl.BlockSpec(memory_space=pltpu.SMEM)
PARAMS = pltpu.CompilerParams(vmem_limit_bytes=48 * 1024 * 1024)


def on_device(
    query_in,
    key_in,
    value_in,
    gate_in,
    write_strength,
    log_decay,
    doc_resets,
    conv_weight,
    output_norm_gain,
    output_projection_weight,
):
    length, heads, depth = query_in.shape
    chunks = length // CHUNK
    taps = conv_weight.shape[1]
    tails = jnp.stack([x[length - taps + 1 :] for x in (query_in, key_in, value_in)])
    rims = from_behind(tails, ("chain", "leaf"), 1)
    rims = jnp.pad(
        jnp.transpose(rims, (0, 2, 1, 3)).astype(F32), ((0, 0), (0, 0), (9 - taps, 0), (0, 0))
    )
    query, key, value, gate = (
        jnp.transpose(x, (1, 0, 2)) for x in (query_in, key_in, value_in, gate_in)
    )
    taps_by_head = jnp.transpose(conv_weight, (0, 2, 1, 3))
    scalars = jnp.concatenate(
        [log_decay.reshape(heads, chunks, CHUNK), write_strength.reshape(heads, chunks, CHUNK)],
        axis=1,
    )
    per_token = jax.ShapeDtypeStruct((heads, length, depth), F32)
    unit_key, solved, starts, own_map = pl.pallas_call(
        maps_kernel,
        out_shape=(
            jax.ShapeDtypeStruct((heads, length, depth), BF16),
            jax.ShapeDtypeStruct((heads, length, 2 * depth), F32),
            jax.ShapeDtypeStruct((heads, chunks - 1, depth, 2 * depth), F32),
            jax.ShapeDtypeStruct((heads, depth, 2 * depth), BF16),
        ),
        in_specs=[SMEM] + [VMEM] * 5,
        out_specs=[VMEM] * 4,
        scratch_shapes=[
            pltpu.VMEM((length + 8, depth), F32),
            pltpu.VMEM((heads, length, depth), BF16),
            pltpu.VMEM((heads, chunks, depth, 2 * depth), F32),
        ],
        compiler_params=PARAMS,
    )(doc_resets, key, value, rims, taps_by_head, scalars)

    leaves = lax.axis_size("leaf")
    maps = [own_map] + [
        lax.ppermute(own_map, "leaf", pairs_at(k, leaves)) for k in range(1, leaves)
    ]
    reach, part, gating = pl.pallas_call(
        reads_kernel,
        out_shape=(per_token, per_token, per_token),
        in_specs=[SMEM] + [VMEM] * 9,
        out_specs=[VMEM] * 3,
        scratch_shapes=[
            pltpu.VMEM((length + 8, depth), F32),
            pltpu.VMEM((length, depth), BF16),
        ],
        compiler_params=PARAMS,
        cost_estimate=pl.CostEstimate(
            flops=6 * 10**9, bytes_accessed=8 * 2**20, transcendentals=10**6
        ),
    )(
        doc_resets, query, gate, output_norm_gain.reshape(1, depth), rims, taps_by_head, scalars,
        unit_key, solved, starts,
    )
    pair = jax.ShapeDtypeStruct((heads, depth, 2 * depth), F32)
    place = lax.axis_index("leaf").astype(jnp.int32).reshape(1)
    before, whole = pl.pallas_call(
        lambda place, *refs: join_kernel(place, leaves, *refs),
        out_shape=(pair, pair),
        in_specs=[SMEM] + [VMEM] * leaves,
        out_specs=[VMEM] * 2,
        scratch_shapes=[pltpu.VMEM((leaves, heads, depth, 2 * depth), BF16)],
        compiler_params=PARAMS,
    )(place, *maps)

    trans, state = whole[..., :depth], whole[..., depth:]
    arrived = from_behind(state.astype(BF16), "chain", 1)
    for _ in range(lax.axis_size("chain") - 2):
        passed = jnp.einsum(
            "hij,hjk->hik", trans, arrived.astype(F32), precision=lax.Precision.HIGHEST
        )
        arrived = from_behind((passed + state).astype(BF16), "chain", 1)

    normed = pl.pallas_call(
        outputs_kernel,
        out_shape=jax.ShapeDtypeStruct((length, heads * depth), BF16),
        in_specs=[VMEM] * 5,
        out_specs=VMEM,
        compiler_params=PARAMS,
    )(arrived, before, reach, part, gating)

    ring = lax.axis_size("head")
    mine = lax.axis_index("head")
    width = heads * depth
    weights = output_projection_weight
    mixed = None
    block = normed
    for k in range(ring):
        owner = lax.rem(mine + ring - k, ring)
        rows = lax.dynamic_slice_in_dim(weights, owner * width, width, 0)
        if k + 1 < ring:
            following = lax.ppermute(block, "head", [(i, (i + 1) % ring) for i in range(ring)])
        term = jnp.dot(block, rows, preferred_element_type=F32)
        mixed = term if mixed is None else mixed + term
        if k + 1 < ring:
            block = following
    return mixed.astype(BF16)


def solution(mesh):
    return jax.shard_map(
        on_device,
        mesh=mesh,
        in_specs=(
            P(("chain", "leaf"), "head", None),
            P(("chain", "leaf"), "head", None),
            P(("chain", "leaf"), "head", None),
            P(("chain", "leaf"), "head", None),
            P("head", ("chain", "leaf")),
            P("head", ("chain", "leaf")),
            P(("chain", "leaf")),
            P(None, None, "head", None),
            P(),
            P(None, "head"),
        ),
        out_specs=P(("chain", "leaf"), "head"),
        check_vma=False,
    )
```

time: 429 us -> 92.9 us (0.22); the launches traced: 423 us -> 92.7 us
  other arithmetic: 183 us -> 0.04 us
  local copies, waits for them, and re-layouts: 76.9 us -> 5.02 us
  waiting for transfers between devices: 95.4 us -> 49.4 us
  matrix products: 44.1 us -> 5.23 us
  Pallas kernels: 0 us -> 20.1 us
  between operations: 14.2 us -> 0.22 us
  starting transfers between devices: 5.01 us -> 12.7 us
  blocking collectives: 4.35 us -> 0 us
    another operation x5 -> x1, other arithmetic: 159 us -> 0.01 us  [on_device(): jnp.stack([x[length - taps + 1:] for x in (query_in, key_in, value_in)])]
    pad x8 -> x0, local copies, waits for them, and re-layouts: 51.5 us -> none  [on_device(): lax.associative_scan(chain_pair, (transition, addition), axis=0)]
    ppermute x1 -> x8, waiting for transfers between devices: 0.01 us -> 49.4 us  [the longest x3 37.3 us: on_device(): lax.ppermute(block, 'head', [(i, (i + 1) % ring) for i in range(ring)])]
    psum x1 -> x0, waiting for transfers between devices: 48.7 us -> none  [from_root(): return lax.psum(jnp.where(mine, shard, jnp.zeros_like(shard)), axis)]
    all_gather x3 -> x0, waiting for transfers between devices: 46.6 us -> none  [the longest x1 46.3 us: on_device(): shard_piece = lax.all_gather(normed, 'head', axis=1, tiled=True)]
    dot_general x23 -> x4, matrix products: 42.2 us -> 5.23 us  [on_device(): term = jnp.dot(block, rows, preferred_element_type=F32)]
    pallas_call x0 -> x4, Pallas kernels: none -> 20.1 us  [the longest x1 9.74 us: on_device(): pl.pallas_call(maps_kernel, out_shape=(jax.ShapeDtypeStruct((heads, lengt...]
    slice x13 -> x1, local copies, waits for them, and re-layouts: 9.97 us -> 0.02 us  [on_device(): trans, state = (whole[..., :depth], whole[..., depth:])]
  transfers between devices with their start and end apart: 5 -> 8, of which waited for: 3 -> 6; matrix products, arithmetic and copies ran while one was open for 20% -> 4% of each run, Pallas kernels for 0% -> 9%
where the time goes in v1:
time: 92.9 us; the launch traced here: 92.7 us
  waiting for transfers between devices  49.4 us (53%)
  Pallas kernels  20.1 us (22%)
  starting transfers between devices  12.7 us (14%)
  matrix products  5.23 us (6%)
  local copies, waits for them, and re-layouts  5.02 us (5%)
    ppermute x3, waiting for transfers between devices, on_device(): lax.ppermute(block, 'head', [(i, (i + 1) % ring) for i in range(ring)])  37.3 us
    ppermute x3, waiting for transfers between devices, on_device(): lax.ppermute(own_map, 'leaf', pairs_at(k, leaves))  10.7 us
    pallas_call x1, Pallas kernels, on_device(): pl.pallas_call(maps_kernel, out_shape=(jax.ShapeDtypeStruct((heads, lengt...  9.74 us
    pallas_call x1, Pallas kernels, on_device(): pl.pallas_call(reads_kernel, out_shape=(per_token, per_token, per_token),...  7.9 us
    ppermute x2, starting transfers between devices, from_behind(): lax.ppermute(value, axis, [(i, i + steps) for i in range(count - steps)])  6.42 us
    dot_general x4, matrix products, on_device(): term = jnp.dot(block, rows, preferred_element_type=F32)  5.23 us
    unnamed x25, local copies, waits for them, and re-layouts  4.95 us
    ppermute x3, starting transfers between devices, on_device(): lax.ppermute(own_map, 'leaf', pairs_at(k, leaves))  4.69 us
  transfers between devices with their start and end apart: 8, of which 6 were waited for; matrix products, arithmetic and copies ran while one was open for 4% of the time, Pallas kernels for 9%

profile of v1, /device:TPU:0, one launch (start us, length us, event | category | flops | bytes accessed | tf_op | source)
XLA Modules:
  0.0 92.7 jit_solution(6642612405695025318)
XLA Ops:
  0.0 1.2 %copy.29 = bf16[512,4,128]{2,0,1:T(8,128)(2,1)S(1)} copy(bf16[512,4,128]{2,1,0:T(4,128)(2,1)} %param.10) | data formatting | bytes 1048576 | tf_op args[0]
  1.2 1.1 %copy.30 = bf16[512,4,128]{2,0,1:T(8,128)(2,1)S(1)} copy(bf16[512,4,128]{2,1,0:T(4,128)(2,1)} %param.11) | data formatting | bytes 1048576 | tf_op args[1]
  2.5 4.9 %collective-permute-start = (bf16[3,3,4,128]{3,1,2,0:T(4,128)(2,1)S(1)}, bf16[3,3,4,128]{3,1,2,0:T(4,128)(2,1)S(1)}, u32[]{:S(2)}, u32[]{:S(2)}) collective-permute-start(bf16[3,3,4,128]{3,1,2,0:T(4,128)(2,1)S(1)} %pad_maximum_fusion.1), channel_id=1, source_target_pairs={{0,4},{4,8},{8,12},{12,16},{16,20},{20,24},{24,28},{1,5},{5,9},{9,... | collective-permute-start | bytes 27656 | tf_op jit(solution)/shard_map/ppermute | solution.py:297
  7.5 1.3 %collective-permute-done = bf16[3,3,4,128]{3,1,2,0:T(4,128)(2,1)S(1)} collective-permute-done((bf16[3,3,4,128]{3,1,2,0:T(4,128)(2,1)S(1)}, bf16[3,3,4,128]{3,1,2,0:T(4,128)(2,1)S(1)}, u32[]{:S(2)}, u32[]{:S(2)}) %collective-permute-start) | collective-permute-done | bytes 9248 | tf_op jit(solution)/shard_map/ppermute | solution.py:297
  8.8 9.7 %shard_map.100 = (bf16[4,512,128]{2,1,0:T(8,128)(2,1)S(1)}, f32[4,512,256]{2,1,0:T(8,128)S(1)}, f32[4,3,128,256]{3,2,1,0:T(8,128)S(1)}, bf16[4,128,256]{2,1,0:T(8,128)(2,1)S(1)}) custom-call(s32[8]{0:T(128)S(1)} %copy-done, bf16[4,512,128]{2,1,0:T(8,128)(2,1)S(1)} %bitcast.26, bf16[4,512,128]{2,1,0:T(8,128)(2,1)S(1)} %bitcast.27, ...), custom_call_target="tpu_custom_call" | custom-call | tf_op jit(solution)/shard_map/pallas_call | solution.py:334
  18.5 1.3 %copy-done.1 = f32[4,512,256]{2,1,0:T(8,128)} copy-done((f32[4,512,256]{2,1,0:T(8,128)}, f32[4,512,256]{2,1,0:T(8,128)S(1)}, u32[]{:S(2)}) %copy-start.1) | copy-done | bytes 2097176
  19.9 1.1 %copy-done.2 = f32[4,3,128,256]{3,2,1,0:T(8,128)} copy-done((f32[4,3,128,256]{3,2,1,0:T(8,128)}, f32[4,3,128,256]{3,2,1,0:T(8,128)S(1)}, u32[]{:S(2)}) %copy-start.2) | copy-done | bytes 1572888
  21.0 3.3 %collective-permute-start.3 = (bf16[4,128,256]{2,1,0:T(8,128)(2,1)S(1)}, bf16[4,128,256]{2,1,0:T(8,128)(2,1)S(1)}, u32[]{:S(2)}, u32[]{:S(2)}) collective-permute-start(bf16[4,128,256]{2,1,0:T(8,128)(2,1)S(1)} %get-tuple-element.14.refs_0_), channel_id=1, source_target_pairs={{0,12},{4,8},{8,4},{12,0},{1,13},{5,9},{9,5},{13,1},{2,14},{6,10},... | collective-permute-start | bytes 786440 | tf_op jit(solution)/shard_map/ppermute | solution.py:354
  24.2 0.5 collective-permute-start.2
  24.7 0.9 %collective-permute-start.1 = (bf16[4,128,256]{2,1,0:T(8,128)(2,1)S(1)}, bf16[4,128,256]{2,1,0:T(8,128)(2,1)S(1)}, u32[]{:S(2)}, u32[]{:S(2)}) collective-permute-start(bf16[4,128,256]{2,1,0:T(8,128)(2,1)S(1)} %get-tuple-element.14.refs_0_), channel_id=1, source_target_pairs={{0,4},{4,0},{8,12},{12,8},{1,5},{5,1},{9,13},{13,9},{2,6},{6,2},{1... | collective-permute-start | bytes 786440 | tf_op jit(solution)/shard_map/ppermute | solution.py:354
  25.8 5.7 %collective-permute-done.3.refs_3_ = bf16[4,128,256]{2,1,0:T(8,128)(2,1)S(1)} collective-permute-done((bf16[4,128,256]{2,1,0:T(8,128)(2,1)S(1)}, bf16[4,128,256]{2,1,0:T(8,128)(2,1)S(1)}, u32[]{:S(2)}, u32[]{:S(2)}) %collective-permute-start.3) | collective-permute-done | bytes 262176 | tf_op jit(solution)/shard_map/ppermute | solution.py:354
  31.4 5.0 %collective-permute-done.2.refs_2_ = bf16[4,128,256]{2,1,0:T(8,128)(2,1)S(1)} collective-permute-done((bf16[4,128,256]{2,1,0:T(8,128)(2,1)S(1)}, bf16[4,128,256]{2,1,0:T(8,128)(2,1)S(1)}, u32[]{:S(2)}, u32[]{:S(2)}) %collective-permute-start.2) | collective-permute-done | bytes 262176 | tf_op jit(solution)/shard_map/ppermute | solution.py:354
  36.5 1.0 %shard_map.101 = (f32[4,128,256]{2,1,0:T(8,128)S(1)}, f32[4,128,256]{2,1,0:T(8,128)S(1)}) custom-call(s32[1]{0:T(128)} %bitcast.place, bf16[4,128,256]{2,1,0:T(8,128)(2,1)S(1)} %get-tuple-element.14.refs_0_, bf16[4,128,256]{2,1,0:T(8,128)(2,1)S(1)} %collective-permute-done.1.refs_1_, bf16[4,128,256]{2,1,0:T(8,128)(2,1)S(1)} %collective-permute-done.2.refs_2_, ...), custom_call_target="tpu_custom_call" | custom-call | tf_op jit(solution)/shard_map/pallas_call | solution.py:375
  37.5 1.6 %collective-permute-start.4 = (bf16[4,128,128]{2,1,0:T(8,128)(2,1)S(1)}, bf16[4,128,128]{2,1,0:T(8,128)(2,1)S(1)}, u32[]{:S(2)}, u32[]{:S(2)}) collective-permute-start(bf16[4,128,128]{2,1,0:T(8,128)(2,1)S(1)} %slice.25), channel_id=1, source_target_pairs={{0,16},{1,17},{2,18},{3,19},{4,20},{5,21},{6,22},{7,23},{8,24},{9,... | collective-permute-start | bytes 393224 | tf_op jit(solution)/shard_map/ppermute | solution.py:297
  39.1 7.9 %shard_map.102 = (f32[4,512,128]{2,1,0:T(8,128)S(1)}, f32[4,512,128]{2,1,0:T(8,128)S(1)}, f32[4,512,128]{2,1,0:T(8,128)S(1)}) custom-call(s32[8]{0:T(128)S(1)} %copy-done, bf16[4,512,128]{2,1,0:T(8,128)(2,1)S(1)} %bitcast.28, bf16[4,512,128]{2,1,0:T(8,128)(2,1)S(1)} %bitcast.29, f32[1,128]{1,0:T(1,128)S(1)} %bitcast.32, ...), custom_call_target="tpu_custom_call" | custom-call | flops 6000000000 | bytes 8388608 | tf_op jit(solution)/shard_map/pallas_call | solution.py:356
  47.0 1.4 %shard_map.103 = bf16[512,512]{1,0:T(8,128)(2,1)S(1)} custom-call(bf16[4,128,128]{2,1,0:T(8,128)(2,1)S(1)} %collective-permute-done.4.arrived_ref, f32[4,128,256]{2,1,0:T(8,128)S(1)} %get-tuple-element.16.before_ref, f32[4,512,128]{2,1,0:T(8,128)S(1)} %get-tuple-element.20.reach_ref, f32[4,512,128]{2,1,0:T(8,128)S(1)} %get-tuple-element.21.part_ref, ...), custom_call_target="tpu_custom_call" | custom-call | tf_op jit(solution)/shard_map/pallas_call | solution.py:392
  48.5 1.6 %collective-permute-start.5 = (bf16[512,512]{1,0:T(8,128)(2,1)S(1)}, bf16[512,512]{1,0:T(8,128)(2,1)S(1)}, u32[]{:S(2)}, u32[]{:S(2)}) collective-permute-start(bf16[512,512]{1,0:T(8,128)(2,1)S(1)} %shard_map.103), channel_id=1, source_target_pairs={{0,1},{1,2},{2,3},{3,0},{4,5},{5,6},{6,7},{7,4},{8,9},{9,10},{10,1... | collective-permute-start | bytes 1572872 | tf_op jit(solution)/shard_map/ppermute | solution.py:410
  50.1 13.5 %collective-permute-done.5 = bf16[512,512]{1,0:T(8,128)(2,1)S(1)} collective-permute-done((bf16[512,512]{1,0:T(8,128)(2,1)S(1)}, bf16[512,512]{1,0:T(8,128)(2,1)S(1)}, u32[]{:S(2)}, u32[]{:S(2)}) %collective-permute-start.5) | collective-permute-done | bytes 524320 | tf_op jit(solution)/shard_map/ppermute | solution.py:410
  63.6 2.1 %fusion.5 = f32[512,1024]{1,0:T(8,128)S(1)} fusion(bf16[512,512]{1,0:T(8,128)(2,1)S(1)} %shard_map.103, bf16[2048,1024]{1,0:T(8,128)(2,1)} %param.19, s32[]{:T(128)S(6)} %select_n.12), kind=kOutput, calls=%fused_computation.6 | convolution fusion | flops 536870912 | bytes 3670020 | tf_op jit(solution)/shard_map/dot_general | solution.py:411
  65.7 12.1 %collective-permute-done.6 = bf16[512,512]{1,0:T(8,128)(2,1)S(1)} collective-permute-done((bf16[512,512]{1,0:T(8,128)(2,1)S(1)}, bf16[512,512]{1,0:T(8,128)(2,1)S(1)}, u32[]{:S(2)}, u32[]{:S(2)}) %collective-permute-start.6) | collective-permute-done | bytes 524320 | tf_op jit(solution)/shard_map/ppermute | solution.py:410
  77.8 0.7 fusion.3
  78.5 0.7 fusion.1
  79.2 11.8 %collective-permute-done.7 = bf16[512,512]{1,0:T(8,128)(2,1)S(1)} collective-permute-done((bf16[512,512]{1,0:T(8,128)(2,1)S(1)}, bf16[512,512]{1,0:T(8,128)(2,1)S(1)}, u32[]{:S(2)}, u32[]{:S(2)}) %collective-permute-start.7) | collective-permute-done | bytes 524320 | tf_op jit(solution)/shard_map/ppermute | solution.py:410
  91.0 1.7 %add_convert_fusion = bf16[512,1024]{1,0:T(8,128)(2,1)} fusion(f32[512,1024]{1,0:T(8,128)S(1)} %fusion.1, f32[512,1024]{1,0:T(8,128)S(1)} %fusion.5, f32[512,1024]{1,0:T(8,128)S(1)} %fusion.3, bf16[512,512]{1,0:T(8,128)(2,1)S(1)} %collective-permute-done.7, bf16[2048,1024]{1,0:T(8,128)(2,1)S(1)} %copy-done.4, s32[]{:T(128)S(6)} %select_n.15), kind=kOutput, calls=%fused_computation | convolution fusion | flops 538968064 | bytes 8912900 | tf_op jit(solution)/shard_map/dot_general | solution.py:411
  (33 shorter events, 0.3 us)
Async XLA Ops:
  0.0 2.4 %copy-start.5 = (bf16[512,4,128]{2,1,0:T(4,128)(2,1)S(1)}, bf16[512,4,128]{2,1,0:T(4,128)(2,1)}, u32[]{:S(2)}) copy-start(bf16[512,4,128]{2,1,0:T(4,128)(2,1)} %param.12) | copy-start | bytes 1572868
  0.0 7.4 %copy-start.8 = (f32[4,512]{1,0:T(4,128)S(1)}, f32[4,512]{1,0:T(4,128)}, u32[]{:S(2)}) copy-start(f32[4,512]{1,0:T(4,128)} %param.14) | copy-start | bytes 24580
  0.0 7.4 %copy-start.9 = (f32[4,512]{1,0:T(4,128)S(1)}, f32[4,512]{1,0:T(4,128)}, u32[]{:S(2)}) copy-start(f32[4,512]{1,0:T(4,128)} %param.15) | copy-start | bytes 24580
  0.0 7.4 %copy-start.7 = (f32[3,4,4,128]{3,2,1,0:T(4,128)S(1)}, f32[3,4,4,128]{3,2,1,0:T(4,128)}, u32[]{:S(2)}) copy-start(f32[3,4,4,128]{3,2,1,0:T(4,128)} %param.17) | copy-start | bytes 73732
  0.0 8.8 %copy-start = (s32[8]{0:T(128)S(1)}, s32[8]{0:T(128)}, u32[]{:S(2)}) copy-start(s32[8]{0:T(128)} %resets.3) | copy-start | bytes 100
  0.0 25.7 %copy-start.6 = (bf16[512,4,128]{2,1,0:T(4,128)(2,1)S(1)}, bf16[512,4,128]{2,1,0:T(4,128)(2,1)}, u32[]{:S(2)}) copy-start(bf16[512,4,128]{2,1,0:T(4,128)(2,1)} %param.13) | copy-start | bytes 1572868
  2.4 36.7 %copy-start.3 = (f32[128]{0:T(128)S(1)}, f32[128]{0:T(128)}, u32[]{:S(2)}) copy-start(f32[128]{0:T(128)} %param.18) | copy-start | bytes 1540
  2.5 6.3 %collective-permute-start = (bf16[3,3,4,128]{3,1,2,0:T(4,128)(2,1)S(1)}, bf16[3,3,4,128]{3,1,2,0:T(4,128)(2,1)S(1)}, u32[]{:S(2)}, u32[]{:S(2)}) collective-permute-start(bf16[3,3,4,128]{3,1,2,0:T(4,128)(2,1)S(1)} %pad_maximum_fusion.1), channel_id=1, source_target_pairs={{0,4},{4,8},{8,12},{12,16},{16,20},{20,24},{24,28},{1,5},{5,9},{9,... | collective-permute-start | bytes 27656 | tf_op jit(solution)/shard_map/ppermute | solution.py:297
  18.5 1.3 %copy-start.1 = (f32[4,512,256]{2,1,0:T(8,128)}, f32[4,512,256]{2,1,0:T(8,128)S(1)}, u32[]{:S(2)}) copy-start(f32[4,512,256]{2,1,0:T(8,128)S(1)} %get-tuple-element.18.solved_ref) | copy-start | bytes 6291460
  19.8 1.1 %copy-start.2 = (f32[4,3,128,256]{3,2,1,0:T(8,128)}, f32[4,3,128,256]{3,2,1,0:T(8,128)S(1)}, u32[]{:S(2)}) copy-start(f32[4,3,128,256]{3,2,1,0:T(8,128)S(1)} %get-tuple-element.19.starts_ref) | copy-start | bytes 4718596
  21.0 10.5 %collective-permute-start.3 = (bf16[4,128,256]{2,1,0:T(8,128)(2,1)S(1)}, bf16[4,128,256]{2,1,0:T(8,128)(2,1)S(1)}, u32[]{:S(2)}, u32[]{:S(2)}) collective-permute-start(bf16[4,128,256]{2,1,0:T(8,128)(2,1)S(1)} %get-tuple-element.14.refs_0_), channel_id=1, source_target_pairs={{0,12},{4,8},{8,4},{12,0},{1,13},{5,9},{9,5},{13,1},{2,14},{6,10},... | collective-permute-start | bytes 786440 | tf_op jit(solution)/shard_map/ppermute | solution.py:354
  24.2 12.2 %collective-permute-start.2 = (bf16[4,128,256]{2,1,0:T(8,128)(2,1)S(1)}, bf16[4,128,256]{2,1,0:T(8,128)(2,1)S(1)}, u32[]{:S(2)}, u32[]{:S(2)}) collective-permute-start(bf16[4,128,256]{2,1,0:T(8,128)(2,1)S(1)} %get-tuple-element.14.refs_0_), channel_id=1, source_target_pairs={{0,8},{4,12},{8,0},{12,4},{1,9},{5,13},{9,1},{13,5},{2,10},{6,14},... | collective-permute-start | bytes 786440 | tf_op jit(solution)/shard_map/ppermute | solution.py:354
  24.7 11.7 %collective-permute-start.1 = (bf16[4,128,256]{2,1,0:T(8,128)(2,1)S(1)}, bf16[4,128,256]{2,1,0:T(8,128)(2,1)S(1)}, u32[]{:S(2)}, u32[]{:S(2)}) collective-permute-start(bf16[4,128,256]{2,1,0:T(8,128)(2,1)S(1)} %get-tuple-element.14.refs_0_), channel_id=1, source_target_pairs={{0,4},{4,0},{8,12},{12,8},{1,5},{5,1},{9,13},{13,9},{2,6},{6,2},{1... | collective-permute-start | bytes 786440 | tf_op jit(solution)/shard_map/ppermute | solution.py:354
  37.5 9.5 %collective-permute-start.4 = (bf16[4,128,128]{2,1,0:T(8,128)(2,1)S(1)}, bf16[4,128,128]{2,1,0:T(8,128)(2,1)S(1)}, u32[]{:S(2)}, u32[]{:S(2)}) collective-permute-start(bf16[4,128,128]{2,1,0:T(8,128)(2,1)S(1)} %slice.25), channel_id=1, source_target_pairs={{0,16},{1,17},{2,18},{3,19},{4,20},{5,21},{6,22},{7,23},{8,24},{9,... | collective-permute-start | bytes 393224 | tf_op jit(solution)/shard_map/ppermute | solution.py:297
  48.5 15.1 %collective-permute-start.5 = (bf16[512,512]{1,0:T(8,128)(2,1)S(1)}, bf16[512,512]{1,0:T(8,128)(2,1)S(1)}, u32[]{:S(2)}, u32[]{:S(2)}) collective-permute-start(bf16[512,512]{1,0:T(8,128)(2,1)S(1)} %shard_map.103), channel_id=1, source_target_pairs={{0,1},{1,2},{2,3},{3,0},{4,5},{5,6},{6,7},{7,4},{8,9},{9,10},{10,1... | collective-permute-start | bytes 1572872 | tf_op jit(solution)/shard_map/ppermute | solution.py:410
  63.6 14.2 %collective-permute-start.6 = (bf16[512,512]{1,0:T(8,128)(2,1)S(1)}, bf16[512,512]{1,0:T(8,128)(2,1)S(1)}, u32[]{:S(2)}, u32[]{:S(2)}) collective-permute-start(bf16[512,512]{1,0:T(8,128)(2,1)S(1)} %collective-permute-done.5), channel_id=1, source_target_pairs={{0,1},{1,2},{2,3},{3,0},{4,5},{5,6},{6,7},{7,4},{8,9},{9,10},{10,1... | collective-permute-start | bytes 1572872 | tf_op jit(solution)/shard_map/ppermute | solution.py:410
  63.6 14.2 %copy-start.4 = (bf16[2048,1024]{1,0:T(8,128)(2,1)S(1)}, bf16[2048,1024]{1,0:T(8,128)(2,1)}, u32[]{:S(2)}) copy-start(bf16[2048,1024]{1,0:T(8,128)(2,1)} %param.19) | copy-start | bytes 12582916
  77.8 13.2 %collective-permute-start.7 = (bf16[512,512]{1,0:T(8,128)(2,1)S(1)}, bf16[512,512]{1,0:T(8,128)(2,1)S(1)}, u32[]{:S(2)}, u32[]{:S(2)}) collective-permute-start(bf16[512,512]{1,0:T(8,128)(2,1)S(1)} %collective-permute-done.6), channel_id=1, source_target_pairs={{0,1},{1,2},{2,3},{3,0},{4,5},{5,6},{6,7},{7,4},{8,9},{9,10},{10,1... | collective-permute-start | bytes 1572872 | tf_op jit(solution)/shard_map/ppermute | solution.py:410

commit v2 on v1

--- a/solution.py
+++ b/solution.py
@@ -9,6 +9,7 @@
 
 BLOCK = 64
 CHUNK = 128
+PARTS = 2
 EPSILON = 1e-06
 FAR = -1e30
 F32 = jnp.float32
@@ -261,21 +262,21 @@
         whole_ref[h] = states[h]
 
 
-def outputs_kernel(arrived_ref, before_ref, reach_ref, part_ref, gating_ref, normed_ref):
-    heads, length, depth = reach_ref.shape
-    chunks = length // CHUNK
+def outputs_kernel(begin, arrived_ref, before_ref, reach_ref, part_ref, gating_ref, normed_ref):
+    heads, _, depth = reach_ref.shape
+    chunks = normed_ref.shape[0] // CHUNK
     for h in range(heads):
         before = before_ref[h]
         incoming = mul_split(before[:, :depth], arrived_ref[h].astype(F32)) + before[:, depth:]
         high, low = split(incoming)
         for c in range(chunks):
-            here = slice(c * CHUNK, (c + 1) * CHUNK)
+            here = slice(begin + c * CHUNK, begin + (c + 1) * CHUNK)
             reach_high, reach_low = split(reach_ref[h, here])
             core = part_ref[h, here] + (
                 mul(reach_high, high) + (mul(reach_high, low) + mul(reach_low, high))
             )
             scale = lax.rsqrt(jnp.sum(core * core, axis=-1, keepdims=True) / depth + EPSILON)
-            normed_ref[here, h * depth : (h + 1) * depth] = (
+            normed_ref[c * CHUNK : (c + 1) * CHUNK, h * depth : (h + 1) * depth] = (
                 core * scale * gating_ref[h, here]
             ).astype(BF16)
 
@@ -299,7 +300,7 @@
 
 VMEM = pl.BlockSpec(memory_space=pltpu.VMEM)
 SMEM = pl.BlockSpec(memory_space=pltpu.SMEM)
-PARAMS = pltpu.CompilerParams(vmem_limit_bytes=48 * 1024 * 1024)
+PARAMS = pltpu.CompilerParams(vmem_limit_bytes=20 * 1024 * 1024)
 
 
 def on_device(
@@ -370,6 +371,7 @@
         doc_resets, query, gate, output_norm_gain.reshape(1, depth), rims, taps_by_head, scalars,
         unit_key, solved, starts,
     )
+    maps, reach, part, gating = lax.optimization_barrier((maps, reach, part, gating))
     pair = jax.ShapeDtypeStruct((heads, depth, 2 * depth), F32)
     place = lax.axis_index("leaf").astype(jnp.int32).reshape(1)
     before, whole = pl.pallas_call(
@@ -389,30 +391,33 @@
         )
         arrived = from_behind((passed + state).astype(BF16), "chain", 1)
 
-    normed = pl.pallas_call(
-        outputs_kernel,
-        out_shape=jax.ShapeDtypeStruct((length, heads * depth), BF16),
-        in_specs=[VMEM] * 5,
-        out_specs=VMEM,
-        compiler_params=PARAMS,
-    )(arrived, before, reach, part, gating)
-
     ring = lax.axis_size("head")
     mine = lax.axis_index("head")
     width = heads * depth
-    weights = output_projection_weight
-    mixed = None
-    block = normed
+    part_rows = length // PARTS
+    blocks = [
+        pl.pallas_call(
+            functools.partial(outputs_kernel, p * part_rows),
+            out_shape=jax.ShapeDtypeStruct((part_rows, width), BF16),
+            in_specs=[VMEM] * 5,
+            out_specs=VMEM,
+            compiler_params=PARAMS,
+        )(arrived, before, reach, part, gating)
+        for p in range(PARTS)
+    ]
+    mixed = [None] * PARTS
+    around = [(i, (i + 1) % ring) for i in range(ring)]
     for k in range(ring):
         owner = lax.rem(mine + ring - k, ring)
-        rows = lax.dynamic_slice_in_dim(weights, owner * width, width, 0)
+        rows = lax.dynamic_slice_in_dim(output_projection_weight, owner * width, width, 0)
         if k + 1 < ring:
-            following = lax.ppermute(block, "head", [(i, (i + 1) % ring) for i in range(ring)])
-        term = jnp.dot(block, rows, preferred_element_type=F32)
-        mixed = term if mixed is None else mixed + term
+            following = [lax.ppermute(block, "head", around) for block in blocks]
+        for p, block in enumerate(blocks):
+            term = jnp.dot(block, rows, preferred_element_type=F32)
+            mixed[p] = term if mixed[p] is None else mixed[p] + term
         if k + 1 < ring:
-            block = following
-    return mixed.astype(BF16)
+            blocks = following
+    return jnp.concatenate([m.astype(BF16) for m in mixed], axis=0)
 
 
 def solution(mesh):

time: 92.9 us -> 82.8 us (0.89)
  waiting for transfers between devices: 49.4 us -> 32.1 us
  local copies, waits for them, and re-layouts: 5.02 us -> 11.4 us
  other arithmetic: 0.04 us -> 1.07 us
    ppermute x3 -> x6, waiting for transfers between devices: 37.3 us -> 28.5 us  [on_device(): following = [lax.ppermute(block, 'head', around) for block in blocks]]
    ppermute x3, waiting for transfers between devices: 10.7 us -> 2.61 us  [on_device(): lax.ppermute(own_map, 'leaf', pairs_at(k, leaves))]
    unnamed x25 -> x21, local copies, waits for them, and re-layouts: 4.95 us -> 9.96 us
    ppermute x3 -> x6, starting transfers between devices: 1.64 us -> 3.29 us  [on_device(): following = [lax.ppermute(block, 'head', around) for block in blocks]]
    pallas_call x1, Pallas kernels: 7.9 us -> 6.39 us  [on_device(): pl.pallas_call(reads_kernel, out_shape=(per_token, per_token, per_token),...]
    ppermute x3, starting transfers between devices: 4.69 us -> 3.55 us  [on_device(): lax.ppermute(own_map, 'leaf', pairs_at(k, leaves))]
    concatenate x0 -> x1, other arithmetic: none -> 1.04 us  [on_device(): return jnp.concatenate([m.astype(BF16) for m in mixed], axis=0)]
    pallas_call x1 -> x2, Pallas kernels: 1.45 us -> 2.39 us  [on_device(): pl.pallas_call(functools.partial(outputs_kernel, p * part_rows), out_shap...]
  transfers between devices with their start and end apart: 8 -> 11, of which waited for: 6 -> 8; matrix products, arithmetic and copies ran while one was open for 4% -> 10% of each run, Pallas kernels for 9% -> 9%
where the time goes in v2:
time: 82.8 us; the launch traced here: 82.2 us
  waiting for transfers between devices  32.1 us (39%)
  Pallas kernels  19.6 us (24%)
  starting transfers between devices  13 us (16%)
  local copies, waits for them, and re-layouts  11.4 us (14%)
  matrix products  4.84 us (6%)
  other arithmetic  1.07 us (1%)
    ppermute x6, waiting for transfers between devices, on_device(): following = [lax.ppermute(block, 'head', around) for block in blocks]  28.5 us
    unnamed x21, local copies, waits for them, and re-layouts  9.96 us
    pallas_call x1, Pallas kernels, on_device(): pl.pallas_call(maps_kernel, out_shape=(jax.ShapeDtypeStruct((heads, lengt...  9.76 us
    pallas_call x1, Pallas kernels, on_device(): pl.pallas_call(reads_kernel, out_shape=(per_token, per_token, per_token),...  6.39 us
    ppermute x2, starting transfers between devices, from_behind(): lax.ppermute(value, axis, [(i, i + steps) for i in range(count - steps)])  6.14 us
    dot_general x8, matrix products, on_device(): term = jnp.dot(block, rows, preferred_element_type=F32)  4.84 us
    ppermute x3, starting transfers between devices, on_device(): lax.ppermute(own_map, 'leaf', pairs_at(k, leaves))  3.55 us
    ppermute x6, starting transfers between devices, on_device(): following = [lax.ppermute(block, 'head', around) for block in blocks]  3.29 us
  transfers between devices with their start and end apart: 11, of which 8 were waited for; matrix products, arithmetic and copies ran while one was open for 10% of the time, Pallas kernels for 9%

profile of v2, /device:TPU:0, one launch (start us, length us, event | category | flops | bytes accessed | tf_op | source)
XLA Modules:
  0.0 82.2 jit_solution(1545433625554494190)
XLA Ops:
  0.0 1.1 %copy.30 = bf16[512,4,128]{2,0,1:T(8,128)(2,1)S(1)} copy(bf16[512,4,128]{2,1,0:T(4,128)(2,1)} %param.11) | data formatting | bytes 1048576 | tf_op args[1]
  1.1 1.1 %copy.31 = bf16[512,4,128]{2,0,1:T(8,128)(2,1)S(1)} copy(bf16[512,4,128]{2,1,0:T(4,128)(2,1)} %param.12) | data formatting | bytes 1048576 | tf_op args[2]
  2.3 1.1 %copy.29 = bf16[512,4,128]{2,0,1:T(8,128)(2,1)S(1)} copy(bf16[512,4,128]{2,1,0:T(4,128)(2,1)} %param.10) | data formatting | bytes 1048576 | tf_op args[0]
  3.4 4.8 %collective-permute-start = (bf16[3,3,4,128]{3,1,2,0:T(4,128)(2,1)S(1)}, bf16[3,3,4,128]{3,1,2,0:T(4,128)(2,1)S(1)}, u32[]{:S(2)}, u32[]{:S(2)}) collective-permute-start(bf16[3,3,4,128]{3,1,2,0:T(4,128)(2,1)S(1)} %pad_maximum_fusion.2), channel_id=1, source_target_pairs={{0,4},{4,8},{8,12},{12,16},{16,20},{20,24},{24,28},{1,5},{5,9},{9,... | collective-permute-start | bytes 27656 | tf_op jit(solution)/shard_map/ppermute | solution.py:298
  10.5 1.9 %copy.27 = bf16[512,4,128]{2,0,1:T(8,128)(2,1)} copy(bf16[512,4,128]{2,1,0:T(4,128)(2,1)} %param.13) | data formatting | bytes 1048576 | tf_op args[3]
  12.4 9.8 %shard_map.100 = (bf16[4,512,128]{2,1,0:T(8,128)(2,1)S(1)}, f32[4,512,256]{2,1,0:T(8,128)S(1)}, f32[4,3,128,256]{3,2,1,0:T(8,128)S(1)}, bf16[4,128,256]{2,1,0:T(8,128)(2,1)S(1)}) custom-call(s32[8]{0:T(128)S(1)} %copy-done.5, bf16[4,512,128]{2,1,0:T(8,128)(2,1)S(1)} %bitcast.30, bf16[4,512,128]{2,1,0:T(8,128)(2,1)S(1)} %bitcast.31, ...), custom_call_target="tpu_custom_call" | custom-call | tf_op jit(solution)/shard_map/pallas_call | solution.py:335
  22.2 1.6 %collective-permute-start.1 = (bf16[4,128,256]{2,1,0:T(8,128)(2,1)S(1)}, bf16[4,128,256]{2,1,0:T(8,128)(2,1)S(1)}, u32[]{:S(2)}, u32[]{:S(2)}) collective-permute-start(bf16[4,128,256]{2,1,0:T(8,128)(2,1)S(1)} %get-tuple-element.28.refs_0_), channel_id=1, source_target_pairs={{0,4},{4,0},{8,12},{12,8},{1,5},{5,1},{9,13},{13,9},{2,6},{6,2},{1... | collective-permute-start | bytes 786440 | tf_op jit(solution)/shard_map/ppermute | solution.py:355
  23.9 1.9 %collective-permute-start.3 = (bf16[4,128,256]{2,1,0:T(8,128)(2,1)S(1)}, bf16[4,128,256]{2,1,0:T(8,128)(2,1)S(1)}, u32[]{:S(2)}, u32[]{:S(2)}) collective-permute-start(bf16[4,128,256]{2,1,0:T(8,128)(2,1)S(1)} %get-tuple-element.28.refs_0_), channel_id=1, source_target_pairs={{0,12},{4,8},{8,4},{12,0},{1,13},{5,9},{9,5},{13,1},{2,14},{6,10},... | collective-permute-start | bytes 786440 | tf_op jit(solution)/shard_map/ppermute | solution.py:355
  25.8 1.0 %copy-done.3 = bf16[512,4,128]{2,0,1:T(8,128)(2,1)S(1)} copy-done((bf16[512,4,128]{2,0,1:T(8,128)(2,1)S(1)}, bf16[512,4,128]{2,0,1:T(8,128)(2,1)}, u32[]{:S(2)}) %copy-start.3) | copy-done | bytes 524312
  27.8 6.4 %shard_map.101 = (f32[4,512,128]{2,1,0:T(8,128)S(1)}, f32[4,512,128]{2,1,0:T(8,128)S(1)}, f32[4,512,128]{2,1,0:T(8,128)S(1)}) custom-call(s32[8]{0:T(128)S(1)} %copy-done.5, bf16[4,512,128]{2,1,0:T(8,128)(2,1)S(1)} %bitcast.32, bf16[4,512,128]{2,1,0:T(8,128)(2,1)S(1)} %bitcast.33, f32[1,128]{1,0:T(1,128)S(1)} %bitcast.36, ...), custom_call_target="tpu_custom_call" | custom-call | flops 6000000000 | bytes 8388608 | tf_op jit(solution)/shard_map/pallas_call | solution.py:357
  34.3 2.6 %collective-permute-done.2.refs_2_ = bf16[4,128,256]{2,1,0:T(8,128)(2,1)S(1)} collective-permute-done((bf16[4,128,256]{2,1,0:T(8,128)(2,1)S(1)}, bf16[4,128,256]{2,1,0:T(8,128)(2,1)S(1)}, u32[]{:S(2)}, u32[]{:S(2)}) %collective-permute-start.2) | collective-permute-done | bytes 262176 | tf_op jit(solution)/shard_map/ppermute | solution.py:355
  37.9 1.3 %collective-permute-start.4 = (bf16[4,128,128]{2,1,0:T(8,128)(2,1)S(1)}, bf16[4,128,128]{2,1,0:T(8,128)(2,1)S(1)}, u32[]{:S(2)}, u32[]{:S(2)}) collective-permute-start(bf16[4,128,128]{2,1,0:T(8,128)(2,1)S(1)} %slice.25), channel_id=1, source_target_pairs={{0,16},{1,17},{2,18},{3,19},{4,20},{5,21},{6,22},{7,23},{8,24},{9,... | collective-permute-start | bytes 393224 | tf_op jit(solution)/shard_map/ppermute | solution.py:298
  40.2 1.2 %shard_map.103 = bf16[256,512]{1,0:T(8,128)(2,1)S(1)} custom-call(bf16[4,128,128]{2,1,0:T(8,128)(2,1)S(1)} %collective-permute-done.4.arrived_ref, f32[4,128,256]{2,1,0:T(8,128)S(1)} %get-tuple-element.33.before_ref, f32[4,512,128]{2,1,0:T(8,128)S(1)} %get-tuple-element.34.reach_ref, f32[4,512,128]{2,1,0:T(8,128)S(1)} %get-tuple-element.35.part_ref, ...), custom_call_target="tpu_custom_call" | custom-call | tf_op jit(solution)/shard_map/pallas_call | solution.py:399
  42.2 1.6 %collective-permute-start.5 = (bf16[256,512]{1,0:T(8,128)(2,1)S(1)}, bf16[256,512]{1,0:T(8,128)(2,1)}, u32[]{:S(2)}, u32[]{:S(2)}) collective-permute-start(bf16[256,512]{1,0:T(8,128)(2,1)S(1)} %shard_map.103), channel_id=1, source_target_pairs={{0,1},{1,2},{2,3},{3,0},{4,5},{5,6},{6,7},{7,4},{8,9},{9,10},{10,1... | collective-permute-start | bytes 786440 | tf_op jit(solution)/shard_map/ppermute | solution.py:414
  43.8 1.0 %copy-done.1 = f32[4,128,256]{2,1,0:T(8,128)S(1)} copy-done((f32[4,128,256]{2,1,0:T(8,128)S(1)}, f32[4,128,256]{2,1,0:T(8,128)}, u32[]{:S(2)}) %copy-start.1) | copy-done | bytes 524312
  44.8 1.2 %shard_map.104 = bf16[256,512]{1,0:T(8,128)(2,1)S(1)} custom-call(bf16[4,128,128]{2,1,0:T(8,128)(2,1)S(1)} %collective-permute-done.4.arrived_ref, f32[4,128,256]{2,1,0:T(8,128)S(1)} %copy-done.1, f32[4,512,128]{2,1,0:T(8,128)S(1)} %get-tuple-element.34.reach_ref, f32[4,512,128]{2,1,0:T(8,128)S(1)} %get-tuple-element.35.part_ref, ...), custom_call_target="tpu_custom_call" | custom-call | tf_op jit(solution)/shard_map/pallas_call | solution.py:399
  46.0 1.6 %collective-permute-start.8 = (bf16[256,512]{1,0:T(8,128)(2,1)S(1)}, bf16[256,512]{1,0:T(8,128)(2,1)S(1)}, u32[]{:S(2)}, u32[]{:S(2)}) collective-permute-start(bf16[256,512]{1,0:T(8,128)(2,1)S(1)} %shard_map.104), channel_id=1, source_target_pairs={{0,1},{1,2},{2,3},{3,0},{4,5},{5,6},{6,7},{7,4},{8,9},{9,10},{10,1... | collective-permute-start | bytes 786440 | tf_op jit(solution)/shard_map/ppermute | solution.py:414
  47.7 5.6 %collective-permute-done.5 = bf16[256,512]{1,0:T(8,128)(2,1)} collective-permute-done((bf16[256,512]{1,0:T(8,128)(2,1)S(1)}, bf16[256,512]{1,0:T(8,128)(2,1)}, u32[]{:S(2)}, u32[]{:S(2)}) %collective-permute-start.5) | collective-permute-done | bytes 262176 | tf_op jit(solution)/shard_map/ppermute | solution.py:414
  53.2 1.7 %fusion.8 = f32[256,1024]{1,0:T(8,128)S(1)} fusion(bf16[256,512]{1,0:T(8,128)(2,1)} %collective-permute-done.5, bf16[2048,1024]{1,0:T(8,128)(2,1)} %param.19, s32[]{:T(128)S(6)} %select_n.13), kind=kOutput, calls=%fused_computation.15 | convolution fusion | flops 268435456 | bytes 2359300 | tf_op jit(solution)/shard_map/dot_general | solution.py:416
  55.4 3.3 %collective-permute-done.8 = bf16[256,512]{1,0:T(8,128)(2,1)S(1)} collective-permute-done((bf16[256,512]{1,0:T(8,128)(2,1)S(1)}, bf16[256,512]{1,0:T(8,128)(2,1)S(1)}, u32[]{:S(2)}, u32[]{:S(2)}) %collective-permute-start.8) | collective-permute-done | bytes 262176 | tf_op jit(solution)/shard_map/ppermute | solution.py:414
  59.7 4.8 %collective-permute-done.6 = bf16[256,512]{1,0:T(8,128)(2,1)S(1)} collective-permute-done((bf16[256,512]{1,0:T(8,128)(2,1)}, bf16[256,512]{1,0:T(8,128)(2,1)S(1)}, u32[]{:S(2)}, u32[]{:S(2)}) %collective-permute-start.6) | collective-permute-done | bytes 262176 | tf_op jit(solution)/shard_map/ppermute | solution.py:414
  64.5 5.8 %collective-permute-done.9 = bf16[256,512]{1,0:T(8,128)(2,1)S(1)} collective-permute-done((bf16[256,512]{1,0:T(8,128)(2,1)S(1)}, bf16[256,512]{1,0:T(8,128)(2,1)S(1)}, u32[]{:S(2)}, u32[]{:S(2)}) %collective-permute-start.9) | collective-permute-done | bytes 262176 | tf_op jit(solution)/shard_map/ppermute | solution.py:414
  71.2 4.7 %collective-permute-done.7 = bf16[256,512]{1,0:T(8,128)(2,1)S(1)} collective-permute-done((bf16[256,512]{1,0:T(8,128)(2,1)S(1)}, bf16[256,512]{1,0:T(8,128)(2,1)S(1)}, u32[]{:S(2)}, u32[]{:S(2)}) %collective-permute-start.7) | collective-permute-done | bytes 262176 | tf_op jit(solution)/shard_map/ppermute | solution.py:414
  76.3 4.4 %collective-permute-done.10 = bf16[256,512]{1,0:T(8,128)(2,1)S(1)} collective-permute-done((bf16[256,512]{1,0:T(8,128)(2,1)S(1)}, bf16[256,512]{1,0:T(8,128)(2,1)S(1)}, u32[]{:S(2)}, u32[]{:S(2)}) %collective-permute-start.10) | collective-permute-done | bytes 262176 | tf_op jit(solution)/shard_map/ppermute | solution.py:414
  (41 shorter events, 10.4 us)
Async XLA Ops:
  0.0 12.4 %copy-start.5 = (s32[8]{0:T(128)S(1)}, s32[8]{0:T(128)}, u32[]{:S(2)}) copy-start(s32[8]{0:T(128)} %resets.3) | copy-start | bytes 100
  0.0 25.8 %copy-start.6 = (f32[128]{0:T(128)S(1)}, f32[128]{0:T(128)}, u32[]{:S(2)}) copy-start(f32[128]{0:T(128)} %param.18) | copy-start | bytes 1540
  3.4 22.4 %copy-start.2 = (bf16[512,4,128]{2,0,1:T(8,128)(2,1)}, bf16[512,4,128]{2,0,1:T(8,128)(2,1)S(1)}, u32[]{:S(2)}) copy-start(bf16[512,4,128]{2,0,1:T(8,128)(2,1)S(1)} %copy.29) | copy-start | bytes 1572868
  3.4 9.0 %collective-permute-start = (bf16[3,3,4,128]{3,1,2,0:T(4,128)(2,1)S(1)}, bf16[3,3,4,128]{3,1,2,0:T(4,128)(2,1)S(1)}, u32[]{:S(2)}, u32[]{:S(2)}) collective-permute-start(bf16[3,3,4,128]{3,1,2,0:T(4,128)(2,1)S(1)} %pad_maximum_fusion.2), channel_id=1, source_target_pairs={{0,4},{4,8},{8,12},{12,16},{16,20},{20,24},{24,28},{1,5},{5,9},{9,... | collective-permute-start | bytes 27656 | tf_op jit(solution)/shard_map/ppermute | solution.py:298
  22.2 12.0 %collective-permute-start.1 = (bf16[4,128,256]{2,1,0:T(8,128)(2,1)S(1)}, bf16[4,128,256]{2,1,0:T(8,128)(2,1)S(1)}, u32[]{:S(2)}, u32[]{:S(2)}) collective-permute-start(bf16[4,128,256]{2,1,0:T(8,128)(2,1)S(1)} %get-tuple-element.28.refs_0_), channel_id=1, source_target_pairs={{0,4},{4,0},{8,12},{12,8},{1,5},{5,1},{9,13},{13,9},{2,6},{6,2},{1... | collective-permute-start | bytes 786440 | tf_op jit(solution)/shard_map/ppermute | solution.py:355
  23.8 13.1 %collective-permute-start.2 = (bf16[4,128,256]{2,1,0:T(8,128)(2,1)S(1)}, bf16[4,128,256]{2,1,0:T(8,128)(2,1)S(1)}, u32[]{:S(2)}, u32[]{:S(2)}) collective-permute-start(bf16[4,128,256]{2,1,0:T(8,128)(2,1)S(1)} %get-tuple-element.28.refs_0_), channel_id=1, source_target_pairs={{0,8},{4,12},{8,0},{12,4},{1,9},{5,13},{9,1},{13,5},{2,10},{6,14},... | collective-permute-start | bytes 786440 | tf_op jit(solution)/shard_map/ppermute | solution.py:355
  23.9 13.0 %collective-permute-start.3 = (bf16[4,128,256]{2,1,0:T(8,128)(2,1)S(1)}, bf16[4,128,256]{2,1,0:T(8,128)(2,1)S(1)}, u32[]{:S(2)}, u32[]{:S(2)}) collective-permute-start(bf16[4,128,256]{2,1,0:T(8,128)(2,1)S(1)} %get-tuple-element.28.refs_0_), channel_id=1, source_target_pairs={{0,12},{4,8},{8,4},{12,0},{1,13},{5,9},{9,5},{13,1},{2,14},{6,10},... | collective-permute-start | bytes 786440 | tf_op jit(solution)/shard_map/ppermute | solution.py:355
  25.8 1.0 %copy-start.3 = (bf16[512,4,128]{2,0,1:T(8,128)(2,1)S(1)}, bf16[512,4,128]{2,0,1:T(8,128)(2,1)}, u32[]{:S(2)}) copy-start(bf16[512,4,128]{2,0,1:T(8,128)(2,1)} %copy-done.2) | copy-start | bytes 1572868
  26.8 1.0 %copy-start.4 = (bf16[512,4,128]{2,0,1:T(8,128)(2,1)S(1)}, bf16[512,4,128]{2,0,1:T(8,128)(2,1)}, u32[]{:S(2)}) copy-start(bf16[512,4,128]{2,0,1:T(8,128)(2,1)} %copy.27) | copy-start | bytes 1572868
  37.9 2.3 %collective-permute-start.4 = (bf16[4,128,128]{2,1,0:T(8,128)(2,1)S(1)}, bf16[4,128,128]{2,1,0:T(8,128)(2,1)S(1)}, u32[]{:S(2)}, u32[]{:S(2)}) collective-permute-start(bf16[4,128,128]{2,1,0:T(8,128)(2,1)S(1)} %slice.25), channel_id=1, source_target_pairs={{0,16},{1,17},{2,18},{3,19},{4,20},{5,21},{6,22},{7,23},{8,24},{9,... | collective-permute-start | bytes 393224 | tf_op jit(solution)/shard_map/ppermute | solution.py:298
  41.4 0.8 copy-start
  42.2 11.0 %collective-permute-start.5 = (bf16[256,512]{1,0:T(8,128)(2,1)S(1)}, bf16[256,512]{1,0:T(8,128)(2,1)}, u32[]{:S(2)}, u32[]{:S(2)}) collective-permute-start(bf16[256,512]{1,0:T(8,128)(2,1)S(1)} %shard_map.103), channel_id=1, source_target_pairs={{0,1},{1,2},{2,3},{3,0},{4,5},{5,6},{6,7},{7,4},{8,9},{9,10},{10,1... | collective-permute-start | bytes 786440 | tf_op jit(solution)/shard_map/ppermute | solution.py:414
  43.8 1.0 %copy-start.1 = (f32[4,128,256]{2,1,0:T(8,128)S(1)}, f32[4,128,256]{2,1,0:T(8,128)}, u32[]{:S(2)}) copy-start(f32[4,128,256]{2,1,0:T(8,128)} %copy-done) | copy-start | bytes 1572868
  44.8 10.1 %copy-start.7 = (bf16[2048,1024]{1,0:T(8,128)(2,1)S(1)}, bf16[2048,1024]{1,0:T(8,128)(2,1)}, u32[]{:S(2)}) copy-start(bf16[2048,1024]{1,0:T(8,128)(2,1)} %param.19) | copy-start | bytes 12582916
  46.0 12.7 %collective-permute-start.8 = (bf16[256,512]{1,0:T(8,128)(2,1)S(1)}, bf16[256,512]{1,0:T(8,128)(2,1)S(1)}, u32[]{:S(2)}, u32[]{:S(2)}) collective-permute-start(bf16[256,512]{1,0:T(8,128)(2,1)S(1)} %shard_map.104), channel_id=1, source_target_pairs={{0,1},{1,2},{2,3},{3,0},{4,5},{5,6},{6,7},{7,4},{8,9},{9,10},{10,1... | collective-permute-start | bytes 786440 | tf_op jit(solution)/shard_map/ppermute | solution.py:414
  53.2 11.2 %collective-permute-start.6 = (bf16[256,512]{1,0:T(8,128)(2,1)}, bf16[256,512]{1,0:T(8,128)(2,1)S(1)}, u32[]{:S(2)}, u32[]{:S(2)}) collective-permute-start(bf16[256,512]{1,0:T(8,128)(2,1)} %collective-permute-done.5), channel_id=1, source_target_pairs={{0,1},{1,2},{2,3},{3,0},{4,5},{5,6},{6,7},{7,4},{8,9},{9,10},{10,1... | collective-permute-start | bytes 786440 | tf_op jit(solution)/shard_map/ppermute | solution.py:414
  59.2 11.1 %collective-permute-start.9 = (bf16[256,512]{1,0:T(8,128)(2,1)S(1)}, bf16[256,512]{1,0:T(8,128)(2,1)S(1)}, u32[]{:S(2)}, u32[]{:S(2)}) collective-permute-start(bf16[256,512]{1,0:T(8,128)(2,1)S(1)} %collective-permute-done.8), channel_id=1, source_target_pairs={{0,1},{1,2},{2,3},{3,0},{4,5},{5,6},{6,7},{7,4},{8,9},{9,10},{10,1... | collective-permute-start | bytes 786440 | tf_op jit(solution)/shard_map/ppermute | solution.py:414
  64.5 11.4 %collective-permute-start.7 = (bf16[256,512]{1,0:T(8,128)(2,1)S(1)}, bf16[256,512]{1,0:T(8,128)(2,1)S(1)}, u32[]{:S(2)}, u32[]{:S(2)}) collective-permute-start(bf16[256,512]{1,0:T(8,128)(2,1)S(1)} %collective-permute-done.6), channel_id=1, source_target_pairs={{0,1},{1,2},{2,3},{3,0},{4,5},{5,6},{6,7},{7,4},{8,9},{9,10},{10,1... | collective-permute-start | bytes 786440 | tf_op jit(solution)/shard_map/ppermute | solution.py:414
  70.3 10.4 %collective-permute-start.10 = (bf16[256,512]{1,0:T(8,128)(2,1)S(1)}, bf16[256,512]{1,0:T(8,128)(2,1)S(1)}, u32[]{:S(2)}, u32[]{:S(2)}) collective-permute-start(bf16[256,512]{1,0:T(8,128)(2,1)S(1)} %collective-permute-done.9), channel_id=1, source_target_pairs={{0,1},{1,2},{2,3},{3,0},{4,5},{5,6},{6,7},{7,4},{8,9},{9,10},{10,1... | collective-permute-start | bytes 786440 | tf_op jit(solution)/shard_map/ppermute | solution.py:414

commit v3 on v1

v3 whole, which is shorter than its diff:
```python
import functools

import jax
import jax.numpy as jnp
from jax import lax
from jax.experimental import pallas as pl
from jax.experimental.pallas import tpu as pltpu
from jax.sharding import PartitionSpec as P

BLOCK = 64
CHUNK = 128
GROUPS = 2
RIM = 8
EPSILON = 1e-06
FAR = -1e30
F32 = jnp.float32
BF16 = jnp.bfloat16
NN = (((1,), (0,)), ((), ()))
NT = (((1,), (1,)), ((), ()))
TN = (((0,), (0,)), ((), ()))


def split(a):
    high = a.astype(BF16)
    return high, (a - high.astype(F32)).astype(BF16)


def mul(a, b, dims=NN):
    return lax.dot_general(a, b, dims, preferred_element_type=F32)


def mul_split(a, b):
    a_high, a_low = split(a)
    b_high, b_low = split(b)
    return mul(a_high, b_high) + (mul(a_low, b_high) + mul(a_high, b_low))


def rows_of(c):
    return slice(c * CHUNK, (c + 1) * CHUNK)


def indices():
    shape = (CHUNK, CHUNK)
    return (
        lax.broadcasted_iota(jnp.int32, shape, 0),
        lax.broadcasted_iota(jnp.int32, shape, 1),
    )


def token_scalars(decay_ref, strength_ref, c):
    row, col = indices()
    cum = lax.dot_general(
        decay_ref[:, rows_of(c)],
        (row <= col).astype(F32),
        NN,
        precision=lax.Precision.HIGHEST,
        preferred_element_type=F32,
    )
    strength = strength_ref[:, rows_of(c)]
    stacked = [cum, strength]
    missing = 8 - 2 * cum.shape[0]
    if missing > 0:
        stacked.append(jnp.zeros((missing, CHUNK), F32))
    return cum, strength, jnp.transpose(jnp.concatenate(stacked, axis=0))


def convolve(x_ref, rims, taps_ref, which, head, padded, store):
    length = x_ref.shape[1]
    padded[0:RIM] = rims[which * RIM : (which + 1) * RIM, head, :]
    padded[RIM : RIM + length] = x_ref[head].astype(F32)
    count = taps_ref.shape[1]
    taps = [taps_ref[which, j, head : head + 1, :] for j in range(count)]
    for c in range(length // CHUNK):
        begin = c * CHUNK + RIM + 1 - count
        total = taps[0] * padded[begin : begin + CHUNK]
        for j in range(1, count):
            total = total + taps[j] * padded[begin + j : begin + j + CHUNK]
        store(c, total / (1.0 + jnp.exp(-total)))


def unit(rows):
    return rows * lax.rsqrt(jnp.sum(rows * rows, axis=-1, keepdims=True) + EPSILON)


def same_document(second_resets, row, col):
    return ((row // BLOCK) - (col // BLOCK)) * second_resets == 0


def lower_inverse(lowers, row, col):
    differ = row ^ col
    eye = (row == col).astype(F32)
    in_block = (differ < 8).astype(F32)
    diagonal = [low * in_block for low in lowers]
    rounded_lowers = [low.astype(BF16) for low in lowers]
    powers = [d.astype(BF16) for d in diagonal]
    squares = [mul(p, p).astype(BF16) for p in powers]
    inverse = [eye - d for d in diagonal]
    fourths = [mul(s, s).astype(BF16) for s in squares]
    inverse = [x + mul(x.astype(BF16), s) for x, s in zip(inverse, squares)]
    inverse = [x + mul(x.astype(BF16), s) for x, s in zip(inverse, fourths)]
    size = 8
    while size < CHUNK:
        joint = ((differ >= size) & (differ < 2 * size)).astype(F32).astype(BF16)
        rounded = [x.astype(BF16) for x in inverse]
        inner = [mul(low * joint, x).astype(BF16) for low, x in zip(rounded_lowers, rounded)]
        inverse = [x - mul(r, i) for x, r, i in zip(inverse, rounded, inner)]
        size *= 2
    return inverse


def rims_kernel(*refs):
    *inputs, packed_ref = refs
    for i, x_ref in enumerate(inputs):
        packed_ref[i * RIM : (i + 1) * RIM] = x_ref[...]


def maps_kernel(
    base, resets, key_ref, value_ref, rim_ref, taps_ref, decay_ref, strength_ref,
    unit_ref, solved_ref, starts_ref, map_ref,
    rims, padded, value_s, step_s,
):
    heads, length, depth = unit_ref.shape
    chunks = length // CHUNK
    total_heads = decay_ref.shape[0]
    row, col = indices()
    rims[...] = rim_ref[...].astype(F32)
    for g in range(heads):

        def store_key(c, rows):
            unit_ref[g, rows_of(c)] = unit(rows).astype(BF16)

        def store_value(c, rows):
            value_s[g, rows_of(c)] = rows.astype(BF16)

        convolve(key_ref, rims, taps_ref, 1, base + g, padded, store_key)
        convolve(value_ref, rims, taps_ref, 2, base + g, padded, store_value)

    parts = []
    lowers = []
    for c in range(chunks):
        cum, strengths, columns = token_scalars(decay_ref, strength_ref, c)
        first, second = resets[2 * c], resets[2 * c + 1]
        strictly = (row > col) & same_document(second, row, col)
        for g in range(heads):
            h = base + g
            cum_col = columns[:, h : h + 1]
            cum_row = cum[h : h + 1]
            key = unit_ref[g, rows_of(c)]
            fading = jnp.exp(jnp.where(strictly, cum_col - cum_row, FAR))
            strength_col = columns[:, total_heads + h : total_heads + h + 1]
            lowers.append(strength_col * fading * mul(key, key, NT))
            parts.append((g, c, first, second, cum_col, cum_row, strengths[h : h + 1]))
    inverses = lower_inverse(lowers, row, col)
    in_first = lax.broadcasted_iota(jnp.int32, (1, CHUNK), 1) < BLOCK
    first_rows = lax.broadcasted_iota(jnp.int32, (CHUNK, 1), 0) < BLOCK
    for (g, c, first, second, cum_col, cum_row, strength_row), inverse in zip(parts, inverses):
        keep_first = (1 - first).astype(F32)
        keep_second = (1 - second).astype(F32)
        keep_both = keep_first * keep_second
        key = unit_ref[g, rows_of(c)]
        value = value_s[g, rows_of(c)]
        growth_row = jnp.exp(cum_row) * jnp.where(in_first, keep_first, keep_both)
        by_strength = inverse * strength_row
        high, low = split(by_strength * growth_row)
        write_keys = mul(high, key) + mul(low, key)
        high, low = split(by_strength)
        local_values = mul(high, value) + mul(low, value)
        solved = jnp.concatenate([write_keys, local_values], axis=1)
        solved_ref[g, rows_of(c)] = solved
        end = cum_row[:, CHUNK - 1 : CHUNK]
        tail = jnp.exp(end - cum_col) * jnp.where(first_rows, keep_second, 1.0)
        high, low = split(tail * solved)
        product = mul(key, high, TN) + mul(key, low, TN)
        passed = jnp.exp(end) * keep_both
        step_s[g, c, :, :depth] = jnp.where(row == col, passed, 0.0) - product[:, :depth]
        step_s[g, c, :, depth:] = product[:, depth:]

    states = [step_s[g, 0] for g in range(heads)]
    for c in range(1, chunks):
        for g in range(heads):
            starts_ref[g, c - 1] = states[g]
            step = step_s[g, c]
            joined = mul_split(step[:, :depth], states[g])
            states[g] = jnp.concatenate(
                [joined[:, :depth], joined[:, depth:] + step[:, depth:]], axis=1
            )
    for g in range(heads):
        map_ref[g] = states[g].astype(BF16)


def reads_kernel(
    base, resets, query_ref, gate_ref, gain_ref, rim_ref, taps_ref, decay_ref, strength_ref,
    unit_ref, solved_ref, starts_ref,
    reach_ref, part_ref, gating_ref,
    rims, padded, query_s,
):
    heads, length, depth = unit_ref.shape
    chunks = length // CHUNK
    row, col = indices()
    first_rows = lax.broadcasted_iota(jnp.int32, (CHUNK, 1), 0) < BLOCK
    rims[...] = rim_ref[...].astype(F32)
    for g in range(heads):

        def store_query(c, rows):
            query_s[g, rows_of(c)] = (unit(rows) * depth**-0.5).astype(BF16)

        convolve(query_ref, rims, taps_ref, 0, base + g, padded, store_query)

    for c in range(chunks):
        here = rows_of(c)
        cum, _, columns = token_scalars(decay_ref, strength_ref, c)
        first, second = resets[2 * c], resets[2 * c + 1]
        keep_first = (1 - first).astype(F32)
        keep_both = keep_first * (1 - second).astype(F32)
        upto = (row >= col) & same_document(second, row, col)
        for g in range(heads):
            h = base + g
            cum_col = columns[:, h : h + 1]
            query = query_s[g, here]
            fading = jnp.exp(jnp.where(upto, cum_col - cum[h : h + 1], FAR))
            mixing = fading * mul(query, unit_ref[g, here], NT)
            own = mul_split(mixing, solved_ref[g, here])
            growth = jnp.exp(cum_col) * jnp.where(first_rows, keep_first, keep_both)
            reach = growth * query.astype(F32) - own[:, :depth]
            part = own[:, depth:]
            if c:
                both = mul_split(reach, starts_ref[g, c - 1])
                reach = both[:, :depth]
                part = part + both[:, depth:]
            reach_ref[g, here] = reach
            part_ref[g, here] = part
            gate = gate_ref[h, here].astype(F32)
            gating_ref[g, here] = gain_ref[...] * (gate / (1.0 + jnp.exp(-gate)))


def partner(place, k, count):
    if count & (count - 1) == 0:
        return place ^ k
    return lax.rem(place + count - k, count)


def pairs_at(k, count):
    if count & (count - 1) == 0:
        return [(i, i ^ k) for i in range(count)]
    return [(i, (i + k) % count) for i in range(count)]


def join_kernel(count, place, *refs):
    maps = refs[:count]
    before_ref, state_ref, whole_ref, ordered = refs[count:]
    heads, depth, _ = before_ref.shape
    me = place[0]
    for k in range(count):
        ordered[partner(me, k, count)] = maps[k][...]
    row, col = indices()
    eye = (row == col).astype(F32)
    states = [jnp.concatenate([eye, jnp.zeros((depth, depth), F32)], axis=1)] * heads
    for lap in range(count):

        @pl.when(lap == me)
        def _():
            for h in range(heads):
                before_ref[h] = states[h]

        for h in range(heads):
            step = ordered[lap, h]
            if lap:
                high, low = split(states[h])
                trans = step[:, :depth]
                joined = mul(trans, high) + mul(trans, low)
                states[h] = jnp.concatenate(
                    [joined[:, :depth], joined[:, depth:] + step[:, depth:].astype(F32)], axis=1
                )
            else:
                states[h] = step.astype(F32)
    for h in range(heads):
        whole_ref[h] = states[h]
        state_ref[h] = states[h][:, depth:].astype(BF16)


def outputs_kernel(arrived_ref, before_ref, reach_ref, part_ref, gating_ref, normed_ref):
    heads, length, depth = reach_ref.shape
    for g in range(heads):
        before = before_ref[g]
        incoming = mul_split(before[:, :depth], arrived_ref[g].astype(F32)) + before[:, depth:]
        high, low = split(incoming)
        for c in range(length // CHUNK):
            here = rows_of(c)
            reach_high, reach_low = split(reach_ref[g, here])
            core = part_ref[g, here] + (
                mul(reach_high, high) + (mul(reach_high, low) + mul(reach_low, high))
            )
            scale = lax.rsqrt(jnp.sum(core * core, axis=-1, keepdims=True) / depth + EPSILON)
            normed_ref[here, g * depth : (g + 1) * depth] = (
                core * scale * gating_ref[g, here]
            ).astype(BF16)


def projected_kernel(section, total_ref, block_ref, weights_ref, out_ref):
    out_ref[...] = total_ref[...] + mul(block_ref[...], weights_ref[...])


def from_behind(value, axis, steps):
    count = lax.axis_size(axis)
    return lax.ppermute(value, axis, [(i, i + steps) for i in range(count - steps)])


VMEM = pl.BlockSpec(memory_space=pltpu.VMEM)
SMEM = pl.BlockSpec(memory_space=pltpu.SMEM)
PARAMS = pltpu.CompilerParams(vmem_limit_bytes=16 * 1024 * 1024)


def pack_rims(inputs):
    length, heads, depth = inputs[0].shape
    last = pl.BlockSpec((RIM, heads, depth), lambda i: (length // RIM - 1, 0, 0))
    packed = (len(inputs) * RIM, heads, depth)
    return pl.pallas_call(
        rims_kernel,
        grid=(1,),
        out_shape=jax.ShapeDtypeStruct(packed, BF16),
        in_specs=[last] * len(inputs),
        out_specs=pl.BlockSpec(packed, lambda i: (0, 0, 0)),
    )(*inputs)


def maps_of(base, heads, resets, key, value, rims, taps, decay, strength):
    _, length, depth = key.shape
    chunks = length // CHUNK
    return pl.pallas_call(
        functools.partial(maps_kernel, base),
        out_shape=(
            jax.ShapeDtypeStruct((heads, length, depth), BF16),
            jax.ShapeDtypeStruct((heads, length, 2 * depth), F32),
            jax.ShapeDtypeStruct((heads, chunks - 1, depth, 2 * depth), F32),
            jax.ShapeDtypeStruct((heads, depth, 2 * depth), BF16),
        ),
        in_specs=[SMEM] + [VMEM] * 6,
        out_specs=[VMEM] * 4,
        scratch_shapes=[
            pltpu.VMEM(rims.shape, F32),
            pltpu.VMEM((length + RIM, depth), F32),
            pltpu.VMEM((heads, length, depth), BF16),
            pltpu.VMEM((heads, chunks, depth, 2 * depth), F32),
        ],
        compiler_params=PARAMS,
        cost_estimate=pl.CostEstimate(
            flops=5 * 10**9, bytes_accessed=4 * 2**20, transcendentals=10**6
        ),
    )(resets, key, value, rims, taps, decay, strength)


def reads_of(base, heads, resets, query, gate, gain, rims, taps, decay, strength, made):
    _, length, depth = query.shape
    per_token = jax.ShapeDtypeStruct((heads, length, depth), F32)
    return pl.pallas_call(
        functools.partial(reads_kernel, base),
        out_shape=(per_token, per_token, per_token),
        in_specs=[SMEM] + [VMEM] * 10,
        out_specs=[VMEM] * 3,
        scratch_shapes=[
            pltpu.VMEM(rims.shape, F32),
            pltpu.VMEM((length + RIM, depth), F32),
            pltpu.VMEM((heads, length, depth), BF16),
        ],
        compiler_params=PARAMS,
        cost_estimate=pl.CostEstimate(
            flops=3 * 10**9, bytes_accessed=4 * 2**20, transcendentals=10**6
        ),
    )(resets, query, gate, gain, rims, taps, decay, strength, *made)


def join(place, maps):
    count = len(maps)
    heads, depth, _ = maps[0].shape
    pair = jax.ShapeDtypeStruct((heads, depth, 2 * depth), F32)
    return pl.pallas_call(
        functools.partial(join_kernel, count),
        out_shape=(pair, jax.ShapeDtypeStruct((heads, depth, depth), BF16), pair),
        in_specs=[SMEM] + [VMEM] * count,
        out_specs=[VMEM] * 3,
        scratch_shapes=[pltpu.VMEM((count, heads, depth, 2 * depth), BF16)],
        compiler_params=PARAMS,
    )(place, *maps)


def outputs_of(arrived, before, reads):
    heads, length, depth = reads[0].shape
    return pl.pallas_call(
        outputs_kernel,
        out_shape=jax.ShapeDtypeStruct((length, heads * depth), BF16),
        in_specs=[VMEM] * 5,
        out_specs=VMEM,
        compiler_params=PARAMS,
    )(arrived, before, *reads)


def projected(section, total, block, weights):
    length, columns = total.shape
    width = block.shape[1]
    return pl.pallas_call(
        projected_kernel,
        out_shape=jax.ShapeDtypeStruct(total.shape, F32),
        grid_spec=pltpu.PrefetchScalarGridSpec(
            num_scalar_prefetch=1,
            grid=(length // CHUNK,),
            in_specs=[
                pl.BlockSpec((CHUNK, columns), lambda i, s: (i, 0)),
                pl.BlockSpec((CHUNK, width), lambda i, s: (i, 0)),
                pl.BlockSpec((width, columns), lambda i, s: (s[0], 0)),
            ],
            out_specs=pl.BlockSpec((CHUNK, columns), lambda i, s: (i, 0)),
        ),
        compiler_params=PARAMS,
    )(section.astype(jnp.int32).reshape(1), total, block, weights)


def after(first, *values):
    return lax.optimization_barrier((first, *values))[1:]


def on_device(
    query_in,
    key_in,
    value_in,
    gate_in,
    write_strength,
    log_decay,
    doc_resets,
    conv_weight,
    output_norm_gain,
    output_projection_weight,
):
    length, heads, depth = query_in.shape
    size = heads // GROUPS
    rims = from_behind(pack_rims((query_in, key_in, value_in)), ("chain", "leaf"), 1)
    key, value = (jnp.transpose(x, (1, 0, 2)) for x in (key_in, value_in))
    gain = output_norm_gain.reshape(1, depth)
    leaves = lax.axis_size("leaf")
    place = lax.axis_index("leaf").astype(jnp.int32).reshape(1)

    made = []
    exchanged = []
    for g in range(GROUPS):
        unit_key, solved, starts, own_map = maps_of(
            g * size, size, doc_resets, key, value, rims, conv_weight, log_decay, write_strength
        )
        made.append((unit_key, solved, starts))
        exchanged.append(
            [own_map]
            + [lax.ppermute(own_map, "leaf", pairs_at(k, leaves)) for k in range(1, leaves)]
        )
        key, value = after(own_map, key, value)
        if g == 0:
            query_in, gate_in = after(own_map, query_in, gate_in)
    query, gate = (jnp.transpose(x, (1, 0, 2)) for x in (query_in, gate_in))

    blocks = []
    for g in range(GROUPS):
        reads = reads_of(
            g * size, size, doc_resets, query, gate, gain, rims, conv_weight, log_decay,
            write_strength, made[g],
        )
        maps, reads = lax.optimization_barrier((exchanged[g], reads))
        before, state, whole = join(place, maps)
        query, gate = after(state, query, gate)
        arrived = from_behind(state, "chain", 1)
        for _ in range(lax.axis_size("chain") - 2):
            passed = jnp.einsum(
                "hij,hjk->hik",
                whole[..., :depth],
                arrived.astype(F32),
                precision=lax.Precision.HIGHEST,
            )
            arrived = from_behind((passed + whole[..., depth:]).astype(BF16), "chain", 1)
        blocks.append(outputs_of(arrived, before, reads))

    ring = lax.axis_size("head")
    mine = lax.axis_index("head")
    width = size * depth
    around = [(i, (i + 1) % ring) for i in range(ring)]
    mixed = None
    for k in range(ring):
        owner = lax.rem(mine + ring - k, ring)
        if k + 1 < ring:
            following = [lax.ppermute(block, "head", around) for block in blocks]
        for g, block in enumerate(blocks):
            section = owner * GROUPS + g
            if k + 1 == ring and g + 2 == GROUPS:
                mixed = projected(section, mixed, block, output_projection_weight)
                continue
            rows = lax.dynamic_slice_in_dim(output_projection_weight, section * width, width, 0)
            term = jnp.dot(block, rows, preferred_element_type=F32)
            mixed = term if mixed is None else mixed + term
        if k + 1 < ring:
            blocks = following
    return mixed.astype(BF16)


def solution(mesh):
    return jax.shard_map(
        on_device,
        mesh=mesh,
        in_specs=(
            P(("chain", "leaf"), "head", None),
            P(("chain", "leaf"), "head", None),
            P(("chain", "leaf"), "head", None),
            P(("chain", "leaf"), "head", None),
            P("head", ("chain", "leaf")),
            P("head", ("chain", "leaf")),
            P(("chain", "leaf")),
            P(None, None, "head", None),
            P(),
            P(None, "head"),
        ),
        out_specs=P(("chain", "leaf"), "head"),
        check_vma=False,
    )
```

time: 92.9 us -> 86.8 us (0.934)
  waiting for transfers between devices: 49.4 us -> 33.9 us
  starting transfers between devices: 12.7 us -> 20.4 us
  Pallas kernels: 20.1 us -> 24 us
  local copies, waits for them, and re-layouts: 5.02 us -> 3.17 us
  matrix products: 5.23 us -> 3.39 us
  other arithmetic: 0.04 us -> 1.29 us
    ppermute x3 -> x6, waiting for transfers between devices: 10.7 us -> 0.02 us  [on_device(): lax.ppermute(own_map, 'leaf', pairs_at(k, leaves))]
    pallas_call x4 -> x10, Pallas kernels: 20.1 us -> 24 us  [the longest x2 9.66 us: maps_of(): pl.pallas_call(functools.partial(maps_kernel, base), out_shape=(jax.Shape...]
    ppermute x3 -> x6, waiting for transfers between devices: 37.3 us -> 33.5 us  [on_device(): following = [lax.ppermute(block, 'head', around) for block in blocks]]
    ppermute x3 -> x6, starting transfers between devices: 4.69 us -> 8.39 us  [on_device(): lax.ppermute(own_map, 'leaf', pairs_at(k, leaves))]
    unnamed x25 -> x20, local copies, waits for them, and re-layouts: 4.95 us -> 1.68 us
    ppermute x3 -> x6, starting transfers between devices: 1.64 us -> 4.62 us  [on_device(): following = [lax.ppermute(block, 'head', around) for block in blocks]]
    dot_general x4 -> x7, matrix products: 5.23 us -> 3.39 us  [on_device(): term = jnp.dot(block, rows, preferred_element_type=F32)]
    transpose x0 -> x1, local copies, waits for them, and re-layouts: none -> 1.34 us  [on_device(): key, value = (jnp.transpose(x, (1, 0, 2)) for x in (key_in, value_in))]
  transfers between devices with their start and end apart: 8 -> 15, of which waited for: 6 -> 5; matrix products, arithmetic and copies ran while one was open for 4% -> 6% of each run, Pallas kernels for 9% -> 18%
where the time goes in v3:
time: 86.8 us; the launch traced here: 86.5 us
  waiting for transfers between devices  33.9 us (39%)
  Pallas kernels  24 us (28%)
  starting transfers between devices  20.4 us (24%)
  matrix products  3.39 us (4%)
  local copies, waits for them, and re-layouts  3.17 us (4%)
  other arithmetic  1.29 us (1%)
    ppermute x6, waiting for transfers between devices, on_device(): following = [lax.ppermute(block, 'head', around) for block in blocks]  33.5 us
    pallas_call x2, Pallas kernels, maps_of(): pl.pallas_call(functools.partial(maps_kernel, base), out_shape=(jax.Shape...  9.66 us
    ppermute x6, starting transfers between devices, on_device(): lax.ppermute(own_map, 'leaf', pairs_at(k, leaves))  8.39 us
    ppermute x3, starting transfers between devices, from_behind(): lax.ppermute(value, axis, [(i, i + steps) for i in range(count - steps)])  7.41 us
    pallas_call x2, Pallas kernels, reads_of(): pl.pallas_call(functools.partial(reads_kernel, base), out_shape=(per_toke...  7.17 us
    ppermute x6, starting transfers between devices, on_device(): following = [lax.ppermute(block, 'head', around) for block in blocks]  4.62 us
    dot_general x7, matrix products, on_device(): term = jnp.dot(block, rows, preferred_element_type=F32)  3.39 us
    pallas_call x2, Pallas kernels, join(): pl.pallas_call(functools.partial(join_kernel, count), out_shape=(pair, ja...  3.09 us
  transfers between devices with their start and end apart: 15, of which 5 were waited for; matrix products, arithmetic and copies ran while one was open for 6% of the time, Pallas kernels for 18%

profile of v3, /device:TPU:0, one launch (start us, length us, event | category | flops | bytes accessed | tf_op | source)
XLA Modules:
  0.0 86.5 jit_solution(7879176801273112713)
XLA Ops:
  0.0 1.4 %shard_map.100 = bf16[24,4,128]{2,1,0:T(4,128)(2,1)} custom-call(bf16[512,4,128]{2,1,0:T(4,128)(2,1)} %refs_0_.1, bf16[512,4,128]{2,1,0:T(4,128)(2,1)} %refs_1_.1, bf16[512,4,128]{2,1,0:T(4,128)(2,1)} %refs_2_.1), custom_call_target="tpu_custom_call" | custom-call | tf_op jit(solution)/shard_map/pallas_call | solution.py:317
  1.4 4.8 %collective-permute-start = (bf16[24,4,128]{2,1,0:T(4,128)(2,1)}, bf16[24,4,128]{2,1,0:T(4,128)(2,1)S(1)}, u32[]{:S(2)}, u32[]{:S(2)}) collective-permute-start(bf16[24,4,128]{2,1,0:T(4,128)(2,1)} %shard_map.100), channel_id=1, source_target_pairs={{0,4},{4,8},{8,12},{12,16},{16,20},{20,24},{24,28},{1,5},{5,9},{9,... | collective-permute-start | bytes 73736 | tf_op jit(solution)/shard_map/ppermute | solution.py:305
  6.2 1.3 %copy_bitcast_fusion.2 = (bf16[4,512,128]{2,1,0:T(8,128)(2,1)S(1)}, bf16[4,512,128]{2,1,0:T(8,128)(2,1)S(1)}) fusion(bf16[512,4,128]{2,1,0:T(4,128)(2,1)} %refs_2_.1, bf16[512,4,128]{2,1,0:T(4,128)(2,1)} %refs_1_.1), kind=kLoop, calls=%fused_computation.4 | loop fusion | bytes 2097152 | tf_op jit(solution)/shard_map/transpose | solution.py:436
  8.0 4.8 %shard_map.101 = (bf16[2,512,128]{2,1,0:T(8,128)(2,1)S(1)}, f32[2,512,256]{2,1,0:T(8,128)S(1)}, f32[2,3,128,256]{3,2,1,0:T(8,128)S(1)}, bf16[2,128,256]{2,1,0:T(8,128)(2,1)S(1)}) custom-call(s32[8]{0:T(128)S(1)} %copy-done.6, bf16[4,512,128]{2,1,0:T(8,128)(2,1)S(1)} %get-tuple-element.61.key_ref, bf16[4,512,128]{2,1,0:T(8,128)(2,1)S(1)} %get-tuple-element.62.value_ref, ...), custom_call_target="tpu_custom_call" | custom-call | flops 5000000000 | bytes 4194304 | tf_op jit(solution)/shard_map/pallas_call | solution.py:329
  12.8 2.4 %collective-permute-start.1 = (bf16[2,128,256]{2,1,0:T(8,128)(2,1)S(1)}, bf16[2,128,256]{2,1,0:T(8,128)(2,1)S(1)}, u32[]{:S(2)}, u32[]{:S(2)}) collective-permute-start(bf16[2,128,256]{2,1,0:T(8,128)(2,1)S(1)} %get-tuple-element.52.refs_0_), channel_id=1, source_target_pairs={{0,4},{4,0},{8,12},{12,8},{1,5},{5,1},{9,13},{13,9},{2,6},{6,2},{1... | collective-permute-start | bytes 393224 | tf_op jit(solution)/shard_map/ppermute | solution.py:450
  15.2 1.5 %collective-permute-start.2 = (bf16[2,128,256]{2,1,0:T(8,128)(2,1)S(1)}, bf16[2,128,256]{2,1,0:T(8,128)(2,1)S(1)}, u32[]{:S(2)}, u32[]{:S(2)}) collective-permute-start(bf16[2,128,256]{2,1,0:T(8,128)(2,1)S(1)} %get-tuple-element.52.refs_0_), channel_id=1, source_target_pairs={{0,8},{4,12},{8,0},{12,4},{1,9},{5,13},{9,1},{13,5},{2,10},{6,14},... | collective-permute-start | bytes 393224 | tf_op jit(solution)/shard_map/ppermute | solution.py:450
  17.6 4.8 %shard_map.105 = (bf16[2,512,128]{2,1,0:T(8,128)(2,1)S(1)}, f32[2,512,256]{2,1,0:T(8,128)S(1)}, f32[2,3,128,256]{3,2,1,0:T(8,128)S(1)}, bf16[2,128,256]{2,1,0:T(8,128)(2,1)S(1)}) custom-call(s32[8]{0:T(128)S(1)} %copy-done.6, bf16[4,512,128]{2,1,0:T(8,128)(2,1)S(1)} %get-tuple-element.61.key_ref, bf16[4,512,128]{2,1,0:T(8,128)(2,1)S(1)} %get-tuple-element.62.value_ref, ...), custom_call_target="tpu_custom_call" | custom-call | flops 5000000000 | bytes 4194304 | tf_op jit(solution)/shard_map/pallas_call | solution.py:329
  22.5 1.2 %collective-permute-start.5 = (bf16[2,128,256]{2,1,0:T(8,128)(2,1)S(1)}, bf16[2,128,256]{2,1,0:T(8,128)(2,1)S(1)}, u32[]{:S(2)}, u32[]{:S(2)}) collective-permute-start(bf16[2,128,256]{2,1,0:T(8,128)(2,1)S(1)} %get-tuple-element.72.refs_0_), channel_id=1, source_target_pairs={{0,4},{4,0},{8,12},{12,8},{1,5},{5,1},{9,13},{13,9},{2,6},{6,2},{1... | collective-permute-start | bytes 393224 | tf_op jit(solution)/shard_map/ppermute | solution.py:450
  23.6 1.5 %collective-permute-start.6 = (bf16[2,128,256]{2,1,0:T(8,128)(2,1)S(1)}, bf16[2,128,256]{2,1,0:T(8,128)(2,1)S(1)}, u32[]{:S(2)}, u32[]{:S(2)}) collective-permute-start(bf16[2,128,256]{2,1,0:T(8,128)(2,1)S(1)} %get-tuple-element.72.refs_0_), channel_id=1, source_target_pairs={{0,8},{4,12},{8,0},{12,4},{1,9},{5,13},{9,1},{13,5},{2,10},{6,14},... | collective-permute-start | bytes 393224 | tf_op jit(solution)/shard_map/ppermute | solution.py:450
  25.3 3.6 %shard_map.102 = (f32[2,512,128]{2,1,0:T(8,128)S(1)}, f32[2,512,128]{2,1,0:T(8,128)S(1)}, f32[2,512,128]{2,1,0:T(8,128)S(1)}) custom-call(s32[8]{0:T(128)S(1)} %copy-done.6, bf16[4,512,128]{2,1,0:T(8,128)(2,1)S(1)} %bitcast.22, bf16[4,512,128]{2,1,0:T(8,128)(2,1)S(1)} %bitcast.20, f32[1,128]{1,0:T(1,128)S(1)} %bitcast.24, ...), custom_call_target="tpu_custom_call" | custom-call | flops 3000000000 | bytes 4194304 | tf_op jit(solution)/shard_map/pallas_call | solution.py:355
  29.9 1.6 %shard_map.103 = (f32[2,128,256]{2,1,0:T(8,128)S(1)}, bf16[2,128,128]{2,1,0:T(8,128)(2,1)}, f32[2,128,256]{2,1,0:T(8,128)}) custom-call(s32[1]{0:T(128)} %bitcast.1.place, bf16[2,128,256]{2,1,0:T(8,128)(2,1)S(1)} %get-tuple-element.52.refs_0_, bf16[2,128,256]{2,1,0:T(8,128)(2,1)S(1)} %collective-permute-done.1.refs_1_, ...), custom_call_target="tpu_custom_call" | custom-call | tf_op jit(solution)/shard_map/pallas_call | solution.py:376
  31.5 3.6 %shard_map.106 = (f32[2,512,128]{2,1,0:T(8,128)S(1)}, f32[2,512,128]{2,1,0:T(8,128)S(1)}, f32[2,512,128]{2,1,0:T(8,128)S(1)}) custom-call(s32[8]{0:T(128)S(1)} %copy-done.6, bf16[4,512,128]{2,1,0:T(8,128)(2,1)S(1)} %bitcast.23, bf16[4,512,128]{2,1,0:T(8,128)(2,1)S(1)} %bitcast.21, f32[1,128]{1,0:T(1,128)S(1)} %bitcast.25, ...), custom_call_target="tpu_custom_call" | custom-call | flops 3000000000 | bytes 4194304 | tf_op jit(solution)/shard_map/pallas_call | solution.py:355
  35.1 1.5 %shard_map.107 = (f32[2,128,256]{2,1,0:T(8,128)S(1)}, bf16[2,128,128]{2,1,0:T(8,128)(2,1)}, f32[2,128,256]{2,1,0:T(8,128)}) custom-call(s32[1]{0:T(128)} %bitcast.1.place, bf16[2,128,256]{2,1,0:T(8,128)(2,1)S(1)} %get-tuple-element.72.refs_0_, bf16[2,128,256]{2,1,0:T(8,128)(2,1)S(1)} %collective-permute-done.5.refs_1_, ...), custom_call_target="tpu_custom_call" | custom-call | tf_op jit(solution)/shard_map/pallas_call | solution.py:376
  37.3 1.3 %collective-permute-start.8 = (bf16[2,128,128]{2,1,0:T(8,128)(2,1)}, bf16[2,128,128]{2,1,0:T(8,128)(2,1)S(1)}, u32[]{:S(2)}, u32[]{:S(2)}) collective-permute-start(bf16[2,128,128]{2,1,0:T(8,128)(2,1)} %get-tuple-element.76), channel_id=1, source_target_pairs={{0,16},{1,17},{2,18},{3,19},{4,20},{5,21},{6,22},{7,23},{8,24},{9,... | collective-permute-start | bytes 196616 | tf_op jit(solution)/shard_map/ppermute | solution.py:305
  38.6 1.3 %collective-permute-start.4 = (bf16[2,128,128]{2,1,0:T(8,128)(2,1)}, bf16[2,128,128]{2,1,0:T(8,128)(2,1)S(1)}, u32[]{:S(2)}, u32[]{:S(2)}) collective-permute-start(bf16[2,128,128]{2,1,0:T(8,128)(2,1)} %get-tuple-element.56), channel_id=1, source_target_pairs={{0,16},{1,17},{2,18},{3,19},{4,20},{5,21},{6,22},{7,23},{8,24},{9,... | collective-permute-start | bytes 196616 | tf_op jit(solution)/shard_map/ppermute | solution.py:305
  41.7 1.6 %collective-permute-start.10 = (bf16[512,256]{1,0:T(8,128)(2,1)S(1)}, bf16[512,256]{1,0:T(8,128)(2,1)S(1)}, u32[]{:S(2)}, u32[]{:S(2)}) collective-permute-start(bf16[512,256]{1,0:T(8,128)(2,1)S(1)} %shard_map.108), channel_id=1, source_target_pairs={{0,1},{1,2},{2,3},{3,0},{4,5},{5,6},{6,7},{7,4},{8,9},{9,10},{10,1... | collective-permute-start | bytes 786440 | tf_op jit(solution)/shard_map/ppermute | solution.py:485
  44.2 1.6 %collective-permute-start.9 = (bf16[512,256]{1,0:T(8,128)(2,1)S(1)}, bf16[512,256]{1,0:T(8,128)(2,1)S(1)}, u32[]{:S(2)}, u32[]{:S(2)}) collective-permute-start(bf16[512,256]{1,0:T(8,128)(2,1)S(1)} %shard_map.104), channel_id=1, source_target_pairs={{0,1},{1,2},{2,3},{3,0},{4,5},{5,6},{6,7},{7,4},{8,9},{9,10},{10,1... | collective-permute-start | bytes 786440 | tf_op jit(solution)/shard_map/ppermute | solution.py:485
  46.7 6.0 %collective-permute-done.10 = bf16[512,256]{1,0:T(8,128)(2,1)S(1)} collective-permute-done((bf16[512,256]{1,0:T(8,128)(2,1)S(1)}, bf16[512,256]{1,0:T(8,128)(2,1)S(1)}, u32[]{:S(2)}, u32[]{:S(2)}) %collective-permute-start.10) | collective-permute-done | bytes 262176 | tf_op jit(solution)/shard_map/ppermute | solution.py:485
  53.2 5.2 %collective-permute-done.9 = bf16[512,256]{1,0:T(8,128)(2,1)S(1)} collective-permute-done((bf16[512,256]{1,0:T(8,128)(2,1)S(1)}, bf16[512,256]{1,0:T(8,128)(2,1)S(1)}, u32[]{:S(2)}, u32[]{:S(2)}) %collective-permute-start.9) | collective-permute-done | bytes 262176 | tf_op jit(solution)/shard_map/ppermute | solution.py:485
  58.8 10.0 %collective-permute-done.11 = bf16[512,256]{1,0:T(8,128)(2,1)S(1)} collective-permute-done((bf16[512,256]{1,0:T(8,128)(2,1)S(1)}, bf16[512,256]{1,0:T(8,128)(2,1)S(1)}, u32[]{:S(2)}, u32[]{:S(2)}) %collective-permute-start.11) | collective-permute-done | bytes 262176 | tf_op jit(solution)/shard_map/ppermute | solution.py:485
  69.2 1.4 %collective-permute-start.14 = (bf16[512,256]{1,0:T(8,128)(2,1)S(1)}, bf16[512,256]{1,0:T(8,128)(2,1)S(1)}, u32[]{:S(2)}, u32[]{:S(2)}) collective-permute-start(bf16[512,256]{1,0:T(8,128)(2,1)S(1)} %collective-permute-done.12), channel_id=1, source_target_pairs={{0,1},{1,2},{2,3},{3,0},{4,5},{5,6},{6,7},{7,4},{8,9},{9,10},{10,1... | collective-permute-start | bytes 786440 | tf_op jit(solution)/shard_map/ppermute | solution.py:485
  71.3 12.4 %collective-permute-done.14 = bf16[512,256]{1,0:T(8,128)(2,1)S(1)} collective-permute-done((bf16[512,256]{1,0:T(8,128)(2,1)S(1)}, bf16[512,256]{1,0:T(8,128)(2,1)S(1)}, u32[]{:S(2)}, u32[]{:S(2)}) %collective-permute-start.14) | collective-permute-done | bytes 262176 | tf_op jit(solution)/shard_map/ppermute | solution.py:485
  84.2 1.0 %shard_map.109 = f32[512,1024]{1,0:T(8,128)S(1)} custom-call(s32[1]{0:T(128)} %bitcast.section, f32[512,1024]{1,0:T(8,128)S(1)} %add_add_fusion.total_ref, bf16[512,256]{1,0:T(8,128)(2,1)S(1)} %collective-permute-done.13.block_ref, bf16[2048,1024]{1,0:T(8,128)(2,1)S(1)} %copy-done), custom_call_target="tpu_custom_call" | custom-call | tf_op jit(solution)/shard_map/pallas_call | solution.py:400
  85.2 1.3 %add_convert_fusion = bf16[512,1024]{1,0:T(8,128)(2,1)} fusion(f32[512,1024]{1,0:T(8,128)S(1)} %shard_map.109, f32[512,1024]{1,0:T(8,128)S(1)} %fusion), kind=kLoop, calls=%fused_computation | loop fusion | flops 1048576 | bytes 5242880 | tf_op jit(solution)/shard_map/convert_element_type | solution.py:496
  (47 shorter events, 9.1 us)
Async XLA Ops:
  0.0 8.0 %copy-start.5 = (f32[4,512]{1,0:T(4,128)S(1)}, f32[4,512]{1,0:T(4,128)}, u32[]{:S(2)}) copy-start(f32[4,512]{1,0:T(4,128)} %strength_ref.7) | copy-start | bytes 24580
  0.0 8.0 %copy-start.4 = (f32[4,512]{1,0:T(4,128)S(1)}, f32[4,512]{1,0:T(4,128)}, u32[]{:S(2)}) copy-start(f32[4,512]{1,0:T(4,128)} %decay_ref.7) | copy-start | bytes 24580
  0.0 8.0 %copy-start.6 = (s32[8]{0:T(128)S(1)}, s32[8]{0:T(128)}, u32[]{:S(2)}) copy-start(s32[8]{0:T(128)} %resets.7) | copy-start | bytes 100
  0.0 8.0 %copy-start.3 = (f32[3,4,4,128]{3,2,1,0:T(4,128)S(1)}, f32[3,4,4,128]{3,2,1,0:T(4,128)}, u32[]{:S(2)}) copy-start(f32[3,4,4,128]{3,2,1,0:T(4,128)} %taps_ref.7) | copy-start | bytes 73732
  1.4 6.6 %collective-permute-start = (bf16[24,4,128]{2,1,0:T(4,128)(2,1)}, bf16[24,4,128]{2,1,0:T(4,128)(2,1)S(1)}, u32[]{:S(2)}, u32[]{:S(2)}) collective-permute-start(bf16[24,4,128]{2,1,0:T(4,128)(2,1)} %shard_map.100), channel_id=1, source_target_pairs={{0,4},{4,8},{8,12},{12,16},{16,20},{20,24},{24,28},{1,5},{5,9},{9,... | collective-permute-start | bytes 73736 | tf_op jit(solution)/shard_map/ppermute | solution.py:305
  12.8 12.3 %copy-start.9 = (bf16[512,4,128]{2,1,0:T(4,128)(2,1)S(1)}, bf16[512,4,128]{2,1,0:T(4,128)(2,1)}, u32[]{:S(2)}) copy-start(bf16[512,4,128]{2,1,0:T(4,128)(2,1)} %param.13) | copy-start | bytes 1572868
  12.8 12.4 %copy-start.8 = (bf16[512,4,128]{2,1,0:T(4,128)(2,1)S(1)}, bf16[512,4,128]{2,1,0:T(4,128)(2,1)}, u32[]{:S(2)}) copy-start(bf16[512,4,128]{2,1,0:T(4,128)(2,1)} %refs_0_.1) | copy-start | bytes 1572868
  12.8 16.1 %collective-permute-start.1 = (bf16[2,128,256]{2,1,0:T(8,128)(2,1)S(1)}, bf16[2,128,256]{2,1,0:T(8,128)(2,1)S(1)}, u32[]{:S(2)}, u32[]{:S(2)}) collective-permute-start(bf16[2,128,256]{2,1,0:T(8,128)(2,1)S(1)} %get-tuple-element.52.refs_0_), channel_id=1, source_target_pairs={{0,4},{4,0},{8,12},{12,8},{1,5},{5,1},{9,13},{13,9},{2,6},{6,2},{1... | collective-permute-start | bytes 393224 | tf_op jit(solution)/shard_map/ppermute | solution.py:450
  15.2 14.6 %collective-permute-start.2 = (bf16[2,128,256]{2,1,0:T(8,128)(2,1)S(1)}, bf16[2,128,256]{2,1,0:T(8,128)(2,1)S(1)}, u32[]{:S(2)}, u32[]{:S(2)}) collective-permute-start(bf16[2,128,256]{2,1,0:T(8,128)(2,1)S(1)} %get-tuple-element.52.refs_0_), channel_id=1, source_target_pairs={{0,8},{4,12},{8,0},{12,4},{1,9},{5,13},{9,1},{13,5},{2,10},{6,14},... | collective-permute-start | bytes 393224 | tf_op jit(solution)/shard_map/ppermute | solution.py:450
  16.7 13.1 %collective-permute-start.3 = (bf16[2,128,256]{2,1,0:T(8,128)(2,1)S(1)}, bf16[2,128,256]{2,1,0:T(8,128)(2,1)S(1)}, u32[]{:S(2)}, u32[]{:S(2)}) collective-permute-start(bf16[2,128,256]{2,1,0:T(8,128)(2,1)S(1)} %get-tuple-element.52.refs_0_), channel_id=1, source_target_pairs={{0,12},{4,8},{8,4},{12,0},{1,13},{5,9},{9,5},{13,1},{2,14},{6,10},... | collective-permute-start | bytes 393224 | tf_op jit(solution)/shard_map/ppermute | solution.py:450
  22.4 2.9 %copy-start.7 = (f32[128]{0:T(128)S(1)}, f32[128]{0:T(128)}, u32[]{:S(2)}) copy-start(f32[128]{0:T(128)} %param.18) | copy-start | bytes 1540
  22.5 12.6 %collective-permute-start.5 = (bf16[2,128,256]{2,1,0:T(8,128)(2,1)S(1)}, bf16[2,128,256]{2,1,0:T(8,128)(2,1)S(1)}, u32[]{:S(2)}, u32[]{:S(2)}) collective-permute-start(bf16[2,128,256]{2,1,0:T(8,128)(2,1)S(1)} %get-tuple-element.72.refs_0_), channel_id=1, source_target_pairs={{0,4},{4,0},{8,12},{12,8},{1,5},{5,1},{9,13},{13,9},{2,6},{6,2},{1... | collective-permute-start | bytes 393224 | tf_op jit(solution)/shard_map/ppermute | solution.py:450
  23.6 11.5 %collective-permute-start.6 = (bf16[2,128,256]{2,1,0:T(8,128)(2,1)S(1)}, bf16[2,128,256]{2,1,0:T(8,128)(2,1)S(1)}, u32[]{:S(2)}, u32[]{:S(2)}) collective-permute-start(bf16[2,128,256]{2,1,0:T(8,128)(2,1)S(1)} %get-tuple-element.72.refs_0_), channel_id=1, source_target_pairs={{0,8},{4,12},{8,0},{12,4},{1,9},{5,13},{9,1},{13,5},{2,10},{6,14},... | collective-permute-start | bytes 393224 | tf_op jit(solution)/shard_map/ppermute | solution.py:450
  28.9 6.2 %collective-permute-start.7 = (bf16[2,128,256]{2,1,0:T(8,128)(2,1)S(1)}, bf16[2,128,256]{2,1,0:T(8,128)(2,1)S(1)}, u32[]{:S(2)}, u32[]{:S(2)}) collective-permute-start(bf16[2,128,256]{2,1,0:T(8,128)(2,1)S(1)} %get-tuple-element.72.refs_0_), channel_id=1, source_target_pairs={{0,12},{4,8},{8,4},{12,0},{1,13},{5,9},{9,5},{13,1},{2,14},{6,10},... | collective-permute-start | bytes 393224 | tf_op jit(solution)/shard_map/ppermute | solution.py:450
  37.3 2.6 %collective-permute-start.8 = (bf16[2,128,128]{2,1,0:T(8,128)(2,1)}, bf16[2,128,128]{2,1,0:T(8,128)(2,1)S(1)}, u32[]{:S(2)}, u32[]{:S(2)}) collective-permute-start(bf16[2,128,128]{2,1,0:T(8,128)(2,1)} %get-tuple-element.76), channel_id=1, source_target_pairs={{0,16},{1,17},{2,18},{3,19},{4,20},{5,21},{6,22},{7,23},{8,24},{9,... | collective-permute-start | bytes 196616 | tf_op jit(solution)/shard_map/ppermute | solution.py:305
  38.6 4.8 %collective-permute-start.4 = (bf16[2,128,128]{2,1,0:T(8,128)(2,1)}, bf16[2,128,128]{2,1,0:T(8,128)(2,1)S(1)}, u32[]{:S(2)}, u32[]{:S(2)}) collective-permute-start(bf16[2,128,128]{2,1,0:T(8,128)(2,1)} %get-tuple-element.56), channel_id=1, source_target_pairs={{0,16},{1,17},{2,18},{3,19},{4,20},{5,21},{6,22},{7,23},{8,24},{9,... | collective-permute-start | bytes 196616 | tf_op jit(solution)/shard_map/ppermute | solution.py:305
  39.9 1.0 %copy-start.2 = (f32[2,128,256]{2,1,0:T(8,128)S(1)}, f32[2,128,256]{2,1,0:T(8,128)}, u32[]{:S(2)}) copy-start(f32[2,128,256]{2,1,0:T(8,128)} %copy-done.1) | copy-start | bytes 786436
  40.9 5.0 %copy-start = (bf16[2048,1024]{1,0:T(8,128)(2,1)S(1)}, bf16[2048,1024]{1,0:T(8,128)(2,1)}, u32[]{:S(2)}) copy-start(bf16[2048,1024]{1,0:T(8,128)(2,1)} %weights_ref.1) | copy-start | bytes 12582916
  41.7 11.0 %collective-permute-start.10 = (bf16[512,256]{1,0:T(8,128)(2,1)S(1)}, bf16[512,256]{1,0:T(8,128)(2,1)S(1)}, u32[]{:S(2)}, u32[]{:S(2)}) collective-permute-start(bf16[512,256]{1,0:T(8,128)(2,1)S(1)} %shard_map.108), channel_id=1, source_target_pairs={{0,1},{1,2},{2,3},{3,0},{4,5},{5,6},{6,7},{7,4},{8,9},{9,10},{10,1... | collective-permute-start | bytes 786440 | tf_op jit(solution)/shard_map/ppermute | solution.py:485
  44.2 14.1 %collective-permute-start.9 = (bf16[512,256]{1,0:T(8,128)(2,1)S(1)}, bf16[512,256]{1,0:T(8,128)(2,1)S(1)}, u32[]{:S(2)}, u32[]{:S(2)}) collective-permute-start(bf16[512,256]{1,0:T(8,128)(2,1)S(1)} %shard_map.104), channel_id=1, source_target_pairs={{0,1},{1,2},{2,3},{3,0},{4,5},{5,6},{6,7},{7,4},{8,9},{9,10},{10,1... | collective-permute-start | bytes 786440 | tf_op jit(solution)/shard_map/ppermute | solution.py:485
  52.7 16.5 %collective-permute-start.12 = (bf16[512,256]{1,0:T(8,128)(2,1)S(1)}, bf16[512,256]{1,0:T(8,128)(2,1)S(1)}, u32[]{:S(2)}, u32[]{:S(2)}) collective-permute-start(bf16[512,256]{1,0:T(8,128)(2,1)S(1)} %collective-permute-done.10), channel_id=1, source_target_pairs={{0,1},{1,2},{2,3},{3,0},{4,5},{5,6},{6,7},{7,4},{8,9},{9,10},{10,1... | collective-permute-start | bytes 786440 | tf_op jit(solution)/shard_map/ppermute | solution.py:485
  58.3 10.4 %collective-permute-start.11 = (bf16[512,256]{1,0:T(8,128)(2,1)S(1)}, bf16[512,256]{1,0:T(8,128)(2,1)S(1)}, u32[]{:S(2)}, u32[]{:S(2)}) collective-permute-start(bf16[512,256]{1,0:T(8,128)(2,1)S(1)} %collective-permute-done.9), channel_id=1, source_target_pairs={{0,1},{1,2},{2,3},{3,0},{4,5},{5,6},{6,7},{7,4},{8,9},{9,10},{10,1... | collective-permute-start | bytes 786440 | tf_op jit(solution)/shard_map/ppermute | solution.py:485
  68.8 15.4 %collective-permute-start.13 = (bf16[512,256]{1,0:T(8,128)(2,1)S(1)}, bf16[512,256]{1,0:T(8,128)(2,1)S(1)}, u32[]{:S(2)}, u32[]{:S(2)}) collective-permute-start(bf16[512,256]{1,0:T(8,128)(2,1)S(1)} %collective-permute-done.11), channel_id=1, source_target_pairs={{0,1},{1,2},{2,3},{3,0},{4,5},{5,6},{6,7},{7,4},{8,9},{9,10},{10,1... | collective-permute-start | bytes 786440 | tf_op jit(solution)/shard_map/ppermute | solution.py:485
  69.2 14.5 %collective-permute-start.14 = (bf16[512,256]{1,0:T(8,128)(2,1)S(1)}, bf16[512,256]{1,0:T(8,128)(2,1)S(1)}, u32[]{:S(2)}, u32[]{:S(2)}) collective-permute-start(bf16[512,256]{1,0:T(8,128)(2,1)S(1)} %collective-permute-done.12), channel_id=1, source_target_pairs={{0,1},{1,2},{2,3},{3,0},{4,5},{5,6},{6,7},{7,4},{8,9},{9,10},{10,1... | collective-permute-start | bytes 786440 | tf_op jit(solution)/shard_map/ppermute | solution.py:485
  (1 other events, 0.7 us)

commit v4 on v3

--- a/solution.py
+++ b/solution.py
@@ -109,9 +109,16 @@
 
 
 def rims_kernel(*refs):
-    *inputs, packed_ref = refs
+    *inputs, packed_ref, arrived = refs
+    copies = []
     for i, x_ref in enumerate(inputs):
-        packed_ref[i * RIM : (i + 1) * RIM] = x_ref[...]
+        last = x_ref.at[pl.ds(x_ref.shape[0] - RIM, RIM)]
+        here = packed_ref.at[pl.ds(i * RIM, RIM)]
+        copies.append(pltpu.make_async_copy(last, here, arrived.at[i]))
+    for copy in copies:
+        copy.start()
+    for copy in copies:
+        copy.wait()
 
 
 def maps_kernel(
@@ -247,7 +254,7 @@
 
 def join_kernel(count, place, *refs):
     maps = refs[:count]
-    before_ref, state_ref, whole_ref, ordered = refs[count:]
+    before_ref, state_ref, *trans_ref, ordered = refs[count:]
     heads, depth, _ = before_ref.shape
     me = place[0]
     for k in range(count):
@@ -274,8 +281,9 @@
             else:
                 states[h] = step.astype(F32)
     for h in range(heads):
-        whole_ref[h] = states[h]
-        state_ref[h] = states[h][:, depth:].astype(BF16)
+        state_ref[h] = states[h][:, depth:].astype(state_ref.dtype)
+        for ref in trans_ref:
+            ref[h] = states[h][:, :depth]
 
 
 def outputs_kernel(arrived_ref, before_ref, reach_ref, part_ref, gating_ref, normed_ref):
@@ -297,7 +305,7 @@
 
 
 def projected_kernel(section, total_ref, block_ref, weights_ref, out_ref):
-    out_ref[...] = total_ref[...] + mul(block_ref[...], weights_ref[...])
+    out_ref[...] = (total_ref[...] + mul(block_ref[...], weights_ref[...])).astype(out_ref.dtype)
 
 
 def from_behind(value, axis, steps):
@@ -311,15 +319,13 @@
 
 
 def pack_rims(inputs):
-    length, heads, depth = inputs[0].shape
-    last = pl.BlockSpec((RIM, heads, depth), lambda i: (length // RIM - 1, 0, 0))
-    packed = (len(inputs) * RIM, heads, depth)
+    _, heads, depth = inputs[0].shape
     return pl.pallas_call(
         rims_kernel,
-        grid=(1,),
-        out_shape=jax.ShapeDtypeStruct(packed, BF16),
-        in_specs=[last] * len(inputs),
-        out_specs=pl.BlockSpec(packed, lambda i: (0, 0, 0)),
+        out_shape=jax.ShapeDtypeStruct((len(inputs) * RIM, heads, depth), BF16),
+        in_specs=[pl.BlockSpec(memory_space=pltpu.HBM)] * len(inputs),
+        out_specs=VMEM,
+        scratch_shapes=[pltpu.SemaphoreType.DMA((len(inputs),))],
     )(*inputs)
 
 
@@ -369,15 +375,20 @@
     )(resets, query, gate, gain, rims, taps, decay, strength, *made)
 
 
-def join(place, maps):
+def join(place, maps, links):
     count = len(maps)
     heads, depth, _ = maps[0].shape
     pair = jax.ShapeDtypeStruct((heads, depth, 2 * depth), F32)
+    square = (heads, depth, depth)
+    if links == 1:
+        totals = (jax.ShapeDtypeStruct(square, BF16),)
+    else:
+        totals = (jax.ShapeDtypeStruct(square, F32),) * 2
     return pl.pallas_call(
         functools.partial(join_kernel, count),
-        out_shape=(pair, jax.ShapeDtypeStruct((heads, depth, depth), BF16), pair),
+        out_shape=(pair, *totals),
         in_specs=[SMEM] + [VMEM] * count,
-        out_specs=[VMEM] * 3,
+        out_specs=[VMEM] * (1 + len(totals)),
         scratch_shapes=[pltpu.VMEM((count, heads, depth, 2 * depth), BF16)],
         compiler_params=PARAMS,
     )(place, *maps)
@@ -394,12 +405,12 @@
     )(arrived, before, *reads)
 
 
-def projected(section, total, block, weights):
+def projected(section, total, block, weights, dtype):
     length, columns = total.shape
     width = block.shape[1]
     return pl.pallas_call(
         projected_kernel,
-        out_shape=jax.ShapeDtypeStruct(total.shape, F32),
+        out_shape=jax.ShapeDtypeStruct(total.shape, dtype),
         grid_spec=pltpu.PrefetchScalarGridSpec(
             num_scalar_prefetch=1,
             grid=(length // CHUNK,),
@@ -411,6 +422,11 @@
             out_specs=pl.BlockSpec((CHUNK, columns), lambda i, s: (i, 0)),
         ),
         compiler_params=PARAMS,
+        cost_estimate=pl.CostEstimate(
+            flops=2 * length * columns * width,
+            bytes_accessed=4 * length * columns,
+            transcendentals=0,
+        ),
     )(section.astype(jnp.int32).reshape(1), total, block, weights)
 
 
@@ -455,24 +471,25 @@
     query, gate = (jnp.transpose(x, (1, 0, 2)) for x in (query_in, gate_in))
 
     blocks = []
+    links = lax.axis_size("chain") - 1
     for g in range(GROUPS):
         reads = reads_of(
             g * size, size, doc_resets, query, gate, gain, rims, conv_weight, log_decay,
             write_strength, made[g],
         )
-        maps, reads = lax.optimization_barrier((exchanged[g], reads))
-        before, state, whole = join(place, maps)
-        query, gate = after(state, query, gate)
-        arrived = from_behind(state, "chain", 1)
-        for _ in range(lax.axis_size("chain") - 2):
+        maps, reads, _ = lax.optimization_barrier((exchanged[g], reads, exchanged[-1][0]))
+        before, state, *trans = join(place, maps, links)
+        arrived = from_behind(state.astype(BF16), "chain", 1)
+        for _ in range(links - 1):
             passed = jnp.einsum(
                 "hij,hjk->hik",
-                whole[..., :depth],
+                trans[0],
                 arrived.astype(F32),
                 precision=lax.Precision.HIGHEST,
             )
-            arrived = from_behind((passed + whole[..., depth:]).astype(BF16), "chain", 1)
+            arrived = from_behind((passed + state).astype(BF16), "chain", 1)
         blocks.append(outputs_of(arrived, before, reads))
+        query, gate = after(blocks[g], query, gate)
 
     ring = lax.axis_size("head")
     mine = lax.axis_index("head")
@@ -485,15 +502,16 @@
             following = [lax.ppermute(block, "head", around) for block in blocks]
         for g, block in enumerate(blocks):
             section = owner * GROUPS + g
-            if k + 1 == ring and g + 2 == GROUPS:
-                mixed = projected(section, mixed, block, output_projection_weight)
+            if k + 1 == ring:
+                dtype = BF16 if g + 1 == GROUPS else F32
+                mixed = projected(section, mixed, block, output_projection_weight, dtype)
                 continue
             rows = lax.dynamic_slice_in_dim(output_projection_weight, section * width, width, 0)
             term = jnp.dot(block, rows, preferred_element_type=F32)
             mixed = term if mixed is None else mixed + term
         if k + 1 < ring:
             blocks = following
-    return mixed.astype(BF16)
+    return mixed
 
 
 def solution(mesh):

time: 86.8 us -> 79.2 us (0.912)
  waiting for transfers between devices: 33.9 us -> 26.9 us
  other arithmetic: 1.29 us -> 0 us
    ppermute x6, waiting for transfers between devices: 33.5 us -> 26.1 us  [on_device(): following = [lax.ppermute(block, 'head', around) for block in blocks]]
    pallas_call x1 -> x2, Pallas kernels: 1.01 us -> 3.11 us  [projected(): pl.pallas_call(projected_kernel, out_shape=jax.ShapeDtypeStruct(total.sha...]
    pallas_call x3, Pallas kernels: 4.48 us -> 2.89 us  [the longest x2 1.48 us: join(): pl.pallas_call(functools.partial(join_kernel, count), out_shape=(pair, *t...]
    convert_element_type x1 -> x0, other arithmetic: 1.29 us -> none  [on_device(): return mixed.astype(BF16)]
    dot_general x7 -> x6, matrix products: 3.39 us -> 2.93 us  [on_device(): term = jnp.dot(block, rows, preferred_element_type=F32)]
    unnamed x20 -> x24, local copies, waits for them, and re-layouts: 1.68 us -> 1.92 us
  transfers between devices with their start and end apart: 15 -> 15, of which waited for: 5 -> 7; matrix products, arithmetic and copies ran while one was open for 6% -> 6% of each run, Pallas kernels for 18% -> 20%
where the time goes in v4:
time: 79.2 us; the launch traced here: 79 us
  waiting for transfers between devices  26.9 us (34%)
  Pallas kernels  24.6 us (31%)
  starting transfers between devices  20.8 us (26%)
  local copies, waits for them, and re-layouts  3.4 us (4%)
  matrix products  2.93 us (4%)
    ppermute x6, waiting for transfers between devices, on_device(): following = [lax.ppermute(block, 'head', around) for block in blocks]  26.1 us
    pallas_call x2, Pallas kernels, maps_of(): pl.pallas_call(functools.partial(maps_kernel, base), out_shape=(jax.Shape...  9.73 us
    ppermute x6, starting transfers between devices, on_device(): lax.ppermute(own_map, 'leaf', pairs_at(k, leaves))  8.33 us
    ppermute x3, starting transfers between devices, from_behind(): lax.ppermute(value, axis, [(i, i + steps) for i in range(count - steps)])  7.43 us
    pallas_call x2, Pallas kernels, reads_of(): pl.pallas_call(functools.partial(reads_kernel, base), out_shape=(per_toke...  7.18 us
    ppermute x6, starting transfers between devices, on_device(): following = [lax.ppermute(block, 'head', around) for block in blocks]  5.07 us
    pallas_call x2, Pallas kernels, projected(): pl.pallas_call(projected_kernel, out_shape=jax.ShapeDtypeStruct(total.sha...  3.11 us
    dot_general x6, matrix products, on_device(): term = jnp.dot(block, rows, preferred_element_type=F32)  2.93 us
  transfers between devices with their start and end apart: 15, of which 7 were waited for; matrix products, arithmetic and copies ran while one was open for 6% of the time, Pallas kernels for 20%

profile of v4, /device:TPU:0, one launch (start us, length us, event | category | flops | bytes accessed | tf_op | source)
XLA Modules:
  0.0 79.0 jit_solution(7204070331692462841)
XLA Ops:
  0.0 1.4 %shard_map.100 = bf16[24,4,128]{2,1,0:T(4,128)(2,1)} custom-call(bf16[512,4,128]{2,1,0:T(4,128)(2,1)} %refs_0_.1, bf16[512,4,128]{2,1,0:T(4,128)(2,1)} %refs_1_.1, bf16[512,4,128]{2,1,0:T(4,128)(2,1)} %refs_2_.1), custom_call_target="tpu_custom_call" | custom-call | tf_op jit(solution)/shard_map/pallas_call | solution.py:323
  1.4 4.8 %collective-permute-start = (bf16[24,4,128]{2,1,0:T(4,128)(2,1)}, bf16[24,4,128]{2,1,0:T(4,128)(2,1)S(1)}, u32[]{:S(2)}, u32[]{:S(2)}) collective-permute-start(bf16[24,4,128]{2,1,0:T(4,128)(2,1)} %shard_map.100), channel_id=1, source_target_pairs={{0,4},{4,8},{8,12},{12,16},{16,20},{20,24},{24,28},{1,5},{5,9},{9,... | collective-permute-start | bytes 73736 | tf_op jit(solution)/shard_map/ppermute | solution.py:313
  6.3 1.3 %copy_bitcast_fusion.2 = (bf16[4,512,128]{2,1,0:T(8,128)(2,1)S(1)}, bf16[4,512,128]{2,1,0:T(8,128)(2,1)S(1)}) fusion(bf16[512,4,128]{2,1,0:T(4,128)(2,1)} %refs_2_.1, bf16[512,4,128]{2,1,0:T(4,128)(2,1)} %refs_1_.1), kind=kLoop, calls=%fused_computation.3 | loop fusion | bytes 2097152 | tf_op jit(solution)/shard_map/transpose | solution.py:452
  8.0 4.9 %shard_map.101 = (bf16[2,512,128]{2,1,0:T(8,128)(2,1)S(1)}, f32[2,512,256]{2,1,0:T(8,128)S(1)}, f32[2,3,128,256]{3,2,1,0:T(8,128)S(1)}, bf16[2,128,256]{2,1,0:T(8,128)(2,1)S(1)}) custom-call(s32[8]{0:T(128)S(1)} %copy-done.4, bf16[4,512,128]{2,1,0:T(8,128)(2,1)S(1)} %get-tuple-element.52.key_ref, bf16[4,512,128]{2,1,0:T(8,128)(2,1)S(1)} %get-tuple-element.53.value_ref, ...), custom_call_target="tpu_custom_call" | custom-call | flops 5000000000 | bytes 4194304 | tf_op jit(solution)/shard_map/pallas_call | solution.py:335
  12.9 2.4 %collective-permute-start.1 = (bf16[2,128,256]{2,1,0:T(8,128)(2,1)S(1)}, bf16[2,128,256]{2,1,0:T(8,128)(2,1)S(1)}, u32[]{:S(2)}, u32[]{:S(2)}) collective-permute-start(bf16[2,128,256]{2,1,0:T(8,128)(2,1)S(1)} %get-tuple-element.55.refs_0_), channel_id=1, source_target_pairs={{0,4},{4,0},{8,12},{12,8},{1,5},{5,1},{9,13},{13,9},{2,6},{6,2},{1... | collective-permute-start | bytes 393224 | tf_op jit(solution)/shard_map/ppermute | solution.py:466
  15.3 1.5 %collective-permute-start.2 = (bf16[2,128,256]{2,1,0:T(8,128)(2,1)S(1)}, bf16[2,128,256]{2,1,0:T(8,128)(2,1)S(1)}, u32[]{:S(2)}, u32[]{:S(2)}) collective-permute-start(bf16[2,128,256]{2,1,0:T(8,128)(2,1)S(1)} %get-tuple-element.55.refs_0_), channel_id=1, source_target_pairs={{0,8},{4,12},{8,0},{12,4},{1,9},{5,13},{9,1},{13,5},{2,10},{6,14},... | collective-permute-start | bytes 393224 | tf_op jit(solution)/shard_map/ppermute | solution.py:466
  17.9 4.9 %shard_map.103 = (bf16[2,512,128]{2,1,0:T(8,128)(2,1)S(1)}, f32[2,512,256]{2,1,0:T(8,128)S(1)}, f32[2,3,128,256]{3,2,1,0:T(8,128)S(1)}, bf16[2,128,256]{2,1,0:T(8,128)(2,1)S(1)}) custom-call(s32[8]{0:T(128)S(1)} %copy-done.4, bf16[4,512,128]{2,1,0:T(8,128)(2,1)S(1)} %get-tuple-element.52.key_ref, bf16[4,512,128]{2,1,0:T(8,128)(2,1)S(1)} %get-tuple-element.53.value_ref, ...), custom_call_target="tpu_custom_call" | custom-call | flops 5000000000 | bytes 4194304 | tf_op jit(solution)/shard_map/pallas_call | solution.py:335
  22.7 1.0 %copy-done.6 = f32[2,512,256]{2,1,0:T(8,128)} copy-done((f32[2,512,256]{2,1,0:T(8,128)}, f32[2,512,256]{2,1,0:T(8,128)S(1)}, u32[]{:S(2)}) %copy-start.6) | copy-done | bytes 1048600
  24.6 3.6 %shard_map.102 = (f32[2,512,128]{2,1,0:T(8,128)S(1)}, f32[2,512,128]{2,1,0:T(8,128)S(1)}, f32[2,512,128]{2,1,0:T(8,128)S(1)}) custom-call(s32[8]{0:T(128)S(1)} %copy-done.4, bf16[4,512,128]{2,1,0:T(8,128)(2,1)S(1)} %bitcast.22, bf16[4,512,128]{2,1,0:T(8,128)(2,1)S(1)} %bitcast.20, f32[1,128]{1,0:T(1,128)S(1)} %bitcast.24, ...), custom_call_target="tpu_custom_call" | custom-call | flops 3000000000 | bytes 4194304 | tf_op jit(solution)/shard_map/pallas_call | solution.py:361
  29.0 1.3 %collective-permute-start.4 = (bf16[2,128,128]{2,1,0:T(8,128)(2,1)S(1)}, bf16[2,128,128]{2,1,0:T(8,128)(2,1)S(1)}, u32[]{:S(2)}, u32[]{:S(2)}) collective-permute-start(bf16[2,128,128]{2,1,0:T(8,128)(2,1)S(1)} %get-tuple-element.59), channel_id=1, source_target_pairs={{0,16},{1,17},{2,18},{3,19},{4,20},{5,21},{6,22},{7,23},{8,24},{9,... | collective-permute-start | bytes 196616 | tf_op jit(solution)/shard_map/ppermute | solution.py:313
  30.4 1.2 %collective-permute-start.5 = (bf16[2,128,256]{2,1,0:T(8,128)(2,1)S(1)}, bf16[2,128,256]{2,1,0:T(8,128)(2,1)S(1)}, u32[]{:S(2)}, u32[]{:S(2)}) collective-permute-start(bf16[2,128,256]{2,1,0:T(8,128)(2,1)S(1)} %get-tuple-element.72.refs_0_), channel_id=1, source_target_pairs={{0,4},{4,0},{8,12},{12,8},{1,5},{5,1},{9,13},{13,9},{2,6},{6,2},{1... | collective-permute-start | bytes 393224 | tf_op jit(solution)/shard_map/ppermute | solution.py:466
  31.5 1.5 %collective-permute-start.6 = (bf16[2,128,256]{2,1,0:T(8,128)(2,1)S(1)}, bf16[2,128,256]{2,1,0:T(8,128)(2,1)S(1)}, u32[]{:S(2)}, u32[]{:S(2)}) collective-permute-start(bf16[2,128,256]{2,1,0:T(8,128)(2,1)S(1)} %get-tuple-element.72.refs_0_), channel_id=1, source_target_pairs={{0,8},{4,12},{8,0},{12,4},{1,9},{5,13},{9,1},{13,5},{2,10},{6,14},... | collective-permute-start | bytes 393224 | tf_op jit(solution)/shard_map/ppermute | solution.py:466
  34.8 1.8 %collective-permute-start.9 = (bf16[512,256]{1,0:T(8,128)(2,1)S(1)}, bf16[512,256]{1,0:T(8,128)(2,1)S(1)}, u32[]{:S(2)}, u32[]{:S(2)}) collective-permute-start(bf16[512,256]{1,0:T(8,128)(2,1)S(1)} %shard_map.105), channel_id=1, source_target_pairs={{0,1},{1,2},{2,3},{3,0},{4,5},{5,6},{6,7},{7,4},{8,9},{9,10},{10,1... | collective-permute-start | bytes 786440 | tf_op jit(solution)/shard_map/ppermute | solution.py:502
  36.6 3.6 %shard_map.106 = (f32[2,512,128]{2,1,0:T(8,128)S(1)}, f32[2,512,128]{2,1,0:T(8,128)S(1)}, f32[2,512,128]{2,1,0:T(8,128)S(1)}) custom-call(s32[8]{0:T(128)S(1)} %copy-done.4, bf16[4,512,128]{2,1,0:T(8,128)(2,1)S(1)} %bitcast.23, bf16[4,512,128]{2,1,0:T(8,128)(2,1)S(1)} %bitcast.21, f32[1,128]{1,0:T(1,128)S(1)} %bitcast.25, ...), custom_call_target="tpu_custom_call" | custom-call | flops 3000000000 | bytes 4194304 | tf_op jit(solution)/shard_map/pallas_call | solution.py:361
  40.9 1.3 %collective-permute-start.8 = (bf16[2,128,128]{2,1,0:T(8,128)(2,1)S(1)}, bf16[2,128,128]{2,1,0:T(8,128)(2,1)S(1)}, u32[]{:S(2)}, u32[]{:S(2)}) collective-permute-start(bf16[2,128,128]{2,1,0:T(8,128)(2,1)S(1)} %get-tuple-element.76), channel_id=1, source_target_pairs={{0,16},{1,17},{2,18},{3,19},{4,20},{5,21},{6,22},{7,23},{8,24},{9,... | collective-permute-start | bytes 196616 | tf_op jit(solution)/shard_map/ppermute | solution.py:313
  44.0 1.6 %collective-permute-start.10 = (bf16[512,256]{1,0:T(8,128)(2,1)S(1)}, bf16[512,256]{1,0:T(8,128)(2,1)S(1)}, u32[]{:S(2)}, u32[]{:S(2)}) collective-permute-start(bf16[512,256]{1,0:T(8,128)(2,1)S(1)} %shard_map.108), channel_id=1, source_target_pairs={{0,1},{1,2},{2,3},{3,0},{4,5},{5,6},{6,7},{7,4},{8,9},{9,10},{10,1... | collective-permute-start | bytes 786440 | tf_op jit(solution)/shard_map/ppermute | solution.py:502
  46.1 1.6 %collective-permute-start.11 = (bf16[512,256]{1,0:T(8,128)(2,1)S(1)}, bf16[512,256]{1,0:T(8,128)(2,1)S(1)}, u32[]{:S(2)}, u32[]{:S(2)}) collective-permute-start(bf16[512,256]{1,0:T(8,128)(2,1)S(1)} %collective-permute-done.9), channel_id=1, source_target_pairs={{0,1},{1,2},{2,3},{3,0},{4,5},{5,6},{6,7},{7,4},{8,9},{9,10},{10,1... | collective-permute-start | bytes 786440 | tf_op jit(solution)/shard_map/ppermute | solution.py:502
  48.1 6.8 %collective-permute-done.10 = bf16[512,256]{1,0:T(8,128)(2,1)S(1)} collective-permute-done((bf16[512,256]{1,0:T(8,128)(2,1)S(1)}, bf16[512,256]{1,0:T(8,128)(2,1)S(1)}, u32[]{:S(2)}, u32[]{:S(2)}) %collective-permute-start.10) | collective-permute-done | bytes 262176 | tf_op jit(solution)/shard_map/ppermute | solution.py:502
  55.4 5.2 %collective-permute-done.11 = bf16[512,256]{1,0:T(8,128)(2,1)S(1)} collective-permute-done((bf16[512,256]{1,0:T(8,128)(2,1)S(1)}, bf16[512,256]{1,0:T(8,128)(2,1)S(1)}, u32[]{:S(2)}, u32[]{:S(2)}) %collective-permute-start.11) | collective-permute-done | bytes 262176 | tf_op jit(solution)/shard_map/ppermute | solution.py:502
  61.0 5.2 %collective-permute-done.12 = bf16[512,256]{1,0:T(8,128)(2,1)S(1)} collective-permute-done((bf16[512,256]{1,0:T(8,128)(2,1)S(1)}, bf16[512,256]{1,0:T(8,128)(2,1)S(1)}, u32[]{:S(2)}, u32[]{:S(2)}) %collective-permute-start.12) | collective-permute-done | bytes 262176 | tf_op jit(solution)/shard_map/ppermute | solution.py:502
  66.9 4.9 %collective-permute-done.13.block_ref = bf16[512,256]{1,0:T(8,128)(2,1)S(1)} collective-permute-done((bf16[512,256]{1,0:T(8,128)(2,1)S(1)}, bf16[512,256]{1,0:T(8,128)(2,1)S(1)}, u32[]{:S(2)}, u32[]{:S(2)}) %collective-permute-start.13) | collective-permute-done | bytes 262176 | tf_op jit(solution)/shard_map/ppermute | solution.py:502
  71.8 1.0 %shard_map.109.total_ref = f32[512,1024]{1,0:T(8,128)S(1)} custom-call(s32[1]{0:T(128)} %bitcast.1.section, f32[512,1024]{1,0:T(8,128)S(1)} %add_add_fusion.total_ref, bf16[512,256]{1,0:T(8,128)(2,1)S(1)} %collective-permute-done.13.block_ref, bf16[2048,1024]{1,0:T(8,128)(2,1)S(1)} %copy-done), custom_call_target="tpu_custom_call" | custom-call | flops 268435456 | bytes 2097152 | tf_op jit(solution)/shard_map/pallas_call | solution.py:411
  72.8 4.1 %collective-permute-done.14.block_ref = bf16[512,256]{1,0:T(8,128)(2,1)S(1)} collective-permute-done((bf16[512,256]{1,0:T(8,128)(2,1)S(1)}, bf16[512,256]{1,0:T(8,128)(2,1)S(1)}, u32[]{:S(2)}, u32[]{:S(2)}) %collective-permute-start.14) | collective-permute-done | bytes 262176 | tf_op jit(solution)/shard_map/ppermute | solution.py:502
  76.9 2.1 %shard_map.110 = bf16[512,1024]{1,0:T(8,128)(2,1)} custom-call(s32[1]{0:T(128)} %bitcast.section, f32[512,1024]{1,0:T(8,128)S(1)} %shard_map.109.total_ref, bf16[512,256]{1,0:T(8,128)(2,1)S(1)} %collective-permute-done.14.block_ref, bf16[2048,1024]{1,0:T(8,128)(2,1)S(1)} %copy-done), custom_call_target="tpu_custom_call" | custom-call | flops 268435456 | bytes 2097152 | tf_op jit(solution)/shard_map/pallas_call | solution.py:411
  (50 shorter events, 9.8 us)
Async XLA Ops:
  0.0 8.0 %copy-start.3 = (f32[4,512]{1,0:T(4,128)S(1)}, f32[4,512]{1,0:T(4,128)}, u32[]{:S(2)}) copy-start(f32[4,512]{1,0:T(4,128)} %strength_ref.7) | copy-start | bytes 24580
  0.0 8.0 %copy-start.2 = (f32[4,512]{1,0:T(4,128)S(1)}, f32[4,512]{1,0:T(4,128)}, u32[]{:S(2)}) copy-start(f32[4,512]{1,0:T(4,128)} %decay_ref.7) | copy-start | bytes 24580
  0.0 8.0 %copy-start.4 = (s32[8]{0:T(128)S(1)}, s32[8]{0:T(128)}, u32[]{:S(2)}) copy-start(s32[8]{0:T(128)} %resets.7) | copy-start | bytes 100
  0.0 8.0 %copy-start.1 = (f32[3,4,4,128]{3,2,1,0:T(4,128)S(1)}, f32[3,4,4,128]{3,2,1,0:T(4,128)}, u32[]{:S(2)}) copy-start(f32[3,4,4,128]{3,2,1,0:T(4,128)} %taps_ref.7) | copy-start | bytes 73732
  1.4 6.6 %collective-permute-start = (bf16[24,4,128]{2,1,0:T(4,128)(2,1)}, bf16[24,4,128]{2,1,0:T(4,128)(2,1)S(1)}, u32[]{:S(2)}, u32[]{:S(2)}) collective-permute-start(bf16[24,4,128]{2,1,0:T(4,128)(2,1)} %shard_map.100), channel_id=1, source_target_pairs={{0,4},{4,8},{8,12},{12,16},{16,20},{20,24},{24,28},{1,5},{5,9},{9,... | collective-permute-start | bytes 73736 | tf_op jit(solution)/shard_map/ppermute | solution.py:313
  8.0 9.7 %copy-start.11 = (bf16[512,4,128]{2,1,0:T(4,128)(2,1)S(1)}, bf16[512,4,128]{2,1,0:T(4,128)(2,1)}, u32[]{:S(2)}) copy-start(bf16[512,4,128]{2,1,0:T(4,128)(2,1)} %param.13) | copy-start | bytes 1572868
  8.0 9.7 %copy-start.10 = (bf16[512,4,128]{2,1,0:T(4,128)(2,1)S(1)}, bf16[512,4,128]{2,1,0:T(4,128)(2,1)}, u32[]{:S(2)}) copy-start(bf16[512,4,128]{2,1,0:T(4,128)(2,1)} %refs_0_.1) | copy-start | bytes 1572868
  12.9 15.3 %collective-permute-start.1 = (bf16[2,128,256]{2,1,0:T(8,128)(2,1)S(1)}, bf16[2,128,256]{2,1,0:T(8,128)(2,1)S(1)}, u32[]{:S(2)}, u32[]{:S(2)}) collective-permute-start(bf16[2,128,256]{2,1,0:T(8,128)(2,1)S(1)} %get-tuple-element.55.refs_0_), channel_id=1, source_target_pairs={{0,4},{4,0},{8,12},{12,8},{1,5},{5,1},{9,13},{13,9},{2,6},{6,2},{1... | collective-permute-start | bytes 393224 | tf_op jit(solution)/shard_map/ppermute | solution.py:466
  15.3 12.9 %collective-permute-start.2 = (bf16[2,128,256]{2,1,0:T(8,128)(2,1)S(1)}, bf16[2,128,256]{2,1,0:T(8,128)(2,1)S(1)}, u32[]{:S(2)}, u32[]{:S(2)}) collective-permute-start(bf16[2,128,256]{2,1,0:T(8,128)(2,1)S(1)} %get-tuple-element.55.refs_0_), channel_id=1, source_target_pairs={{0,8},{4,12},{8,0},{12,4},{1,9},{5,13},{9,1},{13,5},{2,10},{6,14},... | collective-permute-start | bytes 393224 | tf_op jit(solution)/shard_map/ppermute | solution.py:466
  16.8 11.4 %collective-permute-start.3 = (bf16[2,128,256]{2,1,0:T(8,128)(2,1)S(1)}, bf16[2,128,256]{2,1,0:T(8,128)(2,1)S(1)}, u32[]{:S(2)}, u32[]{:S(2)}) collective-permute-start(bf16[2,128,256]{2,1,0:T(8,128)(2,1)S(1)} %get-tuple-element.55.refs_0_), channel_id=1, source_target_pairs={{0,12},{4,8},{8,4},{12,0},{1,13},{5,9},{9,5},{13,1},{2,14},{6,10},... | collective-permute-start | bytes 393224 | tf_op jit(solution)/shard_map/ppermute | solution.py:466
  17.8 6.8 %copy-start.5 = (f32[128]{0:T(128)S(1)}, f32[128]{0:T(128)}, u32[]{:S(2)}) copy-start(f32[128]{0:T(128)} %param.18) | copy-start | bytes 1540
  29.0 4.9 %collective-permute-start.4 = (bf16[2,128,128]{2,1,0:T(8,128)(2,1)S(1)}, bf16[2,128,128]{2,1,0:T(8,128)(2,1)S(1)}, u32[]{:S(2)}, u32[]{:S(2)}) collective-permute-start(bf16[2,128,128]{2,1,0:T(8,128)(2,1)S(1)} %get-tuple-element.59), channel_id=1, source_target_pairs={{0,16},{1,17},{2,18},{3,19},{4,20},{5,21},{6,22},{7,23},{8,24},{9,... | collective-permute-start | bytes 196616 | tf_op jit(solution)/shard_map/ppermute | solution.py:313
  30.3 6.2 %copy-start.7 = (f32[2,512,256]{2,1,0:T(8,128)S(1)}, f32[2,512,256]{2,1,0:T(8,128)}, u32[]{:S(2)}) copy-start(f32[2,512,256]{2,1,0:T(8,128)} %copy-done.6) | copy-start | bytes 3145732
  30.3 6.2 %copy-start.9 = (f32[2,3,128,256]{3,2,1,0:T(8,128)S(1)}, f32[2,3,128,256]{3,2,1,0:T(8,128)}, u32[]{:S(2)}) copy-start(f32[2,3,128,256]{3,2,1,0:T(8,128)} %copy-done.8) | copy-start | bytes 2359300
  30.4 9.8 %collective-permute-start.5 = (bf16[2,128,256]{2,1,0:T(8,128)(2,1)S(1)}, bf16[2,128,256]{2,1,0:T(8,128)(2,1)S(1)}, u32[]{:S(2)}, u32[]{:S(2)}) collective-permute-start(bf16[2,128,256]{2,1,0:T(8,128)(2,1)S(1)} %get-tuple-element.72.refs_0_), channel_id=1, source_target_pairs={{0,4},{4,0},{8,12},{12,8},{1,5},{5,1},{9,13},{13,9},{2,6},{6,2},{1... | collective-permute-start | bytes 393224 | tf_op jit(solution)/shard_map/ppermute | solution.py:466
  31.5 8.7 %collective-permute-start.6 = (bf16[2,128,256]{2,1,0:T(8,128)(2,1)S(1)}, bf16[2,128,256]{2,1,0:T(8,128)(2,1)S(1)}, u32[]{:S(2)}, u32[]{:S(2)}) collective-permute-start(bf16[2,128,256]{2,1,0:T(8,128)(2,1)S(1)} %get-tuple-element.72.refs_0_), channel_id=1, source_target_pairs={{0,8},{4,12},{8,0},{12,4},{1,9},{5,13},{9,1},{13,5},{2,10},{6,14},... | collective-permute-start | bytes 393224 | tf_op jit(solution)/shard_map/ppermute | solution.py:466
  33.0 7.2 %collective-permute-start.7 = (bf16[2,128,256]{2,1,0:T(8,128)(2,1)S(1)}, bf16[2,128,256]{2,1,0:T(8,128)(2,1)S(1)}, u32[]{:S(2)}, u32[]{:S(2)}) collective-permute-start(bf16[2,128,256]{2,1,0:T(8,128)(2,1)S(1)} %get-tuple-element.72.refs_0_), channel_id=1, source_target_pairs={{0,12},{4,8},{8,4},{12,0},{1,13},{5,9},{9,5},{13,1},{2,14},{6,10},... | collective-permute-start | bytes 393224 | tf_op jit(solution)/shard_map/ppermute | solution.py:466
  34.8 11.3 %collective-permute-start.9 = (bf16[512,256]{1,0:T(8,128)(2,1)S(1)}, bf16[512,256]{1,0:T(8,128)(2,1)S(1)}, u32[]{:S(2)}, u32[]{:S(2)}) collective-permute-start(bf16[512,256]{1,0:T(8,128)(2,1)S(1)} %shard_map.105), channel_id=1, source_target_pairs={{0,1},{1,2},{2,3},{3,0},{4,5},{5,6},{6,7},{7,4},{8,9},{9,10},{10,1... | collective-permute-start | bytes 786440 | tf_op jit(solution)/shard_map/ppermute | solution.py:502
  40.9 2.2 %collective-permute-start.8 = (bf16[2,128,128]{2,1,0:T(8,128)(2,1)S(1)}, bf16[2,128,128]{2,1,0:T(8,128)(2,1)S(1)}, u32[]{:S(2)}, u32[]{:S(2)}) collective-permute-start(bf16[2,128,128]{2,1,0:T(8,128)(2,1)S(1)} %get-tuple-element.76), channel_id=1, source_target_pairs={{0,16},{1,17},{2,18},{3,19},{4,20},{5,21},{6,22},{7,23},{8,24},{9,... | collective-permute-start | bytes 196616 | tf_op jit(solution)/shard_map/ppermute | solution.py:313
  44.0 11.0 %collective-permute-start.10 = (bf16[512,256]{1,0:T(8,128)(2,1)S(1)}, bf16[512,256]{1,0:T(8,128)(2,1)S(1)}, u32[]{:S(2)}, u32[]{:S(2)}) collective-permute-start(bf16[512,256]{1,0:T(8,128)(2,1)S(1)} %shard_map.108), channel_id=1, source_target_pairs={{0,1},{1,2},{2,3},{3,0},{4,5},{5,6},{6,7},{7,4},{8,9},{9,10},{10,1... | collective-permute-start | bytes 786440 | tf_op jit(solution)/shard_map/ppermute | solution.py:502
  46.1 14.5 %collective-permute-start.11 = (bf16[512,256]{1,0:T(8,128)(2,1)S(1)}, bf16[512,256]{1,0:T(8,128)(2,1)S(1)}, u32[]{:S(2)}, u32[]{:S(2)}) collective-permute-start(bf16[512,256]{1,0:T(8,128)(2,1)S(1)} %collective-permute-done.9), channel_id=1, source_target_pairs={{0,1},{1,2},{2,3},{3,0},{4,5},{5,6},{6,7},{7,4},{8,9},{9,10},{10,1... | collective-permute-start | bytes 786440 | tf_op jit(solution)/shard_map/ppermute | solution.py:502
  55.0 11.2 %collective-permute-start.12 = (bf16[512,256]{1,0:T(8,128)(2,1)S(1)}, bf16[512,256]{1,0:T(8,128)(2,1)S(1)}, u32[]{:S(2)}, u32[]{:S(2)}) collective-permute-start(bf16[512,256]{1,0:T(8,128)(2,1)S(1)} %collective-permute-done.10), channel_id=1, source_target_pairs={{0,1},{1,2},{2,3},{3,0},{4,5},{5,6},{6,7},{7,4},{8,9},{9,10},{10,1... | collective-permute-start | bytes 786440 | tf_op jit(solution)/shard_map/ppermute | solution.py:502
  60.6 11.2 %collective-permute-start.13 = (bf16[512,256]{1,0:T(8,128)(2,1)S(1)}, bf16[512,256]{1,0:T(8,128)(2,1)S(1)}, u32[]{:S(2)}, u32[]{:S(2)}) collective-permute-start(bf16[512,256]{1,0:T(8,128)(2,1)S(1)} %collective-permute-done.11), channel_id=1, source_target_pairs={{0,1},{1,2},{2,3},{3,0},{4,5},{5,6},{6,7},{7,4},{8,9},{9,10},{10,1... | collective-permute-start | bytes 786440 | tf_op jit(solution)/shard_map/ppermute | solution.py:502
  66.2 10.7 %collective-permute-start.14 = (bf16[512,256]{1,0:T(8,128)(2,1)S(1)}, bf16[512,256]{1,0:T(8,128)(2,1)S(1)}, u32[]{:S(2)}, u32[]{:S(2)}) collective-permute-start(bf16[512,256]{1,0:T(8,128)(2,1)S(1)} %collective-permute-done.12), channel_id=1, source_target_pairs={{0,1},{1,2},{2,3},{3,0},{4,5},{5,6},{6,7},{7,4},{8,9},{9,10},{10,1... | collective-permute-start | bytes 786440 | tf_op jit(solution)/shard_map/ppermute | solution.py:502
  (3 other events, 7.6 us)

commit v5 on v4

--- a/solution.py
+++ b/solution.py
@@ -13,6 +13,8 @@
 RIM = 8
 EPSILON = 1e-06
 FAR = -1e30
+LARGE = 1e38
+AGAIN = 16
 F32 = jnp.float32
 BF16 = jnp.bfloat16
 NN = (((1,), (0,)), ((), ()))
@@ -64,18 +66,22 @@
     return cum, strength, jnp.transpose(jnp.concatenate(stacked, axis=0))
 
 
-def convolve(x_ref, rims, taps_ref, which, head, padded, store):
-    length = x_ref.shape[1]
-    padded[0:RIM] = rims[which * RIM : (which + 1) * RIM, head, :]
-    padded[RIM : RIM + length] = x_ref[head].astype(F32)
-    count = taps_ref.shape[1]
-    taps = [taps_ref[which, j, head : head + 1, :] for j in range(count)]
-    for c in range(length // CHUNK):
-        begin = c * CHUNK + RIM + 1 - count
-        total = taps[0] * padded[begin : begin + CHUNK]
-        for j in range(1, count):
-            total = total + taps[j] * padded[begin + j : begin + j + CHUNK]
-        store(c, total / (1.0 + jnp.exp(-total)))
+def silu(x):
+    below = jnp.minimum(1.0 + jnp.exp(-x), LARGE)
+    inverse = pl.reciprocal(below, approx=True)
+    return x * (inverse * (2.0 - below * inverse))
+
+
+def filtered(padded, taps, begin, length):
+    first = begin + RIM + 1 - len(taps)
+    total = taps[0] * padded[first : first + length]
+    for j in range(1, len(taps)):
+        total = total + taps[j] * padded[first + j : first + j + length]
+    return silu(total)
+
+
+def taps_of(taps_ref, which, head):
+    return [taps_ref[which, j, pl.ds(head, 1), :] for j in range(taps_ref.shape[1])]
 
 
 def unit(rows):
@@ -91,7 +97,6 @@
     eye = (row == col).astype(F32)
     in_block = (differ < 8).astype(F32)
     diagonal = [low * in_block for low in lowers]
-    rounded_lowers = [low.astype(BF16) for low in lowers]
     powers = [d.astype(BF16) for d in diagonal]
     squares = [mul(p, p).astype(BF16) for p in powers]
     inverse = [eye - d for d in diagonal]
@@ -100,12 +105,39 @@
     inverse = [x + mul(x.astype(BF16), s) for x, s in zip(inverse, fourths)]
     size = 8
     while size < CHUNK:
-        joint = ((differ >= size) & (differ < 2 * size)).astype(F32).astype(BF16)
+        joint = odd_blocks(((differ >= size) & (differ < 2 * size)).astype(F32), size)
         rounded = [x.astype(BF16) for x in inverse]
-        inner = [mul(low * joint, x).astype(BF16) for low, x in zip(rounded_lowers, rounded)]
-        inverse = [x - mul(r, i) for x, r, i in zip(inverse, rounded, inner)]
+        inner = [
+            mul((odd_blocks(low, size) * joint).astype(BF16), x)
+            for low, x in zip(lowers, rounded)
+        ]
+        outer = [
+            mul(odd_blocks(x, size).astype(BF16), with_even_zeros(i, size).astype(BF16))
+            for x, i in zip(inverse, inner)
+        ]
+        inverse = [less_in_odd(x, o, size) for x, o in zip(inverse, outer)]
         size *= 2
     return inverse
+
+
+def odd_blocks(a, size):
+    return jnp.concatenate([a[b : b + size] for b in range(size, a.shape[0], 2 * size)], axis=0)
+
+
+def with_even_zeros(odd, size):
+    zeros = jnp.zeros((size, odd.shape[1]), odd.dtype)
+    pieces = []
+    for b in range(0, odd.shape[0], size):
+        pieces += [zeros, odd[b : b + size]]
+    return jnp.concatenate(pieces, axis=0)
+
+
+def less_in_odd(a, odd, size):
+    pieces = []
+    for b in range(0, odd.shape[0], size):
+        pieces.append(a[2 * b : 2 * b + size])
+        pieces.append(a[2 * b + size : 2 * b + 2 * size] - odd[b : b + size])
+    return jnp.concatenate(pieces, axis=0)
 
 
 def rims_kernel(*refs):
@@ -121,8 +153,31 @@
         copy.wait()
 
 
+def filters_kernel(key_ref, value_ref, taps_ref, unit_ref, value_out_ref, first_ref, padded):
+    length, heads, _ = key_ref.shape
+    for i, x_ref in enumerate((key_ref, value_ref)):
+        for c in range(length // CHUNK):
+            begin = RIM + c * CHUNK
+            padded[i, :, begin : begin + CHUNK] = jnp.swapaxes(x_ref[rows_of(c)], 0, 1).astype(F32)
+        padded[i, :, 0:RIM] = jnp.zeros((heads, RIM, padded.shape[3]), F32)
+        first_ref[i] = padded[i, :, RIM : RIM + AGAIN]
+
+    def one_head(h, carry):
+        for i in range(2):
+            taps = taps_of(taps_ref, 1 + i, h)
+            for c in range(length // CHUNK):
+                rows = filtered(padded.at[i, h], taps, c * CHUNK, CHUNK)
+                if i == 0:
+                    unit_ref[h, rows_of(c)] = unit(rows).astype(BF16)
+                else:
+                    value_out_ref[h, rows_of(c)] = rows.astype(BF16)
+        return carry
+
+    lax.fori_loop(0, heads, one_head, 0)
+
+
 def maps_kernel(
-    base, resets, key_ref, value_ref, rim_ref, taps_ref, decay_ref, strength_ref,
+    base, resets, unit_in_ref, value_in_ref, first_ref, rim_ref, taps_ref, decay_ref, strength_ref,
     unit_ref, solved_ref, starts_ref, map_ref,
     rims, padded, value_s, step_s,
 ):
@@ -132,20 +187,22 @@
     row, col = indices()
     rims[...] = rim_ref[...].astype(F32)
     for g in range(heads):
-
-        def store_key(c, rows):
-            unit_ref[g, rows_of(c)] = unit(rows).astype(BF16)
-
-        def store_value(c, rows):
-            value_s[g, rows_of(c)] = rows.astype(BF16)
-
-        convolve(key_ref, rims, taps_ref, 1, base + g, padded, store_key)
-        convolve(value_ref, rims, taps_ref, 2, base + g, padded, store_value)
+        h = base + g
+        unit_ref[g] = unit_in_ref[h]
+        value_s[g] = value_in_ref[h]
+        for i in range(2):
+            padded[g, i, 0:RIM] = rims[(1 + i) * RIM : (2 + i) * RIM, h, :]
+            padded[g, i, RIM : RIM + AGAIN] = first_ref[i, h]
+            rows = filtered(padded.at[g, i], taps_of(taps_ref, 1 + i, h), 0, AGAIN)
+            if i == 0:
+                unit_ref[g, 0:AGAIN] = unit(rows).astype(BF16)
+            else:
+                value_s[g, 0:AGAIN] = rows.astype(BF16)
 
     parts = []
     lowers = []
     for c in range(chunks):
-        cum, strengths, columns = token_scalars(decay_ref, strength_ref, c)
+        cum, _, columns = token_scalars(decay_ref, strength_ref, c)
         first, second = resets[2 * c], resets[2 * c + 1]
         strictly = (row > col) & same_document(second, row, col)
         for g in range(heads):
@@ -156,28 +213,28 @@
             fading = jnp.exp(jnp.where(strictly, cum_col - cum_row, FAR))
             strength_col = columns[:, total_heads + h : total_heads + h + 1]
             lowers.append(strength_col * fading * mul(key, key, NT))
-            parts.append((g, c, first, second, cum_col, cum_row, strengths[h : h + 1]))
+            parts.append((g, c, first, second, cum_col, cum_row, strength_col))
     inverses = lower_inverse(lowers, row, col)
-    in_first = lax.broadcasted_iota(jnp.int32, (1, CHUNK), 1) < BLOCK
+    eye = (row == col).astype(F32)
     first_rows = lax.broadcasted_iota(jnp.int32, (CHUNK, 1), 0) < BLOCK
-    for (g, c, first, second, cum_col, cum_row, strength_row), inverse in zip(parts, inverses):
+    for (g, c, first, second, cum_col, cum_row, strength_col), inverse in zip(parts, inverses):
         keep_first = (1 - first).astype(F32)
         keep_second = (1 - second).astype(F32)
         keep_both = keep_first * keep_second
         key = unit_ref[g, rows_of(c)]
-        value = value_s[g, rows_of(c)]
-        growth_row = jnp.exp(cum_row) * jnp.where(in_first, keep_first, keep_both)
-        by_strength = inverse * strength_row
-        high, low = split(by_strength * growth_row)
-        write_keys = mul(high, key) + mul(low, key)
-        high, low = split(by_strength)
-        local_values = mul(high, value) + mul(low, value)
-        solved = jnp.concatenate([write_keys, local_values], axis=1)
+        growth = jnp.exp(cum_col) * jnp.where(first_rows, keep_first, keep_both)
+        targets = jnp.concatenate(
+            [
+                (strength_col * growth) * key.astype(F32),
+                strength_col * value_s[g, rows_of(c)].astype(F32),
+            ],
+            axis=1,
+        )
+        solved = targets + mul((inverse - eye).astype(BF16), targets.astype(BF16))
         solved_ref[g, rows_of(c)] = solved
         end = cum_row[:, CHUNK - 1 : CHUNK]
         tail = jnp.exp(end - cum_col) * jnp.where(first_rows, keep_second, 1.0)
-        high, low = split(tail * solved)
-        product = mul(key, high, TN) + mul(key, low, TN)
+        product = mul(key, (tail * solved).astype(BF16), TN)
         passed = jnp.exp(end) * keep_both
         step_s[g, c, :, :depth] = jnp.where(row == col, passed, 0.0) - product[:, :depth]
         step_s[g, c, :, depth:] = product[:, depth:]
@@ -187,7 +244,9 @@
         for g in range(heads):
             starts_ref[g, c - 1] = states[g]
             step = step_s[g, c]
-            joined = mul_split(step[:, :depth], states[g])
+            trans = step[:, :depth].astype(BF16)
+            high, low = split(states[g])
+            joined = mul(trans, high) + mul(trans, low)
             states[g] = jnp.concatenate(
                 [joined[:, :depth], joined[:, depth:] + step[:, depth:]], axis=1
             )
@@ -207,11 +266,13 @@
     first_rows = lax.broadcasted_iota(jnp.int32, (CHUNK, 1), 0) < BLOCK
     rims[...] = rim_ref[...].astype(F32)
     for g in range(heads):
-
-        def store_query(c, rows):
+        h = base + g
+        padded[g, 0:RIM] = rims[0:RIM, h, :]
+        padded[g, RIM : RIM + length] = query_ref[h].astype(F32)
+        taps = taps_of(taps_ref, 0, h)
+        for c in range(chunks):
+            rows = filtered(padded.at[g], taps, c * CHUNK, CHUNK)
             query_s[g, rows_of(c)] = (unit(rows) * depth**-0.5).astype(BF16)
-
-        convolve(query_ref, rims, taps_ref, 0, base + g, padded, store_query)
 
     for c in range(chunks):
         here = rows_of(c)
@@ -234,10 +295,10 @@
                 both = mul_split(reach, starts_ref[g, c - 1])
                 reach = both[:, :depth]
                 part = part + both[:, depth:]
-            reach_ref[g, here] = reach
+            reach_ref[g, here] = reach.astype(BF16)
             part_ref[g, here] = part
             gate = gate_ref[h, here].astype(F32)
-            gating_ref[g, here] = gain_ref[...] * (gate / (1.0 + jnp.exp(-gate)))
+            gating_ref[g, here] = gain_ref[...] * silu(gate)
 
 
 def partner(place, k, count):
@@ -294,10 +355,8 @@
         high, low = split(incoming)
         for c in range(length // CHUNK):
             here = rows_of(c)
-            reach_high, reach_low = split(reach_ref[g, here])
-            core = part_ref[g, here] + (
-                mul(reach_high, high) + (mul(reach_high, low) + mul(reach_low, high))
-            )
+            reach = reach_ref[g, here]
+            core = part_ref[g, here] + (mul(reach, high) + mul(reach, low))
             scale = lax.rsqrt(jnp.sum(core * core, axis=-1, keepdims=True) / depth + EPSILON)
             normed_ref[here, g * depth : (g + 1) * depth] = (
                 core * scale * gating_ref[g, here]
@@ -305,7 +364,20 @@
 
 
 def projected_kernel(section, total_ref, block_ref, weights_ref, out_ref):
-    out_ref[...] = (total_ref[...] + mul(block_ref[...], weights_ref[...])).astype(out_ref.dtype)
+    out_ref[...] = total_ref[...] + mul(block_ref[...], weights_ref[...])
+
+
+def last_kernel(section, total_ref, block_ref, weights_ref, out_ref, tiles, written):
+    width = block_ref.shape[1]
+    rows = weights_ref[pl.ds(pl.multiple_of(section[0] * width, width), width), :]
+    copies = []
+    for i in range(total_ref.shape[0] // CHUNK):
+        here = rows_of(i)
+        tiles[here] = (total_ref[here] + mul(block_ref[here], rows)).astype(BF16)
+        copies.append(pltpu.make_async_copy(tiles.at[here], out_ref.at[here], written.at[i]))
+        copies[-1].start()
+    for copy in copies:
+        copy.wait()
 
 
 def from_behind(value, axis, steps):
@@ -315,7 +387,7 @@
 
 VMEM = pl.BlockSpec(memory_space=pltpu.VMEM)
 SMEM = pl.BlockSpec(memory_space=pltpu.SMEM)
-PARAMS = pltpu.CompilerParams(vmem_limit_bytes=16 * 1024 * 1024)
+PARAMS = pltpu.CompilerParams(vmem_limit_bytes=12 * 1024 * 1024)
 
 
 def pack_rims(inputs):
@@ -329,8 +401,24 @@
     )(*inputs)
 
 
-def maps_of(base, heads, resets, key, value, rims, taps, decay, strength):
-    _, length, depth = key.shape
+def filters_of(key_in, value_in, taps):
+    length, heads, depth = key_in.shape
+    per_token = jax.ShapeDtypeStruct((heads, length, depth), BF16)
+    return pl.pallas_call(
+        filters_kernel,
+        out_shape=(per_token, per_token, jax.ShapeDtypeStruct((2, heads, AGAIN, depth), F32)),
+        in_specs=[VMEM] * 3,
+        out_specs=[VMEM] * 3,
+        scratch_shapes=[pltpu.VMEM((2, heads, length + RIM, depth), F32)],
+        compiler_params=PARAMS,
+        cost_estimate=pl.CostEstimate(
+            flops=3 * 10**9, bytes_accessed=4 * 2**20, transcendentals=10**6
+        ),
+    )(key_in, value_in, taps)
+
+
+def maps_of(base, heads, resets, unit_in, value_in, first, rims, taps, decay, strength):
+    _, length, depth = unit_in.shape
     chunks = length // CHUNK
     return pl.pallas_call(
         functools.partial(maps_kernel, base),
@@ -340,11 +428,11 @@
             jax.ShapeDtypeStruct((heads, chunks - 1, depth, 2 * depth), F32),
             jax.ShapeDtypeStruct((heads, depth, 2 * depth), BF16),
         ),
-        in_specs=[SMEM] + [VMEM] * 6,
+        in_specs=[SMEM] + [VMEM] * 7,
         out_specs=[VMEM] * 4,
         scratch_shapes=[
             pltpu.VMEM(rims.shape, F32),
-            pltpu.VMEM((length + RIM, depth), F32),
+            pltpu.VMEM((heads, 2, RIM + AGAIN, depth), F32),
             pltpu.VMEM((heads, length, depth), BF16),
             pltpu.VMEM((heads, chunks, depth, 2 * depth), F32),
         ],
@@ -352,7 +440,7 @@
         cost_estimate=pl.CostEstimate(
             flops=5 * 10**9, bytes_accessed=4 * 2**20, transcendentals=10**6
         ),
-    )(resets, key, value, rims, taps, decay, strength)
+    )(resets, unit_in, value_in, first, rims, taps, decay, strength)
 
 
 def reads_of(base, heads, resets, query, gate, gain, rims, taps, decay, strength, made):
@@ -360,12 +448,12 @@
     per_token = jax.ShapeDtypeStruct((heads, length, depth), F32)
     return pl.pallas_call(
         functools.partial(reads_kernel, base),
-        out_shape=(per_token, per_token, per_token),
+        out_shape=(jax.ShapeDtypeStruct(per_token.shape, BF16), per_token, per_token),
         in_specs=[SMEM] + [VMEM] * 10,
         out_specs=[VMEM] * 3,
         scratch_shapes=[
             pltpu.VMEM(rims.shape, F32),
-            pltpu.VMEM((length + RIM, depth), F32),
+            pltpu.VMEM((heads, length + RIM, depth), F32),
             pltpu.VMEM((heads, length, depth), BF16),
         ],
         compiler_params=PARAMS,
@@ -405,12 +493,12 @@
     )(arrived, before, *reads)
 
 
-def projected(section, total, block, weights, dtype):
+def projected(section, total, block, weights):
     length, columns = total.shape
     width = block.shape[1]
     return pl.pallas_call(
         projected_kernel,
-        out_shape=jax.ShapeDtypeStruct(total.shape, dtype),
+        out_shape=jax.ShapeDtypeStruct(total.shape, F32),
         grid_spec=pltpu.PrefetchScalarGridSpec(
             num_scalar_prefetch=1,
             grid=(length // CHUNK,),
@@ -430,6 +518,20 @@
     )(section.astype(jnp.int32).reshape(1), total, block, weights)
 
 
+def last_projected(section, total, block, weights):
+    return pl.pallas_call(
+        last_kernel,
+        out_shape=jax.ShapeDtypeStruct(total.shape, BF16),
+        in_specs=[SMEM] + [VMEM] * 3,
+        out_specs=pl.BlockSpec(memory_space=pl.ANY),
+        scratch_shapes=[
+            pltpu.VMEM(total.shape, BF16),
+            pltpu.SemaphoreType.DMA((total.shape[0] // CHUNK,)),
+        ],
+        compiler_params=PARAMS,
+    )(section.astype(jnp.int32).reshape(1), total, block, weights)
+
+
 def after(first, *values):
     return lax.optimization_barrier((first, *values))[1:]
 
@@ -449,7 +551,7 @@
     length, heads, depth = query_in.shape
     size = heads // GROUPS
     rims = from_behind(pack_rims((query_in, key_in, value_in)), ("chain", "leaf"), 1)
-    key, value = (jnp.transpose(x, (1, 0, 2)) for x in (key_in, value_in))
+    key, value, first = filters_of(key_in, value_in, conv_weight)
     gain = output_norm_gain.reshape(1, depth)
     leaves = lax.axis_size("leaf")
     place = lax.axis_index("leaf").astype(jnp.int32).reshape(1)
@@ -458,7 +560,8 @@
     exchanged = []
     for g in range(GROUPS):
         unit_key, solved, starts, own_map = maps_of(
-            g * size, size, doc_resets, key, value, rims, conv_weight, log_decay, write_strength
+            g * size, size, doc_resets, key, value, first, rims, conv_weight, log_decay,
+            write_strength,
         )
         made.append((unit_key, solved, starts))
         exchanged.append(
@@ -503,8 +606,8 @@
         for g, block in enumerate(blocks):
             section = owner * GROUPS + g
             if k + 1 == ring:
-                dtype = BF16 if g + 1 == GROUPS else F32
-                mixed = projected(section, mixed, block, output_projection_weight, dtype)
+                add = last_projected if g + 1 == GROUPS else projected
+                mixed = add(section, mixed, block, output_projection_weight)
                 continue
             rows = lax.dynamic_slice_in_dim(output_projection_weight, section * width, width, 0)
             term = jnp.dot(block, rows, preferred_element_type=F32)

time: 79.2 us -> 80.7 us (1.019)
  local copies, waits for them, and re-layouts: 3.4 us -> 6.31 us
  starting transfers between devices: 20.8 us -> 19.6 us
    unnamed x24 -> x30, local copies, waits for them, and re-layouts: 1.92 us -> 6.18 us
    pallas_call x2 -> x4, Pallas kernels: 7.18 us -> 10.9 us  [the longest x2 7.18 us: reads_of(): pl.pallas_call(functools.partial(reads_kernel, base), out_shape=(jax.Shap...]
    pallas_call x2 -> x1, Pallas kernels: 3.11 us -> 0.98 us  [projected(): pl.pallas_call(projected_kernel, out_shape=jax.ShapeDtypeStruct(total.sha...]
    pallas_call x2, Pallas kernels: 9.73 us -> 8.08 us  [maps_of(): pl.pallas_call(functools.partial(maps_kernel, base), out_shape=(jax.Shape...]
    ppermute x6, starting transfers between devices: 8.33 us -> 7.11 us  [on_device(): lax.ppermute(own_map, 'leaf', pairs_at(k, leaves))]
    transpose x1, local copies, waits for them, and re-layouts: 1.34 us -> 0.14 us  [on_device(): query, gate = (jnp.transpose(x, (1, 0, 2)) for x in (query_in, gate_in))]
  transfers between devices with their start and end apart: 15 -> 15, of which waited for: 7 -> 6; matrix products, arithmetic and copies ran while one was open for 6% -> 4% of each run, Pallas kernels for 20% -> 21%
where the time goes in v5:
time: 80.7 us; the launch traced here: 80.2 us
  waiting for transfers between devices  26.6 us (33%)
  Pallas kernels  24.3 us (30%)
  starting transfers between devices  19.6 us (24%)
  local copies, waits for them, and re-layouts  6.31 us (8%)
  matrix products  2.94 us (4%)
    ppermute x6, waiting for transfers between devices, on_device(): following = [lax.ppermute(block, 'head', around) for block in blocks]  26.1 us
    pallas_call x2, Pallas kernels, maps_of(): pl.pallas_call(functools.partial(maps_kernel, base), out_shape=(jax.Shape...  8.08 us
    ppermute x3, starting transfers between devices, from_behind(): lax.ppermute(value, axis, [(i, i + steps) for i in range(count - steps)])  7.43 us
    pallas_call x2, Pallas kernels, reads_of(): pl.pallas_call(functools.partial(reads_kernel, base), out_shape=(jax.Shap...  7.18 us
    ppermute x6, starting transfers between devices, on_device(): lax.ppermute(own_map, 'leaf', pairs_at(k, leaves))  7.11 us
    unnamed x30, local copies, waits for them, and re-layouts  6.18 us
    ppermute x6, starting transfers between devices, on_device(): following = [lax.ppermute(block, 'head', around) for block in blocks]  5.07 us
    dot_general x6, matrix products, on_device(): term = jnp.dot(block, rows, preferred_element_type=F32)  2.94 us
  transfers between devices with their start and end apart: 15, of which 6 were waited for; matrix products, arithmetic and copies ran while one was open for 4% of the time, Pallas kernels for 21%

profile of v5, /device:TPU:0, one launch (start us, length us, event | category | flops | bytes accessed | tf_op | source)
XLA Modules:
  0.0 80.2 jit_solution(15550673641001358065)
XLA Ops:
  0.0 1.4 %shard_map.101 = bf16[24,4,128]{2,1,0:T(4,128)(2,1)} custom-call(bf16[512,4,128]{2,1,0:T(4,128)(2,1)} %refs_0_.1, bf16[512,4,128]{2,1,0:T(4,128)(2,1)} %refs_1_.1, bf16[512,4,128]{2,1,0:T(4,128)(2,1)} %refs_2_.1), custom_call_target="tpu_custom_call" | custom-call | tf_op jit(solution)/shard_map/pallas_call | solution.py:395
  1.4 4.8 %collective-permute-start = (bf16[24,4,128]{2,1,0:T(4,128)(2,1)}, bf16[24,4,128]{2,1,0:T(4,128)(2,1)S(1)}, u32[]{:S(2)}, u32[]{:S(2)}) collective-permute-start(bf16[24,4,128]{2,1,0:T(4,128)(2,1)} %shard_map.101), channel_id=1, source_target_pairs={{0,4},{4,8},{8,12},{12,16},{16,20},{20,24},{24,28},{1,5},{5,9},{9,... | collective-permute-start | bytes 73736 | tf_op jit(solution)/shard_map/ppermute | solution.py:385
  9.1 2.5 %shard_map.100 = (bf16[4,512,128]{2,1,0:T(8,128)(2,1)S(1)}, bf16[4,512,128]{2,1,0:T(8,128)(2,1)S(1)}, f32[2,4,16,128]{3,2,1,0:T(8,128)S(1)}) custom-call(bf16[512,4,128]{2,1,0:T(4,128)(2,1)S(1)} %copy-done.1, bf16[512,4,128]{2,1,0:T(4,128)(2,1)S(1)} %copy-done.2, f32[3,4,4,128]{3,2,1,0:T(4,128)S(1)} %copy-done.3), custom_call_target="tpu_custom_call" | custom-call | flops 3000000000 | bytes 4194304 | tf_op jit(solution)/shard_map/pallas_call | solution.py:407
  11.6 4.0 %shard_map.102 = (bf16[2,512,128]{2,1,0:T(8,128)(2,1)S(1)}, f32[2,512,256]{2,1,0:T(8,128)S(1)}, f32[2,3,128,256]{3,2,1,0:T(8,128)S(1)}, bf16[2,128,256]{2,1,0:T(8,128)(2,1)S(1)}) custom-call(s32[8]{0:T(128)S(1)} %copy-done.7, bf16[4,512,128]{2,1,0:T(8,128)(2,1)S(1)} %get-tuple-element.58.unit_in_ref, ...), custom_call_target="tpu_custom_call" | custom-call | flops 5000000000 | bytes 4194304 | tf_op jit(solution)/shard_map/pallas_call | solution.py:423
  15.7 1.6 %collective-permute-start.1 = (bf16[2,128,256]{2,1,0:T(8,128)(2,1)S(1)}, bf16[2,128,256]{2,1,0:T(8,128)(2,1)S(1)}, u32[]{:S(2)}, u32[]{:S(2)}) collective-permute-start(bf16[2,128,256]{2,1,0:T(8,128)(2,1)S(1)} %get-tuple-element.61.refs_0_), channel_id=1, source_target_pairs={{0,4},{4,0},{8,12},{12,8},{1,5},{5,1},{9,13},{13,9},{2,6},{6,2},{1... | collective-permute-start | bytes 393224 | tf_op jit(solution)/shard_map/ppermute | solution.py:569
  17.3 1.9 %collective-permute-start.3 = (bf16[2,128,256]{2,1,0:T(8,128)(2,1)S(1)}, bf16[2,128,256]{2,1,0:T(8,128)(2,1)S(1)}, u32[]{:S(2)}, u32[]{:S(2)}) collective-permute-start(bf16[2,128,256]{2,1,0:T(8,128)(2,1)S(1)} %get-tuple-element.61.refs_0_), channel_id=1, source_target_pairs={{0,12},{4,8},{8,4},{12,0},{1,13},{5,9},{9,5},{13,1},{2,14},{6,10},... | collective-permute-start | bytes 393224 | tf_op jit(solution)/shard_map/ppermute | solution.py:569
  19.4 4.0 %shard_map.104 = (bf16[2,512,128]{2,1,0:T(8,128)(2,1)S(1)}, f32[2,512,256]{2,1,0:T(8,128)S(1)}, f32[2,3,128,256]{3,2,1,0:T(8,128)S(1)}, bf16[2,128,256]{2,1,0:T(8,128)(2,1)S(1)}) custom-call(s32[8]{0:T(128)S(1)} %copy-done.7, bf16[4,512,128]{2,1,0:T(8,128)(2,1)S(1)} %get-tuple-element.58.unit_in_ref, ...), custom_call_target="tpu_custom_call" | custom-call | flops 5000000000 | bytes 4194304 | tf_op jit(solution)/shard_map/pallas_call | solution.py:423
  24.4 3.6 %shard_map.103 = (bf16[2,512,128]{2,1,0:T(8,128)(2,1)S(1)}, f32[2,512,128]{2,1,0:T(8,128)S(1)}, f32[2,512,128]{2,1,0:T(8,128)S(1)}) custom-call(s32[8]{0:T(128)S(1)} %copy-done.7, bf16[4,512,128]{2,1,0:T(8,128)(2,1)S(1)} %get-tuple-element.70.query_ref, bf16[4,512,128]{2,1,0:T(8,128)(2,1)S(1)} %get-tuple-element.71.gate_ref, f32[1,128]{1,0:T(1,128)S(1)} %bitcast.14, ...), custom_call_target="tpu_custom_call" | custom-call | flops 3000000000 | bytes 4194304 | tf_op jit(solution)/shard_map/pallas_call | solution.py:449
  28.8 1.3 %collective-permute-start.4 = (bf16[2,128,128]{2,1,0:T(8,128)(2,1)S(1)}, bf16[2,128,128]{2,1,0:T(8,128)(2,1)S(1)}, u32[]{:S(2)}, u32[]{:S(2)}) collective-permute-start(bf16[2,128,128]{2,1,0:T(8,128)(2,1)S(1)} %get-tuple-element.65), channel_id=1, source_target_pairs={{0,16},{1,17},{2,18},{3,19},{4,20},{5,21},{6,22},{7,23},{8,24},{9,... | collective-permute-start | bytes 196616 | tf_op jit(solution)/shard_map/ppermute | solution.py:385
  30.2 1.6 %collective-permute-start.5 = (bf16[2,128,256]{2,1,0:T(8,128)(2,1)S(1)}, bf16[2,128,256]{2,1,0:T(8,128)(2,1)S(1)}, u32[]{:S(2)}, u32[]{:S(2)}) collective-permute-start(bf16[2,128,256]{2,1,0:T(8,128)(2,1)S(1)} %get-tuple-element.78.refs_0_), channel_id=1, source_target_pairs={{0,4},{4,0},{8,12},{12,8},{1,5},{5,1},{9,13},{13,9},{2,6},{6,2},{1... | collective-permute-start | bytes 393224 | tf_op jit(solution)/shard_map/ppermute | solution.py:569
  31.8 1.9 %collective-permute-start.7 = (bf16[2,128,256]{2,1,0:T(8,128)(2,1)S(1)}, bf16[2,128,256]{2,1,0:T(8,128)(2,1)S(1)}, u32[]{:S(2)}, u32[]{:S(2)}) collective-permute-start(bf16[2,128,256]{2,1,0:T(8,128)(2,1)S(1)} %get-tuple-element.78.refs_0_), channel_id=1, source_target_pairs={{0,12},{4,8},{8,4},{12,0},{1,13},{5,9},{9,5},{13,1},{2,14},{6,10},... | collective-permute-start | bytes 393224 | tf_op jit(solution)/shard_map/ppermute | solution.py:569
  34.4 1.8 %collective-permute-start.9 = (bf16[512,256]{1,0:T(8,128)(2,1)S(1)}, bf16[512,256]{1,0:T(8,128)(2,1)S(1)}, u32[]{:S(2)}, u32[]{:S(2)}) collective-permute-start(bf16[512,256]{1,0:T(8,128)(2,1)S(1)} %shard_map.106), channel_id=1, source_target_pairs={{0,1},{1,2},{2,3},{3,0},{4,5},{5,6},{6,7},{7,4},{8,9},{9,10},{10,1... | collective-permute-start | bytes 786440 | tf_op jit(solution)/shard_map/ppermute | solution.py:605
  36.3 1.2 %copy-done.10 = f32[2,512,256]{2,1,0:T(8,128)S(1)} copy-done((f32[2,512,256]{2,1,0:T(8,128)S(1)}, f32[2,512,256]{2,1,0:T(8,128)}, u32[]{:S(2)}) %copy-start.10) | copy-done | bytes 1048600
  37.5 1.1 %copy-done.12 = f32[2,3,128,256]{3,2,1,0:T(8,128)S(1)} copy-done((f32[2,3,128,256]{3,2,1,0:T(8,128)S(1)}, f32[2,3,128,256]{3,2,1,0:T(8,128)}, u32[]{:S(2)}) %copy-start.12) | copy-done | bytes 786456
  38.6 3.6 %shard_map.107 = (bf16[2,512,128]{2,1,0:T(8,128)(2,1)S(1)}, f32[2,512,128]{2,1,0:T(8,128)S(1)}, f32[2,512,128]{2,1,0:T(8,128)S(1)}) custom-call(s32[8]{0:T(128)S(1)} %copy-done.7, bf16[4,512,128]{2,1,0:T(8,128)(2,1)S(1)} %get-tuple-element.70.query_ref, bf16[4,512,128]{2,1,0:T(8,128)(2,1)S(1)} %get-tuple-element.71.gate_ref, f32[1,128]{1,0:T(1,128)S(1)} %bitcast.15, ...), custom_call_target="tpu_custom_call" | custom-call | flops 3000000000 | bytes 4194304 | tf_op jit(solution)/shard_map/pallas_call | solution.py:449
  43.0 1.3 %collective-permute-start.8 = (bf16[2,128,128]{2,1,0:T(8,128)(2,1)S(1)}, bf16[2,128,128]{2,1,0:T(8,128)(2,1)S(1)}, u32[]{:S(2)}, u32[]{:S(2)}) collective-permute-start(bf16[2,128,128]{2,1,0:T(8,128)(2,1)S(1)} %get-tuple-element.82), channel_id=1, source_target_pairs={{0,16},{1,17},{2,18},{3,19},{4,20},{5,21},{6,22},{7,23},{8,24},{9,... | collective-permute-start | bytes 196616 | tf_op jit(solution)/shard_map/ppermute | solution.py:385
  45.9 1.6 %collective-permute-start.10 = (bf16[512,256]{1,0:T(8,128)(2,1)S(1)}, bf16[512,256]{1,0:T(8,128)(2,1)S(1)}, u32[]{:S(2)}, u32[]{:S(2)}) collective-permute-start(bf16[512,256]{1,0:T(8,128)(2,1)S(1)} %shard_map.109), channel_id=1, source_target_pairs={{0,1},{1,2},{2,3},{3,0},{4,5},{5,6},{6,7},{7,4},{8,9},{9,10},{10,1... | collective-permute-start | bytes 786440 | tf_op jit(solution)/shard_map/ppermute | solution.py:605
  48.0 1.6 %collective-permute-start.11 = (bf16[512,256]{1,0:T(8,128)(2,1)S(1)}, bf16[512,256]{1,0:T(8,128)(2,1)S(1)}, u32[]{:S(2)}, u32[]{:S(2)}) collective-permute-start(bf16[512,256]{1,0:T(8,128)(2,1)S(1)} %collective-permute-done.9), channel_id=1, source_target_pairs={{0,1},{1,2},{2,3},{3,0},{4,5},{5,6},{6,7},{7,4},{8,9},{9,10},{10,1... | collective-permute-start | bytes 786440 | tf_op jit(solution)/shard_map/ppermute | solution.py:605
  50.1 6.8 %collective-permute-done.10 = bf16[512,256]{1,0:T(8,128)(2,1)S(1)} collective-permute-done((bf16[512,256]{1,0:T(8,128)(2,1)S(1)}, bf16[512,256]{1,0:T(8,128)(2,1)S(1)}, u32[]{:S(2)}, u32[]{:S(2)}) %collective-permute-start.10) | collective-permute-done | bytes 262176 | tf_op jit(solution)/shard_map/ppermute | solution.py:605
  57.3 5.2 %collective-permute-done.11 = bf16[512,256]{1,0:T(8,128)(2,1)S(1)} collective-permute-done((bf16[512,256]{1,0:T(8,128)(2,1)S(1)}, bf16[512,256]{1,0:T(8,128)(2,1)S(1)}, u32[]{:S(2)}, u32[]{:S(2)}) %collective-permute-start.11) | collective-permute-done | bytes 262176 | tf_op jit(solution)/shard_map/ppermute | solution.py:605
  63.0 5.2 %collective-permute-done.12 = bf16[512,256]{1,0:T(8,128)(2,1)S(1)} collective-permute-done((bf16[512,256]{1,0:T(8,128)(2,1)S(1)}, bf16[512,256]{1,0:T(8,128)(2,1)S(1)}, u32[]{:S(2)}, u32[]{:S(2)}) %collective-permute-start.12) | collective-permute-done | bytes 262176 | tf_op jit(solution)/shard_map/ppermute | solution.py:605
  68.9 4.9 %collective-permute-done.13.block_ref = bf16[512,256]{1,0:T(8,128)(2,1)S(1)} collective-permute-done((bf16[512,256]{1,0:T(8,128)(2,1)S(1)}, bf16[512,256]{1,0:T(8,128)(2,1)S(1)}, u32[]{:S(2)}, u32[]{:S(2)}) %collective-permute-start.13) | collective-permute-done | bytes 262176 | tf_op jit(solution)/shard_map/ppermute | solution.py:605
  74.7 4.1 %collective-permute-done.14.block_ref = bf16[512,256]{1,0:T(8,128)(2,1)S(1)} collective-permute-done((bf16[512,256]{1,0:T(8,128)(2,1)S(1)}, bf16[512,256]{1,0:T(8,128)(2,1)S(1)}, u32[]{:S(2)}, u32[]{:S(2)}) %collective-permute-start.14) | collective-permute-done | bytes 262176 | tf_op jit(solution)/shard_map/ppermute | solution.py:605
  78.8 1.3 %shard_map.111 = bf16[512,1024]{1,0:T(8,128)(2,1)} custom-call(s32[1]{0:T(128)} %bitcast.section, f32[512,1024]{1,0:T(8,128)S(1)} %shard_map.110.total_ref, bf16[512,256]{1,0:T(8,128)(2,1)S(1)} %collective-permute-done.14.block_ref, bf16[2048,1024]{1,0:T(8,128)(2,1)S(1)} %copy-done), custom_call_target="tpu_custom_call" | custom-call | tf_op jit(solution)/shard_map/pallas_call | solution.py:522
  (55 shorter events, 11.5 us)
Async XLA Ops:
  1.4 10.2 %collective-permute-start = (bf16[24,4,128]{2,1,0:T(4,128)(2,1)}, bf16[24,4,128]{2,1,0:T(4,128)(2,1)S(1)}, u32[]{:S(2)}, u32[]{:S(2)}) collective-permute-start(bf16[24,4,128]{2,1,0:T(4,128)(2,1)} %shard_map.101), channel_id=1, source_target_pairs={{0,4},{4,8},{8,12},{12,16},{16,20},{20,24},{24,28},{1,5},{5,9},{9,... | collective-permute-start | bytes 73736 | tf_op jit(solution)/shard_map/ppermute | solution.py:385
  9.0 2.5 %copy-start.4 = (f32[3,4,4,128]{3,2,1,0:T(4,128)S(1)}, f32[3,4,4,128]{3,2,1,0:T(4,128)}, u32[]{:S(2)}) copy-start(f32[3,4,4,128]{3,2,1,0:T(4,128)} %taps_ref.9) | copy-start | bytes 73732
  9.0 2.5 %copy-start.5 = (f32[4,512]{1,0:T(4,128)S(1)}, f32[4,512]{1,0:T(4,128)}, u32[]{:S(2)}) copy-start(f32[4,512]{1,0:T(4,128)} %decay_ref.7) | copy-start | bytes 24580
  9.1 2.5 %copy-start.6 = (f32[4,512]{1,0:T(4,128)S(1)}, f32[4,512]{1,0:T(4,128)}, u32[]{:S(2)}) copy-start(f32[4,512]{1,0:T(4,128)} %strength_ref.7) | copy-start | bytes 24580
  9.1 2.6 %copy-start.7 = (s32[8]{0:T(128)S(1)}, s32[8]{0:T(128)}, u32[]{:S(2)}) copy-start(s32[8]{0:T(128)} %resets.7) | copy-start | bytes 100
  11.6 7.6 %copy-start.13 = (bf16[512,4,128]{2,1,0:T(4,128)(2,1)S(1)}, bf16[512,4,128]{2,1,0:T(4,128)(2,1)}, u32[]{:S(2)}) copy-start(bf16[512,4,128]{2,1,0:T(4,128)(2,1)} %refs_0_.1) | copy-start | bytes 1572868
  11.6 7.6 %copy-start.14 = (bf16[512,4,128]{2,1,0:T(4,128)(2,1)S(1)}, bf16[512,4,128]{2,1,0:T(4,128)(2,1)}, u32[]{:S(2)}) copy-start(bf16[512,4,128]{2,1,0:T(4,128)(2,1)} %param.13) | copy-start | bytes 1572868
  15.7 12.4 %collective-permute-start.1 = (bf16[2,128,256]{2,1,0:T(8,128)(2,1)S(1)}, bf16[2,128,256]{2,1,0:T(8,128)(2,1)S(1)}, u32[]{:S(2)}, u32[]{:S(2)}) collective-permute-start(bf16[2,128,256]{2,1,0:T(8,128)(2,1)S(1)} %get-tuple-element.61.refs_0_), channel_id=1, source_target_pairs={{0,4},{4,0},{8,12},{12,8},{1,5},{5,1},{9,13},{13,9},{2,6},{6,2},{1... | collective-permute-start | bytes 393224 | tf_op jit(solution)/shard_map/ppermute | solution.py:569
  17.2 10.8 %collective-permute-start.2 = (bf16[2,128,256]{2,1,0:T(8,128)(2,1)S(1)}, bf16[2,128,256]{2,1,0:T(8,128)(2,1)S(1)}, u32[]{:S(2)}, u32[]{:S(2)}) collective-permute-start(bf16[2,128,256]{2,1,0:T(8,128)(2,1)S(1)} %get-tuple-element.61.refs_0_), channel_id=1, source_target_pairs={{0,8},{4,12},{8,0},{12,4},{1,9},{5,13},{9,1},{13,5},{2,10},{6,14},... | collective-permute-start | bytes 393224 | tf_op jit(solution)/shard_map/ppermute | solution.py:569
  17.3 10.7 %collective-permute-start.3 = (bf16[2,128,256]{2,1,0:T(8,128)(2,1)S(1)}, bf16[2,128,256]{2,1,0:T(8,128)(2,1)S(1)}, u32[]{:S(2)}, u32[]{:S(2)}) collective-permute-start(bf16[2,128,256]{2,1,0:T(8,128)(2,1)S(1)} %get-tuple-element.61.refs_0_), channel_id=1, source_target_pairs={{0,12},{4,8},{8,4},{12,0},{1,13},{5,9},{9,5},{13,1},{2,14},{6,10},... | collective-permute-start | bytes 393224 | tf_op jit(solution)/shard_map/ppermute | solution.py:569
  19.4 5.0 %copy-start.8 = (f32[128]{0:T(128)S(1)}, f32[128]{0:T(128)}, u32[]{:S(2)}) copy-start(f32[128]{0:T(128)} %param.18) | copy-start | bytes 1540
  24.4 3.6 %copy-start.11 = (f32[2,3,128,256]{3,2,1,0:T(8,128)}, f32[2,3,128,256]{3,2,1,0:T(8,128)S(1)}, u32[]{:S(2)}) copy-start(f32[2,3,128,256]{3,2,1,0:T(8,128)S(1)} %get-tuple-element.74.starts_ref) | copy-start | bytes 2359300
  28.8 4.9 %collective-permute-start.4 = (bf16[2,128,128]{2,1,0:T(8,128)(2,1)S(1)}, bf16[2,128,128]{2,1,0:T(8,128)(2,1)S(1)}, u32[]{:S(2)}, u32[]{:S(2)}) collective-permute-start(bf16[2,128,128]{2,1,0:T(8,128)(2,1)S(1)} %get-tuple-element.65), channel_id=1, source_target_pairs={{0,16},{1,17},{2,18},{3,19},{4,20},{5,21},{6,22},{7,23},{8,24},{9,... | collective-permute-start | bytes 196616 | tf_op jit(solution)/shard_map/ppermute | solution.py:385
  30.2 12.1 %collective-permute-start.5 = (bf16[2,128,256]{2,1,0:T(8,128)(2,1)S(1)}, bf16[2,128,256]{2,1,0:T(8,128)(2,1)S(1)}, u32[]{:S(2)}, u32[]{:S(2)}) collective-permute-start(bf16[2,128,256]{2,1,0:T(8,128)(2,1)S(1)} %get-tuple-element.78.refs_0_), channel_id=1, source_target_pairs={{0,4},{4,0},{8,12},{12,8},{1,5},{5,1},{9,13},{13,9},{2,6},{6,2},{1... | collective-permute-start | bytes 393224 | tf_op jit(solution)/shard_map/ppermute | solution.py:569
  31.7 10.5 %collective-permute-start.6 = (bf16[2,128,256]{2,1,0:T(8,128)(2,1)S(1)}, bf16[2,128,256]{2,1,0:T(8,128)(2,1)S(1)}, u32[]{:S(2)}, u32[]{:S(2)}) collective-permute-start(bf16[2,128,256]{2,1,0:T(8,128)(2,1)S(1)} %get-tuple-element.78.refs_0_), channel_id=1, source_target_pairs={{0,8},{4,12},{8,0},{12,4},{1,9},{5,13},{9,1},{13,5},{2,10},{6,14},... | collective-permute-start | bytes 393224 | tf_op jit(solution)/shard_map/ppermute | solution.py:569
  31.8 10.4 %collective-permute-start.7 = (bf16[2,128,256]{2,1,0:T(8,128)(2,1)S(1)}, bf16[2,128,256]{2,1,0:T(8,128)(2,1)S(1)}, u32[]{:S(2)}, u32[]{:S(2)}) collective-permute-start(bf16[2,128,256]{2,1,0:T(8,128)(2,1)S(1)} %get-tuple-element.78.refs_0_), channel_id=1, source_target_pairs={{0,12},{4,8},{8,4},{12,0},{1,13},{5,9},{9,5},{13,1},{2,14},{6,10},... | collective-permute-start | bytes 393224 | tf_op jit(solution)/shard_map/ppermute | solution.py:569
  34.4 13.5 %collective-permute-start.9 = (bf16[512,256]{1,0:T(8,128)(2,1)S(1)}, bf16[512,256]{1,0:T(8,128)(2,1)S(1)}, u32[]{:S(2)}, u32[]{:S(2)}) collective-permute-start(bf16[512,256]{1,0:T(8,128)(2,1)S(1)} %shard_map.106), channel_id=1, source_target_pairs={{0,1},{1,2},{2,3},{3,0},{4,5},{5,6},{6,7},{7,4},{8,9},{9,10},{10,1... | collective-permute-start | bytes 786440 | tf_op jit(solution)/shard_map/ppermute | solution.py:605
  38.6 5.7 %copy-start = (bf16[2048,1024]{1,0:T(8,128)(2,1)S(1)}, bf16[2048,1024]{1,0:T(8,128)(2,1)}, u32[]{:S(2)}) copy-start(bf16[2048,1024]{1,0:T(8,128)(2,1)} %weights_ref.3) | copy-start | bytes 12582916
  43.0 2.2 %collective-permute-start.8 = (bf16[2,128,128]{2,1,0:T(8,128)(2,1)S(1)}, bf16[2,128,128]{2,1,0:T(8,128)(2,1)S(1)}, u32[]{:S(2)}, u32[]{:S(2)}) collective-permute-start(bf16[2,128,128]{2,1,0:T(8,128)(2,1)S(1)} %get-tuple-element.82), channel_id=1, source_target_pairs={{0,16},{1,17},{2,18},{3,19},{4,20},{5,21},{6,22},{7,23},{8,24},{9,... | collective-permute-start | bytes 196616 | tf_op jit(solution)/shard_map/ppermute | solution.py:385
  45.9 11.0 %collective-permute-start.10 = (bf16[512,256]{1,0:T(8,128)(2,1)S(1)}, bf16[512,256]{1,0:T(8,128)(2,1)S(1)}, u32[]{:S(2)}, u32[]{:S(2)}) collective-permute-start(bf16[512,256]{1,0:T(8,128)(2,1)S(1)} %shard_map.109), channel_id=1, source_target_pairs={{0,1},{1,2},{2,3},{3,0},{4,5},{5,6},{6,7},{7,4},{8,9},{9,10},{10,1... | collective-permute-start | bytes 786440 | tf_op jit(solution)/shard_map/ppermute | solution.py:605
  48.0 14.5 %collective-permute-start.11 = (bf16[512,256]{1,0:T(8,128)(2,1)S(1)}, bf16[512,256]{1,0:T(8,128)(2,1)S(1)}, u32[]{:S(2)}, u32[]{:S(2)}) collective-permute-start(bf16[512,256]{1,0:T(8,128)(2,1)S(1)} %collective-permute-done.9), channel_id=1, source_target_pairs={{0,1},{1,2},{2,3},{3,0},{4,5},{5,6},{6,7},{7,4},{8,9},{9,10},{10,1... | collective-permute-start | bytes 786440 | tf_op jit(solution)/shard_map/ppermute | solution.py:605
  56.9 11.2 %collective-permute-start.12 = (bf16[512,256]{1,0:T(8,128)(2,1)S(1)}, bf16[512,256]{1,0:T(8,128)(2,1)S(1)}, u32[]{:S(2)}, u32[]{:S(2)}) collective-permute-start(bf16[512,256]{1,0:T(8,128)(2,1)S(1)} %collective-permute-done.10), channel_id=1, source_target_pairs={{0,1},{1,2},{2,3},{3,0},{4,5},{5,6},{6,7},{7,4},{8,9},{9,10},{10,1... | collective-permute-start | bytes 786440 | tf_op jit(solution)/shard_map/ppermute | solution.py:605
  62.5 11.2 %collective-permute-start.13 = (bf16[512,256]{1,0:T(8,128)(2,1)S(1)}, bf16[512,256]{1,0:T(8,128)(2,1)S(1)}, u32[]{:S(2)}, u32[]{:S(2)}) collective-permute-start(bf16[512,256]{1,0:T(8,128)(2,1)S(1)} %collective-permute-done.11), channel_id=1, source_target_pairs={{0,1},{1,2},{2,3},{3,0},{4,5},{5,6},{6,7},{7,4},{8,9},{9,10},{10,1... | collective-permute-start | bytes 786440 | tf_op jit(solution)/shard_map/ppermute | solution.py:605
  68.1 10.7 %collective-permute-start.14 = (bf16[512,256]{1,0:T(8,128)(2,1)S(1)}, bf16[512,256]{1,0:T(8,128)(2,1)S(1)}, u32[]{:S(2)}, u32[]{:S(2)}) collective-permute-start(bf16[512,256]{1,0:T(8,128)(2,1)S(1)} %collective-permute-done.12), channel_id=1, source_target_pairs={{0,1},{1,2},{2,3},{3,0},{4,5},{5,6},{6,7},{7,4},{8,9},{9,10},{10,1... | collective-permute-start | bytes 786440 | tf_op jit(solution)/shard_map/ppermute | solution.py:605
  (6 other events, 6.2 us)

commit v6 on v5

--- a/solution.py
+++ b/solution.py
@@ -153,27 +153,41 @@
         copy.wait()
 
 
-def filters_kernel(key_ref, value_ref, taps_ref, unit_ref, value_out_ref, first_ref, padded):
-    length, heads, _ = key_ref.shape
-    for i, x_ref in enumerate((key_ref, value_ref)):
-        for c in range(length // CHUNK):
-            begin = RIM + c * CHUNK
-            padded[i, :, begin : begin + CHUNK] = jnp.swapaxes(x_ref[rows_of(c)], 0, 1).astype(F32)
-        padded[i, :, 0:RIM] = jnp.zeros((heads, RIM, padded.shape[3]), F32)
-        first_ref[i] = padded[i, :, RIM : RIM + AGAIN]
-
-    def one_head(h, carry):
+def filters_kernel(
+    key_ref, value_ref, taps_in_ref, unit_ref, value_out_ref, first_ref,
+    raw, padded, taps_ref, arrived, taps_arrived,
+):
+    length, heads, depth = key_ref.shape
+    chunks = length // CHUNK
+    taps_copy = pltpu.make_async_copy(taps_in_ref, taps_ref, taps_arrived)
+    taps_copy.start()
+    copies = {}
+    for c in range(chunks):
+        for i, x_ref in enumerate((key_ref, value_ref)):
+            here = pl.ds(c * CHUNK, CHUNK)
+            copies[c, i] = pltpu.make_async_copy(
+                x_ref.at[here], raw.at[i, here], arrived.at[c, i]
+            )
+            copies[c, i].start()
+    padded[:, :, 0:RIM] = jnp.zeros((2, heads, RIM, depth), F32)
+    taps_copy.wait()
+    for c in range(chunks):
+        begin = RIM + c * CHUNK
         for i in range(2):
-            taps = taps_of(taps_ref, 1 + i, h)
-            for c in range(length // CHUNK):
-                rows = filtered(padded.at[i, h], taps, c * CHUNK, CHUNK)
+            copies[c, i].wait()
+            padded[i, :, begin : begin + CHUNK] = jnp.swapaxes(raw[i, rows_of(c)], 0, 1).astype(F32)
+
+        def one_head(h, carry):
+            for i in range(2):
+                rows = filtered(padded.at[i, h], taps_of(taps_ref, 1 + i, h), c * CHUNK, CHUNK)
                 if i == 0:
                     unit_ref[h, rows_of(c)] = unit(rows).astype(BF16)
                 else:
                     value_out_ref[h, rows_of(c)] = rows.astype(BF16)
-        return carry
-
-    lax.fori_loop(0, heads, one_head, 0)
+            return carry
+
+        lax.fori_loop(0, heads, one_head, 0)
+    first_ref[...] = padded[:, :, RIM : RIM + AGAIN]
 
 
 def maps_kernel(
@@ -239,19 +253,29 @@
         step_s[g, c, :, :depth] = jnp.where(row == col, passed, 0.0) - product[:, :depth]
         step_s[g, c, :, depth:] = product[:, depth:]
 
-    states = [step_s[g, 0] for g in range(heads)]
-    for c in range(1, chunks):
-        for g in range(heads):
+    def compose(later, earlier):
+        high, low = split(earlier)
+        trans = later[:, :depth].astype(BF16)
+        joined = mul(trans, high) + mul(trans, low)
+        return jnp.concatenate([joined[:, :depth], joined[:, depth:] + later[:, depth:]], axis=1)
+
+    every = range(heads)
+    states = [step_s[g, 0] for g in every]
+    half = chunks // 2
+    for c in range(1, half):
+        for g in every:
             starts_ref[g, c - 1] = states[g]
-            step = step_s[g, c]
-            trans = step[:, :depth].astype(BF16)
-            high, low = split(states[g])
-            joined = mul(trans, high) + mul(trans, low)
-            states[g] = jnp.concatenate(
-                [joined[:, :depth], joined[:, depth:] + step[:, depth:]], axis=1
-            )
-    for g in range(heads):
-        map_ref[g] = states[g].astype(BF16)
+        states = [compose(step_s[g, c], states[g]) for g in every]
+    rest = [step_s[g, half] for g in every]
+    for c in range(half + 1, chunks):
+        rest = [compose(step_s[g, c], rest[g]) for g in every]
+    for g in every:
+        map_ref[g] = compose(rest[g], states[g]).astype(BF16)
+    for c in range(half, chunks):
+        for g in every:
+            starts_ref[g, c - 1] = states[g]
+        if c + 1 < chunks:
+            states = [compose(step_s[g, c], states[g]) for g in every]
 
 
 def reads_kernel(
@@ -347,19 +371,20 @@
             ref[h] = states[h][:, :depth]
 
 
-def outputs_kernel(arrived_ref, before_ref, reach_ref, part_ref, gating_ref, normed_ref):
-    heads, length, depth = reach_ref.shape
-    for g in range(heads):
-        before = before_ref[g]
-        incoming = mul_split(before[:, :depth], arrived_ref[g].astype(F32)) + before[:, depth:]
+def outputs_kernel(base, arrived_ref, before_ref, reach_ref, part_ref, gating_ref, normed_ref):
+    _, length, depth = reach_ref.shape
+    for g in range(normed_ref.shape[1] // depth):
+        h = base + g
+        before = before_ref[h]
+        incoming = mul_split(before[:, :depth], arrived_ref[h].astype(F32)) + before[:, depth:]
         high, low = split(incoming)
         for c in range(length // CHUNK):
             here = rows_of(c)
-            reach = reach_ref[g, here]
-            core = part_ref[g, here] + (mul(reach, high) + mul(reach, low))
+            reach = reach_ref[h, here]
+            core = part_ref[h, here] + (mul(reach, high) + mul(reach, low))
             scale = lax.rsqrt(jnp.sum(core * core, axis=-1, keepdims=True) / depth + EPSILON)
             normed_ref[here, g * depth : (g + 1) * depth] = (
-                core * scale * gating_ref[g, here]
+                core * scale * gating_ref[h, here]
             ).astype(BF16)
 
 
@@ -387,6 +412,7 @@
 
 VMEM = pl.BlockSpec(memory_space=pltpu.VMEM)
 SMEM = pl.BlockSpec(memory_space=pltpu.SMEM)
+HBM = pl.BlockSpec(memory_space=pltpu.HBM)
 PARAMS = pltpu.CompilerParams(vmem_limit_bytes=12 * 1024 * 1024)
 
 
@@ -395,21 +421,28 @@
     return pl.pallas_call(
         rims_kernel,
         out_shape=jax.ShapeDtypeStruct((len(inputs) * RIM, heads, depth), BF16),
-        in_specs=[pl.BlockSpec(memory_space=pltpu.HBM)] * len(inputs),
-        out_specs=VMEM,
+        in_specs=[HBM] * len(inputs),
+        out_specs=HBM,
         scratch_shapes=[pltpu.SemaphoreType.DMA((len(inputs),))],
     )(*inputs)
 
 
 def filters_of(key_in, value_in, taps):
     length, heads, depth = key_in.shape
+    chunks = length // CHUNK
     per_token = jax.ShapeDtypeStruct((heads, length, depth), BF16)
     return pl.pallas_call(
         filters_kernel,
         out_shape=(per_token, per_token, jax.ShapeDtypeStruct((2, heads, AGAIN, depth), F32)),
-        in_specs=[VMEM] * 3,
+        in_specs=[HBM] * 3,
         out_specs=[VMEM] * 3,
-        scratch_shapes=[pltpu.VMEM((2, heads, length + RIM, depth), F32)],
+        scratch_shapes=[
+            pltpu.VMEM((2, length, heads, depth), BF16),
+            pltpu.VMEM((2, heads, length + RIM, depth), F32),
+            pltpu.VMEM(taps.shape, F32),
+            pltpu.SemaphoreType.DMA((chunks, 2)),
+            pltpu.SemaphoreType.DMA(()),
+        ],
         compiler_params=PARAMS,
         cost_estimate=pl.CostEstimate(
             flops=3 * 10**9, bytes_accessed=4 * 2**20, transcendentals=10**6
@@ -482,10 +515,10 @@
     )(place, *maps)
 
 
-def outputs_of(arrived, before, reads):
-    heads, length, depth = reads[0].shape
-    return pl.pallas_call(
-        outputs_kernel,
+def outputs_of(base, heads, arrived, before, reads):
+    _, length, depth = reads[0].shape
+    return pl.pallas_call(
+        functools.partial(outputs_kernel, base),
         out_shape=jax.ShapeDtypeStruct((length, heads * depth), BF16),
         in_specs=[VMEM] * 5,
         out_specs=VMEM,
@@ -556,43 +589,30 @@
     leaves = lax.axis_size("leaf")
     place = lax.axis_index("leaf").astype(jnp.int32).reshape(1)
 
-    made = []
-    exchanged = []
+    links = lax.axis_size("chain") - 1
+    *made, own_map = maps_of(
+        0, heads, doc_resets, key, value, first, rims, conv_weight, log_decay, write_strength
+    )
+    maps = [own_map] + [
+        lax.ppermute(own_map, "leaf", pairs_at(k, leaves)) for k in range(1, leaves)
+    ]
+    query_in, gate_in = after(own_map, query_in, gate_in)
+    query, gate = (jnp.transpose(x, (1, 0, 2)) for x in (query_in, gate_in))
+    reads = reads_of(
+        0, heads, doc_resets, query, gate, gain, rims, conv_weight, log_decay, write_strength, made
+    )
+    maps, reads = lax.optimization_barrier((maps, reads))
+    before, state, *trans = join(place, maps, links)
+    arrived = from_behind(state.astype(BF16), "chain", 1)
+    for _ in range(links - 1):
+        passed = jnp.einsum(
+            "hij,hjk->hik", trans[0], arrived.astype(F32), precision=lax.Precision.HIGHEST
+        )
+        arrived = from_behind((passed + state).astype(BF16), "chain", 1)
+    blocks = []
     for g in range(GROUPS):
-        unit_key, solved, starts, own_map = maps_of(
-            g * size, size, doc_resets, key, value, first, rims, conv_weight, log_decay,
-            write_strength,
-        )
-        made.append((unit_key, solved, starts))
-        exchanged.append(
-            [own_map]
-            + [lax.ppermute(own_map, "leaf", pairs_at(k, leaves)) for k in range(1, leaves)]
-        )
-        key, value = after(own_map, key, value)
-        if g == 0:
-            query_in, gate_in = after(own_map, query_in, gate_in)
-    query, gate = (jnp.transpose(x, (1, 0, 2)) for x in (query_in, gate_in))
-
-    blocks = []
-    links = lax.axis_size("chain") - 1
-    for g in range(GROUPS):
-        reads = reads_of(
-            g * size, size, doc_resets, query, gate, gain, rims, conv_weight, log_decay,
-            write_strength, made[g],
-        )
-        maps, reads, _ = lax.optimization_barrier((exchanged[g], reads, exchanged[-1][0]))
-        before, state, *trans = join(place, maps, links)
-        arrived = from_behind(state.astype(BF16), "chain", 1)
-        for _ in range(links - 1):
-            passed = jnp.einsum(
-                "hij,hjk->hik",
-                trans[0],
-                arrived.astype(F32),
-                precision=lax.Precision.HIGHEST,
-            )
-            arrived = from_behind((passed + state).astype(BF16), "chain", 1)
-        blocks.append(outputs_of(arrived, before, reads))
-        query, gate = after(blocks[g], query, gate)
+        blocks.append(outputs_of(g * size, size, arrived, before, reads))
+        arrived = after(blocks[g], arrived)[0]
 
     ring = lax.axis_size("head")
     mine = lax.axis_index("head")

time: 80.7 us -> 85.2 us (1.056)
  waiting for transfers between devices: 26.6 us -> 42.5 us
  starting transfers between devices: 19.6 us -> 14.6 us
  local copies, waits for them, and re-layouts: 6.31 us -> 2.99 us
  Pallas kernels: 24.3 us -> 21.4 us
    ppermute x6, waiting for transfers between devices: 26.1 us -> 36 us  [on_device(): following = [lax.ppermute(block, 'head', around) for block in blocks]]
    ppermute x6 -> x3, waiting for transfers between devices: 0.02 us -> 5.52 us  [on_device(): lax.ppermute(own_map, 'leaf', pairs_at(k, leaves))]
    ppermute x6 -> x3, starting transfers between devices: 7.11 us -> 3.55 us  [on_device(): lax.ppermute(own_map, 'leaf', pairs_at(k, leaves))]
    unnamed x30 -> x22, local copies, waits for them, and re-layouts: 6.18 us -> 2.85 us
    pallas_call x2 -> x1, Pallas kernels: 8.08 us -> 5.04 us  [maps_of(): pl.pallas_call(functools.partial(maps_kernel, base), out_shape=(jax.Shape...]
    pallas_call x1, Pallas kernels: 2.49 us -> 4.4 us  [filters_of(): pl.pallas_call(filters_kernel, out_shape=(per_token, per_token, jax.Shape...]
    pallas_call x2 -> x1, Pallas kernels: 7.18 us -> 5.42 us  [reads_of(): pl.pallas_call(functools.partial(reads_kernel, base), out_shape=(jax.Shap...]
    ppermute x3 -> x2, starting transfers between devices: 7.43 us -> 6.14 us  [from_behind(): lax.ppermute(value, axis, [(i, i + steps) for i in range(count - steps)])]
  transfers between devices with their start and end apart: 15 -> 11, of which waited for: 6 -> 7; matrix products, arithmetic and copies ran while one was open for 4% -> 4% of each run, Pallas kernels for 21% -> 14%
where the time goes in v6:
time: 85.2 us; the launch traced here: 84.9 us
  waiting for transfers between devices  42.5 us (50%)
  Pallas kernels  21.4 us (25%)
  starting transfers between devices  14.6 us (17%)
  matrix products  3.05 us (4%)
  local copies, waits for them, and re-layouts  2.99 us (4%)
    ppermute x6, waiting for transfers between devices, on_device(): following = [lax.ppermute(block, 'head', around) for block in blocks]  36 us
    ppermute x2, starting transfers between devices, from_behind(): lax.ppermute(value, axis, [(i, i + steps) for i in range(count - steps)])  6.14 us
    ppermute x3, waiting for transfers between devices, on_device(): lax.ppermute(own_map, 'leaf', pairs_at(k, leaves))  5.52 us
    pallas_call x1, Pallas kernels, reads_of(): pl.pallas_call(functools.partial(reads_kernel, base), out_shape=(jax.Shap...  5.42 us
    pallas_call x1, Pallas kernels, maps_of(): pl.pallas_call(functools.partial(maps_kernel, base), out_shape=(jax.Shape...  5.04 us
    ppermute x6, starting transfers between devices, on_device(): following = [lax.ppermute(block, 'head', around) for block in blocks]  4.86 us
    pallas_call x1, Pallas kernels, filters_of(): pl.pallas_call(filters_kernel, out_shape=(per_token, per_token, jax.Shape...  4.4 us
    ppermute x3, starting transfers between devices, on_device(): lax.ppermute(own_map, 'leaf', pairs_at(k, leaves))  3.55 us
  transfers between devices with their start and end apart: 11, of which 7 were waited for; matrix products, arithmetic and copies ran while one was open for 4% of the time, Pallas kernels for 14%

profile of v6, /device:TPU:0, one launch (start us, length us, event | category | flops | bytes accessed | tf_op | source)
XLA Modules:
  0.0 84.9 jit_solution(9932571124757547916)
XLA Ops:
  0.0 1.9 %shard_map.101 = bf16[24,4,128]{2,1,0:T(4,128)(2,1)} custom-call(bf16[512,4,128]{2,1,0:T(4,128)(2,1)} %refs_0_.1, bf16[512,4,128]{2,1,0:T(4,128)(2,1)} %refs_1_.1, bf16[512,4,128]{2,1,0:T(4,128)(2,1)} %refs_2_.1), custom_call_target="tpu_custom_call" | custom-call | tf_op jit(solution)/shard_map/pallas_call | solution.py:421
  1.9 4.8 %collective-permute-start = (bf16[24,4,128]{2,1,0:T(4,128)(2,1)}, bf16[24,4,128]{2,1,0:T(4,128)(2,1)S(1)}, u32[]{:S(2)}, u32[]{:S(2)}) collective-permute-start(bf16[24,4,128]{2,1,0:T(4,128)(2,1)} %shard_map.101), channel_id=1, source_target_pairs={{0,4},{4,8},{8,12},{12,16},{16,20},{20,24},{24,28},{1,5},{5,9},{9,... | collective-permute-start | bytes 73736 | tf_op jit(solution)/shard_map/ppermute | solution.py:410
  6.7 1.0 %copy-done.1 = bf16[512,4,128]{2,1,0:T(4,128)(2,1)S(1)} copy-done((bf16[512,4,128]{2,1,0:T(4,128)(2,1)S(1)}, bf16[512,4,128]{2,1,0:T(4,128)(2,1)}, u32[]{:S(2)}) %copy-start.1) | copy-done | bytes 524312
  7.8 1.0 %copy-done.2 = bf16[512,4,128]{2,1,0:T(4,128)(2,1)S(1)} copy-done((bf16[512,4,128]{2,1,0:T(4,128)(2,1)S(1)}, bf16[512,4,128]{2,1,0:T(4,128)(2,1)}, u32[]{:S(2)}) %copy-start.2) | copy-done | bytes 524312
  8.8 0.7 copy-done.3
  9.6 4.4 %shard_map.100 = (bf16[4,512,128]{2,1,0:T(8,128)(2,1)S(1)}, bf16[4,512,128]{2,1,0:T(8,128)(2,1)S(1)}, f32[2,4,16,128]{3,2,1,0:T(8,128)S(1)}) custom-call(bf16[512,4,128]{2,1,0:T(4,128)(2,1)S(1)} %copy-done.1, bf16[512,4,128]{2,1,0:T(4,128)(2,1)S(1)} %copy-done.2, f32[3,4,4,128]{3,2,1,0:T(4,128)S(1)} %copy-done.3), custom_call_target="tpu_custom_call" | custom-call | flops 3000000000 | bytes 4194304 | tf_op jit(solution)/shard_map/pallas_call | solution.py:434
  14.1 5.0 %shard_map.102 = (bf16[4,512,128]{2,1,0:T(8,128)(2,1)S(1)}, f32[4,512,256]{2,1,0:T(8,128)S(1)}, f32[4,3,128,256]{3,2,1,0:T(8,128)S(1)}, bf16[4,128,256]{2,1,0:T(8,128)(2,1)S(1)}) custom-call(s32[8]{0:T(128)S(1)} %copy-done.7, bf16[4,512,128]{2,1,0:T(8,128)(2,1)S(1)} %get-tuple-element.27.unit_in_ref, ...), custom_call_target="tpu_custom_call" | custom-call | flops 5000000000 | bytes 4194304 | tf_op jit(solution)/shard_map/pallas_call | solution.py:456
  19.1 1.6 %collective-permute-start.1 = (bf16[4,128,256]{2,1,0:T(8,128)(2,1)S(1)}, bf16[4,128,256]{2,1,0:T(8,128)(2,1)S(1)}, u32[]{:S(2)}, u32[]{:S(2)}) collective-permute-start(bf16[4,128,256]{2,1,0:T(8,128)(2,1)S(1)} %get-tuple-element.39.refs_0_), channel_id=1, source_target_pairs={{0,4},{4,0},{8,12},{12,8},{1,5},{5,1},{9,13},{13,9},{2,6},{6,2},{1... | collective-permute-start | bytes 786440 | tf_op jit(solution)/shard_map/ppermute | solution.py:597
  20.8 1.9 %collective-permute-start.3 = (bf16[4,128,256]{2,1,0:T(8,128)(2,1)S(1)}, bf16[4,128,256]{2,1,0:T(8,128)(2,1)S(1)}, u32[]{:S(2)}, u32[]{:S(2)}) collective-permute-start(bf16[4,128,256]{2,1,0:T(8,128)(2,1)S(1)} %get-tuple-element.39.refs_0_), channel_id=1, source_target_pairs={{0,12},{4,8},{8,4},{12,0},{1,13},{5,9},{9,5},{13,1},{2,14},{6,10},... | collective-permute-start | bytes 786440 | tf_op jit(solution)/shard_map/ppermute | solution.py:597
  22.8 5.4 %shard_map.103 = (bf16[4,512,128]{2,1,0:T(8,128)(2,1)S(1)}, f32[4,512,128]{2,1,0:T(8,128)S(1)}, f32[4,512,128]{2,1,0:T(8,128)S(1)}) custom-call(s32[8]{0:T(128)S(1)} %copy-done.7, bf16[4,512,128]{2,1,0:T(8,128)(2,1)S(1)} %get-tuple-element.50.query_ref, bf16[4,512,128]{2,1,0:T(8,128)(2,1)S(1)} %get-tuple-element.49.gate_ref, f32[1,128]{1,0:T(1,128)S(1)} %bitcast.14, ...), custom_call_target="tpu_custom_call" | custom-call | flops 3000000000 | bytes 4194304 | tf_op jit(solution)/shard_map/pallas_call | solution.py:482
  28.4 5.4 %collective-permute-done.2.refs_2_ = bf16[4,128,256]{2,1,0:T(8,128)(2,1)S(1)} collective-permute-done((bf16[4,128,256]{2,1,0:T(8,128)(2,1)S(1)}, bf16[4,128,256]{2,1,0:T(8,128)(2,1)S(1)}, u32[]{:S(2)}, u32[]{:S(2)}) %collective-permute-start.2) | collective-permute-done | bytes 262176 | tf_op jit(solution)/shard_map/ppermute | solution.py:597
  33.8 1.0 %shard_map.104 = (f32[4,128,256]{2,1,0:T(8,128)S(1)}, bf16[4,128,128]{2,1,0:T(8,128)(2,1)S(1)}) custom-call(s32[1]{0:T(128)} %bitcast.2.place, bf16[4,128,256]{2,1,0:T(8,128)(2,1)S(1)} %get-tuple-element.39.refs_0_, bf16[4,128,256]{2,1,0:T(8,128)(2,1)S(1)} %collective-permute-done.1.refs_1_, bf16[4,128,256]{2,1,0:T(8,128)(2,1)S(1)} %collective-permute-done.2.refs_2_, ...), custom_call_target="tpu_custom_call" | custom-call | tf_op jit(solution)/shard_map/pallas_call | solution.py:508
  34.8 1.3 %collective-permute-start.4 = (bf16[4,128,128]{2,1,0:T(8,128)(2,1)S(1)}, bf16[4,128,128]{2,1,0:T(8,128)(2,1)S(1)}, u32[]{:S(2)}, u32[]{:S(2)}) collective-permute-start(bf16[4,128,128]{2,1,0:T(8,128)(2,1)S(1)} %get-tuple-element.43), channel_id=1, source_target_pairs={{0,16},{1,17},{2,18},{3,19},{4,20},{5,21},{6,22},{7,23},{8,24},{9,... | collective-permute-start | bytes 393224 | tf_op jit(solution)/shard_map/ppermute | solution.py:410
  36.1 0.9 %collective-permute-done.4.arrived_ref = bf16[4,128,128]{2,1,0:T(8,128)(2,1)S(1)} collective-permute-done((bf16[4,128,128]{2,1,0:T(8,128)(2,1)S(1)}, bf16[4,128,128]{2,1,0:T(8,128)(2,1)S(1)}, u32[]{:S(2)}, u32[]{:S(2)}) %collective-permute-start.4) | collective-permute-done | bytes 131104 | tf_op jit(solution)/shard_map/ppermute | solution.py:410
  37.8 1.6 %collective-permute-start.5 = (bf16[512,256]{1,0:T(8,128)(2,1)S(1)}, bf16[512,256]{1,0:T(8,128)(2,1)S(1)}, u32[]{:S(2)}, u32[]{:S(2)}) collective-permute-start(bf16[512,256]{1,0:T(8,128)(2,1)S(1)} %shard_map.105), channel_id=1, source_target_pairs={{0,1},{1,2},{2,3},{3,0},{4,5},{5,6},{6,7},{7,4},{8,9},{9,10},{10,1... | collective-permute-start | bytes 786440 | tf_op jit(solution)/shard_map/ppermute | solution.py:625
  40.2 1.8 %collective-permute-start.6 = (bf16[512,256]{1,0:T(8,128)(2,1)S(1)}, bf16[512,256]{1,0:T(8,128)(2,1)S(1)}, u32[]{:S(2)}, u32[]{:S(2)}) collective-permute-start(bf16[512,256]{1,0:T(8,128)(2,1)S(1)} %shard_map.106), channel_id=1, source_target_pairs={{0,1},{1,2},{2,3},{3,0},{4,5},{5,6},{6,7},{7,4},{8,9},{9,10},{10,1... | collective-permute-start | bytes 786440 | tf_op jit(solution)/shard_map/ppermute | solution.py:625
  42.9 11.0 %collective-permute-done.6 = bf16[512,256]{1,0:T(8,128)(2,1)S(1)} collective-permute-done((bf16[512,256]{1,0:T(8,128)(2,1)S(1)}, bf16[512,256]{1,0:T(8,128)(2,1)S(1)}, u32[]{:S(2)}, u32[]{:S(2)}) %collective-permute-start.6) | collective-permute-done | bytes 262176 | tf_op jit(solution)/shard_map/ppermute | solution.py:625
  54.4 1.3 %collective-permute-start.7 = (bf16[512,256]{1,0:T(8,128)(2,1)S(1)}, bf16[512,256]{1,0:T(8,128)(2,1)S(1)}, u32[]{:S(2)}, u32[]{:S(2)}) collective-permute-start(bf16[512,256]{1,0:T(8,128)(2,1)S(1)} %collective-permute-done.5), channel_id=1, source_target_pairs={{0,1},{1,2},{2,3},{3,0},{4,5},{5,6},{6,7},{7,4},{8,9},{9,10},{10,1... | collective-permute-start | bytes 786440 | tf_op jit(solution)/shard_map/ppermute | solution.py:625
  56.2 13.0 %collective-permute-done.7 = bf16[512,256]{1,0:T(8,128)(2,1)S(1)} collective-permute-done((bf16[512,256]{1,0:T(8,128)(2,1)S(1)}, bf16[512,256]{1,0:T(8,128)(2,1)S(1)}, u32[]{:S(2)}, u32[]{:S(2)}) %collective-permute-start.7) | collective-permute-done | bytes 262176 | tf_op jit(solution)/shard_map/ppermute | solution.py:625
  69.7 0.8 add_add_fusion.total_ref
  70.5 9.7 %collective-permute-done.9.block_ref = bf16[512,256]{1,0:T(8,128)(2,1)S(1)} collective-permute-done((bf16[512,256]{1,0:T(8,128)(2,1)S(1)}, bf16[512,256]{1,0:T(8,128)(2,1)S(1)}, u32[]{:S(2)}, u32[]{:S(2)}) %collective-permute-start.9) | collective-permute-done | bytes 262176 | tf_op jit(solution)/shard_map/ppermute | solution.py:625
  80.2 1.0 %shard_map.107.total_ref = f32[512,1024]{1,0:T(8,128)S(1)} custom-call(s32[1]{0:T(128)} %bitcast.1.section, f32[512,1024]{1,0:T(8,128)S(1)} %add_add_fusion.total_ref, bf16[512,256]{1,0:T(8,128)(2,1)S(1)} %collective-permute-done.9.block_ref, bf16[2048,1024]{1,0:T(8,128)(2,1)S(1)} %copy-done), custom_call_target="tpu_custom_call" | custom-call | flops 268435456 | bytes 2097152 | tf_op jit(solution)/shard_map/pallas_call | solution.py:532
  81.2 2.3 %collective-permute-done.10.block_ref = bf16[512,256]{1,0:T(8,128)(2,1)S(1)} collective-permute-done((bf16[512,256]{1,0:T(8,128)(2,1)S(1)}, bf16[512,256]{1,0:T(8,128)(2,1)S(1)}, u32[]{:S(2)}, u32[]{:S(2)}) %collective-permute-start.10) | collective-permute-done | bytes 262176 | tf_op jit(solution)/shard_map/ppermute | solution.py:625
  83.5 1.2 %shard_map.108 = bf16[512,1024]{1,0:T(8,128)(2,1)} custom-call(s32[1]{0:T(128)} %bitcast.section, f32[512,1024]{1,0:T(8,128)S(1)} %shard_map.107.total_ref, bf16[512,256]{1,0:T(8,128)(2,1)S(1)} %collective-permute-done.10.block_ref, bf16[2048,1024]{1,0:T(8,128)(2,1)S(1)} %copy-done), custom_call_target="tpu_custom_call" | custom-call | tf_op jit(solution)/shard_map/pallas_call | solution.py:555
  (36 shorter events, 4.2 us)
Async XLA Ops:
  1.9 12.1 %collective-permute-start = (bf16[24,4,128]{2,1,0:T(4,128)(2,1)}, bf16[24,4,128]{2,1,0:T(4,128)(2,1)S(1)}, u32[]{:S(2)}, u32[]{:S(2)}) collective-permute-start(bf16[24,4,128]{2,1,0:T(4,128)(2,1)} %shard_map.101), channel_id=1, source_target_pairs={{0,4},{4,8},{8,12},{12,16},{16,20},{20,24},{24,28},{1,5},{5,9},{9,... | collective-permute-start | bytes 73736 | tf_op jit(solution)/shard_map/ppermute | solution.py:410
  6.7 1.0 %copy-start.1 = (bf16[512,4,128]{2,1,0:T(4,128)(2,1)S(1)}, bf16[512,4,128]{2,1,0:T(4,128)(2,1)}, u32[]{:S(2)}) copy-start(bf16[512,4,128]{2,1,0:T(4,128)(2,1)} %refs_1_.1) | copy-start | bytes 1572868
  7.8 1.0 %copy-start.2 = (bf16[512,4,128]{2,1,0:T(4,128)(2,1)S(1)}, bf16[512,4,128]{2,1,0:T(4,128)(2,1)}, u32[]{:S(2)}) copy-start(bf16[512,4,128]{2,1,0:T(4,128)(2,1)} %refs_2_.1) | copy-start | bytes 1572868
  8.8 0.7 copy-start.3
  9.6 4.4 %copy-start.4 = (f32[3,4,4,128]{3,2,1,0:T(4,128)S(1)}, f32[3,4,4,128]{3,2,1,0:T(4,128)}, u32[]{:S(2)}) copy-start(f32[3,4,4,128]{3,2,1,0:T(4,128)} %taps_ref.3) | copy-start | bytes 73732
  9.6 4.4 %copy-start.5 = (f32[4,512]{1,0:T(4,128)S(1)}, f32[4,512]{1,0:T(4,128)}, u32[]{:S(2)}) copy-start(f32[4,512]{1,0:T(4,128)} %decay_ref.3) | copy-start | bytes 24580
  9.6 4.5 %copy-start.6 = (f32[4,512]{1,0:T(4,128)S(1)}, f32[4,512]{1,0:T(4,128)}, u32[]{:S(2)}) copy-start(f32[4,512]{1,0:T(4,128)} %strength_ref.3) | copy-start | bytes 24580
  9.6 4.5 %copy-start.7 = (s32[8]{0:T(128)S(1)}, s32[8]{0:T(128)}, u32[]{:S(2)}) copy-start(s32[8]{0:T(128)} %resets.3) | copy-start | bytes 100
  14.0 8.6 %copy-start.9 = (bf16[512,4,128]{2,1,0:T(4,128)(2,1)S(1)}, bf16[512,4,128]{2,1,0:T(4,128)(2,1)}, u32[]{:S(2)}) copy-start(bf16[512,4,128]{2,1,0:T(4,128)(2,1)} %refs_0_.1) | copy-start | bytes 1572868
  14.0 8.6 %copy-start.10 = (bf16[512,4,128]{2,1,0:T(4,128)(2,1)S(1)}, bf16[512,4,128]{2,1,0:T(4,128)(2,1)}, u32[]{:S(2)}) copy-start(bf16[512,4,128]{2,1,0:T(4,128)(2,1)} %param.13) | copy-start | bytes 1572868
  19.1 3.7 %copy-start.8 = (f32[128]{0:T(128)S(1)}, f32[128]{0:T(128)}, u32[]{:S(2)}) copy-start(f32[128]{0:T(128)} %param.18) | copy-start | bytes 1540
  19.1 9.3 %collective-permute-start.1 = (bf16[4,128,256]{2,1,0:T(8,128)(2,1)S(1)}, bf16[4,128,256]{2,1,0:T(8,128)(2,1)S(1)}, u32[]{:S(2)}, u32[]{:S(2)}) collective-permute-start(bf16[4,128,256]{2,1,0:T(8,128)(2,1)S(1)} %get-tuple-element.39.refs_0_), channel_id=1, source_target_pairs={{0,4},{4,0},{8,12},{12,8},{1,5},{5,1},{9,13},{13,9},{2,6},{6,2},{1... | collective-permute-start | bytes 786440 | tf_op jit(solution)/shard_map/ppermute | solution.py:597
  20.7 13.1 %collective-permute-start.2 = (bf16[4,128,256]{2,1,0:T(8,128)(2,1)S(1)}, bf16[4,128,256]{2,1,0:T(8,128)(2,1)S(1)}, u32[]{:S(2)}, u32[]{:S(2)}) collective-permute-start(bf16[4,128,256]{2,1,0:T(8,128)(2,1)S(1)} %get-tuple-element.39.refs_0_), channel_id=1, source_target_pairs={{0,8},{4,12},{8,0},{12,4},{1,9},{5,13},{9,1},{13,5},{2,10},{6,14},... | collective-permute-start | bytes 786440 | tf_op jit(solution)/shard_map/ppermute | solution.py:597
  20.8 13.0 %collective-permute-start.3 = (bf16[4,128,256]{2,1,0:T(8,128)(2,1)S(1)}, bf16[4,128,256]{2,1,0:T(8,128)(2,1)S(1)}, u32[]{:S(2)}, u32[]{:S(2)}) collective-permute-start(bf16[4,128,256]{2,1,0:T(8,128)(2,1)S(1)} %get-tuple-element.39.refs_0_), channel_id=1, source_target_pairs={{0,12},{4,8},{8,4},{12,0},{1,13},{5,9},{9,5},{13,1},{2,14},{6,10},... | collective-permute-start | bytes 786440 | tf_op jit(solution)/shard_map/ppermute | solution.py:597
  34.8 2.3 %collective-permute-start.4 = (bf16[4,128,128]{2,1,0:T(8,128)(2,1)S(1)}, bf16[4,128,128]{2,1,0:T(8,128)(2,1)S(1)}, u32[]{:S(2)}, u32[]{:S(2)}) collective-permute-start(bf16[4,128,128]{2,1,0:T(8,128)(2,1)S(1)} %get-tuple-element.43), channel_id=1, source_target_pairs={{0,16},{1,17},{2,18},{3,19},{4,20},{5,21},{6,22},{7,23},{8,24},{9,... | collective-permute-start | bytes 393224 | tf_op jit(solution)/shard_map/ppermute | solution.py:410
  37.1 4.9 %copy-start = (bf16[2048,1024]{1,0:T(8,128)(2,1)S(1)}, bf16[2048,1024]{1,0:T(8,128)(2,1)}, u32[]{:S(2)}) copy-start(bf16[2048,1024]{1,0:T(8,128)(2,1)} %weights_ref.3) | copy-start | bytes 12582916
  37.8 16.6 %collective-permute-start.5 = (bf16[512,256]{1,0:T(8,128)(2,1)S(1)}, bf16[512,256]{1,0:T(8,128)(2,1)S(1)}, u32[]{:S(2)}, u32[]{:S(2)}) collective-permute-start(bf16[512,256]{1,0:T(8,128)(2,1)S(1)} %shard_map.105), channel_id=1, source_target_pairs={{0,1},{1,2},{2,3},{3,0},{4,5},{5,6},{6,7},{7,4},{8,9},{9,10},{10,1... | collective-permute-start | bytes 786440 | tf_op jit(solution)/shard_map/ppermute | solution.py:625
  40.2 13.7 %collective-permute-start.6 = (bf16[512,256]{1,0:T(8,128)(2,1)S(1)}, bf16[512,256]{1,0:T(8,128)(2,1)S(1)}, u32[]{:S(2)}, u32[]{:S(2)}) collective-permute-start(bf16[512,256]{1,0:T(8,128)(2,1)S(1)} %shard_map.106), channel_id=1, source_target_pairs={{0,1},{1,2},{2,3},{3,0},{4,5},{5,6},{6,7},{7,4},{8,9},{9,10},{10,1... | collective-permute-start | bytes 786440 | tf_op jit(solution)/shard_map/ppermute | solution.py:625
  53.9 15.7 %collective-permute-start.8 = (bf16[512,256]{1,0:T(8,128)(2,1)S(1)}, bf16[512,256]{1,0:T(8,128)(2,1)S(1)}, u32[]{:S(2)}, u32[]{:S(2)}) collective-permute-start(bf16[512,256]{1,0:T(8,128)(2,1)S(1)} %collective-permute-done.6), channel_id=1, source_target_pairs={{0,1},{1,2},{2,3},{3,0},{4,5},{5,6},{6,7},{7,4},{8,9},{9,10},{10,1... | collective-permute-start | bytes 786440 | tf_op jit(solution)/shard_map/ppermute | solution.py:625
  54.4 14.8 %collective-permute-start.7 = (bf16[512,256]{1,0:T(8,128)(2,1)S(1)}, bf16[512,256]{1,0:T(8,128)(2,1)S(1)}, u32[]{:S(2)}, u32[]{:S(2)}) collective-permute-start(bf16[512,256]{1,0:T(8,128)(2,1)S(1)} %collective-permute-done.5), channel_id=1, source_target_pairs={{0,1},{1,2},{2,3},{3,0},{4,5},{5,6},{6,7},{7,4},{8,9},{9,10},{10,1... | collective-permute-start | bytes 786440 | tf_op jit(solution)/shard_map/ppermute | solution.py:625
  69.2 11.0 %collective-permute-start.9 = (bf16[512,256]{1,0:T(8,128)(2,1)S(1)}, bf16[512,256]{1,0:T(8,128)(2,1)S(1)}, u32[]{:S(2)}, u32[]{:S(2)}) collective-permute-start(bf16[512,256]{1,0:T(8,128)(2,1)S(1)} %collective-permute-done.7), channel_id=1, source_target_pairs={{0,1},{1,2},{2,3},{3,0},{4,5},{5,6},{6,7},{7,4},{8,9},{9,10},{10,1... | collective-permute-start | bytes 786440 | tf_op jit(solution)/shard_map/ppermute | solution.py:625
  69.6 13.9 %collective-permute-start.10 = (bf16[512,256]{1,0:T(8,128)(2,1)S(1)}, bf16[512,256]{1,0:T(8,128)(2,1)S(1)}, u32[]{:S(2)}, u32[]{:S(2)}) collective-permute-start(bf16[512,256]{1,0:T(8,128)(2,1)S(1)} %collective-permute-done.8), channel_id=1, source_target_pairs={{0,1},{1,2},{2,3},{3,0},{4,5},{5,6},{6,7},{7,4},{8,9},{9,10},{10,1... | collective-permute-start | bytes 786440 | tf_op jit(solution)/shard_map/ppermute | solution.py:625

commit v7 on v6

--- a/solution.py
+++ b/solution.py
@@ -9,7 +9,7 @@
 
 BLOCK = 64
 CHUNK = 128
-GROUPS = 2
+PARTS = 2
 RIM = 8
 EPSILON = 1e-06
 FAR = -1e30
@@ -140,54 +140,44 @@
     return jnp.concatenate(pieces, axis=0)
 
 
-def rims_kernel(*refs):
-    *inputs, packed_ref, arrived = refs
+def load_kernel(query_ref, key_ref, value_ref, taps_ref, rims_ref, *refs):
+    copied, arrived = refs[:-1], refs[-1]
     copies = []
-    for i, x_ref in enumerate(inputs):
+    for i, x_ref in enumerate((query_ref, key_ref, value_ref)):
         last = x_ref.at[pl.ds(x_ref.shape[0] - RIM, RIM)]
-        here = packed_ref.at[pl.ds(i * RIM, RIM)]
-        copies.append(pltpu.make_async_copy(last, here, arrived.at[i]))
+        copies.append((last, rims_ref.at[pl.ds(i * RIM, RIM)]))
+    copies += zip((key_ref, value_ref, taps_ref), copied)
+    copies = [
+        pltpu.make_async_copy(source, target, arrived.at[i])
+        for i, (source, target) in enumerate(copies)
+    ]
     for copy in copies:
         copy.start()
     for copy in copies:
         copy.wait()
 
 
-def filters_kernel(
-    key_ref, value_ref, taps_in_ref, unit_ref, value_out_ref, first_ref,
-    raw, padded, taps_ref, arrived, taps_arrived,
-):
-    length, heads, depth = key_ref.shape
-    chunks = length // CHUNK
-    taps_copy = pltpu.make_async_copy(taps_in_ref, taps_ref, taps_arrived)
-    taps_copy.start()
-    copies = {}
-    for c in range(chunks):
-        for i, x_ref in enumerate((key_ref, value_ref)):
-            here = pl.ds(c * CHUNK, CHUNK)
-            copies[c, i] = pltpu.make_async_copy(
-                x_ref.at[here], raw.at[i, here], arrived.at[c, i]
-            )
-            copies[c, i].start()
-    padded[:, :, 0:RIM] = jnp.zeros((2, heads, RIM, depth), F32)
-    taps_copy.wait()
-    for c in range(chunks):
-        begin = RIM + c * CHUNK
+def filters_kernel(key_ref, value_ref, taps_ref, unit_ref, value_out_ref, first_ref, padded):
+    length, heads, _ = key_ref.shape
+    for i, x_ref in enumerate((key_ref, value_ref)):
+        for c in range(length // CHUNK):
+            begin = RIM + c * CHUNK
+            padded[i, :, begin : begin + CHUNK] = jnp.swapaxes(x_ref[rows_of(c)], 0, 1).astype(F32)
+        padded[i, :, 0:RIM] = jnp.zeros((heads, RIM, padded.shape[3]), F32)
+    first_ref[...] = padded[:, :, RIM : RIM + AGAIN]
+
+    def one_head(h, carry):
         for i in range(2):
-            copies[c, i].wait()
-            padded[i, :, begin : begin + CHUNK] = jnp.swapaxes(raw[i, rows_of(c)], 0, 1).astype(F32)
-
-        def one_head(h, carry):
-            for i in range(2):
-                rows = filtered(padded.at[i, h], taps_of(taps_ref, 1 + i, h), c * CHUNK, CHUNK)
+            taps = taps_of(taps_ref, 1 + i, h)
+            for c in range(length // CHUNK):
+                rows = filtered(padded.at[i, h], taps, c * CHUNK, CHUNK)
                 if i == 0:
                     unit_ref[h, rows_of(c)] = unit(rows).astype(BF16)
                 else:
                     value_out_ref[h, rows_of(c)] = rows.astype(BF16)
-            return carry
-
-        lax.fori_loop(0, heads, one_head, 0)
-    first_ref[...] = padded[:, :, RIM : RIM + AGAIN]
+        return carry
+
+    lax.fori_loop(0, heads, one_head, 0)
 
 
 def maps_kernel(
@@ -371,35 +361,32 @@
             ref[h] = states[h][:, :depth]
 
 
-def outputs_kernel(base, arrived_ref, before_ref, reach_ref, part_ref, gating_ref, normed_ref):
-    _, length, depth = reach_ref.shape
-    for g in range(normed_ref.shape[1] // depth):
-        h = base + g
+def outputs_kernel(begin, arrived_ref, before_ref, reach_ref, part_ref, gating_ref, normed_ref):
+    heads, _, depth = reach_ref.shape
+    for h in range(heads):
         before = before_ref[h]
         incoming = mul_split(before[:, :depth], arrived_ref[h].astype(F32)) + before[:, depth:]
         high, low = split(incoming)
-        for c in range(length // CHUNK):
-            here = rows_of(c)
+        for c in range(normed_ref.shape[0] // CHUNK):
+            here = slice(begin + c * CHUNK, begin + (c + 1) * CHUNK)
             reach = reach_ref[h, here]
             core = part_ref[h, here] + (mul(reach, high) + mul(reach, low))
             scale = lax.rsqrt(jnp.sum(core * core, axis=-1, keepdims=True) / depth + EPSILON)
-            normed_ref[here, g * depth : (g + 1) * depth] = (
+            normed_ref[rows_of(c), h * depth : (h + 1) * depth] = (
                 core * scale * gating_ref[h, here]
             ).astype(BF16)
 
 
-def projected_kernel(section, total_ref, block_ref, weights_ref, out_ref):
-    out_ref[...] = total_ref[...] + mul(block_ref[...], weights_ref[...])
-
-
-def last_kernel(section, total_ref, block_ref, weights_ref, out_ref, tiles, written):
+def last_kernel(begin, section, total_ref, block_ref, weights_ref, *refs):
+    out_ref, tiles, written = refs[-3:]
     width = block_ref.shape[1]
     rows = weights_ref[pl.ds(pl.multiple_of(section[0] * width, width), width), :]
     copies = []
     for i in range(total_ref.shape[0] // CHUNK):
         here = rows_of(i)
         tiles[here] = (total_ref[here] + mul(block_ref[here], rows)).astype(BF16)
-        copies.append(pltpu.make_async_copy(tiles.at[here], out_ref.at[here], written.at[i]))
+        target = out_ref.at[pl.ds(begin + i * CHUNK, CHUNK)]
+        copies.append(pltpu.make_async_copy(tiles.at[here], target, written.at[i]))
         copies[-1].start()
     for copy in copies:
         copy.wait()
@@ -416,38 +403,33 @@
 PARAMS = pltpu.CompilerParams(vmem_limit_bytes=12 * 1024 * 1024)
 
 
-def pack_rims(inputs):
-    _, heads, depth = inputs[0].shape
+def load(query_in, key_in, value_in, taps):
+    _, heads, depth = query_in.shape
+    like = [jax.ShapeDtypeStruct(x.shape, x.dtype) for x in (key_in, value_in, taps)]
     return pl.pallas_call(
-        rims_kernel,
-        out_shape=jax.ShapeDtypeStruct((len(inputs) * RIM, heads, depth), BF16),
-        in_specs=[HBM] * len(inputs),
-        out_specs=HBM,
-        scratch_shapes=[pltpu.SemaphoreType.DMA((len(inputs),))],
-    )(*inputs)
-
-
-def filters_of(key_in, value_in, taps):
-    length, heads, depth = key_in.shape
-    chunks = length // CHUNK
+        load_kernel,
+        out_shape=[jax.ShapeDtypeStruct((3 * RIM, heads, depth), BF16)] + like,
+        in_specs=[HBM] * 4,
+        out_specs=[VMEM] * 4,
+        scratch_shapes=[pltpu.SemaphoreType.DMA((6,))],
+        compiler_params=PARAMS,
+    )(query_in, key_in, value_in, taps)
+
+
+def filters_of(key, value, taps):
+    length, heads, depth = key.shape
     per_token = jax.ShapeDtypeStruct((heads, length, depth), BF16)
     return pl.pallas_call(
         filters_kernel,
         out_shape=(per_token, per_token, jax.ShapeDtypeStruct((2, heads, AGAIN, depth), F32)),
-        in_specs=[HBM] * 3,
+        in_specs=[VMEM] * 3,
         out_specs=[VMEM] * 3,
-        scratch_shapes=[
-            pltpu.VMEM((2, length, heads, depth), BF16),
-            pltpu.VMEM((2, heads, length + RIM, depth), F32),
-            pltpu.VMEM(taps.shape, F32),
-            pltpu.SemaphoreType.DMA((chunks, 2)),
-            pltpu.SemaphoreType.DMA(()),
-        ],
+        scratch_shapes=[pltpu.VMEM((2, heads, length + RIM, depth), F32)],
         compiler_params=PARAMS,
         cost_estimate=pl.CostEstimate(
             flops=3 * 10**9, bytes_accessed=4 * 2**20, transcendentals=10**6
         ),
-    )(key_in, value_in, taps)
+    )(key, value, taps)
 
 
 def maps_of(base, heads, resets, unit_in, value_in, first, rims, taps, decay, strength):
@@ -515,54 +497,33 @@
     )(place, *maps)
 
 
-def outputs_of(base, heads, arrived, before, reads):
-    _, length, depth = reads[0].shape
+def outputs_of(begin, count, arrived, before, reads):
+    heads, _, depth = reads[0].shape
     return pl.pallas_call(
-        functools.partial(outputs_kernel, base),
-        out_shape=jax.ShapeDtypeStruct((length, heads * depth), BF16),
+        functools.partial(outputs_kernel, begin),
+        out_shape=jax.ShapeDtypeStruct((count, heads * depth), BF16),
         in_specs=[VMEM] * 5,
         out_specs=VMEM,
         compiler_params=PARAMS,
     )(arrived, before, *reads)
 
 
-def projected(section, total, block, weights):
-    length, columns = total.shape
-    width = block.shape[1]
+def last_projected(begin, section, total, block, weights, length, result):
+    count, columns = total.shape
+    whole = pl.BlockSpec(memory_space=pl.ANY)
+    earlier = [] if result is None else [result]
     return pl.pallas_call(
-        projected_kernel,
-        out_shape=jax.ShapeDtypeStruct(total.shape, F32),
-        grid_spec=pltpu.PrefetchScalarGridSpec(
-            num_scalar_prefetch=1,
-            grid=(length // CHUNK,),
-            in_specs=[
-                pl.BlockSpec((CHUNK, columns), lambda i, s: (i, 0)),
-                pl.BlockSpec((CHUNK, width), lambda i, s: (i, 0)),
-                pl.BlockSpec((width, columns), lambda i, s: (s[0], 0)),
-            ],
-            out_specs=pl.BlockSpec((CHUNK, columns), lambda i, s: (i, 0)),
-        ),
+        functools.partial(last_kernel, begin),
+        out_shape=jax.ShapeDtypeStruct((length, columns), BF16),
+        in_specs=[SMEM] + [VMEM] * 3 + [whole] * len(earlier),
+        out_specs=whole,
+        scratch_shapes=[
+            pltpu.VMEM((count, columns), BF16),
+            pltpu.SemaphoreType.DMA((count // CHUNK,)),
+        ],
+        input_output_aliases={4: 0} if earlier else {},
         compiler_params=PARAMS,
-        cost_estimate=pl.CostEstimate(
-            flops=2 * length * columns * width,
-            bytes_accessed=4 * length * columns,
-            transcendentals=0,
-        ),
-    )(section.astype(jnp.int32).reshape(1), total, block, weights)
-
-
-def last_projected(section, total, block, weights):
-    return pl.pallas_call(
-        last_kernel,
-        out_shape=jax.ShapeDtypeStruct(total.shape, BF16),
-        in_specs=[SMEM] + [VMEM] * 3,
-        out_specs=pl.BlockSpec(memory_space=pl.ANY),
-        scratch_shapes=[
-            pltpu.VMEM(total.shape, BF16),
-            pltpu.SemaphoreType.DMA((total.shape[0] // CHUNK,)),
-        ],
-        compiler_params=PARAMS,
-    )(section.astype(jnp.int32).reshape(1), total, block, weights)
+    )(section.astype(jnp.int32).reshape(1), total, block, weights, *earlier)
 
 
 def after(first, *values):
@@ -582,16 +543,16 @@
     output_projection_weight,
 ):
     length, heads, depth = query_in.shape
-    size = heads // GROUPS
-    rims = from_behind(pack_rims((query_in, key_in, value_in)), ("chain", "leaf"), 1)
-    key, value, first = filters_of(key_in, value_in, conv_weight)
+    last_rows, key, value, taps = load(query_in, key_in, value_in, conv_weight)
+    rims = from_behind(last_rows, ("chain", "leaf"), 1)
+    key, value, first = filters_of(key, value, taps)
     gain = output_norm_gain.reshape(1, depth)
     leaves = lax.axis_size("leaf")
     place = lax.axis_index("leaf").astype(jnp.int32).reshape(1)
 
     links = lax.axis_size("chain") - 1
     *made, own_map = maps_of(
-        0, heads, doc_resets, key, value, first, rims, conv_weight, log_decay, write_strength
+        0, heads, doc_resets, key, value, first, rims, taps, log_decay, write_strength
     )
     maps = [own_map] + [
         lax.ppermute(own_map, "leaf", pairs_at(k, leaves)) for k in range(1, leaves)
@@ -599,7 +560,7 @@
     query_in, gate_in = after(own_map, query_in, gate_in)
     query, gate = (jnp.transpose(x, (1, 0, 2)) for x in (query_in, gate_in))
     reads = reads_of(
-        0, heads, doc_resets, query, gate, gain, rims, conv_weight, log_decay, write_strength, made
+        0, heads, doc_resets, query, gate, gain, rims, taps, log_decay, write_strength, made
     )
     maps, reads = lax.optimization_barrier((maps, reads))
     before, state, *trans = join(place, maps, links)
@@ -609,32 +570,32 @@
             "hij,hjk->hik", trans[0], arrived.astype(F32), precision=lax.Precision.HIGHEST
         )
         arrived = from_behind((passed + state).astype(BF16), "chain", 1)
+    count = length // PARTS
     blocks = []
-    for g in range(GROUPS):
-        blocks.append(outputs_of(g * size, size, arrived, before, reads))
-        arrived = after(blocks[g], arrived)[0]
+    for p in range(PARTS):
+        blocks.append(outputs_of(p * count, count, arrived, before, reads))
+        arrived = after(blocks[p], arrived)[0]
 
     ring = lax.axis_size("head")
     mine = lax.axis_index("head")
-    width = size * depth
+    width = heads * depth
     around = [(i, (i + 1) % ring) for i in range(ring)]
-    mixed = None
-    for k in range(ring):
+    mixed = [None] * PARTS
+    for k in range(ring - 1):
         owner = lax.rem(mine + ring - k, ring)
-        if k + 1 < ring:
-            following = [lax.ppermute(block, "head", around) for block in blocks]
-        for g, block in enumerate(blocks):
-            section = owner * GROUPS + g
-            if k + 1 == ring:
-                add = last_projected if g + 1 == GROUPS else projected
-                mixed = add(section, mixed, block, output_projection_weight)
-                continue
-            rows = lax.dynamic_slice_in_dim(output_projection_weight, section * width, width, 0)
+        rows = lax.dynamic_slice_in_dim(output_projection_weight, owner * width, width, 0)
+        following = [lax.ppermute(block, "head", around) for block in blocks]
+        for p, block in enumerate(blocks):
             term = jnp.dot(block, rows, preferred_element_type=F32)
-            mixed = term if mixed is None else mixed + term
-        if k + 1 < ring:
-            blocks = following
-    return mixed
+            mixed[p] = term if mixed[p] is None else mixed[p] + term
+        blocks = following
+    result = None
+    for p, block in enumerate(blocks):
+        result = last_projected(
+            p * count, lax.rem(mine + 1, ring), mixed[p], block, output_projection_weight, length,
+            result,
+        )
+    return result
 
 
 def solution(mesh):

time: 85.2 us -> 76 us (0.89)
  waiting for transfers between devices: 42.5 us -> 35.3 us
  Pallas kernels: 21.4 us -> 18.4 us
  starting transfers between devices: 14.6 us -> 13.4 us
  local copies, waits for them, and re-layouts: 2.99 us -> 4.04 us
  matrix products: 3.05 us -> 4.03 us
    ppermute x6, waiting for transfers between devices: 36 us -> 29 us  [on_device(): following = [lax.ppermute(block, 'head', around) for block in blocks]]
    pallas_call x1, Pallas kernels: 4.4 us -> 2.49 us  [filters_of(): pl.pallas_call(filters_kernel, out_shape=(per_token, per_token, jax.Shape...]
    ppermute x6, starting transfers between devices: 4.86 us -> 3.53 us  [on_device(): following = [lax.ppermute(block, 'head', around) for block in blocks]]
    pallas_call x5, Pallas kernels: 5.54 us -> 4.42 us  [the longest x2 2.36 us: last_projected(): pl.pallas_call(functools.partial(last_kernel, begin), out_shape=jax.Shape...]
    unnamed x22, local copies, waits for them, and re-layouts: 2.85 us -> 3.9 us
    dot_general x6, matrix products: 3.05 us -> 4.03 us  [on_device(): term = jnp.dot(block, rows, preferred_element_type=F32)]
  transfers between devices with their start and end apart: 11 -> 11, of which waited for: 7 -> 8; matrix products, arithmetic and copies ran while one was open for 4% -> 6% of each run, Pallas kernels for 14% -> 13%
where the time goes in v7:
time: 76 us; the launch traced here: 75.6 us
  waiting for transfers between devices  35.3 us (46%)
  Pallas kernels  18.4 us (24%)
  starting transfers between devices  13.4 us (18%)
  local copies, waits for them, and re-layouts  4.04 us (5%)
  matrix products  4.03 us (5%)
    ppermute x6, waiting for transfers between devices, on_device(): following = [lax.ppermute(block, 'head', around) for block in blocks]  29 us
    ppermute x2, starting transfers between devices, from_behind(): lax.ppermute(value, axis, [(i, i + steps) for i in range(count - steps)])  6.14 us
    pallas_call x1, Pallas kernels, reads_of(): pl.pallas_call(functools.partial(reads_kernel, base), out_shape=(jax.Shap...  5.43 us
    ppermute x3, waiting for transfers between devices, on_device(): lax.ppermute(own_map, 'leaf', pairs_at(k, leaves))  5.36 us
    pallas_call x1, Pallas kernels, maps_of(): pl.pallas_call(functools.partial(maps_kernel, base), out_shape=(jax.Shape...  5.05 us
    dot_general x6, matrix products, on_device(): term = jnp.dot(block, rows, preferred_element_type=F32)  4.03 us
    unnamed x22, local copies, waits for them, and re-layouts  3.9 us
    ppermute x3, starting transfers between devices, on_device(): lax.ppermute(own_map, 'leaf', pairs_at(k, leaves))  3.7 us
  transfers between devices with their start and end apart: 11, of which 8 were waited for; matrix products, arithmetic and copies ran while one was open for 6% of the time, Pallas kernels for 13%

profile of v7, /device:TPU:0, one launch (start us, length us, event | category | flops | bytes accessed | tf_op | source)
XLA Modules:
  0.0 75.6 jit_solution(18247533100889387712)
XLA Ops:
  0.0 1.0 %copy-done.1 = bf16[512,4,128]{2,1,0:T(4,128)(2,1)S(1)} copy-done((bf16[512,4,128]{2,1,0:T(4,128)(2,1)S(1)}, bf16[512,4,128]{2,1,0:T(4,128)(2,1)}, u32[]{:S(2)}) %copy-start.1) | copy-done | bytes 524312
  1.0 1.0 %copy-done.3 = bf16[512,4,128]{2,1,0:T(4,128)(2,1)S(1)} copy-done((bf16[512,4,128]{2,1,0:T(4,128)(2,1)S(1)}, bf16[512,4,128]{2,1,0:T(4,128)(2,1)}, u32[]{:S(2)}) %copy-start.3) | copy-done | bytes 524312
  2.1 1.0 %copy-done.4 = bf16[512,4,128]{2,1,0:T(4,128)(2,1)S(1)} copy-done((bf16[512,4,128]{2,1,0:T(4,128)(2,1)S(1)}, bf16[512,4,128]{2,1,0:T(4,128)(2,1)}, u32[]{:S(2)}) %copy-start.4) | copy-done | bytes 524312
  4.0 4.8 %collective-permute-start = (bf16[24,4,128]{2,1,0:T(4,128)(2,1)S(1)}, bf16[24,4,128]{2,1,0:T(4,128)(2,1)S(1)}, u32[]{:S(2)}, u32[]{:S(2)}) collective-permute-start(bf16[24,4,128]{2,1,0:T(4,128)(2,1)S(1)} %get-tuple-element.37), channel_id=1, source_target_pairs={{0,4},{4,8},{8,12},{12,16},{16,20},{20,24},{24,28},{1,5},{5,9},{9,... | collective-permute-start | bytes 73736 | tf_op jit(solution)/shard_map/ppermute | solution.py:397
  8.9 2.5 %shard_map.101 = (bf16[4,512,128]{2,1,0:T(8,128)(2,1)S(1)}, bf16[4,512,128]{2,1,0:T(8,128)(2,1)S(1)}, f32[2,4,16,128]{3,2,1,0:T(8,128)S(1)}) custom-call(bf16[512,4,128]{2,1,0:T(4,128)(2,1)S(1)} %get-tuple-element.31.key_ref, bf16[512,4,128]{2,1,0:T(4,128)(2,1)S(1)} %get-tuple-element.32.value_ref, f32[3,4,4,128]{3,2,1,0:T(4,128)S(1)} %get-tuple-element.33.taps_ref), custom_call_target="tpu_custom_call" | custom-call | flops 3000000000 | bytes 4194304 | tf_op jit(solution)/shard_map/pallas_call | solution.py:422
  11.5 5.1 %shard_map.102 = (bf16[4,512,128]{2,1,0:T(8,128)(2,1)S(1)}, f32[4,512,256]{2,1,0:T(8,128)S(1)}, f32[4,3,128,256]{3,2,1,0:T(8,128)S(1)}, bf16[4,128,256]{2,1,0:T(8,128)(2,1)S(1)}) custom-call(s32[8]{0:T(128)S(1)} %copy-done.8, bf16[4,512,128]{2,1,0:T(8,128)(2,1)S(1)} %get-tuple-element.34.unit_in_ref, ...), custom_call_target="tpu_custom_call" | custom-call | flops 5000000000 | bytes 4194304 | tf_op jit(solution)/shard_map/pallas_call | solution.py:438
  16.6 1.6 %collective-permute-start.1 = (bf16[4,128,256]{2,1,0:T(8,128)(2,1)S(1)}, bf16[4,128,256]{2,1,0:T(8,128)(2,1)S(1)}, u32[]{:S(2)}, u32[]{:S(2)}) collective-permute-start(bf16[4,128,256]{2,1,0:T(8,128)(2,1)S(1)} %get-tuple-element.47.refs_0_), channel_id=1, source_target_pairs={{0,4},{4,0},{8,12},{12,8},{1,5},{5,1},{9,13},{13,9},{2,6},{6,2},{1... | collective-permute-start | bytes 786440 | tf_op jit(solution)/shard_map/ppermute | solution.py:558
  18.1 1.3 %collective-permute-start.2 = (bf16[4,128,256]{2,1,0:T(8,128)(2,1)S(1)}, bf16[4,128,256]{2,1,0:T(8,128)(2,1)S(1)}, u32[]{:S(2)}, u32[]{:S(2)}) collective-permute-start(bf16[4,128,256]{2,1,0:T(8,128)(2,1)S(1)} %get-tuple-element.47.refs_0_), channel_id=1, source_target_pairs={{0,8},{4,12},{8,0},{12,4},{1,9},{5,13},{9,1},{13,5},{2,10},{6,14},... | collective-permute-start | bytes 786440 | tf_op jit(solution)/shard_map/ppermute | solution.py:558
  20.4 5.4 %shard_map.103 = (bf16[4,512,128]{2,1,0:T(8,128)(2,1)S(1)}, f32[4,512,128]{2,1,0:T(8,128)S(1)}, f32[4,512,128]{2,1,0:T(8,128)S(1)}) custom-call(s32[8]{0:T(128)S(1)} %copy-done.8, bf16[4,512,128]{2,1,0:T(8,128)(2,1)S(1)} %get-tuple-element.58.query_ref, bf16[4,512,128]{2,1,0:T(8,128)(2,1)S(1)} %get-tuple-element.57.gate_ref, f32[1,128]{1,0:T(1,128)S(1)} %bitcast.13, ...), custom_call_target="tpu_custom_call" | custom-call | flops 3000000000 | bytes 4194304 | tf_op jit(solution)/shard_map/pallas_call | solution.py:464
  25.9 5.4 %collective-permute-done.2.refs_2_ = bf16[4,128,256]{2,1,0:T(8,128)(2,1)S(1)} collective-permute-done((bf16[4,128,256]{2,1,0:T(8,128)(2,1)S(1)}, bf16[4,128,256]{2,1,0:T(8,128)(2,1)S(1)}, u32[]{:S(2)}, u32[]{:S(2)}) %collective-permute-start.2) | collective-permute-done | bytes 262176 | tf_op jit(solution)/shard_map/ppermute | solution.py:558
  31.2 1.0 %shard_map.104 = (f32[4,128,256]{2,1,0:T(8,128)S(1)}, bf16[4,128,128]{2,1,0:T(8,128)(2,1)S(1)}) custom-call(s32[1]{0:T(128)} %bitcast.1.place, bf16[4,128,256]{2,1,0:T(8,128)(2,1)S(1)} %get-tuple-element.47.refs_0_, bf16[4,128,256]{2,1,0:T(8,128)(2,1)S(1)} %collective-permute-done.1.refs_1_, bf16[4,128,256]{2,1,0:T(8,128)(2,1)S(1)} %collective-permute-done.2.refs_2_, ...), custom_call_target="tpu_custom_call" | custom-call | tf_op jit(solution)/shard_map/pallas_call | solution.py:490
  32.3 1.3 %collective-permute-start.4 = (bf16[4,128,128]{2,1,0:T(8,128)(2,1)S(1)}, bf16[4,128,128]{2,1,0:T(8,128)(2,1)S(1)}, u32[]{:S(2)}, u32[]{:S(2)}) collective-permute-start(bf16[4,128,128]{2,1,0:T(8,128)(2,1)S(1)} %get-tuple-element.51), channel_id=1, source_target_pairs={{0,16},{1,17},{2,18},{3,19},{4,20},{5,21},{6,22},{7,23},{8,24},{9,... | collective-permute-start | bytes 393224 | tf_op jit(solution)/shard_map/ppermute | solution.py:397
  33.6 1.0 %collective-permute-done.4.arrived_ref = bf16[4,128,128]{2,1,0:T(8,128)(2,1)S(1)} collective-permute-done((bf16[4,128,128]{2,1,0:T(8,128)(2,1)S(1)}, bf16[4,128,128]{2,1,0:T(8,128)(2,1)S(1)}, u32[]{:S(2)}, u32[]{:S(2)}) %collective-permute-start.4) | collective-permute-done | bytes 131104 | tf_op jit(solution)/shard_map/ppermute | solution.py:397
  35.5 1.8 %collective-permute-start.8 = (bf16[256,512]{1,0:T(8,128)(2,1)S(1)}, bf16[256,512]{1,0:T(8,128)(2,1)}, u32[]{:S(2)}, u32[]{:S(2)}) collective-permute-start(bf16[256,512]{1,0:T(8,128)(2,1)S(1)} %shard_map.105), channel_id=1, source_target_pairs={{0,1},{1,2},{2,3},{3,0},{4,5},{5,6},{6,7},{7,4},{8,9},{9,10},{10,1... | collective-permute-start | bytes 786440 | tf_op jit(solution)/shard_map/ppermute | solution.py:587
  38.3 1.6 %collective-permute-start.5 = (bf16[256,512]{1,0:T(8,128)(2,1)S(1)}, bf16[256,512]{1,0:T(8,128)(2,1)S(1)}, u32[]{:S(2)}, u32[]{:S(2)}) collective-permute-start(bf16[256,512]{1,0:T(8,128)(2,1)S(1)} %shard_map.106), channel_id=1, source_target_pairs={{0,1},{1,2},{2,3},{3,0},{4,5},{5,6},{6,7},{7,4},{8,9},{9,10},{10,1... | collective-permute-start | bytes 786440 | tf_op jit(solution)/shard_map/ppermute | solution.py:587
  39.9 6.8 %collective-permute-done.8 = bf16[256,512]{1,0:T(8,128)(2,1)} collective-permute-done((bf16[256,512]{1,0:T(8,128)(2,1)S(1)}, bf16[256,512]{1,0:T(8,128)(2,1)}, u32[]{:S(2)}, u32[]{:S(2)}) %collective-permute-start.8) | collective-permute-done | bytes 262176 | tf_op jit(solution)/shard_map/ppermute | solution.py:587
  46.7 1.7 %fusion.2 = f32[256,1024]{1,0:T(8,128)S(1)} fusion(bf16[256,512]{1,0:T(8,128)(2,1)} %collective-permute-done.8, bf16[2048,1024]{1,0:T(8,128)(2,1)} %weights_ref.3, s32[]{:T(128)S(6)} %select_n.10), kind=kOutput, calls=%fused_computation.6 | convolution fusion | flops 268435456 | bytes 2359300 | tf_op jit(solution)/shard_map/dot_general | solution.py:589
  49.0 3.3 %collective-permute-done.5 = bf16[256,512]{1,0:T(8,128)(2,1)S(1)} collective-permute-done((bf16[256,512]{1,0:T(8,128)(2,1)S(1)}, bf16[256,512]{1,0:T(8,128)(2,1)S(1)}, u32[]{:S(2)}, u32[]{:S(2)}) %collective-permute-start.5) | collective-permute-done | bytes 262176 | tf_op jit(solution)/shard_map/ppermute | solution.py:587
  53.3 4.7 %collective-permute-done.9 = bf16[256,512]{1,0:T(8,128)(2,1)S(1)} collective-permute-done((bf16[256,512]{1,0:T(8,128)(2,1)}, bf16[256,512]{1,0:T(8,128)(2,1)S(1)}, u32[]{:S(2)}, u32[]{:S(2)}) %collective-permute-start.9) | collective-permute-done | bytes 262176 | tf_op jit(solution)/shard_map/ppermute | solution.py:587
  58.0 5.8 %collective-permute-done.6 = bf16[256,512]{1,0:T(8,128)(2,1)S(1)} collective-permute-done((bf16[256,512]{1,0:T(8,128)(2,1)S(1)}, bf16[256,512]{1,0:T(8,128)(2,1)S(1)}, u32[]{:S(2)}, u32[]{:S(2)}) %collective-permute-start.6) | collective-permute-done | bytes 262176 | tf_op jit(solution)/shard_map/ppermute | solution.py:587
  64.7 4.7 %collective-permute-done.10.block_ref = bf16[256,512]{1,0:T(8,128)(2,1)S(1)} collective-permute-done((bf16[256,512]{1,0:T(8,128)(2,1)S(1)}, bf16[256,512]{1,0:T(8,128)(2,1)S(1)}, u32[]{:S(2)}, u32[]{:S(2)}) %collective-permute-start.10) | collective-permute-done | bytes 262176 | tf_op jit(solution)/shard_map/ppermute | solution.py:587
  69.4 1.2 %shard_map.107.refs_0_ = bf16[512,1024]{1,0:T(8,128)(2,1)} custom-call(s32[1]{0:T(128)} %bitcast.section, f32[256,1024]{1,0:T(8,128)S(1)} %convolution_add_fusion.total_ref, bf16[256,512]{1,0:T(8,128)(2,1)S(1)} %collective-permute-done.10.block_ref, bf16[2048,1024]{1,0:T(8,128)(2,1)S(1)} %copy-done), custom_call_target="tpu_custom_call" | custom-call | tf_op jit(solution)/shard_map/pallas_call | solution.py:515
  70.6 3.6 %collective-permute-done.7.block_ref = bf16[256,512]{1,0:T(8,128)(2,1)S(1)} collective-permute-done((bf16[256,512]{1,0:T(8,128)(2,1)S(1)}, bf16[256,512]{1,0:T(8,128)(2,1)S(1)}, u32[]{:S(2)}, u32[]{:S(2)}) %collective-permute-start.7) | collective-permute-done | bytes 262176 | tf_op jit(solution)/shard_map/ppermute | solution.py:587
  74.2 1.2 %shard_map.108 = bf16[512,1024]{1,0:T(8,128)(2,1)} custom-call(s32[1]{0:T(128)} %bitcast.section, f32[256,1024]{1,0:T(8,128)S(1)} %convolution_add_fusion.2.total_ref, bf16[256,512]{1,0:T(8,128)(2,1)S(1)} %collective-permute-done.7.block_ref, bf16[2048,1024]{1,0:T(8,128)(2,1)S(1)} %copy-done, ...), custom_call_target="tpu_custom_call", output_to_operand_aliasing={{}: (4, {})} | custom-call | tf_op jit(solution)/shard_map/pallas_call | solution.py:515
  (36 shorter events, 6.2 us)
Async XLA Ops:
  0.0 1.0 %copy-start.1 = (bf16[512,4,128]{2,1,0:T(4,128)(2,1)S(1)}, bf16[512,4,128]{2,1,0:T(4,128)(2,1)}, u32[]{:S(2)}) copy-start(bf16[512,4,128]{2,1,0:T(4,128)(2,1)} %query_ref.1) | copy-start | bytes 1572868
  1.0 1.0 %copy-start.3 = (bf16[512,4,128]{2,1,0:T(4,128)(2,1)S(1)}, bf16[512,4,128]{2,1,0:T(4,128)(2,1)}, u32[]{:S(2)}) copy-start(bf16[512,4,128]{2,1,0:T(4,128)(2,1)} %key_ref.1) | copy-start | bytes 1572868
  2.1 1.0 %copy-start.4 = (bf16[512,4,128]{2,1,0:T(4,128)(2,1)S(1)}, bf16[512,4,128]{2,1,0:T(4,128)(2,1)}, u32[]{:S(2)}) copy-start(bf16[512,4,128]{2,1,0:T(4,128)(2,1)} %value_ref.1) | copy-start | bytes 1572868
  3.1 0.7 copy-start.5
  4.0 7.4 %collective-permute-start = (bf16[24,4,128]{2,1,0:T(4,128)(2,1)S(1)}, bf16[24,4,128]{2,1,0:T(4,128)(2,1)S(1)}, u32[]{:S(2)}, u32[]{:S(2)}) collective-permute-start(bf16[24,4,128]{2,1,0:T(4,128)(2,1)S(1)} %get-tuple-element.37), channel_id=1, source_target_pairs={{0,4},{4,8},{8,12},{12,16},{16,20},{20,24},{24,28},{1,5},{5,9},{9,... | collective-permute-start | bytes 73736 | tf_op jit(solution)/shard_map/ppermute | solution.py:397
  8.9 2.6 %copy-start.6 = (f32[4,512]{1,0:T(4,128)S(1)}, f32[4,512]{1,0:T(4,128)}, u32[]{:S(2)}) copy-start(f32[4,512]{1,0:T(4,128)} %decay_ref.3) | copy-start | bytes 24580
  8.9 2.5 %copy-start.7 = (f32[4,512]{1,0:T(4,128)S(1)}, f32[4,512]{1,0:T(4,128)}, u32[]{:S(2)}) copy-start(f32[4,512]{1,0:T(4,128)} %strength_ref.3) | copy-start | bytes 24580
  8.9 2.5 %copy-start.8 = (s32[8]{0:T(128)S(1)}, s32[8]{0:T(128)}, u32[]{:S(2)}) copy-start(s32[8]{0:T(128)} %resets.3) | copy-start | bytes 100
  11.5 8.8 %copy-start.2 = (bf16[512,4,128]{2,1,0:T(4,128)(2,1)S(1)}, bf16[512,4,128]{2,1,0:T(4,128)(2,1)}, u32[]{:S(2)}) copy-start(bf16[512,4,128]{2,1,0:T(4,128)(2,1)} %query_ref.1) | copy-start | bytes 1572868
  11.5 8.8 %copy-start.10 = (bf16[512,4,128]{2,1,0:T(4,128)(2,1)S(1)}, bf16[512,4,128]{2,1,0:T(4,128)(2,1)}, u32[]{:S(2)}) copy-start(bf16[512,4,128]{2,1,0:T(4,128)(2,1)} %param.13) | copy-start | bytes 1572868
  11.5 8.9 %copy-start.9 = (f32[128]{0:T(128)S(1)}, f32[128]{0:T(128)}, u32[]{:S(2)}) copy-start(f32[128]{0:T(128)} %param.18) | copy-start | bytes 1540
  16.6 9.3 %collective-permute-start.1 = (bf16[4,128,256]{2,1,0:T(8,128)(2,1)S(1)}, bf16[4,128,256]{2,1,0:T(8,128)(2,1)S(1)}, u32[]{:S(2)}, u32[]{:S(2)}) collective-permute-start(bf16[4,128,256]{2,1,0:T(8,128)(2,1)S(1)} %get-tuple-element.47.refs_0_), channel_id=1, source_target_pairs={{0,4},{4,0},{8,12},{12,8},{1,5},{5,1},{9,13},{13,9},{2,6},{6,2},{1... | collective-permute-start | bytes 786440 | tf_op jit(solution)/shard_map/ppermute | solution.py:558
  18.1 13.1 %collective-permute-start.2 = (bf16[4,128,256]{2,1,0:T(8,128)(2,1)S(1)}, bf16[4,128,256]{2,1,0:T(8,128)(2,1)S(1)}, u32[]{:S(2)}, u32[]{:S(2)}) collective-permute-start(bf16[4,128,256]{2,1,0:T(8,128)(2,1)S(1)} %get-tuple-element.47.refs_0_), channel_id=1, source_target_pairs={{0,8},{4,12},{8,0},{12,4},{1,9},{5,13},{9,1},{13,5},{2,10},{6,14},... | collective-permute-start | bytes 786440 | tf_op jit(solution)/shard_map/ppermute | solution.py:558
  19.4 11.8 %collective-permute-start.3 = (bf16[4,128,256]{2,1,0:T(8,128)(2,1)S(1)}, bf16[4,128,256]{2,1,0:T(8,128)(2,1)S(1)}, u32[]{:S(2)}, u32[]{:S(2)}) collective-permute-start(bf16[4,128,256]{2,1,0:T(8,128)(2,1)S(1)} %get-tuple-element.47.refs_0_), channel_id=1, source_target_pairs={{0,12},{4,8},{8,4},{12,0},{1,13},{5,9},{9,5},{13,1},{2,14},{6,10},... | collective-permute-start | bytes 786440 | tf_op jit(solution)/shard_map/ppermute | solution.py:558
  32.3 2.3 %collective-permute-start.4 = (bf16[4,128,128]{2,1,0:T(8,128)(2,1)S(1)}, bf16[4,128,128]{2,1,0:T(8,128)(2,1)S(1)}, u32[]{:S(2)}, u32[]{:S(2)}) collective-permute-start(bf16[4,128,128]{2,1,0:T(8,128)(2,1)S(1)} %get-tuple-element.51), channel_id=1, source_target_pairs={{0,16},{1,17},{2,18},{3,19},{4,20},{5,21},{6,22},{7,23},{8,24},{9,... | collective-permute-start | bytes 393224 | tf_op jit(solution)/shard_map/ppermute | solution.py:397
  35.5 11.3 %collective-permute-start.8 = (bf16[256,512]{1,0:T(8,128)(2,1)S(1)}, bf16[256,512]{1,0:T(8,128)(2,1)}, u32[]{:S(2)}, u32[]{:S(2)}) collective-permute-start(bf16[256,512]{1,0:T(8,128)(2,1)S(1)} %shard_map.105), channel_id=1, source_target_pairs={{0,1},{1,2},{2,3},{3,0},{4,5},{5,6},{6,7},{7,4},{8,9},{9,10},{10,1... | collective-permute-start | bytes 786440 | tf_op jit(solution)/shard_map/ppermute | solution.py:587
  37.3 11.2 %copy-start = (bf16[2048,1024]{1,0:T(8,128)(2,1)S(1)}, bf16[2048,1024]{1,0:T(8,128)(2,1)}, u32[]{:S(2)}) copy-start(bf16[2048,1024]{1,0:T(8,128)(2,1)} %weights_ref.3) | copy-start | bytes 12582916
  38.3 14.0 %collective-permute-start.5 = (bf16[256,512]{1,0:T(8,128)(2,1)S(1)}, bf16[256,512]{1,0:T(8,128)(2,1)S(1)}, u32[]{:S(2)}, u32[]{:S(2)}) collective-permute-start(bf16[256,512]{1,0:T(8,128)(2,1)S(1)} %shard_map.106), channel_id=1, source_target_pairs={{0,1},{1,2},{2,3},{3,0},{4,5},{5,6},{6,7},{7,4},{8,9},{9,10},{10,1... | collective-permute-start | bytes 786440 | tf_op jit(solution)/shard_map/ppermute | solution.py:587
  46.7 11.3 %collective-permute-start.9 = (bf16[256,512]{1,0:T(8,128)(2,1)}, bf16[256,512]{1,0:T(8,128)(2,1)S(1)}, u32[]{:S(2)}, u32[]{:S(2)}) collective-permute-start(bf16[256,512]{1,0:T(8,128)(2,1)} %collective-permute-done.8), channel_id=1, source_target_pairs={{0,1},{1,2},{2,3},{3,0},{4,5},{5,6},{6,7},{7,4},{8,9},{9,10},{10,1... | collective-permute-start | bytes 786440 | tf_op jit(solution)/shard_map/ppermute | solution.py:587
  52.7 11.1 %collective-permute-start.6 = (bf16[256,512]{1,0:T(8,128)(2,1)S(1)}, bf16[256,512]{1,0:T(8,128)(2,1)S(1)}, u32[]{:S(2)}, u32[]{:S(2)}) collective-permute-start(bf16[256,512]{1,0:T(8,128)(2,1)S(1)} %collective-permute-done.5), channel_id=1, source_target_pairs={{0,1},{1,2},{2,3},{3,0},{4,5},{5,6},{6,7},{7,4},{8,9},{9,10},{10,1... | collective-permute-start | bytes 786440 | tf_op jit(solution)/shard_map/ppermute | solution.py:587
  58.0 11.4 %collective-permute-start.10 = (bf16[256,512]{1,0:T(8,128)(2,1)S(1)}, bf16[256,512]{1,0:T(8,128)(2,1)S(1)}, u32[]{:S(2)}, u32[]{:S(2)}) collective-permute-start(bf16[256,512]{1,0:T(8,128)(2,1)S(1)} %collective-permute-done.9), channel_id=1, source_target_pairs={{0,1},{1,2},{2,3},{3,0},{4,5},{5,6},{6,7},{7,4},{8,9},{9,10},{10,1... | collective-permute-start | bytes 786440 | tf_op jit(solution)/shard_map/ppermute | solution.py:587
  63.8 10.4 %collective-permute-start.7 = (bf16[256,512]{1,0:T(8,128)(2,1)S(1)}, bf16[256,512]{1,0:T(8,128)(2,1)S(1)}, u32[]{:S(2)}, u32[]{:S(2)}) collective-permute-start(bf16[256,512]{1,0:T(8,128)(2,1)S(1)} %collective-permute-done.6), channel_id=1, source_target_pairs={{0,1},{1,2},{2,3},{3,0},{4,5},{5,6},{6,7},{7,4},{8,9},{9,10},{10,1... | collective-permute-start | bytes 786440 | tf_op jit(solution)/shard_map/ppermute | solution.py:587

commit v8 on v7

--- a/solution.py
+++ b/solution.py
@@ -140,17 +140,13 @@
     return jnp.concatenate(pieces, axis=0)
 
 
-def load_kernel(query_ref, key_ref, value_ref, taps_ref, rims_ref, *refs):
-    copied, arrived = refs[:-1], refs[-1]
+def rims_kernel(*refs):
+    *inputs, packed_ref, arrived = refs
     copies = []
-    for i, x_ref in enumerate((query_ref, key_ref, value_ref)):
+    for i, x_ref in enumerate(inputs):
         last = x_ref.at[pl.ds(x_ref.shape[0] - RIM, RIM)]
-        copies.append((last, rims_ref.at[pl.ds(i * RIM, RIM)]))
-    copies += zip((key_ref, value_ref, taps_ref), copied)
-    copies = [
-        pltpu.make_async_copy(source, target, arrived.at[i])
-        for i, (source, target) in enumerate(copies)
-    ]
+        here = packed_ref.at[pl.ds(i * RIM, RIM)]
+        copies.append(pltpu.make_async_copy(last, here, arrived.at[i]))
     for copy in copies:
         copy.start()
     for copy in copies:
@@ -158,11 +154,9 @@
 
 
 def filters_kernel(key_ref, value_ref, taps_ref, unit_ref, value_out_ref, first_ref, padded):
-    length, heads, _ = key_ref.shape
+    heads, length, _ = key_ref.shape
     for i, x_ref in enumerate((key_ref, value_ref)):
-        for c in range(length // CHUNK):
-            begin = RIM + c * CHUNK
-            padded[i, :, begin : begin + CHUNK] = jnp.swapaxes(x_ref[rows_of(c)], 0, 1).astype(F32)
+        padded[i, :, RIM:] = x_ref[...].astype(F32)
         padded[i, :, 0:RIM] = jnp.zeros((heads, RIM, padded.shape[3]), F32)
     first_ref[...] = padded[:, :, RIM : RIM + AGAIN]
 
@@ -403,21 +397,19 @@
 PARAMS = pltpu.CompilerParams(vmem_limit_bytes=12 * 1024 * 1024)
 
 
-def load(query_in, key_in, value_in, taps):
-    _, heads, depth = query_in.shape
-    like = [jax.ShapeDtypeStruct(x.shape, x.dtype) for x in (key_in, value_in, taps)]
+def pack_rims(inputs):
+    _, heads, depth = inputs[0].shape
     return pl.pallas_call(
-        load_kernel,
-        out_shape=[jax.ShapeDtypeStruct((3 * RIM, heads, depth), BF16)] + like,
-        in_specs=[HBM] * 4,
-        out_specs=[VMEM] * 4,
-        scratch_shapes=[pltpu.SemaphoreType.DMA((6,))],
-        compiler_params=PARAMS,
-    )(query_in, key_in, value_in, taps)
+        rims_kernel,
+        out_shape=jax.ShapeDtypeStruct((len(inputs) * RIM, heads, depth), BF16),
+        in_specs=[HBM] * len(inputs),
+        out_specs=VMEM,
+        scratch_shapes=[pltpu.SemaphoreType.DMA((len(inputs),))],
+    )(*inputs)
 
 
 def filters_of(key, value, taps):
-    length, heads, depth = key.shape
+    heads, length, depth = key.shape
     per_token = jax.ShapeDtypeStruct((heads, length, depth), BF16)
     return pl.pallas_call(
         filters_kernel,
@@ -543,8 +535,9 @@
     output_projection_weight,
 ):
     length, heads, depth = query_in.shape
-    last_rows, key, value, taps = load(query_in, key_in, value_in, conv_weight)
-    rims = from_behind(last_rows, ("chain", "leaf"), 1)
+    taps = conv_weight
+    rims = from_behind(pack_rims((query_in, key_in, value_in)), ("chain", "leaf"), 1)
+    key, value = (jnp.transpose(x, (1, 0, 2)) for x in (key_in, value_in))
     key, value, first = filters_of(key, value, taps)
     gain = output_norm_gain.reshape(1, depth)
     leaves = lax.axis_size("leaf")

time: 76 us -> 74.4 us (0.979)
  local copies, waits for them, and re-layouts: 4.04 us -> 2.25 us
    unnamed x22 -> x18, local copies, waits for them, and re-layouts: 3.9 us -> 0.77 us
    transpose x1, local copies, waits for them, and re-layouts: 0.14 us -> 1.34 us  [on_device(): key, value = (jnp.transpose(x, (1, 0, 2)) for x in (key_in, value_in))]
    pallas_call x1, Pallas kernels: 0.17 us -> 1.36 us  [pack_rims(): pl.pallas_call(rims_kernel, out_shape=jax.ShapeDtypeStruct((len(inputs) *...]
  transfers between devices with their start and end apart: 11 -> 11, of which waited for: 8 -> 9; matrix products, arithmetic and copies ran while one was open for 6% -> 7% of each run, Pallas kernels for 13% -> 13%
where the time goes in v8:
time: 74.4 us; the launch traced here: 74.1 us
  waiting for transfers between devices  35.5 us (48%)
  Pallas kernels  18.9 us (25%)
  starting transfers between devices  13 us (17%)
  matrix products  3.96 us (5%)
  local copies, waits for them, and re-layouts  2.25 us (3%)
    ppermute x6, waiting for transfers between devices, on_device(): following = [lax.ppermute(block, 'head', around) for block in blocks]  29.1 us
    ppermute x2, starting transfers between devices, from_behind(): lax.ppermute(value, axis, [(i, i + steps) for i in range(count - steps)])  6.14 us
    ppermute x3, waiting for transfers between devices, on_device(): lax.ppermute(own_map, 'leaf', pairs_at(k, leaves))  5.48 us
    pallas_call x1, Pallas kernels, reads_of(): pl.pallas_call(functools.partial(reads_kernel, base), out_shape=(jax.Shap...  5.45 us
    pallas_call x1, Pallas kernels, maps_of(): pl.pallas_call(functools.partial(maps_kernel, base), out_shape=(jax.Shape...  5.08 us
    dot_general x6, matrix products, on_device(): term = jnp.dot(block, rows, preferred_element_type=F32)  3.96 us
    ppermute x3, starting transfers between devices, on_device(): lax.ppermute(own_map, 'leaf', pairs_at(k, leaves))  3.55 us
    ppermute x6, starting transfers between devices, on_device(): following = [lax.ppermute(block, 'head', around) for block in blocks]  3.34 us
  transfers between devices with their start and end apart: 11, of which 9 were waited for; matrix products, arithmetic and copies ran while one was open for 7% of the time, Pallas kernels for 13%

profile of v8, /device:TPU:0, one launch (start us, length us, event | category | flops | bytes accessed | tf_op | source)
XLA Modules:
  0.0 74.1 jit_solution(1125100327156480985)
XLA Ops:
  0.0 1.4 %shard_map.101 = bf16[24,4,128]{2,1,0:T(4,128)(2,1)} custom-call(bf16[512,4,128]{2,1,0:T(4,128)(2,1)} %refs_0_.1, bf16[512,4,128]{2,1,0:T(4,128)(2,1)} %refs_1_.1, bf16[512,4,128]{2,1,0:T(4,128)(2,1)} %refs_2_.1), custom_call_target="tpu_custom_call" | custom-call | tf_op jit(solution)/shard_map/pallas_call | solution.py:402
  1.4 4.8 %collective-permute-start = (bf16[24,4,128]{2,1,0:T(4,128)(2,1)}, bf16[24,4,128]{2,1,0:T(4,128)(2,1)S(1)}, u32[]{:S(2)}, u32[]{:S(2)}) collective-permute-start(bf16[24,4,128]{2,1,0:T(4,128)(2,1)} %shard_map.101), channel_id=1, source_target_pairs={{0,4},{4,8},{8,12},{12,16},{16,20},{20,24},{24,28},{1,5},{5,9},{9,... | collective-permute-start | bytes 73736 | tf_op jit(solution)/shard_map/ppermute | solution.py:391
  6.2 1.3 %copy_bitcast_fusion.2 = (bf16[4,512,128]{2,1,0:T(8,128)(2,1)S(1)}, bf16[4,512,128]{2,1,0:T(8,128)(2,1)S(1)}) fusion(bf16[512,4,128]{2,1,0:T(4,128)(2,1)} %refs_2_.1, bf16[512,4,128]{2,1,0:T(4,128)(2,1)} %refs_1_.1), kind=kLoop, calls=%fused_computation.14 | loop fusion | bytes 2097152 | tf_op jit(solution)/shard_map/transpose | solution.py:540
  8.3 1.8 %shard_map.100 = (bf16[4,512,128]{2,1,0:T(8,128)(2,1)S(1)}, bf16[4,512,128]{2,1,0:T(8,128)(2,1)S(1)}, f32[2,4,16,128]{3,2,1,0:T(8,128)S(1)}) custom-call(bf16[4,512,128]{2,1,0:T(8,128)(2,1)S(1)} %get-tuple-element.50.key_ref, bf16[4,512,128]{2,1,0:T(8,128)(2,1)S(1)} %get-tuple-element.49.value_ref, f32[3,4,4,128]{3,2,1,0:T(4,128)S(1)} %copy-done.1), custom_call_target="tpu_custom_call" | custom-call | flops 3000000000 | bytes 4194304 | tf_op jit(solution)/shard_map/pallas_call | solution.py:414
  10.2 5.1 %shard_map.102 = (bf16[4,512,128]{2,1,0:T(8,128)(2,1)S(1)}, f32[4,512,256]{2,1,0:T(8,128)S(1)}, f32[4,3,128,256]{3,2,1,0:T(8,128)S(1)}, bf16[4,128,256]{2,1,0:T(8,128)(2,1)S(1)}) custom-call(s32[8]{0:T(128)S(1)} %copy-done.5, bf16[4,512,128]{2,1,0:T(8,128)(2,1)S(1)} %get-tuple-element.27.unit_in_ref, ...), custom_call_target="tpu_custom_call" | custom-call | flops 5000000000 | bytes 4194304 | tf_op jit(solution)/shard_map/pallas_call | solution.py:430
  15.3 1.6 %collective-permute-start.1 = (bf16[4,128,256]{2,1,0:T(8,128)(2,1)S(1)}, bf16[4,128,256]{2,1,0:T(8,128)(2,1)S(1)}, u32[]{:S(2)}, u32[]{:S(2)}) collective-permute-start(bf16[4,128,256]{2,1,0:T(8,128)(2,1)S(1)} %get-tuple-element.39.refs_0_), channel_id=1, source_target_pairs={{0,4},{4,0},{8,12},{12,8},{1,5},{5,1},{9,13},{13,9},{2,6},{6,2},{1... | collective-permute-start | bytes 786440 | tf_op jit(solution)/shard_map/ppermute | solution.py:551
  17.0 1.9 %collective-permute-start.3 = (bf16[4,128,256]{2,1,0:T(8,128)(2,1)S(1)}, bf16[4,128,256]{2,1,0:T(8,128)(2,1)S(1)}, u32[]{:S(2)}, u32[]{:S(2)}) collective-permute-start(bf16[4,128,256]{2,1,0:T(8,128)(2,1)S(1)} %get-tuple-element.39.refs_0_), channel_id=1, source_target_pairs={{0,12},{4,8},{8,4},{12,0},{1,13},{5,9},{9,5},{13,1},{2,14},{6,10},... | collective-permute-start | bytes 786440 | tf_op jit(solution)/shard_map/ppermute | solution.py:551
  19.0 5.5 %shard_map.103 = (bf16[4,512,128]{2,1,0:T(8,128)(2,1)S(1)}, f32[4,512,128]{2,1,0:T(8,128)S(1)}, f32[4,512,128]{2,1,0:T(8,128)S(1)}) custom-call(s32[8]{0:T(128)S(1)} %copy-done.5, bf16[4,512,128]{2,1,0:T(8,128)(2,1)S(1)} %bitcast.20, bf16[4,512,128]{2,1,0:T(8,128)(2,1)S(1)} %bitcast.19, f32[1,128]{1,0:T(1,128)S(1)} %bitcast.21, ...), custom_call_target="tpu_custom_call" | custom-call | flops 3000000000 | bytes 4194304 | tf_op jit(solution)/shard_map/pallas_call | solution.py:456
  24.6 5.4 %collective-permute-done.2.refs_2_ = bf16[4,128,256]{2,1,0:T(8,128)(2,1)S(1)} collective-permute-done((bf16[4,128,256]{2,1,0:T(8,128)(2,1)S(1)}, bf16[4,128,256]{2,1,0:T(8,128)(2,1)S(1)}, u32[]{:S(2)}, u32[]{:S(2)}) %collective-permute-start.2) | collective-permute-done | bytes 262176 | tf_op jit(solution)/shard_map/ppermute | solution.py:551
  30.0 1.0 %shard_map.104 = (f32[4,128,256]{2,1,0:T(8,128)S(1)}, bf16[4,128,128]{2,1,0:T(8,128)(2,1)S(1)}) custom-call(s32[1]{0:T(128)} %bitcast.1.place, bf16[4,128,256]{2,1,0:T(8,128)(2,1)S(1)} %get-tuple-element.39.refs_0_, bf16[4,128,256]{2,1,0:T(8,128)(2,1)S(1)} %collective-permute-done.1.refs_1_, bf16[4,128,256]{2,1,0:T(8,128)(2,1)S(1)} %collective-permute-done.2.refs_2_, ...), custom_call_target="tpu_custom_call" | custom-call | tf_op jit(solution)/shard_map/pallas_call | solution.py:482
  31.0 1.3 %collective-permute-start.4 = (bf16[4,128,128]{2,1,0:T(8,128)(2,1)S(1)}, bf16[4,128,128]{2,1,0:T(8,128)(2,1)S(1)}, u32[]{:S(2)}, u32[]{:S(2)}) collective-permute-start(bf16[4,128,128]{2,1,0:T(8,128)(2,1)S(1)} %get-tuple-element.43), channel_id=1, source_target_pairs={{0,16},{1,17},{2,18},{3,19},{4,20},{5,21},{6,22},{7,23},{8,24},{9,... | collective-permute-start | bytes 393224 | tf_op jit(solution)/shard_map/ppermute | solution.py:391
  32.3 1.0 %collective-permute-done.4.arrived_ref = bf16[4,128,128]{2,1,0:T(8,128)(2,1)S(1)} collective-permute-done((bf16[4,128,128]{2,1,0:T(8,128)(2,1)S(1)}, bf16[4,128,128]{2,1,0:T(8,128)(2,1)S(1)}, u32[]{:S(2)}, u32[]{:S(2)}) %collective-permute-start.4) | collective-permute-done | bytes 131104 | tf_op jit(solution)/shard_map/ppermute | solution.py:391
  33.3 0.9 %shard_map.105 = bf16[256,512]{1,0:T(8,128)(2,1)S(1)} custom-call(bf16[4,128,128]{2,1,0:T(8,128)(2,1)S(1)} %collective-permute-done.4.arrived_ref, f32[4,128,256]{2,1,0:T(8,128)S(1)} %get-tuple-element.44.before_ref, bf16[4,512,128]{2,1,0:T(8,128)(2,1)S(1)} %get-tuple-element.45.reach_ref, f32[4,512,128]{2,1,0:T(8,128)S(1)} %get-tuple-element.46.part_ref, ...), custom_call_target="tpu_custom_call" | custom-call | tf_op jit(solution)/shard_map/pallas_call | solution.py:494
  34.2 1.6 %collective-permute-start.8 = (bf16[256,512]{1,0:T(8,128)(2,1)S(1)}, bf16[256,512]{1,0:T(8,128)(2,1)}, u32[]{:S(2)}, u32[]{:S(2)}) collective-permute-start(bf16[256,512]{1,0:T(8,128)(2,1)S(1)} %shard_map.105), channel_id=1, source_target_pairs={{0,1},{1,2},{2,3},{3,0},{4,5},{5,6},{6,7},{7,4},{8,9},{9,10},{10,1... | collective-permute-start | bytes 786440 | tf_op jit(solution)/shard_map/ppermute | solution.py:580
  36.8 1.6 %collective-permute-start.5 = (bf16[256,512]{1,0:T(8,128)(2,1)S(1)}, bf16[256,512]{1,0:T(8,128)(2,1)S(1)}, u32[]{:S(2)}, u32[]{:S(2)}) collective-permute-start(bf16[256,512]{1,0:T(8,128)(2,1)S(1)} %shard_map.106), channel_id=1, source_target_pairs={{0,1},{1,2},{2,3},{3,0},{4,5},{5,6},{6,7},{7,4},{8,9},{9,10},{10,1... | collective-permute-start | bytes 786440 | tf_op jit(solution)/shard_map/ppermute | solution.py:580
  38.4 6.9 %collective-permute-done.8 = bf16[256,512]{1,0:T(8,128)(2,1)} collective-permute-done((bf16[256,512]{1,0:T(8,128)(2,1)S(1)}, bf16[256,512]{1,0:T(8,128)(2,1)}, u32[]{:S(2)}, u32[]{:S(2)}) %collective-permute-start.8) | collective-permute-done | bytes 262176 | tf_op jit(solution)/shard_map/ppermute | solution.py:580
  45.3 1.7 %fusion.2 = f32[256,1024]{1,0:T(8,128)S(1)} fusion(bf16[256,512]{1,0:T(8,128)(2,1)} %collective-permute-done.8, bf16[2048,1024]{1,0:T(8,128)(2,1)} %weights_ref.3, s32[]{:T(128)S(6)} %select_n.10), kind=kOutput, calls=%fused_computation.6 | convolution fusion | flops 268435456 | bytes 2359300 | tf_op jit(solution)/shard_map/dot_general | solution.py:582
  47.5 3.3 %collective-permute-done.5 = bf16[256,512]{1,0:T(8,128)(2,1)S(1)} collective-permute-done((bf16[256,512]{1,0:T(8,128)(2,1)S(1)}, bf16[256,512]{1,0:T(8,128)(2,1)S(1)}, u32[]{:S(2)}, u32[]{:S(2)}) %collective-permute-start.5) | collective-permute-done | bytes 262176 | tf_op jit(solution)/shard_map/ppermute | solution.py:580
  51.8 4.8 %collective-permute-done.9 = bf16[256,512]{1,0:T(8,128)(2,1)S(1)} collective-permute-done((bf16[256,512]{1,0:T(8,128)(2,1)}, bf16[256,512]{1,0:T(8,128)(2,1)S(1)}, u32[]{:S(2)}, u32[]{:S(2)}) %collective-permute-start.9) | collective-permute-done | bytes 262176 | tf_op jit(solution)/shard_map/ppermute | solution.py:580
  56.5 5.8 %collective-permute-done.6 = bf16[256,512]{1,0:T(8,128)(2,1)S(1)} collective-permute-done((bf16[256,512]{1,0:T(8,128)(2,1)S(1)}, bf16[256,512]{1,0:T(8,128)(2,1)S(1)}, u32[]{:S(2)}, u32[]{:S(2)}) %collective-permute-start.6) | collective-permute-done | bytes 262176 | tf_op jit(solution)/shard_map/ppermute | solution.py:580
  63.2 4.7 %collective-permute-done.10.block_ref = bf16[256,512]{1,0:T(8,128)(2,1)S(1)} collective-permute-done((bf16[256,512]{1,0:T(8,128)(2,1)S(1)}, bf16[256,512]{1,0:T(8,128)(2,1)S(1)}, u32[]{:S(2)}, u32[]{:S(2)}) %collective-permute-start.10) | collective-permute-done | bytes 262176 | tf_op jit(solution)/shard_map/ppermute | solution.py:580
  68.0 1.2 %shard_map.107.refs_0_ = bf16[512,1024]{1,0:T(8,128)(2,1)} custom-call(s32[1]{0:T(128)} %bitcast.section, f32[256,1024]{1,0:T(8,128)S(1)} %convolution_add_fusion.total_ref, bf16[256,512]{1,0:T(8,128)(2,1)S(1)} %collective-permute-done.10.block_ref, bf16[2048,1024]{1,0:T(8,128)(2,1)S(1)} %copy-done), custom_call_target="tpu_custom_call" | custom-call | tf_op jit(solution)/shard_map/pallas_call | solution.py:507
  69.1 3.6 %collective-permute-done.7.block_ref = bf16[256,512]{1,0:T(8,128)(2,1)S(1)} collective-permute-done((bf16[256,512]{1,0:T(8,128)(2,1)S(1)}, bf16[256,512]{1,0:T(8,128)(2,1)S(1)}, u32[]{:S(2)}, u32[]{:S(2)}) %collective-permute-start.7) | collective-permute-done | bytes 262176 | tf_op jit(solution)/shard_map/ppermute | solution.py:580
  72.8 1.2 %shard_map.108 = bf16[512,1024]{1,0:T(8,128)(2,1)} custom-call(s32[1]{0:T(128)} %bitcast.section, f32[256,1024]{1,0:T(8,128)S(1)} %convolution_add_fusion.2.total_ref, bf16[256,512]{1,0:T(8,128)(2,1)S(1)} %collective-permute-done.7.block_ref, bf16[2048,1024]{1,0:T(8,128)(2,1)S(1)} %copy-done, ...), custom_call_target="tpu_custom_call", output_to_operand_aliasing={{}: (4, {})} | custom-call | tf_op jit(solution)/shard_map/pallas_call | solution.py:507
  (34 shorter events, 4.4 us)
Async XLA Ops:
  1.4 8.7 %collective-permute-start = (bf16[24,4,128]{2,1,0:T(4,128)(2,1)}, bf16[24,4,128]{2,1,0:T(4,128)(2,1)S(1)}, u32[]{:S(2)}, u32[]{:S(2)}) collective-permute-start(bf16[24,4,128]{2,1,0:T(4,128)(2,1)} %shard_map.101), channel_id=1, source_target_pairs={{0,4},{4,8},{8,12},{12,16},{16,20},{20,24},{24,28},{1,5},{5,9},{9,... | collective-permute-start | bytes 73736 | tf_op jit(solution)/shard_map/ppermute | solution.py:391
  7.6 0.7 copy-start.1
  8.3 1.8 %copy-start.2 = (f32[3,4,4,128]{3,2,1,0:T(4,128)S(1)}, f32[3,4,4,128]{3,2,1,0:T(4,128)}, u32[]{:S(2)}) copy-start(f32[3,4,4,128]{3,2,1,0:T(4,128)} %taps_ref.5) | copy-start | bytes 73732
  8.3 1.8 %copy-start.3 = (f32[4,512]{1,0:T(4,128)S(1)}, f32[4,512]{1,0:T(4,128)}, u32[]{:S(2)}) copy-start(f32[4,512]{1,0:T(4,128)} %decay_ref.3) | copy-start | bytes 24580
  8.3 1.8 %copy-start.4 = (f32[4,512]{1,0:T(4,128)S(1)}, f32[4,512]{1,0:T(4,128)}, u32[]{:S(2)}) copy-start(f32[4,512]{1,0:T(4,128)} %strength_ref.3) | copy-start | bytes 24580
  8.3 1.8 %copy-start.5 = (s32[8]{0:T(128)S(1)}, s32[8]{0:T(128)}, u32[]{:S(2)}) copy-start(s32[8]{0:T(128)} %resets.3) | copy-start | bytes 100
  10.2 8.7 %copy-start.8 = (bf16[512,4,128]{2,1,0:T(4,128)(2,1)S(1)}, bf16[512,4,128]{2,1,0:T(4,128)(2,1)}, u32[]{:S(2)}) copy-start(bf16[512,4,128]{2,1,0:T(4,128)(2,1)} %param.13) | copy-start | bytes 1572868
  10.2 8.7 %copy-start.7 = (bf16[512,4,128]{2,1,0:T(4,128)(2,1)S(1)}, bf16[512,4,128]{2,1,0:T(4,128)(2,1)}, u32[]{:S(2)}) copy-start(bf16[512,4,128]{2,1,0:T(4,128)(2,1)} %refs_0_.1) | copy-start | bytes 1572868
  10.2 8.8 %copy-start.6 = (f32[128]{0:T(128)S(1)}, f32[128]{0:T(128)}, u32[]{:S(2)}) copy-start(f32[128]{0:T(128)} %param.18) | copy-start | bytes 1540
  15.3 9.3 %collective-permute-start.1 = (bf16[4,128,256]{2,1,0:T(8,128)(2,1)S(1)}, bf16[4,128,256]{2,1,0:T(8,128)(2,1)S(1)}, u32[]{:S(2)}, u32[]{:S(2)}) collective-permute-start(bf16[4,128,256]{2,1,0:T(8,128)(2,1)S(1)} %get-tuple-element.39.refs_0_), channel_id=1, source_target_pairs={{0,4},{4,0},{8,12},{12,8},{1,5},{5,1},{9,13},{13,9},{2,6},{6,2},{1... | collective-permute-start | bytes 786440 | tf_op jit(solution)/shard_map/ppermute | solution.py:551
  16.9 13.1 %collective-permute-start.2 = (bf16[4,128,256]{2,1,0:T(8,128)(2,1)S(1)}, bf16[4,128,256]{2,1,0:T(8,128)(2,1)S(1)}, u32[]{:S(2)}, u32[]{:S(2)}) collective-permute-start(bf16[4,128,256]{2,1,0:T(8,128)(2,1)S(1)} %get-tuple-element.39.refs_0_), channel_id=1, source_target_pairs={{0,8},{4,12},{8,0},{12,4},{1,9},{5,13},{9,1},{13,5},{2,10},{6,14},... | collective-permute-start | bytes 786440 | tf_op jit(solution)/shard_map/ppermute | solution.py:551
  17.0 13.0 %collective-permute-start.3 = (bf16[4,128,256]{2,1,0:T(8,128)(2,1)S(1)}, bf16[4,128,256]{2,1,0:T(8,128)(2,1)S(1)}, u32[]{:S(2)}, u32[]{:S(2)}) collective-permute-start(bf16[4,128,256]{2,1,0:T(8,128)(2,1)S(1)} %get-tuple-element.39.refs_0_), channel_id=1, source_target_pairs={{0,12},{4,8},{8,4},{12,0},{1,13},{5,9},{9,5},{13,1},{2,14},{6,10},... | collective-permute-start | bytes 786440 | tf_op jit(solution)/shard_map/ppermute | solution.py:551
  31.0 2.3 %collective-permute-start.4 = (bf16[4,128,128]{2,1,0:T(8,128)(2,1)S(1)}, bf16[4,128,128]{2,1,0:T(8,128)(2,1)S(1)}, u32[]{:S(2)}, u32[]{:S(2)}) collective-permute-start(bf16[4,128,128]{2,1,0:T(8,128)(2,1)S(1)} %get-tuple-element.43), channel_id=1, source_target_pairs={{0,16},{1,17},{2,18},{3,19},{4,20},{5,21},{6,22},{7,23},{8,24},{9,... | collective-permute-start | bytes 393224 | tf_op jit(solution)/shard_map/ppermute | solution.py:391
  34.2 11.1 %collective-permute-start.8 = (bf16[256,512]{1,0:T(8,128)(2,1)S(1)}, bf16[256,512]{1,0:T(8,128)(2,1)}, u32[]{:S(2)}, u32[]{:S(2)}) collective-permute-start(bf16[256,512]{1,0:T(8,128)(2,1)S(1)} %shard_map.105), channel_id=1, source_target_pairs={{0,1},{1,2},{2,3},{3,0},{4,5},{5,6},{6,7},{7,4},{8,9},{9,10},{10,1... | collective-permute-start | bytes 786440 | tf_op jit(solution)/shard_map/ppermute | solution.py:580
  35.8 11.2 %copy-start = (bf16[2048,1024]{1,0:T(8,128)(2,1)S(1)}, bf16[2048,1024]{1,0:T(8,128)(2,1)}, u32[]{:S(2)}) copy-start(bf16[2048,1024]{1,0:T(8,128)(2,1)} %weights_ref.3) | copy-start | bytes 12582916
  36.8 14.0 %collective-permute-start.5 = (bf16[256,512]{1,0:T(8,128)(2,1)S(1)}, bf16[256,512]{1,0:T(8,128)(2,1)S(1)}, u32[]{:S(2)}, u32[]{:S(2)}) collective-permute-start(bf16[256,512]{1,0:T(8,128)(2,1)S(1)} %shard_map.106), channel_id=1, source_target_pairs={{0,1},{1,2},{2,3},{3,0},{4,5},{5,6},{6,7},{7,4},{8,9},{9,10},{10,1... | collective-permute-start | bytes 786440 | tf_op jit(solution)/shard_map/ppermute | solution.py:580
  45.3 11.3 %collective-permute-start.9 = (bf16[256,512]{1,0:T(8,128)(2,1)}, bf16[256,512]{1,0:T(8,128)(2,1)S(1)}, u32[]{:S(2)}, u32[]{:S(2)}) collective-permute-start(bf16[256,512]{1,0:T(8,128)(2,1)} %collective-permute-done.8), channel_id=1, source_target_pairs={{0,1},{1,2},{2,3},{3,0},{4,5},{5,6},{6,7},{7,4},{8,9},{9,10},{10,1... | collective-permute-start | bytes 786440 | tf_op jit(solution)/shard_map/ppermute | solution.py:580
  51.2 11.1 %collective-permute-start.6 = (bf16[256,512]{1,0:T(8,128)(2,1)S(1)}, bf16[256,512]{1,0:T(8,128)(2,1)S(1)}, u32[]{:S(2)}, u32[]{:S(2)}) collective-permute-start(bf16[256,512]{1,0:T(8,128)(2,1)S(1)} %collective-permute-done.5), channel_id=1, source_target_pairs={{0,1},{1,2},{2,3},{3,0},{4,5},{5,6},{6,7},{7,4},{8,9},{9,10},{10,1... | collective-permute-start | bytes 786440 | tf_op jit(solution)/shard_map/ppermute | solution.py:580
  56.5 11.4 %collective-permute-start.10 = (bf16[256,512]{1,0:T(8,128)(2,1)S(1)}, bf16[256,512]{1,0:T(8,128)(2,1)S(1)}, u32[]{:S(2)}, u32[]{:S(2)}) collective-permute-start(bf16[256,512]{1,0:T(8,128)(2,1)S(1)} %collective-permute-done.9), channel_id=1, source_target_pairs={{0,1},{1,2},{2,3},{3,0},{4,5},{5,6},{6,7},{7,4},{8,9},{9,10},{10,1... | collective-permute-start | bytes 786440 | tf_op jit(solution)/shard_map/ppermute | solution.py:580
  62.3 10.4 %collective-permute-start.7 = (bf16[256,512]{1,0:T(8,128)(2,1)S(1)}, bf16[256,512]{1,0:T(8,128)(2,1)S(1)}, u32[]{:S(2)}, u32[]{:S(2)}) collective-permute-start(bf16[256,512]{1,0:T(8,128)(2,1)S(1)} %collective-permute-done.6), channel_id=1, source_target_pairs={{0,1},{1,2},{2,3},{3,0},{4,5},{5,6},{6,7},{7,4},{8,9},{9,10},{10,1... | collective-permute-start | bytes 786440 | tf_op jit(solution)/shard_map/ppermute | solution.py:580

commit v9 on v8

--- a/solution.py
+++ b/solution.py
@@ -9,7 +9,7 @@
 
 BLOCK = 64
 CHUNK = 128
-PARTS = 2
+GROUPS = 2
 RIM = 8
 EPSILON = 1e-06
 FAR = -1e30
@@ -100,8 +100,11 @@
     powers = [d.astype(BF16) for d in diagonal]
     squares = [mul(p, p).astype(BF16) for p in powers]
     inverse = [eye - d for d in diagonal]
-    fourths = [mul(s, s).astype(BF16) for s in squares]
-    inverse = [x + mul(x.astype(BF16), s) for x, s in zip(inverse, squares)]
+    stacked = [
+        mul(jnp.concatenate([s, x.astype(BF16)], axis=0), s) for x, s in zip(inverse, squares)
+    ]
+    fourths = [both[:CHUNK].astype(BF16) for both in stacked]
+    inverse = [x + both[CHUNK:] for x, both in zip(inverse, stacked)]
     inverse = [x + mul(x.astype(BF16), s) for x, s in zip(inverse, fourths)]
     size = 8
     while size < CHUNK:
@@ -176,11 +179,12 @@
 
 def maps_kernel(
     base, resets, unit_in_ref, value_in_ref, first_ref, rim_ref, taps_ref, decay_ref, strength_ref,
-    unit_ref, solved_ref, starts_ref, map_ref,
-    rims, padded, value_s, step_s,
+    unit_ref, solved_ref, starts_ref, *refs,
 ):
+    *map_refs, rims, padded, value_s, step_s = refs
     heads, length, depth = unit_ref.shape
     chunks = length // CHUNK
+    size = heads // len(map_refs)
     total_heads = decay_ref.shape[0]
     row, col = indices()
     rims[...] = rim_ref[...].astype(F32)
@@ -254,7 +258,7 @@
     for c in range(half + 1, chunks):
         rest = [compose(step_s[g, c], rest[g]) for g in every]
     for g in every:
-        map_ref[g] = compose(rest[g], states[g]).astype(BF16)
+        map_refs[g // size][g % size] = compose(rest[g], states[g]).astype(BF16)
     for c in range(half, chunks):
         for g in every:
             starts_ref[g, c - 1] = states[g]
@@ -355,32 +359,32 @@
             ref[h] = states[h][:, :depth]
 
 
-def outputs_kernel(begin, arrived_ref, before_ref, reach_ref, part_ref, gating_ref, normed_ref):
-    heads, _, depth = reach_ref.shape
-    for h in range(heads):
-        before = before_ref[h]
-        incoming = mul_split(before[:, :depth], arrived_ref[h].astype(F32)) + before[:, depth:]
+def outputs_kernel(base, arrived_ref, before_ref, reach_ref, part_ref, gating_ref, normed_ref):
+    heads, depth, _ = arrived_ref.shape
+    for g in range(heads):
+        h = base + g
+        before = before_ref[g]
+        incoming = mul_split(before[:, :depth], arrived_ref[g].astype(F32)) + before[:, depth:]
         high, low = split(incoming)
         for c in range(normed_ref.shape[0] // CHUNK):
-            here = slice(begin + c * CHUNK, begin + (c + 1) * CHUNK)
+            here = rows_of(c)
             reach = reach_ref[h, here]
             core = part_ref[h, here] + (mul(reach, high) + mul(reach, low))
             scale = lax.rsqrt(jnp.sum(core * core, axis=-1, keepdims=True) / depth + EPSILON)
-            normed_ref[rows_of(c), h * depth : (h + 1) * depth] = (
+            normed_ref[here, g * depth : (g + 1) * depth] = (
                 core * scale * gating_ref[h, here]
             ).astype(BF16)
 
 
-def last_kernel(begin, section, total_ref, block_ref, weights_ref, *refs):
-    out_ref, tiles, written = refs[-3:]
+def last_kernel(section, first_ref, second_ref, block_ref, weights_ref, out_ref, tiles, written):
     width = block_ref.shape[1]
     rows = weights_ref[pl.ds(pl.multiple_of(section[0] * width, width), width), :]
     copies = []
-    for i in range(total_ref.shape[0] // CHUNK):
+    for i in range(first_ref.shape[0] // CHUNK):
         here = rows_of(i)
-        tiles[here] = (total_ref[here] + mul(block_ref[here], rows)).astype(BF16)
-        target = out_ref.at[pl.ds(begin + i * CHUNK, CHUNK)]
-        copies.append(pltpu.make_async_copy(tiles.at[here], target, written.at[i]))
+        total = (first_ref[here] + second_ref[here]) + mul(block_ref[here], rows)
+        tiles[here] = total.astype(BF16)
+        copies.append(pltpu.make_async_copy(tiles.at[here], out_ref.at[here], written.at[i]))
         copies[-1].start()
     for copy in copies:
         copy.wait()
@@ -405,6 +409,8 @@
         in_specs=[HBM] * len(inputs),
         out_specs=VMEM,
         scratch_shapes=[pltpu.SemaphoreType.DMA((len(inputs),))],
+        compiler_params=pltpu.CompilerParams(vmem_limit_bytes=63 * 2**20),
+        cost_estimate=pl.CostEstimate(flops=10**9, bytes_accessed=2**16, transcendentals=0),
     )(*inputs)
 
 
@@ -433,10 +439,10 @@
             jax.ShapeDtypeStruct((heads, length, depth), BF16),
             jax.ShapeDtypeStruct((heads, length, 2 * depth), F32),
             jax.ShapeDtypeStruct((heads, chunks - 1, depth, 2 * depth), F32),
-            jax.ShapeDtypeStruct((heads, depth, 2 * depth), BF16),
+            *[jax.ShapeDtypeStruct((heads // GROUPS, depth, 2 * depth), BF16)] * GROUPS,
         ),
         in_specs=[SMEM] + [VMEM] * 7,
-        out_specs=[VMEM] * 4,
+        out_specs=[VMEM] * (3 + GROUPS),
         scratch_shapes=[
             pltpu.VMEM(rims.shape, F32),
             pltpu.VMEM((heads, 2, RIM + AGAIN, depth), F32),
@@ -489,33 +495,31 @@
     )(place, *maps)
 
 
-def outputs_of(begin, count, arrived, before, reads):
-    heads, _, depth = reads[0].shape
+def outputs_of(base, arrived, before, reads):
+    heads, depth, _ = arrived.shape
+    length = reads[0].shape[1]
     return pl.pallas_call(
-        functools.partial(outputs_kernel, begin),
-        out_shape=jax.ShapeDtypeStruct((count, heads * depth), BF16),
+        functools.partial(outputs_kernel, base),
+        out_shape=jax.ShapeDtypeStruct((length, heads * depth), BF16),
         in_specs=[VMEM] * 5,
         out_specs=VMEM,
         compiler_params=PARAMS,
     )(arrived, before, *reads)
 
 
-def last_projected(begin, section, total, block, weights, length, result):
-    count, columns = total.shape
-    whole = pl.BlockSpec(memory_space=pl.ANY)
-    earlier = [] if result is None else [result]
+def last_projected(section, first, second, block, weights):
+    length, columns = first.shape
     return pl.pallas_call(
-        functools.partial(last_kernel, begin),
+        last_kernel,
         out_shape=jax.ShapeDtypeStruct((length, columns), BF16),
-        in_specs=[SMEM] + [VMEM] * 3 + [whole] * len(earlier),
-        out_specs=whole,
+        in_specs=[SMEM] + [VMEM] * 4,
+        out_specs=pl.BlockSpec(memory_space=pl.ANY),
         scratch_shapes=[
-            pltpu.VMEM((count, columns), BF16),
-            pltpu.SemaphoreType.DMA((count // CHUNK,)),
+            pltpu.VMEM((length, columns), BF16),
+            pltpu.SemaphoreType.DMA((length // CHUNK,)),
         ],
-        input_output_aliases={4: 0} if earlier else {},
         compiler_params=PARAMS,
-    )(section.astype(jnp.int32).reshape(1), total, block, weights, *earlier)
+    )(section.astype(jnp.int32).reshape(1), first, second, block, weights)
 
 
 def after(first, *values):
@@ -544,51 +548,51 @@
     place = lax.axis_index("leaf").astype(jnp.int32).reshape(1)
 
     links = lax.axis_size("chain") - 1
-    *made, own_map = maps_of(
+    unit_key, solved, starts, *own_maps = maps_of(
         0, heads, doc_resets, key, value, first, rims, taps, log_decay, write_strength
     )
-    maps = [own_map] + [
-        lax.ppermute(own_map, "leaf", pairs_at(k, leaves)) for k in range(1, leaves)
+    exchanged = [
+        [own_map] + [lax.ppermute(own_map, "leaf", pairs_at(k, leaves)) for k in range(1, leaves)]
+        for own_map in own_maps
     ]
-    query_in, gate_in = after(own_map, query_in, gate_in)
+    query_in, gate_in = after(own_maps[-1], query_in, gate_in)
     query, gate = (jnp.transpose(x, (1, 0, 2)) for x in (query_in, gate_in))
     reads = reads_of(
-        0, heads, doc_resets, query, gate, gain, rims, taps, log_decay, write_strength, made
+        0, heads, doc_resets, query, gate, gain, rims, taps, log_decay, write_strength,
+        (unit_key, solved, starts),
     )
-    maps, reads = lax.optimization_barrier((maps, reads))
-    before, state, *trans = join(place, maps, links)
-    arrived = from_behind(state.astype(BF16), "chain", 1)
-    for _ in range(links - 1):
-        passed = jnp.einsum(
-            "hij,hjk->hik", trans[0], arrived.astype(F32), precision=lax.Precision.HIGHEST
-        )
-        arrived = from_behind((passed + state).astype(BF16), "chain", 1)
-    count = length // PARTS
+    size = heads // GROUPS
     blocks = []
-    for p in range(PARTS):
-        blocks.append(outputs_of(p * count, count, arrived, before, reads))
-        arrived = after(blocks[p], arrived)[0]
+    for g, maps in enumerate(exchanged):
+        earlier = blocks[-1] if blocks else reads[0]
+        maps = after(earlier, *maps)
+        before, state, *trans = join(place, maps, links)
+        arrived = from_behind(state.astype(BF16), "chain", 1)
+        for _ in range(links - 1):
+            passed = jnp.einsum(
+                "hij,hjk->hik", trans[0], arrived.astype(F32), precision=lax.Precision.HIGHEST
+            )
+            arrived = from_behind((passed + state).astype(BF16), "chain", 1)
+        blocks.append(outputs_of(g * size, arrived, before, reads))
 
     ring = lax.axis_size("head")
     mine = lax.axis_index("head")
-    width = heads * depth
+    width = size * depth
+    weights = output_projection_weight
     around = [(i, (i + 1) % ring) for i in range(ring)]
-    mixed = [None] * PARTS
-    for k in range(ring - 1):
+    sums = [None] * GROUPS
+    for k in range(ring):
         owner = lax.rem(mine + ring - k, ring)
-        rows = lax.dynamic_slice_in_dim(output_projection_weight, owner * width, width, 0)
-        following = [lax.ppermute(block, "head", around) for block in blocks]
-        for p, block in enumerate(blocks):
+        last = k + 1 == ring
+        following = blocks if last else [lax.ppermute(x, "head", around) for x in blocks]
+        for g, block in enumerate(blocks):
+            section = owner * GROUPS + g
+            if last and g + 1 == GROUPS:
+                return last_projected(section, *sums, block, weights)
+            rows = lax.dynamic_slice_in_dim(weights, section * width, width, 0)
             term = jnp.dot(block, rows, preferred_element_type=F32)
-            mixed[p] = term if mixed[p] is None else mixed[p] + term
+            sums[g] = term if sums[g] is None else sums[g] + term
         blocks = following
-    result = None
-    for p, block in enumerate(blocks):
-        result = last_projected(
-            p * count, lax.rem(mine + 1, ring), mixed[p], block, output_projection_weight, length,
-            result,
-        )
-    return result
 
 
 def solution(mesh):

time: 74.4 us -> 79.7 us (1.071)
  waiting for transfers between devices: 35.5 us -> 28.4 us
  starting transfers between devices: 13 us -> 19.9 us
  local copies, waits for them, and re-layouts: 2.25 us -> 7.73 us
    unnamed x18 -> x34, local copies, waits for them, and re-layouts: 0.77 us -> 6.41 us
    ppermute x3 -> x6, waiting for transfers between devices: 5.48 us -> 0.02 us  [on_device(): lax.ppermute(own_map, 'leaf', pairs_at(k, leaves))]
    ppermute x3 -> x6, starting transfers between devices: 3.55 us -> 8.14 us  [on_device(): lax.ppermute(own_map, 'leaf', pairs_at(k, leaves))]
    ppermute x2 -> x3, starting transfers between devices: 6.14 us -> 8.28 us  [from_behind(): lax.ppermute(value, axis, [(i, i + steps) for i in range(count - steps)])]
    ppermute x6, waiting for transfers between devices: 29.1 us -> 27.3 us  [on_device(): lax.ppermute(x, 'head', around)]
    pallas_call x4 -> x3, Pallas kernels: 4.25 us -> 2.74 us  [the longest x2 1.45 us: outputs_of(): pl.pallas_call(functools.partial(outputs_kernel, base), out_shape=jax.Sha...]
    pallas_call x1 -> x2, Pallas kernels: 1.02 us -> 2.12 us  [join(): pl.pallas_call(functools.partial(join_kernel, count), out_shape=(pair, *t...]
    dot_general x6 -> x7, matrix products: 3.96 us -> 4.34 us  [on_device(): term = jnp.dot(block, rows, preferred_element_type=F32)]
  transfers between devices with their start and end apart: 11 -> 15, of which waited for: 9 -> 7; matrix products, arithmetic and copies ran while one was open for 7% -> 7% of each run, Pallas kernels for 13% -> 14%
where the time goes in v9:
time: 79.7 us; the launch traced here: 79.4 us
  waiting for transfers between devices  28.4 us (36%)
  starting transfers between devices  19.9 us (25%)
  Pallas kernels  18.5 us (23%)
  local copies, waits for them, and re-layouts  7.73 us (10%)
  matrix products  4.34 us (5%)
    ppermute x6, waiting for transfers between devices, on_device(): lax.ppermute(x, 'head', around)  27.3 us
    ppermute x3, starting transfers between devices, from_behind(): lax.ppermute(value, axis, [(i, i + steps) for i in range(count - steps)])  8.28 us
    ppermute x6, starting transfers between devices, on_device(): lax.ppermute(own_map, 'leaf', pairs_at(k, leaves))  8.14 us
    unnamed x34, local copies, waits for them, and re-layouts  6.41 us
    pallas_call x1, Pallas kernels, reads_of(): pl.pallas_call(functools.partial(reads_kernel, base), out_shape=(jax.Shap...  5.42 us
    pallas_call x1, Pallas kernels, maps_of(): pl.pallas_call(functools.partial(maps_kernel, base), out_shape=(jax.Shape...  5.07 us
    dot_general x7, matrix products, on_device(): term = jnp.dot(block, rows, preferred_element_type=F32)  4.34 us
    ppermute x6, starting transfers between devices, on_device(): lax.ppermute(x, 'head', around)  3.46 us
  transfers between devices with their start and end apart: 15, of which 7 were waited for; matrix products, arithmetic and copies ran while one was open for 7% of the time, Pallas kernels for 14%

profile of v9, /device:TPU:0, one launch (start us, length us, event | category | flops | bytes accessed | tf_op | source)
XLA Modules:
  0.0 79.4 jit_solution(13141980010612314989)
XLA Ops:
  0.0 1.4 %shard_map.101 = bf16[24,4,128]{2,1,0:T(4,128)(2,1)} custom-call(bf16[512,4,128]{2,1,0:T(4,128)(2,1)} %refs_0_.1, bf16[512,4,128]{2,1,0:T(4,128)(2,1)} %refs_1_.1, bf16[512,4,128]{2,1,0:T(4,128)(2,1)} %refs_2_.1), custom_call_target="tpu_custom_call" | custom-call | flops 1000000000 | bytes 65536 | tf_op jit(solution)/shard_map/pallas_call | solution.py:406
  1.4 4.8 %collective-permute-start = (bf16[24,4,128]{2,1,0:T(4,128)(2,1)}, bf16[24,4,128]{2,1,0:T(4,128)(2,1)S(1)}, u32[]{:S(2)}, u32[]{:S(2)}) collective-permute-start(bf16[24,4,128]{2,1,0:T(4,128)(2,1)} %shard_map.101), channel_id=1, source_target_pairs={{0,4},{4,8},{8,12},{12,16},{16,20},{20,24},{24,28},{1,5},{5,9},{9,... | collective-permute-start | bytes 73736 | tf_op jit(solution)/shard_map/ppermute | solution.py:395
  7.5 1.8 %shard_map.100 = (bf16[4,512,128]{2,1,0:T(8,128)(2,1)S(1)}, bf16[4,512,128]{2,1,0:T(8,128)(2,1)S(1)}, f32[2,4,16,128]{3,2,1,0:T(8,128)S(1)}) custom-call(bf16[4,512,128]{2,1,0:T(8,128)(2,1)S(1)} %get-tuple-element.56.key_ref, bf16[4,512,128]{2,1,0:T(8,128)(2,1)S(1)} %get-tuple-element.55.value_ref, f32[3,4,4,128]{3,2,1,0:T(4,128)S(1)} %copy-done.3), custom_call_target="tpu_custom_call" | custom-call | flops 3000000000 | bytes 4194304 | tf_op jit(solution)/shard_map/pallas_call | solution.py:420
  9.4 5.1 %shard_map.102 = (bf16[4,512,128]{2,1,0:T(8,128)(2,1)S(1)}, f32[4,512,256]{2,1,0:T(8,128)S(1)}, f32[4,3,128,256]{3,2,1,0:T(8,128)S(1)}, bf16[2,128,256]{2,1,0:T(8,128)(2,1)S(1)}, bf16[2,128,256]{2,1,0:T(8,128)(2,1)S(1)}) custom-call(s32[8]{0:T(128)S(1)} %copy-done.6, bf16[4,512,128]{2,1,0:T(8,128)(2,1)S(1)} %get-tuple-element.30.unit_in_ref, ...), custom_call_target="tpu_custom_call" | custom-call | flops 5000000000 | bytes 4194304 | tf_op jit(solution)/shard_map/pallas_call | solution.py:436
  14.5 1.3 %copy-done.8 = f32[4,512,256]{2,1,0:T(8,128)} copy-done((f32[4,512,256]{2,1,0:T(8,128)}, f32[4,512,256]{2,1,0:T(8,128)S(1)}, u32[]{:S(2)}) %copy-start.8) | copy-done | bytes 2097176
  17.7 1.5 %collective-permute-start.1 = (bf16[2,128,256]{2,1,0:T(8,128)(2,1)S(1)}, bf16[2,128,256]{2,1,0:T(8,128)(2,1)S(1)}, u32[]{:S(2)}, u32[]{:S(2)}) collective-permute-start(bf16[2,128,256]{2,1,0:T(8,128)(2,1)S(1)} %get-tuple-element.41.refs_0_), channel_id=1, source_target_pairs={{0,4},{4,0},{8,12},{12,8},{1,5},{5,1},{9,13},{13,9},{2,6},{6,2},{1... | collective-permute-start | bytes 393224 | tf_op jit(solution)/shard_map/ppermute | solution.py:555
  21.2 1.9 %collective-permute-start.10 = (bf16[2,128,256]{2,1,0:T(8,128)(2,1)S(1)}, bf16[2,128,256]{2,1,0:T(8,128)(2,1)S(1)}, u32[]{:S(2)}, u32[]{:S(2)}) collective-permute-start(bf16[2,128,256]{2,1,0:T(8,128)(2,1)S(1)} %get-tuple-element.49.refs_0_), channel_id=1, source_target_pairs={{0,12},{4,8},{8,4},{12,0},{1,13},{5,9},{9,5},{13,1},{2,14},{6,10},... | collective-permute-start | bytes 393224 | tf_op jit(solution)/shard_map/ppermute | solution.py:555
  23.1 1.4 %collective-permute-start.8 = (bf16[2,128,256]{2,1,0:T(8,128)(2,1)S(1)}, bf16[2,128,256]{2,1,0:T(8,128)(2,1)S(1)}, u32[]{:S(2)}, u32[]{:S(2)}) collective-permute-start(bf16[2,128,256]{2,1,0:T(8,128)(2,1)S(1)} %get-tuple-element.49.refs_0_), channel_id=1, source_target_pairs={{0,4},{4,0},{8,12},{12,8},{1,5},{5,1},{9,13},{13,9},{2,6},{6,2},{1... | collective-permute-start | bytes 393224 | tf_op jit(solution)/shard_map/ppermute | solution.py:555
  25.4 1.3 %collective-permute-start.9 = (bf16[2,128,256]{2,1,0:T(8,128)(2,1)S(1)}, bf16[2,128,256]{2,1,0:T(8,128)(2,1)S(1)}, u32[]{:S(2)}, u32[]{:S(2)}) collective-permute-start(bf16[2,128,256]{2,1,0:T(8,128)(2,1)S(1)} %get-tuple-element.49.refs_0_), channel_id=1, source_target_pairs={{0,8},{4,12},{8,0},{12,4},{1,9},{5,13},{9,1},{13,5},{2,10},{6,14},... | collective-permute-start | bytes 393224 | tf_op jit(solution)/shard_map/ppermute | solution.py:555
  26.7 1.4 %copy-done.11 = f32[4,3,128,256]{3,2,1,0:T(8,128)S(1)} copy-done((f32[4,3,128,256]{3,2,1,0:T(8,128)S(1)}, f32[4,3,128,256]{3,2,1,0:T(8,128)}, u32[]{:S(2)}) %copy-start.11) | copy-done | bytes 1572888
  29.2 5.4 %shard_map.103 = (bf16[4,512,128]{2,1,0:T(8,128)(2,1)S(1)}, f32[4,512,128]{2,1,0:T(8,128)S(1)}, f32[4,512,128]{2,1,0:T(8,128)S(1)}) custom-call(s32[8]{0:T(128)S(1)} %copy-done.6, bf16[4,512,128]{2,1,0:T(8,128)(2,1)S(1)} %bitcast.21, bf16[4,512,128]{2,1,0:T(8,128)(2,1)S(1)} %bitcast.20, f32[1,128]{1,0:T(1,128)S(1)} %bitcast.22, ...), custom_call_target="tpu_custom_call" | custom-call | flops 3000000000 | bytes 4194304 | tf_op jit(solution)/shard_map/pallas_call | solution.py:462
  34.6 1.4 %shard_map.104 = (f32[2,128,256]{2,1,0:T(8,128)S(1)}, bf16[2,128,128]{2,1,0:T(8,128)(2,1)}) custom-call(s32[1]{0:T(128)} %bitcast.1.place, bf16[2,128,256]{2,1,0:T(8,128)(2,1)S(1)} %get-tuple-element.41.refs_0_, bf16[2,128,256]{2,1,0:T(8,128)(2,1)S(1)} %copy-done.2, bf16[2,128,256]{2,1,0:T(8,128)(2,1)S(1)} %collective-permute-done.2.refs_2_, ...), custom_call_target="tpu_custom_call" | custom-call | tf_op jit(solution)/shard_map/pallas_call | solution.py:488
  36.0 1.3 %collective-permute-start.4 = (bf16[2,128,128]{2,1,0:T(8,128)(2,1)}, bf16[2,128,128]{2,1,0:T(8,128)(2,1)S(1)}, u32[]{:S(2)}, u32[]{:S(2)}) collective-permute-start(bf16[2,128,128]{2,1,0:T(8,128)(2,1)} %get-tuple-element.45), channel_id=1, source_target_pairs={{0,16},{1,17},{2,18},{3,19},{4,20},{5,21},{6,22},{7,23},{8,24},{9,... | collective-permute-start | bytes 196616 | tf_op jit(solution)/shard_map/ppermute | solution.py:395
  39.1 1.6 %collective-permute-start.5 = (bf16[512,256]{1,0:T(8,128)(2,1)S(1)}, bf16[512,256]{1,0:T(8,128)(2,1)S(1)}, u32[]{:S(2)}, u32[]{:S(2)}) collective-permute-start(bf16[512,256]{1,0:T(8,128)(2,1)S(1)} %shard_map.105), channel_id=1, source_target_pairs={{0,1},{1,2},{2,3},{3,0},{4,5},{5,6},{6,7},{7,4},{8,9},{9,10},{10,1... | collective-permute-start | bytes 786440 | tf_op jit(solution)/shard_map/ppermute | solution.py:587
  41.5 2.2 %collective-permute-start.11 = (bf16[2,128,128]{2,1,0:T(8,128)(2,1)S(1)}, bf16[2,128,128]{2,1,0:T(8,128)(2,1)S(1)}, u32[]{:S(2)}, u32[]{:S(2)}) collective-permute-start(bf16[2,128,128]{2,1,0:T(8,128)(2,1)S(1)} %get-tuple-element.53), channel_id=1, source_target_pairs={{0,16},{1,17},{2,18},{3,19},{4,20},{5,21},{6,22},{7,23},{8,24},{9,... | collective-permute-start | bytes 196616 | tf_op jit(solution)/shard_map/ppermute | solution.py:395
  43.7 1.6 %fusion.10 = f32[512,1024]{1,0:T(8,128)S(1)} fusion(bf16[512,256]{1,0:T(8,128)(2,1)S(1)} %shard_map.105, bf16[2048,1024]{1,0:T(8,128)(2,1)} %weights_ref.1, s32[]{:T(128)S(6)} %select_n.21), kind=kOutput, calls=%fused_computation.16 | convolution fusion | flops 268435456 | bytes 2883588 | tf_op jit(solution)/shard_map/dot_general | solution.py:593
  46.1 1.6 %collective-permute-start.12 = (bf16[512,256]{1,0:T(8,128)(2,1)S(1)}, bf16[512,256]{1,0:T(8,128)(2,1)S(1)}, u32[]{:S(2)}, u32[]{:S(2)}) collective-permute-start(bf16[512,256]{1,0:T(8,128)(2,1)S(1)} %shard_map.107), channel_id=1, source_target_pairs={{0,1},{1,2},{2,3},{3,0},{4,5},{5,6},{6,7},{7,4},{8,9},{9,10},{10,1... | collective-permute-start | bytes 786440 | tf_op jit(solution)/shard_map/ppermute | solution.py:587
  48.1 1.4 %collective-permute-done.5 = bf16[512,256]{1,0:T(8,128)(2,1)S(1)} collective-permute-done((bf16[512,256]{1,0:T(8,128)(2,1)S(1)}, bf16[512,256]{1,0:T(8,128)(2,1)S(1)}, u32[]{:S(2)}, u32[]{:S(2)}) %collective-permute-start.5) | collective-permute-done | bytes 262176 | tf_op jit(solution)/shard_map/ppermute | solution.py:587
  50.2 6.9 %collective-permute-done.12 = bf16[512,256]{1,0:T(8,128)(2,1)S(1)} collective-permute-done((bf16[512,256]{1,0:T(8,128)(2,1)S(1)}, bf16[512,256]{1,0:T(8,128)(2,1)S(1)}, u32[]{:S(2)}, u32[]{:S(2)}) %collective-permute-start.12) | collective-permute-done | bytes 262176 | tf_op jit(solution)/shard_map/ppermute | solution.py:587
  57.6 5.2 %collective-permute-done.6 = bf16[512,256]{1,0:T(8,128)(2,1)S(1)} collective-permute-done((bf16[512,256]{1,0:T(8,128)(2,1)S(1)}, bf16[512,256]{1,0:T(8,128)(2,1)S(1)}, u32[]{:S(2)}, u32[]{:S(2)}) %collective-permute-start.6) | collective-permute-done | bytes 262176 | tf_op jit(solution)/shard_map/ppermute | solution.py:587
  63.2 5.2 %collective-permute-done.13 = bf16[512,256]{1,0:T(8,128)(2,1)S(1)} collective-permute-done((bf16[512,256]{1,0:T(8,128)(2,1)S(1)}, bf16[512,256]{1,0:T(8,128)(2,1)S(1)}, u32[]{:S(2)}, u32[]{:S(2)}) %collective-permute-start.13) | collective-permute-done | bytes 262176 | tf_op jit(solution)/shard_map/ppermute | solution.py:587
  68.9 5.1 %collective-permute-done.7 = bf16[512,256]{1,0:T(8,128)(2,1)S(1)} collective-permute-done((bf16[512,256]{1,0:T(8,128)(2,1)S(1)}, bf16[512,256]{1,0:T(8,128)(2,1)S(1)}, u32[]{:S(2)}, u32[]{:S(2)}) %collective-permute-start.7) | collective-permute-done | bytes 262176 | tf_op jit(solution)/shard_map/ppermute | solution.py:587
  74.5 3.5 %collective-permute-done.14.block_ref = bf16[512,256]{1,0:T(8,128)(2,1)S(1)} collective-permute-done((bf16[512,256]{1,0:T(8,128)(2,1)S(1)}, bf16[512,256]{1,0:T(8,128)(2,1)S(1)}, u32[]{:S(2)}, u32[]{:S(2)}) %collective-permute-start.14) | collective-permute-done | bytes 262176 | tf_op jit(solution)/shard_map/ppermute | solution.py:587
  78.0 1.3 %shard_map.108 = bf16[512,1024]{1,0:T(8,128)(2,1)} custom-call(s32[1]{0:T(128)} %bitcast.section, f32[512,1024]{1,0:T(8,128)S(1)} %add_add_fusion.1.first_ref, f32[512,1024]{1,0:T(8,128)S(1)} %add_add_fusion.second_ref, bf16[512,256]{1,0:T(8,128)(2,1)S(1)} %collective-permute-done.14.block_ref, bf16[2048,1024]{1,0:T(8,128)(2,1)S(1)} %copy-done), custom_call_target="tpu_custom_call" | custom-call | tf_op jit(solution)/shard_map/pallas_call | solution.py:512
  (59 shorter events, 13.1 us)
Async XLA Ops:
  0.0 6.3 %copy-start.16 = (bf16[512,4,128]{2,1,0:T(4,128)(2,1)S(1)}, bf16[512,4,128]{2,1,0:T(4,128)(2,1)}, u32[]{:S(2)}) copy-start(bf16[512,4,128]{2,1,0:T(4,128)(2,1)} %refs_2_.1) | copy-start | bytes 1572868
  0.0 7.5 %copy-start.3 = (f32[3,4,4,128]{3,2,1,0:T(4,128)S(1)}, f32[3,4,4,128]{3,2,1,0:T(4,128)}, u32[]{:S(2)}) copy-start(f32[3,4,4,128]{3,2,1,0:T(4,128)} %taps_ref.5) | copy-start | bytes 73732
  1.4 7.9 %collective-permute-start = (bf16[24,4,128]{2,1,0:T(4,128)(2,1)}, bf16[24,4,128]{2,1,0:T(4,128)(2,1)S(1)}, u32[]{:S(2)}, u32[]{:S(2)}) collective-permute-start(bf16[24,4,128]{2,1,0:T(4,128)(2,1)} %shard_map.101), channel_id=1, source_target_pairs={{0,4},{4,8},{8,12},{12,16},{16,20},{20,24},{24,28},{1,5},{5,9},{9,... | collective-permute-start | bytes 73736 | tf_op jit(solution)/shard_map/ppermute | solution.py:395
  7.5 1.8 %copy-start.4 = (f32[4,512]{1,0:T(4,128)S(1)}, f32[4,512]{1,0:T(4,128)}, u32[]{:S(2)}) copy-start(f32[4,512]{1,0:T(4,128)} %decay_ref.3) | copy-start | bytes 24580
  9.4 15.2 %copy-start.14 = (bf16[512,4,128]{2,1,0:T(4,128)(2,1)S(1)}, bf16[512,4,128]{2,1,0:T(4,128)(2,1)}, u32[]{:S(2)}) copy-start(bf16[512,4,128]{2,1,0:T(4,128)(2,1)} %param.13) | copy-start | bytes 1572868
  9.4 15.3 %copy-start.15 = (bf16[512,4,128]{2,1,0:T(4,128)(2,1)S(1)}, bf16[512,4,128]{2,1,0:T(4,128)(2,1)}, u32[]{:S(2)}) copy-start(bf16[512,4,128]{2,1,0:T(4,128)(2,1)} %refs_0_.1) | copy-start | bytes 1572868
  17.7 9.0 %copy-start.7 = (f32[128]{0:T(128)S(1)}, f32[128]{0:T(128)}, u32[]{:S(2)}) copy-start(f32[128]{0:T(128)} %param.18) | copy-start | bytes 1540
  17.7 7.0 %collective-permute-start.1 = (bf16[2,128,256]{2,1,0:T(8,128)(2,1)S(1)}, bf16[2,128,256]{2,1,0:T(8,128)(2,1)S(1)}, u32[]{:S(2)}, u32[]{:S(2)}) collective-permute-start(bf16[2,128,256]{2,1,0:T(8,128)(2,1)S(1)} %get-tuple-element.41.refs_0_), channel_id=1, source_target_pairs={{0,4},{4,0},{8,12},{12,8},{1,5},{5,1},{9,13},{13,9},{2,6},{6,2},{1... | collective-permute-start | bytes 393224 | tf_op jit(solution)/shard_map/ppermute | solution.py:555
  19.2 7.5 %copy-start.9 = (f32[4,512,256]{2,1,0:T(8,128)S(1)}, f32[4,512,256]{2,1,0:T(8,128)}, u32[]{:S(2)}) copy-start(f32[4,512,256]{2,1,0:T(8,128)} %copy-done.8) | copy-start | bytes 6291460
  19.2 15.3 %collective-permute-start.2 = (bf16[2,128,256]{2,1,0:T(8,128)(2,1)S(1)}, bf16[2,128,256]{2,1,0:T(8,128)(2,1)S(1)}, u32[]{:S(2)}, u32[]{:S(2)}) collective-permute-start(bf16[2,128,256]{2,1,0:T(8,128)(2,1)S(1)} %get-tuple-element.41.refs_0_), channel_id=1, source_target_pairs={{0,8},{4,12},{8,0},{12,4},{1,9},{5,13},{9,1},{13,5},{2,10},{6,14},... | collective-permute-start | bytes 393224 | tf_op jit(solution)/shard_map/ppermute | solution.py:555
  20.2 14.4 %collective-permute-start.3 = (bf16[2,128,256]{2,1,0:T(8,128)(2,1)S(1)}, bf16[2,128,256]{2,1,0:T(8,128)(2,1)S(1)}, u32[]{:S(2)}, u32[]{:S(2)}) collective-permute-start(bf16[2,128,256]{2,1,0:T(8,128)(2,1)S(1)} %get-tuple-element.41.refs_0_), channel_id=1, source_target_pairs={{0,12},{4,8},{8,4},{12,0},{1,13},{5,9},{9,5},{13,1},{2,14},{6,10},... | collective-permute-start | bytes 393224 | tf_op jit(solution)/shard_map/ppermute | solution.py:555
  21.2 19.5 %collective-permute-start.10 = (bf16[2,128,256]{2,1,0:T(8,128)(2,1)S(1)}, bf16[2,128,256]{2,1,0:T(8,128)(2,1)S(1)}, u32[]{:S(2)}, u32[]{:S(2)}) collective-permute-start(bf16[2,128,256]{2,1,0:T(8,128)(2,1)S(1)} %get-tuple-element.49.refs_0_), channel_id=1, source_target_pairs={{0,12},{4,8},{8,4},{12,0},{1,13},{5,9},{9,5},{13,1},{2,14},{6,10},... | collective-permute-start | bytes 393224 | tf_op jit(solution)/shard_map/ppermute | solution.py:555
  23.1 17.6 %collective-permute-start.8 = (bf16[2,128,256]{2,1,0:T(8,128)(2,1)S(1)}, bf16[2,128,256]{2,1,0:T(8,128)(2,1)S(1)}, u32[]{:S(2)}, u32[]{:S(2)}) collective-permute-start(bf16[2,128,256]{2,1,0:T(8,128)(2,1)S(1)} %get-tuple-element.49.refs_0_), channel_id=1, source_target_pairs={{0,4},{4,0},{8,12},{12,8},{1,5},{5,1},{9,13},{13,9},{2,6},{6,2},{1... | collective-permute-start | bytes 393224 | tf_op jit(solution)/shard_map/ppermute | solution.py:555
  25.4 15.4 %collective-permute-start.9 = (bf16[2,128,256]{2,1,0:T(8,128)(2,1)S(1)}, bf16[2,128,256]{2,1,0:T(8,128)(2,1)S(1)}, u32[]{:S(2)}, u32[]{:S(2)}) collective-permute-start(bf16[2,128,256]{2,1,0:T(8,128)(2,1)S(1)} %get-tuple-element.49.refs_0_), channel_id=1, source_target_pairs={{0,8},{4,12},{8,0},{12,4},{1,9},{5,13},{9,1},{13,5},{2,10},{6,14},... | collective-permute-start | bytes 393224 | tf_op jit(solution)/shard_map/ppermute | solution.py:555
  29.2 5.5 %copy-start.2 = (bf16[2,128,256]{2,1,0:T(8,128)(2,1)S(1)}, bf16[2,128,256]{2,1,0:T(8,128)(2,1)}, u32[]{:S(2)}) copy-start(bf16[2,128,256]{2,1,0:T(8,128)(2,1)} %copy-done.1) | copy-start | bytes 393220
  36.0 2.4 %collective-permute-start.4 = (bf16[2,128,128]{2,1,0:T(8,128)(2,1)}, bf16[2,128,128]{2,1,0:T(8,128)(2,1)S(1)}, u32[]{:S(2)}, u32[]{:S(2)}) collective-permute-start(bf16[2,128,128]{2,1,0:T(8,128)(2,1)} %get-tuple-element.45), channel_id=1, source_target_pairs={{0,16},{1,17},{2,18},{3,19},{4,20},{5,21},{6,22},{7,23},{8,24},{9,... | collective-permute-start | bytes 196616 | tf_op jit(solution)/shard_map/ppermute | solution.py:395
  39.1 10.5 %collective-permute-start.5 = (bf16[512,256]{1,0:T(8,128)(2,1)S(1)}, bf16[512,256]{1,0:T(8,128)(2,1)S(1)}, u32[]{:S(2)}, u32[]{:S(2)}) collective-permute-start(bf16[512,256]{1,0:T(8,128)(2,1)S(1)} %shard_map.105), channel_id=1, source_target_pairs={{0,1},{1,2},{2,3},{3,0},{4,5},{5,6},{6,7},{7,4},{8,9},{9,10},{10,1... | collective-permute-start | bytes 786440 | tf_op jit(solution)/shard_map/ppermute | solution.py:587
  41.5 3.8 %collective-permute-start.11 = (bf16[2,128,128]{2,1,0:T(8,128)(2,1)S(1)}, bf16[2,128,128]{2,1,0:T(8,128)(2,1)S(1)}, u32[]{:S(2)}, u32[]{:S(2)}) collective-permute-start(bf16[2,128,128]{2,1,0:T(8,128)(2,1)S(1)} %get-tuple-element.53), channel_id=1, source_target_pairs={{0,16},{1,17},{2,18},{3,19},{4,20},{5,21},{6,22},{7,23},{8,24},{9,... | collective-permute-start | bytes 196616 | tf_op jit(solution)/shard_map/ppermute | solution.py:395
  43.7 4.0 %copy-start = (bf16[2048,1024]{1,0:T(8,128)(2,1)S(1)}, bf16[2048,1024]{1,0:T(8,128)(2,1)}, u32[]{:S(2)}) copy-start(bf16[2048,1024]{1,0:T(8,128)(2,1)} %weights_ref.1) | copy-start | bytes 12582916
  46.1 11.1 %collective-permute-start.12 = (bf16[512,256]{1,0:T(8,128)(2,1)S(1)}, bf16[512,256]{1,0:T(8,128)(2,1)S(1)}, u32[]{:S(2)}, u32[]{:S(2)}) collective-permute-start(bf16[512,256]{1,0:T(8,128)(2,1)S(1)} %shard_map.107), channel_id=1, source_target_pairs={{0,1},{1,2},{2,3},{3,0},{4,5},{5,6},{6,7},{7,4},{8,9},{9,10},{10,1... | collective-permute-start | bytes 786440 | tf_op jit(solution)/shard_map/ppermute | solution.py:587
  49.6 13.2 %collective-permute-start.6 = (bf16[512,256]{1,0:T(8,128)(2,1)S(1)}, bf16[512,256]{1,0:T(8,128)(2,1)S(1)}, u32[]{:S(2)}, u32[]{:S(2)}) collective-permute-start(bf16[512,256]{1,0:T(8,128)(2,1)S(1)} %collective-permute-done.5), channel_id=1, source_target_pairs={{0,1},{1,2},{2,3},{3,0},{4,5},{5,6},{6,7},{7,4},{8,9},{9,10},{10,1... | collective-permute-start | bytes 786440 | tf_op jit(solution)/shard_map/ppermute | solution.py:587
  57.2 11.2 %collective-permute-start.13 = (bf16[512,256]{1,0:T(8,128)(2,1)S(1)}, bf16[512,256]{1,0:T(8,128)(2,1)S(1)}, u32[]{:S(2)}, u32[]{:S(2)}) collective-permute-start(bf16[512,256]{1,0:T(8,128)(2,1)S(1)} %collective-permute-done.12), channel_id=1, source_target_pairs={{0,1},{1,2},{2,3},{3,0},{4,5},{5,6},{6,7},{7,4},{8,9},{9,10},{10,1... | collective-permute-start | bytes 786440 | tf_op jit(solution)/shard_map/ppermute | solution.py:587
  62.8 11.2 %collective-permute-start.7 = (bf16[512,256]{1,0:T(8,128)(2,1)S(1)}, bf16[512,256]{1,0:T(8,128)(2,1)S(1)}, u32[]{:S(2)}, u32[]{:S(2)}) collective-permute-start(bf16[512,256]{1,0:T(8,128)(2,1)S(1)} %collective-permute-done.6), channel_id=1, source_target_pairs={{0,1},{1,2},{2,3},{3,0},{4,5},{5,6},{6,7},{7,4},{8,9},{9,10},{10,1... | collective-permute-start | bytes 786440 | tf_op jit(solution)/shard_map/ppermute | solution.py:587
  68.4 9.6 %collective-permute-start.14 = (bf16[512,256]{1,0:T(8,128)(2,1)S(1)}, bf16[512,256]{1,0:T(8,128)(2,1)S(1)}, u32[]{:S(2)}, u32[]{:S(2)}) collective-permute-start(bf16[512,256]{1,0:T(8,128)(2,1)S(1)} %collective-permute-done.13), channel_id=1, source_target_pairs={{0,1},{1,2},{2,3},{3,0},{4,5},{5,6},{6,7},{7,4},{8,9},{9,10},{10,1... | collective-permute-start | bytes 786440 | tf_op jit(solution)/shard_map/ppermute | solution.py:587
  (8 other events, 10.0 us)

commit v10 on v9

--- a/solution.py
+++ b/solution.py
@@ -553,13 +553,22 @@
     )
     exchanged = [
         [own_map] + [lax.ppermute(own_map, "leaf", pairs_at(k, leaves)) for k in range(1, leaves)]
-        for own_map in own_maps
+        for own_map in own_maps[:-1]
     ]
     query_in, gate_in = after(own_maps[-1], query_in, gate_in)
     query, gate = (jnp.transpose(x, (1, 0, 2)) for x in (query_in, gate_in))
     reads = reads_of(
         0, heads, doc_resets, query, gate, gain, rims, taps, log_decay, write_strength,
         (unit_key, solved, starts),
+    )
+    own_map = own_maps[-1]
+    later = after(reads[0], own_map)[0]
+    exchanged.append(
+        [own_map]
+        + [
+            lax.ppermute(later if 2 * k == leaves else own_map, "leaf", pairs_at(k, leaves))
+            for k in range(1, leaves)
+        ]
     )
     size = heads // GROUPS
     blocks = []

time: 79.7 us -> 76.9 us (0.965)
  local copies, waits for them, and re-layouts: 7.73 us -> 6.02 us
  starting transfers between devices: 19.9 us -> 18.9 us
    ppermute x6 -> x3, starting transfers between devices: 8.14 us -> 3.55 us  [on_device(): lax.ppermute(own_map, 'leaf', pairs_at(k, leaves))]
    ppermute x0 -> x3, starting transfers between devices: none -> 3.55 us  [on_device(): lax.ppermute(later if 2 * k == leaves else own_map, 'leaf', pairs_at(k, l...]
    unnamed x34 -> x30, local copies, waits for them, and re-layouts: 6.41 us -> 4.7 us
where the time goes in v10:
time: 76.9 us; the launch traced here: 76.7 us
  waiting for transfers between devices  28.4 us (37%)
  starting transfers between devices  18.9 us (25%)
  Pallas kernels  18.6 us (24%)
  local copies, waits for them, and re-layouts  6.02 us (8%)
  matrix products  4.34 us (6%)
    ppermute x6, waiting for transfers between devices, on_device(): lax.ppermute(x, 'head', around)  27.3 us
    ppermute x3, starting transfers between devices, from_behind(): lax.ppermute(value, axis, [(i, i + steps) for i in range(count - steps)])  8.28 us
    pallas_call x1, Pallas kernels, reads_of(): pl.pallas_call(functools.partial(reads_kernel, base), out_shape=(jax.Shap...  5.44 us
    pallas_call x1, Pallas kernels, maps_of(): pl.pallas_call(functools.partial(maps_kernel, base), out_shape=(jax.Shape...  5.07 us
    unnamed x30, local copies, waits for them, and re-layouts  4.7 us
    dot_general x7, matrix products, on_device(): term = jnp.dot(block, rows, preferred_element_type=F32)  4.34 us
    ppermute x3, starting transfers between devices, on_device(): lax.ppermute(later if 2 * k == leaves else own_map, 'leaf', pairs_at(k, l...  3.55 us
    ppermute x3, starting transfers between devices, on_device(): lax.ppermute(own_map, 'leaf', pairs_at(k, leaves))  3.55 us
  transfers between devices with their start and end apart: 15, of which 7 were waited for; matrix products, arithmetic and copies ran while one was open for 7% of the time, Pallas kernels for 14%

profile of v10, /device:TPU:0, one launch (start us, length us, event | category | flops | bytes accessed | tf_op | source)
XLA Modules:
  0.0 76.7 jit_solution(9964438012607484890)
XLA Ops:
  0.0 1.4 %shard_map.101 = bf16[24,4,128]{2,1,0:T(4,128)(2,1)} custom-call(bf16[512,4,128]{2,1,0:T(4,128)(2,1)} %refs_0_.1, bf16[512,4,128]{2,1,0:T(4,128)(2,1)} %refs_1_.1, bf16[512,4,128]{2,1,0:T(4,128)(2,1)} %refs_2_.1), custom_call_target="tpu_custom_call" | custom-call | flops 1000000000 | bytes 65536 | tf_op jit(solution)/shard_map/pallas_call | solution.py:406
  1.4 4.8 %collective-permute-start = (bf16[24,4,128]{2,1,0:T(4,128)(2,1)}, bf16[24,4,128]{2,1,0:T(4,128)(2,1)S(1)}, u32[]{:S(2)}, u32[]{:S(2)}) collective-permute-start(bf16[24,4,128]{2,1,0:T(4,128)(2,1)} %shard_map.101), channel_id=1, source_target_pairs={{0,4},{4,8},{8,12},{12,16},{16,20},{20,24},{24,28},{1,5},{5,9},{9,... | collective-permute-start | bytes 73736 | tf_op jit(solution)/shard_map/ppermute | solution.py:395
  6.3 1.2 %copy_bitcast_fusion.2 = (bf16[4,512,128]{2,1,0:T(8,128)(2,1)S(1)}, bf16[4,512,128]{2,1,0:T(8,128)(2,1)S(1)}) fusion(bf16[512,4,128]{2,1,0:T(4,128)(2,1)S(1)} %copy-done.14, bf16[512,4,128]{2,1,0:T(4,128)(2,1)} %refs_1_.1), kind=kLoop, calls=%fused_computation.4 | loop fusion | bytes 2097152 | tf_op jit(solution)/shard_map/transpose | solution.py:544
  7.5 1.8 %shard_map.100 = (bf16[4,512,128]{2,1,0:T(8,128)(2,1)S(1)}, bf16[4,512,128]{2,1,0:T(8,128)(2,1)S(1)}, f32[2,4,16,128]{3,2,1,0:T(8,128)S(1)}) custom-call(bf16[4,512,128]{2,1,0:T(8,128)(2,1)S(1)} %get-tuple-element.58.key_ref, bf16[4,512,128]{2,1,0:T(8,128)(2,1)S(1)} %get-tuple-element.57.value_ref, f32[3,4,4,128]{3,2,1,0:T(4,128)S(1)} %copy-done.7), custom_call_target="tpu_custom_call" | custom-call | flops 3000000000 | bytes 4194304 | tf_op jit(solution)/shard_map/pallas_call | solution.py:420
  9.4 5.1 %shard_map.102 = (bf16[4,512,128]{2,1,0:T(8,128)(2,1)S(1)}, f32[4,512,256]{2,1,0:T(8,128)S(1)}, f32[4,3,128,256]{3,2,1,0:T(8,128)S(1)}, bf16[2,128,256]{2,1,0:T(8,128)(2,1)S(1)}, bf16[2,128,256]{2,1,0:T(8,128)(2,1)S(1)}) custom-call(s32[8]{0:T(128)S(1)} %copy-done.10, bf16[4,512,128]{2,1,0:T(8,128)(2,1)S(1)} %get-tuple-element.31.unit_in_ref, ...), custom_call_target="tpu_custom_call" | custom-call | flops 5000000000 | bytes 4194304 | tf_op jit(solution)/shard_map/pallas_call | solution.py:436
  14.5 1.6 %collective-permute-start.1 = (bf16[2,128,256]{2,1,0:T(8,128)(2,1)S(1)}, bf16[2,128,256]{2,1,0:T(8,128)(2,1)S(1)}, u32[]{:S(2)}, u32[]{:S(2)}) collective-permute-start(bf16[2,128,256]{2,1,0:T(8,128)(2,1)S(1)} %get-tuple-element.42.refs_0_), channel_id=1, source_target_pairs={{0,4},{4,0},{8,12},{12,8},{1,5},{5,1},{9,13},{13,9},{2,6},{6,2},{1... | collective-permute-start | bytes 393224 | tf_op jit(solution)/shard_map/ppermute | solution.py:555
  17.0 1.0 %collective-permute-start.3 = (bf16[2,128,256]{2,1,0:T(8,128)(2,1)S(1)}, bf16[2,128,256]{2,1,0:T(8,128)(2,1)S(1)}, u32[]{:S(2)}, u32[]{:S(2)}) collective-permute-start(bf16[2,128,256]{2,1,0:T(8,128)(2,1)S(1)} %get-tuple-element.42.refs_0_), channel_id=1, source_target_pairs={{0,12},{4,8},{8,4},{12,0},{1,13},{5,9},{9,5},{13,1},{2,14},{6,10},... | collective-permute-start | bytes 393224 | tf_op jit(solution)/shard_map/ppermute | solution.py:555
  18.0 1.9 %collective-permute-start.10 = (bf16[2,128,256]{2,1,0:T(8,128)(2,1)S(1)}, bf16[2,128,256]{2,1,0:T(8,128)(2,1)S(1)}, u32[]{:S(2)}, u32[]{:S(2)}) collective-permute-start(bf16[2,128,256]{2,1,0:T(8,128)(2,1)S(1)} %get-tuple-element.51.refs_0_), channel_id=1, source_target_pairs={{0,12},{4,8},{8,4},{12,0},{1,13},{5,9},{9,5},{13,1},{2,14},{6,10},... | collective-permute-start | bytes 393224 | tf_op jit(solution)/shard_map/ppermute | solution.py:569
  20.1 5.4 %shard_map.103 = (bf16[4,512,128]{2,1,0:T(8,128)(2,1)S(1)}, f32[4,512,128]{2,1,0:T(8,128)S(1)}, f32[4,512,128]{2,1,0:T(8,128)S(1)}) custom-call(s32[8]{0:T(128)S(1)} %copy-done.10, bf16[4,512,128]{2,1,0:T(8,128)(2,1)S(1)} %bitcast.21, bf16[4,512,128]{2,1,0:T(8,128)(2,1)S(1)} %bitcast.20, f32[1,128]{1,0:T(1,128)S(1)} %bitcast.22, ...), custom_call_target="tpu_custom_call" | custom-call | flops 3000000000 | bytes 4194304 | tf_op jit(solution)/shard_map/pallas_call | solution.py:462
  25.6 1.1 %collective-permute-start.9 = (bf16[2,128,256]{2,1,0:T(8,128)(2,1)S(1)}, bf16[2,128,256]{2,1,0:T(8,128)(2,1)S(1)}, u32[]{:S(2)}, u32[]{:S(2)}) collective-permute-start(bf16[2,128,256]{2,1,0:T(8,128)(2,1)S(1)} %get-tuple-element.51.refs_0_), channel_id=1, source_target_pairs={{0,8},{4,12},{8,0},{12,4},{1,9},{5,13},{9,1},{13,5},{2,10},{6,14},... | collective-permute-start | bytes 393224 | tf_op jit(solution)/shard_map/ppermute | solution.py:569
  31.9 1.4 %shard_map.104 = (f32[2,128,256]{2,1,0:T(8,128)S(1)}, bf16[2,128,128]{2,1,0:T(8,128)(2,1)}) custom-call(s32[1]{0:T(128)} %bitcast.1.place, bf16[2,128,256]{2,1,0:T(8,128)(2,1)S(1)} %get-tuple-element.42.refs_0_, bf16[2,128,256]{2,1,0:T(8,128)(2,1)S(1)} %copy-done.2, bf16[2,128,256]{2,1,0:T(8,128)(2,1)S(1)} %copy-done.4, bf16[2,128,256]{2,1,0:T(8,128)(2,1)S(1)} %copy-done.6), custom_call_target="tpu_custom_call" | custom-call | tf_op jit(solution)/shard_map/pallas_call | solution.py:488
  33.2 1.3 %collective-permute-start.4 = (bf16[2,128,128]{2,1,0:T(8,128)(2,1)}, bf16[2,128,128]{2,1,0:T(8,128)(2,1)S(1)}, u32[]{:S(2)}, u32[]{:S(2)}) collective-permute-start(bf16[2,128,128]{2,1,0:T(8,128)(2,1)} %get-tuple-element.46), channel_id=1, source_target_pairs={{0,16},{1,17},{2,18},{3,19},{4,20},{5,21},{6,22},{7,23},{8,24},{9,... | collective-permute-start | bytes 196616 | tf_op jit(solution)/shard_map/ppermute | solution.py:395
  34.6 1.0 %collective-permute-done.4.arrived_ref = bf16[2,128,128]{2,1,0:T(8,128)(2,1)S(1)} collective-permute-done((bf16[2,128,128]{2,1,0:T(8,128)(2,1)}, bf16[2,128,128]{2,1,0:T(8,128)(2,1)S(1)}, u32[]{:S(2)}, u32[]{:S(2)}) %collective-permute-start.4) | collective-permute-done | bytes 65568 | tf_op jit(solution)/shard_map/ppermute | solution.py:395
  36.3 1.6 %collective-permute-start.5 = (bf16[512,256]{1,0:T(8,128)(2,1)S(1)}, bf16[512,256]{1,0:T(8,128)(2,1)S(1)}, u32[]{:S(2)}, u32[]{:S(2)}) collective-permute-start(bf16[512,256]{1,0:T(8,128)(2,1)S(1)} %shard_map.105), channel_id=1, source_target_pairs={{0,1},{1,2},{2,3},{3,0},{4,5},{5,6},{6,7},{7,4},{8,9},{9,10},{10,1... | collective-permute-start | bytes 786440 | tf_op jit(solution)/shard_map/ppermute | solution.py:596
  38.7 2.2 %collective-permute-start.11 = (bf16[2,128,128]{2,1,0:T(8,128)(2,1)S(1)}, bf16[2,128,128]{2,1,0:T(8,128)(2,1)S(1)}, u32[]{:S(2)}, u32[]{:S(2)}) collective-permute-start(bf16[2,128,128]{2,1,0:T(8,128)(2,1)S(1)} %get-tuple-element.55), channel_id=1, source_target_pairs={{0,16},{1,17},{2,18},{3,19},{4,20},{5,21},{6,22},{7,23},{8,24},{9,... | collective-permute-start | bytes 196616 | tf_op jit(solution)/shard_map/ppermute | solution.py:395
  40.9 1.6 %fusion.10 = f32[512,1024]{1,0:T(8,128)S(1)} fusion(bf16[512,256]{1,0:T(8,128)(2,1)S(1)} %shard_map.105, bf16[2048,1024]{1,0:T(8,128)(2,1)} %weights_ref.1, s32[]{:T(128)S(6)} %select_n.21), kind=kOutput, calls=%fused_computation.16 | convolution fusion | flops 268435456 | bytes 2883588 | tf_op jit(solution)/shard_map/dot_general | solution.py:602
  43.3 1.6 %collective-permute-start.12 = (bf16[512,256]{1,0:T(8,128)(2,1)S(1)}, bf16[512,256]{1,0:T(8,128)(2,1)S(1)}, u32[]{:S(2)}, u32[]{:S(2)}) collective-permute-start(bf16[512,256]{1,0:T(8,128)(2,1)S(1)} %shard_map.107), channel_id=1, source_target_pairs={{0,1},{1,2},{2,3},{3,0},{4,5},{5,6},{6,7},{7,4},{8,9},{9,10},{10,1... | collective-permute-start | bytes 786440 | tf_op jit(solution)/shard_map/ppermute | solution.py:596
  45.4 1.4 %collective-permute-done.5 = bf16[512,256]{1,0:T(8,128)(2,1)S(1)} collective-permute-done((bf16[512,256]{1,0:T(8,128)(2,1)S(1)}, bf16[512,256]{1,0:T(8,128)(2,1)S(1)}, u32[]{:S(2)}, u32[]{:S(2)}) %collective-permute-start.5) | collective-permute-done | bytes 262176 | tf_op jit(solution)/shard_map/ppermute | solution.py:596
  47.5 6.9 %collective-permute-done.12 = bf16[512,256]{1,0:T(8,128)(2,1)S(1)} collective-permute-done((bf16[512,256]{1,0:T(8,128)(2,1)S(1)}, bf16[512,256]{1,0:T(8,128)(2,1)S(1)}, u32[]{:S(2)}, u32[]{:S(2)}) %collective-permute-start.12) | collective-permute-done | bytes 262176 | tf_op jit(solution)/shard_map/ppermute | solution.py:596
  54.8 5.2 %collective-permute-done.6 = bf16[512,256]{1,0:T(8,128)(2,1)S(1)} collective-permute-done((bf16[512,256]{1,0:T(8,128)(2,1)S(1)}, bf16[512,256]{1,0:T(8,128)(2,1)S(1)}, u32[]{:S(2)}, u32[]{:S(2)}) %collective-permute-start.6) | collective-permute-done | bytes 262176 | tf_op jit(solution)/shard_map/ppermute | solution.py:596
  60.5 5.2 %collective-permute-done.13 = bf16[512,256]{1,0:T(8,128)(2,1)S(1)} collective-permute-done((bf16[512,256]{1,0:T(8,128)(2,1)S(1)}, bf16[512,256]{1,0:T(8,128)(2,1)S(1)}, u32[]{:S(2)}, u32[]{:S(2)}) %collective-permute-start.13) | collective-permute-done | bytes 262176 | tf_op jit(solution)/shard_map/ppermute | solution.py:596
  66.1 5.1 %collective-permute-done.7 = bf16[512,256]{1,0:T(8,128)(2,1)S(1)} collective-permute-done((bf16[512,256]{1,0:T(8,128)(2,1)S(1)}, bf16[512,256]{1,0:T(8,128)(2,1)S(1)}, u32[]{:S(2)}, u32[]{:S(2)}) %collective-permute-start.7) | collective-permute-done | bytes 262176 | tf_op jit(solution)/shard_map/ppermute | solution.py:596
  71.7 3.5 %collective-permute-done.14.block_ref = bf16[512,256]{1,0:T(8,128)(2,1)S(1)} collective-permute-done((bf16[512,256]{1,0:T(8,128)(2,1)S(1)}, bf16[512,256]{1,0:T(8,128)(2,1)S(1)}, u32[]{:S(2)}, u32[]{:S(2)}) %collective-permute-start.14) | collective-permute-done | bytes 262176 | tf_op jit(solution)/shard_map/ppermute | solution.py:596
  75.2 1.3 %shard_map.108 = bf16[512,1024]{1,0:T(8,128)(2,1)} custom-call(s32[1]{0:T(128)} %bitcast.section, f32[512,1024]{1,0:T(8,128)S(1)} %add_add_fusion.1.first_ref, f32[512,1024]{1,0:T(8,128)S(1)} %add_add_fusion.second_ref, bf16[512,256]{1,0:T(8,128)(2,1)S(1)} %collective-permute-done.14.block_ref, bf16[2048,1024]{1,0:T(8,128)(2,1)S(1)} %copy-done), custom_call_target="tpu_custom_call" | custom-call | tf_op jit(solution)/shard_map/pallas_call | solution.py:512
  (55 shorter events, 11.5 us)
Async XLA Ops:
  0.0 6.3 %copy-start.14 = (bf16[512,4,128]{2,1,0:T(4,128)(2,1)S(1)}, bf16[512,4,128]{2,1,0:T(4,128)(2,1)}, u32[]{:S(2)}) copy-start(bf16[512,4,128]{2,1,0:T(4,128)(2,1)} %refs_2_.1) | copy-start | bytes 1572868
  0.0 7.5 %copy-start.7 = (f32[3,4,4,128]{3,2,1,0:T(4,128)S(1)}, f32[3,4,4,128]{3,2,1,0:T(4,128)}, u32[]{:S(2)}) copy-start(f32[3,4,4,128]{3,2,1,0:T(4,128)} %taps_ref.5) | copy-start | bytes 73732
  1.4 7.9 %collective-permute-start = (bf16[24,4,128]{2,1,0:T(4,128)(2,1)}, bf16[24,4,128]{2,1,0:T(4,128)(2,1)S(1)}, u32[]{:S(2)}, u32[]{:S(2)}) collective-permute-start(bf16[24,4,128]{2,1,0:T(4,128)(2,1)} %shard_map.101), channel_id=1, source_target_pairs={{0,4},{4,8},{8,12},{12,16},{16,20},{20,24},{24,28},{1,5},{5,9},{9,... | collective-permute-start | bytes 73736 | tf_op jit(solution)/shard_map/ppermute | solution.py:395
  7.5 1.8 %copy-start.8 = (f32[4,512]{1,0:T(4,128)S(1)}, f32[4,512]{1,0:T(4,128)}, u32[]{:S(2)}) copy-start(f32[4,512]{1,0:T(4,128)} %decay_ref.3) | copy-start | bytes 24580
  7.5 1.8 %copy-start.9 = (f32[4,512]{1,0:T(4,128)S(1)}, f32[4,512]{1,0:T(4,128)}, u32[]{:S(2)}) copy-start(f32[4,512]{1,0:T(4,128)} %strength_ref.3) | copy-start | bytes 24580
  7.5 1.8 %copy-start.10 = (s32[8]{0:T(128)S(1)}, s32[8]{0:T(128)}, u32[]{:S(2)}) copy-start(s32[8]{0:T(128)} %resets.3) | copy-start | bytes 100
  9.4 10.6 %copy-start.12 = (bf16[512,4,128]{2,1,0:T(4,128)(2,1)S(1)}, bf16[512,4,128]{2,1,0:T(4,128)(2,1)}, u32[]{:S(2)}) copy-start(bf16[512,4,128]{2,1,0:T(4,128)(2,1)} %param.13) | copy-start | bytes 1572868
  9.4 10.6 %copy-start.13 = (bf16[512,4,128]{2,1,0:T(4,128)(2,1)S(1)}, bf16[512,4,128]{2,1,0:T(4,128)(2,1)}, u32[]{:S(2)}) copy-start(bf16[512,4,128]{2,1,0:T(4,128)(2,1)} %refs_0_.1) | copy-start | bytes 1572868
  14.5 5.6 %copy-start.11 = (f32[128]{0:T(128)S(1)}, f32[128]{0:T(128)}, u32[]{:S(2)}) copy-start(f32[128]{0:T(128)} %param.18) | copy-start | bytes 1540
  14.5 12.2 %collective-permute-start.1 = (bf16[2,128,256]{2,1,0:T(8,128)(2,1)S(1)}, bf16[2,128,256]{2,1,0:T(8,128)(2,1)S(1)}, u32[]{:S(2)}, u32[]{:S(2)}) collective-permute-start(bf16[2,128,256]{2,1,0:T(8,128)(2,1)S(1)} %get-tuple-element.42.refs_0_), channel_id=1, source_target_pairs={{0,4},{4,0},{8,12},{12,8},{1,5},{5,1},{9,13},{13,9},{2,6},{6,2},{1... | collective-permute-start | bytes 393224 | tf_op jit(solution)/shard_map/ppermute | solution.py:555
  16.0 11.8 %collective-permute-start.2 = (bf16[2,128,256]{2,1,0:T(8,128)(2,1)S(1)}, bf16[2,128,256]{2,1,0:T(8,128)(2,1)S(1)}, u32[]{:S(2)}, u32[]{:S(2)}) collective-permute-start(bf16[2,128,256]{2,1,0:T(8,128)(2,1)S(1)} %get-tuple-element.42.refs_0_), channel_id=1, source_target_pairs={{0,8},{4,12},{8,0},{12,4},{1,9},{5,13},{9,1},{13,5},{2,10},{6,14},... | collective-permute-start | bytes 393224 | tf_op jit(solution)/shard_map/ppermute | solution.py:555
  17.0 11.5 %collective-permute-start.3 = (bf16[2,128,256]{2,1,0:T(8,128)(2,1)S(1)}, bf16[2,128,256]{2,1,0:T(8,128)(2,1)S(1)}, u32[]{:S(2)}, u32[]{:S(2)}) collective-permute-start(bf16[2,128,256]{2,1,0:T(8,128)(2,1)S(1)} %get-tuple-element.42.refs_0_), channel_id=1, source_target_pairs={{0,12},{4,8},{8,4},{12,0},{1,13},{5,9},{9,5},{13,1},{2,14},{6,10},... | collective-permute-start | bytes 393224 | tf_op jit(solution)/shard_map/ppermute | solution.py:555
  18.0 20.0 %collective-permute-start.10 = (bf16[2,128,256]{2,1,0:T(8,128)(2,1)S(1)}, bf16[2,128,256]{2,1,0:T(8,128)(2,1)S(1)}, u32[]{:S(2)}, u32[]{:S(2)}) collective-permute-start(bf16[2,128,256]{2,1,0:T(8,128)(2,1)S(1)} %get-tuple-element.51.refs_0_), channel_id=1, source_target_pairs={{0,12},{4,8},{8,4},{12,0},{1,13},{5,9},{9,5},{13,1},{2,14},{6,10},... | collective-permute-start | bytes 393224 | tf_op jit(solution)/shard_map/ppermute | solution.py:569
  25.6 12.4 %collective-permute-start.9 = (bf16[2,128,256]{2,1,0:T(8,128)(2,1)S(1)}, bf16[2,128,256]{2,1,0:T(8,128)(2,1)S(1)}, u32[]{:S(2)}, u32[]{:S(2)}) collective-permute-start(bf16[2,128,256]{2,1,0:T(8,128)(2,1)S(1)} %get-tuple-element.51.refs_0_), channel_id=1, source_target_pairs={{0,8},{4,12},{8,0},{12,4},{1,9},{5,13},{9,1},{13,5},{2,10},{6,14},... | collective-permute-start | bytes 393224 | tf_op jit(solution)/shard_map/ppermute | solution.py:569
  27.3 10.7 %collective-permute-start.8 = (bf16[2,128,256]{2,1,0:T(8,128)(2,1)S(1)}, bf16[2,128,256]{2,1,0:T(8,128)(2,1)S(1)}, u32[]{:S(2)}, u32[]{:S(2)}) collective-permute-start(bf16[2,128,256]{2,1,0:T(8,128)(2,1)S(1)} %get-tuple-element.51.refs_0_), channel_id=1, source_target_pairs={{0,4},{4,0},{8,12},{12,8},{1,5},{5,1},{9,13},{13,9},{2,6},{6,2},{1... | collective-permute-start | bytes 393224 | tf_op jit(solution)/shard_map/ppermute | solution.py:569
  33.2 2.4 %collective-permute-start.4 = (bf16[2,128,128]{2,1,0:T(8,128)(2,1)}, bf16[2,128,128]{2,1,0:T(8,128)(2,1)S(1)}, u32[]{:S(2)}, u32[]{:S(2)}) collective-permute-start(bf16[2,128,128]{2,1,0:T(8,128)(2,1)} %get-tuple-element.46), channel_id=1, source_target_pairs={{0,16},{1,17},{2,18},{3,19},{4,20},{5,21},{6,22},{7,23},{8,24},{9,... | collective-permute-start | bytes 196616 | tf_op jit(solution)/shard_map/ppermute | solution.py:395
  36.3 10.5 %collective-permute-start.5 = (bf16[512,256]{1,0:T(8,128)(2,1)S(1)}, bf16[512,256]{1,0:T(8,128)(2,1)S(1)}, u32[]{:S(2)}, u32[]{:S(2)}) collective-permute-start(bf16[512,256]{1,0:T(8,128)(2,1)S(1)} %shard_map.105), channel_id=1, source_target_pairs={{0,1},{1,2},{2,3},{3,0},{4,5},{5,6},{6,7},{7,4},{8,9},{9,10},{10,1... | collective-permute-start | bytes 786440 | tf_op jit(solution)/shard_map/ppermute | solution.py:596
  38.7 3.8 %collective-permute-start.11 = (bf16[2,128,128]{2,1,0:T(8,128)(2,1)S(1)}, bf16[2,128,128]{2,1,0:T(8,128)(2,1)S(1)}, u32[]{:S(2)}, u32[]{:S(2)}) collective-permute-start(bf16[2,128,128]{2,1,0:T(8,128)(2,1)S(1)} %get-tuple-element.55), channel_id=1, source_target_pairs={{0,16},{1,17},{2,18},{3,19},{4,20},{5,21},{6,22},{7,23},{8,24},{9,... | collective-permute-start | bytes 196616 | tf_op jit(solution)/shard_map/ppermute | solution.py:395
  40.9 4.0 %copy-start = (bf16[2048,1024]{1,0:T(8,128)(2,1)S(1)}, bf16[2048,1024]{1,0:T(8,128)(2,1)}, u32[]{:S(2)}) copy-start(bf16[2048,1024]{1,0:T(8,128)(2,1)} %weights_ref.1) | copy-start | bytes 12582916
  43.3 11.1 %collective-permute-start.12 = (bf16[512,256]{1,0:T(8,128)(2,1)S(1)}, bf16[512,256]{1,0:T(8,128)(2,1)S(1)}, u32[]{:S(2)}, u32[]{:S(2)}) collective-permute-start(bf16[512,256]{1,0:T(8,128)(2,1)S(1)} %shard_map.107), channel_id=1, source_target_pairs={{0,1},{1,2},{2,3},{3,0},{4,5},{5,6},{6,7},{7,4},{8,9},{9,10},{10,1... | collective-permute-start | bytes 786440 | tf_op jit(solution)/shard_map/ppermute | solution.py:596
  46.8 13.2 %collective-permute-start.6 = (bf16[512,256]{1,0:T(8,128)(2,1)S(1)}, bf16[512,256]{1,0:T(8,128)(2,1)S(1)}, u32[]{:S(2)}, u32[]{:S(2)}) collective-permute-start(bf16[512,256]{1,0:T(8,128)(2,1)S(1)} %collective-permute-done.5), channel_id=1, source_target_pairs={{0,1},{1,2},{2,3},{3,0},{4,5},{5,6},{6,7},{7,4},{8,9},{9,10},{10,1... | collective-permute-start | bytes 786440 | tf_op jit(solution)/shard_map/ppermute | solution.py:596
  54.4 11.2 %collective-permute-start.13 = (bf16[512,256]{1,0:T(8,128)(2,1)S(1)}, bf16[512,256]{1,0:T(8,128)(2,1)S(1)}, u32[]{:S(2)}, u32[]{:S(2)}) collective-permute-start(bf16[512,256]{1,0:T(8,128)(2,1)S(1)} %collective-permute-done.12), channel_id=1, source_target_pairs={{0,1},{1,2},{2,3},{3,0},{4,5},{5,6},{6,7},{7,4},{8,9},{9,10},{10,1... | collective-permute-start | bytes 786440 | tf_op jit(solution)/shard_map/ppermute | solution.py:596
  60.0 11.2 %collective-permute-start.7 = (bf16[512,256]{1,0:T(8,128)(2,1)S(1)}, bf16[512,256]{1,0:T(8,128)(2,1)S(1)}, u32[]{:S(2)}, u32[]{:S(2)}) collective-permute-start(bf16[512,256]{1,0:T(8,128)(2,1)S(1)} %collective-permute-done.6), channel_id=1, source_target_pairs={{0,1},{1,2},{2,3},{3,0},{4,5},{5,6},{6,7},{7,4},{8,9},{9,10},{10,1... | collective-permute-start | bytes 786440 | tf_op jit(solution)/shard_map/ppermute | solution.py:596
  65.6 9.6 %collective-permute-start.14 = (bf16[512,256]{1,0:T(8,128)(2,1)S(1)}, bf16[512,256]{1,0:T(8,128)(2,1)S(1)}, u32[]{:S(2)}, u32[]{:S(2)}) collective-permute-start(bf16[512,256]{1,0:T(8,128)(2,1)S(1)} %collective-permute-done.13), channel_id=1, source_target_pairs={{0,1},{1,2},{2,3},{3,0},{4,5},{5,6},{6,7},{7,4},{8,9},{9,10},{10,1... | collective-permute-start | bytes 786440 | tf_op jit(solution)/shard_map/ppermute | solution.py:596
  (6 other events, 4.7 us)

commit v11 on v9

--- a/solution.py
+++ b/solution.py
@@ -395,10 +395,16 @@
     return lax.ppermute(value, axis, [(i, i + steps) for i in range(count - steps)])
 
 
+def exchange(own_map, leaves):
+    received = [lax.ppermute(own_map, "leaf", pairs_at(k, leaves)) for k in range(1, leaves)]
+    return [own_map] + received
+
+
 VMEM = pl.BlockSpec(memory_space=pltpu.VMEM)
 SMEM = pl.BlockSpec(memory_space=pltpu.SMEM)
 HBM = pl.BlockSpec(memory_space=pltpu.HBM)
-PARAMS = pltpu.CompilerParams(vmem_limit_bytes=12 * 1024 * 1024)
+PARAMS = pltpu.CompilerParams(vmem_limit_bytes=8 * 1024 * 1024)
+LAST_PARAMS = pltpu.CompilerParams(vmem_limit_bytes=12 * 1024 * 1024)
 
 
 def pack_rims(inputs):
@@ -518,7 +524,7 @@
             pltpu.VMEM((length, columns), BF16),
             pltpu.SemaphoreType.DMA((length // CHUNK,)),
         ],
-        compiler_params=PARAMS,
+        compiler_params=LAST_PARAMS,
     )(section.astype(jnp.int32).reshape(1), first, second, block, weights)
 
 
@@ -551,10 +557,6 @@
     unit_key, solved, starts, *own_maps = maps_of(
         0, heads, doc_resets, key, value, first, rims, taps, log_decay, write_strength
     )
-    exchanged = [
-        [own_map] + [lax.ppermute(own_map, "leaf", pairs_at(k, leaves)) for k in range(1, leaves)]
-        for own_map in own_maps
-    ]
     query_in, gate_in = after(own_maps[-1], query_in, gate_in)
     query, gate = (jnp.transpose(x, (1, 0, 2)) for x in (query_in, gate_in))
     reads = reads_of(
@@ -563,10 +565,13 @@
     )
     size = heads // GROUPS
     blocks = []
-    for g, maps in enumerate(exchanged):
+    exchanged = [exchange(own_maps[0], leaves)]
+    for g in range(GROUPS):
         earlier = blocks[-1] if blocks else reads[0]
-        maps = after(earlier, *maps)
+        maps = after(earlier, *exchanged[g])
         before, state, *trans = join(place, maps, links)
+        if g + 1 < GROUPS:
+            exchanged.append(exchange(*after(state, own_maps[g + 1]), leaves))
         arrived = from_behind(state.astype(BF16), "chain", 1)
         for _ in range(links - 1):
             passed = jnp.einsum(

time: 79.7 us -> 71.5 us (0.90)
  local copies, waits for them, and re-layouts: 7.73 us -> 1.37 us
  starting transfers between devices: 19.9 us -> 18.6 us
    unnamed x34 -> x18, local copies, waits for them, and re-layouts: 6.41 us -> 0.05 us
    ppermute x6, starting transfers between devices: 8.14 us -> 7.11 us  [exchange(): lax.ppermute(own_map, 'leaf', pairs_at(k, leaves))]
  transfers between devices with their start and end apart: 15 -> 15, of which waited for: 7 -> 8; matrix products, arithmetic and copies ran while one was open for 7% -> 8% of each run, Pallas kernels for 14% -> 13%
where the time goes in v11:
time: 71.5 us; the launch traced here: 71.2 us
  waiting for transfers between devices  28.5 us (40%)
  starting transfers between devices  18.6 us (26%)
  Pallas kernels  17.9 us (25%)
  matrix products  4.34 us (6%)
  local copies, waits for them, and re-layouts  1.37 us (2%)
    ppermute x6, waiting for transfers between devices, on_device(): lax.ppermute(x, 'head', around)  27.3 us
    ppermute x3, starting transfers between devices, from_behind(): lax.ppermute(value, axis, [(i, i + steps) for i in range(count - steps)])  8.03 us
    ppermute x6, starting transfers between devices, exchange(): lax.ppermute(own_map, 'leaf', pairs_at(k, leaves))  7.11 us
    pallas_call x1, Pallas kernels, reads_of(): pl.pallas_call(functools.partial(reads_kernel, base), out_shape=(jax.Shap...  5.44 us
    pallas_call x1, Pallas kernels, maps_of(): pl.pallas_call(functools.partial(maps_kernel, base), out_shape=(jax.Shape...  5.07 us
    dot_general x7, matrix products, on_device(): term = jnp.dot(block, rows, preferred_element_type=F32)  4.34 us
    ppermute x6, starting transfers between devices, on_device(): lax.ppermute(x, 'head', around)  3.46 us
    pallas_call x1, Pallas kernels, filters_of(): pl.pallas_call(filters_kernel, out_shape=(per_token, per_token, jax.Shape...  1.78 us
  transfers between devices with their start and end apart: 15, of which 8 were waited for; matrix products, arithmetic and copies ran while one was open for 8% of the time, Pallas kernels for 13%

profile of v11, /device:TPU:0, one launch (start us, length us, event | category | flops | bytes accessed | tf_op | source)
XLA Modules:
  0.0 71.2 jit_solution(16719549738380622976)
XLA Ops:
  0.0 1.4 %shard_map.101 = bf16[24,4,128]{2,1,0:T(4,128)(2,1)} custom-call(bf16[512,4,128]{2,1,0:T(4,128)(2,1)} %refs_0_.1, bf16[512,4,128]{2,1,0:T(4,128)(2,1)} %refs_1_.1, bf16[512,4,128]{2,1,0:T(4,128)(2,1)} %refs_2_.1), custom_call_target="tpu_custom_call" | custom-call | flops 1000000000 | bytes 65536 | tf_op jit(solution)/shard_map/pallas_call | solution.py:412
  1.4 4.8 %collective-permute-start = (bf16[24,4,128]{2,1,0:T(4,128)(2,1)}, bf16[24,4,128]{2,1,0:T(4,128)(2,1)S(1)}, u32[]{:S(2)}, u32[]{:S(2)}) collective-permute-start(bf16[24,4,128]{2,1,0:T(4,128)(2,1)} %shard_map.101), channel_id=1, source_target_pairs={{0,4},{4,8},{8,12},{12,16},{16,20},{20,24},{24,28},{1,5},{5,9},{9,... | collective-permute-start | bytes 73736 | tf_op jit(solution)/shard_map/ppermute | solution.py:395
  6.3 1.2 %copy_bitcast_fusion.2 = (bf16[4,512,128]{2,1,0:T(8,128)(2,1)S(1)}, bf16[4,512,128]{2,1,0:T(8,128)(2,1)S(1)}) fusion(bf16[512,4,128]{2,1,0:T(4,128)(2,1)S(1)} %copy-done.8, bf16[512,4,128]{2,1,0:T(4,128)(2,1)} %refs_1_.1), kind=kLoop, calls=%fused_computation.4 | loop fusion | bytes 2097152 | tf_op jit(solution)/shard_map/transpose | solution.py:550
  7.5 1.8 %shard_map.100 = (bf16[4,512,128]{2,1,0:T(8,128)(2,1)S(1)}, bf16[4,512,128]{2,1,0:T(8,128)(2,1)S(1)}, f32[2,4,16,128]{3,2,1,0:T(8,128)S(1)}) custom-call(bf16[4,512,128]{2,1,0:T(8,128)(2,1)S(1)} %get-tuple-element.58.key_ref, bf16[4,512,128]{2,1,0:T(8,128)(2,1)S(1)} %get-tuple-element.57.value_ref, f32[3,4,4,128]{3,2,1,0:T(4,128)S(1)} %copy-done.1), custom_call_target="tpu_custom_call" | custom-call | flops 3000000000 | bytes 4194304 | tf_op jit(solution)/shard_map/pallas_call | solution.py:426
  9.4 5.1 %shard_map.102 = (bf16[4,512,128]{2,1,0:T(8,128)(2,1)S(1)}, f32[4,512,256]{2,1,0:T(8,128)S(1)}, f32[4,3,128,256]{3,2,1,0:T(8,128)S(1)}, bf16[2,128,256]{2,1,0:T(8,128)(2,1)S(1)}, bf16[2,128,256]{2,1,0:T(8,128)(2,1)S(1)}) custom-call(s32[8]{0:T(128)S(1)} %copy-done.4, bf16[4,512,128]{2,1,0:T(8,128)(2,1)S(1)} %get-tuple-element.31.unit_in_ref, ...), custom_call_target="tpu_custom_call" | custom-call | flops 5000000000 | bytes 4194304 | tf_op jit(solution)/shard_map/pallas_call | solution.py:442
  14.5 1.6 %collective-permute-start.1 = (bf16[2,128,256]{2,1,0:T(8,128)(2,1)S(1)}, bf16[2,128,256]{2,1,0:T(8,128)(2,1)S(1)}, u32[]{:S(2)}, u32[]{:S(2)}) collective-permute-start(bf16[2,128,256]{2,1,0:T(8,128)(2,1)S(1)} %get-tuple-element.42.refs_0_), channel_id=1, source_target_pairs={{0,4},{4,0},{8,12},{12,8},{1,5},{5,1},{9,13},{13,9},{2,6},{6,2},{1... | collective-permute-start | bytes 393224 | tf_op jit(solution)/shard_map/ppermute | solution.py:399
  16.0 1.0 %collective-permute-start.2 = (bf16[2,128,256]{2,1,0:T(8,128)(2,1)S(1)}, bf16[2,128,256]{2,1,0:T(8,128)(2,1)S(1)}, u32[]{:S(2)}, u32[]{:S(2)}) collective-permute-start(bf16[2,128,256]{2,1,0:T(8,128)(2,1)S(1)} %get-tuple-element.42.refs_0_), channel_id=1, source_target_pairs={{0,8},{4,12},{8,0},{12,4},{1,9},{5,13},{9,1},{13,5},{2,10},{6,14},... | collective-permute-start | bytes 393224 | tf_op jit(solution)/shard_map/ppermute | solution.py:399
  17.0 1.0 %collective-permute-start.3 = (bf16[2,128,256]{2,1,0:T(8,128)(2,1)S(1)}, bf16[2,128,256]{2,1,0:T(8,128)(2,1)S(1)}, u32[]{:S(2)}, u32[]{:S(2)}) collective-permute-start(bf16[2,128,256]{2,1,0:T(8,128)(2,1)S(1)} %get-tuple-element.42.refs_0_), channel_id=1, source_target_pairs={{0,12},{4,8},{8,4},{12,0},{1,13},{5,9},{9,5},{13,1},{2,14},{6,10},... | collective-permute-start | bytes 393224 | tf_op jit(solution)/shard_map/ppermute | solution.py:399
  18.2 5.4 %shard_map.103 = (bf16[4,512,128]{2,1,0:T(8,128)(2,1)S(1)}, f32[4,512,128]{2,1,0:T(8,128)S(1)}, f32[4,512,128]{2,1,0:T(8,128)S(1)}) custom-call(s32[8]{0:T(128)S(1)} %copy-done.4, bf16[4,512,128]{2,1,0:T(8,128)(2,1)S(1)} %bitcast.21, bf16[4,512,128]{2,1,0:T(8,128)(2,1)S(1)} %bitcast.20, f32[1,128]{1,0:T(1,128)S(1)} %bitcast.22, ...), custom_call_target="tpu_custom_call" | custom-call | flops 3000000000 | bytes 4194304 | tf_op jit(solution)/shard_map/pallas_call | solution.py:468
  24.4 2.0 %collective-permute-start.10 = (bf16[2,128,256]{2,1,0:T(8,128)(2,1)S(1)}, bf16[2,128,256]{2,1,0:T(8,128)(2,1)S(1)}, u32[]{:S(2)}, u32[]{:S(2)}) collective-permute-start(bf16[2,128,256]{2,1,0:T(8,128)(2,1)S(1)} %get-tuple-element.51.refs_0_), channel_id=1, source_target_pairs={{0,12},{4,8},{8,4},{12,0},{1,13},{5,9},{9,5},{13,1},{2,14},{6,10},... | collective-permute-start | bytes 393224 | tf_op jit(solution)/shard_map/ppermute | solution.py:399
  26.4 1.4 %collective-permute-start.8 = (bf16[2,128,256]{2,1,0:T(8,128)(2,1)S(1)}, bf16[2,128,256]{2,1,0:T(8,128)(2,1)S(1)}, u32[]{:S(2)}, u32[]{:S(2)}) collective-permute-start(bf16[2,128,256]{2,1,0:T(8,128)(2,1)S(1)} %get-tuple-element.51.refs_0_), channel_id=1, source_target_pairs={{0,4},{4,0},{8,12},{12,8},{1,5},{5,1},{9,13},{13,9},{2,6},{6,2},{1... | collective-permute-start | bytes 393224 | tf_op jit(solution)/shard_map/ppermute | solution.py:399
  28.0 1.3 %collective-permute-start.4 = (bf16[2,128,128]{2,1,0:T(8,128)(2,1)S(1)}, bf16[2,128,128]{2,1,0:T(8,128)(2,1)S(1)}, u32[]{:S(2)}, u32[]{:S(2)}) collective-permute-start(bf16[2,128,128]{2,1,0:T(8,128)(2,1)S(1)} %get-tuple-element.46), channel_id=1, source_target_pairs={{0,16},{1,17},{2,18},{3,19},{4,20},{5,21},{6,22},{7,23},{8,24},{9,... | collective-permute-start | bytes 196616 | tf_op jit(solution)/shard_map/ppermute | solution.py:395
  29.3 0.8 %collective-permute-done.4.arrived_ref = bf16[2,128,128]{2,1,0:T(8,128)(2,1)S(1)} collective-permute-done((bf16[2,128,128]{2,1,0:T(8,128)(2,1)S(1)}, bf16[2,128,128]{2,1,0:T(8,128)(2,1)S(1)}, u32[]{:S(2)}, u32[]{:S(2)}) %collective-permute-start.4) | collective-permute-done | bytes 65568 | tf_op jit(solution)/shard_map/ppermute | solution.py:395
  30.9 1.6 %collective-permute-start.5 = (bf16[512,256]{1,0:T(8,128)(2,1)S(1)}, bf16[512,256]{1,0:T(8,128)(2,1)S(1)}, u32[]{:S(2)}, u32[]{:S(2)}) collective-permute-start(bf16[512,256]{1,0:T(8,128)(2,1)S(1)} %shard_map.105), channel_id=1, source_target_pairs={{0,1},{1,2},{2,3},{3,0},{4,5},{5,6},{6,7},{7,4},{8,9},{9,10},{10,1... | collective-permute-start | bytes 786440 | tf_op jit(solution)/shard_map/ppermute | solution.py:592
  33.5 1.9 %collective-permute-start.11 = (bf16[2,128,128]{2,1,0:T(8,128)(2,1)S(1)}, bf16[2,128,128]{2,1,0:T(8,128)(2,1)S(1)}, u32[]{:S(2)}, u32[]{:S(2)}) collective-permute-start(bf16[2,128,128]{2,1,0:T(8,128)(2,1)S(1)} %get-tuple-element.55), channel_id=1, source_target_pairs={{0,16},{1,17},{2,18},{3,19},{4,20},{5,21},{6,22},{7,23},{8,24},{9,... | collective-permute-start | bytes 196616 | tf_op jit(solution)/shard_map/ppermute | solution.py:395
  35.5 1.6 %fusion.10 = f32[512,1024]{1,0:T(8,128)S(1)} fusion(bf16[512,256]{1,0:T(8,128)(2,1)S(1)} %shard_map.105, bf16[2048,1024]{1,0:T(8,128)(2,1)} %weights_ref.1, s32[]{:T(128)S(6)} %select_n.21), kind=kOutput, calls=%fused_computation.16 | convolution fusion | flops 268435456 | bytes 2883588 | tf_op jit(solution)/shard_map/dot_general | solution.py:598
  37.9 1.6 %collective-permute-start.12 = (bf16[512,256]{1,0:T(8,128)(2,1)S(1)}, bf16[512,256]{1,0:T(8,128)(2,1)S(1)}, u32[]{:S(2)}, u32[]{:S(2)}) collective-permute-start(bf16[512,256]{1,0:T(8,128)(2,1)S(1)} %shard_map.107), channel_id=1, source_target_pairs={{0,1},{1,2},{2,3},{3,0},{4,5},{5,6},{6,7},{7,4},{8,9},{9,10},{10,1... | collective-permute-start | bytes 786440 | tf_op jit(solution)/shard_map/ppermute | solution.py:592
  39.9 1.4 %collective-permute-done.5 = bf16[512,256]{1,0:T(8,128)(2,1)S(1)} collective-permute-done((bf16[512,256]{1,0:T(8,128)(2,1)S(1)}, bf16[512,256]{1,0:T(8,128)(2,1)S(1)}, u32[]{:S(2)}, u32[]{:S(2)}) %collective-permute-start.5) | collective-permute-done | bytes 262176 | tf_op jit(solution)/shard_map/ppermute | solution.py:592
  42.0 6.9 %collective-permute-done.12 = bf16[512,256]{1,0:T(8,128)(2,1)S(1)} collective-permute-done((bf16[512,256]{1,0:T(8,128)(2,1)S(1)}, bf16[512,256]{1,0:T(8,128)(2,1)S(1)}, u32[]{:S(2)}, u32[]{:S(2)}) %collective-permute-start.12) | collective-permute-done | bytes 262176 | tf_op jit(solution)/shard_map/ppermute | solution.py:592
  49.4 5.2 %collective-permute-done.6 = bf16[512,256]{1,0:T(8,128)(2,1)S(1)} collective-permute-done((bf16[512,256]{1,0:T(8,128)(2,1)S(1)}, bf16[512,256]{1,0:T(8,128)(2,1)S(1)}, u32[]{:S(2)}, u32[]{:S(2)}) %collective-permute-start.6) | collective-permute-done | bytes 262176 | tf_op jit(solution)/shard_map/ppermute | solution.py:592
  55.0 5.2 %collective-permute-done.13 = bf16[512,256]{1,0:T(8,128)(2,1)S(1)} collective-permute-done((bf16[512,256]{1,0:T(8,128)(2,1)S(1)}, bf16[512,256]{1,0:T(8,128)(2,1)S(1)}, u32[]{:S(2)}, u32[]{:S(2)}) %collective-permute-start.13) | collective-permute-done | bytes 262176 | tf_op jit(solution)/shard_map/ppermute | solution.py:592
  60.7 5.1 %collective-permute-done.7 = bf16[512,256]{1,0:T(8,128)(2,1)S(1)} collective-permute-done((bf16[512,256]{1,0:T(8,128)(2,1)S(1)}, bf16[512,256]{1,0:T(8,128)(2,1)S(1)}, u32[]{:S(2)}, u32[]{:S(2)}) %collective-permute-start.7) | collective-permute-done | bytes 262176 | tf_op jit(solution)/shard_map/ppermute | solution.py:592
  66.3 3.5 %collective-permute-done.14.block_ref = bf16[512,256]{1,0:T(8,128)(2,1)S(1)} collective-permute-done((bf16[512,256]{1,0:T(8,128)(2,1)S(1)}, bf16[512,256]{1,0:T(8,128)(2,1)S(1)}, u32[]{:S(2)}, u32[]{:S(2)}) %collective-permute-start.14) | collective-permute-done | bytes 262176 | tf_op jit(solution)/shard_map/ppermute | solution.py:592
  69.8 1.3 %shard_map.108 = bf16[512,1024]{1,0:T(8,128)(2,1)} custom-call(s32[1]{0:T(128)} %bitcast.section, f32[512,1024]{1,0:T(8,128)S(1)} %add_add_fusion.1.first_ref, f32[512,1024]{1,0:T(8,128)S(1)} %add_add_fusion.second_ref, bf16[512,256]{1,0:T(8,128)(2,1)S(1)} %collective-permute-done.14.block_ref, bf16[2048,1024]{1,0:T(8,128)(2,1)S(1)} %copy-done), custom_call_target="tpu_custom_call" | custom-call | tf_op jit(solution)/shard_map/pallas_call | solution.py:518
  (43 shorter events, 6.5 us)
Async XLA Ops:
  0.0 6.3 %copy-start.8 = (bf16[512,4,128]{2,1,0:T(4,128)(2,1)S(1)}, bf16[512,4,128]{2,1,0:T(4,128)(2,1)}, u32[]{:S(2)}) copy-start(bf16[512,4,128]{2,1,0:T(4,128)(2,1)} %refs_2_.1) | copy-start | bytes 1572868
  0.0 7.5 %copy-start.1 = (f32[3,4,4,128]{3,2,1,0:T(4,128)S(1)}, f32[3,4,4,128]{3,2,1,0:T(4,128)}, u32[]{:S(2)}) copy-start(f32[3,4,4,128]{3,2,1,0:T(4,128)} %taps_ref.5) | copy-start | bytes 73732
  1.4 7.9 %collective-permute-start = (bf16[24,4,128]{2,1,0:T(4,128)(2,1)}, bf16[24,4,128]{2,1,0:T(4,128)(2,1)S(1)}, u32[]{:S(2)}, u32[]{:S(2)}) collective-permute-start(bf16[24,4,128]{2,1,0:T(4,128)(2,1)} %shard_map.101), channel_id=1, source_target_pairs={{0,4},{4,8},{8,12},{12,16},{16,20},{20,24},{24,28},{1,5},{5,9},{9,... | collective-permute-start | bytes 73736 | tf_op jit(solution)/shard_map/ppermute | solution.py:395
  7.5 1.8 %copy-start.2 = (f32[4,512]{1,0:T(4,128)S(1)}, f32[4,512]{1,0:T(4,128)}, u32[]{:S(2)}) copy-start(f32[4,512]{1,0:T(4,128)} %decay_ref.3) | copy-start | bytes 24580
  7.5 1.8 %copy-start.3 = (f32[4,512]{1,0:T(4,128)S(1)}, f32[4,512]{1,0:T(4,128)}, u32[]{:S(2)}) copy-start(f32[4,512]{1,0:T(4,128)} %strength_ref.3) | copy-start | bytes 24580
  7.5 1.8 %copy-start.4 = (s32[8]{0:T(128)S(1)}, s32[8]{0:T(128)}, u32[]{:S(2)}) copy-start(s32[8]{0:T(128)} %resets.3) | copy-start | bytes 100
  9.4 8.7 %copy-start.6 = (bf16[512,4,128]{2,1,0:T(4,128)(2,1)S(1)}, bf16[512,4,128]{2,1,0:T(4,128)(2,1)}, u32[]{:S(2)}) copy-start(bf16[512,4,128]{2,1,0:T(4,128)(2,1)} %param.13) | copy-start | bytes 1572868
  9.4 8.7 %copy-start.7 = (bf16[512,4,128]{2,1,0:T(4,128)(2,1)S(1)}, bf16[512,4,128]{2,1,0:T(4,128)(2,1)}, u32[]{:S(2)}) copy-start(bf16[512,4,128]{2,1,0:T(4,128)(2,1)} %refs_0_.1) | copy-start | bytes 1572868
  14.5 3.7 %copy-start.5 = (f32[128]{0:T(128)S(1)}, f32[128]{0:T(128)}, u32[]{:S(2)}) copy-start(f32[128]{0:T(128)} %param.18) | copy-start | bytes 1540
  14.5 9.2 %collective-permute-start.1 = (bf16[2,128,256]{2,1,0:T(8,128)(2,1)S(1)}, bf16[2,128,256]{2,1,0:T(8,128)(2,1)S(1)}, u32[]{:S(2)}, u32[]{:S(2)}) collective-permute-start(bf16[2,128,256]{2,1,0:T(8,128)(2,1)S(1)} %get-tuple-element.42.refs_0_), channel_id=1, source_target_pairs={{0,4},{4,0},{8,12},{12,8},{1,5},{5,1},{9,13},{13,9},{2,6},{6,2},{1... | collective-permute-start | bytes 393224 | tf_op jit(solution)/shard_map/ppermute | solution.py:399
  16.0 7.6 %collective-permute-start.2 = (bf16[2,128,256]{2,1,0:T(8,128)(2,1)S(1)}, bf16[2,128,256]{2,1,0:T(8,128)(2,1)S(1)}, u32[]{:S(2)}, u32[]{:S(2)}) collective-permute-start(bf16[2,128,256]{2,1,0:T(8,128)(2,1)S(1)} %get-tuple-element.42.refs_0_), channel_id=1, source_target_pairs={{0,8},{4,12},{8,0},{12,4},{1,9},{5,13},{9,1},{13,5},{2,10},{6,14},... | collective-permute-start | bytes 393224 | tf_op jit(solution)/shard_map/ppermute | solution.py:399
  17.0 6.7 %collective-permute-start.3 = (bf16[2,128,256]{2,1,0:T(8,128)(2,1)S(1)}, bf16[2,128,256]{2,1,0:T(8,128)(2,1)S(1)}, u32[]{:S(2)}, u32[]{:S(2)}) collective-permute-start(bf16[2,128,256]{2,1,0:T(8,128)(2,1)S(1)} %get-tuple-element.42.refs_0_), channel_id=1, source_target_pairs={{0,12},{4,8},{8,4},{12,0},{1,13},{5,9},{9,5},{13,1},{2,14},{6,10},... | collective-permute-start | bytes 393224 | tf_op jit(solution)/shard_map/ppermute | solution.py:399
  24.4 8.1 %collective-permute-start.10 = (bf16[2,128,256]{2,1,0:T(8,128)(2,1)S(1)}, bf16[2,128,256]{2,1,0:T(8,128)(2,1)S(1)}, u32[]{:S(2)}, u32[]{:S(2)}) collective-permute-start(bf16[2,128,256]{2,1,0:T(8,128)(2,1)S(1)} %get-tuple-element.51.refs_0_), channel_id=1, source_target_pairs={{0,12},{4,8},{8,4},{12,0},{1,13},{5,9},{9,5},{13,1},{2,14},{6,10},... | collective-permute-start | bytes 393224 | tf_op jit(solution)/shard_map/ppermute | solution.py:399
  26.4 6.1 %collective-permute-start.8 = (bf16[2,128,256]{2,1,0:T(8,128)(2,1)S(1)}, bf16[2,128,256]{2,1,0:T(8,128)(2,1)S(1)}, u32[]{:S(2)}, u32[]{:S(2)}) collective-permute-start(bf16[2,128,256]{2,1,0:T(8,128)(2,1)S(1)} %get-tuple-element.51.refs_0_), channel_id=1, source_target_pairs={{0,4},{4,0},{8,12},{12,8},{1,5},{5,1},{9,13},{13,9},{2,6},{6,2},{1... | collective-permute-start | bytes 393224 | tf_op jit(solution)/shard_map/ppermute | solution.py:399
  27.8 5.0 %collective-permute-start.9 = (bf16[2,128,256]{2,1,0:T(8,128)(2,1)S(1)}, bf16[2,128,256]{2,1,0:T(8,128)(2,1)S(1)}, u32[]{:S(2)}, u32[]{:S(2)}) collective-permute-start(bf16[2,128,256]{2,1,0:T(8,128)(2,1)S(1)} %get-tuple-element.51.refs_0_), channel_id=1, source_target_pairs={{0,8},{4,12},{8,0},{12,4},{1,9},{5,13},{9,1},{13,5},{2,10},{6,14},... | collective-permute-start | bytes 393224 | tf_op jit(solution)/shard_map/ppermute | solution.py:399
  28.0 2.2 %collective-permute-start.4 = (bf16[2,128,128]{2,1,0:T(8,128)(2,1)S(1)}, bf16[2,128,128]{2,1,0:T(8,128)(2,1)S(1)}, u32[]{:S(2)}, u32[]{:S(2)}) collective-permute-start(bf16[2,128,128]{2,1,0:T(8,128)(2,1)S(1)} %get-tuple-element.46), channel_id=1, source_target_pairs={{0,16},{1,17},{2,18},{3,19},{4,20},{5,21},{6,22},{7,23},{8,24},{9,... | collective-permute-start | bytes 196616 | tf_op jit(solution)/shard_map/ppermute | solution.py:395
  30.9 10.5 %collective-permute-start.5 = (bf16[512,256]{1,0:T(8,128)(2,1)S(1)}, bf16[512,256]{1,0:T(8,128)(2,1)S(1)}, u32[]{:S(2)}, u32[]{:S(2)}) collective-permute-start(bf16[512,256]{1,0:T(8,128)(2,1)S(1)} %shard_map.105), channel_id=1, source_target_pairs={{0,1},{1,2},{2,3},{3,0},{4,5},{5,6},{6,7},{7,4},{8,9},{9,10},{10,1... | collective-permute-start | bytes 786440 | tf_op jit(solution)/shard_map/ppermute | solution.py:592
  33.5 3.6 %collective-permute-start.11 = (bf16[2,128,128]{2,1,0:T(8,128)(2,1)S(1)}, bf16[2,128,128]{2,1,0:T(8,128)(2,1)S(1)}, u32[]{:S(2)}, u32[]{:S(2)}) collective-permute-start(bf16[2,128,128]{2,1,0:T(8,128)(2,1)S(1)} %get-tuple-element.55), channel_id=1, source_target_pairs={{0,16},{1,17},{2,18},{3,19},{4,20},{5,21},{6,22},{7,23},{8,24},{9,... | collective-permute-start | bytes 196616 | tf_op jit(solution)/shard_map/ppermute | solution.py:395
  35.5 4.0 %copy-start = (bf16[2048,1024]{1,0:T(8,128)(2,1)S(1)}, bf16[2048,1024]{1,0:T(8,128)(2,1)}, u32[]{:S(2)}) copy-start(bf16[2048,1024]{1,0:T(8,128)(2,1)} %weights_ref.1) | copy-start | bytes 12582916
  37.9 11.1 %collective-permute-start.12 = (bf16[512,256]{1,0:T(8,128)(2,1)S(1)}, bf16[512,256]{1,0:T(8,128)(2,1)S(1)}, u32[]{:S(2)}, u32[]{:S(2)}) collective-permute-start(bf16[512,256]{1,0:T(8,128)(2,1)S(1)} %shard_map.107), channel_id=1, source_target_pairs={{0,1},{1,2},{2,3},{3,0},{4,5},{5,6},{6,7},{7,4},{8,9},{9,10},{10,1... | collective-permute-start | bytes 786440 | tf_op jit(solution)/shard_map/ppermute | solution.py:592
  41.4 13.2 %collective-permute-start.6 = (bf16[512,256]{1,0:T(8,128)(2,1)S(1)}, bf16[512,256]{1,0:T(8,128)(2,1)S(1)}, u32[]{:S(2)}, u32[]{:S(2)}) collective-permute-start(bf16[512,256]{1,0:T(8,128)(2,1)S(1)} %collective-permute-done.5), channel_id=1, source_target_pairs={{0,1},{1,2},{2,3},{3,0},{4,5},{5,6},{6,7},{7,4},{8,9},{9,10},{10,1... | collective-permute-start | bytes 786440 | tf_op jit(solution)/shard_map/ppermute | solution.py:592
  49.0 11.2 %collective-permute-start.13 = (bf16[512,256]{1,0:T(8,128)(2,1)S(1)}, bf16[512,256]{1,0:T(8,128)(2,1)S(1)}, u32[]{:S(2)}, u32[]{:S(2)}) collective-permute-start(bf16[512,256]{1,0:T(8,128)(2,1)S(1)} %collective-permute-done.12), channel_id=1, source_target_pairs={{0,1},{1,2},{2,3},{3,0},{4,5},{5,6},{6,7},{7,4},{8,9},{9,10},{10,1... | collective-permute-start | bytes 786440 | tf_op jit(solution)/shard_map/ppermute | solution.py:592
  54.6 11.2 %collective-permute-start.7 = (bf16[512,256]{1,0:T(8,128)(2,1)S(1)}, bf16[512,256]{1,0:T(8,128)(2,1)S(1)}, u32[]{:S(2)}, u32[]{:S(2)}) collective-permute-start(bf16[512,256]{1,0:T(8,128)(2,1)S(1)} %collective-permute-done.6), channel_id=1, source_target_pairs={{0,1},{1,2},{2,3},{3,0},{4,5},{5,6},{6,7},{7,4},{8,9},{9,10},{10,1... | collective-permute-start | bytes 786440 | tf_op jit(solution)/shard_map/ppermute | solution.py:592
  60.2 9.6 %collective-permute-start.14 = (bf16[512,256]{1,0:T(8,128)(2,1)S(1)}, bf16[512,256]{1,0:T(8,128)(2,1)S(1)}, u32[]{:S(2)}, u32[]{:S(2)}) collective-permute-start(bf16[512,256]{1,0:T(8,128)(2,1)S(1)} %collective-permute-done.13), channel_id=1, source_target_pairs={{0,1},{1,2},{2,3},{3,0},{4,5},{5,6},{6,7},{7,4},{8,9},{9,10},{10,1... | collective-permute-start | bytes 786440 | tf_op jit(solution)/shard_map/ppermute | solution.py:592

commit v12 on v11

--- a/solution.py
+++ b/solution.py
@@ -58,12 +58,16 @@
         precision=lax.Precision.HIGHEST,
         preferred_element_type=F32,
     )
-    strength = strength_ref[:, rows_of(c)]
-    stacked = [cum, strength]
+    stacked = [cum, strength_ref[:, rows_of(c)]]
     missing = 8 - 2 * cum.shape[0]
     if missing > 0:
         stacked.append(jnp.zeros((missing, CHUNK), F32))
-    return cum, strength, jnp.transpose(jnp.concatenate(stacked, axis=0))
+    return jnp.concatenate(stacked, axis=0)
+
+
+def lower_of(key, cum_col, cum_row, strength_col, strictly):
+    fading = jnp.exp(jnp.where(strictly, cum_col - cum_row, FAR))
+    return strength_col * fading * mul(key, key, NT)
 
 
 def silu(x):
@@ -156,8 +160,13 @@
         copy.wait()
 
 
-def filters_kernel(key_ref, value_ref, taps_ref, unit_ref, value_out_ref, first_ref, padded):
+def filters_kernel(
+    resets, key_ref, value_ref, taps_ref, decay_ref, strength_ref,
+    unit_ref, value_out_ref, first_ref, across_ref, down_ref, lowers_ref,
+    padded,
+):
     heads, length, _ = key_ref.shape
+    row, col = indices()
     for i, x_ref in enumerate((key_ref, value_ref)):
         padded[i, :, RIM:] = x_ref[...].astype(F32)
         padded[i, :, 0:RIM] = jnp.zeros((heads, RIM, padded.shape[3]), F32)
@@ -175,21 +184,32 @@
         return carry
 
     lax.fori_loop(0, heads, one_head, 0)
+    for c in range(length // CHUNK):
+        across = token_scalars(decay_ref, strength_ref, c)
+        down = jnp.transpose(across)
+        across_ref[c] = across
+        down_ref[c] = down
+        if c:
+            strictly = (row > col) & same_document(resets[2 * c + 1], row, col)
+            for h in range(heads):
+                lowers_ref[c - 1, h] = lower_of(
+                    unit_ref[h, rows_of(c)], down[:, h : h + 1], across[h : h + 1],
+                    down[:, heads + h : heads + h + 1], strictly,
+                )
 
 
 def maps_kernel(
-    base, resets, unit_in_ref, value_in_ref, first_ref, rim_ref, taps_ref, decay_ref, strength_ref,
+    resets, unit_in_ref, value_in_ref, first_ref, across_ref, down_ref, lowers_ref, rim_ref, taps_ref,
     unit_ref, solved_ref, starts_ref, *refs,
 ):
     *map_refs, rims, padded, value_s, step_s = refs
     heads, length, depth = unit_ref.shape
     chunks = length // CHUNK
     size = heads // len(map_refs)
-    total_heads = decay_ref.shape[0]
     row, col = indices()
     rims[...] = rim_ref[...].astype(F32)
     for g in range(heads):
-        h = base + g
+        h = g
         unit_ref[g] = unit_in_ref[h]
         value_s[g] = value_in_ref[h]
         for i in range(2):
@@ -204,17 +224,17 @@
     parts = []
     lowers = []
     for c in range(chunks):
-        cum, _, columns = token_scalars(decay_ref, strength_ref, c)
         first, second = resets[2 * c], resets[2 * c + 1]
+        across, down = across_ref[c], down_ref[c]
         strictly = (row > col) & same_document(second, row, col)
         for g in range(heads):
-            h = base + g
-            cum_col = columns[:, h : h + 1]
-            cum_row = cum[h : h + 1]
-            key = unit_ref[g, rows_of(c)]
-            fading = jnp.exp(jnp.where(strictly, cum_col - cum_row, FAR))
-            strength_col = columns[:, total_heads + h : total_heads + h + 1]
-            lowers.append(strength_col * fading * mul(key, key, NT))
+            cum_col, cum_row = down[:, g : g + 1], across[g : g + 1]
+            strength_col = down[:, heads + g : heads + g + 1]
+            if c:
+                lowers.append(lowers_ref[c - 1, g])
+            else:
+                key = unit_ref[g, rows_of(c)]
+                lowers.append(lower_of(key, cum_col, cum_row, strength_col, strictly))
             parts.append((g, c, first, second, cum_col, cum_row, strength_col))
     inverses = lower_inverse(lowers, row, col)
     eye = (row == col).astype(F32)
@@ -267,7 +287,7 @@
 
 
 def reads_kernel(
-    base, resets, query_ref, gate_ref, gain_ref, rim_ref, taps_ref, decay_ref, strength_ref,
+    resets, query_ref, gate_ref, gain_ref, across_ref, down_ref, rim_ref, taps_ref,
     unit_ref, solved_ref, starts_ref,
     reach_ref, part_ref, gating_ref,
     rims, padded, query_s,
@@ -278,7 +298,7 @@
     first_rows = lax.broadcasted_iota(jnp.int32, (CHUNK, 1), 0) < BLOCK
     rims[...] = rim_ref[...].astype(F32)
     for g in range(heads):
-        h = base + g
+        h = g
         padded[g, 0:RIM] = rims[0:RIM, h, :]
         padded[g, RIM : RIM + length] = query_ref[h].astype(F32)
         taps = taps_of(taps_ref, 0, h)
@@ -288,13 +308,13 @@
 
     for c in range(chunks):
         here = rows_of(c)
-        cum, _, columns = token_scalars(decay_ref, strength_ref, c)
+        cum, columns = across_ref[c], down_ref[c]
         first, second = resets[2 * c], resets[2 * c + 1]
         keep_first = (1 - first).astype(F32)
         keep_both = keep_first * (1 - second).astype(F32)
         upto = (row >= col) & same_document(second, row, col)
         for g in range(heads):
-            h = base + g
+            h = g
             cum_col = columns[:, h : h + 1]
             query = query_s[g, here]
             fading = jnp.exp(jnp.where(upto, cum_col - cum[h : h + 1], FAR))
@@ -304,7 +324,9 @@
             reach = growth * query.astype(F32) - own[:, :depth]
             part = own[:, depth:]
             if c:
-                both = mul_split(reach, starts_ref[g, c - 1])
+                high, low = split(starts_ref[g, c - 1])
+                rounded = reach.astype(BF16)
+                both = mul(rounded, high) + mul(rounded, low)
                 reach = both[:, :depth]
                 part = part + both[:, depth:]
             reach_ref[g, here] = reach.astype(BF16)
@@ -380,8 +402,8 @@
     width = block_ref.shape[1]
     rows = weights_ref[pl.ds(pl.multiple_of(section[0] * width, width), width), :]
     copies = []
-    for i in range(first_ref.shape[0] // CHUNK):
-        here = rows_of(i)
+    for i in range(first_ref.shape[0] // BLOCK):
+        here = slice(i * BLOCK, (i + 1) * BLOCK)
         total = (first_ref[here] + second_ref[here]) + mul(block_ref[here], rows)
         tiles[here] = total.astype(BF16)
         copies.append(pltpu.make_async_copy(tiles.at[here], out_ref.at[here], written.at[i]))
@@ -420,34 +442,43 @@
     )(*inputs)
 
 
-def filters_of(key, value, taps):
+def filters_of(resets, key, value, taps, decay, strength):
     heads, length, depth = key.shape
+    chunks = length // CHUNK
+    lines = max(8, 2 * heads)
     per_token = jax.ShapeDtypeStruct((heads, length, depth), BF16)
     return pl.pallas_call(
         filters_kernel,
-        out_shape=(per_token, per_token, jax.ShapeDtypeStruct((2, heads, AGAIN, depth), F32)),
-        in_specs=[VMEM] * 3,
-        out_specs=[VMEM] * 3,
+        out_shape=(
+            per_token,
+            per_token,
+            jax.ShapeDtypeStruct((2, heads, AGAIN, depth), F32),
+            jax.ShapeDtypeStruct((chunks, lines, CHUNK), F32),
+            jax.ShapeDtypeStruct((chunks, CHUNK, lines), F32),
+            jax.ShapeDtypeStruct((chunks - 1, heads, CHUNK, CHUNK), F32),
+        ),
+        in_specs=[SMEM] + [VMEM] * 5,
+        out_specs=[VMEM] * 6,
         scratch_shapes=[pltpu.VMEM((2, heads, length + RIM, depth), F32)],
         compiler_params=PARAMS,
         cost_estimate=pl.CostEstimate(
             flops=3 * 10**9, bytes_accessed=4 * 2**20, transcendentals=10**6
         ),
-    )(key, value, taps)
-
-
-def maps_of(base, heads, resets, unit_in, value_in, first, rims, taps, decay, strength):
-    _, length, depth = unit_in.shape
+    )(resets, key, value, taps, decay, strength)
+
+
+def maps_of(resets, made, rims, taps):
+    heads, length, depth = made[0].shape
     chunks = length // CHUNK
     return pl.pallas_call(
-        functools.partial(maps_kernel, base),
+        maps_kernel,
         out_shape=(
             jax.ShapeDtypeStruct((heads, length, depth), BF16),
             jax.ShapeDtypeStruct((heads, length, 2 * depth), F32),
             jax.ShapeDtypeStruct((heads, chunks - 1, depth, 2 * depth), F32),
             *[jax.ShapeDtypeStruct((heads // GROUPS, depth, 2 * depth), BF16)] * GROUPS,
         ),
-        in_specs=[SMEM] + [VMEM] * 7,
+        in_specs=[SMEM] + [VMEM] * 8,
         out_specs=[VMEM] * (3 + GROUPS),
         scratch_shapes=[
             pltpu.VMEM(rims.shape, F32),
@@ -459,14 +490,14 @@
         cost_estimate=pl.CostEstimate(
             flops=5 * 10**9, bytes_accessed=4 * 2**20, transcendentals=10**6
         ),
-    )(resets, unit_in, value_in, first, rims, taps, decay, strength)
-
-
-def reads_of(base, heads, resets, query, gate, gain, rims, taps, decay, strength, made):
-    _, length, depth = query.shape
+    )(resets, *made, rims, taps)
+
+
+def reads_of(resets, query, gate, gain, across, down, rims, taps, made):
+    heads, length, depth = query.shape
     per_token = jax.ShapeDtypeStruct((heads, length, depth), F32)
     return pl.pallas_call(
-        functools.partial(reads_kernel, base),
+        reads_kernel,
         out_shape=(jax.ShapeDtypeStruct(per_token.shape, BF16), per_token, per_token),
         in_specs=[SMEM] + [VMEM] * 10,
         out_specs=[VMEM] * 3,
@@ -479,7 +510,7 @@
         cost_estimate=pl.CostEstimate(
             flops=3 * 10**9, bytes_accessed=4 * 2**20, transcendentals=10**6
         ),
-    )(resets, query, gate, gain, rims, taps, decay, strength, *made)
+    )(resets, query, gate, gain, across, down, rims, taps, *made)
 
 
 def join(place, maps, links):
@@ -522,7 +553,7 @@
         out_specs=pl.BlockSpec(memory_space=pl.ANY),
         scratch_shapes=[
             pltpu.VMEM((length, columns), BF16),
-            pltpu.SemaphoreType.DMA((length // CHUNK,)),
+            pltpu.SemaphoreType.DMA((length // BLOCK,)),
         ],
         compiler_params=LAST_PARAMS,
     )(section.astype(jnp.int32).reshape(1), first, second, block, weights)
@@ -548,20 +579,18 @@
     taps = conv_weight
     rims = from_behind(pack_rims((query_in, key_in, value_in)), ("chain", "leaf"), 1)
     key, value = (jnp.transpose(x, (1, 0, 2)) for x in (key_in, value_in))
-    key, value, first = filters_of(key, value, taps)
+    filtered_keys = filters_of(doc_resets, key, value, taps, log_decay, write_strength)
+    across, down = filtered_keys[3:5]
     gain = output_norm_gain.reshape(1, depth)
     leaves = lax.axis_size("leaf")
     place = lax.axis_index("leaf").astype(jnp.int32).reshape(1)
-
     links = lax.axis_size("chain") - 1
-    unit_key, solved, starts, *own_maps = maps_of(
-        0, heads, doc_resets, key, value, first, rims, taps, log_decay, write_strength
-    )
+
+    unit_key, solved, starts, *own_maps = maps_of(doc_resets, filtered_keys, rims, taps)
     query_in, gate_in = after(own_maps[-1], query_in, gate_in)
     query, gate = (jnp.transpose(x, (1, 0, 2)) for x in (query_in, gate_in))
     reads = reads_of(
-        0, heads, doc_resets, query, gate, gain, rims, taps, log_decay, write_strength,
-        (unit_key, solved, starts),
+        doc_resets, query, gate, gain, across, down, rims, taps, (unit_key, solved, starts)
     )
     size = heads // GROUPS
     blocks = []
@@ -590,6 +619,8 @@
         owner = lax.rem(mine + ring - k, ring)
         last = k + 1 == ring
         following = blocks if last else [lax.ppermute(x, "head", around) for x in blocks]
+        if k == 0:
+            blocks[:-1] = after(following[0], *blocks[:-1])
         for g, block in enumerate(blocks):
             section = owner * GROUPS + g
             if last and g + 1 == GROUPS:

time: 71.5 us -> 75.5 us (1.056)
  waiting for transfers between devices: 28.5 us -> 31.3 us
  Pallas kernels: 17.9 us -> 19.9 us
    pallas_call x1, Pallas kernels: 1.78 us -> 3.58 us  [filters_of(): pl.pallas_call(filters_kernel, out_shape=(per_token, per_token, jax.Shape...]
    ppermute x6, waiting for transfers between devices: 27.3 us -> 28.9 us  [on_device(): lax.ppermute(x, 'head', around)]
    ppermute x6, waiting for transfers between devices: 0.28 us -> 1.56 us  [exchange(): lax.ppermute(own_map, 'leaf', pairs_at(k, leaves))]
  transfers between devices with their start and end apart: 15 -> 15, of which waited for: 8 -> 10; matrix products, arithmetic and copies ran while one was open for 8% -> 7% of each run, Pallas kernels for 13% -> 15%
where the time goes in v12:
time: 75.5 us; the launch traced here: 75.2 us
  waiting for transfers between devices  31.3 us (41%)
  Pallas kernels  19.9 us (26%)
  starting transfers between devices  18 us (24%)
  matrix products  4.19 us (6%)
  local copies, waits for them, and re-layouts  1.36 us (2%)
    ppermute x6, waiting for transfers between devices, on_device(): lax.ppermute(x, 'head', around)  28.9 us
    ppermute x3, starting transfers between devices, from_behind(): lax.ppermute(value, axis, [(i, i + steps) for i in range(count - steps)])  7.43 us
    ppermute x6, starting transfers between devices, exchange(): lax.ppermute(own_map, 'leaf', pairs_at(k, leaves))  7.11 us
    pallas_call x1, Pallas kernels, reads_of(): pl.pallas_call(reads_kernel, out_shape=(jax.ShapeDtypeStruct(per_token.sh...  6.07 us
    pallas_call x1, Pallas kernels, maps_of(): pl.pallas_call(maps_kernel, out_shape=(jax.ShapeDtypeStruct((heads, lengt...  4.2 us
    dot_general x7, matrix products, on_device(): term = jnp.dot(block, rows, preferred_element_type=F32)  4.19 us
    pallas_call x1, Pallas kernels, filters_of(): pl.pallas_call(filters_kernel, out_shape=(per_token, per_token, jax.Shape...  3.58 us
    ppermute x6, starting transfers between devices, on_device(): lax.ppermute(x, 'head', around)  3.49 us
  transfers between devices with their start and end apart: 15, of which 10 were waited for; matrix products, arithmetic and copies ran while one was open for 7% of the time, Pallas kernels for 15%

profile of v12, /device:TPU:0, one launch (start us, length us, event | category | flops | bytes accessed | tf_op | source)
XLA Modules:
  0.0 75.2 jit_solution(7984819181421601072)
XLA Ops:
  0.0 1.4 %shard_map.101 = bf16[24,4,128]{2,1,0:T(4,128)(2,1)} custom-call(bf16[512,4,128]{2,1,0:T(4,128)(2,1)} %refs_0_.1, bf16[512,4,128]{2,1,0:T(4,128)(2,1)} %refs_1_.1, bf16[512,4,128]{2,1,0:T(4,128)(2,1)} %refs_2_.1), custom_call_target="tpu_custom_call" | custom-call | flops 1000000000 | bytes 65536 | tf_op jit(solution)/shard_map/pallas_call | solution.py:434
  1.4 4.9 %collective-permute-start = (bf16[24,4,128]{2,1,0:T(4,128)(2,1)}, bf16[24,4,128]{2,1,0:T(4,128)(2,1)S(1)}, u32[]{:S(2)}, u32[]{:S(2)}) collective-permute-start(bf16[24,4,128]{2,1,0:T(4,128)(2,1)} %shard_map.101), channel_id=1, source_target_pairs={{0,4},{4,8},{8,12},{12,16},{16,20},{20,24},{24,28},{1,5},{5,9},{9,... | collective-permute-start | bytes 73736 | tf_op jit(solution)/shard_map/ppermute | solution.py:417
  6.3 1.2 %copy_bitcast_fusion.2 = (bf16[4,512,128]{2,1,0:T(8,128)(2,1)S(1)}, bf16[4,512,128]{2,1,0:T(8,128)(2,1)S(1)}) fusion(bf16[512,4,128]{2,1,0:T(4,128)(2,1)S(1)} %copy-done.8, bf16[512,4,128]{2,1,0:T(4,128)(2,1)} %refs_1_.1), kind=kLoop, calls=%fused_computation.4 | loop fusion | bytes 2097152 | tf_op jit(solution)/shard_map/transpose | solution.py:581
  7.5 3.6 %shard_map.100 = (bf16[4,512,128]{2,1,0:T(8,128)(2,1)S(1)}, bf16[4,512,128]{2,1,0:T(8,128)(2,1)S(1)}, f32[2,4,16,128]{3,2,1,0:T(8,128)S(1)}, f32[4,8,128]{2,1,0:...) custom-call(s32[8]{0:T(128)S(1)} %copy-done.4, ...), custom_call_target="tpu_custom_call" | custom-call | flops 3000000000 | bytes 4194304 | tf_op jit(solution)/shard_map/pallas_call | solution.py:450
  11.2 4.2 %shard_map.102 = (bf16[4,512,128]{2,1,0:T(8,128)(2,1)S(1)}, f32[4,512,256]{2,1,0:T(8,128)S(1)}, f32[4,3,128,256]{3,2,1,0:T(8,128)S(1)}, bf16[2,128,256]{2,1,0:T(8,128)(2,1)S(1)}, bf16[2,128,256]{2,1,0:T(8,128)(2,1)S(1)}) custom-call(s32[8]{0:T(128)S(1)} %copy-done.4, bf16[4,512,128]{2,1,0:T(8,128)(2,1)S(1)} %get-tuple-element.35.unit_in_ref, ...), custom_call_target="tpu_custom_call" | custom-call | flops 5000000000 | bytes 4194304 | tf_op jit(solution)/shard_map/pallas_call | solution.py:473
  15.4 1.0 %collective-permute-start.3 = (bf16[2,128,256]{2,1,0:T(8,128)(2,1)S(1)}, bf16[2,128,256]{2,1,0:T(8,128)(2,1)S(1)}, u32[]{:S(2)}, u32[]{:S(2)}) collective-permute-start(bf16[2,128,256]{2,1,0:T(8,128)(2,1)S(1)} %get-tuple-element.49.refs_0_), channel_id=1, source_target_pairs={{0,12},{4,8},{8,4},{12,0},{1,13},{5,9},{9,5},{13,1},{2,14},{6,10},... | collective-permute-start | bytes 393224 | tf_op jit(solution)/shard_map/ppermute | solution.py:421
  16.4 2.0 %collective-permute-start.2 = (bf16[2,128,256]{2,1,0:T(8,128)(2,1)S(1)}, bf16[2,128,256]{2,1,0:T(8,128)(2,1)S(1)}, u32[]{:S(2)}, u32[]{:S(2)}) collective-permute-start(bf16[2,128,256]{2,1,0:T(8,128)(2,1)S(1)} %get-tuple-element.49.refs_0_), channel_id=1, source_target_pairs={{0,8},{4,12},{8,0},{12,4},{1,9},{5,13},{9,1},{13,5},{2,10},{6,14},... | collective-permute-start | bytes 393224 | tf_op jit(solution)/shard_map/ppermute | solution.py:421
  19.1 6.1 %shard_map.103 = (bf16[4,512,128]{2,1,0:T(8,128)(2,1)S(1)}, f32[4,512,128]{2,1,0:T(8,128)S(1)}, f32[4,512,128]{2,1,0:T(8,128)S(1)}) custom-call(s32[8]{0:T(128)S(1)} %copy-done.4, bf16[4,512,128]{2,1,0:T(8,128)(2,1)S(1)} %bitcast.20, bf16[4,512,128]{2,1,0:T(8,128)(2,1)S(1)} %bitcast.21, f32[1,128]{1,0:T(1,128)S(1)} %bitcast.22, ...), custom_call_target="tpu_custom_call" | custom-call | flops 3000000000 | bytes 4194304 | tf_op jit(solution)/shard_map/pallas_call | solution.py:499
  26.0 1.0 %collective-permute-start.10 = (bf16[2,128,256]{2,1,0:T(8,128)(2,1)S(1)}, bf16[2,128,256]{2,1,0:T(8,128)(2,1)S(1)}, u32[]{:S(2)}, u32[]{:S(2)}) collective-permute-start(bf16[2,128,256]{2,1,0:T(8,128)(2,1)S(1)} %get-tuple-element.59.refs_0_), channel_id=1, source_target_pairs={{0,12},{4,8},{8,4},{12,0},{1,13},{5,9},{9,5},{13,1},{2,14},{6,10},... | collective-permute-start | bytes 393224 | tf_op jit(solution)/shard_map/ppermute | solution.py:421
  27.0 2.0 %collective-permute-start.9 = (bf16[2,128,256]{2,1,0:T(8,128)(2,1)S(1)}, bf16[2,128,256]{2,1,0:T(8,128)(2,1)S(1)}, u32[]{:S(2)}, u32[]{:S(2)}) collective-permute-start(bf16[2,128,256]{2,1,0:T(8,128)(2,1)S(1)} %get-tuple-element.59.refs_0_), channel_id=1, source_target_pairs={{0,8},{4,12},{8,0},{12,4},{1,9},{5,13},{9,1},{13,5},{2,10},{6,14},... | collective-permute-start | bytes 393224 | tf_op jit(solution)/shard_map/ppermute | solution.py:421
  29.5 1.3 %collective-permute-start.4 = (bf16[2,128,128]{2,1,0:T(8,128)(2,1)S(1)}, bf16[2,128,128]{2,1,0:T(8,128)(2,1)S(1)}, u32[]{:S(2)}, u32[]{:S(2)}) collective-permute-start(bf16[2,128,128]{2,1,0:T(8,128)(2,1)S(1)} %get-tuple-element.53), channel_id=1, source_target_pairs={{0,16},{1,17},{2,18},{3,19},{4,20},{5,21},{6,22},{7,23},{8,24},{9,... | collective-permute-start | bytes 196616 | tf_op jit(solution)/shard_map/ppermute | solution.py:417
  30.8 0.9 %collective-permute-done.4.arrived_ref = bf16[2,128,128]{2,1,0:T(8,128)(2,1)S(1)} collective-permute-done((bf16[2,128,128]{2,1,0:T(8,128)(2,1)S(1)}, bf16[2,128,128]{2,1,0:T(8,128)(2,1)S(1)}, u32[]{:S(2)}, u32[]{:S(2)}) %collective-permute-start.4) | collective-permute-done | bytes 65568 | tf_op jit(solution)/shard_map/ppermute | solution.py:417
  32.8 1.1 %collective-permute-done.9.refs_2_ = bf16[2,128,256]{2,1,0:T(8,128)(2,1)S(1)} collective-permute-done((bf16[2,128,256]{2,1,0:T(8,128)(2,1)S(1)}, bf16[2,128,256]{2,1,0:T(8,128)(2,1)S(1)}, u32[]{:S(2)}, u32[]{:S(2)}) %collective-permute-start.9) | collective-permute-done | bytes 131104 | tf_op jit(solution)/shard_map/ppermute | solution.py:421
  34.7 1.3 %collective-permute-start.11 = (bf16[2,128,128]{2,1,0:T(8,128)(2,1)S(1)}, bf16[2,128,128]{2,1,0:T(8,128)(2,1)S(1)}, u32[]{:S(2)}, u32[]{:S(2)}) collective-permute-start(bf16[2,128,128]{2,1,0:T(8,128)(2,1)S(1)} %get-tuple-element.63), channel_id=1, source_target_pairs={{0,16},{1,17},{2,18},{3,19},{4,20},{5,21},{6,22},{7,23},{8,24},{9,... | collective-permute-start | bytes 196616 | tf_op jit(solution)/shard_map/ppermute | solution.py:417
  36.1 1.6 %collective-permute-start.5 = (bf16[512,256]{1,0:T(8,128)(2,1)S(1)}, bf16[512,256]{1,0:T(8,128)(2,1)S(1)}, u32[]{:S(2)}, u32[]{:S(2)}) collective-permute-start(bf16[512,256]{1,0:T(8,128)(2,1)S(1)} %shard_map.105), channel_id=1, source_target_pairs={{0,1},{1,2},{2,3},{3,0},{4,5},{5,6},{6,7},{7,4},{8,9},{9,10},{10,1... | collective-permute-start | bytes 786440 | tf_op jit(solution)/shard_map/ppermute | solution.py:621
  38.4 1.8 %collective-permute-start.12 = (bf16[512,256]{1,0:T(8,128)(2,1)S(1)}, bf16[512,256]{1,0:T(8,128)(2,1)S(1)}, u32[]{:S(2)}, u32[]{:S(2)}) collective-permute-start(bf16[512,256]{1,0:T(8,128)(2,1)S(1)} %shard_map.107), channel_id=1, source_target_pairs={{0,1},{1,2},{2,3},{3,0},{4,5},{5,6},{6,7},{7,4},{8,9},{9,10},{10,1... | collective-permute-start | bytes 786440 | tf_op jit(solution)/shard_map/ppermute | solution.py:621
  40.2 1.5 %fusion.3 = f32[512,1024]{1,0:T(8,128)S(1)} fusion(bf16[512,256]{1,0:T(8,128)(2,1)S(1)} %shard_map.107, bf16[2048,1024]{1,0:T(8,128)(2,1)} %weights_ref.1, s32[]{:T(128)S(6)} %select_n.25), kind=kOutput, calls=%fused_computation.9 | convolution fusion | flops 268435456 | bytes 2883588 | tf_op jit(solution)/shard_map/dot_general | solution.py:629
  41.7 5.5 %collective-permute-done.5 = bf16[512,256]{1,0:T(8,128)(2,1)S(1)} collective-permute-done((bf16[512,256]{1,0:T(8,128)(2,1)S(1)}, bf16[512,256]{1,0:T(8,128)(2,1)S(1)}, u32[]{:S(2)}, u32[]{:S(2)}) %collective-permute-start.5) | collective-permute-done | bytes 262176 | tf_op jit(solution)/shard_map/ppermute | solution.py:621
  48.1 4.6 %collective-permute-done.12 = bf16[512,256]{1,0:T(8,128)(2,1)S(1)} collective-permute-done((bf16[512,256]{1,0:T(8,128)(2,1)S(1)}, bf16[512,256]{1,0:T(8,128)(2,1)S(1)}, u32[]{:S(2)}, u32[]{:S(2)}) %collective-permute-start.12) | collective-permute-done | bytes 262176 | tf_op jit(solution)/shard_map/ppermute | solution.py:621
  53.2 5.5 %collective-permute-done.6 = bf16[512,256]{1,0:T(8,128)(2,1)S(1)} collective-permute-done((bf16[512,256]{1,0:T(8,128)(2,1)S(1)}, bf16[512,256]{1,0:T(8,128)(2,1)S(1)}, u32[]{:S(2)}, u32[]{:S(2)}) %collective-permute-start.6) | collective-permute-done | bytes 262176 | tf_op jit(solution)/shard_map/ppermute | solution.py:621
  59.2 5.2 %collective-permute-done.13 = bf16[512,256]{1,0:T(8,128)(2,1)S(1)} collective-permute-done((bf16[512,256]{1,0:T(8,128)(2,1)S(1)}, bf16[512,256]{1,0:T(8,128)(2,1)S(1)}, u32[]{:S(2)}, u32[]{:S(2)}) %collective-permute-start.13) | collective-permute-done | bytes 262176 | tf_op jit(solution)/shard_map/ppermute | solution.py:621
  64.8 5.1 %collective-permute-done.7 = bf16[512,256]{1,0:T(8,128)(2,1)S(1)} collective-permute-done((bf16[512,256]{1,0:T(8,128)(2,1)S(1)}, bf16[512,256]{1,0:T(8,128)(2,1)S(1)}, u32[]{:S(2)}, u32[]{:S(2)}) %collective-permute-start.7) | collective-permute-done | bytes 262176 | tf_op jit(solution)/shard_map/ppermute | solution.py:621
  70.4 3.0 %collective-permute-done.14.block_ref = bf16[512,256]{1,0:T(8,128)(2,1)S(1)} collective-permute-done((bf16[512,256]{1,0:T(8,128)(2,1)S(1)}, bf16[512,256]{1,0:T(8,128)(2,1)S(1)}, u32[]{:S(2)}, u32[]{:S(2)}) %collective-permute-start.14) | collective-permute-done | bytes 262176 | tf_op jit(solution)/shard_map/ppermute | solution.py:621
  73.4 1.7 %shard_map.108 = bf16[512,1024]{1,0:T(8,128)(2,1)} custom-call(s32[1]{0:T(128)} %bitcast.section, f32[512,1024]{1,0:T(8,128)S(1)} %add_add_fusion.1.first_ref, f32[512,1024]{1,0:T(8,128)S(1)} %add_add_fusion.second_ref, bf16[512,256]{1,0:T(8,128)(2,1)S(1)} %collective-permute-done.14.block_ref, bf16[2048,1024]{1,0:T(8,128)(2,1)S(1)} %copy-done), custom_call_target="tpu_custom_call" | custom-call | tf_op jit(solution)/shard_map/pallas_call | solution.py:549
  (43 shorter events, 7.4 us)
Async XLA Ops:
  0.0 6.3 %copy-start.8 = (bf16[512,4,128]{2,1,0:T(4,128)(2,1)S(1)}, bf16[512,4,128]{2,1,0:T(4,128)(2,1)}, u32[]{:S(2)}) copy-start(bf16[512,4,128]{2,1,0:T(4,128)(2,1)} %refs_2_.1) | copy-start | bytes 1572868
  0.0 7.5 %copy-start.1 = (f32[3,4,4,128]{3,2,1,0:T(4,128)S(1)}, f32[3,4,4,128]{3,2,1,0:T(4,128)}, u32[]{:S(2)}) copy-start(f32[3,4,4,128]{3,2,1,0:T(4,128)} %taps_ref.5) | copy-start | bytes 73732
  0.0 7.5 %copy-start.4 = (s32[8]{0:T(128)S(1)}, s32[8]{0:T(128)}, u32[]{:S(2)}) copy-start(s32[8]{0:T(128)} %resets.5) | copy-start | bytes 100
  0.0 7.5 %copy-start.2 = (f32[4,512]{1,0:T(4,128)S(1)}, f32[4,512]{1,0:T(4,128)}, u32[]{:S(2)}) copy-start(f32[4,512]{1,0:T(4,128)} %decay_ref.1) | copy-start | bytes 24580
  0.0 7.5 %copy-start.3 = (f32[4,512]{1,0:T(4,128)S(1)}, f32[4,512]{1,0:T(4,128)}, u32[]{:S(2)}) copy-start(f32[4,512]{1,0:T(4,128)} %strength_ref.1) | copy-start | bytes 24580
  1.4 9.7 %collective-permute-start = (bf16[24,4,128]{2,1,0:T(4,128)(2,1)}, bf16[24,4,128]{2,1,0:T(4,128)(2,1)S(1)}, u32[]{:S(2)}, u32[]{:S(2)}) collective-permute-start(bf16[24,4,128]{2,1,0:T(4,128)(2,1)} %shard_map.101), channel_id=1, source_target_pairs={{0,4},{4,8},{8,12},{12,16},{16,20},{20,24},{24,28},{1,5},{5,9},{9,... | collective-permute-start | bytes 73736 | tf_op jit(solution)/shard_map/ppermute | solution.py:417
  11.1 7.8 %copy-start.6 = (bf16[512,4,128]{2,1,0:T(4,128)(2,1)S(1)}, bf16[512,4,128]{2,1,0:T(4,128)(2,1)}, u32[]{:S(2)}) copy-start(bf16[512,4,128]{2,1,0:T(4,128)(2,1)} %refs_0_.1) | copy-start | bytes 1572868
  11.2 7.9 %copy-start.7 = (bf16[512,4,128]{2,1,0:T(4,128)(2,1)S(1)}, bf16[512,4,128]{2,1,0:T(4,128)(2,1)}, u32[]{:S(2)}) copy-start(bf16[512,4,128]{2,1,0:T(4,128)(2,1)} %param.13) | copy-start | bytes 1572868
  15.4 3.7 %copy-start.5 = (f32[128]{0:T(128)S(1)}, f32[128]{0:T(128)}, u32[]{:S(2)}) copy-start(f32[128]{0:T(128)} %param.18) | copy-start | bytes 1540
  15.4 9.8 %collective-permute-start.3 = (bf16[2,128,256]{2,1,0:T(8,128)(2,1)S(1)}, bf16[2,128,256]{2,1,0:T(8,128)(2,1)S(1)}, u32[]{:S(2)}, u32[]{:S(2)}) collective-permute-start(bf16[2,128,256]{2,1,0:T(8,128)(2,1)S(1)} %get-tuple-element.49.refs_0_), channel_id=1, source_target_pairs={{0,12},{4,8},{8,4},{12,0},{1,13},{5,9},{9,5},{13,1},{2,14},{6,10},... | collective-permute-start | bytes 393224 | tf_op jit(solution)/shard_map/ppermute | solution.py:421
  16.4 8.8 %collective-permute-start.2 = (bf16[2,128,256]{2,1,0:T(8,128)(2,1)S(1)}, bf16[2,128,256]{2,1,0:T(8,128)(2,1)S(1)}, u32[]{:S(2)}, u32[]{:S(2)}) collective-permute-start(bf16[2,128,256]{2,1,0:T(8,128)(2,1)S(1)} %get-tuple-element.49.refs_0_), channel_id=1, source_target_pairs={{0,8},{4,12},{8,0},{12,4},{1,9},{5,13},{9,1},{13,5},{2,10},{6,14},... | collective-permute-start | bytes 393224 | tf_op jit(solution)/shard_map/ppermute | solution.py:421
  18.4 6.8 %collective-permute-start.1 = (bf16[2,128,256]{2,1,0:T(8,128)(2,1)S(1)}, bf16[2,128,256]{2,1,0:T(8,128)(2,1)S(1)}, u32[]{:S(2)}, u32[]{:S(2)}) collective-permute-start(bf16[2,128,256]{2,1,0:T(8,128)(2,1)S(1)} %get-tuple-element.49.refs_0_), channel_id=1, source_target_pairs={{0,4},{4,0},{8,12},{12,8},{1,5},{5,1},{9,13},{13,9},{2,6},{6,2},{1... | collective-permute-start | bytes 393224 | tf_op jit(solution)/shard_map/ppermute | solution.py:421
  26.0 6.8 %collective-permute-start.10 = (bf16[2,128,256]{2,1,0:T(8,128)(2,1)S(1)}, bf16[2,128,256]{2,1,0:T(8,128)(2,1)S(1)}, u32[]{:S(2)}, u32[]{:S(2)}) collective-permute-start(bf16[2,128,256]{2,1,0:T(8,128)(2,1)S(1)} %get-tuple-element.59.refs_0_), channel_id=1, source_target_pairs={{0,12},{4,8},{8,4},{12,0},{1,13},{5,9},{9,5},{13,1},{2,14},{6,10},... | collective-permute-start | bytes 393224 | tf_op jit(solution)/shard_map/ppermute | solution.py:421
  27.0 6.9 %collective-permute-start.9 = (bf16[2,128,256]{2,1,0:T(8,128)(2,1)S(1)}, bf16[2,128,256]{2,1,0:T(8,128)(2,1)S(1)}, u32[]{:S(2)}, u32[]{:S(2)}) collective-permute-start(bf16[2,128,256]{2,1,0:T(8,128)(2,1)S(1)} %get-tuple-element.59.refs_0_), channel_id=1, source_target_pairs={{0,8},{4,12},{8,0},{12,4},{1,9},{5,13},{9,1},{13,5},{2,10},{6,14},... | collective-permute-start | bytes 393224 | tf_op jit(solution)/shard_map/ppermute | solution.py:421
  29.0 5.0 %collective-permute-start.8 = (bf16[2,128,256]{2,1,0:T(8,128)(2,1)S(1)}, bf16[2,128,256]{2,1,0:T(8,128)(2,1)S(1)}, u32[]{:S(2)}, u32[]{:S(2)}) collective-permute-start(bf16[2,128,256]{2,1,0:T(8,128)(2,1)S(1)} %get-tuple-element.59.refs_0_), channel_id=1, source_target_pairs={{0,4},{4,0},{8,12},{12,8},{1,5},{5,1},{9,13},{13,9},{2,6},{6,2},{1... | collective-permute-start | bytes 393224 | tf_op jit(solution)/shard_map/ppermute | solution.py:421
  29.5 2.2 %collective-permute-start.4 = (bf16[2,128,128]{2,1,0:T(8,128)(2,1)S(1)}, bf16[2,128,128]{2,1,0:T(8,128)(2,1)S(1)}, u32[]{:S(2)}, u32[]{:S(2)}) collective-permute-start(bf16[2,128,128]{2,1,0:T(8,128)(2,1)S(1)} %get-tuple-element.53), channel_id=1, source_target_pairs={{0,16},{1,17},{2,18},{3,19},{4,20},{5,21},{6,22},{7,23},{8,24},{9,... | collective-permute-start | bytes 196616 | tf_op jit(solution)/shard_map/ppermute | solution.py:417
  34.7 3.0 %collective-permute-start.11 = (bf16[2,128,128]{2,1,0:T(8,128)(2,1)S(1)}, bf16[2,128,128]{2,1,0:T(8,128)(2,1)S(1)}, u32[]{:S(2)}, u32[]{:S(2)}) collective-permute-start(bf16[2,128,128]{2,1,0:T(8,128)(2,1)S(1)} %get-tuple-element.63), channel_id=1, source_target_pairs={{0,16},{1,17},{2,18},{3,19},{4,20},{5,21},{6,22},{7,23},{8,24},{9,... | collective-permute-start | bytes 196616 | tf_op jit(solution)/shard_map/ppermute | solution.py:417
  36.1 11.1 %collective-permute-start.5 = (bf16[512,256]{1,0:T(8,128)(2,1)S(1)}, bf16[512,256]{1,0:T(8,128)(2,1)S(1)}, u32[]{:S(2)}, u32[]{:S(2)}) collective-permute-start(bf16[512,256]{1,0:T(8,128)(2,1)S(1)} %shard_map.105), channel_id=1, source_target_pairs={{0,1},{1,2},{2,3},{3,0},{4,5},{5,6},{6,7},{7,4},{8,9},{9,10},{10,1... | collective-permute-start | bytes 786440 | tf_op jit(solution)/shard_map/ppermute | solution.py:621
  37.7 9.5 %copy-start = (bf16[2048,1024]{1,0:T(8,128)(2,1)S(1)}, bf16[2048,1024]{1,0:T(8,128)(2,1)}, u32[]{:S(2)}) copy-start(bf16[2048,1024]{1,0:T(8,128)(2,1)} %weights_ref.1) | copy-start | bytes 12582916
  38.4 14.3 %collective-permute-start.12 = (bf16[512,256]{1,0:T(8,128)(2,1)S(1)}, bf16[512,256]{1,0:T(8,128)(2,1)S(1)}, u32[]{:S(2)}, u32[]{:S(2)}) collective-permute-start(bf16[512,256]{1,0:T(8,128)(2,1)S(1)} %shard_map.107), channel_id=1, source_target_pairs={{0,1},{1,2},{2,3},{3,0},{4,5},{5,6},{6,7},{7,4},{8,9},{9,10},{10,1... | collective-permute-start | bytes 786440 | tf_op jit(solution)/shard_map/ppermute | solution.py:621
  47.6 11.1 %collective-permute-start.6 = (bf16[512,256]{1,0:T(8,128)(2,1)S(1)}, bf16[512,256]{1,0:T(8,128)(2,1)S(1)}, u32[]{:S(2)}, u32[]{:S(2)}) collective-permute-start(bf16[512,256]{1,0:T(8,128)(2,1)S(1)} %collective-permute-done.5), channel_id=1, source_target_pairs={{0,1},{1,2},{2,3},{3,0},{4,5},{5,6},{6,7},{7,4},{8,9},{9,10},{10,1... | collective-permute-start | bytes 786440 | tf_op jit(solution)/shard_map/ppermute | solution.py:621
  52.8 11.5 %collective-permute-start.13 = (bf16[512,256]{1,0:T(8,128)(2,1)S(1)}, bf16[512,256]{1,0:T(8,128)(2,1)S(1)}, u32[]{:S(2)}, u32[]{:S(2)}) collective-permute-start(bf16[512,256]{1,0:T(8,128)(2,1)S(1)} %collective-permute-done.12), channel_id=1, source_target_pairs={{0,1},{1,2},{2,3},{3,0},{4,5},{5,6},{6,7},{7,4},{8,9},{9,10},{10,1... | collective-permute-start | bytes 786440 | tf_op jit(solution)/shard_map/ppermute | solution.py:621
  58.7 11.2 %collective-permute-start.7 = (bf16[512,256]{1,0:T(8,128)(2,1)S(1)}, bf16[512,256]{1,0:T(8,128)(2,1)S(1)}, u32[]{:S(2)}, u32[]{:S(2)}) collective-permute-start(bf16[512,256]{1,0:T(8,128)(2,1)S(1)} %collective-permute-done.6), channel_id=1, source_target_pairs={{0,1},{1,2},{2,3},{3,0},{4,5},{5,6},{6,7},{7,4},{8,9},{9,10},{10,1... | collective-permute-start | bytes 786440 | tf_op jit(solution)/shard_map/ppermute | solution.py:621
  64.3 9.1 %collective-permute-start.14 = (bf16[512,256]{1,0:T(8,128)(2,1)S(1)}, bf16[512,256]{1,0:T(8,128)(2,1)S(1)}, u32[]{:S(2)}, u32[]{:S(2)}) collective-permute-start(bf16[512,256]{1,0:T(8,128)(2,1)S(1)} %collective-permute-done.13), channel_id=1, source_target_pairs={{0,1},{1,2},{2,3},{3,0},{4,5},{5,6},{6,7},{7,4},{8,9},{9,10},{10,1... | collective-permute-start | bytes 786440 | tf_op jit(solution)/shard_map/ppermute | solution.py:621

commit v13 on v11

--- a/solution.py
+++ b/solution.py
@@ -359,20 +359,28 @@
             ref[h] = states[h][:, :depth]
 
 
-def outputs_kernel(base, arrived_ref, before_ref, reach_ref, part_ref, gating_ref, normed_ref):
+def placed_kernel(base, before_ref, reach_ref, part_ref, through_ref, fixed_ref):
+    heads, depth, _ = before_ref.shape
+    for g in range(heads):
+        high, low = split(before_ref[g])
+        for c in range(through_ref.shape[1] // CHUNK):
+            here = rows_of(c)
+            reach = reach_ref[base + g, here]
+            both = mul(reach, high) + mul(reach, low)
+            through_ref[g, here] = both[:, :depth].astype(BF16)
+            fixed_ref[g, here] = part_ref[base + g, here] + both[:, depth:]
+
+
+def outputs_kernel(base, arrived_ref, through_ref, fixed_ref, gating_ref, normed_ref):
     heads, depth, _ = arrived_ref.shape
     for g in range(heads):
-        h = base + g
-        before = before_ref[g]
-        incoming = mul_split(before[:, :depth], arrived_ref[g].astype(F32)) + before[:, depth:]
-        high, low = split(incoming)
+        arrived = arrived_ref[g]
         for c in range(normed_ref.shape[0] // CHUNK):
             here = rows_of(c)
-            reach = reach_ref[h, here]
-            core = part_ref[h, here] + (mul(reach, high) + mul(reach, low))
+            core = fixed_ref[g, here] + mul(through_ref[g, here], arrived)
             scale = lax.rsqrt(jnp.sum(core * core, axis=-1, keepdims=True) / depth + EPSILON)
             normed_ref[here, g * depth : (g + 1) * depth] = (
-                core * scale * gating_ref[h, here]
+                core * scale * gating_ref[base + g, here]
             ).astype(BF16)
 
 
@@ -501,16 +509,33 @@
     )(place, *maps)
 
 
-def outputs_of(base, arrived, before, reads):
+def placed_of(base, before, reach, part):
+    heads, depth, _ = before.shape
+    length = reach.shape[1]
+    per_token = (heads, length, depth)
+    return pl.pallas_call(
+        functools.partial(placed_kernel, base),
+        out_shape=(
+            jax.ShapeDtypeStruct(per_token, BF16),
+            jax.ShapeDtypeStruct(per_token, F32),
+        ),
+        in_specs=[VMEM] * 3,
+        out_specs=[VMEM] * 2,
+        compiler_params=PARAMS,
+        cost_estimate=pl.CostEstimate(flops=2 * 10**9, bytes_accessed=2**20, transcendentals=0),
+    )(before, reach, part)
+
+
+def outputs_of(base, arrived, placed, gating):
     heads, depth, _ = arrived.shape
-    length = reads[0].shape[1]
+    length = gating.shape[1]
     return pl.pallas_call(
         functools.partial(outputs_kernel, base),
         out_shape=jax.ShapeDtypeStruct((length, heads * depth), BF16),
-        in_specs=[VMEM] * 5,
+        in_specs=[VMEM] * 4,
         out_specs=VMEM,
         compiler_params=PARAMS,
-    )(arrived, before, *reads)
+    )(arrived, *placed, gating)
 
 
 def last_projected(section, first, second, block, weights):
@@ -578,7 +603,9 @@
                 "hij,hjk->hik", trans[0], arrived.astype(F32), precision=lax.Precision.HIGHEST
             )
             arrived = from_behind((passed + state).astype(BF16), "chain", 1)
-        blocks.append(outputs_of(g * size, arrived, before, reads))
+        reach, part, gating = reads
+        placed = placed_of(g * size, before, reach, part)
+        blocks.append(outputs_of(g * size, arrived, placed, gating))
 
     ring = lax.axis_size("head")
     mine = lax.axis_index("head")
@@ -590,6 +617,8 @@
         owner = lax.rem(mine + ring - k, ring)
         last = k + 1 == ring
         following = blocks if last else [lax.ppermute(x, "head", around) for x in blocks]
+        if k == 0:
+            blocks[:-1] = after(following[0], *blocks[:-1])
         for g, block in enumerate(blocks):
             section = owner * GROUPS + g
             if last and g + 1 == GROUPS:

time: 71.5 us -> 74.5 us (1.042)
  local copies, waits for them, and re-layouts: 1.37 us -> 3.19 us
  starting transfers between devices: 18.6 us -> 19.9 us
  matrix products: 4.34 us -> 3.16 us
  waiting for transfers between devices: 28.5 us -> 29.5 us
    ppermute x6, waiting for transfers between devices: 0.28 us -> 2.54 us  [exchange(): lax.ppermute(own_map, 'leaf', pairs_at(k, leaves))]
    unnamed x18 -> x22, local copies, waits for them, and re-layouts: 0.05 us -> 1.87 us
    ppermute x6, starting transfers between devices: 3.46 us -> 5.05 us  [on_device(): lax.ppermute(x, 'head', around)]
    dot_general x7, matrix products: 4.34 us -> 3.16 us  [on_device(): term = jnp.dot(block, rows, preferred_element_type=F32)]
    ppermute x6, waiting for transfers between devices: 27.3 us -> 26.5 us  [on_device(): lax.ppermute(x, 'head', around)]
    pallas_call x0 -> x2, Pallas kernels: none -> 0.84 us  [placed_of(): pl.pallas_call(functools.partial(placed_kernel, base), out_shape=(jax.Sha...]
  transfers between devices with their start and end apart: 15 -> 15, of which waited for: 8 -> 9; matrix products, arithmetic and copies ran while one was open for 8% -> 6% of each run, Pallas kernels for 13% -> 13%
where the time goes in v13:
time: 74.5 us; the launch traced here: 74.3 us
  waiting for transfers between devices  29.5 us (40%)
  starting transfers between devices  19.9 us (27%)
  Pallas kernels  18.1 us (24%)
  local copies, waits for them, and re-layouts  3.19 us (4%)
  matrix products  3.16 us (4%)
    ppermute x6, waiting for transfers between devices, on_device(): lax.ppermute(x, 'head', around)  26.5 us
    ppermute x3, starting transfers between devices, from_behind(): lax.ppermute(value, axis, [(i, i + steps) for i in range(count - steps)])  7.77 us
    ppermute x6, starting transfers between devices, exchange(): lax.ppermute(own_map, 'leaf', pairs_at(k, leaves))  7.11 us
    pallas_call x1, Pallas kernels, reads_of(): pl.pallas_call(functools.partial(reads_kernel, base), out_shape=(jax.Shap...  5.45 us
    pallas_call x1, Pallas kernels, maps_of(): pl.pallas_call(functools.partial(maps_kernel, base), out_shape=(jax.Shape...  5.06 us
    ppermute x6, starting transfers between devices, on_device(): lax.ppermute(x, 'head', around)  5.05 us
    dot_general x7, matrix products, on_device(): term = jnp.dot(block, rows, preferred_element_type=F32)  3.16 us
    ppermute x6, waiting for transfers between devices, exchange(): lax.ppermute(own_map, 'leaf', pairs_at(k, leaves))  2.54 us
  transfers between devices with their start and end apart: 15, of which 9 were waited for; matrix products, arithmetic and copies ran while one was open for 6% of the time, Pallas kernels for 13%

profile of v13, /device:TPU:0, one launch (start us, length us, event | category | flops | bytes accessed | tf_op | source)
XLA Modules:
  0.0 74.3 jit_solution(16507183077286444367)
XLA Ops:
  0.0 1.4 %shard_map.101 = bf16[24,4,128]{2,1,0:T(4,128)(2,1)} custom-call(bf16[512,4,128]{2,1,0:T(4,128)(2,1)} %refs_0_.1, bf16[512,4,128]{2,1,0:T(4,128)(2,1)} %refs_1_.1, bf16[512,4,128]{2,1,0:T(4,128)(2,1)} %refs_2_.1), custom_call_target="tpu_custom_call" | custom-call | flops 1000000000 | bytes 65536 | tf_op jit(solution)/shard_map/pallas_call | solution.py:420
  1.4 4.8 %collective-permute-start = (bf16[24,4,128]{2,1,0:T(4,128)(2,1)}, bf16[24,4,128]{2,1,0:T(4,128)(2,1)S(1)}, u32[]{:S(2)}, u32[]{:S(2)}) collective-permute-start(bf16[24,4,128]{2,1,0:T(4,128)(2,1)} %shard_map.101), channel_id=1, source_target_pairs={{0,4},{4,8},{8,12},{12,16},{16,20},{20,24},{24,28},{1,5},{5,9},{9,... | collective-permute-start | bytes 73736 | tf_op jit(solution)/shard_map/ppermute | solution.py:403
  6.3 1.2 %copy_bitcast_fusion.2 = (bf16[4,512,128]{2,1,0:T(8,128)(2,1)S(1)}, bf16[4,512,128]{2,1,0:T(8,128)(2,1)S(1)}) fusion(bf16[512,4,128]{2,1,0:T(4,128)(2,1)S(1)} %copy-done.10, bf16[512,4,128]{2,1,0:T(4,128)(2,1)} %refs_1_.1), kind=kLoop, calls=%fused_computation.4 | loop fusion | bytes 2097152 | tf_op jit(solution)/shard_map/transpose | solution.py:575
  7.5 1.8 %shard_map.100 = (bf16[4,512,128]{2,1,0:T(8,128)(2,1)S(1)}, bf16[4,512,128]{2,1,0:T(8,128)(2,1)S(1)}, f32[2,4,16,128]{3,2,1,0:T(8,128)S(1)}) custom-call(bf16[4,512,128]{2,1,0:T(8,128)(2,1)S(1)} %get-tuple-element.68.key_ref, bf16[4,512,128]{2,1,0:T(8,128)(2,1)S(1)} %get-tuple-element.67.value_ref, f32[3,4,4,128]{3,2,1,0:T(4,128)S(1)} %copy-done.1), custom_call_target="tpu_custom_call" | custom-call | flops 3000000000 | bytes 4194304 | tf_op jit(solution)/shard_map/pallas_call | solution.py:434
  10.1 1.0 %copy-done.7 = bf16[4,512,128]{2,1,0:T(8,128)(2,1)S(1)} copy-done((bf16[4,512,128]{2,1,0:T(8,128)(2,1)S(1)}, bf16[4,512,128]{2,1,0:T(8,128)(2,1)}, u32[]{:S(2)}) %copy-start.7) | copy-done | bytes 524312
  11.2 5.1 %shard_map.102 = (bf16[4,512,128]{2,1,0:T(8,128)(2,1)S(1)}, f32[4,512,256]{2,1,0:T(8,128)S(1)}, f32[4,3,128,256]{3,2,1,0:T(8,128)S(1)}, bf16[2,128,256]{2,1,0:T(8,128)(2,1)S(1)}, bf16[2,128,256]{2,1,0:T(8,128)(2,1)S(1)}) custom-call(s32[8]{0:T(128)S(1)} %copy-done.4, bf16[4,512,128]{2,1,0:T(8,128)(2,1)S(1)} %get-tuple-element.36.unit_in_ref, ...), custom_call_target="tpu_custom_call" | custom-call | flops 5000000000 | bytes 4194304 | tf_op jit(solution)/shard_map/pallas_call | solution.py:450
  16.3 1.2 %collective-permute-start.3 = (bf16[2,128,256]{2,1,0:T(8,128)(2,1)S(1)}, bf16[2,128,256]{2,1,0:T(8,128)(2,1)S(1)}, u32[]{:S(2)}, u32[]{:S(2)}) collective-permute-start(bf16[2,128,256]{2,1,0:T(8,128)(2,1)S(1)} %get-tuple-element.47.refs_0_), channel_id=1, source_target_pairs={{0,12},{4,8},{8,4},{12,0},{1,13},{5,9},{9,5},{13,1},{2,14},{6,10},... | collective-permute-start | bytes 393224 | tf_op jit(solution)/shard_map/ppermute | solution.py:407
  17.5 1.8 %collective-permute-start.2 = (bf16[2,128,256]{2,1,0:T(8,128)(2,1)S(1)}, bf16[2,128,256]{2,1,0:T(8,128)(2,1)S(1)}, u32[]{:S(2)}, u32[]{:S(2)}) collective-permute-start(bf16[2,128,256]{2,1,0:T(8,128)(2,1)S(1)} %get-tuple-element.47.refs_0_), channel_id=1, source_target_pairs={{0,8},{4,12},{8,0},{12,4},{1,9},{5,13},{9,1},{13,5},{2,10},{6,14},... | collective-permute-start | bytes 393224 | tf_op jit(solution)/shard_map/ppermute | solution.py:407
  20.0 5.4 %shard_map.103 = (bf16[4,512,128]{2,1,0:T(8,128)(2,1)S(1)}, f32[4,512,128]{2,1,0:T(8,128)S(1)}, f32[4,512,128]{2,1,0:T(8,128)S(1)}) custom-call(s32[8]{0:T(128)S(1)} %copy-done.4, bf16[4,512,128]{2,1,0:T(8,128)(2,1)S(1)} %bitcast.20, bf16[4,512,128]{2,1,0:T(8,128)(2,1)S(1)} %bitcast.21, f32[1,128]{1,0:T(1,128)S(1)} %bitcast.22, ...), custom_call_target="tpu_custom_call" | custom-call | flops 3000000000 | bytes 4194304 | tf_op jit(solution)/shard_map/pallas_call | solution.py:476
  26.2 1.4 %collective-permute-start.4 = (bf16[2,128,128]{2,1,0:T(8,128)(2,1)S(1)}, bf16[2,128,128]{2,1,0:T(8,128)(2,1)S(1)}, u32[]{:S(2)}, u32[]{:S(2)}) collective-permute-start(bf16[2,128,128]{2,1,0:T(8,128)(2,1)S(1)} %get-tuple-element.51), channel_id=1, source_target_pairs={{0,16},{1,17},{2,18},{3,19},{4,20},{5,21},{6,22},{7,23},{8,24},{9,... | collective-permute-start | bytes 196616 | tf_op jit(solution)/shard_map/ppermute | solution.py:403
  27.6 1.1 %collective-permute-start.10 = (bf16[2,128,256]{2,1,0:T(8,128)(2,1)S(1)}, bf16[2,128,256]{2,1,0:T(8,128)(2,1)S(1)}, u32[]{:S(2)}, u32[]{:S(2)}) collective-permute-start(bf16[2,128,256]{2,1,0:T(8,128)(2,1)S(1)} %get-tuple-element.59.refs_0_), channel_id=1, source_target_pairs={{0,12},{4,8},{8,4},{12,0},{1,13},{5,9},{9,5},{13,1},{2,14},{6,10},... | collective-permute-start | bytes 393224 | tf_op jit(solution)/shard_map/ppermute | solution.py:407
  28.7 1.8 %collective-permute-start.9 = (bf16[2,128,256]{2,1,0:T(8,128)(2,1)S(1)}, bf16[2,128,256]{2,1,0:T(8,128)(2,1)S(1)}, u32[]{:S(2)}, u32[]{:S(2)}) collective-permute-start(bf16[2,128,256]{2,1,0:T(8,128)(2,1)S(1)} %get-tuple-element.59.refs_0_), channel_id=1, source_target_pairs={{0,8},{4,12},{8,0},{12,4},{1,9},{5,13},{9,1},{13,5},{2,10},{6,14},... | collective-permute-start | bytes 393224 | tf_op jit(solution)/shard_map/ppermute | solution.py:407
  32.0 1.6 %collective-permute-start.5 = (bf16[512,256]{1,0:T(8,128)(2,1)S(1)}, bf16[512,256]{1,0:T(8,128)(2,1)S(1)}, u32[]{:S(2)}, u32[]{:S(2)}) collective-permute-start(bf16[512,256]{1,0:T(8,128)(2,1)S(1)} %shard_map.106), channel_id=1, source_target_pairs={{0,1},{1,2},{2,3},{3,0},{4,5},{5,6},{6,7},{7,4},{8,9},{9,10},{10,1... | collective-permute-start | bytes 786440 | tf_op jit(solution)/shard_map/ppermute | solution.py:619
  33.6 1.2 %collective-permute-done.10.refs_3_ = bf16[2,128,256]{2,1,0:T(8,128)(2,1)S(1)} collective-permute-done((bf16[2,128,256]{2,1,0:T(8,128)(2,1)S(1)}, bf16[2,128,256]{2,1,0:T(8,128)(2,1)S(1)}, u32[]{:S(2)}, u32[]{:S(2)}) %collective-permute-start.10) | collective-permute-done | bytes 131104 | tf_op jit(solution)/shard_map/ppermute | solution.py:407
  34.8 1.3 %collective-permute-done.9.refs_2_ = bf16[2,128,256]{2,1,0:T(8,128)(2,1)S(1)} collective-permute-done((bf16[2,128,256]{2,1,0:T(8,128)(2,1)S(1)}, bf16[2,128,256]{2,1,0:T(8,128)(2,1)S(1)}, u32[]{:S(2)}, u32[]{:S(2)}) %collective-permute-start.9) | collective-permute-done | bytes 131104 | tf_op jit(solution)/shard_map/ppermute | solution.py:407
  36.9 1.5 %collective-permute-start.11 = (bf16[2,128,128]{2,1,0:T(8,128)(2,1)S(1)}, bf16[2,128,128]{2,1,0:T(8,128)(2,1)S(1)}, u32[]{:S(2)}, u32[]{:S(2)}) collective-permute-start(bf16[2,128,128]{2,1,0:T(8,128)(2,1)S(1)} %get-tuple-element.63), channel_id=1, source_target_pairs={{0,16},{1,17},{2,18},{3,19},{4,20},{5,21},{6,22},{7,23},{8,24},{9,... | collective-permute-start | bytes 196616 | tf_op jit(solution)/shard_map/ppermute | solution.py:403
  39.7 1.8 %collective-permute-start.12 = (bf16[512,256]{1,0:T(8,128)(2,1)S(1)}, bf16[512,256]{1,0:T(8,128)(2,1)S(1)}, u32[]{:S(2)}, u32[]{:S(2)}) collective-permute-start(bf16[512,256]{1,0:T(8,128)(2,1)S(1)} %shard_map.109), channel_id=1, source_target_pairs={{0,1},{1,2},{2,3},{3,0},{4,5},{5,6},{6,7},{7,4},{8,9},{9,10},{10,1... | collective-permute-start | bytes 786440 | tf_op jit(solution)/shard_map/ppermute | solution.py:619
  42.4 1.6 %collective-permute-start.6 = (bf16[512,256]{1,0:T(8,128)(2,1)S(1)}, bf16[512,256]{1,0:T(8,128)(2,1)S(1)}, u32[]{:S(2)}, u32[]{:S(2)}) collective-permute-start(bf16[512,256]{1,0:T(8,128)(2,1)S(1)} %collective-permute-done.5), channel_id=1, source_target_pairs={{0,1},{1,2},{2,3},{3,0},{4,5},{5,6},{6,7},{7,4},{8,9},{9,10},{10,1... | collective-permute-start | bytes 786440 | tf_op jit(solution)/shard_map/ppermute | solution.py:619
  44.5 6.4 %collective-permute-done.12 = bf16[512,256]{1,0:T(8,128)(2,1)S(1)} collective-permute-done((bf16[512,256]{1,0:T(8,128)(2,1)S(1)}, bf16[512,256]{1,0:T(8,128)(2,1)S(1)}, u32[]{:S(2)}, u32[]{:S(2)}) %collective-permute-start.12) | collective-permute-done | bytes 262176 | tf_op jit(solution)/shard_map/ppermute | solution.py:619
  51.3 5.2 %collective-permute-done.6 = bf16[512,256]{1,0:T(8,128)(2,1)S(1)} collective-permute-done((bf16[512,256]{1,0:T(8,128)(2,1)S(1)}, bf16[512,256]{1,0:T(8,128)(2,1)S(1)}, u32[]{:S(2)}, u32[]{:S(2)}) %collective-permute-start.6) | collective-permute-done | bytes 262176 | tf_op jit(solution)/shard_map/ppermute | solution.py:619
  56.9 5.2 %collective-permute-done.13 = bf16[512,256]{1,0:T(8,128)(2,1)S(1)} collective-permute-done((bf16[512,256]{1,0:T(8,128)(2,1)S(1)}, bf16[512,256]{1,0:T(8,128)(2,1)S(1)}, u32[]{:S(2)}, u32[]{:S(2)}) %collective-permute-start.13) | collective-permute-done | bytes 262176 | tf_op jit(solution)/shard_map/ppermute | solution.py:619
  62.6 5.1 %collective-permute-done.7 = bf16[512,256]{1,0:T(8,128)(2,1)S(1)} collective-permute-done((bf16[512,256]{1,0:T(8,128)(2,1)S(1)}, bf16[512,256]{1,0:T(8,128)(2,1)S(1)}, u32[]{:S(2)}, u32[]{:S(2)}) %collective-permute-start.7) | collective-permute-done | bytes 262176 | tf_op jit(solution)/shard_map/ppermute | solution.py:619
  68.2 4.6 %collective-permute-done.14.block_ref = bf16[512,256]{1,0:T(8,128)(2,1)S(1)} collective-permute-done((bf16[512,256]{1,0:T(8,128)(2,1)S(1)}, bf16[512,256]{1,0:T(8,128)(2,1)S(1)}, u32[]{:S(2)}, u32[]{:S(2)}) %collective-permute-start.14) | collective-permute-done | bytes 262176 | tf_op jit(solution)/shard_map/ppermute | solution.py:619
  72.8 1.3 %shard_map.110 = bf16[512,1024]{1,0:T(8,128)(2,1)} custom-call(s32[1]{0:T(128)} %bitcast.section, f32[512,1024]{1,0:T(8,128)S(1)} %add_add_fusion.1.first_ref, f32[512,1024]{1,0:T(8,128)S(1)} %add_add_fusion.second_ref, bf16[512,256]{1,0:T(8,128)(2,1)S(1)} %collective-permute-done.14.block_ref, bf16[2048,1024]{1,0:T(8,128)(2,1)S(1)} %copy-done), custom_call_target="tpu_custom_call" | custom-call | tf_op jit(solution)/shard_map/pallas_call | solution.py:543
  (49 shorter events, 8.9 us)
Async XLA Ops:
  0.0 6.3 %copy-start.10 = (bf16[512,4,128]{2,1,0:T(4,128)(2,1)S(1)}, bf16[512,4,128]{2,1,0:T(4,128)(2,1)}, u32[]{:S(2)}) copy-start(bf16[512,4,128]{2,1,0:T(4,128)(2,1)} %refs_2_.1) | copy-start | bytes 1572868
  0.0 7.5 %copy-start.1 = (f32[3,4,4,128]{3,2,1,0:T(4,128)S(1)}, f32[3,4,4,128]{3,2,1,0:T(4,128)}, u32[]{:S(2)}) copy-start(f32[3,4,4,128]{3,2,1,0:T(4,128)} %taps_ref.5) | copy-start | bytes 73732
  1.4 8.7 %collective-permute-start = (bf16[24,4,128]{2,1,0:T(4,128)(2,1)}, bf16[24,4,128]{2,1,0:T(4,128)(2,1)S(1)}, u32[]{:S(2)}, u32[]{:S(2)}) collective-permute-start(bf16[24,4,128]{2,1,0:T(4,128)(2,1)} %shard_map.101), channel_id=1, source_target_pairs={{0,4},{4,8},{8,12},{12,16},{16,20},{20,24},{24,28},{1,5},{5,9},{9,... | collective-permute-start | bytes 73736 | tf_op jit(solution)/shard_map/ppermute | solution.py:403
  7.5 2.6 %copy-start.2 = (f32[4,512]{1,0:T(4,128)S(1)}, f32[4,512]{1,0:T(4,128)}, u32[]{:S(2)}) copy-start(f32[4,512]{1,0:T(4,128)} %decay_ref.3) | copy-start | bytes 24580
  7.5 2.6 %copy-start.3 = (f32[4,512]{1,0:T(4,128)S(1)}, f32[4,512]{1,0:T(4,128)}, u32[]{:S(2)}) copy-start(f32[4,512]{1,0:T(4,128)} %strength_ref.3) | copy-start | bytes 24580
  7.5 2.6 %copy-start.4 = (s32[8]{0:T(128)S(1)}, s32[8]{0:T(128)}, u32[]{:S(2)}) copy-start(s32[8]{0:T(128)} %resets.3) | copy-start | bytes 100
  11.2 8.6 %copy-start.8 = (bf16[512,4,128]{2,1,0:T(4,128)(2,1)S(1)}, bf16[512,4,128]{2,1,0:T(4,128)(2,1)}, u32[]{:S(2)}) copy-start(bf16[512,4,128]{2,1,0:T(4,128)(2,1)} %refs_0_.1) | copy-start | bytes 1572868
  11.2 8.7 %copy-start.9 = (bf16[512,4,128]{2,1,0:T(4,128)(2,1)S(1)}, bf16[512,4,128]{2,1,0:T(4,128)(2,1)}, u32[]{:S(2)}) copy-start(bf16[512,4,128]{2,1,0:T(4,128)(2,1)} %param.13) | copy-start | bytes 1572868
  16.3 3.7 %copy-start.5 = (f32[128]{0:T(128)S(1)}, f32[128]{0:T(128)}, u32[]{:S(2)}) copy-start(f32[128]{0:T(128)} %param.18) | copy-start | bytes 1540
  16.3 9.2 %collective-permute-start.3 = (bf16[2,128,256]{2,1,0:T(8,128)(2,1)S(1)}, bf16[2,128,256]{2,1,0:T(8,128)(2,1)S(1)}, u32[]{:S(2)}, u32[]{:S(2)}) collective-permute-start(bf16[2,128,256]{2,1,0:T(8,128)(2,1)S(1)} %get-tuple-element.47.refs_0_), channel_id=1, source_target_pairs={{0,12},{4,8},{8,4},{12,0},{1,13},{5,9},{9,5},{13,1},{2,14},{6,10},... | collective-permute-start | bytes 393224 | tf_op jit(solution)/shard_map/ppermute | solution.py:407
  17.5 8.0 %collective-permute-start.2 = (bf16[2,128,256]{2,1,0:T(8,128)(2,1)S(1)}, bf16[2,128,256]{2,1,0:T(8,128)(2,1)S(1)}, u32[]{:S(2)}, u32[]{:S(2)}) collective-permute-start(bf16[2,128,256]{2,1,0:T(8,128)(2,1)S(1)} %get-tuple-element.47.refs_0_), channel_id=1, source_target_pairs={{0,8},{4,12},{8,0},{12,4},{1,9},{5,13},{9,1},{13,5},{2,10},{6,14},... | collective-permute-start | bytes 393224 | tf_op jit(solution)/shard_map/ppermute | solution.py:407
  19.3 6.2 %collective-permute-start.1 = (bf16[2,128,256]{2,1,0:T(8,128)(2,1)S(1)}, bf16[2,128,256]{2,1,0:T(8,128)(2,1)S(1)}, u32[]{:S(2)}, u32[]{:S(2)}) collective-permute-start(bf16[2,128,256]{2,1,0:T(8,128)(2,1)S(1)} %get-tuple-element.47.refs_0_), channel_id=1, source_target_pairs={{0,4},{4,0},{8,12},{12,8},{1,5},{5,1},{9,13},{13,9},{2,6},{6,2},{1... | collective-permute-start | bytes 393224 | tf_op jit(solution)/shard_map/ppermute | solution.py:407
  26.2 5.4 %collective-permute-start.4 = (bf16[2,128,128]{2,1,0:T(8,128)(2,1)S(1)}, bf16[2,128,128]{2,1,0:T(8,128)(2,1)S(1)}, u32[]{:S(2)}, u32[]{:S(2)}) collective-permute-start(bf16[2,128,128]{2,1,0:T(8,128)(2,1)S(1)} %get-tuple-element.51), channel_id=1, source_target_pairs={{0,16},{1,17},{2,18},{3,19},{4,20},{5,21},{6,22},{7,23},{8,24},{9,... | collective-permute-start | bytes 196616 | tf_op jit(solution)/shard_map/ppermute | solution.py:403
  27.6 7.2 %collective-permute-start.10 = (bf16[2,128,256]{2,1,0:T(8,128)(2,1)S(1)}, bf16[2,128,256]{2,1,0:T(8,128)(2,1)S(1)}, u32[]{:S(2)}, u32[]{:S(2)}) collective-permute-start(bf16[2,128,256]{2,1,0:T(8,128)(2,1)S(1)} %get-tuple-element.59.refs_0_), channel_id=1, source_target_pairs={{0,12},{4,8},{8,4},{12,0},{1,13},{5,9},{9,5},{13,1},{2,14},{6,10},... | collective-permute-start | bytes 393224 | tf_op jit(solution)/shard_map/ppermute | solution.py:407
  28.7 7.4 %collective-permute-start.9 = (bf16[2,128,256]{2,1,0:T(8,128)(2,1)S(1)}, bf16[2,128,256]{2,1,0:T(8,128)(2,1)S(1)}, u32[]{:S(2)}, u32[]{:S(2)}) collective-permute-start(bf16[2,128,256]{2,1,0:T(8,128)(2,1)S(1)} %get-tuple-element.59.refs_0_), channel_id=1, source_target_pairs={{0,8},{4,12},{8,0},{12,4},{1,9},{5,13},{9,1},{13,5},{2,10},{6,14},... | collective-permute-start | bytes 393224 | tf_op jit(solution)/shard_map/ppermute | solution.py:407
  30.6 5.6 %collective-permute-start.8 = (bf16[2,128,256]{2,1,0:T(8,128)(2,1)S(1)}, bf16[2,128,256]{2,1,0:T(8,128)(2,1)S(1)}, u32[]{:S(2)}, u32[]{:S(2)}) collective-permute-start(bf16[2,128,256]{2,1,0:T(8,128)(2,1)S(1)} %get-tuple-element.59.refs_0_), channel_id=1, source_target_pairs={{0,4},{4,0},{8,12},{12,8},{1,5},{5,1},{9,13},{13,9},{2,6},{6,2},{1... | collective-permute-start | bytes 393224 | tf_op jit(solution)/shard_map/ppermute | solution.py:407
  32.0 10.0 %collective-permute-start.5 = (bf16[512,256]{1,0:T(8,128)(2,1)S(1)}, bf16[512,256]{1,0:T(8,128)(2,1)S(1)}, u32[]{:S(2)}, u32[]{:S(2)}) collective-permute-start(bf16[512,256]{1,0:T(8,128)(2,1)S(1)} %shard_map.106), channel_id=1, source_target_pairs={{0,1},{1,2},{2,3},{3,0},{4,5},{5,6},{6,7},{7,4},{8,9},{9,10},{10,1... | collective-permute-start | bytes 786440 | tf_op jit(solution)/shard_map/ppermute | solution.py:619
  36.9 2.4 %collective-permute-start.11 = (bf16[2,128,128]{2,1,0:T(8,128)(2,1)S(1)}, bf16[2,128,128]{2,1,0:T(8,128)(2,1)S(1)}, u32[]{:S(2)}, u32[]{:S(2)}) collective-permute-start(bf16[2,128,128]{2,1,0:T(8,128)(2,1)S(1)} %get-tuple-element.63), channel_id=1, source_target_pairs={{0,16},{1,17},{2,18},{3,19},{4,20},{5,21},{6,22},{7,23},{8,24},{9,... | collective-permute-start | bytes 196616 | tf_op jit(solution)/shard_map/ppermute | solution.py:403
  38.5 3.1 %copy-start = (bf16[2048,1024]{1,0:T(8,128)(2,1)S(1)}, bf16[2048,1024]{1,0:T(8,128)(2,1)}, u32[]{:S(2)}) copy-start(bf16[2048,1024]{1,0:T(8,128)(2,1)} %weights_ref.1) | copy-start | bytes 12582916
  39.7 11.1 %collective-permute-start.12 = (bf16[512,256]{1,0:T(8,128)(2,1)S(1)}, bf16[512,256]{1,0:T(8,128)(2,1)S(1)}, u32[]{:S(2)}, u32[]{:S(2)}) collective-permute-start(bf16[512,256]{1,0:T(8,128)(2,1)S(1)} %shard_map.109), channel_id=1, source_target_pairs={{0,1},{1,2},{2,3},{3,0},{4,5},{5,6},{6,7},{7,4},{8,9},{9,10},{10,1... | collective-permute-start | bytes 786440 | tf_op jit(solution)/shard_map/ppermute | solution.py:619
  42.4 14.1 %collective-permute-start.6 = (bf16[512,256]{1,0:T(8,128)(2,1)S(1)}, bf16[512,256]{1,0:T(8,128)(2,1)S(1)}, u32[]{:S(2)}, u32[]{:S(2)}) collective-permute-start(bf16[512,256]{1,0:T(8,128)(2,1)S(1)} %collective-permute-done.5), channel_id=1, source_target_pairs={{0,1},{1,2},{2,3},{3,0},{4,5},{5,6},{6,7},{7,4},{8,9},{9,10},{10,1... | collective-permute-start | bytes 786440 | tf_op jit(solution)/shard_map/ppermute | solution.py:619
  50.9 11.2 %collective-permute-start.13 = (bf16[512,256]{1,0:T(8,128)(2,1)S(1)}, bf16[512,256]{1,0:T(8,128)(2,1)S(1)}, u32[]{:S(2)}, u32[]{:S(2)}) collective-permute-start(bf16[512,256]{1,0:T(8,128)(2,1)S(1)} %collective-permute-done.12), channel_id=1, source_target_pairs={{0,1},{1,2},{2,3},{3,0},{4,5},{5,6},{6,7},{7,4},{8,9},{9,10},{10,1... | collective-permute-start | bytes 786440 | tf_op jit(solution)/shard_map/ppermute | solution.py:619
  56.5 11.2 %collective-permute-start.7 = (bf16[512,256]{1,0:T(8,128)(2,1)S(1)}, bf16[512,256]{1,0:T(8,128)(2,1)S(1)}, u32[]{:S(2)}, u32[]{:S(2)}) collective-permute-start(bf16[512,256]{1,0:T(8,128)(2,1)S(1)} %collective-permute-done.6), channel_id=1, source_target_pairs={{0,1},{1,2},{2,3},{3,0},{4,5},{5,6},{6,7},{7,4},{8,9},{9,10},{10,1... | collective-permute-start | bytes 786440 | tf_op jit(solution)/shard_map/ppermute | solution.py:619
  62.1 10.7 %collective-permute-start.14 = (bf16[512,256]{1,0:T(8,128)(2,1)S(1)}, bf16[512,256]{1,0:T(8,128)(2,1)S(1)}, u32[]{:S(2)}, u32[]{:S(2)}) collective-permute-start(bf16[512,256]{1,0:T(8,128)(2,1)S(1)} %collective-permute-done.13), channel_id=1, source_target_pairs={{0,1},{1,2},{2,3},{3,0},{4,5},{5,6},{6,7},{7,4},{8,9},{9,10},{10,1... | collective-permute-start | bytes 786440 | tf_op jit(solution)/shard_map/ppermute | solution.py:619
  (2 other events, 1.8 us)

commit v14 on v13

--- a/solution.py
+++ b/solution.py
@@ -403,8 +403,11 @@
     return lax.ppermute(value, axis, [(i, i + steps) for i in range(count - steps)])
 
 
-def exchange(own_map, leaves):
-    received = [lax.ppermute(own_map, "leaf", pairs_at(k, leaves)) for k in range(1, leaves)]
+def exchange(own_map, later, leaves):
+    received = [
+        lax.ppermute(later if k == 1 else own_map, "leaf", pairs_at(k, leaves))
+        for k in range(1, leaves)
+    ]
     return [own_map] + received
 
 
@@ -590,13 +593,14 @@
     )
     size = heads // GROUPS
     blocks = []
-    exchanged = [exchange(own_maps[0], leaves)]
+    exchanged = [exchange(own_maps[0], own_maps[0], leaves)]
     for g in range(GROUPS):
         earlier = blocks[-1] if blocks else reads[0]
         maps = after(earlier, *exchanged[g])
         before, state, *trans = join(place, maps, links)
         if g + 1 < GROUPS:
-            exchanged.append(exchange(*after(state, own_maps[g + 1]), leaves))
+            own_map = own_maps[g + 1]
+            exchanged.append(exchange(*after(earlier, own_map), *after(state, own_map), leaves))
         arrived = from_behind(state.astype(BF16), "chain", 1)
         for _ in range(links - 1):
             passed = jnp.einsum(

time: 74.5 us -> 73.7 us (0.989)
  starting transfers between devices: 19.9 us -> 18.5 us
    ppermute x6, waiting for transfers between devices: 26.5 us -> 27.6 us  [on_device(): lax.ppermute(x, 'head', around)]
    ppermute x6, starting transfers between devices: 5.05 us -> 3.95 us  [on_device(): lax.ppermute(x, 'head', around)]
  transfers between devices with their start and end apart: 15 -> 15, of which waited for: 9 -> 8; matrix products, arithmetic and copies ran while one was open for 6% -> 6% of each run, Pallas kernels for 13% -> 14%
where the time goes in v14:
time: 73.7 us; the launch traced here: 73.5 us
  waiting for transfers between devices  30.1 us (41%)
  starting transfers between devices  18.5 us (25%)
  Pallas kernels  18.1 us (25%)
  local copies, waits for them, and re-layouts  3.19 us (4%)
  matrix products  3.16 us (4%)
    ppermute x6, waiting for transfers between devices, on_device(): lax.ppermute(x, 'head', around)  27.6 us
    ppermute x3, starting transfers between devices, from_behind(): lax.ppermute(value, axis, [(i, i + steps) for i in range(count - steps)])  7.43 us
    ppermute x6, starting transfers between devices, exchange(): lax.ppermute(later if k == 1 else own_map, 'leaf', pairs_at(k, leaves))  7.17 us
    pallas_call x1, Pallas kernels, reads_of(): pl.pallas_call(functools.partial(reads_kernel, base), out_shape=(jax.Shap...  5.44 us
    pallas_call x1, Pallas kernels, maps_of(): pl.pallas_call(functools.partial(maps_kernel, base), out_shape=(jax.Shape...  5.06 us
    ppermute x6, starting transfers between devices, on_device(): lax.ppermute(x, 'head', around)  3.95 us
    dot_general x7, matrix products, on_device(): term = jnp.dot(block, rows, preferred_element_type=F32)  3.16 us
    ppermute x6, waiting for transfers between devices, exchange(): lax.ppermute(later if k == 1 else own_map, 'leaf', pairs_at(k, leaves))  1.99 us
  transfers between devices with their start and end apart: 15, of which 8 were waited for; matrix products, arithmetic and copies ran while one was open for 6% of the time, Pallas kernels for 14%

profile of v14, /device:TPU:0, one launch (start us, length us, event | category | flops | bytes accessed | tf_op | source)
XLA Modules:
  0.0 73.5 jit_solution(6900593333203008043)
XLA Ops:
  0.0 1.4 %shard_map.101 = bf16[24,4,128]{2,1,0:T(4,128)(2,1)} custom-call(bf16[512,4,128]{2,1,0:T(4,128)(2,1)} %refs_0_.1, bf16[512,4,128]{2,1,0:T(4,128)(2,1)} %refs_1_.1, bf16[512,4,128]{2,1,0:T(4,128)(2,1)} %refs_2_.1), custom_call_target="tpu_custom_call" | custom-call | flops 1000000000 | bytes 65536 | tf_op jit(solution)/shard_map/pallas_call | solution.py:423
  1.4 4.8 %collective-permute-start = (bf16[24,4,128]{2,1,0:T(4,128)(2,1)}, bf16[24,4,128]{2,1,0:T(4,128)(2,1)S(1)}, u32[]{:S(2)}, u32[]{:S(2)}) collective-permute-start(bf16[24,4,128]{2,1,0:T(4,128)(2,1)} %shard_map.101), channel_id=1, source_target_pairs={{0,4},{4,8},{8,12},{12,16},{16,20},{20,24},{24,28},{1,5},{5,9},{9,... | collective-permute-start | bytes 73736 | tf_op jit(solution)/shard_map/ppermute | solution.py:403
  6.3 1.2 %copy_bitcast_fusion.2 = (bf16[4,512,128]{2,1,0:T(8,128)(2,1)S(1)}, bf16[4,512,128]{2,1,0:T(8,128)(2,1)S(1)}) fusion(bf16[512,4,128]{2,1,0:T(4,128)(2,1)S(1)} %copy-done.10, bf16[512,4,128]{2,1,0:T(4,128)(2,1)} %refs_1_.1), kind=kLoop, calls=%fused_computation.4 | loop fusion | bytes 2097152 | tf_op jit(solution)/shard_map/transpose | solution.py:578
  7.5 1.8 %shard_map.100 = (bf16[4,512,128]{2,1,0:T(8,128)(2,1)S(1)}, bf16[4,512,128]{2,1,0:T(8,128)(2,1)S(1)}, f32[2,4,16,128]{3,2,1,0:T(8,128)S(1)}) custom-call(bf16[4,512,128]{2,1,0:T(8,128)(2,1)S(1)} %get-tuple-element.70.key_ref, bf16[4,512,128]{2,1,0:T(8,128)(2,1)S(1)} %get-tuple-element.69.value_ref, f32[3,4,4,128]{3,2,1,0:T(4,128)S(1)} %copy-done.1), custom_call_target="tpu_custom_call" | custom-call | flops 3000000000 | bytes 4194304 | tf_op jit(solution)/shard_map/pallas_call | solution.py:437
  9.3 0.8 %copy-done.6 = bf16[4,512,128]{2,1,0:T(8,128)(2,1)} copy-done((bf16[4,512,128]{2,1,0:T(8,128)(2,1)}, bf16[4,512,128]{2,1,0:T(8,128)(2,1)S(1)}, u32[]{:S(2)}) %copy-start.6) | copy-done | bytes 524312
  10.1 1.0 %copy-done.7 = bf16[4,512,128]{2,1,0:T(8,128)(2,1)S(1)} copy-done((bf16[4,512,128]{2,1,0:T(8,128)(2,1)S(1)}, bf16[4,512,128]{2,1,0:T(8,128)(2,1)}, u32[]{:S(2)}) %copy-start.7) | copy-done | bytes 524312
  11.2 5.1 %shard_map.102 = (bf16[4,512,128]{2,1,0:T(8,128)(2,1)S(1)}, f32[4,512,256]{2,1,0:T(8,128)S(1)}, f32[4,3,128,256]{3,2,1,0:T(8,128)S(1)}, bf16[2,128,256]{2,1,0:T(8,128)(2,1)S(1)}, bf16[2,128,256]{2,1,0:T(8,128)(2,1)S(1)}) custom-call(s32[8]{0:T(128)S(1)} %copy-done.4, bf16[4,512,128]{2,1,0:T(8,128)(2,1)S(1)} %get-tuple-element.37.unit_in_ref, ...), custom_call_target="tpu_custom_call" | custom-call | flops 5000000000 | bytes 4194304 | tf_op jit(solution)/shard_map/pallas_call | solution.py:453
  16.3 1.2 %collective-permute-start.3 = (bf16[2,128,256]{2,1,0:T(8,128)(2,1)S(1)}, bf16[2,128,256]{2,1,0:T(8,128)(2,1)S(1)}, u32[]{:S(2)}, u32[]{:S(2)}) collective-permute-start(bf16[2,128,256]{2,1,0:T(8,128)(2,1)S(1)} %get-tuple-element.48.refs_0_), channel_id=1, source_target_pairs={{0,12},{4,8},{8,4},{12,0},{1,13},{5,9},{9,5},{13,1},{2,14},{6,10},... | collective-permute-start | bytes 393224 | tf_op jit(solution)/shard_map/ppermute | solution.py:408
  17.5 1.8 %collective-permute-start.2 = (bf16[2,128,256]{2,1,0:T(8,128)(2,1)S(1)}, bf16[2,128,256]{2,1,0:T(8,128)(2,1)S(1)}, u32[]{:S(2)}, u32[]{:S(2)}) collective-permute-start(bf16[2,128,256]{2,1,0:T(8,128)(2,1)S(1)} %get-tuple-element.48.refs_0_), channel_id=1, source_target_pairs={{0,8},{4,12},{8,0},{12,4},{1,9},{5,13},{9,1},{13,5},{2,10},{6,14},... | collective-permute-start | bytes 393224 | tf_op jit(solution)/shard_map/ppermute | solution.py:408
  20.0 5.4 %shard_map.103 = (bf16[4,512,128]{2,1,0:T(8,128)(2,1)S(1)}, f32[4,512,128]{2,1,0:T(8,128)S(1)}, f32[4,512,128]{2,1,0:T(8,128)S(1)}) custom-call(s32[8]{0:T(128)S(1)} %copy-done.4, bf16[4,512,128]{2,1,0:T(8,128)(2,1)S(1)} %bitcast.20, bf16[4,512,128]{2,1,0:T(8,128)(2,1)S(1)} %bitcast.21, f32[1,128]{1,0:T(1,128)S(1)} %bitcast.22, ...), custom_call_target="tpu_custom_call" | custom-call | flops 3000000000 | bytes 4194304 | tf_op jit(solution)/shard_map/pallas_call | solution.py:479
  25.4 1.2 %collective-permute-start.10 = (bf16[2,128,256]{2,1,0:T(8,128)(2,1)S(1)}, bf16[2,128,256]{2,1,0:T(8,128)(2,1)S(1)}, u32[]{:S(2)}, u32[]{:S(2)}) collective-permute-start(bf16[2,128,256]{2,1,0:T(8,128)(2,1)S(1)} %get-tuple-element.61.refs_0_), channel_id=1, source_target_pairs={{0,12},{4,8},{8,4},{12,0},{1,13},{5,9},{9,5},{13,1},{2,14},{6,10},... | collective-permute-start | bytes 393224 | tf_op jit(solution)/shard_map/ppermute | solution.py:408
  26.6 1.8 %collective-permute-start.9 = (bf16[2,128,256]{2,1,0:T(8,128)(2,1)S(1)}, bf16[2,128,256]{2,1,0:T(8,128)(2,1)S(1)}, u32[]{:S(2)}, u32[]{:S(2)}) collective-permute-start(bf16[2,128,256]{2,1,0:T(8,128)(2,1)S(1)} %get-tuple-element.61.refs_0_), channel_id=1, source_target_pairs={{0,8},{4,12},{8,0},{12,4},{1,9},{5,13},{9,1},{13,5},{2,10},{6,14},... | collective-permute-start | bytes 393224 | tf_op jit(solution)/shard_map/ppermute | solution.py:408
  29.2 1.3 %collective-permute-start.4 = (bf16[2,128,128]{2,1,0:T(8,128)(2,1)S(1)}, bf16[2,128,128]{2,1,0:T(8,128)(2,1)S(1)}, u32[]{:S(2)}, u32[]{:S(2)}) collective-permute-start(bf16[2,128,128]{2,1,0:T(8,128)(2,1)S(1)} %get-tuple-element.52), channel_id=1, source_target_pairs={{0,16},{1,17},{2,18},{3,19},{4,20},{5,21},{6,22},{7,23},{8,24},{9,... | collective-permute-start | bytes 196616 | tf_op jit(solution)/shard_map/ppermute | solution.py:403
  32.0 1.6 %collective-permute-start.5 = (bf16[512,256]{1,0:T(8,128)(2,1)S(1)}, bf16[512,256]{1,0:T(8,128)(2,1)S(1)}, u32[]{:S(2)}, u32[]{:S(2)}) collective-permute-start(bf16[512,256]{1,0:T(8,128)(2,1)S(1)} %shard_map.106), channel_id=1, source_target_pairs={{0,1},{1,2},{2,3},{3,0},{4,5},{5,6},{6,7},{7,4},{8,9},{9,10},{10,1... | collective-permute-start | bytes 786440 | tf_op jit(solution)/shard_map/ppermute | solution.py:623
  33.6 2.0 %collective-permute-done.8.refs_1_ = bf16[2,128,256]{2,1,0:T(8,128)(2,1)S(1)} collective-permute-done((bf16[2,128,256]{2,1,0:T(8,128)(2,1)S(1)}, bf16[2,128,256]{2,1,0:T(8,128)(2,1)S(1)}, u32[]{:S(2)}, u32[]{:S(2)}) %collective-permute-start.8) | collective-permute-done | bytes 131104 | tf_op jit(solution)/shard_map/ppermute | solution.py:408
  36.3 1.3 %collective-permute-start.11 = (bf16[2,128,128]{2,1,0:T(8,128)(2,1)S(1)}, bf16[2,128,128]{2,1,0:T(8,128)(2,1)S(1)}, u32[]{:S(2)}, u32[]{:S(2)}) collective-permute-start(bf16[2,128,128]{2,1,0:T(8,128)(2,1)S(1)} %get-tuple-element.65), channel_id=1, source_target_pairs={{0,16},{1,17},{2,18},{3,19},{4,20},{5,21},{6,22},{7,23},{8,24},{9,... | collective-permute-start | bytes 196616 | tf_op jit(solution)/shard_map/ppermute | solution.py:403
  38.9 1.8 %collective-permute-start.12 = (bf16[512,256]{1,0:T(8,128)(2,1)S(1)}, bf16[512,256]{1,0:T(8,128)(2,1)S(1)}, u32[]{:S(2)}, u32[]{:S(2)}) collective-permute-start(bf16[512,256]{1,0:T(8,128)(2,1)S(1)} %shard_map.109), channel_id=1, source_target_pairs={{0,1},{1,2},{2,3},{3,0},{4,5},{5,6},{6,7},{7,4},{8,9},{9,10},{10,1... | collective-permute-start | bytes 786440 | tf_op jit(solution)/shard_map/ppermute | solution.py:623
  41.1 1.1 %collective-permute-done.5 = bf16[512,256]{1,0:T(8,128)(2,1)S(1)} collective-permute-done((bf16[512,256]{1,0:T(8,128)(2,1)S(1)}, bf16[512,256]{1,0:T(8,128)(2,1)S(1)}, u32[]{:S(2)}, u32[]{:S(2)}) %collective-permute-start.5) | collective-permute-done | bytes 262176 | tf_op jit(solution)/shard_map/ppermute | solution.py:623
  43.7 6.4 %collective-permute-done.12 = bf16[512,256]{1,0:T(8,128)(2,1)S(1)} collective-permute-done((bf16[512,256]{1,0:T(8,128)(2,1)S(1)}, bf16[512,256]{1,0:T(8,128)(2,1)S(1)}, u32[]{:S(2)}, u32[]{:S(2)}) %collective-permute-start.12) | collective-permute-done | bytes 262176 | tf_op jit(solution)/shard_map/ppermute | solution.py:623
  50.5 5.2 %collective-permute-done.6 = bf16[512,256]{1,0:T(8,128)(2,1)S(1)} collective-permute-done((bf16[512,256]{1,0:T(8,128)(2,1)S(1)}, bf16[512,256]{1,0:T(8,128)(2,1)S(1)}, u32[]{:S(2)}, u32[]{:S(2)}) %collective-permute-start.6) | collective-permute-done | bytes 262176 | tf_op jit(solution)/shard_map/ppermute | solution.py:623
  56.1 5.2 %collective-permute-done.13 = bf16[512,256]{1,0:T(8,128)(2,1)S(1)} collective-permute-done((bf16[512,256]{1,0:T(8,128)(2,1)S(1)}, bf16[512,256]{1,0:T(8,128)(2,1)S(1)}, u32[]{:S(2)}, u32[]{:S(2)}) %collective-permute-start.13) | collective-permute-done | bytes 262176 | tf_op jit(solution)/shard_map/ppermute | solution.py:623
  61.8 5.1 %collective-permute-done.7 = bf16[512,256]{1,0:T(8,128)(2,1)S(1)} collective-permute-done((bf16[512,256]{1,0:T(8,128)(2,1)S(1)}, bf16[512,256]{1,0:T(8,128)(2,1)S(1)}, u32[]{:S(2)}, u32[]{:S(2)}) %collective-permute-start.7) | collective-permute-done | bytes 262176 | tf_op jit(solution)/shard_map/ppermute | solution.py:623
  67.3 4.7 %collective-permute-done.14.block_ref = bf16[512,256]{1,0:T(8,128)(2,1)S(1)} collective-permute-done((bf16[512,256]{1,0:T(8,128)(2,1)S(1)}, bf16[512,256]{1,0:T(8,128)(2,1)S(1)}, u32[]{:S(2)}, u32[]{:S(2)}) %collective-permute-start.14) | collective-permute-done | bytes 262176 | tf_op jit(solution)/shard_map/ppermute | solution.py:623
  72.0 1.3 %shard_map.110 = bf16[512,1024]{1,0:T(8,128)(2,1)} custom-call(s32[1]{0:T(128)} %bitcast.section, f32[512,1024]{1,0:T(8,128)S(1)} %add_add_fusion.1.first_ref, f32[512,1024]{1,0:T(8,128)S(1)} %add_add_fusion.second_ref, bf16[512,256]{1,0:T(8,128)(2,1)S(1)} %collective-permute-done.14.block_ref, bf16[2048,1024]{1,0:T(8,128)(2,1)S(1)} %copy-done), custom_call_target="tpu_custom_call" | custom-call | tf_op jit(solution)/shard_map/pallas_call | solution.py:546
  (49 shorter events, 8.5 us)
Async XLA Ops:
  0.0 6.3 %copy-start.10 = (bf16[512,4,128]{2,1,0:T(4,128)(2,1)S(1)}, bf16[512,4,128]{2,1,0:T(4,128)(2,1)}, u32[]{:S(2)}) copy-start(bf16[512,4,128]{2,1,0:T(4,128)(2,1)} %refs_2_.1) | copy-start | bytes 1572868
  0.0 7.5 %copy-start.1 = (f32[3,4,4,128]{3,2,1,0:T(4,128)S(1)}, f32[3,4,4,128]{3,2,1,0:T(4,128)}, u32[]{:S(2)}) copy-start(f32[3,4,4,128]{3,2,1,0:T(4,128)} %taps_ref.5) | copy-start | bytes 73732
  1.4 8.7 %collective-permute-start = (bf16[24,4,128]{2,1,0:T(4,128)(2,1)}, bf16[24,4,128]{2,1,0:T(4,128)(2,1)S(1)}, u32[]{:S(2)}, u32[]{:S(2)}) collective-permute-start(bf16[24,4,128]{2,1,0:T(4,128)(2,1)} %shard_map.101), channel_id=1, source_target_pairs={{0,4},{4,8},{8,12},{12,16},{16,20},{20,24},{24,28},{1,5},{5,9},{9,... | collective-permute-start | bytes 73736 | tf_op jit(solution)/shard_map/ppermute | solution.py:403
  7.5 2.6 %copy-start.2 = (f32[4,512]{1,0:T(4,128)S(1)}, f32[4,512]{1,0:T(4,128)}, u32[]{:S(2)}) copy-start(f32[4,512]{1,0:T(4,128)} %decay_ref.3) | copy-start | bytes 24580
  7.5 2.6 %copy-start.3 = (f32[4,512]{1,0:T(4,128)S(1)}, f32[4,512]{1,0:T(4,128)}, u32[]{:S(2)}) copy-start(f32[4,512]{1,0:T(4,128)} %strength_ref.3) | copy-start | bytes 24580
  7.5 2.6 %copy-start.4 = (s32[8]{0:T(128)S(1)}, s32[8]{0:T(128)}, u32[]{:S(2)}) copy-start(s32[8]{0:T(128)} %resets.3) | copy-start | bytes 100
  11.2 8.6 %copy-start.8 = (bf16[512,4,128]{2,1,0:T(4,128)(2,1)S(1)}, bf16[512,4,128]{2,1,0:T(4,128)(2,1)}, u32[]{:S(2)}) copy-start(bf16[512,4,128]{2,1,0:T(4,128)(2,1)} %refs_0_.1) | copy-start | bytes 1572868
  11.2 8.7 %copy-start.9 = (bf16[512,4,128]{2,1,0:T(4,128)(2,1)S(1)}, bf16[512,4,128]{2,1,0:T(4,128)(2,1)}, u32[]{:S(2)}) copy-start(bf16[512,4,128]{2,1,0:T(4,128)(2,1)} %param.13) | copy-start | bytes 1572868
  16.3 3.7 %copy-start.5 = (f32[128]{0:T(128)S(1)}, f32[128]{0:T(128)}, u32[]{:S(2)}) copy-start(f32[128]{0:T(128)} %param.18) | copy-start | bytes 1540
  16.3 12.2 %collective-permute-start.3 = (bf16[2,128,256]{2,1,0:T(8,128)(2,1)S(1)}, bf16[2,128,256]{2,1,0:T(8,128)(2,1)S(1)}, u32[]{:S(2)}, u32[]{:S(2)}) collective-permute-start(bf16[2,128,256]{2,1,0:T(8,128)(2,1)S(1)} %get-tuple-element.48.refs_0_), channel_id=1, source_target_pairs={{0,12},{4,8},{8,4},{12,0},{1,13},{5,9},{9,5},{13,1},{2,14},{6,10},... | collective-permute-start | bytes 393224 | tf_op jit(solution)/shard_map/ppermute | solution.py:408
  17.5 11.0 %collective-permute-start.2 = (bf16[2,128,256]{2,1,0:T(8,128)(2,1)S(1)}, bf16[2,128,256]{2,1,0:T(8,128)(2,1)S(1)}, u32[]{:S(2)}, u32[]{:S(2)}) collective-permute-start(bf16[2,128,256]{2,1,0:T(8,128)(2,1)S(1)} %get-tuple-element.48.refs_0_), channel_id=1, source_target_pairs={{0,8},{4,12},{8,0},{12,4},{1,9},{5,13},{9,1},{13,5},{2,10},{6,14},... | collective-permute-start | bytes 393224 | tf_op jit(solution)/shard_map/ppermute | solution.py:408
  19.3 9.2 %collective-permute-start.1 = (bf16[2,128,256]{2,1,0:T(8,128)(2,1)S(1)}, bf16[2,128,256]{2,1,0:T(8,128)(2,1)S(1)}, u32[]{:S(2)}, u32[]{:S(2)}) collective-permute-start(bf16[2,128,256]{2,1,0:T(8,128)(2,1)S(1)} %get-tuple-element.48.refs_0_), channel_id=1, source_target_pairs={{0,4},{4,0},{8,12},{12,8},{1,5},{5,1},{9,13},{13,9},{2,6},{6,2},{1... | collective-permute-start | bytes 393224 | tf_op jit(solution)/shard_map/ppermute | solution.py:408
  25.4 8.1 %collective-permute-start.10 = (bf16[2,128,256]{2,1,0:T(8,128)(2,1)S(1)}, bf16[2,128,256]{2,1,0:T(8,128)(2,1)S(1)}, u32[]{:S(2)}, u32[]{:S(2)}) collective-permute-start(bf16[2,128,256]{2,1,0:T(8,128)(2,1)S(1)} %get-tuple-element.61.refs_0_), channel_id=1, source_target_pairs={{0,12},{4,8},{8,4},{12,0},{1,13},{5,9},{9,5},{13,1},{2,14},{6,10},... | collective-permute-start | bytes 393224 | tf_op jit(solution)/shard_map/ppermute | solution.py:408
  26.6 7.0 %collective-permute-start.9 = (bf16[2,128,256]{2,1,0:T(8,128)(2,1)S(1)}, bf16[2,128,256]{2,1,0:T(8,128)(2,1)S(1)}, u32[]{:S(2)}, u32[]{:S(2)}) collective-permute-start(bf16[2,128,256]{2,1,0:T(8,128)(2,1)S(1)} %get-tuple-element.61.refs_0_), channel_id=1, source_target_pairs={{0,8},{4,12},{8,0},{12,4},{1,9},{5,13},{9,1},{13,5},{2,10},{6,14},... | collective-permute-start | bytes 393224 | tf_op jit(solution)/shard_map/ppermute | solution.py:408
  29.2 2.3 %collective-permute-start.4 = (bf16[2,128,128]{2,1,0:T(8,128)(2,1)S(1)}, bf16[2,128,128]{2,1,0:T(8,128)(2,1)S(1)}, u32[]{:S(2)}, u32[]{:S(2)}) collective-permute-start(bf16[2,128,128]{2,1,0:T(8,128)(2,1)S(1)} %get-tuple-element.52), channel_id=1, source_target_pairs={{0,16},{1,17},{2,18},{3,19},{4,20},{5,21},{6,22},{7,23},{8,24},{9,... | collective-permute-start | bytes 196616 | tf_op jit(solution)/shard_map/ppermute | solution.py:403
  30.5 5.0 %collective-permute-start.8 = (bf16[2,128,256]{2,1,0:T(8,128)(2,1)S(1)}, bf16[2,128,256]{2,1,0:T(8,128)(2,1)S(1)}, u32[]{:S(2)}, u32[]{:S(2)}) collective-permute-start(bf16[2,128,256]{2,1,0:T(8,128)(2,1)S(1)} %get-tuple-element.61.refs_0_), channel_id=1, source_target_pairs={{0,4},{4,0},{8,12},{12,8},{1,5},{5,1},{9,13},{13,9},{2,6},{6,2},{1... | collective-permute-start | bytes 393224 | tf_op jit(solution)/shard_map/ppermute | solution.py:408
  32.0 10.3 %collective-permute-start.5 = (bf16[512,256]{1,0:T(8,128)(2,1)S(1)}, bf16[512,256]{1,0:T(8,128)(2,1)S(1)}, u32[]{:S(2)}, u32[]{:S(2)}) collective-permute-start(bf16[512,256]{1,0:T(8,128)(2,1)S(1)} %shard_map.106), channel_id=1, source_target_pairs={{0,1},{1,2},{2,3},{3,0},{4,5},{5,6},{6,7},{7,4},{8,9},{9,10},{10,1... | collective-permute-start | bytes 786440 | tf_op jit(solution)/shard_map/ppermute | solution.py:623
  36.3 2.2 %collective-permute-start.11 = (bf16[2,128,128]{2,1,0:T(8,128)(2,1)S(1)}, bf16[2,128,128]{2,1,0:T(8,128)(2,1)S(1)}, u32[]{:S(2)}, u32[]{:S(2)}) collective-permute-start(bf16[2,128,128]{2,1,0:T(8,128)(2,1)S(1)} %get-tuple-element.65), channel_id=1, source_target_pairs={{0,16},{1,17},{2,18},{3,19},{4,20},{5,21},{6,22},{7,23},{8,24},{9,... | collective-permute-start | bytes 196616 | tf_op jit(solution)/shard_map/ppermute | solution.py:403
  37.6 3.1 %copy-start = (bf16[2048,1024]{1,0:T(8,128)(2,1)S(1)}, bf16[2048,1024]{1,0:T(8,128)(2,1)}, u32[]{:S(2)}) copy-start(bf16[2048,1024]{1,0:T(8,128)(2,1)} %weights_ref.1) | copy-start | bytes 12582916
  38.9 11.1 %collective-permute-start.12 = (bf16[512,256]{1,0:T(8,128)(2,1)S(1)}, bf16[512,256]{1,0:T(8,128)(2,1)S(1)}, u32[]{:S(2)}, u32[]{:S(2)}) collective-permute-start(bf16[512,256]{1,0:T(8,128)(2,1)S(1)} %shard_map.109), channel_id=1, source_target_pairs={{0,1},{1,2},{2,3},{3,0},{4,5},{5,6},{6,7},{7,4},{8,9},{9,10},{10,1... | collective-permute-start | bytes 786440 | tf_op jit(solution)/shard_map/ppermute | solution.py:623
  42.7 12.9 %collective-permute-start.6 = (bf16[512,256]{1,0:T(8,128)(2,1)S(1)}, bf16[512,256]{1,0:T(8,128)(2,1)S(1)}, u32[]{:S(2)}, u32[]{:S(2)}) collective-permute-start(bf16[512,256]{1,0:T(8,128)(2,1)S(1)} %collective-permute-done.5), channel_id=1, source_target_pairs={{0,1},{1,2},{2,3},{3,0},{4,5},{5,6},{6,7},{7,4},{8,9},{9,10},{10,1... | collective-permute-start | bytes 786440 | tf_op jit(solution)/shard_map/ppermute | solution.py:623
  50.0 11.2 %collective-permute-start.13 = (bf16[512,256]{1,0:T(8,128)(2,1)S(1)}, bf16[512,256]{1,0:T(8,128)(2,1)S(1)}, u32[]{:S(2)}, u32[]{:S(2)}) collective-permute-start(bf16[512,256]{1,0:T(8,128)(2,1)S(1)} %collective-permute-done.12), channel_id=1, source_target_pairs={{0,1},{1,2},{2,3},{3,0},{4,5},{5,6},{6,7},{7,4},{8,9},{9,10},{10,1... | collective-permute-start | bytes 786440 | tf_op jit(solution)/shard_map/ppermute | solution.py:623
  55.6 11.2 %collective-permute-start.7 = (bf16[512,256]{1,0:T(8,128)(2,1)S(1)}, bf16[512,256]{1,0:T(8,128)(2,1)S(1)}, u32[]{:S(2)}, u32[]{:S(2)}) collective-permute-start(bf16[512,256]{1,0:T(8,128)(2,1)S(1)} %collective-permute-done.6), channel_id=1, source_target_pairs={{0,1},{1,2},{2,3},{3,0},{4,5},{5,6},{6,7},{7,4},{8,9},{9,10},{10,1... | collective-permute-start | bytes 786440 | tf_op jit(solution)/shard_map/ppermute | solution.py:623
  61.3 10.8 %collective-permute-start.14 = (bf16[512,256]{1,0:T(8,128)(2,1)S(1)}, bf16[512,256]{1,0:T(8,128)(2,1)S(1)}, u32[]{:S(2)}, u32[]{:S(2)}) collective-permute-start(bf16[512,256]{1,0:T(8,128)(2,1)S(1)} %collective-permute-done.13), channel_id=1, source_target_pairs={{0,1},{1,2},{2,3},{3,0},{4,5},{5,6},{6,7},{7,4},{8,9},{9,10},{10,1... | collective-permute-start | bytes 786440 | tf_op jit(solution)/shard_map/ppermute | solution.py:623
  (2 other events, 1.8 us)

commit v15 on v14

--- a/solution.py
+++ b/solution.py
@@ -156,7 +156,7 @@
         copy.wait()
 
 
-def filters_kernel(key_ref, value_ref, taps_ref, unit_ref, value_out_ref, first_ref, padded):
+def filters_kernel(key_ref, value_ref, taps_ref, filtered_ref, first_ref, padded):
     heads, length, _ = key_ref.shape
     for i, x_ref in enumerate((key_ref, value_ref)):
         padded[i, :, RIM:] = x_ref[...].astype(F32)
@@ -168,17 +168,15 @@
             taps = taps_of(taps_ref, 1 + i, h)
             for c in range(length // CHUNK):
                 rows = filtered(padded.at[i, h], taps, c * CHUNK, CHUNK)
-                if i == 0:
-                    unit_ref[h, rows_of(c)] = unit(rows).astype(BF16)
-                else:
-                    value_out_ref[h, rows_of(c)] = rows.astype(BF16)
+                rows = unit(rows) if i == 0 else rows
+                filtered_ref[i, h, rows_of(c)] = rows.astype(BF16)
         return carry
 
     lax.fori_loop(0, heads, one_head, 0)
 
 
 def maps_kernel(
-    base, resets, unit_in_ref, value_in_ref, first_ref, rim_ref, taps_ref, decay_ref, strength_ref,
+    base, resets, filtered_ref, first_ref, rim_ref, taps_ref, decay_ref, strength_ref,
     unit_ref, solved_ref, starts_ref, *refs,
 ):
     *map_refs, rims, padded, value_s, step_s = refs
@@ -190,8 +188,8 @@
     rims[...] = rim_ref[...].astype(F32)
     for g in range(heads):
         h = base + g
-        unit_ref[g] = unit_in_ref[h]
-        value_s[g] = value_in_ref[h]
+        unit_ref[g] = filtered_ref[0, h]
+        value_s[g] = filtered_ref[1, h]
         for i in range(2):
             padded[g, i, 0:RIM] = rims[(1 + i) * RIM : (2 + i) * RIM, h, :]
             padded[g, i, RIM : RIM + AGAIN] = first_ref[i, h]
@@ -414,7 +412,7 @@
 VMEM = pl.BlockSpec(memory_space=pltpu.VMEM)
 SMEM = pl.BlockSpec(memory_space=pltpu.SMEM)
 HBM = pl.BlockSpec(memory_space=pltpu.HBM)
-PARAMS = pltpu.CompilerParams(vmem_limit_bytes=8 * 1024 * 1024)
+PARAMS = pltpu.CompilerParams(vmem_limit_bytes=6 * 1024 * 1024)
 LAST_PARAMS = pltpu.CompilerParams(vmem_limit_bytes=12 * 1024 * 1024)
 
 
@@ -433,12 +431,14 @@
 
 def filters_of(key, value, taps):
     heads, length, depth = key.shape
-    per_token = jax.ShapeDtypeStruct((heads, length, depth), BF16)
     return pl.pallas_call(
         filters_kernel,
-        out_shape=(per_token, per_token, jax.ShapeDtypeStruct((2, heads, AGAIN, depth), F32)),
+        out_shape=(
+            jax.ShapeDtypeStruct((2, heads, length, depth), BF16),
+            jax.ShapeDtypeStruct((2, heads, AGAIN, depth), F32),
+        ),
         in_specs=[VMEM] * 3,
-        out_specs=[VMEM] * 3,
+        out_specs=[VMEM] * 2,
         scratch_shapes=[pltpu.VMEM((2, heads, length + RIM, depth), F32)],
         compiler_params=PARAMS,
         cost_estimate=pl.CostEstimate(
@@ -447,8 +447,8 @@
     )(key, value, taps)
 
 
-def maps_of(base, heads, resets, unit_in, value_in, first, rims, taps, decay, strength):
-    _, length, depth = unit_in.shape
+def maps_of(base, heads, resets, filtered, first, rims, taps, decay, strength):
+    _, _, length, depth = filtered.shape
     chunks = length // CHUNK
     return pl.pallas_call(
         functools.partial(maps_kernel, base),
@@ -458,7 +458,7 @@
             jax.ShapeDtypeStruct((heads, chunks - 1, depth, 2 * depth), F32),
             *[jax.ShapeDtypeStruct((heads // GROUPS, depth, 2 * depth), BF16)] * GROUPS,
         ),
-        in_specs=[SMEM] + [VMEM] * 7,
+        in_specs=[SMEM] + [VMEM] * 6,
         out_specs=[VMEM] * (3 + GROUPS),
         scratch_shapes=[
             pltpu.VMEM(rims.shape, F32),
@@ -470,7 +470,7 @@
         cost_estimate=pl.CostEstimate(
             flops=5 * 10**9, bytes_accessed=4 * 2**20, transcendentals=10**6
         ),
-    )(resets, unit_in, value_in, first, rims, taps, decay, strength)
+    )(resets, filtered, first, rims, taps, decay, strength)
 
 
 def reads_of(base, heads, resets, query, gate, gain, rims, taps, decay, strength, made):
@@ -576,14 +576,14 @@
     taps = conv_weight
     rims = from_behind(pack_rims((query_in, key_in, value_in)), ("chain", "leaf"), 1)
     key, value = (jnp.transpose(x, (1, 0, 2)) for x in (key_in, value_in))
-    key, value, first = filters_of(key, value, taps)
+    filtered, first = filters_of(key, value, taps)
     gain = output_norm_gain.reshape(1, depth)
     leaves = lax.axis_size("leaf")
     place = lax.axis_index("leaf").astype(jnp.int32).reshape(1)
 
     links = lax.axis_size("chain") - 1
     unit_key, solved, starts, *own_maps = maps_of(
-        0, heads, doc_resets, key, value, first, rims, taps, log_decay, write_strength
+        0, heads, doc_resets, filtered, first, rims, taps, log_decay, write_strength
     )
     query_in, gate_in = after(own_maps[-1], query_in, gate_in)
     query, gate = (jnp.transpose(x, (1, 0, 2)) for x in (query_in, gate_in))
@@ -622,7 +622,7 @@
         last = k + 1 == ring
         following = blocks if last else [lax.ppermute(x, "head", around) for x in blocks]
         if k == 0:
-            blocks[:-1] = after(following[0], *blocks[:-1])
+            blocks[:-1] = after(following[-1], *blocks[:-1])
         for g, block in enumerate(blocks):
             section = owner * GROUPS + g
             if last and g + 1 == GROUPS:

time: 73.7 us -> 74.1 us (level)
  transfers between devices with their start and end apart: 15 -> 15, of which waited for: 8 -> 9; matrix products, arithmetic and copies ran while one was open for 6% -> 6% of each run, Pallas kernels for 14% -> 14%
where the time goes in v15:
time: 74.1 us; the launch traced here: 73.8 us
  waiting for transfers between devices  30 us (40%)
  starting transfers between devices  18.6 us (25%)
  Pallas kernels  18.1 us (24%)
  local copies, waits for them, and re-layouts  3.55 us (5%)
  matrix products  3.16 us (4%)
    ppermute x6, waiting for transfers between devices, on_device(): lax.ppermute(x, 'head', around)  27.6 us
    ppermute x3, starting transfers between devices, from_behind(): lax.ppermute(value, axis, [(i, i + steps) for i in range(count - steps)])  7.43 us
    ppermute x6, starting transfers between devices, exchange(): lax.ppermute(later if k == 1 else own_map, 'leaf', pairs_at(k, leaves))  7.17 us
    pallas_call x1, Pallas kernels, reads_of(): pl.pallas_call(functools.partial(reads_kernel, base), out_shape=(jax.Shap...  5.44 us
    pallas_call x1, Pallas kernels, maps_of(): pl.pallas_call(functools.partial(maps_kernel, base), out_shape=(jax.Shape...  5.07 us
    ppermute x6, starting transfers between devices, on_device(): lax.ppermute(x, 'head', around)  3.99 us
    dot_general x7, matrix products, on_device(): term = jnp.dot(block, rows, preferred_element_type=F32)  3.16 us
    unnamed x22, local copies, waits for them, and re-layouts  2.23 us
  transfers between devices with their start and end apart: 15, of which 9 were waited for; matrix products, arithmetic and copies ran while one was open for 6% of the time, Pallas kernels for 14%

profile of v15, /device:TPU:0, one launch (start us, length us, event | category | flops | bytes accessed | tf_op | source)
XLA Modules:
  0.0 73.8 jit_solution(12492637956233132055)
XLA Ops:
  0.0 1.4 %shard_map.101 = bf16[24,4,128]{2,1,0:T(4,128)(2,1)} custom-call(bf16[512,4,128]{2,1,0:T(4,128)(2,1)} %refs_0_.1, bf16[512,4,128]{2,1,0:T(4,128)(2,1)} %refs_1_.1, bf16[512,4,128]{2,1,0:T(4,128)(2,1)} %refs_2_.1), custom_call_target="tpu_custom_call" | custom-call | flops 1000000000 | bytes 65536 | tf_op jit(solution)/shard_map/pallas_call | solution.py:421
  1.4 4.8 %collective-permute-start = (bf16[24,4,128]{2,1,0:T(4,128)(2,1)}, bf16[24,4,128]{2,1,0:T(4,128)(2,1)S(1)}, u32[]{:S(2)}, u32[]{:S(2)}) collective-permute-start(bf16[24,4,128]{2,1,0:T(4,128)(2,1)} %shard_map.101), channel_id=1, source_target_pairs={{0,4},{4,8},{8,12},{12,16},{16,20},{20,24},{24,28},{1,5},{5,9},{9,... | collective-permute-start | bytes 73736 | tf_op jit(solution)/shard_map/ppermute | solution.py:401
  6.3 1.2 %copy_bitcast_fusion.2 = (bf16[4,512,128]{2,1,0:T(8,128)(2,1)S(1)}, bf16[4,512,128]{2,1,0:T(8,128)(2,1)S(1)}) fusion(bf16[512,4,128]{2,1,0:T(4,128)(2,1)S(1)} %copy-done.10, bf16[512,4,128]{2,1,0:T(4,128)(2,1)} %refs_1_.1), kind=kLoop, calls=%fused_computation.4 | loop fusion | bytes 2097152 | tf_op jit(solution)/shard_map/transpose | solution.py:578
  7.5 1.8 %shard_map.100 = (bf16[2,4,512,128]{3,2,1,0:T(8,128)(2,1)S(1)}, f32[2,4,16,128]{3,2,1,0:T(8,128)S(1)}) custom-call(bf16[4,512,128]{2,1,0:T(8,128)(2,1)S(1)} %get-tuple-element.68.key_ref, bf16[4,512,128]{2,1,0:T(8,128)(2,1)S(1)} %get-tuple-element.67.value_ref, f32[3,4,4,128]{3,2,1,0:T(4,128)S(1)} %copy-done.1), custom_call_target="tpu_custom_call" | custom-call | flops 3000000000 | bytes 4194304 | tf_op jit(solution)/shard_map/pallas_call | solution.py:434
  9.3 1.0 %copy-done.6 = bf16[2,4,512,128]{3,2,1,0:T(8,128)(2,1)} copy-done((bf16[2,4,512,128]{3,2,1,0:T(8,128)(2,1)}, bf16[2,4,512,128]{3,2,1,0:T(8,128)(2,1)S(1)}, u32[]{:S(2)}) %copy-start.6) | copy-done | bytes 1048600
  10.3 1.2 %copy-done.7 = bf16[2,4,512,128]{3,2,1,0:T(8,128)(2,1)S(1)} copy-done((bf16[2,4,512,128]{3,2,1,0:T(8,128)(2,1)S(1)}, bf16[2,4,512,128]{3,2,1,0:T(8,128)(2,1)}, u32[]{:S(2)}) %copy-start.7) | copy-done | bytes 1048600
  11.5 5.1 %shard_map.102 = (bf16[4,512,128]{2,1,0:T(8,128)(2,1)S(1)}, f32[4,512,256]{2,1,0:T(8,128)S(1)}, f32[4,3,128,256]{3,2,1,0:T(8,128)S(1)}, bf16[2,128,256]{2,1,0:T(8,128)(2,1)S(1)}, bf16[2,128,256]{2,1,0:T(8,128)(2,1)S(1)}) custom-call(s32[8]{0:T(128)S(1)} %copy-done.4, bf16[2,4,512,128]{3,2,1,0:T(8,128)(2,1)S(1)} %copy-done.7, ...), custom_call_target="tpu_custom_call" | custom-call | flops 5000000000 | bytes 4194304 | tf_op jit(solution)/shard_map/pallas_call | solution.py:453
  16.6 1.5 %collective-permute-start.1 = (bf16[2,128,256]{2,1,0:T(8,128)(2,1)S(1)}, bf16[2,128,256]{2,1,0:T(8,128)(2,1)S(1)}, u32[]{:S(2)}, u32[]{:S(2)}) collective-permute-start(bf16[2,128,256]{2,1,0:T(8,128)(2,1)S(1)} %get-tuple-element.46.refs_0_), channel_id=1, source_target_pairs={{0,4},{4,0},{8,12},{12,8},{1,5},{5,1},{9,13},{13,9},{2,6},{6,2},{1... | collective-permute-start | bytes 393224 | tf_op jit(solution)/shard_map/ppermute | solution.py:406
  18.3 1.9 %collective-permute-start.3 = (bf16[2,128,256]{2,1,0:T(8,128)(2,1)S(1)}, bf16[2,128,256]{2,1,0:T(8,128)(2,1)S(1)}, u32[]{:S(2)}, u32[]{:S(2)}) collective-permute-start(bf16[2,128,256]{2,1,0:T(8,128)(2,1)S(1)} %get-tuple-element.46.refs_0_), channel_id=1, source_target_pairs={{0,12},{4,8},{8,4},{12,0},{1,13},{5,9},{9,5},{13,1},{2,14},{6,10},... | collective-permute-start | bytes 393224 | tf_op jit(solution)/shard_map/ppermute | solution.py:406
  20.4 5.4 %shard_map.103 = (bf16[4,512,128]{2,1,0:T(8,128)(2,1)S(1)}, f32[4,512,128]{2,1,0:T(8,128)S(1)}, f32[4,512,128]{2,1,0:T(8,128)S(1)}) custom-call(s32[8]{0:T(128)S(1)} %copy-done.4, bf16[4,512,128]{2,1,0:T(8,128)(2,1)S(1)} %bitcast.20, bf16[4,512,128]{2,1,0:T(8,128)(2,1)S(1)} %bitcast.21, f32[1,128]{1,0:T(1,128)S(1)} %bitcast.22, ...), custom_call_target="tpu_custom_call" | custom-call | flops 3000000000 | bytes 4194304 | tf_op jit(solution)/shard_map/pallas_call | solution.py:479
  25.8 1.6 %collective-permute-start.6 = (bf16[2,128,256]{2,1,0:T(8,128)(2,1)S(1)}, bf16[2,128,256]{2,1,0:T(8,128)(2,1)S(1)}, u32[]{:S(2)}, u32[]{:S(2)}) collective-permute-start(bf16[2,128,256]{2,1,0:T(8,128)(2,1)S(1)} %get-tuple-element.58.refs_0_), channel_id=1, source_target_pairs={{0,8},{4,12},{8,0},{12,4},{1,9},{5,13},{9,1},{13,5},{2,10},{6,14},... | collective-permute-start | bytes 393224 | tf_op jit(solution)/shard_map/ppermute | solution.py:406
  27.4 1.4 %collective-permute-start.7 = (bf16[2,128,256]{2,1,0:T(8,128)(2,1)S(1)}, bf16[2,128,256]{2,1,0:T(8,128)(2,1)S(1)}, u32[]{:S(2)}, u32[]{:S(2)}) collective-permute-start(bf16[2,128,256]{2,1,0:T(8,128)(2,1)S(1)} %get-tuple-element.58.refs_0_), channel_id=1, source_target_pairs={{0,12},{4,8},{8,4},{12,0},{1,13},{5,9},{9,5},{13,1},{2,14},{6,10},... | collective-permute-start | bytes 393224 | tf_op jit(solution)/shard_map/ppermute | solution.py:406
  29.6 1.3 %collective-permute-start.4 = (bf16[2,128,128]{2,1,0:T(8,128)(2,1)S(1)}, bf16[2,128,128]{2,1,0:T(8,128)(2,1)S(1)}, u32[]{:S(2)}, u32[]{:S(2)}) collective-permute-start(bf16[2,128,128]{2,1,0:T(8,128)(2,1)S(1)} %get-tuple-element.50), channel_id=1, source_target_pairs={{0,16},{1,17},{2,18},{3,19},{4,20},{5,21},{6,22},{7,23},{8,24},{9,... | collective-permute-start | bytes 196616 | tf_op jit(solution)/shard_map/ppermute | solution.py:401
  32.3 1.6 %collective-permute-start.10 = (bf16[512,256]{1,0:T(8,128)(2,1)S(1)}, bf16[512,256]{1,0:T(8,128)(2,1)S(1)}, u32[]{:S(2)}, u32[]{:S(2)}) collective-permute-start(bf16[512,256]{1,0:T(8,128)(2,1)S(1)} %shard_map.106), channel_id=1, source_target_pairs={{0,1},{1,2},{2,3},{3,0},{4,5},{5,6},{6,7},{7,4},{8,9},{9,10},{10,1... | collective-permute-start | bytes 786440 | tf_op jit(solution)/shard_map/ppermute | solution.py:623
  34.3 1.6 %collective-permute-done.5.refs_1_ = bf16[2,128,256]{2,1,0:T(8,128)(2,1)S(1)} collective-permute-done((bf16[2,128,256]{2,1,0:T(8,128)(2,1)S(1)}, bf16[2,128,256]{2,1,0:T(8,128)(2,1)S(1)}, u32[]{:S(2)}, u32[]{:S(2)}) %collective-permute-start.5) | collective-permute-done | bytes 131104 | tf_op jit(solution)/shard_map/ppermute | solution.py:406
  36.7 1.3 %collective-permute-start.8 = (bf16[2,128,128]{2,1,0:T(8,128)(2,1)S(1)}, bf16[2,128,128]{2,1,0:T(8,128)(2,1)S(1)}, u32[]{:S(2)}, u32[]{:S(2)}) collective-permute-start(bf16[2,128,128]{2,1,0:T(8,128)(2,1)S(1)} %get-tuple-element.62), channel_id=1, source_target_pairs={{0,16},{1,17},{2,18},{3,19},{4,20},{5,21},{6,22},{7,23},{8,24},{9,... | collective-permute-start | bytes 196616 | tf_op jit(solution)/shard_map/ppermute | solution.py:401
  39.2 1.8 %collective-permute-start.9 = (bf16[512,256]{1,0:T(8,128)(2,1)S(1)}, bf16[512,256]{1,0:T(8,128)(2,1)S(1)}, u32[]{:S(2)}, u32[]{:S(2)}) collective-permute-start(bf16[512,256]{1,0:T(8,128)(2,1)S(1)} %shard_map.109), channel_id=1, source_target_pairs={{0,1},{1,2},{2,3},{3,0},{4,5},{5,6},{6,7},{7,4},{8,9},{9,10},{10,1... | collective-permute-start | bytes 786440 | tf_op jit(solution)/shard_map/ppermute | solution.py:623
  41.5 1.1 %collective-permute-done.10 = bf16[512,256]{1,0:T(8,128)(2,1)S(1)} collective-permute-done((bf16[512,256]{1,0:T(8,128)(2,1)S(1)}, bf16[512,256]{1,0:T(8,128)(2,1)S(1)}, u32[]{:S(2)}, u32[]{:S(2)}) %collective-permute-start.10) | collective-permute-done | bytes 262176 | tf_op jit(solution)/shard_map/ppermute | solution.py:623
  43.6 6.8 %collective-permute-done.9 = bf16[512,256]{1,0:T(8,128)(2,1)S(1)} collective-permute-done((bf16[512,256]{1,0:T(8,128)(2,1)S(1)}, bf16[512,256]{1,0:T(8,128)(2,1)S(1)}, u32[]{:S(2)}, u32[]{:S(2)}) %collective-permute-start.9) | collective-permute-done | bytes 262176 | tf_op jit(solution)/shard_map/ppermute | solution.py:623
  51.3 4.7 %collective-permute-done.11 = bf16[512,256]{1,0:T(8,128)(2,1)S(1)} collective-permute-done((bf16[512,256]{1,0:T(8,128)(2,1)S(1)}, bf16[512,256]{1,0:T(8,128)(2,1)S(1)}, u32[]{:S(2)}, u32[]{:S(2)}) %collective-permute-start.11) | collective-permute-done | bytes 262176 | tf_op jit(solution)/shard_map/ppermute | solution.py:623
  56.5 5.5 %collective-permute-done.13 = bf16[512,256]{1,0:T(8,128)(2,1)S(1)} collective-permute-done((bf16[512,256]{1,0:T(8,128)(2,1)S(1)}, bf16[512,256]{1,0:T(8,128)(2,1)S(1)}, u32[]{:S(2)}, u32[]{:S(2)}) %collective-permute-start.13) | collective-permute-done | bytes 262176 | tf_op jit(solution)/shard_map/ppermute | solution.py:623
  62.4 5.1 %collective-permute-done.12 = bf16[512,256]{1,0:T(8,128)(2,1)S(1)} collective-permute-done((bf16[512,256]{1,0:T(8,128)(2,1)S(1)}, bf16[512,256]{1,0:T(8,128)(2,1)S(1)}, u32[]{:S(2)}, u32[]{:S(2)}) %collective-permute-start.12) | collective-permute-done | bytes 262176 | tf_op jit(solution)/shard_map/ppermute | solution.py:623
  68.0 4.4 %collective-permute-done.14.block_ref = bf16[512,256]{1,0:T(8,128)(2,1)S(1)} collective-permute-done((bf16[512,256]{1,0:T(8,128)(2,1)S(1)}, bf16[512,256]{1,0:T(8,128)(2,1)S(1)}, u32[]{:S(2)}, u32[]{:S(2)}) %collective-permute-start.14) | collective-permute-done | bytes 262176 | tf_op jit(solution)/shard_map/ppermute | solution.py:623
  72.4 1.3 %shard_map.110 = bf16[512,1024]{1,0:T(8,128)(2,1)} custom-call(s32[1]{0:T(128)} %bitcast.section, f32[512,1024]{1,0:T(8,128)S(1)} %add_add_fusion.1.first_ref, f32[512,1024]{1,0:T(8,128)S(1)} %add_add_fusion.second_ref, bf16[512,256]{1,0:T(8,128)(2,1)S(1)} %collective-permute-done.14.block_ref, bf16[2048,1024]{1,0:T(8,128)(2,1)S(1)} %copy-done), custom_call_target="tpu_custom_call" | custom-call | tf_op jit(solution)/shard_map/pallas_call | solution.py:546
  (49 shorter events, 8.5 us)
Async XLA Ops:
  0.0 6.3 %copy-start.10 = (bf16[512,4,128]{2,1,0:T(4,128)(2,1)S(1)}, bf16[512,4,128]{2,1,0:T(4,128)(2,1)}, u32[]{:S(2)}) copy-start(bf16[512,4,128]{2,1,0:T(4,128)(2,1)} %refs_2_.1) | copy-start | bytes 1572868
  0.0 7.5 %copy-start.1 = (f32[3,4,4,128]{3,2,1,0:T(4,128)S(1)}, f32[3,4,4,128]{3,2,1,0:T(4,128)}, u32[]{:S(2)}) copy-start(f32[3,4,4,128]{3,2,1,0:T(4,128)} %taps_ref.5) | copy-start | bytes 73732
  1.4 8.9 %collective-permute-start = (bf16[24,4,128]{2,1,0:T(4,128)(2,1)}, bf16[24,4,128]{2,1,0:T(4,128)(2,1)S(1)}, u32[]{:S(2)}, u32[]{:S(2)}) collective-permute-start(bf16[24,4,128]{2,1,0:T(4,128)(2,1)} %shard_map.101), channel_id=1, source_target_pairs={{0,4},{4,8},{8,12},{12,16},{16,20},{20,24},{24,28},{1,5},{5,9},{9,... | collective-permute-start | bytes 73736 | tf_op jit(solution)/shard_map/ppermute | solution.py:401
  7.5 2.8 %copy-start.2 = (f32[4,512]{1,0:T(4,128)S(1)}, f32[4,512]{1,0:T(4,128)}, u32[]{:S(2)}) copy-start(f32[4,512]{1,0:T(4,128)} %decay_ref.3) | copy-start | bytes 24580
  7.5 2.8 %copy-start.3 = (f32[4,512]{1,0:T(4,128)S(1)}, f32[4,512]{1,0:T(4,128)}, u32[]{:S(2)}) copy-start(f32[4,512]{1,0:T(4,128)} %strength_ref.3) | copy-start | bytes 24580
  7.5 2.8 %copy-start.4 = (s32[8]{0:T(128)S(1)}, s32[8]{0:T(128)}, u32[]{:S(2)}) copy-start(s32[8]{0:T(128)} %resets.3) | copy-start | bytes 100
  11.5 8.7 %copy-start.8 = (bf16[512,4,128]{2,1,0:T(4,128)(2,1)S(1)}, bf16[512,4,128]{2,1,0:T(4,128)(2,1)}, u32[]{:S(2)}) copy-start(bf16[512,4,128]{2,1,0:T(4,128)(2,1)} %refs_0_.1) | copy-start | bytes 1572868
  11.5 8.7 %copy-start.9 = (bf16[512,4,128]{2,1,0:T(4,128)(2,1)S(1)}, bf16[512,4,128]{2,1,0:T(4,128)(2,1)}, u32[]{:S(2)}) copy-start(bf16[512,4,128]{2,1,0:T(4,128)(2,1)} %param.13) | copy-start | bytes 1572868
  16.6 3.7 %copy-start.5 = (f32[128]{0:T(128)S(1)}, f32[128]{0:T(128)}, u32[]{:S(2)}) copy-start(f32[128]{0:T(128)} %param.18) | copy-start | bytes 1540
  16.6 12.2 %collective-permute-start.1 = (bf16[2,128,256]{2,1,0:T(8,128)(2,1)S(1)}, bf16[2,128,256]{2,1,0:T(8,128)(2,1)S(1)}, u32[]{:S(2)}, u32[]{:S(2)}) collective-permute-start(bf16[2,128,256]{2,1,0:T(8,128)(2,1)S(1)} %get-tuple-element.46.refs_0_), channel_id=1, source_target_pairs={{0,4},{4,0},{8,12},{12,8},{1,5},{5,1},{9,13},{13,9},{2,6},{6,2},{1... | collective-permute-start | bytes 393224 | tf_op jit(solution)/shard_map/ppermute | solution.py:406
  18.2 10.7 %collective-permute-start.2 = (bf16[2,128,256]{2,1,0:T(8,128)(2,1)S(1)}, bf16[2,128,256]{2,1,0:T(8,128)(2,1)S(1)}, u32[]{:S(2)}, u32[]{:S(2)}) collective-permute-start(bf16[2,128,256]{2,1,0:T(8,128)(2,1)S(1)} %get-tuple-element.46.refs_0_), channel_id=1, source_target_pairs={{0,8},{4,12},{8,0},{12,4},{1,9},{5,13},{9,1},{13,5},{2,10},{6,14},... | collective-permute-start | bytes 393224 | tf_op jit(solution)/shard_map/ppermute | solution.py:406
  18.3 10.5 %collective-permute-start.3 = (bf16[2,128,256]{2,1,0:T(8,128)(2,1)S(1)}, bf16[2,128,256]{2,1,0:T(8,128)(2,1)S(1)}, u32[]{:S(2)}, u32[]{:S(2)}) collective-permute-start(bf16[2,128,256]{2,1,0:T(8,128)(2,1)S(1)} %get-tuple-element.46.refs_0_), channel_id=1, source_target_pairs={{0,12},{4,8},{8,4},{12,0},{1,13},{5,9},{9,5},{13,1},{2,14},{6,10},... | collective-permute-start | bytes 393224 | tf_op jit(solution)/shard_map/ppermute | solution.py:406
  25.8 8.1 %collective-permute-start.6 = (bf16[2,128,256]{2,1,0:T(8,128)(2,1)S(1)}, bf16[2,128,256]{2,1,0:T(8,128)(2,1)S(1)}, u32[]{:S(2)}, u32[]{:S(2)}) collective-permute-start(bf16[2,128,256]{2,1,0:T(8,128)(2,1)S(1)} %get-tuple-element.58.refs_0_), channel_id=1, source_target_pairs={{0,8},{4,12},{8,0},{12,4},{1,9},{5,13},{9,1},{13,5},{2,10},{6,14},... | collective-permute-start | bytes 393224 | tf_op jit(solution)/shard_map/ppermute | solution.py:406
  27.4 6.9 %collective-permute-start.7 = (bf16[2,128,256]{2,1,0:T(8,128)(2,1)S(1)}, bf16[2,128,256]{2,1,0:T(8,128)(2,1)S(1)}, u32[]{:S(2)}, u32[]{:S(2)}) collective-permute-start(bf16[2,128,256]{2,1,0:T(8,128)(2,1)S(1)} %get-tuple-element.58.refs_0_), channel_id=1, source_target_pairs={{0,12},{4,8},{8,4},{12,0},{1,13},{5,9},{9,5},{13,1},{2,14},{6,10},... | collective-permute-start | bytes 393224 | tf_op jit(solution)/shard_map/ppermute | solution.py:406
  29.6 2.3 %collective-permute-start.4 = (bf16[2,128,128]{2,1,0:T(8,128)(2,1)S(1)}, bf16[2,128,128]{2,1,0:T(8,128)(2,1)S(1)}, u32[]{:S(2)}, u32[]{:S(2)}) collective-permute-start(bf16[2,128,128]{2,1,0:T(8,128)(2,1)S(1)} %get-tuple-element.50), channel_id=1, source_target_pairs={{0,16},{1,17},{2,18},{3,19},{4,20},{5,21},{6,22},{7,23},{8,24},{9,... | collective-permute-start | bytes 196616 | tf_op jit(solution)/shard_map/ppermute | solution.py:401
  30.9 5.0 %collective-permute-start.5 = (bf16[2,128,256]{2,1,0:T(8,128)(2,1)S(1)}, bf16[2,128,256]{2,1,0:T(8,128)(2,1)S(1)}, u32[]{:S(2)}, u32[]{:S(2)}) collective-permute-start(bf16[2,128,256]{2,1,0:T(8,128)(2,1)S(1)} %get-tuple-element.58.refs_0_), channel_id=1, source_target_pairs={{0,4},{4,0},{8,12},{12,8},{1,5},{5,1},{9,13},{13,9},{2,6},{6,2},{1... | collective-permute-start | bytes 393224 | tf_op jit(solution)/shard_map/ppermute | solution.py:406
  32.3 10.3 %collective-permute-start.10 = (bf16[512,256]{1,0:T(8,128)(2,1)S(1)}, bf16[512,256]{1,0:T(8,128)(2,1)S(1)}, u32[]{:S(2)}, u32[]{:S(2)}) collective-permute-start(bf16[512,256]{1,0:T(8,128)(2,1)S(1)} %shard_map.106), channel_id=1, source_target_pairs={{0,1},{1,2},{2,3},{3,0},{4,5},{5,6},{6,7},{7,4},{8,9},{9,10},{10,1... | collective-permute-start | bytes 786440 | tf_op jit(solution)/shard_map/ppermute | solution.py:623
  36.7 2.2 %collective-permute-start.8 = (bf16[2,128,128]{2,1,0:T(8,128)(2,1)S(1)}, bf16[2,128,128]{2,1,0:T(8,128)(2,1)S(1)}, u32[]{:S(2)}, u32[]{:S(2)}) collective-permute-start(bf16[2,128,128]{2,1,0:T(8,128)(2,1)S(1)} %get-tuple-element.62), channel_id=1, source_target_pairs={{0,16},{1,17},{2,18},{3,19},{4,20},{5,21},{6,22},{7,23},{8,24},{9,... | collective-permute-start | bytes 196616 | tf_op jit(solution)/shard_map/ppermute | solution.py:401
  38.0 3.1 %copy-start = (bf16[2048,1024]{1,0:T(8,128)(2,1)S(1)}, bf16[2048,1024]{1,0:T(8,128)(2,1)}, u32[]{:S(2)}) copy-start(bf16[2048,1024]{1,0:T(8,128)(2,1)} %weights_ref.1) | copy-start | bytes 12582916
  39.2 11.1 %collective-permute-start.9 = (bf16[512,256]{1,0:T(8,128)(2,1)S(1)}, bf16[512,256]{1,0:T(8,128)(2,1)S(1)}, u32[]{:S(2)}, u32[]{:S(2)}) collective-permute-start(bf16[512,256]{1,0:T(8,128)(2,1)S(1)} %shard_map.109), channel_id=1, source_target_pairs={{0,1},{1,2},{2,3},{3,0},{4,5},{5,6},{6,7},{7,4},{8,9},{9,10},{10,1... | collective-permute-start | bytes 786440 | tf_op jit(solution)/shard_map/ppermute | solution.py:623
  42.6 13.4 %collective-permute-start.11 = (bf16[512,256]{1,0:T(8,128)(2,1)S(1)}, bf16[512,256]{1,0:T(8,128)(2,1)S(1)}, u32[]{:S(2)}, u32[]{:S(2)}) collective-permute-start(bf16[512,256]{1,0:T(8,128)(2,1)S(1)} %collective-permute-done.10), channel_id=1, source_target_pairs={{0,1},{1,2},{2,3},{3,0},{4,5},{5,6},{6,7},{7,4},{8,9},{9,10},{10,1... | collective-permute-start | bytes 786440 | tf_op jit(solution)/shard_map/ppermute | solution.py:623
  50.8 11.1 %collective-permute-start.13 = (bf16[512,256]{1,0:T(8,128)(2,1)S(1)}, bf16[512,256]{1,0:T(8,128)(2,1)S(1)}, u32[]{:S(2)}, u32[]{:S(2)}) collective-permute-start(bf16[512,256]{1,0:T(8,128)(2,1)S(1)} %collective-permute-done.9), channel_id=1, source_target_pairs={{0,1},{1,2},{2,3},{3,0},{4,5},{5,6},{6,7},{7,4},{8,9},{9,10},{10,1... | collective-permute-start | bytes 786440 | tf_op jit(solution)/shard_map/ppermute | solution.py:623
  56.0 11.5 %collective-permute-start.12 = (bf16[512,256]{1,0:T(8,128)(2,1)S(1)}, bf16[512,256]{1,0:T(8,128)(2,1)S(1)}, u32[]{:S(2)}, u32[]{:S(2)}) collective-permute-start(bf16[512,256]{1,0:T(8,128)(2,1)S(1)} %collective-permute-done.11), channel_id=1, source_target_pairs={{0,1},{1,2},{2,3},{3,0},{4,5},{5,6},{6,7},{7,4},{8,9},{9,10},{10,1... | collective-permute-start | bytes 786440 | tf_op jit(solution)/shard_map/ppermute | solution.py:623
  61.9 10.5 %collective-permute-start.14 = (bf16[512,256]{1,0:T(8,128)(2,1)S(1)}, bf16[512,256]{1,0:T(8,128)(2,1)S(1)}, u32[]{:S(2)}, u32[]{:S(2)}) collective-permute-start(bf16[512,256]{1,0:T(8,128)(2,1)S(1)} %collective-permute-done.13), channel_id=1, source_target_pairs={{0,1},{1,2},{2,3},{3,0},{4,5},{5,6},{6,7},{7,4},{8,9},{9,10},{10,1... | collective-permute-start | bytes 786440 | tf_op jit(solution)/shard_map/ppermute | solution.py:623
  (2 other events, 2.2 us)

commit v16 on v11

--- a/solution.py
+++ b/solution.py
@@ -190,8 +190,10 @@
     rims[...] = rim_ref[...].astype(F32)
     for g in range(heads):
         h = base + g
-        unit_ref[g] = unit_in_ref[h]
-        value_s[g] = value_in_ref[h]
+        for c in range(1, chunks):
+            unit_ref[g, rows_of(c)] = unit_in_ref[h, rows_of(c)]
+        unit_ref[g, AGAIN:CHUNK] = unit_in_ref[h, AGAIN:CHUNK]
+        value_s[g, AGAIN:CHUNK] = value_in_ref[h, AGAIN:CHUNK]
         for i in range(2):
             padded[g, i, 0:RIM] = rims[(1 + i) * RIM : (2 + i) * RIM, h, :]
             padded[g, i, RIM : RIM + AGAIN] = first_ref[i, h]
@@ -211,7 +213,7 @@
             h = base + g
             cum_col = columns[:, h : h + 1]
             cum_row = cum[h : h + 1]
-            key = unit_ref[g, rows_of(c)]
+            key = unit_in_ref[h, rows_of(c)] if c else unit_ref[g, rows_of(c)]
             fading = jnp.exp(jnp.where(strictly, cum_col - cum_row, FAR))
             strength_col = columns[:, total_heads + h : total_heads + h + 1]
             lowers.append(strength_col * fading * mul(key, key, NT))
@@ -223,12 +225,14 @@
         keep_first = (1 - first).astype(F32)
         keep_second = (1 - second).astype(F32)
         keep_both = keep_first * keep_second
-        key = unit_ref[g, rows_of(c)]
+        h = base + g
+        key = unit_in_ref[h, rows_of(c)] if c else unit_ref[g, rows_of(c)]
+        value = value_in_ref[h, rows_of(c)] if c else value_s[g]
         growth = jnp.exp(cum_col) * jnp.where(first_rows, keep_first, keep_both)
         targets = jnp.concatenate(
             [
                 (strength_col * growth) * key.astype(F32),
-                strength_col * value_s[g, rows_of(c)].astype(F32),
+                strength_col * value.astype(F32),
             ],
             axis=1,
         )
@@ -270,7 +274,7 @@
     base, resets, query_ref, gate_ref, gain_ref, rim_ref, taps_ref, decay_ref, strength_ref,
     unit_ref, solved_ref, starts_ref,
     reach_ref, part_ref, gating_ref,
-    rims, padded, query_s,
+    rims, padded,
 ):
     heads, length, depth = unit_ref.shape
     chunks = length // CHUNK
@@ -281,10 +285,6 @@
         h = base + g
         padded[g, 0:RIM] = rims[0:RIM, h, :]
         padded[g, RIM : RIM + length] = query_ref[h].astype(F32)
-        taps = taps_of(taps_ref, 0, h)
-        for c in range(chunks):
-            rows = filtered(padded.at[g], taps, c * CHUNK, CHUNK)
-            query_s[g, rows_of(c)] = (unit(rows) * depth**-0.5).astype(BF16)
 
     for c in range(chunks):
         here = rows_of(c)
@@ -296,7 +296,8 @@
         for g in range(heads):
             h = base + g
             cum_col = columns[:, h : h + 1]
-            query = query_s[g, here]
+            filtered_rows = filtered(padded.at[g], taps_of(taps_ref, 0, h), c * CHUNK, CHUNK)
+            query = (unit(filtered_rows) * depth**-0.5).astype(BF16)
             fading = jnp.exp(jnp.where(upto, cum_col - cum[h : h + 1], FAR))
             mixing = fading * mul(query, unit_ref[g, here], NT)
             own = mul_split(mixing, solved_ref[g, here])
@@ -415,7 +416,7 @@
         in_specs=[HBM] * len(inputs),
         out_specs=VMEM,
         scratch_shapes=[pltpu.SemaphoreType.DMA((len(inputs),))],
-        compiler_params=pltpu.CompilerParams(vmem_limit_bytes=63 * 2**20),
+        compiler_params=pltpu.CompilerParams(vmem_limit_bytes=65_700_000),
         cost_estimate=pl.CostEstimate(flops=10**9, bytes_accessed=2**16, transcendentals=0),
     )(*inputs)
 
@@ -452,7 +453,7 @@
         scratch_shapes=[
             pltpu.VMEM(rims.shape, F32),
             pltpu.VMEM((heads, 2, RIM + AGAIN, depth), F32),
-            pltpu.VMEM((heads, length, depth), BF16),
+            pltpu.VMEM((heads, CHUNK, depth), BF16),
             pltpu.VMEM((heads, chunks, depth, 2 * depth), F32),
         ],
         compiler_params=PARAMS,
@@ -473,7 +474,6 @@
         scratch_shapes=[
             pltpu.VMEM(rims.shape, F32),
             pltpu.VMEM((heads, length + RIM, depth), F32),
-            pltpu.VMEM((heads, length, depth), BF16),
         ],
         compiler_params=PARAMS,
         cost_estimate=pl.CostEstimate(

time: 71.5 us -> 71.4 us (level)
  no operation moved by 1% of the time
where the time goes in v16:
time: 71.4 us; the launch traced here: 71.2 us
  waiting for transfers between devices  28.5 us (40%)
  starting transfers between devices  18.6 us (26%)
  Pallas kernels  17.9 us (25%)
  matrix products  4.35 us (6%)
  local copies, waits for them, and re-layouts  1.37 us (2%)
    ppermute x6, waiting for transfers between devices, on_device(): lax.ppermute(x, 'head', around)  27.3 us
    ppermute x3, starting transfers between devices, from_behind(): lax.ppermute(value, axis, [(i, i + steps) for i in range(count - steps)])  8.02 us
    ppermute x6, starting transfers between devices, exchange(): lax.ppermute(own_map, 'leaf', pairs_at(k, leaves))  7.11 us
    pallas_call x1, Pallas kernels, reads_of(): pl.pallas_call(functools.partial(reads_kernel, base), out_shape=(jax.Shap...  5.42 us
    pallas_call x1, Pallas kernels, maps_of(): pl.pallas_call(functools.partial(maps_kernel, base), out_shape=(jax.Shape...  5.05 us
    dot_general x7, matrix products, on_device(): term = jnp.dot(block, rows, preferred_element_type=F32)  4.35 us
    ppermute x6, starting transfers between devices, on_device(): lax.ppermute(x, 'head', around)  3.46 us
    pallas_call x1, Pallas kernels, filters_of(): pl.pallas_call(filters_kernel, out_shape=(per_token, per_token, jax.Shape...  1.78 us
  transfers between devices with their start and end apart: 15, of which 8 were waited for; matrix products, arithmetic and copies ran while one was open for 8% of the time, Pallas kernels for 13%

profile of v16, /device:TPU:0, one launch (start us, length us, event | category | flops | bytes accessed | tf_op | source)
XLA Modules:
  0.0 71.2 jit_solution(8965496453853234565)
XLA Ops:
  0.0 1.4 %shard_map.101 = bf16[24,4,128]{2,1,0:T(4,128)(2,1)} custom-call(bf16[512,4,128]{2,1,0:T(4,128)(2,1)} %refs_0_.1, bf16[512,4,128]{2,1,0:T(4,128)(2,1)} %refs_1_.1, bf16[512,4,128]{2,1,0:T(4,128)(2,1)} %refs_2_.1), custom_call_target="tpu_custom_call" | custom-call | flops 1000000000 | bytes 65536 | tf_op jit(solution)/shard_map/pallas_call | solution.py:413
  1.4 4.8 %collective-permute-start = (bf16[24,4,128]{2,1,0:T(4,128)(2,1)}, bf16[24,4,128]{2,1,0:T(4,128)(2,1)S(1)}, u32[]{:S(2)}, u32[]{:S(2)}) collective-permute-start(bf16[24,4,128]{2,1,0:T(4,128)(2,1)} %shard_map.101), channel_id=1, source_target_pairs={{0,4},{4,8},{8,12},{12,16},{16,20},{20,24},{24,28},{1,5},{5,9},{9,... | collective-permute-start | bytes 73736 | tf_op jit(solution)/shard_map/ppermute | solution.py:396
  6.3 1.2 %copy_bitcast_fusion.2 = (bf16[4,512,128]{2,1,0:T(8,128)(2,1)S(1)}, bf16[4,512,128]{2,1,0:T(8,128)(2,1)S(1)}) fusion(bf16[512,4,128]{2,1,0:T(4,128)(2,1)S(1)} %copy-done.8, bf16[512,4,128]{2,1,0:T(4,128)(2,1)} %refs_1_.1), kind=kLoop, calls=%fused_computation.4 | loop fusion | bytes 2097152 | tf_op jit(solution)/shard_map/transpose | solution.py:550
  7.5 1.8 %shard_map.100 = (bf16[4,512,128]{2,1,0:T(8,128)(2,1)S(1)}, bf16[4,512,128]{2,1,0:T(8,128)(2,1)S(1)}, f32[2,4,16,128]{3,2,1,0:T(8,128)S(1)}) custom-call(bf16[4,512,128]{2,1,0:T(8,128)(2,1)S(1)} %get-tuple-element.58.key_ref, bf16[4,512,128]{2,1,0:T(8,128)(2,1)S(1)} %get-tuple-element.57.value_ref, f32[3,4,4,128]{3,2,1,0:T(4,128)S(1)} %copy-done.1), custom_call_target="tpu_custom_call" | custom-call | flops 3000000000 | bytes 4194304 | tf_op jit(solution)/shard_map/pallas_call | solution.py:427
  9.4 5.1 %shard_map.102 = (bf16[4,512,128]{2,1,0:T(8,128)(2,1)S(1)}, f32[4,512,256]{2,1,0:T(8,128)S(1)}, f32[4,3,128,256]{3,2,1,0:T(8,128)S(1)}, bf16[2,128,256]{2,1,0:T(8,128)(2,1)S(1)}, bf16[2,128,256]{2,1,0:T(8,128)(2,1)S(1)}) custom-call(s32[8]{0:T(128)S(1)} %copy-done.4, bf16[4,512,128]{2,1,0:T(8,128)(2,1)S(1)} %get-tuple-element.31.unit_in_ref, ...), custom_call_target="tpu_custom_call" | custom-call | flops 5000000000 | bytes 4194304 | tf_op jit(solution)/shard_map/pallas_call | solution.py:443
  14.5 1.6 %collective-permute-start.1 = (bf16[2,128,256]{2,1,0:T(8,128)(2,1)S(1)}, bf16[2,128,256]{2,1,0:T(8,128)(2,1)S(1)}, u32[]{:S(2)}, u32[]{:S(2)}) collective-permute-start(bf16[2,128,256]{2,1,0:T(8,128)(2,1)S(1)} %get-tuple-element.42.refs_0_), channel_id=1, source_target_pairs={{0,4},{4,0},{8,12},{12,8},{1,5},{5,1},{9,13},{13,9},{2,6},{6,2},{1... | collective-permute-start | bytes 393224 | tf_op jit(solution)/shard_map/ppermute | solution.py:400
  16.0 1.0 %collective-permute-start.2 = (bf16[2,128,256]{2,1,0:T(8,128)(2,1)S(1)}, bf16[2,128,256]{2,1,0:T(8,128)(2,1)S(1)}, u32[]{:S(2)}, u32[]{:S(2)}) collective-permute-start(bf16[2,128,256]{2,1,0:T(8,128)(2,1)S(1)} %get-tuple-element.42.refs_0_), channel_id=1, source_target_pairs={{0,8},{4,12},{8,0},{12,4},{1,9},{5,13},{9,1},{13,5},{2,10},{6,14},... | collective-permute-start | bytes 393224 | tf_op jit(solution)/shard_map/ppermute | solution.py:400
  17.0 1.0 %collective-permute-start.3 = (bf16[2,128,256]{2,1,0:T(8,128)(2,1)S(1)}, bf16[2,128,256]{2,1,0:T(8,128)(2,1)S(1)}, u32[]{:S(2)}, u32[]{:S(2)}) collective-permute-start(bf16[2,128,256]{2,1,0:T(8,128)(2,1)S(1)} %get-tuple-element.42.refs_0_), channel_id=1, source_target_pairs={{0,12},{4,8},{8,4},{12,0},{1,13},{5,9},{9,5},{13,1},{2,14},{6,10},... | collective-permute-start | bytes 393224 | tf_op jit(solution)/shard_map/ppermute | solution.py:400
  18.2 5.4 %shard_map.103 = (bf16[4,512,128]{2,1,0:T(8,128)(2,1)S(1)}, f32[4,512,128]{2,1,0:T(8,128)S(1)}, f32[4,512,128]{2,1,0:T(8,128)S(1)}) custom-call(s32[8]{0:T(128)S(1)} %copy-done.4, bf16[4,512,128]{2,1,0:T(8,128)(2,1)S(1)} %bitcast.21, bf16[4,512,128]{2,1,0:T(8,128)(2,1)S(1)} %bitcast.20, f32[1,128]{1,0:T(1,128)S(1)} %bitcast.22, ...), custom_call_target="tpu_custom_call" | custom-call | flops 3000000000 | bytes 4194304 | tf_op jit(solution)/shard_map/pallas_call | solution.py:469
  24.4 2.0 %collective-permute-start.10 = (bf16[2,128,256]{2,1,0:T(8,128)(2,1)S(1)}, bf16[2,128,256]{2,1,0:T(8,128)(2,1)S(1)}, u32[]{:S(2)}, u32[]{:S(2)}) collective-permute-start(bf16[2,128,256]{2,1,0:T(8,128)(2,1)S(1)} %get-tuple-element.51.refs_0_), channel_id=1, source_target_pairs={{0,12},{4,8},{8,4},{12,0},{1,13},{5,9},{9,5},{13,1},{2,14},{6,10},... | collective-permute-start | bytes 393224 | tf_op jit(solution)/shard_map/ppermute | solution.py:400
  26.4 1.4 %collective-permute-start.8 = (bf16[2,128,256]{2,1,0:T(8,128)(2,1)S(1)}, bf16[2,128,256]{2,1,0:T(8,128)(2,1)S(1)}, u32[]{:S(2)}, u32[]{:S(2)}) collective-permute-start(bf16[2,128,256]{2,1,0:T(8,128)(2,1)S(1)} %get-tuple-element.51.refs_0_), channel_id=1, source_target_pairs={{0,4},{4,0},{8,12},{12,8},{1,5},{5,1},{9,13},{13,9},{2,6},{6,2},{1... | collective-permute-start | bytes 393224 | tf_op jit(solution)/shard_map/ppermute | solution.py:400
  28.0 1.3 %collective-permute-start.4 = (bf16[2,128,128]{2,1,0:T(8,128)(2,1)S(1)}, bf16[2,128,128]{2,1,0:T(8,128)(2,1)S(1)}, u32[]{:S(2)}, u32[]{:S(2)}) collective-permute-start(bf16[2,128,128]{2,1,0:T(8,128)(2,1)S(1)} %get-tuple-element.46), channel_id=1, source_target_pairs={{0,16},{1,17},{2,18},{3,19},{4,20},{5,21},{6,22},{7,23},{8,24},{9,... | collective-permute-start | bytes 196616 | tf_op jit(solution)/shard_map/ppermute | solution.py:396
  29.3 0.8 %collective-permute-done.4.arrived_ref = bf16[2,128,128]{2,1,0:T(8,128)(2,1)S(1)} collective-permute-done((bf16[2,128,128]{2,1,0:T(8,128)(2,1)S(1)}, bf16[2,128,128]{2,1,0:T(8,128)(2,1)S(1)}, u32[]{:S(2)}, u32[]{:S(2)}) %collective-permute-start.4) | collective-permute-done | bytes 65568 | tf_op jit(solution)/shard_map/ppermute | solution.py:396
  30.9 1.6 %collective-permute-start.5 = (bf16[512,256]{1,0:T(8,128)(2,1)S(1)}, bf16[512,256]{1,0:T(8,128)(2,1)S(1)}, u32[]{:S(2)}, u32[]{:S(2)}) collective-permute-start(bf16[512,256]{1,0:T(8,128)(2,1)S(1)} %shard_map.105), channel_id=1, source_target_pairs={{0,1},{1,2},{2,3},{3,0},{4,5},{5,6},{6,7},{7,4},{8,9},{9,10},{10,1... | collective-permute-start | bytes 786440 | tf_op jit(solution)/shard_map/ppermute | solution.py:592
  33.5 1.9 %collective-permute-start.11 = (bf16[2,128,128]{2,1,0:T(8,128)(2,1)S(1)}, bf16[2,128,128]{2,1,0:T(8,128)(2,1)S(1)}, u32[]{:S(2)}, u32[]{:S(2)}) collective-permute-start(bf16[2,128,128]{2,1,0:T(8,128)(2,1)S(1)} %get-tuple-element.55), channel_id=1, source_target_pairs={{0,16},{1,17},{2,18},{3,19},{4,20},{5,21},{6,22},{7,23},{8,24},{9,... | collective-permute-start | bytes 196616 | tf_op jit(solution)/shard_map/ppermute | solution.py:396
  35.4 1.6 %fusion.10 = f32[512,1024]{1,0:T(8,128)S(1)} fusion(bf16[512,256]{1,0:T(8,128)(2,1)S(1)} %shard_map.105, bf16[2048,1024]{1,0:T(8,128)(2,1)} %weights_ref.1, s32[]{:T(128)S(6)} %select_n.21), kind=kOutput, calls=%fused_computation.16 | convolution fusion | flops 268435456 | bytes 2883588 | tf_op jit(solution)/shard_map/dot_general | solution.py:598
  37.8 1.6 %collective-permute-start.12 = (bf16[512,256]{1,0:T(8,128)(2,1)S(1)}, bf16[512,256]{1,0:T(8,128)(2,1)S(1)}, u32[]{:S(2)}, u32[]{:S(2)}) collective-permute-start(bf16[512,256]{1,0:T(8,128)(2,1)S(1)} %shard_map.107), channel_id=1, source_target_pairs={{0,1},{1,2},{2,3},{3,0},{4,5},{5,6},{6,7},{7,4},{8,9},{9,10},{10,1... | collective-permute-start | bytes 786440 | tf_op jit(solution)/shard_map/ppermute | solution.py:592
  39.9 1.4 %collective-permute-done.5 = bf16[512,256]{1,0:T(8,128)(2,1)S(1)} collective-permute-done((bf16[512,256]{1,0:T(8,128)(2,1)S(1)}, bf16[512,256]{1,0:T(8,128)(2,1)S(1)}, u32[]{:S(2)}, u32[]{:S(2)}) %collective-permute-start.5) | collective-permute-done | bytes 262176 | tf_op jit(solution)/shard_map/ppermute | solution.py:592
  42.0 6.9 %collective-permute-done.12 = bf16[512,256]{1,0:T(8,128)(2,1)S(1)} collective-permute-done((bf16[512,256]{1,0:T(8,128)(2,1)S(1)}, bf16[512,256]{1,0:T(8,128)(2,1)S(1)}, u32[]{:S(2)}, u32[]{:S(2)}) %collective-permute-start.12) | collective-permute-done | bytes 262176 | tf_op jit(solution)/shard_map/ppermute | solution.py:592
  49.4 5.2 %collective-permute-done.6 = bf16[512,256]{1,0:T(8,128)(2,1)S(1)} collective-permute-done((bf16[512,256]{1,0:T(8,128)(2,1)S(1)}, bf16[512,256]{1,0:T(8,128)(2,1)S(1)}, u32[]{:S(2)}, u32[]{:S(2)}) %collective-permute-start.6) | collective-permute-done | bytes 262176 | tf_op jit(solution)/shard_map/ppermute | solution.py:592
  55.0 5.2 %collective-permute-done.13 = bf16[512,256]{1,0:T(8,128)(2,1)S(1)} collective-permute-done((bf16[512,256]{1,0:T(8,128)(2,1)S(1)}, bf16[512,256]{1,0:T(8,128)(2,1)S(1)}, u32[]{:S(2)}, u32[]{:S(2)}) %collective-permute-start.13) | collective-permute-done | bytes 262176 | tf_op jit(solution)/shard_map/ppermute | solution.py:592
  60.6 5.1 %collective-permute-done.7 = bf16[512,256]{1,0:T(8,128)(2,1)S(1)} collective-permute-done((bf16[512,256]{1,0:T(8,128)(2,1)S(1)}, bf16[512,256]{1,0:T(8,128)(2,1)S(1)}, u32[]{:S(2)}, u32[]{:S(2)}) %collective-permute-start.7) | collective-permute-done | bytes 262176 | tf_op jit(solution)/shard_map/ppermute | solution.py:592
  66.2 3.5 %collective-permute-done.14.block_ref = bf16[512,256]{1,0:T(8,128)(2,1)S(1)} collective-permute-done((bf16[512,256]{1,0:T(8,128)(2,1)S(1)}, bf16[512,256]{1,0:T(8,128)(2,1)S(1)}, u32[]{:S(2)}, u32[]{:S(2)}) %collective-permute-start.14) | collective-permute-done | bytes 262176 | tf_op jit(solution)/shard_map/ppermute | solution.py:592
  69.7 1.3 %shard_map.108 = bf16[512,1024]{1,0:T(8,128)(2,1)} custom-call(s32[1]{0:T(128)} %bitcast.section, f32[512,1024]{1,0:T(8,128)S(1)} %add_add_fusion.1.first_ref, f32[512,1024]{1,0:T(8,128)S(1)} %add_add_fusion.second_ref, bf16[512,256]{1,0:T(8,128)(2,1)S(1)} %collective-permute-done.14.block_ref, bf16[2048,1024]{1,0:T(8,128)(2,1)S(1)} %copy-done), custom_call_target="tpu_custom_call" | custom-call | tf_op jit(solution)/shard_map/pallas_call | solution.py:518
  (43 shorter events, 6.5 us)
Async XLA Ops:
  0.0 6.3 %copy-start.8 = (bf16[512,4,128]{2,1,0:T(4,128)(2,1)S(1)}, bf16[512,4,128]{2,1,0:T(4,128)(2,1)}, u32[]{:S(2)}) copy-start(bf16[512,4,128]{2,1,0:T(4,128)(2,1)} %refs_2_.1) | copy-start | bytes 1572868
  0.0 7.5 %copy-start.1 = (f32[3,4,4,128]{3,2,1,0:T(4,128)S(1)}, f32[3,4,4,128]{3,2,1,0:T(4,128)}, u32[]{:S(2)}) copy-start(f32[3,4,4,128]{3,2,1,0:T(4,128)} %taps_ref.5) | copy-start | bytes 73732
  1.4 7.9 %collective-permute-start = (bf16[24,4,128]{2,1,0:T(4,128)(2,1)}, bf16[24,4,128]{2,1,0:T(4,128)(2,1)S(1)}, u32[]{:S(2)}, u32[]{:S(2)}) collective-permute-start(bf16[24,4,128]{2,1,0:T(4,128)(2,1)} %shard_map.101), channel_id=1, source_target_pairs={{0,4},{4,8},{8,12},{12,16},{16,20},{20,24},{24,28},{1,5},{5,9},{9,... | collective-permute-start | bytes 73736 | tf_op jit(solution)/shard_map/ppermute | solution.py:396
  7.5 1.8 %copy-start.2 = (f32[4,512]{1,0:T(4,128)S(1)}, f32[4,512]{1,0:T(4,128)}, u32[]{:S(2)}) copy-start(f32[4,512]{1,0:T(4,128)} %decay_ref.3) | copy-start | bytes 24580
  7.5 1.8 %copy-start.3 = (f32[4,512]{1,0:T(4,128)S(1)}, f32[4,512]{1,0:T(4,128)}, u32[]{:S(2)}) copy-start(f32[4,512]{1,0:T(4,128)} %strength_ref.3) | copy-start | bytes 24580
  7.5 1.8 %copy-start.4 = (s32[8]{0:T(128)S(1)}, s32[8]{0:T(128)}, u32[]{:S(2)}) copy-start(s32[8]{0:T(128)} %resets.3) | copy-start | bytes 100
  9.4 8.7 %copy-start.6 = (bf16[512,4,128]{2,1,0:T(4,128)(2,1)S(1)}, bf16[512,4,128]{2,1,0:T(4,128)(2,1)}, u32[]{:S(2)}) copy-start(bf16[512,4,128]{2,1,0:T(4,128)(2,1)} %param.13) | copy-start | bytes 1572868
  9.4 8.7 %copy-start.7 = (bf16[512,4,128]{2,1,0:T(4,128)(2,1)S(1)}, bf16[512,4,128]{2,1,0:T(4,128)(2,1)}, u32[]{:S(2)}) copy-start(bf16[512,4,128]{2,1,0:T(4,128)(2,1)} %refs_0_.1) | copy-start | bytes 1572868
  14.4 3.7 %copy-start.5 = (f32[128]{0:T(128)S(1)}, f32[128]{0:T(128)}, u32[]{:S(2)}) copy-start(f32[128]{0:T(128)} %param.18) | copy-start | bytes 1540
  14.5 9.2 %collective-permute-start.1 = (bf16[2,128,256]{2,1,0:T(8,128)(2,1)S(1)}, bf16[2,128,256]{2,1,0:T(8,128)(2,1)S(1)}, u32[]{:S(2)}, u32[]{:S(2)}) collective-permute-start(bf16[2,128,256]{2,1,0:T(8,128)(2,1)S(1)} %get-tuple-element.42.refs_0_), channel_id=1, source_target_pairs={{0,4},{4,0},{8,12},{12,8},{1,5},{5,1},{9,13},{13,9},{2,6},{6,2},{1... | collective-permute-start | bytes 393224 | tf_op jit(solution)/shard_map/ppermute | solution.py:400
  16.0 7.6 %collective-permute-start.2 = (bf16[2,128,256]{2,1,0:T(8,128)(2,1)S(1)}, bf16[2,128,256]{2,1,0:T(8,128)(2,1)S(1)}, u32[]{:S(2)}, u32[]{:S(2)}) collective-permute-start(bf16[2,128,256]{2,1,0:T(8,128)(2,1)S(1)} %get-tuple-element.42.refs_0_), channel_id=1, source_target_pairs={{0,8},{4,12},{8,0},{12,4},{1,9},{5,13},{9,1},{13,5},{2,10},{6,14},... | collective-permute-start | bytes 393224 | tf_op jit(solution)/shard_map/ppermute | solution.py:400
  17.0 6.6 %collective-permute-start.3 = (bf16[2,128,256]{2,1,0:T(8,128)(2,1)S(1)}, bf16[2,128,256]{2,1,0:T(8,128)(2,1)S(1)}, u32[]{:S(2)}, u32[]{:S(2)}) collective-permute-start(bf16[2,128,256]{2,1,0:T(8,128)(2,1)S(1)} %get-tuple-element.42.refs_0_), channel_id=1, source_target_pairs={{0,12},{4,8},{8,4},{12,0},{1,13},{5,9},{9,5},{13,1},{2,14},{6,10},... | collective-permute-start | bytes 393224 | tf_op jit(solution)/shard_map/ppermute | solution.py:400
  24.4 8.1 %collective-permute-start.10 = (bf16[2,128,256]{2,1,0:T(8,128)(2,1)S(1)}, bf16[2,128,256]{2,1,0:T(8,128)(2,1)S(1)}, u32[]{:S(2)}, u32[]{:S(2)}) collective-permute-start(bf16[2,128,256]{2,1,0:T(8,128)(2,1)S(1)} %get-tuple-element.51.refs_0_), channel_id=1, source_target_pairs={{0,12},{4,8},{8,4},{12,0},{1,13},{5,9},{9,5},{13,1},{2,14},{6,10},... | collective-permute-start | bytes 393224 | tf_op jit(solution)/shard_map/ppermute | solution.py:400
  26.4 6.1 %collective-permute-start.8 = (bf16[2,128,256]{2,1,0:T(8,128)(2,1)S(1)}, bf16[2,128,256]{2,1,0:T(8,128)(2,1)S(1)}, u32[]{:S(2)}, u32[]{:S(2)}) collective-permute-start(bf16[2,128,256]{2,1,0:T(8,128)(2,1)S(1)} %get-tuple-element.51.refs_0_), channel_id=1, source_target_pairs={{0,4},{4,0},{8,12},{12,8},{1,5},{5,1},{9,13},{13,9},{2,6},{6,2},{1... | collective-permute-start | bytes 393224 | tf_op jit(solution)/shard_map/ppermute | solution.py:400
  27.8 5.0 %collective-permute-start.9 = (bf16[2,128,256]{2,1,0:T(8,128)(2,1)S(1)}, bf16[2,128,256]{2,1,0:T(8,128)(2,1)S(1)}, u32[]{:S(2)}, u32[]{:S(2)}) collective-permute-start(bf16[2,128,256]{2,1,0:T(8,128)(2,1)S(1)} %get-tuple-element.51.refs_0_), channel_id=1, source_target_pairs={{0,8},{4,12},{8,0},{12,4},{1,9},{5,13},{9,1},{13,5},{2,10},{6,14},... | collective-permute-start | bytes 393224 | tf_op jit(solution)/shard_map/ppermute | solution.py:400
  28.0 2.2 %collective-permute-start.4 = (bf16[2,128,128]{2,1,0:T(8,128)(2,1)S(1)}, bf16[2,128,128]{2,1,0:T(8,128)(2,1)S(1)}, u32[]{:S(2)}, u32[]{:S(2)}) collective-permute-start(bf16[2,128,128]{2,1,0:T(8,128)(2,1)S(1)} %get-tuple-element.46), channel_id=1, source_target_pairs={{0,16},{1,17},{2,18},{3,19},{4,20},{5,21},{6,22},{7,23},{8,24},{9,... | collective-permute-start | bytes 196616 | tf_op jit(solution)/shard_map/ppermute | solution.py:396
  30.9 10.5 %collective-permute-start.5 = (bf16[512,256]{1,0:T(8,128)(2,1)S(1)}, bf16[512,256]{1,0:T(8,128)(2,1)S(1)}, u32[]{:S(2)}, u32[]{:S(2)}) collective-permute-start(bf16[512,256]{1,0:T(8,128)(2,1)S(1)} %shard_map.105), channel_id=1, source_target_pairs={{0,1},{1,2},{2,3},{3,0},{4,5},{5,6},{6,7},{7,4},{8,9},{9,10},{10,1... | collective-permute-start | bytes 786440 | tf_op jit(solution)/shard_map/ppermute | solution.py:592
  33.5 3.6 %collective-permute-start.11 = (bf16[2,128,128]{2,1,0:T(8,128)(2,1)S(1)}, bf16[2,128,128]{2,1,0:T(8,128)(2,1)S(1)}, u32[]{:S(2)}, u32[]{:S(2)}) collective-permute-start(bf16[2,128,128]{2,1,0:T(8,128)(2,1)S(1)} %get-tuple-element.55), channel_id=1, source_target_pairs={{0,16},{1,17},{2,18},{3,19},{4,20},{5,21},{6,22},{7,23},{8,24},{9,... | collective-permute-start | bytes 196616 | tf_op jit(solution)/shard_map/ppermute | solution.py:396
  35.4 4.0 %copy-start = (bf16[2048,1024]{1,0:T(8,128)(2,1)S(1)}, bf16[2048,1024]{1,0:T(8,128)(2,1)}, u32[]{:S(2)}) copy-start(bf16[2048,1024]{1,0:T(8,128)(2,1)} %weights_ref.1) | copy-start | bytes 12582916
  37.8 11.1 %collective-permute-start.12 = (bf16[512,256]{1,0:T(8,128)(2,1)S(1)}, bf16[512,256]{1,0:T(8,128)(2,1)S(1)}, u32[]{:S(2)}, u32[]{:S(2)}) collective-permute-start(bf16[512,256]{1,0:T(8,128)(2,1)S(1)} %shard_map.107), channel_id=1, source_target_pairs={{0,1},{1,2},{2,3},{3,0},{4,5},{5,6},{6,7},{7,4},{8,9},{9,10},{10,1... | collective-permute-start | bytes 786440 | tf_op jit(solution)/shard_map/ppermute | solution.py:592
  41.3 13.2 %collective-permute-start.6 = (bf16[512,256]{1,0:T(8,128)(2,1)S(1)}, bf16[512,256]{1,0:T(8,128)(2,1)S(1)}, u32[]{:S(2)}, u32[]{:S(2)}) collective-permute-start(bf16[512,256]{1,0:T(8,128)(2,1)S(1)} %collective-permute-done.5), channel_id=1, source_target_pairs={{0,1},{1,2},{2,3},{3,0},{4,5},{5,6},{6,7},{7,4},{8,9},{9,10},{10,1... | collective-permute-start | bytes 786440 | tf_op jit(solution)/shard_map/ppermute | solution.py:592
  48.9 11.2 %collective-permute-start.13 = (bf16[512,256]{1,0:T(8,128)(2,1)S(1)}, bf16[512,256]{1,0:T(8,128)(2,1)S(1)}, u32[]{:S(2)}, u32[]{:S(2)}) collective-permute-start(bf16[512,256]{1,0:T(8,128)(2,1)S(1)} %collective-permute-done.12), channel_id=1, source_target_pairs={{0,1},{1,2},{2,3},{3,0},{4,5},{5,6},{6,7},{7,4},{8,9},{9,10},{10,1... | collective-permute-start | bytes 786440 | tf_op jit(solution)/shard_map/ppermute | solution.py:592
  54.5 11.2 %collective-permute-start.7 = (bf16[512,256]{1,0:T(8,128)(2,1)S(1)}, bf16[512,256]{1,0:T(8,128)(2,1)S(1)}, u32[]{:S(2)}, u32[]{:S(2)}) collective-permute-start(bf16[512,256]{1,0:T(8,128)(2,1)S(1)} %collective-permute-done.6), channel_id=1, source_target_pairs={{0,1},{1,2},{2,3},{3,0},{4,5},{5,6},{6,7},{7,4},{8,9},{9,10},{10,1... | collective-permute-start | bytes 786440 | tf_op jit(solution)/shard_map/ppermute | solution.py:592
  60.1 9.6 %collective-permute-start.14 = (bf16[512,256]{1,0:T(8,128)(2,1)S(1)}, bf16[512,256]{1,0:T(8,128)(2,1)S(1)}, u32[]{:S(2)}, u32[]{:S(2)}) collective-permute-start(bf16[512,256]{1,0:T(8,128)(2,1)S(1)} %collective-permute-done.13), channel_id=1, source_target_pairs={{0,1},{1,2},{2,3},{3,0},{4,5},{5,6},{6,7},{7,4},{8,9},{9,10},{10,1... | collective-permute-start | bytes 786440 | tf_op jit(solution)/shard_map/ppermute | solution.py:592

commit v17 on v16

--- a/solution.py
+++ b/solution.py
@@ -35,6 +35,14 @@
     a_high, a_low = split(a)
     b_high, b_low = split(b)
     return mul(a_high, b_high) + (mul(a_low, b_high) + mul(a_high, b_low))
+
+
+def mul_stacked(a, b_high, b_low=None):
+    rows = a.shape[0]
+    a_high, a_low = split(a)
+    both = mul(jnp.concatenate([a_high, a_low], axis=0), b_high)
+    product = both[:rows] + both[rows:]
+    return product if b_low is None else product + mul(a_high, b_low)
 
 
 def rows_of(c):
@@ -256,7 +264,7 @@
     half = chunks // 2
     for c in range(1, half):
         for g in every:
-            starts_ref[g, c - 1] = states[g]
+            starts_ref[g, c - 1] = states[g].astype(BF16)
         states = [compose(step_s[g, c], states[g]) for g in every]
     rest = [step_s[g, half] for g in every]
     for c in range(half + 1, chunks):
@@ -265,7 +273,7 @@
         map_refs[g // size][g % size] = compose(rest[g], states[g]).astype(BF16)
     for c in range(half, chunks):
         for g in every:
-            starts_ref[g, c - 1] = states[g]
+            starts_ref[g, c - 1] = states[g].astype(BF16)
         if c + 1 < chunks:
             states = [compose(step_s[g, c], states[g]) for g in every]
 
@@ -300,12 +308,12 @@
             query = (unit(filtered_rows) * depth**-0.5).astype(BF16)
             fading = jnp.exp(jnp.where(upto, cum_col - cum[h : h + 1], FAR))
             mixing = fading * mul(query, unit_ref[g, here], NT)
-            own = mul_split(mixing, solved_ref[g, here])
+            own = mul_stacked(mixing, *split(solved_ref[g, here]))
             growth = jnp.exp(cum_col) * jnp.where(first_rows, keep_first, keep_both)
             reach = growth * query.astype(F32) - own[:, :depth]
             part = own[:, depth:]
             if c:
-                both = mul_split(reach, starts_ref[g, c - 1])
+                both = mul_stacked(reach, starts_ref[g, c - 1])
                 reach = both[:, :depth]
                 part = part + both[:, depth:]
             reach_ref[g, here] = reach.astype(BF16)
@@ -377,6 +385,31 @@
             ).astype(BF16)
 
 
+def placed_kernel(base, before_ref, reach_ref, part_ref, through_ref, fixed_ref):
+    heads, depth, _ = before_ref.shape
+    for g in range(heads):
+        high, low = split(before_ref[g])
+        for c in range(through_ref.shape[1] // CHUNK):
+            here = rows_of(c)
+            reach = reach_ref[base + g, here]
+            both = mul(reach, high) + mul(reach, low)
+            through_ref[g, here] = both[:, :depth].astype(BF16)
+            fixed_ref[g, here] = part_ref[base + g, here] + both[:, depth:]
+
+
+def placed_outputs_kernel(base, arrived_ref, through_ref, fixed_ref, gating_ref, normed_ref):
+    heads, depth, _ = arrived_ref.shape
+    for g in range(heads):
+        arrived = arrived_ref[g]
+        for c in range(normed_ref.shape[0] // CHUNK):
+            here = rows_of(c)
+            core = fixed_ref[g, here] + mul(through_ref[g, here], arrived)
+            scale = lax.rsqrt(jnp.sum(core * core, axis=-1, keepdims=True) / depth + EPSILON)
+            normed_ref[here, g * depth : (g + 1) * depth] = (
+                core * scale * gating_ref[base + g, here]
+            ).astype(BF16)
+
+
 def last_kernel(section, first_ref, second_ref, block_ref, weights_ref, out_ref, tiles, written):
     width = block_ref.shape[1]
     rows = weights_ref[pl.ds(pl.multiple_of(section[0] * width, width), width), :]
@@ -445,7 +478,7 @@
         out_shape=(
             jax.ShapeDtypeStruct((heads, length, depth), BF16),
             jax.ShapeDtypeStruct((heads, length, 2 * depth), F32),
-            jax.ShapeDtypeStruct((heads, chunks - 1, depth, 2 * depth), F32),
+            jax.ShapeDtypeStruct((heads, chunks - 1, depth, 2 * depth), BF16),
             *[jax.ShapeDtypeStruct((heads // GROUPS, depth, 2 * depth), BF16)] * GROUPS,
         ),
         in_specs=[SMEM] + [VMEM] * 7,
@@ -511,6 +544,35 @@
         out_specs=VMEM,
         compiler_params=PARAMS,
     )(arrived, before, *reads)
+
+
+def placed_of(base, before, reach, part):
+    heads, depth, _ = before.shape
+    length = reach.shape[1]
+    per_token = (heads, length, depth)
+    return pl.pallas_call(
+        functools.partial(placed_kernel, base),
+        out_shape=(
+            jax.ShapeDtypeStruct(per_token, BF16),
+            jax.ShapeDtypeStruct(per_token, F32),
+        ),
+        in_specs=[VMEM] * 3,
+        out_specs=[VMEM] * 2,
+        compiler_params=PARAMS,
+        cost_estimate=pl.CostEstimate(flops=2 * 10**9, bytes_accessed=2**20, transcendentals=0),
+    )(before, reach, part)
+
+
+def placed_outputs_of(base, arrived, placed, gating):
+    heads, depth, _ = arrived.shape
+    length = gating.shape[1]
+    return pl.pallas_call(
+        functools.partial(placed_outputs_kernel, base),
+        out_shape=jax.ShapeDtypeStruct((length, heads * depth), BF16),
+        in_specs=[VMEM] * 4,
+        out_specs=VMEM,
+        compiler_params=PARAMS,
+    )(arrived, *placed, gating)
 
 
 def last_projected(section, first, second, block, weights):
@@ -578,7 +640,12 @@
                 "hij,hjk->hik", trans[0], arrived.astype(F32), precision=lax.Precision.HIGHEST
             )
             arrived = from_behind((passed + state).astype(BF16), "chain", 1)
-        blocks.append(outputs_of(g * size, arrived, before, reads))
+        if g + 1 < GROUPS:
+            blocks.append(outputs_of(g * size, arrived, before, reads))
+        else:
+            reach, part, gating = reads
+            placed = placed_of(g * size, before, reach, part)
+            blocks.append(placed_outputs_of(g * size, arrived, placed, gating))
 
     ring = lax.axis_size("head")
     mine = lax.axis_index("head")
@@ -590,6 +657,8 @@
         owner = lax.rem(mine + ring - k, ring)
         last = k + 1 == ring
         following = blocks if last else [lax.ppermute(x, "head", around) for x in blocks]
+        if k == 0:
+            blocks[:-1] = after(following[-1], *blocks[:-1])
         for g, block in enumerate(blocks):
             section = owner * GROUPS + g
             if last and g + 1 == GROUPS:

time: 71.4 us -> 72.2 us (1.011)
  matrix products: 4.35 us -> 3.16 us
  Pallas kernels: 17.9 us -> 19 us
  waiting for transfers between devices: 28.5 us -> 29.6 us
    dot_general x7, matrix products: 4.35 us -> 3.16 us  [on_device(): term = jnp.dot(block, rows, preferred_element_type=F32)]
    pallas_call x1, Pallas kernels: 5.42 us -> 6.42 us  [reads_of(): pl.pallas_call(functools.partial(reads_kernel, base), out_shape=(jax.Shap...]
    pallas_call x0 -> x2, Pallas kernels: none -> 0.79 us  [the longest x1 0.42 us: placed_of(): pl.pallas_call(functools.partial(placed_kernel, base), out_shape=(jax.Sha...]
    pallas_call x2 -> x1, Pallas kernels: 1.45 us -> 0.73 us  [outputs_of(): pl.pallas_call(functools.partial(outputs_kernel, base), out_shape=jax.Sha...]
  transfers between devices with their start and end apart: 15 -> 15, of which waited for: 8 -> 9; matrix products, arithmetic and copies ran while one was open for 8% -> 6% of each run, Pallas kernels for 13% -> 15%
where the time goes in v17:
time: 72.2 us; the launch traced here: 72 us
  waiting for transfers between devices  29.6 us (41%)
  Pallas kernels  19 us (26%)
  starting transfers between devices  18.4 us (25%)
  matrix products  3.16 us (4%)
  local copies, waits for them, and re-layouts  1.37 us (2%)
    ppermute x6, waiting for transfers between devices, on_device(): lax.ppermute(x, 'head', around)  28 us
    ppermute x3, starting transfers between devices, from_behind(): lax.ppermute(value, axis, [(i, i + steps) for i in range(count - steps)])  7.81 us
    ppermute x6, starting transfers between devices, exchange(): lax.ppermute(own_map, 'leaf', pairs_at(k, leaves))  7.11 us
    pallas_call x1, Pallas kernels, reads_of(): pl.pallas_call(functools.partial(reads_kernel, base), out_shape=(jax.Shap...  6.42 us
    pallas_call x1, Pallas kernels, maps_of(): pl.pallas_call(functools.partial(maps_kernel, base), out_shape=(jax.Shape...  5.05 us
    ppermute x6, starting transfers between devices, on_device(): lax.ppermute(x, 'head', around)  3.51 us
    dot_general x7, matrix products, on_device(): term = jnp.dot(block, rows, preferred_element_type=F32)  3.16 us
    pallas_call x1, Pallas kernels, filters_of(): pl.pallas_call(filters_kernel, out_shape=(per_token, per_token, jax.Shape...  1.78 us
  transfers between devices with their start and end apart: 15, of which 9 were waited for; matrix products, arithmetic and copies ran while one was open for 6% of the time, Pallas kernels for 15%

profile of v17, /device:TPU:0, one launch (start us, length us, event | category | flops | bytes accessed | tf_op | source)
XLA Modules:
  0.0 72.0 jit_solution(4572662135597920)
XLA Ops:
  0.0 1.4 %shard_map.101 = bf16[24,4,128]{2,1,0:T(4,128)(2,1)} custom-call(bf16[512,4,128]{2,1,0:T(4,128)(2,1)} %refs_0_.1, bf16[512,4,128]{2,1,0:T(4,128)(2,1)} %refs_1_.1, bf16[512,4,128]{2,1,0:T(4,128)(2,1)} %refs_2_.1), custom_call_target="tpu_custom_call" | custom-call | flops 1000000000 | bytes 65536 | tf_op jit(solution)/shard_map/pallas_call | solution.py:446
  1.4 4.8 %collective-permute-start = (bf16[24,4,128]{2,1,0:T(4,128)(2,1)}, bf16[24,4,128]{2,1,0:T(4,128)(2,1)S(1)}, u32[]{:S(2)}, u32[]{:S(2)}) collective-permute-start(bf16[24,4,128]{2,1,0:T(4,128)(2,1)} %shard_map.101), channel_id=1, source_target_pairs={{0,4},{4,8},{8,12},{12,16},{16,20},{20,24},{24,28},{1,5},{5,9},{9,... | collective-permute-start | bytes 73736 | tf_op jit(solution)/shard_map/ppermute | solution.py:429
  6.3 1.2 %copy_bitcast_fusion.2 = (bf16[4,512,128]{2,1,0:T(8,128)(2,1)S(1)}, bf16[4,512,128]{2,1,0:T(8,128)(2,1)S(1)}) fusion(bf16[512,4,128]{2,1,0:T(4,128)(2,1)S(1)} %copy-done.8, bf16[512,4,128]{2,1,0:T(4,128)(2,1)} %refs_1_.1), kind=kLoop, calls=%fused_computation.4 | loop fusion | bytes 2097152 | tf_op jit(solution)/shard_map/transpose | solution.py:612
  7.5 1.8 %shard_map.100 = (bf16[4,512,128]{2,1,0:T(8,128)(2,1)S(1)}, bf16[4,512,128]{2,1,0:T(8,128)(2,1)S(1)}, f32[2,4,16,128]{3,2,1,0:T(8,128)S(1)}) custom-call(bf16[4,512,128]{2,1,0:T(8,128)(2,1)S(1)} %get-tuple-element.64.key_ref, bf16[4,512,128]{2,1,0:T(8,128)(2,1)S(1)} %get-tuple-element.63.value_ref, f32[3,4,4,128]{3,2,1,0:T(4,128)S(1)} %copy-done.1), custom_call_target="tpu_custom_call" | custom-call | flops 3000000000 | bytes 4194304 | tf_op jit(solution)/shard_map/pallas_call | solution.py:460
  9.4 5.1 %shard_map.102 = (bf16[4,512,128]{2,1,0:T(8,128)(2,1)S(1)}, f32[4,512,256]{2,1,0:T(8,128)S(1)}, bf16[4,3,128,256]{3,2,1,0:T(8,128)(2,1)S(1)}, bf16[2,128,256]{2,1,0:T(8,128)(2,1)S(1)}, bf16[2,128,256]{2,1,0:T(8,128)(2,1)S(1)}) custom-call(s32[8]{0:T(128)S(1)} %copy-done.4, bf16[4,512,128]{2,1,0:T(8,128)(2,1)S(1)} %get-tuple-element.34.unit_in_ref, ...), custom_call_target="tpu_custom_call" | custom-call | flops 5000000000 | bytes 4194304 | tf_op jit(solution)/shard_map/pallas_call | solution.py:476
  14.5 1.6 %collective-permute-start.1 = (bf16[2,128,256]{2,1,0:T(8,128)(2,1)S(1)}, bf16[2,128,256]{2,1,0:T(8,128)(2,1)S(1)}, u32[]{:S(2)}, u32[]{:S(2)}) collective-permute-start(bf16[2,128,256]{2,1,0:T(8,128)(2,1)S(1)} %get-tuple-element.45.refs_0_), channel_id=1, source_target_pairs={{0,4},{4,0},{8,12},{12,8},{1,5},{5,1},{9,13},{13,9},{2,6},{6,2},{1... | collective-permute-start | bytes 393224 | tf_op jit(solution)/shard_map/ppermute | solution.py:433
  16.0 1.0 %collective-permute-start.2 = (bf16[2,128,256]{2,1,0:T(8,128)(2,1)S(1)}, bf16[2,128,256]{2,1,0:T(8,128)(2,1)S(1)}, u32[]{:S(2)}, u32[]{:S(2)}) collective-permute-start(bf16[2,128,256]{2,1,0:T(8,128)(2,1)S(1)} %get-tuple-element.45.refs_0_), channel_id=1, source_target_pairs={{0,8},{4,12},{8,0},{12,4},{1,9},{5,13},{9,1},{13,5},{2,10},{6,14},... | collective-permute-start | bytes 393224 | tf_op jit(solution)/shard_map/ppermute | solution.py:433
  17.0 1.0 %collective-permute-start.3 = (bf16[2,128,256]{2,1,0:T(8,128)(2,1)S(1)}, bf16[2,128,256]{2,1,0:T(8,128)(2,1)S(1)}, u32[]{:S(2)}, u32[]{:S(2)}) collective-permute-start(bf16[2,128,256]{2,1,0:T(8,128)(2,1)S(1)} %get-tuple-element.45.refs_0_), channel_id=1, source_target_pairs={{0,12},{4,8},{8,4},{12,0},{1,13},{5,9},{9,5},{13,1},{2,14},{6,10},... | collective-permute-start | bytes 393224 | tf_op jit(solution)/shard_map/ppermute | solution.py:433
  18.2 6.4 %shard_map.103 = (bf16[4,512,128]{2,1,0:T(8,128)(2,1)S(1)}, f32[4,512,128]{2,1,0:T(8,128)S(1)}, f32[4,512,128]{2,1,0:T(8,128)S(1)}) custom-call(s32[8]{0:T(128)S(1)} %copy-done.4, bf16[4,512,128]{2,1,0:T(8,128)(2,1)S(1)} %bitcast.20, bf16[4,512,128]{2,1,0:T(8,128)(2,1)S(1)} %bitcast.21, f32[1,128]{1,0:T(1,128)S(1)} %bitcast.22, ...), custom_call_target="tpu_custom_call" | custom-call | flops 3000000000 | bytes 4194304 | tf_op jit(solution)/shard_map/pallas_call | solution.py:502
  25.4 1.6 %collective-permute-start.5 = (bf16[2,128,256]{2,1,0:T(8,128)(2,1)S(1)}, bf16[2,128,256]{2,1,0:T(8,128)(2,1)S(1)}, u32[]{:S(2)}, u32[]{:S(2)}) collective-permute-start(bf16[2,128,256]{2,1,0:T(8,128)(2,1)S(1)} %get-tuple-element.54.refs_0_), channel_id=1, source_target_pairs={{0,4},{4,0},{8,12},{12,8},{1,5},{5,1},{9,13},{13,9},{2,6},{6,2},{1... | collective-permute-start | bytes 393224 | tf_op jit(solution)/shard_map/ppermute | solution.py:433
  27.0 1.0 %collective-permute-start.6 = (bf16[2,128,256]{2,1,0:T(8,128)(2,1)S(1)}, bf16[2,128,256]{2,1,0:T(8,128)(2,1)S(1)}, u32[]{:S(2)}, u32[]{:S(2)}) collective-permute-start(bf16[2,128,256]{2,1,0:T(8,128)(2,1)S(1)} %get-tuple-element.54.refs_0_), channel_id=1, source_target_pairs={{0,8},{4,12},{8,0},{12,4},{1,9},{5,13},{9,1},{13,5},{2,10},{6,14},... | collective-permute-start | bytes 393224 | tf_op jit(solution)/shard_map/ppermute | solution.py:433
  27.9 1.0 %collective-permute-start.7 = (bf16[2,128,256]{2,1,0:T(8,128)(2,1)S(1)}, bf16[2,128,256]{2,1,0:T(8,128)(2,1)S(1)}, u32[]{:S(2)}, u32[]{:S(2)}) collective-permute-start(bf16[2,128,256]{2,1,0:T(8,128)(2,1)S(1)} %get-tuple-element.54.refs_0_), channel_id=1, source_target_pairs={{0,12},{4,8},{8,4},{12,0},{1,13},{5,9},{9,5},{13,1},{2,14},{6,10},... | collective-permute-start | bytes 393224 | tf_op jit(solution)/shard_map/ppermute | solution.py:433
  29.0 1.3 %collective-permute-start.4 = (bf16[2,128,128]{2,1,0:T(8,128)(2,1)S(1)}, bf16[2,128,128]{2,1,0:T(8,128)(2,1)S(1)}, u32[]{:S(2)}, u32[]{:S(2)}) collective-permute-start(bf16[2,128,128]{2,1,0:T(8,128)(2,1)S(1)} %get-tuple-element.49), channel_id=1, source_target_pairs={{0,16},{1,17},{2,18},{3,19},{4,20},{5,21},{6,22},{7,23},{8,24},{9,... | collective-permute-start | bytes 196616 | tf_op jit(solution)/shard_map/ppermute | solution.py:429
  30.3 0.8 %collective-permute-done.4.arrived_ref = bf16[2,128,128]{2,1,0:T(8,128)(2,1)S(1)} collective-permute-done((bf16[2,128,128]{2,1,0:T(8,128)(2,1)S(1)}, bf16[2,128,128]{2,1,0:T(8,128)(2,1)S(1)}, u32[]{:S(2)}, u32[]{:S(2)}) %collective-permute-start.4) | collective-permute-done | bytes 65568 | tf_op jit(solution)/shard_map/ppermute | solution.py:429
  31.9 1.6 %collective-permute-start.10 = (bf16[512,256]{1,0:T(8,128)(2,1)S(1)}, bf16[512,256]{1,0:T(8,128)(2,1)S(1)}, u32[]{:S(2)}, u32[]{:S(2)}) collective-permute-start(bf16[512,256]{1,0:T(8,128)(2,1)S(1)} %shard_map.105), channel_id=1, source_target_pairs={{0,1},{1,2},{2,3},{3,0},{4,5},{5,6},{6,7},{7,4},{8,9},{9,10},{10,1... | collective-permute-start | bytes 786440 | tf_op jit(solution)/shard_map/ppermute | solution.py:659
  34.5 1.7 %collective-permute-start.8 = (bf16[2,128,128]{2,1,0:T(8,128)(2,1)S(1)}, bf16[2,128,128]{2,1,0:T(8,128)(2,1)S(1)}, u32[]{:S(2)}, u32[]{:S(2)}) collective-permute-start(bf16[2,128,128]{2,1,0:T(8,128)(2,1)S(1)} %get-tuple-element.58), channel_id=1, source_target_pairs={{0,16},{1,17},{2,18},{3,19},{4,20},{5,21},{6,22},{7,23},{8,24},{9,... | collective-permute-start | bytes 196616 | tf_op jit(solution)/shard_map/ppermute | solution.py:429
  37.5 1.8 %collective-permute-start.9 = (bf16[512,256]{1,0:T(8,128)(2,1)S(1)}, bf16[512,256]{1,0:T(8,128)(2,1)S(1)}, u32[]{:S(2)}, u32[]{:S(2)}) collective-permute-start(bf16[512,256]{1,0:T(8,128)(2,1)S(1)} %shard_map.108), channel_id=1, source_target_pairs={{0,1},{1,2},{2,3},{3,0},{4,5},{5,6},{6,7},{7,4},{8,9},{9,10},{10,1... | collective-permute-start | bytes 786440 | tf_op jit(solution)/shard_map/ppermute | solution.py:659
  39.8 2.6 %collective-permute-done.10 = bf16[512,256]{1,0:T(8,128)(2,1)S(1)} collective-permute-done((bf16[512,256]{1,0:T(8,128)(2,1)S(1)}, bf16[512,256]{1,0:T(8,128)(2,1)S(1)}, u32[]{:S(2)}, u32[]{:S(2)}) %collective-permute-start.10) | collective-permute-done | bytes 262176 | tf_op jit(solution)/shard_map/ppermute | solution.py:659
  42.8 5.9 %collective-permute-done.9 = bf16[512,256]{1,0:T(8,128)(2,1)S(1)} collective-permute-done((bf16[512,256]{1,0:T(8,128)(2,1)S(1)}, bf16[512,256]{1,0:T(8,128)(2,1)S(1)}, u32[]{:S(2)}, u32[]{:S(2)}) %collective-permute-start.9) | collective-permute-done | bytes 262176 | tf_op jit(solution)/shard_map/ppermute | solution.py:659
  49.6 4.7 %collective-permute-done.11 = bf16[512,256]{1,0:T(8,128)(2,1)S(1)} collective-permute-done((bf16[512,256]{1,0:T(8,128)(2,1)S(1)}, bf16[512,256]{1,0:T(8,128)(2,1)S(1)}, u32[]{:S(2)}, u32[]{:S(2)}) %collective-permute-start.11) | collective-permute-done | bytes 262176 | tf_op jit(solution)/shard_map/ppermute | solution.py:659
  54.7 5.5 %collective-permute-done.13 = bf16[512,256]{1,0:T(8,128)(2,1)S(1)} collective-permute-done((bf16[512,256]{1,0:T(8,128)(2,1)S(1)}, bf16[512,256]{1,0:T(8,128)(2,1)S(1)}, u32[]{:S(2)}, u32[]{:S(2)}) %collective-permute-start.13) | collective-permute-done | bytes 262176 | tf_op jit(solution)/shard_map/ppermute | solution.py:659
  60.7 5.1 %collective-permute-done.12 = bf16[512,256]{1,0:T(8,128)(2,1)S(1)} collective-permute-done((bf16[512,256]{1,0:T(8,128)(2,1)S(1)}, bf16[512,256]{1,0:T(8,128)(2,1)S(1)}, u32[]{:S(2)}, u32[]{:S(2)}) %collective-permute-start.12) | collective-permute-done | bytes 262176 | tf_op jit(solution)/shard_map/ppermute | solution.py:659
  66.3 4.3 %collective-permute-done.14.block_ref = bf16[512,256]{1,0:T(8,128)(2,1)S(1)} collective-permute-done((bf16[512,256]{1,0:T(8,128)(2,1)S(1)}, bf16[512,256]{1,0:T(8,128)(2,1)S(1)}, u32[]{:S(2)}, u32[]{:S(2)}) %collective-permute-start.14) | collective-permute-done | bytes 262176 | tf_op jit(solution)/shard_map/ppermute | solution.py:659
  70.6 1.3 %shard_map.109 = bf16[512,1024]{1,0:T(8,128)(2,1)} custom-call(s32[1]{0:T(128)} %bitcast.section, f32[512,1024]{1,0:T(8,128)S(1)} %add_add_fusion.1.first_ref, f32[512,1024]{1,0:T(8,128)S(1)} %add_add_fusion.second_ref, bf16[512,256]{1,0:T(8,128)(2,1)S(1)} %collective-permute-done.14.block_ref, bf16[2048,1024]{1,0:T(8,128)(2,1)S(1)} %copy-done), custom_call_target="tpu_custom_call" | custom-call | tf_op jit(solution)/shard_map/pallas_call | solution.py:580
  (44 shorter events, 7.2 us)
Async XLA Ops:
  0.0 6.3 %copy-start.8 = (bf16[512,4,128]{2,1,0:T(4,128)(2,1)S(1)}, bf16[512,4,128]{2,1,0:T(4,128)(2,1)}, u32[]{:S(2)}) copy-start(bf16[512,4,128]{2,1,0:T(4,128)(2,1)} %refs_2_.1) | copy-start | bytes 1572868
  0.0 7.5 %copy-start.1 = (f32[3,4,4,128]{3,2,1,0:T(4,128)S(1)}, f32[3,4,4,128]{3,2,1,0:T(4,128)}, u32[]{:S(2)}) copy-start(f32[3,4,4,128]{3,2,1,0:T(4,128)} %taps_ref.5) | copy-start | bytes 73732
  1.4 7.9 %collective-permute-start = (bf16[24,4,128]{2,1,0:T(4,128)(2,1)}, bf16[24,4,128]{2,1,0:T(4,128)(2,1)S(1)}, u32[]{:S(2)}, u32[]{:S(2)}) collective-permute-start(bf16[24,4,128]{2,1,0:T(4,128)(2,1)} %shard_map.101), channel_id=1, source_target_pairs={{0,4},{4,8},{8,12},{12,16},{16,20},{20,24},{24,28},{1,5},{5,9},{9,... | collective-permute-start | bytes 73736 | tf_op jit(solution)/shard_map/ppermute | solution.py:429
  7.5 1.8 %copy-start.2 = (f32[4,512]{1,0:T(4,128)S(1)}, f32[4,512]{1,0:T(4,128)}, u32[]{:S(2)}) copy-start(f32[4,512]{1,0:T(4,128)} %decay_ref.3) | copy-start | bytes 24580
  7.5 1.8 %copy-start.3 = (f32[4,512]{1,0:T(4,128)S(1)}, f32[4,512]{1,0:T(4,128)}, u32[]{:S(2)}) copy-start(f32[4,512]{1,0:T(4,128)} %strength_ref.3) | copy-start | bytes 24580
  7.5 1.8 %copy-start.4 = (s32[8]{0:T(128)S(1)}, s32[8]{0:T(128)}, u32[]{:S(2)}) copy-start(s32[8]{0:T(128)} %resets.3) | copy-start | bytes 100
  9.4 8.7 %copy-start.6 = (bf16[512,4,128]{2,1,0:T(4,128)(2,1)S(1)}, bf16[512,4,128]{2,1,0:T(4,128)(2,1)}, u32[]{:S(2)}) copy-start(bf16[512,4,128]{2,1,0:T(4,128)(2,1)} %refs_0_.1) | copy-start | bytes 1572868
  9.4 8.7 %copy-start.7 = (bf16[512,4,128]{2,1,0:T(4,128)(2,1)S(1)}, bf16[512,4,128]{2,1,0:T(4,128)(2,1)}, u32[]{:S(2)}) copy-start(bf16[512,4,128]{2,1,0:T(4,128)(2,1)} %param.13) | copy-start | bytes 1572868
  14.4 3.7 %copy-start.5 = (f32[128]{0:T(128)S(1)}, f32[128]{0:T(128)}, u32[]{:S(2)}) copy-start(f32[128]{0:T(128)} %param.18) | copy-start | bytes 1540
  14.5 10.2 %collective-permute-start.1 = (bf16[2,128,256]{2,1,0:T(8,128)(2,1)S(1)}, bf16[2,128,256]{2,1,0:T(8,128)(2,1)S(1)}, u32[]{:S(2)}, u32[]{:S(2)}) collective-permute-start(bf16[2,128,256]{2,1,0:T(8,128)(2,1)S(1)} %get-tuple-element.45.refs_0_), channel_id=1, source_target_pairs={{0,4},{4,0},{8,12},{12,8},{1,5},{5,1},{9,13},{13,9},{2,6},{6,2},{1... | collective-permute-start | bytes 393224 | tf_op jit(solution)/shard_map/ppermute | solution.py:433
  16.0 8.6 %collective-permute-start.2 = (bf16[2,128,256]{2,1,0:T(8,128)(2,1)S(1)}, bf16[2,128,256]{2,1,0:T(8,128)(2,1)S(1)}, u32[]{:S(2)}, u32[]{:S(2)}) collective-permute-start(bf16[2,128,256]{2,1,0:T(8,128)(2,1)S(1)} %get-tuple-element.45.refs_0_), channel_id=1, source_target_pairs={{0,8},{4,12},{8,0},{12,4},{1,9},{5,13},{9,1},{13,5},{2,10},{6,14},... | collective-permute-start | bytes 393224 | tf_op jit(solution)/shard_map/ppermute | solution.py:433
  17.0 7.6 %collective-permute-start.3 = (bf16[2,128,256]{2,1,0:T(8,128)(2,1)S(1)}, bf16[2,128,256]{2,1,0:T(8,128)(2,1)S(1)}, u32[]{:S(2)}, u32[]{:S(2)}) collective-permute-start(bf16[2,128,256]{2,1,0:T(8,128)(2,1)S(1)} %get-tuple-element.45.refs_0_), channel_id=1, source_target_pairs={{0,12},{4,8},{8,4},{12,0},{1,13},{5,9},{9,5},{13,1},{2,14},{6,10},... | collective-permute-start | bytes 393224 | tf_op jit(solution)/shard_map/ppermute | solution.py:433
  25.4 8.1 %collective-permute-start.5 = (bf16[2,128,256]{2,1,0:T(8,128)(2,1)S(1)}, bf16[2,128,256]{2,1,0:T(8,128)(2,1)S(1)}, u32[]{:S(2)}, u32[]{:S(2)}) collective-permute-start(bf16[2,128,256]{2,1,0:T(8,128)(2,1)S(1)} %get-tuple-element.54.refs_0_), channel_id=1, source_target_pairs={{0,4},{4,0},{8,12},{12,8},{1,5},{5,1},{9,13},{13,9},{2,6},{6,2},{1... | collective-permute-start | bytes 393224 | tf_op jit(solution)/shard_map/ppermute | solution.py:433
  27.0 6.5 %collective-permute-start.6 = (bf16[2,128,256]{2,1,0:T(8,128)(2,1)S(1)}, bf16[2,128,256]{2,1,0:T(8,128)(2,1)S(1)}, u32[]{:S(2)}, u32[]{:S(2)}) collective-permute-start(bf16[2,128,256]{2,1,0:T(8,128)(2,1)S(1)} %get-tuple-element.54.refs_0_), channel_id=1, source_target_pairs={{0,8},{4,12},{8,0},{12,4},{1,9},{5,13},{9,1},{13,5},{2,10},{6,14},... | collective-permute-start | bytes 393224 | tf_op jit(solution)/shard_map/ppermute | solution.py:433
  27.9 5.9 %collective-permute-start.7 = (bf16[2,128,256]{2,1,0:T(8,128)(2,1)S(1)}, bf16[2,128,256]{2,1,0:T(8,128)(2,1)S(1)}, u32[]{:S(2)}, u32[]{:S(2)}) collective-permute-start(bf16[2,128,256]{2,1,0:T(8,128)(2,1)S(1)} %get-tuple-element.54.refs_0_), channel_id=1, source_target_pairs={{0,12},{4,8},{8,4},{12,0},{1,13},{5,9},{9,5},{13,1},{2,14},{6,10},... | collective-permute-start | bytes 393224 | tf_op jit(solution)/shard_map/ppermute | solution.py:433
  29.0 2.2 %collective-permute-start.4 = (bf16[2,128,128]{2,1,0:T(8,128)(2,1)S(1)}, bf16[2,128,128]{2,1,0:T(8,128)(2,1)S(1)}, u32[]{:S(2)}, u32[]{:S(2)}) collective-permute-start(bf16[2,128,128]{2,1,0:T(8,128)(2,1)S(1)} %get-tuple-element.49), channel_id=1, source_target_pairs={{0,16},{1,17},{2,18},{3,19},{4,20},{5,21},{6,22},{7,23},{8,24},{9,... | collective-permute-start | bytes 196616 | tf_op jit(solution)/shard_map/ppermute | solution.py:429
  31.9 10.5 %collective-permute-start.10 = (bf16[512,256]{1,0:T(8,128)(2,1)S(1)}, bf16[512,256]{1,0:T(8,128)(2,1)S(1)}, u32[]{:S(2)}, u32[]{:S(2)}) collective-permute-start(bf16[512,256]{1,0:T(8,128)(2,1)S(1)} %shard_map.105), channel_id=1, source_target_pairs={{0,1},{1,2},{2,3},{3,0},{4,5},{5,6},{6,7},{7,4},{8,9},{9,10},{10,1... | collective-permute-start | bytes 786440 | tf_op jit(solution)/shard_map/ppermute | solution.py:659
  34.5 2.6 %collective-permute-start.8 = (bf16[2,128,128]{2,1,0:T(8,128)(2,1)S(1)}, bf16[2,128,128]{2,1,0:T(8,128)(2,1)S(1)}, u32[]{:S(2)}, u32[]{:S(2)}) collective-permute-start(bf16[2,128,128]{2,1,0:T(8,128)(2,1)S(1)} %get-tuple-element.58), channel_id=1, source_target_pairs={{0,16},{1,17},{2,18},{3,19},{4,20},{5,21},{6,22},{7,23},{8,24},{9,... | collective-permute-start | bytes 196616 | tf_op jit(solution)/shard_map/ppermute | solution.py:429
  36.2 3.1 %copy-start = (bf16[2048,1024]{1,0:T(8,128)(2,1)S(1)}, bf16[2048,1024]{1,0:T(8,128)(2,1)}, u32[]{:S(2)}) copy-start(bf16[2048,1024]{1,0:T(8,128)(2,1)} %weights_ref.1) | copy-start | bytes 12582916
  37.5 11.2 %collective-permute-start.9 = (bf16[512,256]{1,0:T(8,128)(2,1)S(1)}, bf16[512,256]{1,0:T(8,128)(2,1)S(1)}, u32[]{:S(2)}, u32[]{:S(2)}) collective-permute-start(bf16[512,256]{1,0:T(8,128)(2,1)S(1)} %shard_map.108), channel_id=1, source_target_pairs={{0,1},{1,2},{2,3},{3,0},{4,5},{5,6},{6,7},{7,4},{8,9},{9,10},{10,1... | collective-permute-start | bytes 786440 | tf_op jit(solution)/shard_map/ppermute | solution.py:659
  42.3 11.9 %collective-permute-start.11 = (bf16[512,256]{1,0:T(8,128)(2,1)S(1)}, bf16[512,256]{1,0:T(8,128)(2,1)S(1)}, u32[]{:S(2)}, u32[]{:S(2)}) collective-permute-start(bf16[512,256]{1,0:T(8,128)(2,1)S(1)} %collective-permute-done.10), channel_id=1, source_target_pairs={{0,1},{1,2},{2,3},{3,0},{4,5},{5,6},{6,7},{7,4},{8,9},{9,10},{10,1... | collective-permute-start | bytes 786440 | tf_op jit(solution)/shard_map/ppermute | solution.py:659
  49.1 11.1 %collective-permute-start.13 = (bf16[512,256]{1,0:T(8,128)(2,1)S(1)}, bf16[512,256]{1,0:T(8,128)(2,1)S(1)}, u32[]{:S(2)}, u32[]{:S(2)}) collective-permute-start(bf16[512,256]{1,0:T(8,128)(2,1)S(1)} %collective-permute-done.9), channel_id=1, source_target_pairs={{0,1},{1,2},{2,3},{3,0},{4,5},{5,6},{6,7},{7,4},{8,9},{9,10},{10,1... | collective-permute-start | bytes 786440 | tf_op jit(solution)/shard_map/ppermute | solution.py:659
  54.3 11.5 %collective-permute-start.12 = (bf16[512,256]{1,0:T(8,128)(2,1)S(1)}, bf16[512,256]{1,0:T(8,128)(2,1)S(1)}, u32[]{:S(2)}, u32[]{:S(2)}) collective-permute-start(bf16[512,256]{1,0:T(8,128)(2,1)S(1)} %collective-permute-done.11), channel_id=1, source_target_pairs={{0,1},{1,2},{2,3},{3,0},{4,5},{5,6},{6,7},{7,4},{8,9},{9,10},{10,1... | collective-permute-start | bytes 786440 | tf_op jit(solution)/shard_map/ppermute | solution.py:659
  60.2 10.4 %collective-permute-start.14 = (bf16[512,256]{1,0:T(8,128)(2,1)S(1)}, bf16[512,256]{1,0:T(8,128)(2,1)S(1)}, u32[]{:S(2)}, u32[]{:S(2)}) collective-permute-start(bf16[512,256]{1,0:T(8,128)(2,1)S(1)} %collective-permute-done.13), channel_id=1, source_target_pairs={{0,1},{1,2},{2,3},{3,0},{4,5},{5,6},{6,7},{7,4},{8,9},{9,10},{10,1... | collective-permute-start | bytes 786440 | tf_op jit(solution)/shard_map/ppermute | solution.py:659

commit v18 on v16

--- a/solution.py
+++ b/solution.py
@@ -256,7 +256,7 @@
     half = chunks // 2
     for c in range(1, half):
         for g in every:
-            starts_ref[g, c - 1] = states[g]
+            starts_ref[g, c - 1] = states[g].astype(BF16)
         states = [compose(step_s[g, c], states[g]) for g in every]
     rest = [step_s[g, half] for g in every]
     for c in range(half + 1, chunks):
@@ -265,7 +265,7 @@
         map_refs[g // size][g % size] = compose(rest[g], states[g]).astype(BF16)
     for c in range(half, chunks):
         for g in every:
-            starts_ref[g, c - 1] = states[g]
+            starts_ref[g, c - 1] = states[g].astype(BF16)
         if c + 1 < chunks:
             states = [compose(step_s[g, c], states[g]) for g in every]
 
@@ -305,7 +305,8 @@
             reach = growth * query.astype(F32) - own[:, :depth]
             part = own[:, depth:]
             if c:
-                both = mul_split(reach, starts_ref[g, c - 1])
+                high, low = split(reach)
+                both = mul(high, starts_ref[g, c - 1]) + mul(low, starts_ref[g, c - 1])
                 reach = both[:, :depth]
                 part = part + both[:, depth:]
             reach_ref[g, here] = reach.astype(BF16)
@@ -445,7 +446,7 @@
         out_shape=(
             jax.ShapeDtypeStruct((heads, length, depth), BF16),
             jax.ShapeDtypeStruct((heads, length, 2 * depth), F32),
-            jax.ShapeDtypeStruct((heads, chunks - 1, depth, 2 * depth), F32),
+            jax.ShapeDtypeStruct((heads, chunks - 1, depth, 2 * depth), BF16),
             *[jax.ShapeDtypeStruct((heads // GROUPS, depth, 2 * depth), BF16)] * GROUPS,
         ),
         in_specs=[SMEM] + [VMEM] * 7,

time: 71.4 us -> 72.4 us (1.014)
  Pallas kernels: 17.9 us -> 18.9 us
    pallas_call x1, Pallas kernels: 5.42 us -> 6.46 us  [reads_of(): pl.pallas_call(functools.partial(reads_kernel, base), out_shape=(jax.Shap...]
  transfers between devices with their start and end apart: 15 -> 15, of which waited for: 8 -> 8; matrix products, arithmetic and copies ran while one was open for 8% -> 8% of each run, Pallas kernels for 13% -> 14%
where the time goes in v18:
time: 72.4 us; the launch traced here: 72.2 us
  waiting for transfers between devices  28.5 us (39%)
  Pallas kernels  18.9 us (26%)
  starting transfers between devices  18.6 us (26%)
  matrix products  4.34 us (6%)
  local copies, waits for them, and re-layouts  1.37 us (2%)
    ppermute x6, waiting for transfers between devices, on_device(): lax.ppermute(x, 'head', around)  27.3 us
    ppermute x3, starting transfers between devices, from_behind(): lax.ppermute(value, axis, [(i, i + steps) for i in range(count - steps)])  8.01 us
    ppermute x6, starting transfers between devices, exchange(): lax.ppermute(own_map, 'leaf', pairs_at(k, leaves))  7.11 us
    pallas_call x1, Pallas kernels, reads_of(): pl.pallas_call(functools.partial(reads_kernel, base), out_shape=(jax.Shap...  6.46 us
    pallas_call x1, Pallas kernels, maps_of(): pl.pallas_call(functools.partial(maps_kernel, base), out_shape=(jax.Shape...  5.05 us
    dot_general x7, matrix products, on_device(): term = jnp.dot(block, rows, preferred_element_type=F32)  4.34 us
    ppermute x6, starting transfers between devices, on_device(): lax.ppermute(x, 'head', around)  3.46 us
    pallas_call x1, Pallas kernels, filters_of(): pl.pallas_call(filters_kernel, out_shape=(per_token, per_token, jax.Shape...  1.78 us
  transfers between devices with their start and end apart: 15, of which 8 were waited for; matrix products, arithmetic and copies ran while one was open for 8% of the time, Pallas kernels for 14%

profile of v18, /device:TPU:0, one launch (start us, length us, event | category | flops | bytes accessed | tf_op | source)
XLA Modules:
  0.0 72.2 jit_solution(11160808678574394114)
XLA Ops:
  0.0 1.4 %shard_map.101 = bf16[24,4,128]{2,1,0:T(4,128)(2,1)} custom-call(bf16[512,4,128]{2,1,0:T(4,128)(2,1)} %refs_0_.1, bf16[512,4,128]{2,1,0:T(4,128)(2,1)} %refs_1_.1, bf16[512,4,128]{2,1,0:T(4,128)(2,1)} %refs_2_.1), custom_call_target="tpu_custom_call" | custom-call | flops 1000000000 | bytes 65536 | tf_op jit(solution)/shard_map/pallas_call | solution.py:414
  1.4 4.8 %collective-permute-start = (bf16[24,4,128]{2,1,0:T(4,128)(2,1)}, bf16[24,4,128]{2,1,0:T(4,128)(2,1)S(1)}, u32[]{:S(2)}, u32[]{:S(2)}) collective-permute-start(bf16[24,4,128]{2,1,0:T(4,128)(2,1)} %shard_map.101), channel_id=1, source_target_pairs={{0,4},{4,8},{8,12},{12,16},{16,20},{20,24},{24,28},{1,5},{5,9},{9,... | collective-permute-start | bytes 73736 | tf_op jit(solution)/shard_map/ppermute | solution.py:397
  6.3 1.2 %copy_bitcast_fusion.2 = (bf16[4,512,128]{2,1,0:T(8,128)(2,1)S(1)}, bf16[4,512,128]{2,1,0:T(8,128)(2,1)S(1)}) fusion(bf16[512,4,128]{2,1,0:T(4,128)(2,1)S(1)} %copy-done.8, bf16[512,4,128]{2,1,0:T(4,128)(2,1)} %refs_1_.1), kind=kLoop, calls=%fused_computation.4 | loop fusion | bytes 2097152 | tf_op jit(solution)/shard_map/transpose | solution.py:551
  7.5 1.8 %shard_map.100 = (bf16[4,512,128]{2,1,0:T(8,128)(2,1)S(1)}, bf16[4,512,128]{2,1,0:T(8,128)(2,1)S(1)}, f32[2,4,16,128]{3,2,1,0:T(8,128)S(1)}) custom-call(bf16[4,512,128]{2,1,0:T(8,128)(2,1)S(1)} %get-tuple-element.58.key_ref, bf16[4,512,128]{2,1,0:T(8,128)(2,1)S(1)} %get-tuple-element.57.value_ref, f32[3,4,4,128]{3,2,1,0:T(4,128)S(1)} %copy-done.1), custom_call_target="tpu_custom_call" | custom-call | flops 3000000000 | bytes 4194304 | tf_op jit(solution)/shard_map/pallas_call | solution.py:428
  9.4 5.1 %shard_map.102 = (bf16[4,512,128]{2,1,0:T(8,128)(2,1)S(1)}, f32[4,512,256]{2,1,0:T(8,128)S(1)}, bf16[4,3,128,256]{3,2,1,0:T(8,128)(2,1)S(1)}, bf16[2,128,256]{2,1,0:T(8,128)(2,1)S(1)}, bf16[2,128,256]{2,1,0:T(8,128)(2,1)S(1)}) custom-call(s32[8]{0:T(128)S(1)} %copy-done.4, bf16[4,512,128]{2,1,0:T(8,128)(2,1)S(1)} %get-tuple-element.31.unit_in_ref, ...), custom_call_target="tpu_custom_call" | custom-call | flops 5000000000 | bytes 4194304 | tf_op jit(solution)/shard_map/pallas_call | solution.py:444
  14.5 1.6 %collective-permute-start.1 = (bf16[2,128,256]{2,1,0:T(8,128)(2,1)S(1)}, bf16[2,128,256]{2,1,0:T(8,128)(2,1)S(1)}, u32[]{:S(2)}, u32[]{:S(2)}) collective-permute-start(bf16[2,128,256]{2,1,0:T(8,128)(2,1)S(1)} %get-tuple-element.42.refs_0_), channel_id=1, source_target_pairs={{0,4},{4,0},{8,12},{12,8},{1,5},{5,1},{9,13},{13,9},{2,6},{6,2},{1... | collective-permute-start | bytes 393224 | tf_op jit(solution)/shard_map/ppermute | solution.py:401
  16.0 1.0 %collective-permute-start.2 = (bf16[2,128,256]{2,1,0:T(8,128)(2,1)S(1)}, bf16[2,128,256]{2,1,0:T(8,128)(2,1)S(1)}, u32[]{:S(2)}, u32[]{:S(2)}) collective-permute-start(bf16[2,128,256]{2,1,0:T(8,128)(2,1)S(1)} %get-tuple-element.42.refs_0_), channel_id=1, source_target_pairs={{0,8},{4,12},{8,0},{12,4},{1,9},{5,13},{9,1},{13,5},{2,10},{6,14},... | collective-permute-start | bytes 393224 | tf_op jit(solution)/shard_map/ppermute | solution.py:401
  17.0 1.0 %collective-permute-start.3 = (bf16[2,128,256]{2,1,0:T(8,128)(2,1)S(1)}, bf16[2,128,256]{2,1,0:T(8,128)(2,1)S(1)}, u32[]{:S(2)}, u32[]{:S(2)}) collective-permute-start(bf16[2,128,256]{2,1,0:T(8,128)(2,1)S(1)} %get-tuple-element.42.refs_0_), channel_id=1, source_target_pairs={{0,12},{4,8},{8,4},{12,0},{1,13},{5,9},{9,5},{13,1},{2,14},{6,10},... | collective-permute-start | bytes 393224 | tf_op jit(solution)/shard_map/ppermute | solution.py:401
  18.2 6.5 %shard_map.103 = (bf16[4,512,128]{2,1,0:T(8,128)(2,1)S(1)}, f32[4,512,128]{2,1,0:T(8,128)S(1)}, f32[4,512,128]{2,1,0:T(8,128)S(1)}) custom-call(s32[8]{0:T(128)S(1)} %copy-done.4, bf16[4,512,128]{2,1,0:T(8,128)(2,1)S(1)} %bitcast.21, bf16[4,512,128]{2,1,0:T(8,128)(2,1)S(1)} %bitcast.20, f32[1,128]{1,0:T(1,128)S(1)} %bitcast.22, ...), custom_call_target="tpu_custom_call" | custom-call | flops 3000000000 | bytes 4194304 | tf_op jit(solution)/shard_map/pallas_call | solution.py:470
  25.4 2.0 %collective-permute-start.10 = (bf16[2,128,256]{2,1,0:T(8,128)(2,1)S(1)}, bf16[2,128,256]{2,1,0:T(8,128)(2,1)S(1)}, u32[]{:S(2)}, u32[]{:S(2)}) collective-permute-start(bf16[2,128,256]{2,1,0:T(8,128)(2,1)S(1)} %get-tuple-element.51.refs_0_), channel_id=1, source_target_pairs={{0,12},{4,8},{8,4},{12,0},{1,13},{5,9},{9,5},{13,1},{2,14},{6,10},... | collective-permute-start | bytes 393224 | tf_op jit(solution)/shard_map/ppermute | solution.py:401
  27.4 1.4 %collective-permute-start.8 = (bf16[2,128,256]{2,1,0:T(8,128)(2,1)S(1)}, bf16[2,128,256]{2,1,0:T(8,128)(2,1)S(1)}, u32[]{:S(2)}, u32[]{:S(2)}) collective-permute-start(bf16[2,128,256]{2,1,0:T(8,128)(2,1)S(1)} %get-tuple-element.51.refs_0_), channel_id=1, source_target_pairs={{0,4},{4,0},{8,12},{12,8},{1,5},{5,1},{9,13},{13,9},{2,6},{6,2},{1... | collective-permute-start | bytes 393224 | tf_op jit(solution)/shard_map/ppermute | solution.py:401
  29.0 1.3 %collective-permute-start.4 = (bf16[2,128,128]{2,1,0:T(8,128)(2,1)S(1)}, bf16[2,128,128]{2,1,0:T(8,128)(2,1)S(1)}, u32[]{:S(2)}, u32[]{:S(2)}) collective-permute-start(bf16[2,128,128]{2,1,0:T(8,128)(2,1)S(1)} %get-tuple-element.46), channel_id=1, source_target_pairs={{0,16},{1,17},{2,18},{3,19},{4,20},{5,21},{6,22},{7,23},{8,24},{9,... | collective-permute-start | bytes 196616 | tf_op jit(solution)/shard_map/ppermute | solution.py:397
  30.3 0.8 %collective-permute-done.4.arrived_ref = bf16[2,128,128]{2,1,0:T(8,128)(2,1)S(1)} collective-permute-done((bf16[2,128,128]{2,1,0:T(8,128)(2,1)S(1)}, bf16[2,128,128]{2,1,0:T(8,128)(2,1)S(1)}, u32[]{:S(2)}, u32[]{:S(2)}) %collective-permute-start.4) | collective-permute-done | bytes 65568 | tf_op jit(solution)/shard_map/ppermute | solution.py:397
  31.9 1.6 %collective-permute-start.5 = (bf16[512,256]{1,0:T(8,128)(2,1)S(1)}, bf16[512,256]{1,0:T(8,128)(2,1)S(1)}, u32[]{:S(2)}, u32[]{:S(2)}) collective-permute-start(bf16[512,256]{1,0:T(8,128)(2,1)S(1)} %shard_map.105), channel_id=1, source_target_pairs={{0,1},{1,2},{2,3},{3,0},{4,5},{5,6},{6,7},{7,4},{8,9},{9,10},{10,1... | collective-permute-start | bytes 786440 | tf_op jit(solution)/shard_map/ppermute | solution.py:593
  34.6 1.9 %collective-permute-start.11 = (bf16[2,128,128]{2,1,0:T(8,128)(2,1)S(1)}, bf16[2,128,128]{2,1,0:T(8,128)(2,1)S(1)}, u32[]{:S(2)}, u32[]{:S(2)}) collective-permute-start(bf16[2,128,128]{2,1,0:T(8,128)(2,1)S(1)} %get-tuple-element.55), channel_id=1, source_target_pairs={{0,16},{1,17},{2,18},{3,19},{4,20},{5,21},{6,22},{7,23},{8,24},{9,... | collective-permute-start | bytes 196616 | tf_op jit(solution)/shard_map/ppermute | solution.py:397
  36.5 1.6 %fusion.10 = f32[512,1024]{1,0:T(8,128)S(1)} fusion(bf16[512,256]{1,0:T(8,128)(2,1)S(1)} %shard_map.105, bf16[2048,1024]{1,0:T(8,128)(2,1)} %weights_ref.1, s32[]{:T(128)S(6)} %select_n.21), kind=kOutput, calls=%fused_computation.16 | convolution fusion | flops 268435456 | bytes 2883588 | tf_op jit(solution)/shard_map/dot_general | solution.py:599
  38.9 1.6 %collective-permute-start.12 = (bf16[512,256]{1,0:T(8,128)(2,1)S(1)}, bf16[512,256]{1,0:T(8,128)(2,1)S(1)}, u32[]{:S(2)}, u32[]{:S(2)}) collective-permute-start(bf16[512,256]{1,0:T(8,128)(2,1)S(1)} %shard_map.107), channel_id=1, source_target_pairs={{0,1},{1,2},{2,3},{3,0},{4,5},{5,6},{6,7},{7,4},{8,9},{9,10},{10,1... | collective-permute-start | bytes 786440 | tf_op jit(solution)/shard_map/ppermute | solution.py:593
  40.9 1.4 %collective-permute-done.5 = bf16[512,256]{1,0:T(8,128)(2,1)S(1)} collective-permute-done((bf16[512,256]{1,0:T(8,128)(2,1)S(1)}, bf16[512,256]{1,0:T(8,128)(2,1)S(1)}, u32[]{:S(2)}, u32[]{:S(2)}) %collective-permute-start.5) | collective-permute-done | bytes 262176 | tf_op jit(solution)/shard_map/ppermute | solution.py:593
  43.0 6.9 %collective-permute-done.12 = bf16[512,256]{1,0:T(8,128)(2,1)S(1)} collective-permute-done((bf16[512,256]{1,0:T(8,128)(2,1)S(1)}, bf16[512,256]{1,0:T(8,128)(2,1)S(1)}, u32[]{:S(2)}, u32[]{:S(2)}) %collective-permute-start.12) | collective-permute-done | bytes 262176 | tf_op jit(solution)/shard_map/ppermute | solution.py:593
  50.4 5.2 %collective-permute-done.6 = bf16[512,256]{1,0:T(8,128)(2,1)S(1)} collective-permute-done((bf16[512,256]{1,0:T(8,128)(2,1)S(1)}, bf16[512,256]{1,0:T(8,128)(2,1)S(1)}, u32[]{:S(2)}, u32[]{:S(2)}) %collective-permute-start.6) | collective-permute-done | bytes 262176 | tf_op jit(solution)/shard_map/ppermute | solution.py:593
  56.0 5.2 %collective-permute-done.13 = bf16[512,256]{1,0:T(8,128)(2,1)S(1)} collective-permute-done((bf16[512,256]{1,0:T(8,128)(2,1)S(1)}, bf16[512,256]{1,0:T(8,128)(2,1)S(1)}, u32[]{:S(2)}, u32[]{:S(2)}) %collective-permute-start.13) | collective-permute-done | bytes 262176 | tf_op jit(solution)/shard_map/ppermute | solution.py:593
  61.7 5.1 %collective-permute-done.7 = bf16[512,256]{1,0:T(8,128)(2,1)S(1)} collective-permute-done((bf16[512,256]{1,0:T(8,128)(2,1)S(1)}, bf16[512,256]{1,0:T(8,128)(2,1)S(1)}, u32[]{:S(2)}, u32[]{:S(2)}) %collective-permute-start.7) | collective-permute-done | bytes 262176 | tf_op jit(solution)/shard_map/ppermute | solution.py:593
  67.3 3.5 %collective-permute-done.14.block_ref = bf16[512,256]{1,0:T(8,128)(2,1)S(1)} collective-permute-done((bf16[512,256]{1,0:T(8,128)(2,1)S(1)}, bf16[512,256]{1,0:T(8,128)(2,1)S(1)}, u32[]{:S(2)}, u32[]{:S(2)}) %collective-permute-start.14) | collective-permute-done | bytes 262176 | tf_op jit(solution)/shard_map/ppermute | solution.py:593
  70.8 1.3 %shard_map.108 = bf16[512,1024]{1,0:T(8,128)(2,1)} custom-call(s32[1]{0:T(128)} %bitcast.section, f32[512,1024]{1,0:T(8,128)S(1)} %add_add_fusion.1.first_ref, f32[512,1024]{1,0:T(8,128)S(1)} %add_add_fusion.second_ref, bf16[512,256]{1,0:T(8,128)(2,1)S(1)} %collective-permute-done.14.block_ref, bf16[2048,1024]{1,0:T(8,128)(2,1)S(1)} %copy-done), custom_call_target="tpu_custom_call" | custom-call | tf_op jit(solution)/shard_map/pallas_call | solution.py:519
  (43 shorter events, 6.5 us)
Async XLA Ops:
  0.0 6.3 %copy-start.8 = (bf16[512,4,128]{2,1,0:T(4,128)(2,1)S(1)}, bf16[512,4,128]{2,1,0:T(4,128)(2,1)}, u32[]{:S(2)}) copy-start(bf16[512,4,128]{2,1,0:T(4,128)(2,1)} %refs_2_.1) | copy-start | bytes 1572868
  0.0 7.5 %copy-start.1 = (f32[3,4,4,128]{3,2,1,0:T(4,128)S(1)}, f32[3,4,4,128]{3,2,1,0:T(4,128)}, u32[]{:S(2)}) copy-start(f32[3,4,4,128]{3,2,1,0:T(4,128)} %taps_ref.5) | copy-start | bytes 73732
  1.4 7.9 %collective-permute-start = (bf16[24,4,128]{2,1,0:T(4,128)(2,1)}, bf16[24,4,128]{2,1,0:T(4,128)(2,1)S(1)}, u32[]{:S(2)}, u32[]{:S(2)}) collective-permute-start(bf16[24,4,128]{2,1,0:T(4,128)(2,1)} %shard_map.101), channel_id=1, source_target_pairs={{0,4},{4,8},{8,12},{12,16},{16,20},{20,24},{24,28},{1,5},{5,9},{9,... | collective-permute-start | bytes 73736 | tf_op jit(solution)/shard_map/ppermute | solution.py:397
  7.5 1.8 %copy-start.2 = (f32[4,512]{1,0:T(4,128)S(1)}, f32[4,512]{1,0:T(4,128)}, u32[]{:S(2)}) copy-start(f32[4,512]{1,0:T(4,128)} %decay_ref.3) | copy-start | bytes 24580
  7.5 1.8 %copy-start.3 = (f32[4,512]{1,0:T(4,128)S(1)}, f32[4,512]{1,0:T(4,128)}, u32[]{:S(2)}) copy-start(f32[4,512]{1,0:T(4,128)} %strength_ref.3) | copy-start | bytes 24580
  7.5 1.8 %copy-start.4 = (s32[8]{0:T(128)S(1)}, s32[8]{0:T(128)}, u32[]{:S(2)}) copy-start(s32[8]{0:T(128)} %resets.3) | copy-start | bytes 100
  9.4 8.7 %copy-start.6 = (bf16[512,4,128]{2,1,0:T(4,128)(2,1)S(1)}, bf16[512,4,128]{2,1,0:T(4,128)(2,1)}, u32[]{:S(2)}) copy-start(bf16[512,4,128]{2,1,0:T(4,128)(2,1)} %param.13) | copy-start | bytes 1572868
  9.4 8.7 %copy-start.7 = (bf16[512,4,128]{2,1,0:T(4,128)(2,1)S(1)}, bf16[512,4,128]{2,1,0:T(4,128)(2,1)}, u32[]{:S(2)}) copy-start(bf16[512,4,128]{2,1,0:T(4,128)(2,1)} %refs_0_.1) | copy-start | bytes 1572868
  14.4 3.7 %copy-start.5 = (f32[128]{0:T(128)S(1)}, f32[128]{0:T(128)}, u32[]{:S(2)}) copy-start(f32[128]{0:T(128)} %param.18) | copy-start | bytes 1540
  14.5 10.2 %collective-permute-start.1 = (bf16[2,128,256]{2,1,0:T(8,128)(2,1)S(1)}, bf16[2,128,256]{2,1,0:T(8,128)(2,1)S(1)}, u32[]{:S(2)}, u32[]{:S(2)}) collective-permute-start(bf16[2,128,256]{2,1,0:T(8,128)(2,1)S(1)} %get-tuple-element.42.refs_0_), channel_id=1, source_target_pairs={{0,4},{4,0},{8,12},{12,8},{1,5},{5,1},{9,13},{13,9},{2,6},{6,2},{1... | collective-permute-start | bytes 393224 | tf_op jit(solution)/shard_map/ppermute | solution.py:401
  16.0 8.7 %collective-permute-start.2 = (bf16[2,128,256]{2,1,0:T(8,128)(2,1)S(1)}, bf16[2,128,256]{2,1,0:T(8,128)(2,1)S(1)}, u32[]{:S(2)}, u32[]{:S(2)}) collective-permute-start(bf16[2,128,256]{2,1,0:T(8,128)(2,1)S(1)} %get-tuple-element.42.refs_0_), channel_id=1, source_target_pairs={{0,8},{4,12},{8,0},{12,4},{1,9},{5,13},{9,1},{13,5},{2,10},{6,14},... | collective-permute-start | bytes 393224 | tf_op jit(solution)/shard_map/ppermute | solution.py:401
  17.0 7.7 %collective-permute-start.3 = (bf16[2,128,256]{2,1,0:T(8,128)(2,1)S(1)}, bf16[2,128,256]{2,1,0:T(8,128)(2,1)S(1)}, u32[]{:S(2)}, u32[]{:S(2)}) collective-permute-start(bf16[2,128,256]{2,1,0:T(8,128)(2,1)S(1)} %get-tuple-element.42.refs_0_), channel_id=1, source_target_pairs={{0,12},{4,8},{8,4},{12,0},{1,13},{5,9},{9,5},{13,1},{2,14},{6,10},... | collective-permute-start | bytes 393224 | tf_op jit(solution)/shard_map/ppermute | solution.py:401
  25.4 8.1 %collective-permute-start.10 = (bf16[2,128,256]{2,1,0:T(8,128)(2,1)S(1)}, bf16[2,128,256]{2,1,0:T(8,128)(2,1)S(1)}, u32[]{:S(2)}, u32[]{:S(2)}) collective-permute-start(bf16[2,128,256]{2,1,0:T(8,128)(2,1)S(1)} %get-tuple-element.51.refs_0_), channel_id=1, source_target_pairs={{0,12},{4,8},{8,4},{12,0},{1,13},{5,9},{9,5},{13,1},{2,14},{6,10},... | collective-permute-start | bytes 393224 | tf_op jit(solution)/shard_map/ppermute | solution.py:401
  27.4 6.1 %collective-permute-start.8 = (bf16[2,128,256]{2,1,0:T(8,128)(2,1)S(1)}, bf16[2,128,256]{2,1,0:T(8,128)(2,1)S(1)}, u32[]{:S(2)}, u32[]{:S(2)}) collective-permute-start(bf16[2,128,256]{2,1,0:T(8,128)(2,1)S(1)} %get-tuple-element.51.refs_0_), channel_id=1, source_target_pairs={{0,4},{4,0},{8,12},{12,8},{1,5},{5,1},{9,13},{13,9},{2,6},{6,2},{1... | collective-permute-start | bytes 393224 | tf_op jit(solution)/shard_map/ppermute | solution.py:401
  28.9 5.0 %collective-permute-start.9 = (bf16[2,128,256]{2,1,0:T(8,128)(2,1)S(1)}, bf16[2,128,256]{2,1,0:T(8,128)(2,1)S(1)}, u32[]{:S(2)}, u32[]{:S(2)}) collective-permute-start(bf16[2,128,256]{2,1,0:T(8,128)(2,1)S(1)} %get-tuple-element.51.refs_0_), channel_id=1, source_target_pairs={{0,8},{4,12},{8,0},{12,4},{1,9},{5,13},{9,1},{13,5},{2,10},{6,14},... | collective-permute-start | bytes 393224 | tf_op jit(solution)/shard_map/ppermute | solution.py:401
  29.0 2.2 %collective-permute-start.4 = (bf16[2,128,128]{2,1,0:T(8,128)(2,1)S(1)}, bf16[2,128,128]{2,1,0:T(8,128)(2,1)S(1)}, u32[]{:S(2)}, u32[]{:S(2)}) collective-permute-start(bf16[2,128,128]{2,1,0:T(8,128)(2,1)S(1)} %get-tuple-element.46), channel_id=1, source_target_pairs={{0,16},{1,17},{2,18},{3,19},{4,20},{5,21},{6,22},{7,23},{8,24},{9,... | collective-permute-start | bytes 196616 | tf_op jit(solution)/shard_map/ppermute | solution.py:397
  31.9 10.5 %collective-permute-start.5 = (bf16[512,256]{1,0:T(8,128)(2,1)S(1)}, bf16[512,256]{1,0:T(8,128)(2,1)S(1)}, u32[]{:S(2)}, u32[]{:S(2)}) collective-permute-start(bf16[512,256]{1,0:T(8,128)(2,1)S(1)} %shard_map.105), channel_id=1, source_target_pairs={{0,1},{1,2},{2,3},{3,0},{4,5},{5,6},{6,7},{7,4},{8,9},{9,10},{10,1... | collective-permute-start | bytes 786440 | tf_op jit(solution)/shard_map/ppermute | solution.py:593
  34.6 3.6 %collective-permute-start.11 = (bf16[2,128,128]{2,1,0:T(8,128)(2,1)S(1)}, bf16[2,128,128]{2,1,0:T(8,128)(2,1)S(1)}, u32[]{:S(2)}, u32[]{:S(2)}) collective-permute-start(bf16[2,128,128]{2,1,0:T(8,128)(2,1)S(1)} %get-tuple-element.55), channel_id=1, source_target_pairs={{0,16},{1,17},{2,18},{3,19},{4,20},{5,21},{6,22},{7,23},{8,24},{9,... | collective-permute-start | bytes 196616 | tf_op jit(solution)/shard_map/ppermute | solution.py:397
  36.5 4.0 %copy-start = (bf16[2048,1024]{1,0:T(8,128)(2,1)S(1)}, bf16[2048,1024]{1,0:T(8,128)(2,1)}, u32[]{:S(2)}) copy-start(bf16[2048,1024]{1,0:T(8,128)(2,1)} %weights_ref.1) | copy-start | bytes 12582916
  38.9 11.1 %collective-permute-start.12 = (bf16[512,256]{1,0:T(8,128)(2,1)S(1)}, bf16[512,256]{1,0:T(8,128)(2,1)S(1)}, u32[]{:S(2)}, u32[]{:S(2)}) collective-permute-start(bf16[512,256]{1,0:T(8,128)(2,1)S(1)} %shard_map.107), channel_id=1, source_target_pairs={{0,1},{1,2},{2,3},{3,0},{4,5},{5,6},{6,7},{7,4},{8,9},{9,10},{10,1... | collective-permute-start | bytes 786440 | tf_op jit(solution)/shard_map/ppermute | solution.py:593
  42.4 13.2 %collective-permute-start.6 = (bf16[512,256]{1,0:T(8,128)(2,1)S(1)}, bf16[512,256]{1,0:T(8,128)(2,1)S(1)}, u32[]{:S(2)}, u32[]{:S(2)}) collective-permute-start(bf16[512,256]{1,0:T(8,128)(2,1)S(1)} %collective-permute-done.5), channel_id=1, source_target_pairs={{0,1},{1,2},{2,3},{3,0},{4,5},{5,6},{6,7},{7,4},{8,9},{9,10},{10,1... | collective-permute-start | bytes 786440 | tf_op jit(solution)/shard_map/ppermute | solution.py:593
  50.0 11.2 %collective-permute-start.13 = (bf16[512,256]{1,0:T(8,128)(2,1)S(1)}, bf16[512,256]{1,0:T(8,128)(2,1)S(1)}, u32[]{:S(2)}, u32[]{:S(2)}) collective-permute-start(bf16[512,256]{1,0:T(8,128)(2,1)S(1)} %collective-permute-done.12), channel_id=1, source_target_pairs={{0,1},{1,2},{2,3},{3,0},{4,5},{5,6},{6,7},{7,4},{8,9},{9,10},{10,1... | collective-permute-start | bytes 786440 | tf_op jit(solution)/shard_map/ppermute | solution.py:593
  55.6 11.2 %collective-permute-start.7 = (bf16[512,256]{1,0:T(8,128)(2,1)S(1)}, bf16[512,256]{1,0:T(8,128)(2,1)S(1)}, u32[]{:S(2)}, u32[]{:S(2)}) collective-permute-start(bf16[512,256]{1,0:T(8,128)(2,1)S(1)} %collective-permute-done.6), channel_id=1, source_target_pairs={{0,1},{1,2},{2,3},{3,0},{4,5},{5,6},{6,7},{7,4},{8,9},{9,10},{10,1... | collective-permute-start | bytes 786440 | tf_op jit(solution)/shard_map/ppermute | solution.py:593
  61.2 9.6 %collective-permute-start.14 = (bf16[512,256]{1,0:T(8,128)(2,1)S(1)}, bf16[512,256]{1,0:T(8,128)(2,1)S(1)}, u32[]{:S(2)}, u32[]{:S(2)}) collective-permute-start(bf16[512,256]{1,0:T(8,128)(2,1)S(1)} %collective-permute-done.13), channel_id=1, source_target_pairs={{0,1},{1,2},{2,3},{3,0},{4,5},{5,6},{6,7},{7,4},{8,9},{9,10},{10,1... | collective-permute-start | bytes 786440 | tf_op jit(solution)/shard_map/ppermute | solution.py:593

commit v19 on v16

--- a/solution.py
+++ b/solution.py
@@ -377,14 +377,13 @@
             ).astype(BF16)
 
 
-def last_kernel(section, first_ref, second_ref, block_ref, weights_ref, out_ref, tiles, written):
+def last_kernel(section, total_ref, block_ref, weights_ref, out_ref, tiles, written):
     width = block_ref.shape[1]
     rows = weights_ref[pl.ds(pl.multiple_of(section[0] * width, width), width), :]
     copies = []
-    for i in range(first_ref.shape[0] // CHUNK):
+    for i in range(total_ref.shape[0] // CHUNK):
         here = rows_of(i)
-        total = (first_ref[here] + second_ref[here]) + mul(block_ref[here], rows)
-        tiles[here] = total.astype(BF16)
+        tiles[here] = (total_ref[here] + mul(block_ref[here], rows)).astype(BF16)
         copies.append(pltpu.make_async_copy(tiles.at[here], out_ref.at[here], written.at[i]))
         copies[-1].start()
     for copy in copies:
@@ -396,8 +395,11 @@
     return lax.ppermute(value, axis, [(i, i + steps) for i in range(count - steps)])
 
 
-def exchange(own_map, leaves):
-    received = [lax.ppermute(own_map, "leaf", pairs_at(k, leaves)) for k in range(1, leaves)]
+def exchange(own_map, later, leaves):
+    received = [
+        lax.ppermute(later if k == 1 else own_map, "leaf", pairs_at(k, leaves))
+        for k in range(1, leaves)
+    ]
     return [own_map] + received
 
 
@@ -417,7 +419,7 @@
         out_specs=VMEM,
         scratch_shapes=[pltpu.SemaphoreType.DMA((len(inputs),))],
         compiler_params=pltpu.CompilerParams(vmem_limit_bytes=65_700_000),
-        cost_estimate=pl.CostEstimate(flops=10**9, bytes_accessed=2**16, transcendentals=0),
+        cost_estimate=pl.CostEstimate(flops=4 * 10**9, bytes_accessed=2**16, transcendentals=0),
     )(*inputs)
 
 
@@ -513,19 +515,19 @@
     )(arrived, before, *reads)
 
 
-def last_projected(section, first, second, block, weights):
-    length, columns = first.shape
+def last_projected(section, total, block, weights):
+    length, columns = total.shape
     return pl.pallas_call(
         last_kernel,
         out_shape=jax.ShapeDtypeStruct((length, columns), BF16),
-        in_specs=[SMEM] + [VMEM] * 4,
+        in_specs=[SMEM] + [VMEM] * 3,
         out_specs=pl.BlockSpec(memory_space=pl.ANY),
         scratch_shapes=[
             pltpu.VMEM((length, columns), BF16),
             pltpu.SemaphoreType.DMA((length // CHUNK,)),
         ],
         compiler_params=LAST_PARAMS,
-    )(section.astype(jnp.int32).reshape(1), first, second, block, weights)
+    )(section.astype(jnp.int32).reshape(1), total, block, weights)
 
 
 def after(first, *values):
@@ -565,13 +567,14 @@
     )
     size = heads // GROUPS
     blocks = []
-    exchanged = [exchange(own_maps[0], leaves)]
+    exchanged = [exchange(own_maps[0], own_maps[0], leaves)]
     for g in range(GROUPS):
         earlier = blocks[-1] if blocks else reads[0]
         maps = after(earlier, *exchanged[g])
         before, state, *trans = join(place, maps, links)
         if g + 1 < GROUPS:
-            exchanged.append(exchange(*after(state, own_maps[g + 1]), leaves))
+            own_map = own_maps[g + 1]
+            exchanged.append(exchange(own_map, *after(state, own_map), leaves))
         arrived = from_behind(state.astype(BF16), "chain", 1)
         for _ in range(links - 1):
             passed = jnp.einsum(
@@ -593,7 +596,7 @@
         for g, block in enumerate(blocks):
             section = owner * GROUPS + g
             if last and g + 1 == GROUPS:
-                return last_projected(section, *sums, block, weights)
+                return last_projected(section, sum(sums[1:], sums[0]), block, weights)
             rows = lax.dynamic_slice_in_dim(weights, section * width, width, 0)
             term = jnp.dot(block, rows, preferred_element_type=F32)
             sums[g] = term if sums[g] is None else sums[g] + term

time: 71.4 us -> 72.3 us (1.013)
  starting transfers between devices: 18.6 us -> 19.7 us
    ppermute x6, starting transfers between devices: 7.11 us -> 7.97 us  [exchange(): lax.ppermute(later if k == 1 else own_map, 'leaf', pairs_at(k, leaves))]
  transfers between devices with their start and end apart: 15 -> 15, of which waited for: 8 -> 7; matrix products, arithmetic and copies ran while one was open for 8% -> 8% of each run, Pallas kernels for 13% -> 14%
where the time goes in v19:
time: 72.3 us; the launch traced here: 72 us
  waiting for transfers between devices  28 us (39%)
  starting transfers between devices  19.7 us (27%)
  Pallas kernels  17.9 us (25%)
  matrix products  4.59 us (6%)
  local copies, waits for them, and re-layouts  1.38 us (2%)
    ppermute x6, waiting for transfers between devices, on_device(): lax.ppermute(x, 'head', around)  27.1 us
    ppermute x3, starting transfers between devices, from_behind(): lax.ppermute(value, axis, [(i, i + steps) for i in range(count - steps)])  8.28 us
    ppermute x6, starting transfers between devices, exchange(): lax.ppermute(later if k == 1 else own_map, 'leaf', pairs_at(k, leaves))  7.97 us
    pallas_call x1, Pallas kernels, reads_of(): pl.pallas_call(functools.partial(reads_kernel, base), out_shape=(jax.Shap...  5.42 us
    pallas_call x1, Pallas kernels, maps_of(): pl.pallas_call(functools.partial(maps_kernel, base), out_shape=(jax.Shape...  5.05 us
    dot_general x7, matrix products, on_device(): term = jnp.dot(block, rows, preferred_element_type=F32)  4.59 us
    ppermute x6, starting transfers between devices, on_device(): lax.ppermute(x, 'head', around)  3.45 us
    pallas_call x1, Pallas kernels, filters_of(): pl.pallas_call(filters_kernel, out_shape=(per_token, per_token, jax.Shape...  1.78 us
  transfers between devices with their start and end apart: 15, of which 7 were waited for; matrix products, arithmetic and copies ran while one was open for 8% of the time, Pallas kernels for 14%

profile of v19, /device:TPU:0, one launch (start us, length us, event | category | flops | bytes accessed | tf_op | source)
XLA Modules:
  0.0 72.0 jit_solution(6932167581365181194)
XLA Ops:
  0.0 1.4 %shard_map.101 = bf16[24,4,128]{2,1,0:T(4,128)(2,1)} custom-call(bf16[512,4,128]{2,1,0:T(4,128)(2,1)} %refs_0_.1, bf16[512,4,128]{2,1,0:T(4,128)(2,1)} %refs_1_.1, bf16[512,4,128]{2,1,0:T(4,128)(2,1)} %refs_2_.1), custom_call_target="tpu_custom_call" | custom-call | flops 4000000000 | bytes 65536 | tf_op jit(solution)/shard_map/pallas_call | solution.py:415
  1.4 4.8 %collective-permute-start = (bf16[24,4,128]{2,1,0:T(4,128)(2,1)}, bf16[24,4,128]{2,1,0:T(4,128)(2,1)S(1)}, u32[]{:S(2)}, u32[]{:S(2)}) collective-permute-start(bf16[24,4,128]{2,1,0:T(4,128)(2,1)} %shard_map.101), channel_id=1, source_target_pairs={{0,4},{4,8},{8,12},{12,16},{16,20},{20,24},{24,28},{1,5},{5,9},{9,... | collective-permute-start | bytes 73736 | tf_op jit(solution)/shard_map/ppermute | solution.py:395
  6.3 1.2 %copy_bitcast_fusion.2 = (bf16[4,512,128]{2,1,0:T(8,128)(2,1)S(1)}, bf16[4,512,128]{2,1,0:T(8,128)(2,1)S(1)}) fusion(bf16[512,4,128]{2,1,0:T(4,128)(2,1)S(1)} %copy-done.8, bf16[512,4,128]{2,1,0:T(4,128)(2,1)} %refs_1_.1), kind=kLoop, calls=%fused_computation.3 | loop fusion | bytes 2097152 | tf_op jit(solution)/shard_map/transpose | solution.py:552
  7.5 1.8 %shard_map.100 = (bf16[4,512,128]{2,1,0:T(8,128)(2,1)S(1)}, bf16[4,512,128]{2,1,0:T(8,128)(2,1)S(1)}, f32[2,4,16,128]{3,2,1,0:T(8,128)S(1)}) custom-call(bf16[4,512,128]{2,1,0:T(8,128)(2,1)S(1)} %get-tuple-element.58.key_ref, bf16[4,512,128]{2,1,0:T(8,128)(2,1)S(1)} %get-tuple-element.57.value_ref, f32[3,4,4,128]{3,2,1,0:T(4,128)S(1)} %copy-done.1), custom_call_target="tpu_custom_call" | custom-call | flops 3000000000 | bytes 4194304 | tf_op jit(solution)/shard_map/pallas_call | solution.py:429
  9.4 5.1 %shard_map.102 = (bf16[4,512,128]{2,1,0:T(8,128)(2,1)S(1)}, f32[4,512,256]{2,1,0:T(8,128)S(1)}, f32[4,3,128,256]{3,2,1,0:T(8,128)S(1)}, bf16[2,128,256]{2,1,0:T(8,128)(2,1)S(1)}, bf16[2,128,256]{2,1,0:T(8,128)(2,1)S(1)}) custom-call(s32[8]{0:T(128)S(1)} %copy-done.4, bf16[4,512,128]{2,1,0:T(8,128)(2,1)S(1)} %get-tuple-element.31.unit_in_ref, ...), custom_call_target="tpu_custom_call" | custom-call | flops 5000000000 | bytes 4194304 | tf_op jit(solution)/shard_map/pallas_call | solution.py:445
  14.5 2.0 %collective-permute-start.3 = (bf16[2,128,256]{2,1,0:T(8,128)(2,1)S(1)}, bf16[2,128,256]{2,1,0:T(8,128)(2,1)S(1)}, u32[]{:S(2)}, u32[]{:S(2)}) collective-permute-start(bf16[2,128,256]{2,1,0:T(8,128)(2,1)S(1)} %get-tuple-element.42.refs_0_), channel_id=1, source_target_pairs={{0,12},{4,8},{8,4},{12,0},{1,13},{5,9},{9,5},{13,1},{2,14},{6,10},... | collective-permute-start | bytes 393224 | tf_op jit(solution)/shard_map/ppermute | solution.py:400
  16.4 1.1 %collective-permute-start.2 = (bf16[2,128,256]{2,1,0:T(8,128)(2,1)S(1)}, bf16[2,128,256]{2,1,0:T(8,128)(2,1)S(1)}, u32[]{:S(2)}, u32[]{:S(2)}) collective-permute-start(bf16[2,128,256]{2,1,0:T(8,128)(2,1)S(1)} %get-tuple-element.42.refs_0_), channel_id=1, source_target_pairs={{0,8},{4,12},{8,0},{12,4},{1,9},{5,13},{9,1},{13,5},{2,10},{6,14},... | collective-permute-start | bytes 393224 | tf_op jit(solution)/shard_map/ppermute | solution.py:400
  18.0 1.9 %collective-permute-start.10 = (bf16[2,128,256]{2,1,0:T(8,128)(2,1)S(1)}, bf16[2,128,256]{2,1,0:T(8,128)(2,1)S(1)}, u32[]{:S(2)}, u32[]{:S(2)}) collective-permute-start(bf16[2,128,256]{2,1,0:T(8,128)(2,1)S(1)} %get-tuple-element.51.refs_0_), channel_id=1, source_target_pairs={{0,12},{4,8},{8,4},{12,0},{1,13},{5,9},{9,5},{13,1},{2,14},{6,10},... | collective-permute-start | bytes 393224 | tf_op jit(solution)/shard_map/ppermute | solution.py:400
  19.9 1.1 %collective-permute-start.9 = (bf16[2,128,256]{2,1,0:T(8,128)(2,1)S(1)}, bf16[2,128,256]{2,1,0:T(8,128)(2,1)S(1)}, u32[]{:S(2)}, u32[]{:S(2)}) collective-permute-start(bf16[2,128,256]{2,1,0:T(8,128)(2,1)S(1)} %get-tuple-element.51.refs_0_), channel_id=1, source_target_pairs={{0,8},{4,12},{8,0},{12,4},{1,9},{5,13},{9,1},{13,5},{2,10},{6,14},... | collective-permute-start | bytes 393224 | tf_op jit(solution)/shard_map/ppermute | solution.py:400
  21.2 5.4 %shard_map.103 = (bf16[4,512,128]{2,1,0:T(8,128)(2,1)S(1)}, f32[4,512,128]{2,1,0:T(8,128)S(1)}, f32[4,512,128]{2,1,0:T(8,128)S(1)}) custom-call(s32[8]{0:T(128)S(1)} %copy-done.4, bf16[4,512,128]{2,1,0:T(8,128)(2,1)S(1)} %bitcast.20, bf16[4,512,128]{2,1,0:T(8,128)(2,1)S(1)} %bitcast.21, f32[1,128]{1,0:T(1,128)S(1)} %bitcast.22, ...), custom_call_target="tpu_custom_call" | custom-call | flops 3000000000 | bytes 4194304 | tf_op jit(solution)/shard_map/pallas_call | solution.py:471
  27.4 1.5 %collective-permute-start.8 = (bf16[2,128,256]{2,1,0:T(8,128)(2,1)S(1)}, bf16[2,128,256]{2,1,0:T(8,128)(2,1)S(1)}, u32[]{:S(2)}, u32[]{:S(2)}) collective-permute-start(bf16[2,128,256]{2,1,0:T(8,128)(2,1)S(1)} %get-tuple-element.51.refs_0_), channel_id=1, source_target_pairs={{0,4},{4,0},{8,12},{12,8},{1,5},{5,1},{9,13},{13,9},{2,6},{6,2},{1... | collective-permute-start | bytes 393224 | tf_op jit(solution)/shard_map/ppermute | solution.py:400
  28.8 1.3 %collective-permute-start.4 = (bf16[2,128,128]{2,1,0:T(8,128)(2,1)S(1)}, bf16[2,128,128]{2,1,0:T(8,128)(2,1)S(1)}, u32[]{:S(2)}, u32[]{:S(2)}) collective-permute-start(bf16[2,128,128]{2,1,0:T(8,128)(2,1)S(1)} %get-tuple-element.46), channel_id=1, source_target_pairs={{0,16},{1,17},{2,18},{3,19},{4,20},{5,21},{6,22},{7,23},{8,24},{9,... | collective-permute-start | bytes 196616 | tf_op jit(solution)/shard_map/ppermute | solution.py:395
  30.2 0.8 %collective-permute-done.4.arrived_ref = bf16[2,128,128]{2,1,0:T(8,128)(2,1)S(1)} collective-permute-done((bf16[2,128,128]{2,1,0:T(8,128)(2,1)S(1)}, bf16[2,128,128]{2,1,0:T(8,128)(2,1)S(1)}, u32[]{:S(2)}, u32[]{:S(2)}) %collective-permute-start.4) | collective-permute-done | bytes 65568 | tf_op jit(solution)/shard_map/ppermute | solution.py:395
  31.7 1.6 %collective-permute-start.5 = (bf16[512,256]{1,0:T(8,128)(2,1)S(1)}, bf16[512,256]{1,0:T(8,128)(2,1)S(1)}, u32[]{:S(2)}, u32[]{:S(2)}) collective-permute-start(bf16[512,256]{1,0:T(8,128)(2,1)S(1)} %shard_map.105), channel_id=1, source_target_pairs={{0,1},{1,2},{2,3},{3,0},{4,5},{5,6},{6,7},{7,4},{8,9},{9,10},{10,1... | collective-permute-start | bytes 786440 | tf_op jit(solution)/shard_map/ppermute | solution.py:595
  34.1 2.2 %collective-permute-start.11 = (bf16[2,128,128]{2,1,0:T(8,128)(2,1)S(1)}, bf16[2,128,128]{2,1,0:T(8,128)(2,1)S(1)}, u32[]{:S(2)}, u32[]{:S(2)}) collective-permute-start(bf16[2,128,128]{2,1,0:T(8,128)(2,1)S(1)} %get-tuple-element.55), channel_id=1, source_target_pairs={{0,16},{1,17},{2,18},{3,19},{4,20},{5,21},{6,22},{7,23},{8,24},{9,... | collective-permute-start | bytes 196616 | tf_op jit(solution)/shard_map/ppermute | solution.py:395
  36.3 1.6 %fusion.11 = f32[512,1024]{1,0:T(8,128)S(1)} fusion(bf16[512,256]{1,0:T(8,128)(2,1)S(1)} %shard_map.105, bf16[2048,1024]{1,0:T(8,128)(2,1)} %weights_ref.1, s32[]{:T(128)S(6)} %select_n.21), kind=kOutput, calls=%fused_computation.16 | convolution fusion | flops 268435456 | bytes 2883588 | tf_op jit(solution)/shard_map/dot_general | solution.py:601
  38.7 1.6 %collective-permute-start.12 = (bf16[512,256]{1,0:T(8,128)(2,1)S(1)}, bf16[512,256]{1,0:T(8,128)(2,1)S(1)}, u32[]{:S(2)}, u32[]{:S(2)}) collective-permute-start(bf16[512,256]{1,0:T(8,128)(2,1)S(1)} %shard_map.107), channel_id=1, source_target_pairs={{0,1},{1,2},{2,3},{3,0},{4,5},{5,6},{6,7},{7,4},{8,9},{9,10},{10,1... | collective-permute-start | bytes 786440 | tf_op jit(solution)/shard_map/ppermute | solution.py:595
  40.7 1.4 %collective-permute-done.5 = bf16[512,256]{1,0:T(8,128)(2,1)S(1)} collective-permute-done((bf16[512,256]{1,0:T(8,128)(2,1)S(1)}, bf16[512,256]{1,0:T(8,128)(2,1)S(1)}, u32[]{:S(2)}, u32[]{:S(2)}) %collective-permute-start.5) | collective-permute-done | bytes 262176 | tf_op jit(solution)/shard_map/ppermute | solution.py:595
  42.8 6.9 %collective-permute-done.12 = bf16[512,256]{1,0:T(8,128)(2,1)S(1)} collective-permute-done((bf16[512,256]{1,0:T(8,128)(2,1)S(1)}, bf16[512,256]{1,0:T(8,128)(2,1)S(1)}, u32[]{:S(2)}, u32[]{:S(2)}) %collective-permute-start.12) | collective-permute-done | bytes 262176 | tf_op jit(solution)/shard_map/ppermute | solution.py:595
  50.2 5.2 %collective-permute-done.6 = bf16[512,256]{1,0:T(8,128)(2,1)S(1)} collective-permute-done((bf16[512,256]{1,0:T(8,128)(2,1)S(1)}, bf16[512,256]{1,0:T(8,128)(2,1)S(1)}, u32[]{:S(2)}, u32[]{:S(2)}) %collective-permute-start.6) | collective-permute-done | bytes 262176 | tf_op jit(solution)/shard_map/ppermute | solution.py:595
  55.8 5.2 %collective-permute-done.13 = bf16[512,256]{1,0:T(8,128)(2,1)S(1)} collective-permute-done((bf16[512,256]{1,0:T(8,128)(2,1)S(1)}, bf16[512,256]{1,0:T(8,128)(2,1)S(1)}, u32[]{:S(2)}, u32[]{:S(2)}) %collective-permute-start.13) | collective-permute-done | bytes 262176 | tf_op jit(solution)/shard_map/ppermute | solution.py:595
  61.5 5.2 %collective-permute-done.7 = bf16[512,256]{1,0:T(8,128)(2,1)S(1)} collective-permute-done((bf16[512,256]{1,0:T(8,128)(2,1)S(1)}, bf16[512,256]{1,0:T(8,128)(2,1)S(1)}, u32[]{:S(2)}, u32[]{:S(2)}) %collective-permute-start.7) | collective-permute-done | bytes 262176 | tf_op jit(solution)/shard_map/ppermute | solution.py:595
  67.4 3.2 %collective-permute-done.14.block_ref = bf16[512,256]{1,0:T(8,128)(2,1)S(1)} collective-permute-done((bf16[512,256]{1,0:T(8,128)(2,1)S(1)}, bf16[512,256]{1,0:T(8,128)(2,1)S(1)}, u32[]{:S(2)}, u32[]{:S(2)}) %collective-permute-start.14) | collective-permute-done | bytes 262176 | tf_op jit(solution)/shard_map/ppermute | solution.py:595
  70.6 1.2 %shard_map.108 = bf16[512,1024]{1,0:T(8,128)(2,1)} custom-call(s32[1]{0:T(128)} %bitcast.section, f32[512,1024]{1,0:T(8,128)S(1)} %add_add_fusion.total_ref, bf16[512,256]{1,0:T(8,128)(2,1)S(1)} %collective-permute-done.14.block_ref, bf16[2048,1024]{1,0:T(8,128)(2,1)S(1)} %copy-done), custom_call_target="tpu_custom_call" | custom-call | tf_op jit(solution)/shard_map/pallas_call | solution.py:520
  (43 shorter events, 6.8 us)
Async XLA Ops:
  0.0 6.3 %copy-start.8 = (bf16[512,4,128]{2,1,0:T(4,128)(2,1)S(1)}, bf16[512,4,128]{2,1,0:T(4,128)(2,1)}, u32[]{:S(2)}) copy-start(bf16[512,4,128]{2,1,0:T(4,128)(2,1)} %refs_2_.1) | copy-start | bytes 1572868
  1.4 6.1 %copy-start.1 = (f32[3,4,4,128]{3,2,1,0:T(4,128)S(1)}, f32[3,4,4,128]{3,2,1,0:T(4,128)}, u32[]{:S(2)}) copy-start(f32[3,4,4,128]{3,2,1,0:T(4,128)} %taps_ref.5) | copy-start | bytes 73732
  1.4 7.9 %collective-permute-start = (bf16[24,4,128]{2,1,0:T(4,128)(2,1)}, bf16[24,4,128]{2,1,0:T(4,128)(2,1)S(1)}, u32[]{:S(2)}, u32[]{:S(2)}) collective-permute-start(bf16[24,4,128]{2,1,0:T(4,128)(2,1)} %shard_map.101), channel_id=1, source_target_pairs={{0,4},{4,8},{8,12},{12,16},{16,20},{20,24},{24,28},{1,5},{5,9},{9,... | collective-permute-start | bytes 73736 | tf_op jit(solution)/shard_map/ppermute | solution.py:395
  7.5 1.8 %copy-start.2 = (f32[4,512]{1,0:T(4,128)S(1)}, f32[4,512]{1,0:T(4,128)}, u32[]{:S(2)}) copy-start(f32[4,512]{1,0:T(4,128)} %decay_ref.3) | copy-start | bytes 24580
  7.5 1.8 %copy-start.3 = (f32[4,512]{1,0:T(4,128)S(1)}, f32[4,512]{1,0:T(4,128)}, u32[]{:S(2)}) copy-start(f32[4,512]{1,0:T(4,128)} %strength_ref.3) | copy-start | bytes 24580
  7.5 1.8 %copy-start.4 = (s32[8]{0:T(128)S(1)}, s32[8]{0:T(128)}, u32[]{:S(2)}) copy-start(s32[8]{0:T(128)} %resets.3) | copy-start | bytes 100
  9.4 11.6 %copy-start.6 = (bf16[512,4,128]{2,1,0:T(4,128)(2,1)S(1)}, bf16[512,4,128]{2,1,0:T(4,128)(2,1)}, u32[]{:S(2)}) copy-start(bf16[512,4,128]{2,1,0:T(4,128)(2,1)} %refs_0_.1) | copy-start | bytes 1572868
  9.4 11.7 %copy-start.7 = (bf16[512,4,128]{2,1,0:T(4,128)(2,1)S(1)}, bf16[512,4,128]{2,1,0:T(4,128)(2,1)}, u32[]{:S(2)}) copy-start(bf16[512,4,128]{2,1,0:T(4,128)(2,1)} %param.13) | copy-start | bytes 1572868
  14.5 6.7 %copy-start.5 = (f32[128]{0:T(128)S(1)}, f32[128]{0:T(128)}, u32[]{:S(2)}) copy-start(f32[128]{0:T(128)} %param.18) | copy-start | bytes 1540
  14.5 12.1 %collective-permute-start.3 = (bf16[2,128,256]{2,1,0:T(8,128)(2,1)S(1)}, bf16[2,128,256]{2,1,0:T(8,128)(2,1)S(1)}, u32[]{:S(2)}, u32[]{:S(2)}) collective-permute-start(bf16[2,128,256]{2,1,0:T(8,128)(2,1)S(1)} %get-tuple-element.42.refs_0_), channel_id=1, source_target_pairs={{0,12},{4,8},{8,4},{12,0},{1,13},{5,9},{9,5},{13,1},{2,14},{6,10},... | collective-permute-start | bytes 393224 | tf_op jit(solution)/shard_map/ppermute | solution.py:400
  16.4 10.2 %collective-permute-start.2 = (bf16[2,128,256]{2,1,0:T(8,128)(2,1)S(1)}, bf16[2,128,256]{2,1,0:T(8,128)(2,1)S(1)}, u32[]{:S(2)}, u32[]{:S(2)}) collective-permute-start(bf16[2,128,256]{2,1,0:T(8,128)(2,1)S(1)} %get-tuple-element.42.refs_0_), channel_id=1, source_target_pairs={{0,8},{4,12},{8,0},{12,4},{1,9},{5,13},{9,1},{13,5},{2,10},{6,14},... | collective-permute-start | bytes 393224 | tf_op jit(solution)/shard_map/ppermute | solution.py:400
  17.5 9.1 %collective-permute-start.1 = (bf16[2,128,256]{2,1,0:T(8,128)(2,1)S(1)}, bf16[2,128,256]{2,1,0:T(8,128)(2,1)S(1)}, u32[]{:S(2)}, u32[]{:S(2)}) collective-permute-start(bf16[2,128,256]{2,1,0:T(8,128)(2,1)S(1)} %get-tuple-element.42.refs_0_), channel_id=1, source_target_pairs={{0,4},{4,0},{8,12},{12,8},{1,5},{5,1},{9,13},{13,9},{2,6},{6,2},{1... | collective-permute-start | bytes 393224 | tf_op jit(solution)/shard_map/ppermute | solution.py:400
  18.0 15.3 %collective-permute-start.10 = (bf16[2,128,256]{2,1,0:T(8,128)(2,1)S(1)}, bf16[2,128,256]{2,1,0:T(8,128)(2,1)S(1)}, u32[]{:S(2)}, u32[]{:S(2)}) collective-permute-start(bf16[2,128,256]{2,1,0:T(8,128)(2,1)S(1)} %get-tuple-element.51.refs_0_), channel_id=1, source_target_pairs={{0,12},{4,8},{8,4},{12,0},{1,13},{5,9},{9,5},{13,1},{2,14},{6,10},... | collective-permute-start | bytes 393224 | tf_op jit(solution)/shard_map/ppermute | solution.py:400
  19.9 13.4 %collective-permute-start.9 = (bf16[2,128,256]{2,1,0:T(8,128)(2,1)S(1)}, bf16[2,128,256]{2,1,0:T(8,128)(2,1)S(1)}, u32[]{:S(2)}, u32[]{:S(2)}) collective-permute-start(bf16[2,128,256]{2,1,0:T(8,128)(2,1)S(1)} %get-tuple-element.51.refs_0_), channel_id=1, source_target_pairs={{0,8},{4,12},{8,0},{12,4},{1,9},{5,13},{9,1},{13,5},{2,10},{6,14},... | collective-permute-start | bytes 393224 | tf_op jit(solution)/shard_map/ppermute | solution.py:400
  27.4 6.0 %collective-permute-start.8 = (bf16[2,128,256]{2,1,0:T(8,128)(2,1)S(1)}, bf16[2,128,256]{2,1,0:T(8,128)(2,1)S(1)}, u32[]{:S(2)}, u32[]{:S(2)}) collective-permute-start(bf16[2,128,256]{2,1,0:T(8,128)(2,1)S(1)} %get-tuple-element.51.refs_0_), channel_id=1, source_target_pairs={{0,4},{4,0},{8,12},{12,8},{1,5},{5,1},{9,13},{13,9},{2,6},{6,2},{1... | collective-permute-start | bytes 393224 | tf_op jit(solution)/shard_map/ppermute | solution.py:400
  28.8 2.2 %collective-permute-start.4 = (bf16[2,128,128]{2,1,0:T(8,128)(2,1)S(1)}, bf16[2,128,128]{2,1,0:T(8,128)(2,1)S(1)}, u32[]{:S(2)}, u32[]{:S(2)}) collective-permute-start(bf16[2,128,128]{2,1,0:T(8,128)(2,1)S(1)} %get-tuple-element.46), channel_id=1, source_target_pairs={{0,16},{1,17},{2,18},{3,19},{4,20},{5,21},{6,22},{7,23},{8,24},{9,... | collective-permute-start | bytes 196616 | tf_op jit(solution)/shard_map/ppermute | solution.py:395
  31.7 10.5 %collective-permute-start.5 = (bf16[512,256]{1,0:T(8,128)(2,1)S(1)}, bf16[512,256]{1,0:T(8,128)(2,1)S(1)}, u32[]{:S(2)}, u32[]{:S(2)}) collective-permute-start(bf16[512,256]{1,0:T(8,128)(2,1)S(1)} %shard_map.105), channel_id=1, source_target_pairs={{0,1},{1,2},{2,3},{3,0},{4,5},{5,6},{6,7},{7,4},{8,9},{9,10},{10,1... | collective-permute-start | bytes 786440 | tf_op jit(solution)/shard_map/ppermute | solution.py:595
  34.1 3.8 %collective-permute-start.11 = (bf16[2,128,128]{2,1,0:T(8,128)(2,1)S(1)}, bf16[2,128,128]{2,1,0:T(8,128)(2,1)S(1)}, u32[]{:S(2)}, u32[]{:S(2)}) collective-permute-start(bf16[2,128,128]{2,1,0:T(8,128)(2,1)S(1)} %get-tuple-element.55), channel_id=1, source_target_pairs={{0,16},{1,17},{2,18},{3,19},{4,20},{5,21},{6,22},{7,23},{8,24},{9,... | collective-permute-start | bytes 196616 | tf_op jit(solution)/shard_map/ppermute | solution.py:395
  36.3 4.0 %copy-start = (bf16[2048,1024]{1,0:T(8,128)(2,1)S(1)}, bf16[2048,1024]{1,0:T(8,128)(2,1)}, u32[]{:S(2)}) copy-start(bf16[2048,1024]{1,0:T(8,128)(2,1)} %weights_ref.1) | copy-start | bytes 12582916
  38.7 11.1 %collective-permute-start.12 = (bf16[512,256]{1,0:T(8,128)(2,1)S(1)}, bf16[512,256]{1,0:T(8,128)(2,1)S(1)}, u32[]{:S(2)}, u32[]{:S(2)}) collective-permute-start(bf16[512,256]{1,0:T(8,128)(2,1)S(1)} %shard_map.107), channel_id=1, source_target_pairs={{0,1},{1,2},{2,3},{3,0},{4,5},{5,6},{6,7},{7,4},{8,9},{9,10},{10,1... | collective-permute-start | bytes 786440 | tf_op jit(solution)/shard_map/ppermute | solution.py:595
  42.2 13.2 %collective-permute-start.6 = (bf16[512,256]{1,0:T(8,128)(2,1)S(1)}, bf16[512,256]{1,0:T(8,128)(2,1)S(1)}, u32[]{:S(2)}, u32[]{:S(2)}) collective-permute-start(bf16[512,256]{1,0:T(8,128)(2,1)S(1)} %collective-permute-done.5), channel_id=1, source_target_pairs={{0,1},{1,2},{2,3},{3,0},{4,5},{5,6},{6,7},{7,4},{8,9},{9,10},{10,1... | collective-permute-start | bytes 786440 | tf_op jit(solution)/shard_map/ppermute | solution.py:595
  49.8 11.2 %collective-permute-start.13 = (bf16[512,256]{1,0:T(8,128)(2,1)S(1)}, bf16[512,256]{1,0:T(8,128)(2,1)S(1)}, u32[]{:S(2)}, u32[]{:S(2)}) collective-permute-start(bf16[512,256]{1,0:T(8,128)(2,1)S(1)} %collective-permute-done.12), channel_id=1, source_target_pairs={{0,1},{1,2},{2,3},{3,0},{4,5},{5,6},{6,7},{7,4},{8,9},{9,10},{10,1... | collective-permute-start | bytes 786440 | tf_op jit(solution)/shard_map/ppermute | solution.py:595
  55.4 11.2 %collective-permute-start.7 = (bf16[512,256]{1,0:T(8,128)(2,1)S(1)}, bf16[512,256]{1,0:T(8,128)(2,1)S(1)}, u32[]{:S(2)}, u32[]{:S(2)}) collective-permute-start(bf16[512,256]{1,0:T(8,128)(2,1)S(1)} %collective-permute-done.6), channel_id=1, source_target_pairs={{0,1},{1,2},{2,3},{3,0},{4,5},{5,6},{6,7},{7,4},{8,9},{9,10},{10,1... | collective-permute-start | bytes 786440 | tf_op jit(solution)/shard_map/ppermute | solution.py:595
  61.0 9.6 %collective-permute-start.14 = (bf16[512,256]{1,0:T(8,128)(2,1)S(1)}, bf16[512,256]{1,0:T(8,128)(2,1)S(1)}, u32[]{:S(2)}, u32[]{:S(2)}) collective-permute-start(bf16[512,256]{1,0:T(8,128)(2,1)S(1)} %collective-permute-done.13), channel_id=1, source_target_pairs={{0,1},{1,2},{2,3},{3,0},{4,5},{5,6},{6,7},{7,4},{8,9},{9,10},{10,1... | collective-permute-start | bytes 786440 | tf_op jit(solution)/shard_map/ppermute | solution.py:595

commit v20 on v16

--- a/solution.py
+++ b/solution.py
@@ -179,27 +179,30 @@
 
 def maps_kernel(
     base, resets, unit_in_ref, value_in_ref, first_ref, rim_ref, taps_ref, decay_ref, strength_ref,
-    unit_ref, solved_ref, starts_ref, *refs,
+    *refs,
 ):
-    *map_refs, rims, padded, value_s, step_s = refs
-    heads, length, depth = unit_ref.shape
+    *results, rims, padded, value_s, step_s = refs
+    heads, length, depth = unit_in_ref.shape
+    unit_refs, solved_refs, starts_refs, map_refs = (
+        results[i * GROUPS : (i + 1) * GROUPS] for i in range(4)
+    )
     chunks = length // CHUNK
-    size = heads // len(map_refs)
+    size = heads // GROUPS
     total_heads = decay_ref.shape[0]
     row, col = indices()
     rims[...] = rim_ref[...].astype(F32)
     for g in range(heads):
         h = base + g
         for c in range(1, chunks):
-            unit_ref[g, rows_of(c)] = unit_in_ref[h, rows_of(c)]
-        unit_ref[g, AGAIN:CHUNK] = unit_in_ref[h, AGAIN:CHUNK]
+            unit_refs[g // size][g % size, rows_of(c)] = unit_in_ref[h, rows_of(c)]
+        unit_refs[g // size][g % size, AGAIN:CHUNK] = unit_in_ref[h, AGAIN:CHUNK]
         value_s[g, AGAIN:CHUNK] = value_in_ref[h, AGAIN:CHUNK]
         for i in range(2):
             padded[g, i, 0:RIM] = rims[(1 + i) * RIM : (2 + i) * RIM, h, :]
             padded[g, i, RIM : RIM + AGAIN] = first_ref[i, h]
             rows = filtered(padded.at[g, i], taps_of(taps_ref, 1 + i, h), 0, AGAIN)
             if i == 0:
-                unit_ref[g, 0:AGAIN] = unit(rows).astype(BF16)
+                unit_refs[g // size][g % size, 0:AGAIN] = unit(rows).astype(BF16)
             else:
                 value_s[g, 0:AGAIN] = rows.astype(BF16)
 
@@ -213,7 +216,7 @@
             h = base + g
             cum_col = columns[:, h : h + 1]
             cum_row = cum[h : h + 1]
-            key = unit_in_ref[h, rows_of(c)] if c else unit_ref[g, rows_of(c)]
+            key = unit_in_ref[h, rows_of(c)] if c else unit_refs[g // size][g % size, rows_of(c)]
             fading = jnp.exp(jnp.where(strictly, cum_col - cum_row, FAR))
             strength_col = columns[:, total_heads + h : total_heads + h + 1]
             lowers.append(strength_col * fading * mul(key, key, NT))
@@ -226,7 +229,7 @@
         keep_second = (1 - second).astype(F32)
         keep_both = keep_first * keep_second
         h = base + g
-        key = unit_in_ref[h, rows_of(c)] if c else unit_ref[g, rows_of(c)]
+        key = unit_in_ref[h, rows_of(c)] if c else unit_refs[g // size][g % size, rows_of(c)]
         value = value_in_ref[h, rows_of(c)] if c else value_s[g]
         growth = jnp.exp(cum_col) * jnp.where(first_rows, keep_first, keep_both)
         targets = jnp.concatenate(
@@ -237,7 +240,7 @@
             axis=1,
         )
         solved = targets + mul((inverse - eye).astype(BF16), targets.astype(BF16))
-        solved_ref[g, rows_of(c)] = solved
+        solved_refs[g // size][g % size, rows_of(c)] = solved
         end = cum_row[:, CHUNK - 1 : CHUNK]
         tail = jnp.exp(end - cum_col) * jnp.where(first_rows, keep_second, 1.0)
         product = mul(key, (tail * solved).astype(BF16), TN)
@@ -256,7 +259,7 @@
     half = chunks // 2
     for c in range(1, half):
         for g in every:
-            starts_ref[g, c - 1] = states[g]
+            starts_refs[g // size][g % size, c - 1] = states[g]
         states = [compose(step_s[g, c], states[g]) for g in every]
     rest = [step_s[g, half] for g in every]
     for c in range(half + 1, chunks):
@@ -265,7 +268,7 @@
         map_refs[g // size][g % size] = compose(rest[g], states[g]).astype(BF16)
     for c in range(half, chunks):
         for g in every:
-            starts_ref[g, c - 1] = states[g]
+            starts_refs[g // size][g % size, c - 1] = states[g]
         if c + 1 < chunks:
             states = [compose(step_s[g, c], states[g]) for g in every]
 
@@ -396,8 +399,11 @@
     return lax.ppermute(value, axis, [(i, i + steps) for i in range(count - steps)])
 
 
-def exchange(own_map, leaves):
-    received = [lax.ppermute(own_map, "leaf", pairs_at(k, leaves)) for k in range(1, leaves)]
+def exchange(own_map, later, leaves):
+    received = [
+        lax.ppermute(later if k == 1 else own_map, "leaf", pairs_at(k, leaves))
+        for k in range(1, leaves)
+    ]
     return [own_map] + received
 
 
@@ -440,16 +446,17 @@
 def maps_of(base, heads, resets, unit_in, value_in, first, rims, taps, decay, strength):
     _, length, depth = unit_in.shape
     chunks = length // CHUNK
+    size = heads // GROUPS
     return pl.pallas_call(
         functools.partial(maps_kernel, base),
         out_shape=(
-            jax.ShapeDtypeStruct((heads, length, depth), BF16),
-            jax.ShapeDtypeStruct((heads, length, 2 * depth), F32),
-            jax.ShapeDtypeStruct((heads, chunks - 1, depth, 2 * depth), F32),
-            *[jax.ShapeDtypeStruct((heads // GROUPS, depth, 2 * depth), BF16)] * GROUPS,
+            *[jax.ShapeDtypeStruct((size, length, depth), BF16)] * GROUPS,
+            *[jax.ShapeDtypeStruct((size, length, 2 * depth), F32)] * GROUPS,
+            *[jax.ShapeDtypeStruct((size, chunks - 1, depth, 2 * depth), F32)] * GROUPS,
+            *[jax.ShapeDtypeStruct((size, depth, 2 * depth), BF16)] * GROUPS,
         ),
         in_specs=[SMEM] + [VMEM] * 7,
-        out_specs=[VMEM] * (3 + GROUPS),
+        out_specs=[VMEM] * (4 * GROUPS),
         scratch_shapes=[
             pltpu.VMEM(rims.shape, F32),
             pltpu.VMEM((heads, 2, RIM + AGAIN, depth), F32),
@@ -554,31 +561,31 @@
     place = lax.axis_index("leaf").astype(jnp.int32).reshape(1)
 
     links = lax.axis_size("chain") - 1
-    unit_key, solved, starts, *own_maps = maps_of(
-        0, heads, doc_resets, key, value, first, rims, taps, log_decay, write_strength
-    )
+    made = maps_of(0, heads, doc_resets, key, value, first, rims, taps, log_decay, write_strength)
+    own_maps = made[3 * GROUPS :]
+    size = heads // GROUPS
     query_in, gate_in = after(own_maps[-1], query_in, gate_in)
     query, gate = (jnp.transpose(x, (1, 0, 2)) for x in (query_in, gate_in))
-    reads = reads_of(
-        0, heads, doc_resets, query, gate, gain, rims, taps, log_decay, write_strength,
-        (unit_key, solved, starts),
-    )
-    size = heads // GROUPS
+    exchanged = exchange(own_maps[0], own_maps[0], leaves)
     blocks = []
-    exchanged = [exchange(own_maps[0], leaves)]
     for g in range(GROUPS):
-        earlier = blocks[-1] if blocks else reads[0]
-        maps = after(earlier, *exchanged[g])
+        reads = reads_of(
+            g * size, size, doc_resets, query, gate, gain, rims, taps, log_decay, write_strength,
+            made[g : 3 * GROUPS : GROUPS],
+        )
+        maps = after(blocks[-1] if blocks else reads[0], *exchanged)
         before, state, *trans = join(place, maps, links)
         if g + 1 < GROUPS:
-            exchanged.append(exchange(*after(state, own_maps[g + 1]), leaves))
+            own_map = own_maps[g + 1]
+            exchanged = exchange(*after(reads[0], own_map), *after(state, own_map), leaves)
         arrived = from_behind(state.astype(BF16), "chain", 1)
         for _ in range(links - 1):
             passed = jnp.einsum(
                 "hij,hjk->hik", trans[0], arrived.astype(F32), precision=lax.Precision.HIGHEST
             )
             arrived = from_behind((passed + state).astype(BF16), "chain", 1)
-        blocks.append(outputs_of(g * size, arrived, before, reads))
+        blocks.append(outputs_of(0, arrived, before, reads))
+        query, gate = after(blocks[-1], query, gate)
 
     ring = lax.axis_size("head")
     mine = lax.axis_index("head")
@@ -590,6 +597,8 @@
         owner = lax.rem(mine + ring - k, ring)
         last = k + 1 == ring
         following = blocks if last else [lax.ppermute(x, "head", around) for x in blocks]
+        if k == 0:
+            blocks[:-1] = after(following[-1], *blocks[:-1])
         for g, block in enumerate(blocks):
             section = owner * GROUPS + g
             if last and g + 1 == GROUPS:

time: 71.4 us -> 74.2 us (1.039)
  starting transfers between devices: 18.6 us -> 21.6 us
  waiting for transfers between devices: 28.5 us -> 26.2 us
  Pallas kernels: 17.9 us -> 19.6 us
  local copies, waits for them, and re-layouts: 1.37 us -> 2.89 us
  matrix products: 4.35 us -> 3.17 us
    unnamed x18 -> x32, local copies, waits for them, and re-layouts: 0.05 us -> 2.61 us
    ppermute x6, waiting for transfers between devices: 27.3 us -> 25.4 us  [on_device(): lax.ppermute(x, 'head', around)]
    pallas_call x1 -> x2, Pallas kernels: 5.42 us -> 7.08 us  [reads_of(): pl.pallas_call(functools.partial(reads_kernel, base), out_shape=(jax.Shap...]
    ppermute x6, starting transfers between devices: 3.46 us -> 4.93 us  [on_device(): lax.ppermute(x, 'head', around)]
    ppermute x6, starting transfers between devices: 7.11 us -> 8.34 us  [exchange(): lax.ppermute(later if k == 1 else own_map, 'leaf', pairs_at(k, leaves))]
    dot_general x7, matrix products: 4.35 us -> 3.17 us  [on_device(): term = jnp.dot(block, rows, preferred_element_type=F32)]
    transpose x1, local copies, waits for them, and re-layouts: 1.18 us -> 0.14 us  [on_device(): key, value = (jnp.transpose(x, (1, 0, 2)) for x in (key_in, value_in))]
  transfers between devices with their start and end apart: 15 -> 15, of which waited for: 8 -> 6; matrix products, arithmetic and copies ran while one was open for 8% -> 5% of each run, Pallas kernels for 13% -> 16%
where the time goes in v20:
time: 74.2 us; the launch traced here: 74 us
  waiting for transfers between devices  26.2 us (35%)
  starting transfers between devices  21.6 us (29%)
  Pallas kernels  19.6 us (26%)
  matrix products  3.17 us (4%)
  local copies, waits for them, and re-layouts  2.89 us (4%)
    ppermute x6, waiting for transfers between devices, on_device(): lax.ppermute(x, 'head', around)  25.4 us
    ppermute x6, starting transfers between devices, exchange(): lax.ppermute(later if k == 1 else own_map, 'leaf', pairs_at(k, leaves))  8.34 us
    ppermute x3, starting transfers between devices, from_behind(): lax.ppermute(value, axis, [(i, i + steps) for i in range(count - steps)])  8.3 us
    pallas_call x2, Pallas kernels, reads_of(): pl.pallas_call(functools.partial(reads_kernel, base), out_shape=(jax.Shap...  7.08 us
    pallas_call x1, Pallas kernels, maps_of(): pl.pallas_call(functools.partial(maps_kernel, base), out_shape=(*[jax.Sha...  5.05 us
    ppermute x6, starting transfers between devices, on_device(): lax.ppermute(x, 'head', around)  4.93 us
    dot_general x7, matrix products, on_device(): term = jnp.dot(block, rows, preferred_element_type=F32)  3.17 us
    unnamed x32, local copies, waits for them, and re-layouts  2.61 us
  transfers between devices with their start and end apart: 15, of which 6 were waited for; matrix products, arithmetic and copies ran while one was open for 5% of the time, Pallas kernels for 16%

profile of v20, /device:TPU:0, one launch (start us, length us, event | category | flops | bytes accessed | tf_op | source)
XLA Modules:
  0.0 74.0 jit_solution(2855280536274592502)
XLA Ops:
  0.0 1.4 %shard_map.101 = bf16[24,4,128]{2,1,0:T(4,128)(2,1)} custom-call(bf16[512,4,128]{2,1,0:T(4,128)(2,1)} %refs_0_.1, bf16[512,4,128]{2,1,0:T(4,128)(2,1)} %refs_1_.1, bf16[512,4,128]{2,1,0:T(4,128)(2,1)} %refs_2_.1), custom_call_target="tpu_custom_call" | custom-call | flops 1000000000 | bytes 65536 | tf_op jit(solution)/shard_map/pallas_call | solution.py:419
  1.5 4.8 %collective-permute-start = (bf16[24,4,128]{2,1,0:T(4,128)(2,1)}, bf16[24,4,128]{2,1,0:T(4,128)(2,1)S(1)}, u32[]{:S(2)}, u32[]{:S(2)}) collective-permute-start(bf16[24,4,128]{2,1,0:T(4,128)(2,1)} %shard_map.101), channel_id=1, source_target_pairs={{0,4},{4,8},{8,12},{12,16},{16,20},{20,24},{24,28},{1,5},{5,9},{9,... | collective-permute-start | bytes 73736 | tf_op jit(solution)/shard_map/ppermute | solution.py:399
  6.5 1.8 %shard_map.100 = (bf16[4,512,128]{2,1,0:T(8,128)(2,1)S(1)}, bf16[4,512,128]{2,1,0:T(8,128)(2,1)S(1)}, f32[2,4,16,128]{3,2,1,0:T(8,128)S(1)}) custom-call(bf16[4,512,128]{2,1,0:T(8,128)(2,1)S(1)} %get-tuple-element.78.key_ref, bf16[4,512,128]{2,1,0:T(8,128)(2,1)S(1)} %get-tuple-element.77.value_ref, f32[3,4,4,128]{3,2,1,0:T(4,128)S(1)} %copy-done.1), custom_call_target="tpu_custom_call" | custom-call | flops 3000000000 | bytes 4194304 | tf_op jit(solution)/shard_map/pallas_call | solution.py:433
  8.4 5.0 %shard_map.102 = (bf16[2,512,128]{2,1,0:T(8,128)(2,1)S(1)}, bf16[2,512,128]{2,1,0:T(8,128)(2,1)S(1)}, f32[2,512,256]{2,1,0:T(8,128)S(1)}, f32[2,512,256]{2,1,0:T...) custom-call(s32[8]{0:T(128)S(1)} %copy-done.4, ...), custom_call_target="tpu_custom_call" | custom-call | flops 5000000000 | bytes 4194304 | tf_op jit(solution)/shard_map/pallas_call | solution.py:450
  13.5 1.0 %copy-done.6 = f32[2,512,256]{2,1,0:T(8,128)} copy-done((f32[2,512,256]{2,1,0:T(8,128)}, f32[2,512,256]{2,1,0:T(8,128)S(1)}, u32[]{:S(2)}) %copy-start.6) | copy-done | bytes 1048600
  14.4 0.9 %copy-done.8 = f32[2,3,128,256]{3,2,1,0:T(8,128)} copy-done((f32[2,3,128,256]{3,2,1,0:T(8,128)}, f32[2,3,128,256]{3,2,1,0:T(8,128)S(1)}, u32[]{:S(2)}) %copy-start.8) | copy-done | bytes 786456
  16.0 2.0 %collective-permute-start.1 = (bf16[2,128,256]{2,1,0:T(8,128)(2,1)S(1)}, bf16[2,128,256]{2,1,0:T(8,128)(2,1)S(1)}, u32[]{:S(2)}, u32[]{:S(2)}) collective-permute-start(bf16[2,128,256]{2,1,0:T(8,128)(2,1)S(1)} %get-tuple-element.52.refs_0_), channel_id=1, source_target_pairs={{0,4},{4,0},{8,12},{12,8},{1,5},{5,1},{9,13},{13,9},{2,6},{6,2},{1... | collective-permute-start | bytes 393224 | tf_op jit(solution)/shard_map/ppermute | solution.py:404
  18.0 1.5 %collective-permute-start.2 = (bf16[2,128,256]{2,1,0:T(8,128)(2,1)S(1)}, bf16[2,128,256]{2,1,0:T(8,128)(2,1)S(1)}, u32[]{:S(2)}, u32[]{:S(2)}) collective-permute-start(bf16[2,128,256]{2,1,0:T(8,128)(2,1)S(1)} %get-tuple-element.52.refs_0_), channel_id=1, source_target_pairs={{0,8},{4,12},{8,0},{12,4},{1,9},{5,13},{9,1},{13,5},{2,10},{6,14},... | collective-permute-start | bytes 393224 | tf_op jit(solution)/shard_map/ppermute | solution.py:404
  19.5 0.9 %collective-permute-start.3 = (bf16[2,128,256]{2,1,0:T(8,128)(2,1)S(1)}, bf16[2,128,256]{2,1,0:T(8,128)(2,1)S(1)}, u32[]{:S(2)}, u32[]{:S(2)}) collective-permute-start(bf16[2,128,256]{2,1,0:T(8,128)(2,1)S(1)} %get-tuple-element.52.refs_0_), channel_id=1, source_target_pairs={{0,12},{4,8},{8,4},{12,0},{1,13},{5,9},{9,5},{13,1},{2,14},{6,10},... | collective-permute-start | bytes 393224 | tf_op jit(solution)/shard_map/ppermute | solution.py:404
  20.6 3.5 %shard_map.103 = (bf16[2,512,128]{2,1,0:T(8,128)(2,1)S(1)}, f32[2,512,128]{2,1,0:T(8,128)S(1)}, f32[2,512,128]{2,1,0:T(8,128)S(1)}) custom-call(s32[8]{0:T(128)S(1)} %copy-done.4, bf16[4,512,128]{2,1,0:T(8,128)(2,1)S(1)} %bitcast.20, bf16[4,512,128]{2,1,0:T(8,128)(2,1)S(1)} %bitcast.22, f32[1,128]{1,0:T(1,128)S(1)} %bitcast.24, ...), custom_call_target="tpu_custom_call" | custom-call | flops 3000000000 | bytes 4194304 | tf_op jit(solution)/shard_map/pallas_call | solution.py:476
  24.1 2.1 %collective-permute-start.6 = (bf16[2,128,256]{2,1,0:T(8,128)(2,1)S(1)}, bf16[2,128,256]{2,1,0:T(8,128)(2,1)S(1)}, u32[]{:S(2)}, u32[]{:S(2)}) collective-permute-start(bf16[2,128,256]{2,1,0:T(8,128)(2,1)S(1)} %get-tuple-element.62.refs_0_), channel_id=1, source_target_pairs={{0,8},{4,12},{8,0},{12,4},{1,9},{5,13},{9,1},{13,5},{2,10},{6,14},... | collective-permute-start | bytes 393224 | tf_op jit(solution)/shard_map/ppermute | solution.py:404
  27.5 1.3 %collective-permute-start.5 = (bf16[2,128,256]{2,1,0:T(8,128)(2,1)S(1)}, bf16[2,128,256]{2,1,0:T(8,128)(2,1)S(1)}, u32[]{:S(2)}, u32[]{:S(2)}) collective-permute-start(bf16[2,128,256]{2,1,0:T(8,128)(2,1)S(1)} %get-tuple-element.62.refs_0_), channel_id=1, source_target_pairs={{0,4},{4,0},{8,12},{12,8},{1,5},{5,1},{9,13},{13,9},{2,6},{6,2},{1... | collective-permute-start | bytes 393224 | tf_op jit(solution)/shard_map/ppermute | solution.py:404
  28.8 1.3 %collective-permute-start.4 = (bf16[2,128,128]{2,1,0:T(8,128)(2,1)S(1)}, bf16[2,128,128]{2,1,0:T(8,128)(2,1)S(1)}, u32[]{:S(2)}, u32[]{:S(2)}) collective-permute-start(bf16[2,128,128]{2,1,0:T(8,128)(2,1)S(1)} %get-tuple-element.56), channel_id=1, source_target_pairs={{0,16},{1,17},{2,18},{3,19},{4,20},{5,21},{6,22},{7,23},{8,24},{9,... | collective-permute-start | bytes 196616 | tf_op jit(solution)/shard_map/ppermute | solution.py:399
  31.7 1.6 %collective-permute-start.10 = (bf16[512,256]{1,0:T(8,128)(2,1)S(1)}, bf16[512,256]{1,0:T(8,128)(2,1)S(1)}, u32[]{:S(2)}, u32[]{:S(2)}) collective-permute-start(bf16[512,256]{1,0:T(8,128)(2,1)S(1)} %shard_map.105), channel_id=1, source_target_pairs={{0,1},{1,2},{2,3},{3,0},{4,5},{5,6},{6,7},{7,4},{8,9},{9,10},{10,1... | collective-permute-start | bytes 786440 | tf_op jit(solution)/shard_map/ppermute | solution.py:599
  34.1 2.2 %collective-permute-start.8 = (bf16[2,128,128]{2,1,0:T(8,128)(2,1)S(1)}, bf16[2,128,128]{2,1,0:T(8,128)(2,1)S(1)}, u32[]{:S(2)}, u32[]{:S(2)}) collective-permute-start(bf16[2,128,128]{2,1,0:T(8,128)(2,1)S(1)} %get-tuple-element.66), channel_id=1, source_target_pairs={{0,16},{1,17},{2,18},{3,19},{4,20},{5,21},{6,22},{7,23},{8,24},{9,... | collective-permute-start | bytes 196616 | tf_op jit(solution)/shard_map/ppermute | solution.py:399
  36.3 3.5 %shard_map.107 = (bf16[2,512,128]{2,1,0:T(8,128)(2,1)S(1)}, f32[2,512,128]{2,1,0:T(8,128)S(1)}, f32[2,512,128]{2,1,0:T(8,128)S(1)}) custom-call(s32[8]{0:T(128)S(1)} %copy-done.4, bf16[4,512,128]{2,1,0:T(8,128)(2,1)S(1)} %bitcast.21, bf16[4,512,128]{2,1,0:T(8,128)(2,1)S(1)} %bitcast.23, f32[1,128]{1,0:T(1,128)S(1)} %bitcast.25, ...), custom_call_target="tpu_custom_call" | custom-call | flops 3000000000 | bytes 4194304 | tf_op jit(solution)/shard_map/pallas_call | solution.py:476
  40.6 1.6 %collective-permute-start.9 = (bf16[512,256]{1,0:T(8,128)(2,1)S(1)}, bf16[512,256]{1,0:T(8,128)(2,1)S(1)}, u32[]{:S(2)}, u32[]{:S(2)}) collective-permute-start(bf16[512,256]{1,0:T(8,128)(2,1)S(1)} %shard_map.108), channel_id=1, source_target_pairs={{0,1},{1,2},{2,3},{3,0},{4,5},{5,6},{6,7},{7,4},{8,9},{9,10},{10,1... | collective-permute-start | bytes 786440 | tf_op jit(solution)/shard_map/ppermute | solution.py:599
  42.7 1.6 %collective-permute-start.11 = (bf16[512,256]{1,0:T(8,128)(2,1)S(1)}, bf16[512,256]{1,0:T(8,128)(2,1)S(1)}, u32[]{:S(2)}, u32[]{:S(2)}) collective-permute-start(bf16[512,256]{1,0:T(8,128)(2,1)S(1)} %collective-permute-done.10), channel_id=1, source_target_pairs={{0,1},{1,2},{2,3},{3,0},{4,5},{5,6},{6,7},{7,4},{8,9},{9,10},{10,1... | collective-permute-start | bytes 786440 | tf_op jit(solution)/shard_map/ppermute | solution.py:599
  44.8 6.9 %collective-permute-done.9 = bf16[512,256]{1,0:T(8,128)(2,1)S(1)} collective-permute-done((bf16[512,256]{1,0:T(8,128)(2,1)S(1)}, bf16[512,256]{1,0:T(8,128)(2,1)S(1)}, u32[]{:S(2)}, u32[]{:S(2)}) %collective-permute-start.9) | collective-permute-done | bytes 262176 | tf_op jit(solution)/shard_map/ppermute | solution.py:599
  52.7 4.6 %collective-permute-done.11 = bf16[512,256]{1,0:T(8,128)(2,1)S(1)} collective-permute-done((bf16[512,256]{1,0:T(8,128)(2,1)S(1)}, bf16[512,256]{1,0:T(8,128)(2,1)S(1)}, u32[]{:S(2)}, u32[]{:S(2)}) %collective-permute-start.11) | collective-permute-done | bytes 262176 | tf_op jit(solution)/shard_map/ppermute | solution.py:599
  57.8 5.5 %collective-permute-done.13 = bf16[512,256]{1,0:T(8,128)(2,1)S(1)} collective-permute-done((bf16[512,256]{1,0:T(8,128)(2,1)S(1)}, bf16[512,256]{1,0:T(8,128)(2,1)S(1)}, u32[]{:S(2)}, u32[]{:S(2)}) %collective-permute-start.13) | collective-permute-done | bytes 262176 | tf_op jit(solution)/shard_map/ppermute | solution.py:599
  63.8 5.1 %collective-permute-done.12 = bf16[512,256]{1,0:T(8,128)(2,1)S(1)} collective-permute-done((bf16[512,256]{1,0:T(8,128)(2,1)S(1)}, bf16[512,256]{1,0:T(8,128)(2,1)S(1)}, u32[]{:S(2)}, u32[]{:S(2)}) %collective-permute-start.12) | collective-permute-done | bytes 262176 | tf_op jit(solution)/shard_map/ppermute | solution.py:599
  69.4 3.2 %collective-permute-done.14.block_ref = bf16[512,256]{1,0:T(8,128)(2,1)S(1)} collective-permute-done((bf16[512,256]{1,0:T(8,128)(2,1)S(1)}, bf16[512,256]{1,0:T(8,128)(2,1)S(1)}, u32[]{:S(2)}, u32[]{:S(2)}) %collective-permute-start.14) | collective-permute-done | bytes 262176 | tf_op jit(solution)/shard_map/ppermute | solution.py:599
  72.6 1.3 %shard_map.109 = bf16[512,1024]{1,0:T(8,128)(2,1)} custom-call(s32[1]{0:T(128)} %bitcast.section, f32[512,1024]{1,0:T(8,128)S(1)} %add_add_fusion.1.first_ref, f32[512,1024]{1,0:T(8,128)S(1)} %add_add_fusion.second_ref, bf16[512,256]{1,0:T(8,128)(2,1)S(1)} %collective-permute-done.14.block_ref, bf16[2048,1024]{1,0:T(8,128)(2,1)S(1)} %copy-done), custom_call_target="tpu_custom_call" | custom-call | tf_op jit(solution)/shard_map/pallas_call | solution.py:525
  (58 shorter events, 8.6 us)
Async XLA Ops:
  0.0 6.3 %copy-start.14 = (bf16[512,4,128]{2,1,0:T(4,128)(2,1)S(1)}, bf16[512,4,128]{2,1,0:T(4,128)(2,1)}, u32[]{:S(2)}) copy-start(bf16[512,4,128]{2,1,0:T(4,128)(2,1)} %refs_2_.1) | copy-start | bytes 1572868
  0.0 6.3 %copy-start.15 = (bf16[512,4,128]{2,1,0:T(4,128)(2,1)S(1)}, bf16[512,4,128]{2,1,0:T(4,128)(2,1)}, u32[]{:S(2)}) copy-start(bf16[512,4,128]{2,1,0:T(4,128)(2,1)} %refs_1_.1) | copy-start | bytes 1572868
  0.0 6.5 %copy-start.1 = (f32[3,4,4,128]{3,2,1,0:T(4,128)S(1)}, f32[3,4,4,128]{3,2,1,0:T(4,128)}, u32[]{:S(2)}) copy-start(f32[3,4,4,128]{3,2,1,0:T(4,128)} %taps_ref.7) | copy-start | bytes 73732
  1.5 6.9 %collective-permute-start = (bf16[24,4,128]{2,1,0:T(4,128)(2,1)}, bf16[24,4,128]{2,1,0:T(4,128)(2,1)S(1)}, u32[]{:S(2)}, u32[]{:S(2)}) collective-permute-start(bf16[24,4,128]{2,1,0:T(4,128)(2,1)} %shard_map.101), channel_id=1, source_target_pairs={{0,4},{4,8},{8,12},{12,16},{16,20},{20,24},{24,28},{1,5},{5,9},{9,... | collective-permute-start | bytes 73736 | tf_op jit(solution)/shard_map/ppermute | solution.py:399
  8.4 12.0 %copy-start.12 = (bf16[512,4,128]{2,1,0:T(4,128)(2,1)S(1)}, bf16[512,4,128]{2,1,0:T(4,128)(2,1)}, u32[]{:S(2)}) copy-start(bf16[512,4,128]{2,1,0:T(4,128)(2,1)} %refs_0_.1) | copy-start | bytes 1572868
  8.4 12.1 %copy-start.13 = (bf16[512,4,128]{2,1,0:T(4,128)(2,1)S(1)}, bf16[512,4,128]{2,1,0:T(4,128)(2,1)}, u32[]{:S(2)}) copy-start(bf16[512,4,128]{2,1,0:T(4,128)(2,1)} %param.13) | copy-start | bytes 1572868
  16.0 10.7 %collective-permute-start.1 = (bf16[2,128,256]{2,1,0:T(8,128)(2,1)S(1)}, bf16[2,128,256]{2,1,0:T(8,128)(2,1)S(1)}, u32[]{:S(2)}, u32[]{:S(2)}) collective-permute-start(bf16[2,128,256]{2,1,0:T(8,128)(2,1)S(1)} %get-tuple-element.52.refs_0_), channel_id=1, source_target_pairs={{0,4},{4,0},{8,12},{12,8},{1,5},{5,1},{9,13},{13,9},{2,6},{6,2},{1... | collective-permute-start | bytes 393224 | tf_op jit(solution)/shard_map/ppermute | solution.py:404
  18.0 8.8 %collective-permute-start.2 = (bf16[2,128,256]{2,1,0:T(8,128)(2,1)S(1)}, bf16[2,128,256]{2,1,0:T(8,128)(2,1)S(1)}, u32[]{:S(2)}, u32[]{:S(2)}) collective-permute-start(bf16[2,128,256]{2,1,0:T(8,128)(2,1)S(1)} %get-tuple-element.52.refs_0_), channel_id=1, source_target_pairs={{0,8},{4,12},{8,0},{12,4},{1,9},{5,13},{9,1},{13,5},{2,10},{6,14},... | collective-permute-start | bytes 393224 | tf_op jit(solution)/shard_map/ppermute | solution.py:404
  19.5 7.2 %collective-permute-start.3 = (bf16[2,128,256]{2,1,0:T(8,128)(2,1)S(1)}, bf16[2,128,256]{2,1,0:T(8,128)(2,1)S(1)}, u32[]{:S(2)}, u32[]{:S(2)}) collective-permute-start(bf16[2,128,256]{2,1,0:T(8,128)(2,1)S(1)} %get-tuple-element.52.refs_0_), channel_id=1, source_target_pairs={{0,12},{4,8},{8,4},{12,0},{1,13},{5,9},{9,5},{13,1},{2,14},{6,10},... | collective-permute-start | bytes 393224 | tf_op jit(solution)/shard_map/ppermute | solution.py:404
  24.1 9.3 %collective-permute-start.6 = (bf16[2,128,256]{2,1,0:T(8,128)(2,1)S(1)}, bf16[2,128,256]{2,1,0:T(8,128)(2,1)S(1)}, u32[]{:S(2)}, u32[]{:S(2)}) collective-permute-start(bf16[2,128,256]{2,1,0:T(8,128)(2,1)S(1)} %get-tuple-element.62.refs_0_), channel_id=1, source_target_pairs={{0,8},{4,12},{8,0},{12,4},{1,9},{5,13},{9,1},{13,5},{2,10},{6,14},... | collective-permute-start | bytes 393224 | tf_op jit(solution)/shard_map/ppermute | solution.py:404
  26.2 7.2 %collective-permute-start.7 = (bf16[2,128,256]{2,1,0:T(8,128)(2,1)S(1)}, bf16[2,128,256]{2,1,0:T(8,128)(2,1)S(1)}, u32[]{:S(2)}, u32[]{:S(2)}) collective-permute-start(bf16[2,128,256]{2,1,0:T(8,128)(2,1)S(1)} %get-tuple-element.62.refs_0_), channel_id=1, source_target_pairs={{0,12},{4,8},{8,4},{12,0},{1,13},{5,9},{9,5},{13,1},{2,14},{6,10},... | collective-permute-start | bytes 393224 | tf_op jit(solution)/shard_map/ppermute | solution.py:404
  27.5 5.9 %collective-permute-start.5 = (bf16[2,128,256]{2,1,0:T(8,128)(2,1)S(1)}, bf16[2,128,256]{2,1,0:T(8,128)(2,1)S(1)}, u32[]{:S(2)}, u32[]{:S(2)}) collective-permute-start(bf16[2,128,256]{2,1,0:T(8,128)(2,1)S(1)} %get-tuple-element.62.refs_0_), channel_id=1, source_target_pairs={{0,4},{4,0},{8,12},{12,8},{1,5},{5,1},{9,13},{13,9},{2,6},{6,2},{1... | collective-permute-start | bytes 393224 | tf_op jit(solution)/shard_map/ppermute | solution.py:404
  28.8 2.2 %collective-permute-start.4 = (bf16[2,128,128]{2,1,0:T(8,128)(2,1)S(1)}, bf16[2,128,128]{2,1,0:T(8,128)(2,1)S(1)}, u32[]{:S(2)}, u32[]{:S(2)}) collective-permute-start(bf16[2,128,128]{2,1,0:T(8,128)(2,1)S(1)} %get-tuple-element.56), channel_id=1, source_target_pairs={{0,16},{1,17},{2,18},{3,19},{4,20},{5,21},{6,22},{7,23},{8,24},{9,... | collective-permute-start | bytes 196616 | tf_op jit(solution)/shard_map/ppermute | solution.py:399
  30.2 6.1 %copy-start.7 = (f32[2,512,256]{2,1,0:T(8,128)S(1)}, f32[2,512,256]{2,1,0:T(8,128)}, u32[]{:S(2)}) copy-start(f32[2,512,256]{2,1,0:T(8,128)} %copy-done.6) | copy-start | bytes 3145732
  30.2 6.1 %copy-start.9 = (f32[2,3,128,256]{3,2,1,0:T(8,128)S(1)}, f32[2,3,128,256]{3,2,1,0:T(8,128)}, u32[]{:S(2)}) copy-start(f32[2,3,128,256]{3,2,1,0:T(8,128)} %copy-done.8) | copy-start | bytes 2359300
  30.2 6.1 %copy-start.11 = (bf16[2,512,128]{2,1,0:T(8,128)(2,1)S(1)}, bf16[2,512,128]{2,1,0:T(8,128)(2,1)}, u32[]{:S(2)}) copy-start(bf16[2,512,128]{2,1,0:T(8,128)(2,1)} %copy-done.10) | copy-start | bytes 786436
  31.7 11.0 %collective-permute-start.10 = (bf16[512,256]{1,0:T(8,128)(2,1)S(1)}, bf16[512,256]{1,0:T(8,128)(2,1)S(1)}, u32[]{:S(2)}, u32[]{:S(2)}) collective-permute-start(bf16[512,256]{1,0:T(8,128)(2,1)S(1)} %shard_map.105), channel_id=1, source_target_pairs={{0,1},{1,2},{2,3},{3,0},{4,5},{5,6},{6,7},{7,4},{8,9},{9,10},{10,1... | collective-permute-start | bytes 786440 | tf_op jit(solution)/shard_map/ppermute | solution.py:599
  34.1 5.8 %collective-permute-start.8 = (bf16[2,128,128]{2,1,0:T(8,128)(2,1)S(1)}, bf16[2,128,128]{2,1,0:T(8,128)(2,1)S(1)}, u32[]{:S(2)}, u32[]{:S(2)}) collective-permute-start(bf16[2,128,128]{2,1,0:T(8,128)(2,1)S(1)} %get-tuple-element.66), channel_id=1, source_target_pairs={{0,16},{1,17},{2,18},{3,19},{4,20},{5,21},{6,22},{7,23},{8,24},{9,... | collective-permute-start | bytes 196616 | tf_op jit(solution)/shard_map/ppermute | solution.py:399
  36.3 5.9 %copy-start = (bf16[2048,1024]{1,0:T(8,128)(2,1)S(1)}, bf16[2048,1024]{1,0:T(8,128)(2,1)}, u32[]{:S(2)}) copy-start(bf16[2048,1024]{1,0:T(8,128)(2,1)} %weights_ref.1) | copy-start | bytes 12582916
  40.6 11.1 %collective-permute-start.9 = (bf16[512,256]{1,0:T(8,128)(2,1)S(1)}, bf16[512,256]{1,0:T(8,128)(2,1)S(1)}, u32[]{:S(2)}, u32[]{:S(2)}) collective-permute-start(bf16[512,256]{1,0:T(8,128)(2,1)S(1)} %shard_map.108), channel_id=1, source_target_pairs={{0,1},{1,2},{2,3},{3,0},{4,5},{5,6},{6,7},{7,4},{8,9},{9,10},{10,1... | collective-permute-start | bytes 786440 | tf_op jit(solution)/shard_map/ppermute | solution.py:599
  42.7 14.6 %collective-permute-start.11 = (bf16[512,256]{1,0:T(8,128)(2,1)S(1)}, bf16[512,256]{1,0:T(8,128)(2,1)S(1)}, u32[]{:S(2)}, u32[]{:S(2)}) collective-permute-start(bf16[512,256]{1,0:T(8,128)(2,1)S(1)} %collective-permute-done.10), channel_id=1, source_target_pairs={{0,1},{1,2},{2,3},{3,0},{4,5},{5,6},{6,7},{7,4},{8,9},{9,10},{10,1... | collective-permute-start | bytes 786440 | tf_op jit(solution)/shard_map/ppermute | solution.py:599
  52.2 11.1 %collective-permute-start.13 = (bf16[512,256]{1,0:T(8,128)(2,1)S(1)}, bf16[512,256]{1,0:T(8,128)(2,1)S(1)}, u32[]{:S(2)}, u32[]{:S(2)}) collective-permute-start(bf16[512,256]{1,0:T(8,128)(2,1)S(1)} %collective-permute-done.9), channel_id=1, source_target_pairs={{0,1},{1,2},{2,3},{3,0},{4,5},{5,6},{6,7},{7,4},{8,9},{9,10},{10,1... | collective-permute-start | bytes 786440 | tf_op jit(solution)/shard_map/ppermute | solution.py:599
  57.4 11.5 %collective-permute-start.12 = (bf16[512,256]{1,0:T(8,128)(2,1)S(1)}, bf16[512,256]{1,0:T(8,128)(2,1)S(1)}, u32[]{:S(2)}, u32[]{:S(2)}) collective-permute-start(bf16[512,256]{1,0:T(8,128)(2,1)S(1)} %collective-permute-done.11), channel_id=1, source_target_pairs={{0,1},{1,2},{2,3},{3,0},{4,5},{5,6},{6,7},{7,4},{8,9},{9,10},{10,1... | collective-permute-start | bytes 786440 | tf_op jit(solution)/shard_map/ppermute | solution.py:599
  63.3 9.3 %collective-permute-start.14 = (bf16[512,256]{1,0:T(8,128)(2,1)S(1)}, bf16[512,256]{1,0:T(8,128)(2,1)S(1)}, u32[]{:S(2)}, u32[]{:S(2)}) collective-permute-start(bf16[512,256]{1,0:T(8,128)(2,1)S(1)} %collective-permute-done.13), channel_id=1, source_target_pairs={{0,1},{1,2},{2,3},{3,0},{4,5},{5,6},{6,7},{7,4},{8,9},{9,10},{10,1... | collective-permute-start | bytes 786440 | tf_op jit(solution)/shard_map/ppermute | solution.py:599
  (7 other events, 12.6 us)

commit v21 on v16

--- a/solution.py
+++ b/solution.py
@@ -15,6 +15,7 @@
 FAR = -1e30
 LARGE = 1e38
 AGAIN = 16
+TILE = 256
 F32 = jnp.float32
 BF16 = jnp.bfloat16
 NN = (((1,), (0,)), ((), ()))
@@ -367,25 +368,29 @@
         before = before_ref[g]
         incoming = mul_split(before[:, :depth], arrived_ref[g].astype(F32)) + before[:, depth:]
         high, low = split(incoming)
+        reach = reach_ref[h]
+        reached = mul(reach, high) + mul(reach, low)
         for c in range(normed_ref.shape[0] // CHUNK):
             here = rows_of(c)
-            reach = reach_ref[h, here]
-            core = part_ref[h, here] + (mul(reach, high) + mul(reach, low))
+            core = part_ref[h, here] + reached[here]
             scale = lax.rsqrt(jnp.sum(core * core, axis=-1, keepdims=True) / depth + EPSILON)
             normed_ref[here, g * depth : (g + 1) * depth] = (
                 core * scale * gating_ref[h, here]
             ).astype(BF16)
 
 
-def last_kernel(section, first_ref, second_ref, block_ref, weights_ref, out_ref, tiles, written):
+def last_kernel(section, total_ref, block_ref, weights_ref, out_ref, tiles, written):
     width = block_ref.shape[1]
-    rows = weights_ref[pl.ds(pl.multiple_of(section[0] * width, width), width), :]
+    rows = pl.ds(pl.multiple_of(section[0] * width, width), width)
     copies = []
-    for i in range(first_ref.shape[0] // CHUNK):
-        here = rows_of(i)
-        total = (first_ref[here] + second_ref[here]) + mul(block_ref[here], rows)
-        tiles[here] = total.astype(BF16)
-        copies.append(pltpu.make_async_copy(tiles.at[here], out_ref.at[here], written.at[i]))
+    for i in range(total_ref.shape[1] // TILE):
+        here = slice(i * TILE, (i + 1) * TILE)
+        term = mul(block_ref[...], weights_ref[rows, here])
+        tiles[:, here] = (total_ref[:, here] + term).astype(BF16)
+        columns = pl.ds(i * TILE, TILE)
+        copies.append(
+            pltpu.make_async_copy(tiles.at[:, columns], out_ref.at[:, columns], written.at[i])
+        )
         copies[-1].start()
     for copy in copies:
         copy.wait()
@@ -513,19 +518,19 @@
     )(arrived, before, *reads)
 
 
-def last_projected(section, first, second, block, weights):
-    length, columns = first.shape
+def last_projected(section, total, block, weights):
+    length, columns = total.shape
     return pl.pallas_call(
         last_kernel,
         out_shape=jax.ShapeDtypeStruct((length, columns), BF16),
-        in_specs=[SMEM] + [VMEM] * 4,
+        in_specs=[SMEM] + [VMEM] * 3,
         out_specs=pl.BlockSpec(memory_space=pl.ANY),
         scratch_shapes=[
             pltpu.VMEM((length, columns), BF16),
-            pltpu.SemaphoreType.DMA((length // CHUNK,)),
+            pltpu.SemaphoreType.DMA((columns // TILE,)),
         ],
         compiler_params=LAST_PARAMS,
-    )(section.astype(jnp.int32).reshape(1), first, second, block, weights)
+    )(section.astype(jnp.int32).reshape(1), total, block, weights)
 
 
 def after(first, *values):
@@ -593,7 +598,7 @@
         for g, block in enumerate(blocks):
             section = owner * GROUPS + g
             if last and g + 1 == GROUPS:
-                return last_projected(section, *sums, block, weights)
+                return last_projected(section, sum(sums[1:], sums[0]), block, weights)
             rows = lax.dynamic_slice_in_dim(weights, section * width, width, 0)
             term = jnp.dot(block, rows, preferred_element_type=F32)
             sums[g] = term if sums[g] is None else sums[g] + term

time: 71.4 us -> 71.2 us (level)
  transfers between devices with their start and end apart: 15 -> 15, of which waited for: 8 -> 9; matrix products, arithmetic and copies ran while one was open for 8% -> 8% of each run, Pallas kernels for 13% -> 13%
where the time goes in v21:
time: 71.2 us; the launch traced here: 71 us
  waiting for transfers between devices  28.5 us (40%)
  starting transfers between devices  18.3 us (26%)
  Pallas kernels  17.7 us (25%)
  matrix products  4.59 us (6%)
  local copies, waits for them, and re-layouts  1.37 us (2%)
    ppermute x6, waiting for transfers between devices, on_device(): lax.ppermute(x, 'head', around)  27.2 us
    ppermute x3, starting transfers between devices, from_behind(): lax.ppermute(value, axis, [(i, i + steps) for i in range(count - steps)])  7.86 us
    ppermute x6, starting transfers between devices, exchange(): lax.ppermute(own_map, 'leaf', pairs_at(k, leaves))  7.11 us
    pallas_call x1, Pallas kernels, reads_of(): pl.pallas_call(functools.partial(reads_kernel, base), out_shape=(jax.Shap...  5.42 us
    pallas_call x1, Pallas kernels, maps_of(): pl.pallas_call(functools.partial(maps_kernel, base), out_shape=(jax.Shape...  5.05 us
    dot_general x7, matrix products, on_device(): term = jnp.dot(block, rows, preferred_element_type=F32)  4.59 us
    ppermute x6, starting transfers between devices, on_device(): lax.ppermute(x, 'head', around)  3.34 us
    pallas_call x1, Pallas kernels, filters_of(): pl.pallas_call(filters_kernel, out_shape=(per_token, per_token, jax.Shape...  1.78 us
  transfers between devices with their start and end apart: 15, of which 9 were waited for; matrix products, arithmetic and copies ran while one was open for 8% of the time, Pallas kernels for 13%

profile of v21, /device:TPU:0, one launch (start us, length us, event | category | flops | bytes accessed | tf_op | source)
XLA Modules:
  0.0 71.0 jit_solution(7374531829464961204)
XLA Ops:
  0.0 1.4 %shard_map.101 = bf16[24,4,128]{2,1,0:T(4,128)(2,1)} custom-call(bf16[512,4,128]{2,1,0:T(4,128)(2,1)} %refs_0_.1, bf16[512,4,128]{2,1,0:T(4,128)(2,1)} %refs_1_.1, bf16[512,4,128]{2,1,0:T(4,128)(2,1)} %refs_2_.1), custom_call_target="tpu_custom_call" | custom-call | flops 1000000000 | bytes 65536 | tf_op jit(solution)/shard_map/pallas_call | solution.py:418
  1.4 4.8 %collective-permute-start = (bf16[24,4,128]{2,1,0:T(4,128)(2,1)}, bf16[24,4,128]{2,1,0:T(4,128)(2,1)S(1)}, u32[]{:S(2)}, u32[]{:S(2)}) collective-permute-start(bf16[24,4,128]{2,1,0:T(4,128)(2,1)} %shard_map.101), channel_id=1, source_target_pairs={{0,4},{4,8},{8,12},{12,16},{16,20},{20,24},{24,28},{1,5},{5,9},{9,... | collective-permute-start | bytes 73736 | tf_op jit(solution)/shard_map/ppermute | solution.py:401
  6.3 1.2 %copy_bitcast_fusion.2 = (bf16[4,512,128]{2,1,0:T(8,128)(2,1)S(1)}, bf16[4,512,128]{2,1,0:T(8,128)(2,1)S(1)}) fusion(bf16[512,4,128]{2,1,0:T(4,128)(2,1)S(1)} %copy-done.8, bf16[512,4,128]{2,1,0:T(4,128)(2,1)} %refs_1_.1), kind=kLoop, calls=%fused_computation.3 | loop fusion | bytes 2097152 | tf_op jit(solution)/shard_map/transpose | solution.py:555
  7.5 1.8 %shard_map.100 = (bf16[4,512,128]{2,1,0:T(8,128)(2,1)S(1)}, bf16[4,512,128]{2,1,0:T(8,128)(2,1)S(1)}, f32[2,4,16,128]{3,2,1,0:T(8,128)S(1)}) custom-call(bf16[4,512,128]{2,1,0:T(8,128)(2,1)S(1)} %get-tuple-element.58.key_ref, bf16[4,512,128]{2,1,0:T(8,128)(2,1)S(1)} %get-tuple-element.57.value_ref, f32[3,4,4,128]{3,2,1,0:T(4,128)S(1)} %copy-done.1), custom_call_target="tpu_custom_call" | custom-call | flops 3000000000 | bytes 4194304 | tf_op jit(solution)/shard_map/pallas_call | solution.py:432
  9.4 5.1 %shard_map.102 = (bf16[4,512,128]{2,1,0:T(8,128)(2,1)S(1)}, f32[4,512,256]{2,1,0:T(8,128)S(1)}, f32[4,3,128,256]{3,2,1,0:T(8,128)S(1)}, bf16[2,128,256]{2,1,0:T(8,128)(2,1)S(1)}, bf16[2,128,256]{2,1,0:T(8,128)(2,1)S(1)}) custom-call(s32[8]{0:T(128)S(1)} %copy-done.4, bf16[4,512,128]{2,1,0:T(8,128)(2,1)S(1)} %get-tuple-element.31.unit_in_ref, ...), custom_call_target="tpu_custom_call" | custom-call | flops 5000000000 | bytes 4194304 | tf_op jit(solution)/shard_map/pallas_call | solution.py:448
  14.5 2.0 %collective-permute-start.3 = (bf16[2,128,256]{2,1,0:T(8,128)(2,1)S(1)}, bf16[2,128,256]{2,1,0:T(8,128)(2,1)S(1)}, u32[]{:S(2)}, u32[]{:S(2)}) collective-permute-start(bf16[2,128,256]{2,1,0:T(8,128)(2,1)S(1)} %get-tuple-element.42.refs_0_), channel_id=1, source_target_pairs={{0,12},{4,8},{8,4},{12,0},{1,13},{5,9},{9,5},{13,1},{2,14},{6,10},... | collective-permute-start | bytes 393224 | tf_op jit(solution)/shard_map/ppermute | solution.py:405
  16.4 1.1 %collective-permute-start.2 = (bf16[2,128,256]{2,1,0:T(8,128)(2,1)S(1)}, bf16[2,128,256]{2,1,0:T(8,128)(2,1)S(1)}, u32[]{:S(2)}, u32[]{:S(2)}) collective-permute-start(bf16[2,128,256]{2,1,0:T(8,128)(2,1)S(1)} %get-tuple-element.42.refs_0_), channel_id=1, source_target_pairs={{0,8},{4,12},{8,0},{12,4},{1,9},{5,13},{9,1},{13,5},{2,10},{6,14},... | collective-permute-start | bytes 393224 | tf_op jit(solution)/shard_map/ppermute | solution.py:405
  18.2 5.4 %shard_map.103 = (bf16[4,512,128]{2,1,0:T(8,128)(2,1)S(1)}, f32[4,512,128]{2,1,0:T(8,128)S(1)}, f32[4,512,128]{2,1,0:T(8,128)S(1)}) custom-call(s32[8]{0:T(128)S(1)} %copy-done.4, bf16[4,512,128]{2,1,0:T(8,128)(2,1)S(1)} %bitcast.20, bf16[4,512,128]{2,1,0:T(8,128)(2,1)S(1)} %bitcast.21, f32[1,128]{1,0:T(1,128)S(1)} %bitcast.22, ...), custom_call_target="tpu_custom_call" | custom-call | flops 3000000000 | bytes 4194304 | tf_op jit(solution)/shard_map/pallas_call | solution.py:474
  24.4 2.0 %collective-permute-start.10 = (bf16[2,128,256]{2,1,0:T(8,128)(2,1)S(1)}, bf16[2,128,256]{2,1,0:T(8,128)(2,1)S(1)}, u32[]{:S(2)}, u32[]{:S(2)}) collective-permute-start(bf16[2,128,256]{2,1,0:T(8,128)(2,1)S(1)} %get-tuple-element.51.refs_0_), channel_id=1, source_target_pairs={{0,12},{4,8},{8,4},{12,0},{1,13},{5,9},{9,5},{13,1},{2,14},{6,10},... | collective-permute-start | bytes 393224 | tf_op jit(solution)/shard_map/ppermute | solution.py:405
  26.4 1.1 %collective-permute-start.9 = (bf16[2,128,256]{2,1,0:T(8,128)(2,1)S(1)}, bf16[2,128,256]{2,1,0:T(8,128)(2,1)S(1)}, u32[]{:S(2)}, u32[]{:S(2)}) collective-permute-start(bf16[2,128,256]{2,1,0:T(8,128)(2,1)S(1)} %get-tuple-element.51.refs_0_), channel_id=1, source_target_pairs={{0,8},{4,12},{8,0},{12,4},{1,9},{5,13},{9,1},{13,5},{2,10},{6,14},... | collective-permute-start | bytes 393224 | tf_op jit(solution)/shard_map/ppermute | solution.py:405
  28.0 1.3 %collective-permute-start.4 = (bf16[2,128,128]{2,1,0:T(8,128)(2,1)S(1)}, bf16[2,128,128]{2,1,0:T(8,128)(2,1)S(1)}, u32[]{:S(2)}, u32[]{:S(2)}) collective-permute-start(bf16[2,128,128]{2,1,0:T(8,128)(2,1)S(1)} %get-tuple-element.46), channel_id=1, source_target_pairs={{0,16},{1,17},{2,18},{3,19},{4,20},{5,21},{6,22},{7,23},{8,24},{9,... | collective-permute-start | bytes 196616 | tf_op jit(solution)/shard_map/ppermute | solution.py:401
  29.3 0.8 %collective-permute-done.4.arrived_ref = bf16[2,128,128]{2,1,0:T(8,128)(2,1)S(1)} collective-permute-done((bf16[2,128,128]{2,1,0:T(8,128)(2,1)S(1)}, bf16[2,128,128]{2,1,0:T(8,128)(2,1)S(1)}, u32[]{:S(2)}, u32[]{:S(2)}) %collective-permute-start.4) | collective-permute-done | bytes 65568 | tf_op jit(solution)/shard_map/ppermute | solution.py:401
  30.7 1.6 %collective-permute-start.5 = (bf16[512,256]{1,0:T(8,128)(2,1)S(1)}, bf16[512,256]{1,0:T(8,128)(2,1)S(1)}, u32[]{:S(2)}, u32[]{:S(2)}) collective-permute-start(bf16[512,256]{1,0:T(8,128)(2,1)S(1)} %shard_map.105), channel_id=1, source_target_pairs={{0,1},{1,2},{2,3},{3,0},{4,5},{5,6},{6,7},{7,4},{8,9},{9,10},{10,1... | collective-permute-start | bytes 786440 | tf_op jit(solution)/shard_map/ppermute | solution.py:597
  33.5 1.7 %collective-permute-start.11 = (bf16[2,128,128]{2,1,0:T(8,128)(2,1)S(1)}, bf16[2,128,128]{2,1,0:T(8,128)(2,1)S(1)}, u32[]{:S(2)}, u32[]{:S(2)}) collective-permute-start(bf16[2,128,128]{2,1,0:T(8,128)(2,1)S(1)} %get-tuple-element.55), channel_id=1, source_target_pairs={{0,16},{1,17},{2,18},{3,19},{4,20},{5,21},{6,22},{7,23},{8,24},{9,... | collective-permute-start | bytes 196616 | tf_op jit(solution)/shard_map/ppermute | solution.py:401
  35.3 1.6 %fusion.11 = f32[512,1024]{1,0:T(8,128)S(1)} fusion(bf16[512,256]{1,0:T(8,128)(2,1)S(1)} %shard_map.105, bf16[2048,1024]{1,0:T(8,128)(2,1)} %weights_ref.1, s32[]{:T(128)S(6)} %select_n.21), kind=kOutput, calls=%fused_computation.16 | convolution fusion | flops 268435456 | bytes 2883588 | tf_op jit(solution)/shard_map/dot_general | solution.py:603
  37.6 1.6 %collective-permute-start.12 = (bf16[512,256]{1,0:T(8,128)(2,1)S(1)}, bf16[512,256]{1,0:T(8,128)(2,1)S(1)}, u32[]{:S(2)}, u32[]{:S(2)}) collective-permute-start(bf16[512,256]{1,0:T(8,128)(2,1)S(1)} %shard_map.107), channel_id=1, source_target_pairs={{0,1},{1,2},{2,3},{3,0},{4,5},{5,6},{6,7},{7,4},{8,9},{9,10},{10,1... | collective-permute-start | bytes 786440 | tf_op jit(solution)/shard_map/ppermute | solution.py:597
  39.6 1.6 %collective-permute-done.5 = bf16[512,256]{1,0:T(8,128)(2,1)S(1)} collective-permute-done((bf16[512,256]{1,0:T(8,128)(2,1)S(1)}, bf16[512,256]{1,0:T(8,128)(2,1)S(1)}, u32[]{:S(2)}, u32[]{:S(2)}) %collective-permute-start.5) | collective-permute-done | bytes 262176 | tf_op jit(solution)/shard_map/ppermute | solution.py:597
  41.7 6.9 %collective-permute-done.12 = bf16[512,256]{1,0:T(8,128)(2,1)S(1)} collective-permute-done((bf16[512,256]{1,0:T(8,128)(2,1)S(1)}, bf16[512,256]{1,0:T(8,128)(2,1)S(1)}, u32[]{:S(2)}, u32[]{:S(2)}) %collective-permute-start.12) | collective-permute-done | bytes 262176 | tf_op jit(solution)/shard_map/ppermute | solution.py:597
  49.1 5.2 %collective-permute-done.6 = bf16[512,256]{1,0:T(8,128)(2,1)S(1)} collective-permute-done((bf16[512,256]{1,0:T(8,128)(2,1)S(1)}, bf16[512,256]{1,0:T(8,128)(2,1)S(1)}, u32[]{:S(2)}, u32[]{:S(2)}) %collective-permute-start.6) | collective-permute-done | bytes 262176 | tf_op jit(solution)/shard_map/ppermute | solution.py:597
  54.7 5.2 %collective-permute-done.13 = bf16[512,256]{1,0:T(8,128)(2,1)S(1)} collective-permute-done((bf16[512,256]{1,0:T(8,128)(2,1)S(1)}, bf16[512,256]{1,0:T(8,128)(2,1)S(1)}, u32[]{:S(2)}, u32[]{:S(2)}) %collective-permute-start.13) | collective-permute-done | bytes 262176 | tf_op jit(solution)/shard_map/ppermute | solution.py:597
  60.3 5.2 %collective-permute-done.7 = bf16[512,256]{1,0:T(8,128)(2,1)S(1)} collective-permute-done((bf16[512,256]{1,0:T(8,128)(2,1)S(1)}, bf16[512,256]{1,0:T(8,128)(2,1)S(1)}, u32[]{:S(2)}, u32[]{:S(2)}) %collective-permute-start.7) | collective-permute-done | bytes 262176 | tf_op jit(solution)/shard_map/ppermute | solution.py:597
  65.5 0.8 %add_add_fusion.total_ref = f32[512,1024]{1,0:T(8,128)S(1)} fusion(f32[512,1024]{1,0:T(8,128)S(1)} %fusion, f32[512,1024]{1,0:T(8,128)S(1)} %fusion.4, f32[512,1024]{1,0:T(8,128)S(1)} %fusion.2, f32[512,1024]{1,0:T(8,128)S(1)} %fusion.7, f32[512,1024]{1,0:T(8,128)S(1)} %fusion.11, f32[512,1024]{1,0:T(8,128)S(1)} %fusion.9, ...), kind=kOutput, calls=%fused_computation | convolution fusion | flops 271581184 | bytes 15466500 | tf_op jit(solution)/shard_map/dot_general | solution.py:603
  66.3 3.2 %collective-permute-done.14.block_ref = bf16[512,256]{1,0:T(8,128)(2,1)S(1)} collective-permute-done((bf16[512,256]{1,0:T(8,128)(2,1)S(1)}, bf16[512,256]{1,0:T(8,128)(2,1)S(1)}, u32[]{:S(2)}, u32[]{:S(2)}) %collective-permute-start.14) | collective-permute-done | bytes 262176 | tf_op jit(solution)/shard_map/ppermute | solution.py:597
  69.5 1.3 %shard_map.108 = bf16[512,1024]{1,0:T(8,128)(2,1)} custom-call(s32[1]{0:T(128)} %bitcast.section, f32[512,1024]{1,0:T(8,128)S(1)} %add_add_fusion.total_ref, bf16[512,256]{1,0:T(8,128)(2,1)S(1)} %collective-permute-done.14.block_ref, bf16[2048,1024]{1,0:T(8,128)(2,1)S(1)} %copy-done), custom_call_target="tpu_custom_call" | custom-call | tf_op jit(solution)/shard_map/pallas_call | solution.py:523
  (43 shorter events, 6.7 us)
Async XLA Ops:
  0.0 6.3 %copy-start.8 = (bf16[512,4,128]{2,1,0:T(4,128)(2,1)S(1)}, bf16[512,4,128]{2,1,0:T(4,128)(2,1)}, u32[]{:S(2)}) copy-start(bf16[512,4,128]{2,1,0:T(4,128)(2,1)} %refs_2_.1) | copy-start | bytes 1572868
  0.0 7.5 %copy-start.1 = (f32[3,4,4,128]{3,2,1,0:T(4,128)S(1)}, f32[3,4,4,128]{3,2,1,0:T(4,128)}, u32[]{:S(2)}) copy-start(f32[3,4,4,128]{3,2,1,0:T(4,128)} %taps_ref.5) | copy-start | bytes 73732
  1.4 7.9 %collective-permute-start = (bf16[24,4,128]{2,1,0:T(4,128)(2,1)}, bf16[24,4,128]{2,1,0:T(4,128)(2,1)S(1)}, u32[]{:S(2)}, u32[]{:S(2)}) collective-permute-start(bf16[24,4,128]{2,1,0:T(4,128)(2,1)} %shard_map.101), channel_id=1, source_target_pairs={{0,4},{4,8},{8,12},{12,16},{16,20},{20,24},{24,28},{1,5},{5,9},{9,... | collective-permute-start | bytes 73736 | tf_op jit(solution)/shard_map/ppermute | solution.py:401
  7.5 1.8 %copy-start.2 = (f32[4,512]{1,0:T(4,128)S(1)}, f32[4,512]{1,0:T(4,128)}, u32[]{:S(2)}) copy-start(f32[4,512]{1,0:T(4,128)} %decay_ref.3) | copy-start | bytes 24580
  7.5 1.8 %copy-start.3 = (f32[4,512]{1,0:T(4,128)S(1)}, f32[4,512]{1,0:T(4,128)}, u32[]{:S(2)}) copy-start(f32[4,512]{1,0:T(4,128)} %strength_ref.3) | copy-start | bytes 24580
  7.5 1.8 %copy-start.4 = (s32[8]{0:T(128)S(1)}, s32[8]{0:T(128)}, u32[]{:S(2)}) copy-start(s32[8]{0:T(128)} %resets.3) | copy-start | bytes 100
  9.4 8.7 %copy-start.6 = (bf16[512,4,128]{2,1,0:T(4,128)(2,1)S(1)}, bf16[512,4,128]{2,1,0:T(4,128)(2,1)}, u32[]{:S(2)}) copy-start(bf16[512,4,128]{2,1,0:T(4,128)(2,1)} %refs_0_.1) | copy-start | bytes 1572868
  9.4 8.7 %copy-start.7 = (bf16[512,4,128]{2,1,0:T(4,128)(2,1)S(1)}, bf16[512,4,128]{2,1,0:T(4,128)(2,1)}, u32[]{:S(2)}) copy-start(bf16[512,4,128]{2,1,0:T(4,128)(2,1)} %param.13) | copy-start | bytes 1572868
  14.4 3.7 %copy-start.5 = (f32[128]{0:T(128)S(1)}, f32[128]{0:T(128)}, u32[]{:S(2)}) copy-start(f32[128]{0:T(128)} %param.18) | copy-start | bytes 1540
  14.5 9.2 %collective-permute-start.3 = (bf16[2,128,256]{2,1,0:T(8,128)(2,1)S(1)}, bf16[2,128,256]{2,1,0:T(8,128)(2,1)S(1)}, u32[]{:S(2)}, u32[]{:S(2)}) collective-permute-start(bf16[2,128,256]{2,1,0:T(8,128)(2,1)S(1)} %get-tuple-element.42.refs_0_), channel_id=1, source_target_pairs={{0,12},{4,8},{8,4},{12,0},{1,13},{5,9},{9,5},{13,1},{2,14},{6,10},... | collective-permute-start | bytes 393224 | tf_op jit(solution)/shard_map/ppermute | solution.py:405
  16.4 7.2 %collective-permute-start.2 = (bf16[2,128,256]{2,1,0:T(8,128)(2,1)S(1)}, bf16[2,128,256]{2,1,0:T(8,128)(2,1)S(1)}, u32[]{:S(2)}, u32[]{:S(2)}) collective-permute-start(bf16[2,128,256]{2,1,0:T(8,128)(2,1)S(1)} %get-tuple-element.42.refs_0_), channel_id=1, source_target_pairs={{0,8},{4,12},{8,0},{12,4},{1,9},{5,13},{9,1},{13,5},{2,10},{6,14},... | collective-permute-start | bytes 393224 | tf_op jit(solution)/shard_map/ppermute | solution.py:405
  17.5 6.2 %collective-permute-start.1 = (bf16[2,128,256]{2,1,0:T(8,128)(2,1)S(1)}, bf16[2,128,256]{2,1,0:T(8,128)(2,1)S(1)}, u32[]{:S(2)}, u32[]{:S(2)}) collective-permute-start(bf16[2,128,256]{2,1,0:T(8,128)(2,1)S(1)} %get-tuple-element.42.refs_0_), channel_id=1, source_target_pairs={{0,4},{4,0},{8,12},{12,8},{1,5},{5,1},{9,13},{13,9},{2,6},{6,2},{1... | collective-permute-start | bytes 393224 | tf_op jit(solution)/shard_map/ppermute | solution.py:405
  24.4 8.0 %collective-permute-start.10 = (bf16[2,128,256]{2,1,0:T(8,128)(2,1)S(1)}, bf16[2,128,256]{2,1,0:T(8,128)(2,1)S(1)}, u32[]{:S(2)}, u32[]{:S(2)}) collective-permute-start(bf16[2,128,256]{2,1,0:T(8,128)(2,1)S(1)} %get-tuple-element.51.refs_0_), channel_id=1, source_target_pairs={{0,12},{4,8},{8,4},{12,0},{1,13},{5,9},{9,5},{13,1},{2,14},{6,10},... | collective-permute-start | bytes 393224 | tf_op jit(solution)/shard_map/ppermute | solution.py:405
  26.4 6.3 %collective-permute-start.9 = (bf16[2,128,256]{2,1,0:T(8,128)(2,1)S(1)}, bf16[2,128,256]{2,1,0:T(8,128)(2,1)S(1)}, u32[]{:S(2)}, u32[]{:S(2)}) collective-permute-start(bf16[2,128,256]{2,1,0:T(8,128)(2,1)S(1)} %get-tuple-element.51.refs_0_), channel_id=1, source_target_pairs={{0,8},{4,12},{8,0},{12,4},{1,9},{5,13},{9,1},{13,5},{2,10},{6,14},... | collective-permute-start | bytes 393224 | tf_op jit(solution)/shard_map/ppermute | solution.py:405
  27.4 5.4 %collective-permute-start.8 = (bf16[2,128,256]{2,1,0:T(8,128)(2,1)S(1)}, bf16[2,128,256]{2,1,0:T(8,128)(2,1)S(1)}, u32[]{:S(2)}, u32[]{:S(2)}) collective-permute-start(bf16[2,128,256]{2,1,0:T(8,128)(2,1)S(1)} %get-tuple-element.51.refs_0_), channel_id=1, source_target_pairs={{0,4},{4,0},{8,12},{12,8},{1,5},{5,1},{9,13},{13,9},{2,6},{6,2},{1... | collective-permute-start | bytes 393224 | tf_op jit(solution)/shard_map/ppermute | solution.py:405
  28.0 2.2 %collective-permute-start.4 = (bf16[2,128,128]{2,1,0:T(8,128)(2,1)S(1)}, bf16[2,128,128]{2,1,0:T(8,128)(2,1)S(1)}, u32[]{:S(2)}, u32[]{:S(2)}) collective-permute-start(bf16[2,128,128]{2,1,0:T(8,128)(2,1)S(1)} %get-tuple-element.46), channel_id=1, source_target_pairs={{0,16},{1,17},{2,18},{3,19},{4,20},{5,21},{6,22},{7,23},{8,24},{9,... | collective-permute-start | bytes 196616 | tf_op jit(solution)/shard_map/ppermute | solution.py:401
  30.7 10.5 %collective-permute-start.5 = (bf16[512,256]{1,0:T(8,128)(2,1)S(1)}, bf16[512,256]{1,0:T(8,128)(2,1)S(1)}, u32[]{:S(2)}, u32[]{:S(2)}) collective-permute-start(bf16[512,256]{1,0:T(8,128)(2,1)S(1)} %shard_map.105), channel_id=1, source_target_pairs={{0,1},{1,2},{2,3},{3,0},{4,5},{5,6},{6,7},{7,4},{8,9},{9,10},{10,1... | collective-permute-start | bytes 786440 | tf_op jit(solution)/shard_map/ppermute | solution.py:597
  33.5 3.4 %collective-permute-start.11 = (bf16[2,128,128]{2,1,0:T(8,128)(2,1)S(1)}, bf16[2,128,128]{2,1,0:T(8,128)(2,1)S(1)}, u32[]{:S(2)}, u32[]{:S(2)}) collective-permute-start(bf16[2,128,128]{2,1,0:T(8,128)(2,1)S(1)} %get-tuple-element.55), channel_id=1, source_target_pairs={{0,16},{1,17},{2,18},{3,19},{4,20},{5,21},{6,22},{7,23},{8,24},{9,... | collective-permute-start | bytes 196616 | tf_op jit(solution)/shard_map/ppermute | solution.py:401
  35.3 3.9 %copy-start = (bf16[2048,1024]{1,0:T(8,128)(2,1)S(1)}, bf16[2048,1024]{1,0:T(8,128)(2,1)}, u32[]{:S(2)}) copy-start(bf16[2048,1024]{1,0:T(8,128)(2,1)} %weights_ref.1) | copy-start | bytes 12582916
  37.6 11.1 %collective-permute-start.12 = (bf16[512,256]{1,0:T(8,128)(2,1)S(1)}, bf16[512,256]{1,0:T(8,128)(2,1)S(1)}, u32[]{:S(2)}, u32[]{:S(2)}) collective-permute-start(bf16[512,256]{1,0:T(8,128)(2,1)S(1)} %shard_map.107), channel_id=1, source_target_pairs={{0,1},{1,2},{2,3},{3,0},{4,5},{5,6},{6,7},{7,4},{8,9},{9,10},{10,1... | collective-permute-start | bytes 786440 | tf_op jit(solution)/shard_map/ppermute | solution.py:597
  41.2 13.1 %collective-permute-start.6 = (bf16[512,256]{1,0:T(8,128)(2,1)S(1)}, bf16[512,256]{1,0:T(8,128)(2,1)S(1)}, u32[]{:S(2)}, u32[]{:S(2)}) collective-permute-start(bf16[512,256]{1,0:T(8,128)(2,1)S(1)} %collective-permute-done.5), channel_id=1, source_target_pairs={{0,1},{1,2},{2,3},{3,0},{4,5},{5,6},{6,7},{7,4},{8,9},{9,10},{10,1... | collective-permute-start | bytes 786440 | tf_op jit(solution)/shard_map/ppermute | solution.py:597
  48.7 11.2 %collective-permute-start.13 = (bf16[512,256]{1,0:T(8,128)(2,1)S(1)}, bf16[512,256]{1,0:T(8,128)(2,1)S(1)}, u32[]{:S(2)}, u32[]{:S(2)}) collective-permute-start(bf16[512,256]{1,0:T(8,128)(2,1)S(1)} %collective-permute-done.12), channel_id=1, source_target_pairs={{0,1},{1,2},{2,3},{3,0},{4,5},{5,6},{6,7},{7,4},{8,9},{9,10},{10,1... | collective-permute-start | bytes 786440 | tf_op jit(solution)/shard_map/ppermute | solution.py:597
  54.3 11.2 %collective-permute-start.7 = (bf16[512,256]{1,0:T(8,128)(2,1)S(1)}, bf16[512,256]{1,0:T(8,128)(2,1)S(1)}, u32[]{:S(2)}, u32[]{:S(2)}) collective-permute-start(bf16[512,256]{1,0:T(8,128)(2,1)S(1)} %collective-permute-done.6), channel_id=1, source_target_pairs={{0,1},{1,2},{2,3},{3,0},{4,5},{5,6},{6,7},{7,4},{8,9},{9,10},{10,1... | collective-permute-start | bytes 786440 | tf_op jit(solution)/shard_map/ppermute | solution.py:597
  59.9 9.6 %collective-permute-start.14 = (bf16[512,256]{1,0:T(8,128)(2,1)S(1)}, bf16[512,256]{1,0:T(8,128)(2,1)S(1)}, u32[]{:S(2)}, u32[]{:S(2)}) collective-permute-start(bf16[512,256]{1,0:T(8,128)(2,1)S(1)} %collective-permute-done.13), channel_id=1, source_target_pairs={{0,1},{1,2},{2,3},{3,0},{4,5},{5,6},{6,7},{7,4},{8,9},{9,10},{10,1... | collective-permute-start | bytes 786440 | tf_op jit(solution)/shard_map/ppermute | solution.py:597

commit v22 on v21

--- a/solution.py
+++ b/solution.py
@@ -379,18 +379,18 @@
             ).astype(BF16)
 
 
-def last_kernel(section, total_ref, block_ref, weights_ref, out_ref, tiles, written):
-    width = block_ref.shape[1]
+def last_kernel(begin, section, total_ref, block_ref, weights_ref, *refs):
+    out_ref, tiles, written = refs[-3:]
+    count, width = block_ref.shape
     rows = pl.ds(pl.multiple_of(section[0] * width, width), width)
     copies = []
     for i in range(total_ref.shape[1] // TILE):
         here = slice(i * TILE, (i + 1) * TILE)
         term = mul(block_ref[...], weights_ref[rows, here])
-        tiles[:, here] = (total_ref[:, here] + term).astype(BF16)
+        tiles[:, here] = (total_ref[begin : begin + count, here] + term).astype(BF16)
         columns = pl.ds(i * TILE, TILE)
-        copies.append(
-            pltpu.make_async_copy(tiles.at[:, columns], out_ref.at[:, columns], written.at[i])
-        )
+        target = out_ref.at[pl.ds(begin, count), columns]
+        copies.append(pltpu.make_async_copy(tiles.at[:, columns], target, written.at[i]))
         copies[-1].start()
     for copy in copies:
         copy.wait()
@@ -518,19 +518,21 @@
     )(arrived, before, *reads)
 
 
-def last_projected(section, total, block, weights):
+def last_projected(begin, section, total, block, weights, earlier):
     length, columns = total.shape
+    whole = pl.BlockSpec(memory_space=pl.ANY)
     return pl.pallas_call(
-        last_kernel,
+        functools.partial(last_kernel, begin),
         out_shape=jax.ShapeDtypeStruct((length, columns), BF16),
-        in_specs=[SMEM] + [VMEM] * 3,
-        out_specs=pl.BlockSpec(memory_space=pl.ANY),
+        in_specs=[SMEM] + [VMEM] * 3 + [whole] * len(earlier),
+        out_specs=whole,
         scratch_shapes=[
-            pltpu.VMEM((length, columns), BF16),
+            pltpu.VMEM((block.shape[0], columns), BF16),
             pltpu.SemaphoreType.DMA((columns // TILE,)),
         ],
+        input_output_aliases={4: 0} if earlier else {},
         compiler_params=LAST_PARAMS,
-    )(section.astype(jnp.int32).reshape(1), total, block, weights)
+    )(section.astype(jnp.int32).reshape(1), total, block, weights, *earlier)
 
 
 def after(first, *values):
@@ -594,11 +596,22 @@
     for k in range(ring):
         owner = lax.rem(mine + ring - k, ring)
         last = k + 1 == ring
-        following = blocks if last else [lax.ppermute(x, "head", around) for x in blocks]
+        following = blocks if last else [lax.ppermute(x, "head", around) for x in blocks[:-1]]
+        if k + 2 == ring:
+            count = length // 2
+            following.append(
+                [lax.ppermute(x, "head", around) for x in (blocks[-1][:count], blocks[-1][count:])]
+            )
+        elif not last:
+            following.append(lax.ppermute(blocks[-1], "head", around))
         for g, block in enumerate(blocks):
             section = owner * GROUPS + g
             if last and g + 1 == GROUPS:
-                return last_projected(section, sum(sums[1:], sums[0]), block, weights)
+                total = sum(sums[1:], sums[0])
+                result = []
+                for i, half in enumerate(block):
+                    result = [last_projected(i * count, section, total, half, weights, result)]
+                return result[0]
             rows = lax.dynamic_slice_in_dim(weights, section * width, width, 0)
             term = jnp.dot(block, rows, preferred_element_type=F32)
             sums[g] = term if sums[g] is None else sums[g] + term

time: 71.2 us -> 70.9 us (level)
  waiting for transfers between devices: 28.5 us -> 26 us
  starting transfers between devices: 18.3 us -> 19.7 us
  Pallas kernels: 17.7 us -> 18.5 us
    ppermute x6 -> x5, waiting for transfers between devices: 27.2 us -> 12.6 us  [on_device(): lax.ppermute(x, 'head', around)]
    ppermute x0 -> x2, waiting for transfers between devices: none -> 12.1 us  [on_device(): following.append(lax.ppermute(blocks[-1], 'head', around))]
    ppermute x0 -> x2, starting transfers between devices: none -> 1.63 us  [on_device(): following.append(lax.ppermute(blocks[-1], 'head', around))]
    pallas_call x1 -> x2, Pallas kernels: 1.31 us -> 2.11 us  [last_projected(): pl.pallas_call(functools.partial(last_kernel, begin), out_shape=jax.Shape...]
    ppermute x6 -> x5, starting transfers between devices: 3.34 us -> 3.1 us  [on_device(): lax.ppermute(x, 'head', around)]
  transfers between devices with their start and end apart: 15 -> 16, of which waited for: 9 -> 10; matrix products, arithmetic and copies ran while one was open for 8% -> 8% of each run, Pallas kernels for 13% -> 14%
where the time goes in v22:
time: 70.9 us; the launch traced here: 70.7 us
  waiting for transfers between devices  26 us (37%)
  starting transfers between devices  19.7 us (28%)
  Pallas kernels  18.5 us (26%)
  matrix products  4.59 us (6%)
  local copies, waits for them, and re-layouts  1.39 us (2%)
    ppermute x5, waiting for transfers between devices, on_device(): lax.ppermute(x, 'head', around)  12.6 us
    ppermute x2, waiting for transfers between devices, on_device(): following.append(lax.ppermute(blocks[-1], 'head', around))  12.1 us
    ppermute x3, starting transfers between devices, from_behind(): lax.ppermute(value, axis, [(i, i + steps) for i in range(count - steps)])  7.86 us
    ppermute x6, starting transfers between devices, exchange(): lax.ppermute(own_map, 'leaf', pairs_at(k, leaves))  7.11 us
    pallas_call x1, Pallas kernels, reads_of(): pl.pallas_call(functools.partial(reads_kernel, base), out_shape=(jax.Shap...  5.42 us
    pallas_call x1, Pallas kernels, maps_of(): pl.pallas_call(functools.partial(maps_kernel, base), out_shape=(jax.Shape...  5.05 us
    dot_general x7, matrix products, on_device(): term = jnp.dot(block, rows, preferred_element_type=F32)  4.59 us
    ppermute x5, starting transfers between devices, on_device(): lax.ppermute(x, 'head', around)  3.1 us
  transfers between devices with their start and end apart: 16, of which 10 were waited for; matrix products, arithmetic and copies ran while one was open for 8% of the time, Pallas kernels for 14%

profile of v22, /device:TPU:0, one launch (start us, length us, event | category | flops | bytes accessed | tf_op | source)
XLA Modules:
  0.0 70.7 jit_solution(5385616999426944051)
XLA Ops:
  0.0 1.4 %shard_map.101 = bf16[24,4,128]{2,1,0:T(4,128)(2,1)} custom-call(bf16[512,4,128]{2,1,0:T(4,128)(2,1)} %refs_0_.1, bf16[512,4,128]{2,1,0:T(4,128)(2,1)} %refs_1_.1, bf16[512,4,128]{2,1,0:T(4,128)(2,1)} %refs_2_.1), custom_call_target="tpu_custom_call" | custom-call | flops 1000000000 | bytes 65536 | tf_op jit(solution)/shard_map/pallas_call | solution.py:418
  1.4 4.8 %collective-permute-start = (bf16[24,4,128]{2,1,0:T(4,128)(2,1)}, bf16[24,4,128]{2,1,0:T(4,128)(2,1)S(1)}, u32[]{:S(2)}, u32[]{:S(2)}) collective-permute-start(bf16[24,4,128]{2,1,0:T(4,128)(2,1)} %shard_map.101), channel_id=1, source_target_pairs={{0,4},{4,8},{8,12},{12,16},{16,20},{20,24},{24,28},{1,5},{5,9},{9,... | collective-permute-start | bytes 73736 | tf_op jit(solution)/shard_map/ppermute | solution.py:401
  6.3 1.2 %copy_bitcast_fusion.2 = (bf16[4,512,128]{2,1,0:T(8,128)(2,1)S(1)}, bf16[4,512,128]{2,1,0:T(8,128)(2,1)S(1)}) fusion(bf16[512,4,128]{2,1,0:T(4,128)(2,1)S(1)} %copy-done.8, bf16[512,4,128]{2,1,0:T(4,128)(2,1)} %refs_1_.1), kind=kLoop, calls=%fused_computation.3 | loop fusion | bytes 2097152 | tf_op jit(solution)/shard_map/transpose | solution.py:557
  7.5 1.8 %shard_map.100 = (bf16[4,512,128]{2,1,0:T(8,128)(2,1)S(1)}, bf16[4,512,128]{2,1,0:T(8,128)(2,1)S(1)}, f32[2,4,16,128]{3,2,1,0:T(8,128)S(1)}) custom-call(bf16[4,512,128]{2,1,0:T(8,128)(2,1)S(1)} %get-tuple-element.60.key_ref, bf16[4,512,128]{2,1,0:T(8,128)(2,1)S(1)} %get-tuple-element.59.value_ref, f32[3,4,4,128]{3,2,1,0:T(4,128)S(1)} %copy-done.1), custom_call_target="tpu_custom_call" | custom-call | flops 3000000000 | bytes 4194304 | tf_op jit(solution)/shard_map/pallas_call | solution.py:432
  9.4 5.1 %shard_map.102 = (bf16[4,512,128]{2,1,0:T(8,128)(2,1)S(1)}, f32[4,512,256]{2,1,0:T(8,128)S(1)}, f32[4,3,128,256]{3,2,1,0:T(8,128)S(1)}, bf16[2,128,256]{2,1,0:T(8,128)(2,1)S(1)}, bf16[2,128,256]{2,1,0:T(8,128)(2,1)S(1)}) custom-call(s32[8]{0:T(128)S(1)} %copy-done.4, bf16[4,512,128]{2,1,0:T(8,128)(2,1)S(1)} %get-tuple-element.31.unit_in_ref, ...), custom_call_target="tpu_custom_call" | custom-call | flops 5000000000 | bytes 4194304 | tf_op jit(solution)/shard_map/pallas_call | solution.py:448
  14.5 2.0 %collective-permute-start.3 = (bf16[2,128,256]{2,1,0:T(8,128)(2,1)S(1)}, bf16[2,128,256]{2,1,0:T(8,128)(2,1)S(1)}, u32[]{:S(2)}, u32[]{:S(2)}) collective-permute-start(bf16[2,128,256]{2,1,0:T(8,128)(2,1)S(1)} %get-tuple-element.42.refs_0_), channel_id=1, source_target_pairs={{0,12},{4,8},{8,4},{12,0},{1,13},{5,9},{9,5},{13,1},{2,14},{6,10},... | collective-permute-start | bytes 393224 | tf_op jit(solution)/shard_map/ppermute | solution.py:405
  16.4 1.1 %collective-permute-start.2 = (bf16[2,128,256]{2,1,0:T(8,128)(2,1)S(1)}, bf16[2,128,256]{2,1,0:T(8,128)(2,1)S(1)}, u32[]{:S(2)}, u32[]{:S(2)}) collective-permute-start(bf16[2,128,256]{2,1,0:T(8,128)(2,1)S(1)} %get-tuple-element.42.refs_0_), channel_id=1, source_target_pairs={{0,8},{4,12},{8,0},{12,4},{1,9},{5,13},{9,1},{13,5},{2,10},{6,14},... | collective-permute-start | bytes 393224 | tf_op jit(solution)/shard_map/ppermute | solution.py:405
  18.2 5.4 %shard_map.103 = (bf16[4,512,128]{2,1,0:T(8,128)(2,1)S(1)}, f32[4,512,128]{2,1,0:T(8,128)S(1)}, f32[4,512,128]{2,1,0:T(8,128)S(1)}) custom-call(s32[8]{0:T(128)S(1)} %copy-done.4, bf16[4,512,128]{2,1,0:T(8,128)(2,1)S(1)} %bitcast.20, bf16[4,512,128]{2,1,0:T(8,128)(2,1)S(1)} %bitcast.21, f32[1,128]{1,0:T(1,128)S(1)} %bitcast.22, ...), custom_call_target="tpu_custom_call" | custom-call | flops 3000000000 | bytes 4194304 | tf_op jit(solution)/shard_map/pallas_call | solution.py:474
  24.4 2.0 %collective-permute-start.10 = (bf16[2,128,256]{2,1,0:T(8,128)(2,1)S(1)}, bf16[2,128,256]{2,1,0:T(8,128)(2,1)S(1)}, u32[]{:S(2)}, u32[]{:S(2)}) collective-permute-start(bf16[2,128,256]{2,1,0:T(8,128)(2,1)S(1)} %get-tuple-element.51.refs_0_), channel_id=1, source_target_pairs={{0,12},{4,8},{8,4},{12,0},{1,13},{5,9},{9,5},{13,1},{2,14},{6,10},... | collective-permute-start | bytes 393224 | tf_op jit(solution)/shard_map/ppermute | solution.py:405
  26.4 1.1 %collective-permute-start.9 = (bf16[2,128,256]{2,1,0:T(8,128)(2,1)S(1)}, bf16[2,128,256]{2,1,0:T(8,128)(2,1)S(1)}, u32[]{:S(2)}, u32[]{:S(2)}) collective-permute-start(bf16[2,128,256]{2,1,0:T(8,128)(2,1)S(1)} %get-tuple-element.51.refs_0_), channel_id=1, source_target_pairs={{0,8},{4,12},{8,0},{12,4},{1,9},{5,13},{9,1},{13,5},{2,10},{6,14},... | collective-permute-start | bytes 393224 | tf_op jit(solution)/shard_map/ppermute | solution.py:405
  28.0 1.3 %collective-permute-start.4 = (bf16[2,128,128]{2,1,0:T(8,128)(2,1)S(1)}, bf16[2,128,128]{2,1,0:T(8,128)(2,1)S(1)}, u32[]{:S(2)}, u32[]{:S(2)}) collective-permute-start(bf16[2,128,128]{2,1,0:T(8,128)(2,1)S(1)} %get-tuple-element.46), channel_id=1, source_target_pairs={{0,16},{1,17},{2,18},{3,19},{4,20},{5,21},{6,22},{7,23},{8,24},{9,... | collective-permute-start | bytes 196616 | tf_op jit(solution)/shard_map/ppermute | solution.py:401
  30.7 1.6 %collective-permute-start.5 = (bf16[512,256]{1,0:T(8,128)(2,1)S(1)}, bf16[512,256]{1,0:T(8,128)(2,1)S(1)}, u32[]{:S(2)}, u32[]{:S(2)}) collective-permute-start(bf16[512,256]{1,0:T(8,128)(2,1)S(1)} %shard_map.105), channel_id=1, source_target_pairs={{0,1},{1,2},{2,3},{3,0},{4,5},{5,6},{6,7},{7,4},{8,9},{9,10},{10,1... | collective-permute-start | bytes 786440 | tf_op jit(solution)/shard_map/ppermute | solution.py:599
  33.5 1.7 %collective-permute-start.11 = (bf16[2,128,128]{2,1,0:T(8,128)(2,1)S(1)}, bf16[2,128,128]{2,1,0:T(8,128)(2,1)S(1)}, u32[]{:S(2)}, u32[]{:S(2)}) collective-permute-start(bf16[2,128,128]{2,1,0:T(8,128)(2,1)S(1)} %get-tuple-element.55), channel_id=1, source_target_pairs={{0,16},{1,17},{2,18},{3,19},{4,20},{5,21},{6,22},{7,23},{8,24},{9,... | collective-permute-start | bytes 196616 | tf_op jit(solution)/shard_map/ppermute | solution.py:401
  35.3 1.6 %fusion.11 = f32[512,1024]{1,0:T(8,128)S(1)} fusion(bf16[512,256]{1,0:T(8,128)(2,1)S(1)} %shard_map.105, bf16[2048,1024]{1,0:T(8,128)(2,1)} %weights_ref.3, s32[]{:T(128)S(6)} %select_n.21), kind=kOutput, calls=%fused_computation.16 | convolution fusion | flops 268435456 | bytes 2883588 | tf_op jit(solution)/shard_map/dot_general | solution.py:616
  37.6 1.6 %collective-permute-start.12 = (bf16[512,256]{1,0:T(8,128)(2,1)S(1)}, bf16[512,256]{1,0:T(8,128)(2,1)S(1)}, u32[]{:S(2)}, u32[]{:S(2)}) collective-permute-start(bf16[512,256]{1,0:T(8,128)(2,1)S(1)} %shard_map.107), channel_id=1, source_target_pairs={{0,1},{1,2},{2,3},{3,0},{4,5},{5,6},{6,7},{7,4},{8,9},{9,10},{10,1... | collective-permute-start | bytes 786440 | tf_op jit(solution)/shard_map/ppermute | solution.py:606
  39.6 1.6 %collective-permute-done.5 = bf16[512,256]{1,0:T(8,128)(2,1)S(1)} collective-permute-done((bf16[512,256]{1,0:T(8,128)(2,1)S(1)}, bf16[512,256]{1,0:T(8,128)(2,1)S(1)}, u32[]{:S(2)}, u32[]{:S(2)}) %collective-permute-start.5) | collective-permute-done | bytes 262176 | tf_op jit(solution)/shard_map/ppermute | solution.py:599
  41.7 6.9 %collective-permute-done.12 = bf16[512,256]{1,0:T(8,128)(2,1)S(1)} collective-permute-done((bf16[512,256]{1,0:T(8,128)(2,1)S(1)}, bf16[512,256]{1,0:T(8,128)(2,1)S(1)}, u32[]{:S(2)}, u32[]{:S(2)}) %collective-permute-start.12) | collective-permute-done | bytes 262176 | tf_op jit(solution)/shard_map/ppermute | solution.py:606
  49.1 5.2 %collective-permute-done.6 = bf16[512,256]{1,0:T(8,128)(2,1)S(1)} collective-permute-done((bf16[512,256]{1,0:T(8,128)(2,1)S(1)}, bf16[512,256]{1,0:T(8,128)(2,1)S(1)}, u32[]{:S(2)}, u32[]{:S(2)}) %collective-permute-start.6) | collective-permute-done | bytes 262176 | tf_op jit(solution)/shard_map/ppermute | solution.py:599
  54.7 5.2 %collective-permute-done.13 = bf16[512,256]{1,0:T(8,128)(2,1)S(1)} collective-permute-done((bf16[512,256]{1,0:T(8,128)(2,1)S(1)}, bf16[512,256]{1,0:T(8,128)(2,1)S(1)}, u32[]{:S(2)}, u32[]{:S(2)}) %collective-permute-start.13) | collective-permute-done | bytes 262176 | tf_op jit(solution)/shard_map/ppermute | solution.py:606
  60.0 1.3 %collective-permute-start.14 = (bf16[256,256]{1,0:T(8,128)(2,1)S(1)}, bf16[256,256]{1,0:T(8,128)(2,1)S(1)}, u32[]{:S(2)}, u32[]{:S(2)}) collective-permute-start(bf16[256,256]{1,0:T(8,128)(2,1)S(1)} %get-tuple-element.58), channel_id=1, source_target_pairs={{0,1},{1,2},{2,3},{3,0},{4,5},{5,6},{6,7},{7,4},{8,9},{9,10},{10,1... | collective-permute-start | bytes 393224 | tf_op jit(solution)/shard_map/ppermute | solution.py:603
  61.8 3.7 %collective-permute-done.7 = bf16[512,256]{1,0:T(8,128)(2,1)S(1)} collective-permute-done((bf16[512,256]{1,0:T(8,128)(2,1)S(1)}, bf16[512,256]{1,0:T(8,128)(2,1)S(1)}, u32[]{:S(2)}, u32[]{:S(2)}) %collective-permute-start.7) | collective-permute-done | bytes 262176 | tf_op jit(solution)/shard_map/ppermute | solution.py:599
  66.3 1.8 %collective-permute-done.15.block_ref = bf16[256,256]{1,0:T(8,128)(2,1)S(1)} collective-permute-done((bf16[256,256]{1,0:T(8,128)(2,1)S(1)}, bf16[256,256]{1,0:T(8,128)(2,1)S(1)}, u32[]{:S(2)}, u32[]{:S(2)}) %collective-permute-start.15) | collective-permute-done | bytes 131104 | tf_op jit(solution)/shard_map/ppermute | solution.py:603
  68.1 1.1 %shard_map.108.refs_0_ = bf16[512,1024]{1,0:T(8,128)(2,1)} custom-call(s32[1]{0:T(128)} %bitcast.section, f32[512,1024]{1,0:T(8,128)S(1)} %add_add_fusion.total_ref, bf16[256,256]{1,0:T(8,128)(2,1)S(1)} %collective-permute-done.15.block_ref, bf16[2048,1024]{1,0:T(8,128)(2,1)S(1)} %copy-done), custom_call_target="tpu_custom_call" | custom-call | tf_op jit(solution)/shard_map/pallas_call | solution.py:524
  69.5 1.1 %shard_map.109 = bf16[512,1024]{1,0:T(8,128)(2,1)} custom-call(s32[1]{0:T(128)} %bitcast.section, f32[512,1024]{1,0:T(8,128)S(1)} %add_add_fusion.total_ref, bf16[256,256]{1,0:T(8,128)(2,1)S(1)} %collective-permute-done.14.block_ref, bf16[2048,1024]{1,0:T(8,128)(2,1)S(1)} %copy-done, ...), custom_call_target="tpu_custom_call", output_to_operand_aliasing={{}: (4, {})} | custom-call | tf_op jit(solution)/shard_map/pallas_call | solution.py:524
  (47 shorter events, 8.7 us)
Async XLA Ops:
  0.0 6.3 %copy-start.8 = (bf16[512,4,128]{2,1,0:T(4,128)(2,1)S(1)}, bf16[512,4,128]{2,1,0:T(4,128)(2,1)}, u32[]{:S(2)}) copy-start(bf16[512,4,128]{2,1,0:T(4,128)(2,1)} %refs_2_.1) | copy-start | bytes 1572868
  0.0 7.5 %copy-start.1 = (f32[3,4,4,128]{3,2,1,0:T(4,128)S(1)}, f32[3,4,4,128]{3,2,1,0:T(4,128)}, u32[]{:S(2)}) copy-start(f32[3,4,4,128]{3,2,1,0:T(4,128)} %taps_ref.5) | copy-start | bytes 73732
  1.4 7.9 %collective-permute-start = (bf16[24,4,128]{2,1,0:T(4,128)(2,1)}, bf16[24,4,128]{2,1,0:T(4,128)(2,1)S(1)}, u32[]{:S(2)}, u32[]{:S(2)}) collective-permute-start(bf16[24,4,128]{2,1,0:T(4,128)(2,1)} %shard_map.101), channel_id=1, source_target_pairs={{0,4},{4,8},{8,12},{12,16},{16,20},{20,24},{24,28},{1,5},{5,9},{9,... | collective-permute-start | bytes 73736 | tf_op jit(solution)/shard_map/ppermute | solution.py:401
  7.5 1.8 %copy-start.2 = (f32[4,512]{1,0:T(4,128)S(1)}, f32[4,512]{1,0:T(4,128)}, u32[]{:S(2)}) copy-start(f32[4,512]{1,0:T(4,128)} %decay_ref.3) | copy-start | bytes 24580
  7.5 1.8 %copy-start.3 = (f32[4,512]{1,0:T(4,128)S(1)}, f32[4,512]{1,0:T(4,128)}, u32[]{:S(2)}) copy-start(f32[4,512]{1,0:T(4,128)} %strength_ref.3) | copy-start | bytes 24580
  9.4 8.7 %copy-start.6 = (bf16[512,4,128]{2,1,0:T(4,128)(2,1)S(1)}, bf16[512,4,128]{2,1,0:T(4,128)(2,1)}, u32[]{:S(2)}) copy-start(bf16[512,4,128]{2,1,0:T(4,128)(2,1)} %refs_0_.1) | copy-start | bytes 1572868
  9.4 8.7 %copy-start.7 = (bf16[512,4,128]{2,1,0:T(4,128)(2,1)S(1)}, bf16[512,4,128]{2,1,0:T(4,128)(2,1)}, u32[]{:S(2)}) copy-start(bf16[512,4,128]{2,1,0:T(4,128)(2,1)} %param.13) | copy-start | bytes 1572868
  14.4 3.7 %copy-start.5 = (f32[128]{0:T(128)S(1)}, f32[128]{0:T(128)}, u32[]{:S(2)}) copy-start(f32[128]{0:T(128)} %param.18) | copy-start | bytes 1540
  14.5 9.2 %collective-permute-start.3 = (bf16[2,128,256]{2,1,0:T(8,128)(2,1)S(1)}, bf16[2,128,256]{2,1,0:T(8,128)(2,1)S(1)}, u32[]{:S(2)}, u32[]{:S(2)}) collective-permute-start(bf16[2,128,256]{2,1,0:T(8,128)(2,1)S(1)} %get-tuple-element.42.refs_0_), channel_id=1, source_target_pairs={{0,12},{4,8},{8,4},{12,0},{1,13},{5,9},{9,5},{13,1},{2,14},{6,10},... | collective-permute-start | bytes 393224 | tf_op jit(solution)/shard_map/ppermute | solution.py:405
  16.4 7.2 %collective-permute-start.2 = (bf16[2,128,256]{2,1,0:T(8,128)(2,1)S(1)}, bf16[2,128,256]{2,1,0:T(8,128)(2,1)S(1)}, u32[]{:S(2)}, u32[]{:S(2)}) collective-permute-start(bf16[2,128,256]{2,1,0:T(8,128)(2,1)S(1)} %get-tuple-element.42.refs_0_), channel_id=1, source_target_pairs={{0,8},{4,12},{8,0},{12,4},{1,9},{5,13},{9,1},{13,5},{2,10},{6,14},... | collective-permute-start | bytes 393224 | tf_op jit(solution)/shard_map/ppermute | solution.py:405
  17.5 6.2 %collective-permute-start.1 = (bf16[2,128,256]{2,1,0:T(8,128)(2,1)S(1)}, bf16[2,128,256]{2,1,0:T(8,128)(2,1)S(1)}, u32[]{:S(2)}, u32[]{:S(2)}) collective-permute-start(bf16[2,128,256]{2,1,0:T(8,128)(2,1)S(1)} %get-tuple-element.42.refs_0_), channel_id=1, source_target_pairs={{0,4},{4,0},{8,12},{12,8},{1,5},{5,1},{9,13},{13,9},{2,6},{6,2},{1... | collective-permute-start | bytes 393224 | tf_op jit(solution)/shard_map/ppermute | solution.py:405
  24.4 8.0 %collective-permute-start.10 = (bf16[2,128,256]{2,1,0:T(8,128)(2,1)S(1)}, bf16[2,128,256]{2,1,0:T(8,128)(2,1)S(1)}, u32[]{:S(2)}, u32[]{:S(2)}) collective-permute-start(bf16[2,128,256]{2,1,0:T(8,128)(2,1)S(1)} %get-tuple-element.51.refs_0_), channel_id=1, source_target_pairs={{0,12},{4,8},{8,4},{12,0},{1,13},{5,9},{9,5},{13,1},{2,14},{6,10},... | collective-permute-start | bytes 393224 | tf_op jit(solution)/shard_map/ppermute | solution.py:405
  26.4 6.3 %collective-permute-start.9 = (bf16[2,128,256]{2,1,0:T(8,128)(2,1)S(1)}, bf16[2,128,256]{2,1,0:T(8,128)(2,1)S(1)}, u32[]{:S(2)}, u32[]{:S(2)}) collective-permute-start(bf16[2,128,256]{2,1,0:T(8,128)(2,1)S(1)} %get-tuple-element.51.refs_0_), channel_id=1, source_target_pairs={{0,8},{4,12},{8,0},{12,4},{1,9},{5,13},{9,1},{13,5},{2,10},{6,14},... | collective-permute-start | bytes 393224 | tf_op jit(solution)/shard_map/ppermute | solution.py:405
  27.4 5.4 %collective-permute-start.8 = (bf16[2,128,256]{2,1,0:T(8,128)(2,1)S(1)}, bf16[2,128,256]{2,1,0:T(8,128)(2,1)S(1)}, u32[]{:S(2)}, u32[]{:S(2)}) collective-permute-start(bf16[2,128,256]{2,1,0:T(8,128)(2,1)S(1)} %get-tuple-element.51.refs_0_), channel_id=1, source_target_pairs={{0,4},{4,0},{8,12},{12,8},{1,5},{5,1},{9,13},{13,9},{2,6},{6,2},{1... | collective-permute-start | bytes 393224 | tf_op jit(solution)/shard_map/ppermute | solution.py:405
  28.0 2.2 %collective-permute-start.4 = (bf16[2,128,128]{2,1,0:T(8,128)(2,1)S(1)}, bf16[2,128,128]{2,1,0:T(8,128)(2,1)S(1)}, u32[]{:S(2)}, u32[]{:S(2)}) collective-permute-start(bf16[2,128,128]{2,1,0:T(8,128)(2,1)S(1)} %get-tuple-element.46), channel_id=1, source_target_pairs={{0,16},{1,17},{2,18},{3,19},{4,20},{5,21},{6,22},{7,23},{8,24},{9,... | collective-permute-start | bytes 196616 | tf_op jit(solution)/shard_map/ppermute | solution.py:401
  30.7 10.5 %collective-permute-start.5 = (bf16[512,256]{1,0:T(8,128)(2,1)S(1)}, bf16[512,256]{1,0:T(8,128)(2,1)S(1)}, u32[]{:S(2)}, u32[]{:S(2)}) collective-permute-start(bf16[512,256]{1,0:T(8,128)(2,1)S(1)} %shard_map.105), channel_id=1, source_target_pairs={{0,1},{1,2},{2,3},{3,0},{4,5},{5,6},{6,7},{7,4},{8,9},{9,10},{10,1... | collective-permute-start | bytes 786440 | tf_op jit(solution)/shard_map/ppermute | solution.py:599
  33.5 3.4 %collective-permute-start.11 = (bf16[2,128,128]{2,1,0:T(8,128)(2,1)S(1)}, bf16[2,128,128]{2,1,0:T(8,128)(2,1)S(1)}, u32[]{:S(2)}, u32[]{:S(2)}) collective-permute-start(bf16[2,128,128]{2,1,0:T(8,128)(2,1)S(1)} %get-tuple-element.55), channel_id=1, source_target_pairs={{0,16},{1,17},{2,18},{3,19},{4,20},{5,21},{6,22},{7,23},{8,24},{9,... | collective-permute-start | bytes 196616 | tf_op jit(solution)/shard_map/ppermute | solution.py:401
  35.3 3.9 %copy-start = (bf16[2048,1024]{1,0:T(8,128)(2,1)S(1)}, bf16[2048,1024]{1,0:T(8,128)(2,1)}, u32[]{:S(2)}) copy-start(bf16[2048,1024]{1,0:T(8,128)(2,1)} %weights_ref.3) | copy-start | bytes 12582916
  37.6 11.1 %collective-permute-start.12 = (bf16[512,256]{1,0:T(8,128)(2,1)S(1)}, bf16[512,256]{1,0:T(8,128)(2,1)S(1)}, u32[]{:S(2)}, u32[]{:S(2)}) collective-permute-start(bf16[512,256]{1,0:T(8,128)(2,1)S(1)} %shard_map.107), channel_id=1, source_target_pairs={{0,1},{1,2},{2,3},{3,0},{4,5},{5,6},{6,7},{7,4},{8,9},{9,10},{10,1... | collective-permute-start | bytes 786440 | tf_op jit(solution)/shard_map/ppermute | solution.py:606
  41.2 13.1 %collective-permute-start.6 = (bf16[512,256]{1,0:T(8,128)(2,1)S(1)}, bf16[512,256]{1,0:T(8,128)(2,1)S(1)}, u32[]{:S(2)}, u32[]{:S(2)}) collective-permute-start(bf16[512,256]{1,0:T(8,128)(2,1)S(1)} %collective-permute-done.5), channel_id=1, source_target_pairs={{0,1},{1,2},{2,3},{3,0},{4,5},{5,6},{6,7},{7,4},{8,9},{9,10},{10,1... | collective-permute-start | bytes 786440 | tf_op jit(solution)/shard_map/ppermute | solution.py:599
  48.7 11.2 %collective-permute-start.13 = (bf16[512,256]{1,0:T(8,128)(2,1)S(1)}, bf16[512,256]{1,0:T(8,128)(2,1)S(1)}, u32[]{:S(2)}, u32[]{:S(2)}) collective-permute-start(bf16[512,256]{1,0:T(8,128)(2,1)S(1)} %collective-permute-done.12), channel_id=1, source_target_pairs={{0,1},{1,2},{2,3},{3,0},{4,5},{5,6},{6,7},{7,4},{8,9},{9,10},{10,1... | collective-permute-start | bytes 786440 | tf_op jit(solution)/shard_map/ppermute | solution.py:606
  54.3 11.2 %collective-permute-start.7 = (bf16[512,256]{1,0:T(8,128)(2,1)S(1)}, bf16[512,256]{1,0:T(8,128)(2,1)S(1)}, u32[]{:S(2)}, u32[]{:S(2)}) collective-permute-start(bf16[512,256]{1,0:T(8,128)(2,1)S(1)} %collective-permute-done.6), channel_id=1, source_target_pairs={{0,1},{1,2},{2,3},{3,0},{4,5},{5,6},{6,7},{7,4},{8,9},{9,10},{10,1... | collective-permute-start | bytes 786440 | tf_op jit(solution)/shard_map/ppermute | solution.py:599
  59.9 8.2 %collective-permute-start.15 = (bf16[256,256]{1,0:T(8,128)(2,1)S(1)}, bf16[256,256]{1,0:T(8,128)(2,1)S(1)}, u32[]{:S(2)}, u32[]{:S(2)}) collective-permute-start(bf16[256,256]{1,0:T(8,128)(2,1)S(1)} %get-tuple-element.57), channel_id=1, source_target_pairs={{0,1},{1,2},{2,3},{3,0},{4,5},{5,6},{6,7},{7,4},{8,9},{9,10},{10,1... | collective-permute-start | bytes 393224 | tf_op jit(solution)/shard_map/ppermute | solution.py:603
  60.0 9.5 %collective-permute-start.14 = (bf16[256,256]{1,0:T(8,128)(2,1)S(1)}, bf16[256,256]{1,0:T(8,128)(2,1)S(1)}, u32[]{:S(2)}, u32[]{:S(2)}) collective-permute-start(bf16[256,256]{1,0:T(8,128)(2,1)S(1)} %get-tuple-element.58), channel_id=1, source_target_pairs={{0,1},{1,2},{2,3},{3,0},{4,5},{5,6},{6,7},{7,4},{8,9},{9,10},{10,1... | collective-permute-start | bytes 393224 | tf_op jit(solution)/shard_map/ppermute | solution.py:603
  (1 other events, 1.8 us)

commit v23 on v21

--- a/solution.py
+++ b/solution.py
@@ -366,7 +366,9 @@
     for g in range(heads):
         h = base + g
         before = before_ref[g]
-        incoming = mul_split(before[:, :depth], arrived_ref[g].astype(F32)) + before[:, depth:]
+        arrived = arrived_ref[g]
+        high, low = split(before[:, :depth])
+        incoming = (mul(high, arrived) + mul(low, arrived)) + before[:, depth:]
         high, low = split(incoming)
         reach = reach_ref[h]
         reached = mul(reach, high) + mul(reach, low)

time: 71.2 us -> 71.3 us (level)
  no operation moved by 1% of the time
where the time goes in v23:
time: 71.3 us; the launch traced here: 71.1 us
  waiting for transfers between devices  28.7 us (40%)
  starting transfers between devices  18.3 us (26%)
  Pallas kernels  17.6 us (25%)
  matrix products  4.59 us (6%)
  local copies, waits for them, and re-layouts  1.37 us (2%)
    ppermute x6, waiting for transfers between devices, on_device(): lax.ppermute(x, 'head', around)  27.4 us
    ppermute x3, starting transfers between devices, from_behind(): lax.ppermute(value, axis, [(i, i + steps) for i in range(count - steps)])  7.67 us
    ppermute x6, starting transfers between devices, exchange(): lax.ppermute(own_map, 'leaf', pairs_at(k, leaves))  7.11 us
    pallas_call x1, Pallas kernels, reads_of(): pl.pallas_call(functools.partial(reads_kernel, base), out_shape=(jax.Shap...  5.42 us
    pallas_call x1, Pallas kernels, maps_of(): pl.pallas_call(functools.partial(maps_kernel, base), out_shape=(jax.Shape...  5.05 us
    dot_general x7, matrix products, on_device(): term = jnp.dot(block, rows, preferred_element_type=F32)  4.59 us
    ppermute x6, starting transfers between devices, on_device(): lax.ppermute(x, 'head', around)  3.51 us
    pallas_call x1, Pallas kernels, filters_of(): pl.pallas_call(filters_kernel, out_shape=(per_token, per_token, jax.Shape...  1.78 us
  transfers between devices with their start and end apart: 15, of which 9 were waited for; matrix products, arithmetic and copies ran while one was open for 8% of the time, Pallas kernels for 13%

profile of v23, /device:TPU:0, one launch (start us, length us, event | category | flops | bytes accessed | tf_op | source)
XLA Modules:
  0.0 71.1 jit_solution(11821428859518439229)
XLA Ops:
  0.0 1.4 %shard_map.101 = bf16[24,4,128]{2,1,0:T(4,128)(2,1)} custom-call(bf16[512,4,128]{2,1,0:T(4,128)(2,1)} %refs_0_.1, bf16[512,4,128]{2,1,0:T(4,128)(2,1)} %refs_1_.1, bf16[512,4,128]{2,1,0:T(4,128)(2,1)} %refs_2_.1), custom_call_target="tpu_custom_call" | custom-call | flops 1000000000 | bytes 65536 | tf_op jit(solution)/shard_map/pallas_call | solution.py:420
  1.4 4.8 %collective-permute-start = (bf16[24,4,128]{2,1,0:T(4,128)(2,1)}, bf16[24,4,128]{2,1,0:T(4,128)(2,1)S(1)}, u32[]{:S(2)}, u32[]{:S(2)}) collective-permute-start(bf16[24,4,128]{2,1,0:T(4,128)(2,1)} %shard_map.101), channel_id=1, source_target_pairs={{0,4},{4,8},{8,12},{12,16},{16,20},{20,24},{24,28},{1,5},{5,9},{9,... | collective-permute-start | bytes 73736 | tf_op jit(solution)/shard_map/ppermute | solution.py:403
  6.3 1.2 %copy_bitcast_fusion.2 = (bf16[4,512,128]{2,1,0:T(8,128)(2,1)S(1)}, bf16[4,512,128]{2,1,0:T(8,128)(2,1)S(1)}) fusion(bf16[512,4,128]{2,1,0:T(4,128)(2,1)S(1)} %copy-done.8, bf16[512,4,128]{2,1,0:T(4,128)(2,1)} %refs_1_.1), kind=kLoop, calls=%fused_computation.3 | loop fusion | bytes 2097152 | tf_op jit(solution)/shard_map/transpose | solution.py:557
  7.5 1.8 %shard_map.100 = (bf16[4,512,128]{2,1,0:T(8,128)(2,1)S(1)}, bf16[4,512,128]{2,1,0:T(8,128)(2,1)S(1)}, f32[2,4,16,128]{3,2,1,0:T(8,128)S(1)}) custom-call(bf16[4,512,128]{2,1,0:T(8,128)(2,1)S(1)} %get-tuple-element.58.key_ref, bf16[4,512,128]{2,1,0:T(8,128)(2,1)S(1)} %get-tuple-element.57.value_ref, f32[3,4,4,128]{3,2,1,0:T(4,128)S(1)} %copy-done.1), custom_call_target="tpu_custom_call" | custom-call | flops 3000000000 | bytes 4194304 | tf_op jit(solution)/shard_map/pallas_call | solution.py:434
  9.4 5.1 %shard_map.102 = (bf16[4,512,128]{2,1,0:T(8,128)(2,1)S(1)}, f32[4,512,256]{2,1,0:T(8,128)S(1)}, f32[4,3,128,256]{3,2,1,0:T(8,128)S(1)}, bf16[2,128,256]{2,1,0:T(8,128)(2,1)S(1)}, bf16[2,128,256]{2,1,0:T(8,128)(2,1)S(1)}) custom-call(s32[8]{0:T(128)S(1)} %copy-done.4, bf16[4,512,128]{2,1,0:T(8,128)(2,1)S(1)} %get-tuple-element.31.unit_in_ref, ...), custom_call_target="tpu_custom_call" | custom-call | flops 5000000000 | bytes 4194304 | tf_op jit(solution)/shard_map/pallas_call | solution.py:450
  14.5 2.0 %collective-permute-start.3 = (bf16[2,128,256]{2,1,0:T(8,128)(2,1)S(1)}, bf16[2,128,256]{2,1,0:T(8,128)(2,1)S(1)}, u32[]{:S(2)}, u32[]{:S(2)}) collective-permute-start(bf16[2,128,256]{2,1,0:T(8,128)(2,1)S(1)} %get-tuple-element.42.refs_0_), channel_id=1, source_target_pairs={{0,12},{4,8},{8,4},{12,0},{1,13},{5,9},{9,5},{13,1},{2,14},{6,10},... | collective-permute-start | bytes 393224 | tf_op jit(solution)/shard_map/ppermute | solution.py:407
  16.4 1.1 %collective-permute-start.2 = (bf16[2,128,256]{2,1,0:T(8,128)(2,1)S(1)}, bf16[2,128,256]{2,1,0:T(8,128)(2,1)S(1)}, u32[]{:S(2)}, u32[]{:S(2)}) collective-permute-start(bf16[2,128,256]{2,1,0:T(8,128)(2,1)S(1)} %get-tuple-element.42.refs_0_), channel_id=1, source_target_pairs={{0,8},{4,12},{8,0},{12,4},{1,9},{5,13},{9,1},{13,5},{2,10},{6,14},... | collective-permute-start | bytes 393224 | tf_op jit(solution)/shard_map/ppermute | solution.py:407
  18.2 5.4 %shard_map.103 = (bf16[4,512,128]{2,1,0:T(8,128)(2,1)S(1)}, f32[4,512,128]{2,1,0:T(8,128)S(1)}, f32[4,512,128]{2,1,0:T(8,128)S(1)}) custom-call(s32[8]{0:T(128)S(1)} %copy-done.4, bf16[4,512,128]{2,1,0:T(8,128)(2,1)S(1)} %bitcast.20, bf16[4,512,128]{2,1,0:T(8,128)(2,1)S(1)} %bitcast.21, f32[1,128]{1,0:T(1,128)S(1)} %bitcast.22, ...), custom_call_target="tpu_custom_call" | custom-call | flops 3000000000 | bytes 4194304 | tf_op jit(solution)/shard_map/pallas_call | solution.py:476
  24.4 2.0 %collective-permute-start.10 = (bf16[2,128,256]{2,1,0:T(8,128)(2,1)S(1)}, bf16[2,128,256]{2,1,0:T(8,128)(2,1)S(1)}, u32[]{:S(2)}, u32[]{:S(2)}) collective-permute-start(bf16[2,128,256]{2,1,0:T(8,128)(2,1)S(1)} %get-tuple-element.51.refs_0_), channel_id=1, source_target_pairs={{0,12},{4,8},{8,4},{12,0},{1,13},{5,9},{9,5},{13,1},{2,14},{6,10},... | collective-permute-start | bytes 393224 | tf_op jit(solution)/shard_map/ppermute | solution.py:407
  26.4 1.1 %collective-permute-start.9 = (bf16[2,128,256]{2,1,0:T(8,128)(2,1)S(1)}, bf16[2,128,256]{2,1,0:T(8,128)(2,1)S(1)}, u32[]{:S(2)}, u32[]{:S(2)}) collective-permute-start(bf16[2,128,256]{2,1,0:T(8,128)(2,1)S(1)} %get-tuple-element.51.refs_0_), channel_id=1, source_target_pairs={{0,8},{4,12},{8,0},{12,4},{1,9},{5,13},{9,1},{13,5},{2,10},{6,14},... | collective-permute-start | bytes 393224 | tf_op jit(solution)/shard_map/ppermute | solution.py:407
  28.0 1.3 %collective-permute-start.4 = (bf16[2,128,128]{2,1,0:T(8,128)(2,1)S(1)}, bf16[2,128,128]{2,1,0:T(8,128)(2,1)S(1)}, u32[]{:S(2)}, u32[]{:S(2)}) collective-permute-start(bf16[2,128,128]{2,1,0:T(8,128)(2,1)S(1)} %get-tuple-element.46), channel_id=1, source_target_pairs={{0,16},{1,17},{2,18},{3,19},{4,20},{5,21},{6,22},{7,23},{8,24},{9,... | collective-permute-start | bytes 196616 | tf_op jit(solution)/shard_map/ppermute | solution.py:403
  29.3 0.8 %collective-permute-done.4.arrived_ref = bf16[2,128,128]{2,1,0:T(8,128)(2,1)S(1)} collective-permute-done((bf16[2,128,128]{2,1,0:T(8,128)(2,1)S(1)}, bf16[2,128,128]{2,1,0:T(8,128)(2,1)S(1)}, u32[]{:S(2)}, u32[]{:S(2)}) %collective-permute-start.4) | collective-permute-done | bytes 65568 | tf_op jit(solution)/shard_map/ppermute | solution.py:403
  30.7 1.6 %collective-permute-start.5 = (bf16[512,256]{1,0:T(8,128)(2,1)S(1)}, bf16[512,256]{1,0:T(8,128)(2,1)S(1)}, u32[]{:S(2)}, u32[]{:S(2)}) collective-permute-start(bf16[512,256]{1,0:T(8,128)(2,1)S(1)} %shard_map.105), channel_id=1, source_target_pairs={{0,1},{1,2},{2,3},{3,0},{4,5},{5,6},{6,7},{7,4},{8,9},{9,10},{10,1... | collective-permute-start | bytes 786440 | tf_op jit(solution)/shard_map/ppermute | solution.py:599
  33.5 1.5 %collective-permute-start.11 = (bf16[2,128,128]{2,1,0:T(8,128)(2,1)S(1)}, bf16[2,128,128]{2,1,0:T(8,128)(2,1)S(1)}, u32[]{:S(2)}, u32[]{:S(2)}) collective-permute-start(bf16[2,128,128]{2,1,0:T(8,128)(2,1)S(1)} %get-tuple-element.55), channel_id=1, source_target_pairs={{0,16},{1,17},{2,18},{3,19},{4,20},{5,21},{6,22},{7,23},{8,24},{9,... | collective-permute-start | bytes 196616 | tf_op jit(solution)/shard_map/ppermute | solution.py:403
  35.1 1.6 %fusion.11 = f32[512,1024]{1,0:T(8,128)S(1)} fusion(bf16[512,256]{1,0:T(8,128)(2,1)S(1)} %shard_map.105, bf16[2048,1024]{1,0:T(8,128)(2,1)} %weights_ref.1, s32[]{:T(128)S(6)} %select_n.21), kind=kOutput, calls=%fused_computation.16 | convolution fusion | flops 268435456 | bytes 2883588 | tf_op jit(solution)/shard_map/dot_general | solution.py:605
  37.4 1.8 %collective-permute-start.12 = (bf16[512,256]{1,0:T(8,128)(2,1)S(1)}, bf16[512,256]{1,0:T(8,128)(2,1)S(1)}, u32[]{:S(2)}, u32[]{:S(2)}) collective-permute-start(bf16[512,256]{1,0:T(8,128)(2,1)S(1)} %shard_map.107), channel_id=1, source_target_pairs={{0,1},{1,2},{2,3},{3,0},{4,5},{5,6},{6,7},{7,4},{8,9},{9,10},{10,1... | collective-permute-start | bytes 786440 | tf_op jit(solution)/shard_map/ppermute | solution.py:599
  39.6 1.6 %collective-permute-done.5 = bf16[512,256]{1,0:T(8,128)(2,1)S(1)} collective-permute-done((bf16[512,256]{1,0:T(8,128)(2,1)S(1)}, bf16[512,256]{1,0:T(8,128)(2,1)S(1)}, u32[]{:S(2)}, u32[]{:S(2)}) %collective-permute-start.5) | collective-permute-done | bytes 262176 | tf_op jit(solution)/shard_map/ppermute | solution.py:599
  41.7 6.9 %collective-permute-done.12 = bf16[512,256]{1,0:T(8,128)(2,1)S(1)} collective-permute-done((bf16[512,256]{1,0:T(8,128)(2,1)S(1)}, bf16[512,256]{1,0:T(8,128)(2,1)S(1)}, u32[]{:S(2)}, u32[]{:S(2)}) %collective-permute-start.12) | collective-permute-done | bytes 262176 | tf_op jit(solution)/shard_map/ppermute | solution.py:599
  49.1 5.2 %collective-permute-done.6 = bf16[512,256]{1,0:T(8,128)(2,1)S(1)} collective-permute-done((bf16[512,256]{1,0:T(8,128)(2,1)S(1)}, bf16[512,256]{1,0:T(8,128)(2,1)S(1)}, u32[]{:S(2)}, u32[]{:S(2)}) %collective-permute-start.6) | collective-permute-done | bytes 262176 | tf_op jit(solution)/shard_map/ppermute | solution.py:599
  54.7 5.2 %collective-permute-done.13 = bf16[512,256]{1,0:T(8,128)(2,1)S(1)} collective-permute-done((bf16[512,256]{1,0:T(8,128)(2,1)S(1)}, bf16[512,256]{1,0:T(8,128)(2,1)S(1)}, u32[]{:S(2)}, u32[]{:S(2)}) %collective-permute-start.13) | collective-permute-done | bytes 262176 | tf_op jit(solution)/shard_map/ppermute | solution.py:599
  60.3 5.2 %collective-permute-done.7 = bf16[512,256]{1,0:T(8,128)(2,1)S(1)} collective-permute-done((bf16[512,256]{1,0:T(8,128)(2,1)S(1)}, bf16[512,256]{1,0:T(8,128)(2,1)S(1)}, u32[]{:S(2)}, u32[]{:S(2)}) %collective-permute-start.7) | collective-permute-done | bytes 262176 | tf_op jit(solution)/shard_map/ppermute | solution.py:599
  65.5 0.8 %add_add_fusion.total_ref = f32[512,1024]{1,0:T(8,128)S(1)} fusion(f32[512,1024]{1,0:T(8,128)S(1)} %fusion, f32[512,1024]{1,0:T(8,128)S(1)} %fusion.4, f32[512,1024]{1,0:T(8,128)S(1)} %fusion.2, f32[512,1024]{1,0:T(8,128)S(1)} %fusion.7, f32[512,1024]{1,0:T(8,128)S(1)} %fusion.11, f32[512,1024]{1,0:T(8,128)S(1)} %fusion.9, ...), kind=kOutput, calls=%fused_computation | convolution fusion | flops 271581184 | bytes 15466500 | tf_op jit(solution)/shard_map/dot_general | solution.py:605
  66.3 3.4 %collective-permute-done.14.block_ref = bf16[512,256]{1,0:T(8,128)(2,1)S(1)} collective-permute-done((bf16[512,256]{1,0:T(8,128)(2,1)S(1)}, bf16[512,256]{1,0:T(8,128)(2,1)S(1)}, u32[]{:S(2)}, u32[]{:S(2)}) %collective-permute-start.14) | collective-permute-done | bytes 262176 | tf_op jit(solution)/shard_map/ppermute | solution.py:599
  69.6 1.3 %shard_map.108 = bf16[512,1024]{1,0:T(8,128)(2,1)} custom-call(s32[1]{0:T(128)} %bitcast.section, f32[512,1024]{1,0:T(8,128)S(1)} %add_add_fusion.total_ref, bf16[512,256]{1,0:T(8,128)(2,1)S(1)} %collective-permute-done.14.block_ref, bf16[2048,1024]{1,0:T(8,128)(2,1)S(1)} %copy-done), custom_call_target="tpu_custom_call" | custom-call | tf_op jit(solution)/shard_map/pallas_call | solution.py:525
  (43 shorter events, 6.6 us)
Async XLA Ops:
  0.0 6.3 %copy-start.8 = (bf16[512,4,128]{2,1,0:T(4,128)(2,1)S(1)}, bf16[512,4,128]{2,1,0:T(4,128)(2,1)}, u32[]{:S(2)}) copy-start(bf16[512,4,128]{2,1,0:T(4,128)(2,1)} %refs_2_.1) | copy-start | bytes 1572868
  0.0 7.5 %copy-start.1 = (f32[3,4,4,128]{3,2,1,0:T(4,128)S(1)}, f32[3,4,4,128]{3,2,1,0:T(4,128)}, u32[]{:S(2)}) copy-start(f32[3,4,4,128]{3,2,1,0:T(4,128)} %taps_ref.5) | copy-start | bytes 73732
  1.4 7.9 %collective-permute-start = (bf16[24,4,128]{2,1,0:T(4,128)(2,1)}, bf16[24,4,128]{2,1,0:T(4,128)(2,1)S(1)}, u32[]{:S(2)}, u32[]{:S(2)}) collective-permute-start(bf16[24,4,128]{2,1,0:T(4,128)(2,1)} %shard_map.101), channel_id=1, source_target_pairs={{0,4},{4,8},{8,12},{12,16},{16,20},{20,24},{24,28},{1,5},{5,9},{9,... | collective-permute-start | bytes 73736 | tf_op jit(solution)/shard_map/ppermute | solution.py:403
  7.5 1.8 %copy-start.2 = (f32[4,512]{1,0:T(4,128)S(1)}, f32[4,512]{1,0:T(4,128)}, u32[]{:S(2)}) copy-start(f32[4,512]{1,0:T(4,128)} %decay_ref.3) | copy-start | bytes 24580
  7.5 1.8 %copy-start.3 = (f32[4,512]{1,0:T(4,128)S(1)}, f32[4,512]{1,0:T(4,128)}, u32[]{:S(2)}) copy-start(f32[4,512]{1,0:T(4,128)} %strength_ref.3) | copy-start | bytes 24580
  7.5 1.8 %copy-start.4 = (s32[8]{0:T(128)S(1)}, s32[8]{0:T(128)}, u32[]{:S(2)}) copy-start(s32[8]{0:T(128)} %resets.3) | copy-start | bytes 100
  9.4 8.7 %copy-start.6 = (bf16[512,4,128]{2,1,0:T(4,128)(2,1)S(1)}, bf16[512,4,128]{2,1,0:T(4,128)(2,1)}, u32[]{:S(2)}) copy-start(bf16[512,4,128]{2,1,0:T(4,128)(2,1)} %refs_0_.1) | copy-start | bytes 1572868
  9.4 8.7 %copy-start.7 = (bf16[512,4,128]{2,1,0:T(4,128)(2,1)S(1)}, bf16[512,4,128]{2,1,0:T(4,128)(2,1)}, u32[]{:S(2)}) copy-start(bf16[512,4,128]{2,1,0:T(4,128)(2,1)} %param.13) | copy-start | bytes 1572868
  14.4 3.7 %copy-start.5 = (f32[128]{0:T(128)S(1)}, f32[128]{0:T(128)}, u32[]{:S(2)}) copy-start(f32[128]{0:T(128)} %param.18) | copy-start | bytes 1540
  14.5 9.2 %collective-permute-start.3 = (bf16[2,128,256]{2,1,0:T(8,128)(2,1)S(1)}, bf16[2,128,256]{2,1,0:T(8,128)(2,1)S(1)}, u32[]{:S(2)}, u32[]{:S(2)}) collective-permute-start(bf16[2,128,256]{2,1,0:T(8,128)(2,1)S(1)} %get-tuple-element.42.refs_0_), channel_id=1, source_target_pairs={{0,12},{4,8},{8,4},{12,0},{1,13},{5,9},{9,5},{13,1},{2,14},{6,10},... | collective-permute-start | bytes 393224 | tf_op jit(solution)/shard_map/ppermute | solution.py:407
  16.4 7.2 %collective-permute-start.2 = (bf16[2,128,256]{2,1,0:T(8,128)(2,1)S(1)}, bf16[2,128,256]{2,1,0:T(8,128)(2,1)S(1)}, u32[]{:S(2)}, u32[]{:S(2)}) collective-permute-start(bf16[2,128,256]{2,1,0:T(8,128)(2,1)S(1)} %get-tuple-element.42.refs_0_), channel_id=1, source_target_pairs={{0,8},{4,12},{8,0},{12,4},{1,9},{5,13},{9,1},{13,5},{2,10},{6,14},... | collective-permute-start | bytes 393224 | tf_op jit(solution)/shard_map/ppermute | solution.py:407
  17.5 6.2 %collective-permute-start.1 = (bf16[2,128,256]{2,1,0:T(8,128)(2,1)S(1)}, bf16[2,128,256]{2,1,0:T(8,128)(2,1)S(1)}, u32[]{:S(2)}, u32[]{:S(2)}) collective-permute-start(bf16[2,128,256]{2,1,0:T(8,128)(2,1)S(1)} %get-tuple-element.42.refs_0_), channel_id=1, source_target_pairs={{0,4},{4,0},{8,12},{12,8},{1,5},{5,1},{9,13},{13,9},{2,6},{6,2},{1... | collective-permute-start | bytes 393224 | tf_op jit(solution)/shard_map/ppermute | solution.py:407
  24.4 8.0 %collective-permute-start.10 = (bf16[2,128,256]{2,1,0:T(8,128)(2,1)S(1)}, bf16[2,128,256]{2,1,0:T(8,128)(2,1)S(1)}, u32[]{:S(2)}, u32[]{:S(2)}) collective-permute-start(bf16[2,128,256]{2,1,0:T(8,128)(2,1)S(1)} %get-tuple-element.51.refs_0_), channel_id=1, source_target_pairs={{0,12},{4,8},{8,4},{12,0},{1,13},{5,9},{9,5},{13,1},{2,14},{6,10},... | collective-permute-start | bytes 393224 | tf_op jit(solution)/shard_map/ppermute | solution.py:407
  26.4 6.3 %collective-permute-start.9 = (bf16[2,128,256]{2,1,0:T(8,128)(2,1)S(1)}, bf16[2,128,256]{2,1,0:T(8,128)(2,1)S(1)}, u32[]{:S(2)}, u32[]{:S(2)}) collective-permute-start(bf16[2,128,256]{2,1,0:T(8,128)(2,1)S(1)} %get-tuple-element.51.refs_0_), channel_id=1, source_target_pairs={{0,8},{4,12},{8,0},{12,4},{1,9},{5,13},{9,1},{13,5},{2,10},{6,14},... | collective-permute-start | bytes 393224 | tf_op jit(solution)/shard_map/ppermute | solution.py:407
  27.4 5.4 %collective-permute-start.8 = (bf16[2,128,256]{2,1,0:T(8,128)(2,1)S(1)}, bf16[2,128,256]{2,1,0:T(8,128)(2,1)S(1)}, u32[]{:S(2)}, u32[]{:S(2)}) collective-permute-start(bf16[2,128,256]{2,1,0:T(8,128)(2,1)S(1)} %get-tuple-element.51.refs_0_), channel_id=1, source_target_pairs={{0,4},{4,0},{8,12},{12,8},{1,5},{5,1},{9,13},{13,9},{2,6},{6,2},{1... | collective-permute-start | bytes 393224 | tf_op jit(solution)/shard_map/ppermute | solution.py:407
  28.0 2.2 %collective-permute-start.4 = (bf16[2,128,128]{2,1,0:T(8,128)(2,1)S(1)}, bf16[2,128,128]{2,1,0:T(8,128)(2,1)S(1)}, u32[]{:S(2)}, u32[]{:S(2)}) collective-permute-start(bf16[2,128,128]{2,1,0:T(8,128)(2,1)S(1)} %get-tuple-element.46), channel_id=1, source_target_pairs={{0,16},{1,17},{2,18},{3,19},{4,20},{5,21},{6,22},{7,23},{8,24},{9,... | collective-permute-start | bytes 196616 | tf_op jit(solution)/shard_map/ppermute | solution.py:403
  30.7 10.5 %collective-permute-start.5 = (bf16[512,256]{1,0:T(8,128)(2,1)S(1)}, bf16[512,256]{1,0:T(8,128)(2,1)S(1)}, u32[]{:S(2)}, u32[]{:S(2)}) collective-permute-start(bf16[512,256]{1,0:T(8,128)(2,1)S(1)} %shard_map.105), channel_id=1, source_target_pairs={{0,1},{1,2},{2,3},{3,0},{4,5},{5,6},{6,7},{7,4},{8,9},{9,10},{10,1... | collective-permute-start | bytes 786440 | tf_op jit(solution)/shard_map/ppermute | solution.py:599
  33.5 3.2 %collective-permute-start.11 = (bf16[2,128,128]{2,1,0:T(8,128)(2,1)S(1)}, bf16[2,128,128]{2,1,0:T(8,128)(2,1)S(1)}, u32[]{:S(2)}, u32[]{:S(2)}) collective-permute-start(bf16[2,128,128]{2,1,0:T(8,128)(2,1)S(1)} %get-tuple-element.55), channel_id=1, source_target_pairs={{0,16},{1,17},{2,18},{3,19},{4,20},{5,21},{6,22},{7,23},{8,24},{9,... | collective-permute-start | bytes 196616 | tf_op jit(solution)/shard_map/ppermute | solution.py:403
  35.1 4.1 %copy-start = (bf16[2048,1024]{1,0:T(8,128)(2,1)S(1)}, bf16[2048,1024]{1,0:T(8,128)(2,1)}, u32[]{:S(2)}) copy-start(bf16[2048,1024]{1,0:T(8,128)(2,1)} %weights_ref.1) | copy-start | bytes 12582916
  37.4 11.3 %collective-permute-start.12 = (bf16[512,256]{1,0:T(8,128)(2,1)S(1)}, bf16[512,256]{1,0:T(8,128)(2,1)S(1)}, u32[]{:S(2)}, u32[]{:S(2)}) collective-permute-start(bf16[512,256]{1,0:T(8,128)(2,1)S(1)} %shard_map.107), channel_id=1, source_target_pairs={{0,1},{1,2},{2,3},{3,0},{4,5},{5,6},{6,7},{7,4},{8,9},{9,10},{10,1... | collective-permute-start | bytes 786440 | tf_op jit(solution)/shard_map/ppermute | solution.py:599
  41.2 13.0 %collective-permute-start.6 = (bf16[512,256]{1,0:T(8,128)(2,1)S(1)}, bf16[512,256]{1,0:T(8,128)(2,1)S(1)}, u32[]{:S(2)}, u32[]{:S(2)}) collective-permute-start(bf16[512,256]{1,0:T(8,128)(2,1)S(1)} %collective-permute-done.5), channel_id=1, source_target_pairs={{0,1},{1,2},{2,3},{3,0},{4,5},{5,6},{6,7},{7,4},{8,9},{9,10},{10,1... | collective-permute-start | bytes 786440 | tf_op jit(solution)/shard_map/ppermute | solution.py:599
  48.6 11.2 %collective-permute-start.13 = (bf16[512,256]{1,0:T(8,128)(2,1)S(1)}, bf16[512,256]{1,0:T(8,128)(2,1)S(1)}, u32[]{:S(2)}, u32[]{:S(2)}) collective-permute-start(bf16[512,256]{1,0:T(8,128)(2,1)S(1)} %collective-permute-done.12), channel_id=1, source_target_pairs={{0,1},{1,2},{2,3},{3,0},{4,5},{5,6},{6,7},{7,4},{8,9},{9,10},{10,1... | collective-permute-start | bytes 786440 | tf_op jit(solution)/shard_map/ppermute | solution.py:599
  54.2 11.2 %collective-permute-start.7 = (bf16[512,256]{1,0:T(8,128)(2,1)S(1)}, bf16[512,256]{1,0:T(8,128)(2,1)S(1)}, u32[]{:S(2)}, u32[]{:S(2)}) collective-permute-start(bf16[512,256]{1,0:T(8,128)(2,1)S(1)} %collective-permute-done.6), channel_id=1, source_target_pairs={{0,1},{1,2},{2,3},{3,0},{4,5},{5,6},{6,7},{7,4},{8,9},{9,10},{10,1... | collective-permute-start | bytes 786440 | tf_op jit(solution)/shard_map/ppermute | solution.py:599
  59.9 9.8 %collective-permute-start.14 = (bf16[512,256]{1,0:T(8,128)(2,1)S(1)}, bf16[512,256]{1,0:T(8,128)(2,1)S(1)}, u32[]{:S(2)}, u32[]{:S(2)}) collective-permute-start(bf16[512,256]{1,0:T(8,128)(2,1)S(1)} %collective-permute-done.13), channel_id=1, source_target_pairs={{0,1},{1,2},{2,3},{3,0},{4,5},{5,6},{6,7},{7,4},{8,9},{9,10},{10,1... | collective-permute-start | bytes 786440 | tf_op jit(solution)/shard_map/ppermute | solution.py:599
